TPU v7x, 32 devices: a whole 2x2x4 slice. The times are simulated.
32 devices in a mesh: leaf: 4 (over z), rows: 8 (over y, x, core).
Axes of the slice: x: 2, y: 2, z: 4, core: 2. Of those that a mesh axis runs over, the one named last changes fastest.
Arguments:
- rhs: bfloat16 [147456, 512], P(('leaf', 'rows')), may hold values from -6 to 6
- leaf_order: int32 [576, 256], P(('leaf', 'rows')), may hold values from 0 to 255, each once within a row
- leaf_inv: bfloat16 [576, 256, 256], P(('leaf', 'rows')), may hold values from -0.375 to 0.375
- right_basis: bfloat16 [3, 147456, 128], P(None, ('leaf', 'rows')), may hold values from -0.03125 to 0.03125
- left_basis: bfloat16 [3, 147456, 128], P(None, ('leaf', 'rows')), may hold values from -0.375 to 0.375
- rank_perm: int32 [3, 128], replicated, may hold values from 0 to 127, each once within a row
- joined: float32 [7, 256, 256], replicated, may hold values from -0.375 to 0.375
Outputs:
- solution: float32 [147456, 512], P(('leaf', 'rows'))
Inputs may be any that keep to these rules, and one draw needn't show every extreme that they name: Each row of leaf_order names every number below 256 once. Each row of rank_perm names every number below 128 once.
All inputs are finite; a program needn't handle non-finite values.
Results may differ from a plain program's by a relative error of at most 0.0003.
Values sent between devices are 32-bit elements; how exact they have to be, the bound alone decides.
No kernel may reach another device: no remote copies, remote signals or barrier semaphores. Data moves between devices by JAX's collectives and lax.ppermute only.
A program may use at most 128 MiB of HBM per device.

v0:
```python
import jax
import jax.numpy as jnp
from jax import lax
from jax.sharding import PartitionSpec as P

HIGHEST = lax.Precision.HIGHEST


def partner(block, axis, bit):
    count = lax.axis_size(axis)
    route = []
    for low in range(count):
        high = low | 1 << bit
        if high != low and high < count:
            route += [(low, high), (high, low)]
    return lax.ppermute(block, axis, route)


def split_halves(value):
    high_part = lax.optimization_barrier(value.astype(jnp.bfloat16))
    low_part = (value - high_part.astype(jnp.float32)).astype(jnp.bfloat16)
    return (high_part, low_part)


def project(basis_rows, current):
    high_part, low_part = split_halves(current)
    return jnp.einsum(
        "mk,mr->kr", basis_rows, high_part, preferred_element_type=jnp.float32
    ) + jnp.einsum("mk,mr->kr", basis_rows, low_part, preferred_element_type=jnp.float32)


def expand(basis_rows, coefficient):
    high_part, low_part = split_halves(coefficient)
    return jnp.dot(basis_rows, high_part, preferred_element_type=jnp.float32) + jnp.dot(
        basis_rows, low_part, preferred_element_type=jnp.float32
    )


def add_child(partial_value, bit_list):
    for swap_bit in bit_list:
        partial_value = partial_value + partner(partial_value, ("leaf", "rows"), swap_bit)
    return partial_value


def join_pair(child_total, rank_order, node_inverse, child_side, pair_bit, rank_width):
    own_proj = jnp.take(child_total, rank_order, axis=0)
    own_columns = lax.dynamic_slice_in_dim(node_inverse, child_side * rank_width, rank_width, 1)
    own_term = jnp.dot(own_columns, own_proj, precision=HIGHEST, preferred_element_type=jnp.float32)
    pair_sum = own_term + partner(own_term, ("leaf", "rows"), pair_bit)
    return lax.dynamic_slice_in_dim(pair_sum, child_side * rank_width, rank_width, 0)


def per_device(rhs, leaf_order, leaf_inv, right_basis, left_basis, rank_perm, joined):
    level_count = right_basis.shape[0]
    rank_width = right_basis.shape[2]
    nblocks = leaf_inv.shape[0]
    block_width = leaf_inv.shape[1]
    columns = rhs.shape[1]
    leaves = lax.axis_size("leaf")
    row_count = lax.axis_size("rows")
    row_bits = row_count.bit_length() - 1
    flat_index = lax.axis_index("leaf") * row_count + lax.axis_index("rows")
    blocks = rhs.reshape(nblocks, block_width, columns)
    ordered = jnp.take_along_axis(blocks, leaf_order[:, :, None], axis=1)
    current = jnp.einsum(
        "bij,bjr->bir", leaf_inv, ordered, preferred_element_type=jnp.float32
    ).reshape(nblocks * block_width, columns)
    partial_value = project(right_basis[0], current)
    for tree_level in range(level_count):
        low_bit = row_bits - 1 + tree_level
        node_index = flat_index // 2 ** (low_bit + 1)
        child_side = flat_index // 2**low_bit % 2
        offset = 2 * leaves - 2 * leaves // 2**tree_level
        node_inverse = lax.dynamic_index_in_dim(joined, offset + node_index, 0, keepdims=False)
        rank_order = rank_perm[tree_level]
        last_level = tree_level + 1 >= level_count
        if tree_level == 0:
            child_total = add_child(partial_value, list(range(row_bits - 1)))
            coefficient = join_pair(
                child_total, rank_order, node_inverse, child_side, low_bit, rank_width
            )
        else:
            leaf_bits = list(range(row_bits, row_bits + tree_level - 1))
            column_share = lax.psum_scatter(partial_value, "rows", scatter_dimension=1, tiled=True)
            child_total = add_child(column_share, leaf_bits)
            share_coef = join_pair(
                child_total, rank_order, node_inverse, child_side, low_bit, rank_width
            )
            coefficient = lax.all_gather(share_coef, "rows", axis=1, tiled=True)
        current = current - expand(left_basis[tree_level], coefficient)
        if not last_level:
            partial_value = project(right_basis[tree_level + 1], current)
    return current


def solution(mesh):
    return jax.shard_map(
        per_device,
        mesh=mesh,
        in_specs=(
            P(("leaf", "rows"), None),
            P(("leaf", "rows"), None),
            P(("leaf", "rows"), None, None),
            P(None, ("leaf", "rows"), None),
            P(None, ("leaf", "rows"), None),
            P(),
            P(),
        ),
        out_specs=P(("leaf", "rows"), None),
        check_vma=False,
    )
```

profile of v0, /device:TPU:0, one launch (start us, length us, event | category | flops | bytes accessed | tf_op | source)
XLA Modules:
  0.0 310.7 jit_solution(7965586252503742422)
XLA Ops:
  6.5 0.0 copy-start
  6.5 0.0 reduce-scatter.7.cloned.1.call-start
  6.5 0.9 bitcast_or_fusion
  7.4 0.8 compare_and_fusion
  8.2 84.9 %gather_fusion.1 = bf16[4608,512]{1,0:T(8,128)(2,1)} fusion(bf16[18,256,512]{2,1,0:T(8,128)(2,1)} %bitcast.96, s32[4608]{0:T(1024)S(1)} %reshape.82), kind=kCustom, calls=%fused_computation.3 | custom fusion | bytes 9474048 | tf_op jit(solution)/shard_map/jit(take_along_axis)/gather | solution.py:64
  93.1 0.0 copy-done
  93.1 4.2 %fusion.3 = f32[18,512,256]{1,2,0:T(8,128)S(1)} fusion(bf16[18,256,256]{2,1,0:T(8,128)(2,1)S(1)} %copy-done, bf16[18,256,512]{2,1,0:T(8,128)(2,1)} %bitcast.99, pred[18,256]{1,0:T(8,128)(4,1)S(1)} %compare_and_fusion), kind=kOutput, calls=%fused_computation.13 | convolution fusion | flops 1210318848 | bytes 16519680 | tf_op jit(solution)/shard_map/bij,bjr->bir/dot_general | solution.py:65
  97.4 0.0 copy-start.2
  97.4 1.9 bitcast_convert_fusion
  99.4 1.8 copy-done.2
  101.2 3.2 %fusion = f32[512,128]{1,0:T(8,128)S(1)} fusion(f32[4608,512]{1,0:T(8,128)S(1)} %bitcast.97, bf16[4608,512]{1,0:T(8,128)(2,1)S(1)} %bitcast_convert_fusion, bf16[3,4608,128]{2,1,0:T(8,128)(2,1)} %param.12), kind=kOutput, calls=%fused_computation.10 | convolution fusion | flops 611057664 | bytes 15597568 | tf_op jit(solution)/shard_map/mk,mr->kr/dot_general | solution.py:29
  104.4 0.0 copy-start.6
  104.4 2.7 fusion.37
  107.1 0.5 collective-permute-start
  107.6 0.0 copy-done.6
  107.6 1.2 collective-permute-done
  108.8 2.9 collective-permute-start.1
  111.8 6.6 %collective-permute-done.1 = f32[128,512]{0,1:T(8,128)S(1)} collective-permute-done((f32[128,512]{0,1:T(8,128)S(1)}, f32[128,512]{0,1:T(8,128)S(1)}, u32[]{:S(2)}, u32[]{:S(2)}) %collective-permute-start.1) | collective-permute-done | bytes 262176 | tf_op jit(solution)/shard_map/ppermute | solution.py:16
  118.4 0.1 copy.16
  118.5 0.8 gather_fusion
  119.3 1.6 fusion.52
  120.9 1.8 collective-permute-start.2
  122.7 9.6 %copy.17 = f32[4608,512]{0,1:T(8,128)} copy(f32[4608,512]{1,0:T(8,128)} %bitcast.98) | data formatting | bytes 18874368 | tf_op jit(solution)/shard_map/reshape | solution.py:67
  132.3 2.1 collective-permute-done.2
  134.5 6.5 %fusion.19 = f32[512,4608]{1,0:T(8,128)} fusion(bf16[3,4608,128]{2,1,0:T(8,128)(2,1)} %param.13, bf16[128,512]{1,0:T(8,128)(2,1)S(1)} %fusion.64, f32[256,512]{1,0:T(8,128)S(1)} %collective-permute-done.2, s32[]{:T(128)S(6)} %select_n.109, f32[256,512]{1,0:T(8,128)S(1)} %fusion.52), kind=kOutput, calls=%fused_computation.29 | convolution fusion | flops 604241920 | bytes 11272196 | tf_op jit(solution)/shard_map/dot_general | solution.py:34
  140.9 8.1 %fusion.80 = (bf16[4608,512]{0,1:T(8,128)(2,1)S(1)}, f32[4608,512]{0,1:T(8,128)S(1)}) fusion(f32[4608,512]{0,1:T(8,128)} %copy.17, f32[512,4608]{1,0:T(8,128)} %fusion.19, bf16[128,512]{1,0:T(8,128)(2,1)S(1)} %fusion.64, bf16[3,4608,128]{2,1,0:T(8,128)(2,1)} %param.13), kind=kOutput, calls=%fused_computation.100 | convolution fusion | flops 611057664 | bytes 34340864 | tf_op jit(solution)/shard_map/dot_general | solution.py:34
  149.0 0.0 copy-start.5
  149.1 3.6 %fusion.1 = f32[512,128]{1,0:T(8,128)S(1)} fusion(f32[4608,512]{0,1:T(8,128)S(1)} %get-tuple-element.14, bf16[4608,512]{0,1:T(8,128)(2,1)S(1)} %get-tuple-element.13, bf16[3,4608,128]{2,1,0:T(8,128)(2,1)} %param.12), kind=kOutput, calls=%fused_computation.11 | convolution fusion | flops 611057664 | bytes 15597568 | tf_op jit(solution)/shard_map/mk,mr->kr/dot_general | solution.py:29
  152.6 0.2 copy-done.5
  152.8 3.4 %fusion.28 = f32[512,128]{1,0:T(8,128)} fusion(f32[512,128]{1,0:T(8,128)S(1)} %fusion.1, bf16[4608,512]{0,1:T(8,128)(2,1)S(1)} %get-tuple-element.13, bf16[3,4608,128]{2,1,0:T(8,128)(2,1)} %param.12), kind=kOutput, calls=%fused_computation.36 | convolution fusion | flops 604045312 | bytes 6422528 | tf_op jit(solution)/shard_map/mk,mr->kr/dot_general | solution.py:27
  156.2 0.0 reduce-scatter.7.cloned.1.call-update
  156.2 0.0 reduce-scatter.5.cloned.1.call-start
  156.3 34.8 %reduce-scatter.7.cloned.1.call-done = f32[64,128]{1,0:T(8,128)} async-done(((f32[512,128]{1,0:T(8,128)}), f32[64,128]{1,0:T(8,128)}) %reduce-scatter.7.cloned.1.call-update) | async-done | bytes 32784
  191.1 0.8 copy.22
  191.9 0.7 gather_fusion.2
  192.6 1.3 fusion.56
  193.9 1.5 collective-permute-start.3
  195.4 2.8 collective-permute-done.3
  198.2 9.2 %all_gather.6 = f32[128,512]{0,1:T(8,128)S(1)} all-gather(f32[128,64]{0,1:T(8,128)S(1)} %dynamic-slice_add_fusion.3), channel_id=1, replica_groups=mesh['leaf'=4,'rows'=8] {'rows'}, dimensions={1}, use_global_device_ids=true | all-gather | bytes 294912 | tf_op jit(solution)/shard_map/all_gather | solution.py:89
  207.5 6.3 %fusion.14 = f32[512,4608]{1,0:T(8,128)} fusion(bf16[128,512]{0,1:T(8,128)(2,1)S(1)} %convert_element_type.63, bf16[3,4608,128]{2,1,0:T(8,128)(2,1)} %param.13), kind=kOutput, calls=%fused_computation.24 | convolution fusion | flops 603979776 | bytes 10747904 | tf_op jit(solution)/shard_map/dot_general | solution.py:34
  213.8 7.6 %fusion.81 = (bf16[4608,512]{0,1:T(8,128)(2,1)S(1)}, f32[4608,512]{0,1:T(8,128)S(1)}) fusion(f32[4608,512]{0,1:T(8,128)} %copy-done.5, f32[512,4608]{1,0:T(8,128)} %fusion.14, bf16[3,4608,128]{2,1,0:T(8,128)(2,1)} %param.13, f32[128,512]{0,1:T(8,128)S(1)} %all_gather.6, bf16[128,512]{0,1:T(8,128)(2,1)S(1)} %convert_element_type.63), kind=kOutput, calls=%fused_computation.101 | convolution fusion | flops 611254272 | bytes 34603008 | tf_op jit(solution)/shard_map/dot_general | solution.py:34
  221.4 0.0 copy-start.3
  221.4 3.6 %fusion.2 = f32[512,128]{1,0:T(8,128)S(1)} fusion(f32[4608,512]{0,1:T(8,128)S(1)} %get-tuple-element.16, bf16[4608,512]{0,1:T(8,128)(2,1)S(1)} %get-tuple-element.15, bf16[3,4608,128]{2,1,0:T(8,128)(2,1)} %param.12), kind=kOutput, calls=%fused_computation.12 | convolution fusion | flops 611057664 | bytes 15597568 | tf_op jit(solution)/shard_map/mk,mr->kr/dot_general | solution.py:29
  225.0 0.2 copy-done.3
  225.2 3.4 %fusion.34 = f32[128,512]{0,1:T(8,128)} fusion(f32[512,128]{1,0:T(8,128)S(1)} %fusion.2, bf16[4608,512]{0,1:T(8,128)(2,1)S(1)} %get-tuple-element.15, bf16[3,4608,128]{2,1,0:T(8,128)(2,1)} %param.12), kind=kOutput, calls=%fused_computation.38 | convolution fusion | flops 604045312 | bytes 6422528 | tf_op jit(solution)/shard_map/mk,mr->kr/dot_general | solution.py:27
  228.5 0.0 reduce-scatter.5.cloned.1.call-update
  228.6 33.7 %reduce-scatter.5.cloned.1.call-done = f32[128,64]{0,1:T(8,128)} async-done(((f32[128,512]{0,1:T(8,128)}), f32[128,64]{0,1:T(8,128)}) %reduce-scatter.5.cloned.1.call-update) | async-done | bytes 32784 | tf_op jit(solution)/shard_map/reduce_scatter | solution.py:84
  262.3 1.5 collective-permute-start.4
  263.8 2.6 collective-permute-done.4
  266.4 0.8 add.180
  267.2 0.1 copy.19
  267.3 0.7 gather_fusion.3
  267.9 1.3 fusion.54
  269.3 2.4 collective-permute-start.5
  271.7 2.8 collective-permute-done.5
  274.5 9.2 %all_gather.7 = f32[128,512]{0,1:T(8,128)S(1)} all-gather(f32[128,64]{0,1:T(8,128)S(1)} %dynamic-slice_add_fusion.2), channel_id=1, replica_groups=mesh['leaf'=4,'rows'=8] {'rows'}, dimensions={1}, use_global_device_ids=true | all-gather | bytes 294912 | tf_op jit(solution)/shard_map/all_gather | solution.py:89
  283.8 0.0 copy-start.4
  283.8 2.8 fusion.8
  286.6 1.2 copy-done.4
  287.8 6.4 %bitcast_subtract_fusion = f32[4608,512]{0,1:T(8,128)} fusion(f32[4608,512]{0,1:T(8,128)S(1)} %copy-done.4, f32[512,4608]{1,0:T(8,128)S(1)} %fusion.8, bf16[3,4608,128]{2,1,0:T(8,128)(2,1)} %param.13, f32[128,512]{0,1:T(8,128)S(1)} %all_gather.7, bf16[128,512]{0,1:T(8,128)(2,1)S(1)} %convert_element_type.69), kind=kOutput, calls=%fused_computation.4 | convolution fusion | flops 608894976 | bytes 29884416 | tf_op jit(solution)/shard_map/dot_general | solution.py:34
  294.1 0.0 copy-start.1
  294.2 9.7 %copy.20 = f32[4608,512]{1,0:T(8,128)} copy(f32[4608,512]{0,1:T(8,128)} %bitcast_subtract_fusion) | data formatting | bytes 18874368 | tf_op jit(solution)/shard_map/sub | solution.py:90
  303.9 0.0 copy-done.1
  (13 shorter events, 0.2 us)
Async XLA Ops:
  6.5 86.6 %copy-start = (bf16[18,256,256]{2,1,0:T(8,128)(2,1)S(1)}, bf16[18,256,256]{2,1,0:T(8,128)(2,1)}, u32[]{:S(2)}) copy-start(bf16[18,256,256]{2,1,0:T(8,128)(2,1)} %param.11) | copy-start | bytes 7077892
  6.5 184.5 %reduce-scatter.7.cloned.1.call-start = ((), (), s32[]{:S(2)}) async-start(), calls=%async_computation.3 | async-start | bytes 294912
  97.4 3.8 %copy-start.2 = (f32[18,512,256]{1,2,0:T(8,128)}, f32[18,512,256]{1,2,0:T(8,128)S(1)}, u32[]{:S(2)}) copy-start(f32[18,512,256]{1,2,0:T(8,128)S(1)} %fusion.3) | copy-start | bytes 28311556
  104.4 3.2 %copy-start.6 = (s32[3,128]{1,0:T(4,128)S(1)}, s32[3,128]{1,0:T(4,128)}, u32[]{:S(2)}) copy-start(s32[3,128]{1,0:T(4,128)} %param.14) | copy-start | bytes 4612
  107.1 1.7 collective-permute-start
  108.8 9.5 %collective-permute-start.1 = (f32[128,512]{0,1:T(8,128)S(1)}, f32[128,512]{0,1:T(8,128)S(1)}, u32[]{:S(2)}, u32[]{:S(2)}) collective-permute-start(f32[128,512]{0,1:T(8,128)S(1)} %add.159), channel_id=1, source_target_pairs={{0,2},{2,0},{1,3},{3,1},{4,6},{6,4},{5,7},{7,5},{8,10},{10,8},{9,1... | collective-permute-start | bytes 786440 | tf_op jit(solution)/shard_map/ppermute | solution.py:16
  120.9 13.5 %collective-permute-start.2 = (f32[256,512]{1,0:T(8,128)S(1)}, f32[256,512]{1,0:T(8,128)S(1)}, u32[]{:S(2)}, u32[]{:S(2)}) collective-permute-start(f32[256,512]{1,0:T(8,128)S(1)} %fusion.52), channel_id=1, source_target_pairs={{0,4},{4,0},{1,5},{5,1},{2,6},{6,2},{3,7},{7,3},{8,12},{12,8},{9,1... | collective-permute-start | bytes 1572872 | tf_op jit(solution)/shard_map/ppermute | solution.py:16
  149.0 3.7 %copy-start.5 = (f32[4608,512]{0,1:T(8,128)}, f32[4608,512]{0,1:T(8,128)S(1)}, u32[]{:S(2)}) copy-start(f32[4608,512]{0,1:T(8,128)S(1)} %get-tuple-element.14) | copy-start | bytes 28311556
  156.2 106.1 %reduce-scatter.5.cloned.1.call-start = ((), (), s32[]{:S(2)}) async-start(), calls=%async_computation.2 | async-start | bytes 294912 | tf_op jit(solution)/shard_map/reduce_scatter | solution.py:84
  193.9 4.3 %collective-permute-start.3 = (f32[256,64]{0,1:T(8,128)S(1)}, f32[256,64]{0,1:T(8,128)S(1)}, u32[]{:S(2)}, u32[]{:S(2)}) collective-permute-start(f32[256,64]{0,1:T(8,128)S(1)} %fusion.56), channel_id=1, source_target_pairs={{0,8},{8,0},{1,9},{9,1},{2,10},{10,2},{3,11},{11,3},{4,12},{12,4},... | collective-permute-start | bytes 196616 | tf_op jit(solution)/shard_map/ppermute | solution.py:16
  221.4 3.7 %copy-start.3 = (f32[4608,512]{0,1:T(8,128)}, f32[4608,512]{0,1:T(8,128)S(1)}, u32[]{:S(2)}) copy-start(f32[4608,512]{0,1:T(8,128)S(1)} %get-tuple-element.16) | copy-start | bytes 28311556
  262.3 4.1 %collective-permute-start.4 = (f32[128,64]{0,1:T(8,128)}, f32[128,64]{0,1:T(8,128)S(1)}, u32[]{:S(2)}, u32[]{:S(2)}) collective-permute-start(f32[128,64]{0,1:T(8,128)} %reduce-scatter.5.cloned.1.call-done), channel_id=1, source_target_pairs={{0,8},{8,0},{1,9},{9,1},{2,10},{10,2},{3,11},{11,3},{4,12},{12,4},... | collective-permute-start | bytes 98312 | tf_op jit(solution)/shard_map/ppermute | solution.py:16
  269.3 5.2 %collective-permute-start.5 = (f32[256,64]{0,1:T(8,128)S(1)}, f32[256,64]{0,1:T(8,128)S(1)}, u32[]{:S(2)}, u32[]{:S(2)}) collective-permute-start(f32[256,64]{0,1:T(8,128)S(1)} %fusion.54), channel_id=1, source_target_pairs={{0,16},{16,0},{1,17},{17,1},{2,18},{18,2},{3,19},{19,3},{4,20},{20... | collective-permute-start | bytes 196616 | tf_op jit(solution)/shard_map/ppermute | solution.py:16
  283.8 4.0 %copy-start.4 = (f32[4608,512]{0,1:T(8,128)S(1)}, f32[4608,512]{0,1:T(8,128)}, u32[]{:S(2)}) copy-start(f32[4608,512]{0,1:T(8,128)} %copy-done.3) | copy-start | bytes 28311556
  294.1 9.7 %copy-start.1 = (bf16[18,256,256]{2,1,0:T(8,128)(2,1)S(1)}, bf16[18,256,256]{2,1,0:T(8,128)(2,1)}, u32[]{:S(2)}) copy-start(bf16[18,256,256]{2,1,0:T(8,128)(2,1)} %param.11) | copy-start | bytes 7077892
Sparse Core Ops, SparseCore 0:
  156.3 34.7 reduce-scatter.6
  228.7 33.5 reduce-scatter.4
where the time goes:
time: 313 us; the launch traced here: 311 us
  local copies, waits for them, and re-layouts  111 us (35%)
  waiting for transfers between devices  86.7 us (28%)
  matrix products  66 us (21%)
  blocking collectives  18.5 us (6%)
  between operations  13.6 us (4%)
  starting transfers between devices  10.7 us (3%)
  other arithmetic  4.52 us (1%)
    gather x2, local copies, waits for them, and re-layouts, per_device(): ordered = jnp.take_along_axis(blocks, leaf_order[:, :, None], axis=1)  84.9 us
    unnamed x3, waiting for transfers between devices  34.8 us
    reduce_scatter x1, waiting for transfers between devices, per_device(): lax.psum_scatter(partial_value, 'rows', scatter_dimension=1, tiled=True)  33.7 us
    dot_general x3, matrix products, expand(): jnp.dot(basis_rows, low_part, preferred_element_type=jnp.float32)  20.4 us
    all_gather x2, blocking collectives, per_device(): coefficient = lax.all_gather(share_coef, 'rows', axis=1, tiled=True)  18.5 us
    ppermute x6, waiting for transfers between devices, partner(): return lax.ppermute(block, axis, route)  18.1 us
    dot_general x3, matrix products, expand(): jnp.dot(basis_rows, high_part, preferred_element_type=jnp.float32)  17.3 us
    ppermute x6, starting transfers between devices, partner(): return lax.ppermute(block, axis, route)  10.6 us
  transfers between devices with their start and end apart: 8, of which 8 were waited for; matrix products, arithmetic and copies ran while one was open for 3% of the time, Pallas kernels for 0%

commit v1 on v0

v1 whole, which is shorter than its diff:
```python
import functools

import jax
import jax.numpy as jnp
from jax import lax
from jax.experimental import pallas as pl
from jax.experimental.pallas import tpu as pltpu
from jax.sharding import PartitionSpec as P

HIGHEST = lax.Precision.HIGHEST
MIB = 1 << 20


def dot(a, b, contract, exact=False):
    return lax.dot_general(
        a, b, ((contract[:1], contract[1:]), ((), ())),
        precision=HIGHEST if exact else None, preferred_element_type=jnp.float32,
    )


def halves(value):
    high_part = value.astype(jnp.bfloat16)
    low_part = (value - high_part.astype(jnp.float32)).astype(jnp.bfloat16)
    return high_part, low_part


def blocks_per_step(nblocks, most):
    return max(size for size in range(1, most + 1) if nblocks % size == 0)


def gram_kernel(levels, right_ref, left_ref, gram_ref):
    @pl.when(pl.program_id(0) == 0)
    def _():
        gram_ref[...] = jnp.zeros_like(gram_ref)

    right = jnp.concatenate([right_ref[l] for l in range(1, levels)], axis=1)
    left = jnp.concatenate([left_ref[l] for l in range(levels - 1)], axis=1)
    gram_ref[...] += dot(right, left, (0, 0))


def project_kernel(levels, per_step, width, order_ref, inv_ref, right_ref, rhs_ref,
                   moved_ref, out_ref, factor_ref, total_ref):
    step = pl.program_id(0)
    rank = right_ref.shape[2]
    kinds = levels * rank
    place = lax.broadcasted_iota(jnp.int32, (width, width), 0)
    for b in range(per_step):
        order = order_ref[pl.ds(step * per_step + b, 1), :]
        chosen = (place == order).astype(jnp.float32).astype(jnp.bfloat16)
        moved = dot(inv_ref[b], chosen, (1, 1)).astype(jnp.bfloat16)
        moved_ref[b] = moved
        rows = pl.ds(b * width, width)
        right = jnp.concatenate([right_ref[l, rows, :] for l in range(levels)], axis=1)
        high_part, low_part = halves(dot(right, moved, (0, 0)))
        factor_ref[:kinds, rows] = high_part
        factor_ref[kinds:, rows] = low_part
    term = dot(factor_ref[...], rhs_ref[...], (1, 0))

    @pl.when(step == 0)
    def _():
        total_ref[...] = term

    @pl.when(step > 0)
    def _():
        total_ref[...] += term

    @pl.when(step == pl.num_programs(0) - 1)
    def _():
        out_ref[...] = (total_ref[:kinds] + total_ref[kinds:]).T


def picker(perm_ref, level, rank):
    spot = lax.broadcasted_iota(jnp.int32, (rank, rank), 0)
    return (spot == perm_ref[level:level + 1, :]).astype(jnp.float32)


def node_kernel(levels, parts_ref, gram_ref, joined_ref, perm_ref, coef_ref, rest_ref):
    count, share, _ = parts_ref.shape
    rank = perm_ref.shape[1]
    half = count // 2
    low_sum = sum(parts_ref[s] for s in range(half))
    high_sum = sum(parts_ref[s] for s in range(half, count))
    own = jnp.concatenate([low_sum[:, :rank], high_sum[:, :rank]], axis=0)
    picked = dot(own, picker(perm_ref, 0, rank), (1, 0), True)
    picked = jnp.concatenate([picked[:share], picked[share:]], axis=1)
    coef = dot(picked, joined_ref[...], (1, 1), True)
    rest = low_sum[:, rank:] + high_sum[:, rank:]
    size = (levels - 1) * rank
    for side in range(2):
        part = coef[:, side * rank:(side + 1) * rank]
        coef_ref[side] = part
        gram = gram_ref[:, side, :, :rank].reshape(size, rank)
        rest = rest - dot(part, gram, (1, 1), True)
    rest_ref[...] = rest


def tree_kernel(levels, rest_ref, gram_ref, coef_ref, joined_ref, perm_ref, leaf_ref, out_ref):
    leaves, share, _ = rest_ref.shape
    count = out_ref.shape[0]
    rank = perm_ref.shape[1]
    leaf = leaf_ref[0]
    own = []
    found = {}
    for level in range(1, levels):
        span = 2 ** (level - 1)
        children = leaves // span
        totals = []
        for child in range(children):
            total = 0.0
            for member in range(child * span, (child + 1) * span):
                total = total + rest_ref[member, :, (level - 1) * rank:level * rank]
                for below in range(1, level):
                    gram = gram_ref[member, (level - 2) * rank:(level - 1) * rank,
                                    (below - 1) * rank:below * rank]
                    total = total - dot(found[below, member // 2 ** (below - 1)], gram, (1, 1), True)
            totals.append(total)
        picked = dot(jnp.concatenate(totals, axis=0), picker(perm_ref, level, rank), (1, 0), True)
        offset = 2 * leaves - 2 * leaves // 2 ** level
        chosen = jnp.zeros((share, rank), jnp.float32)
        for node in range(children // 2):
            pair = jnp.concatenate(
                [picked[(2 * node + side) * share:(2 * node + side + 1) * share] for side in range(2)],
                axis=1)
            coef = dot(pair, joined_ref[offset + node], (1, 1), True)
            for side in range(2):
                part = coef[:, side * rank:(side + 1) * rank]
                found[level, 2 * node + side] = part
                chosen = jnp.where(leaf // span == 2 * node + side, part, chosen)
        own.append(chosen)
    for target in range(count):
        out_ref[target] = jnp.concatenate([coef_ref[target // (count // 2)]] + own, axis=1)


def expand_kernel(levels, per_step, width, coef_ref, moved_ref, rhs_ref, left_ref, out_ref, factor_ref):
    kinds = coef_ref.shape[1]

    @pl.when(pl.program_id(0) == 0)
    def _():
        high_part, low_part = halves(coef_ref[...].T)
        factor_ref[:kinds, :] = high_part
        factor_ref[kinds:, :] = low_part

    for b in range(per_step):
        rows = pl.ds(b * width, width)
        left = jnp.concatenate([left_ref[l, rows, :] for l in range(levels)] * 2, axis=1)
        out_ref[rows, :] = dot(moved_ref[b], rhs_ref[rows, :], (1, 0)) - dot(left, factor_ref[...], (1, 0))


def whole(shape):
    return pl.BlockSpec(shape, lambda *_: (0,) * len(shape))


def params(mib):
    return pltpu.CompilerParams(vmem_limit_bytes=mib * MIB)


def per_device(rhs, leaf_order, leaf_inv, right_basis, left_basis, rank_perm, joined):
    levels, rows, rank = right_basis.shape
    nblocks, width, _ = leaf_inv.shape
    columns = rhs.shape[1]
    leaves = lax.axis_size("leaf")
    count = lax.axis_size("rows")
    leaf = lax.axis_index("leaf")
    kinds = levels * rank
    size = kinds - rank
    share = columns // count

    per_step = blocks_per_step(nblocks, 6)
    steps = nblocks // per_step
    tile = per_step * width
    gram = pl.pallas_call(
        functools.partial(gram_kernel, levels),
        grid=(steps,),
        in_specs=[pl.BlockSpec((levels, tile, rank), lambda i: (0, i, 0))] * 2,
        out_specs=whole((size, size)),
        out_shape=jax.ShapeDtypeStruct((size, size), jnp.float32),
        compiler_params=params(32),
        name="gram",
    )(right_basis, left_basis)

    per_step = blocks_per_step(nblocks, 3)
    steps = nblocks // per_step
    tile = per_step * width
    moved, partial_value = pl.pallas_call(
        functools.partial(project_kernel, levels, per_step, width),
        grid=(steps,),
        in_specs=[
            whole((nblocks, width)),
            pl.BlockSpec((per_step, width, width), lambda i: (i, 0, 0)),
            pl.BlockSpec((levels, tile, rank), lambda i: (0, i, 0)),
            pl.BlockSpec((tile, columns), lambda i: (i, 0)),
        ],
        out_specs=[
            pl.BlockSpec((per_step, width, width), lambda i: (i, 0, 0)),
            whole((columns, kinds)),
        ],
        out_shape=[
            jax.ShapeDtypeStruct((nblocks, width, width), jnp.bfloat16),
            jax.ShapeDtypeStruct((columns, kinds), jnp.float32),
        ],
        scratch_shapes=[
            pltpu.VMEM((2 * kinds, tile), jnp.bfloat16),
            pltpu.VMEM((2 * kinds, columns), jnp.float32),
        ],
        compiler_params=params(32),
        name="project",
    )(leaf_order, leaf_inv, right_basis, rhs)

    gram_rows = size // count
    gram_parts = lax.all_to_all(gram, "rows", 0, 0, tiled=True).reshape(2, count // 2, gram_rows, size)
    gram_all = lax.all_gather(gram_parts.sum(1), "rows", axis=0)
    deeper = size - rank
    gram_leaf = (gram_all[:, 0] + gram_all[:, 1]).reshape(size, size)[rank:, rank:]
    gram_leaves = lax.all_gather(gram_leaf, "leaf", axis=0)

    parts = lax.all_to_all(partial_value, "rows", 0, 0, tiled=True).reshape(count, share, kinds)
    coef, rest = pl.pallas_call(
        functools.partial(node_kernel, levels),
        out_shape=[
            jax.ShapeDtypeStruct((2, share, rank), jnp.float32),
            jax.ShapeDtypeStruct((share, size), jnp.float32),
        ],
        compiler_params=params(16),
        name="node",
    )(parts, gram_all, lax.dynamic_index_in_dim(joined, leaf, 0, keepdims=False), rank_perm)

    rest_all = lax.all_gather(rest, "leaf", axis=0)
    coef_out = pl.pallas_call(
        functools.partial(tree_kernel, levels),
        in_specs=[pl.BlockSpec()] * 5 + [pl.BlockSpec(memory_space=pltpu.SMEM)],
        out_shape=jax.ShapeDtypeStruct((count, share, kinds), jnp.float32),
        compiler_params=params(24),
        name="tree",
    )(rest_all, gram_leaves, coef, joined, rank_perm, leaf.reshape(1).astype(jnp.int32))
    coef_all = lax.all_to_all(coef_out, "rows", 0, 0, tiled=True).reshape(columns, kinds)

    return pl.pallas_call(
        functools.partial(expand_kernel, levels, per_step, width),
        grid=(steps,),
        in_specs=[
            whole((columns, kinds)),
            pl.BlockSpec((per_step, width, width), lambda i: (i, 0, 0)),
            pl.BlockSpec((tile, columns), lambda i: (i, 0)),
            pl.BlockSpec((levels, tile, rank), lambda i: (0, i, 0)),
        ],
        out_specs=pl.BlockSpec((tile, columns), lambda i: (i, 0)),
        out_shape=jax.ShapeDtypeStruct((rows, columns), jnp.float32),
        scratch_shapes=[pltpu.VMEM((2 * kinds, columns), jnp.bfloat16)],
        compiler_params=params(32),
        name="expand",
    )(coef_all, moved, rhs, left_basis)


def solution(mesh):
    return jax.shard_map(
        per_device,
        mesh=mesh,
        in_specs=(
            P(("leaf", "rows"), None),
            P(("leaf", "rows"), None),
            P(("leaf", "rows"), None, None),
            P(None, ("leaf", "rows"), None),
            P(None, ("leaf", "rows"), None),
            P(),
            P(),
        ),
        out_specs=P(("leaf", "rows"), None),
        check_vma=False,
    )
```

time: 313 us -> 115 us (0.37)
  local copies, waits for them, and re-layouts: 111 us -> 21 us
  waiting for transfers between devices: 86.7 us -> 0.01 us
  matrix products: 66 us -> 0 us
  blocking collectives: 18.5 us -> 59.3 us
  Pallas kernels: 0 us -> 23 us
  between operations: 13.6 us -> 0.1 us
  other arithmetic: 4.52 us -> 1.01 us
    gather x5 -> x0, local copies, waits for them, and re-layouts: 87 us -> none  [the longest x2 84.9 us: per_device(): ordered = jnp.take_along_axis(blocks, leaf_order[:, :, None], axis=1)]
    dot_general x16 -> x0, matrix products: 66 us -> none  [the longest x3 20.4 us: expand(): jnp.dot(basis_rows, low_part, preferred_element_type=jnp.float32)]
    unnamed x3 -> x0, waiting for transfers between devices: 34.8 us -> none
    reduce_scatter x1 -> x0, waiting for transfers between devices: 33.7 us -> none  [per_device(): lax.psum_scatter(partial_value, 'rows', scatter_dimension=1, tiled=True)]
    all_gather x2 -> x3, blocking collectives: 18.5 us -> 44.3 us  [the longest x1 15.2 us: per_device(): gram_leaves = lax.all_gather(gram_leaf, 'leaf', axis=0)]
    pallas_call x0 -> x5, Pallas kernels: none -> 23 us  [the longest x1 9.01 us: per_device(): pl.pallas_call(functools.partial(project_kernel, levels, per_step, width)...]
    ppermute x6 -> x0, waiting for transfers between devices: 18.1 us -> none  [partner(): return lax.ppermute(block, axis, route)]
    unnamed x15 -> x36, local copies, waits for them, and re-layouts: 4.2 us -> 19.3 us
  transfers between devices with their start and end apart: 8 -> 2, of which waited for: 8 -> 0; matrix products, arithmetic and copies ran while one was open for 3% -> 2% of each run, Pallas kernels for 0% -> 8%
where the time goes in v1:
time: 115 us; the launch traced here: 114 us
  blocking collectives  59.3 us (52%)
  Pallas kernels  23 us (20%)
  local copies, waits for them, and re-layouts  21 us (18%)
  starting transfers between devices  9.53 us (8%)
    unnamed x36, local copies, waits for them, and re-layouts  19.3 us
    all_gather x1, blocking collectives, per_device(): gram_leaves = lax.all_gather(gram_leaf, 'leaf', axis=0)  15.2 us
    all_to_all x1, blocking collectives, per_device(): lax.all_to_all(coef_out, 'rows', 0, 0, tiled=True).reshape(columns, kinds)  15.1 us
    all_gather x1, blocking collectives, per_device(): rest_all = lax.all_gather(rest, 'leaf', axis=0)  14.7 us
    all_gather x1, blocking collectives, per_device(): gram_all = lax.all_gather(gram_parts.sum(1), 'rows', axis=0)  14.3 us
    pallas_call x1, Pallas kernels, per_device(): pl.pallas_call(functools.partial(project_kernel, levels, per_step, width)...  9.01 us
    pallas_call x1, Pallas kernels, per_device(): pl.pallas_call(functools.partial(expand_kernel, levels, per_step, width),...  7.84 us
    all_to_all x1, starting transfers between devices, per_device(): lax.all_to_all(gram, 'rows', 0, 0, tiled=True)  5.18 us
  transfers between devices with their start and end apart: 2, of which 0 were waited for; matrix products, arithmetic and copies ran while one was open for 2% of the time, Pallas kernels for 8%

profile of v1, /device:TPU:0, one launch (start us, length us, event | category | flops | bytes accessed | tf_op | source)
XLA Modules:
  0.0 114.0 jit_solution(14949538395476605987)
XLA Ops:
  0.0 0.0 copy-start.2
  0.0 2.0 %copy-done.2 = bf16[3,4608,128]{2,1,0:T(8,128)(2,1)S(1)} copy-done((bf16[3,4608,128]{2,1,0:T(8,128)(2,1)S(1)}, bf16[3,4608,128]{2,1,0:T(8,128)(2,1)}, u32[]{:S(2)}) %copy-start.2) | copy-done | bytes 3538968
  2.0 0.0 copy-start.4
  2.0 2.0 %copy-done.4 = bf16[3,4608,128]{2,1,0:T(8,128)(2,1)S(1)} copy-done((bf16[3,4608,128]{2,1,0:T(8,128)(2,1)S(1)}, bf16[3,4608,128]{2,1,0:T(8,128)(2,1)}, u32[]{:S(2)}) %copy-start.4) | copy-done | bytes 3538968
  4.0 0.0 copy-start.3
  4.0 1.8 %gram.1 = f32[256,256]{1,0:T(8,128)S(1)} custom-call(bf16[3,4608,128]{2,1,0:T(8,128)(2,1)S(1)} %copy-done.2, bf16[3,4608,128]{2,1,0:T(8,128)(2,1)S(1)} %copy-done.4), custom_call_target="tpu_custom_call" | custom-call | tf_op jit(solution)/shard_map/gram/pallas_call | solution.py:171
  5.8 0.0 copy-start.13
  5.8 0.7 copy-done.13
  6.5 5.2 %all-to-all-start.1 = ((f32[8,32,256]{2,1,0:T(8,128)}), f32[8,32,256]{2,1,0:T(8,128)}, u32[]{:S(2)}, u32[]{:S(2)}) async-start(f32[8,32,256]{2,1,0:T(8,128)} %bitcast.17), calls=%async_computation.1 | async-start | bytes 524288 | tf_op jit(solution)/shard_map/all_to_all | solution.py:210
  11.7 0.0 copy-done.3
  11.7 0.0 copy-start
  11.7 2.3 %copy-done = bf16[4608,512]{1,0:T(8,128)(2,1)S(1)} copy-done((bf16[4608,512]{1,0:T(8,128)(2,1)S(1)}, bf16[4608,512]{1,0:T(8,128)(2,1)}, u32[]{:S(2)}) %copy-start) | copy-done | bytes 4718616
  14.0 0.0 copy-start.11
  14.0 1.7 %copy-done.11 = bf16[18,256,256]{2,1,0:T(8,128)(2,1)S(1)} copy-done((bf16[18,256,256]{2,1,0:T(8,128)(2,1)S(1)}, bf16[18,256,256]{2,1,0:T(8,128)(2,1)}, u32[]{:S(2)}) %copy-start.11) | copy-done | bytes 2359320
  15.7 0.0 copy-start.16
  15.7 0.7 copy-done.16
  16.4 9.0 %project.1 = (bf16[18,256,256]{2,1,0:T(8,128)(2,1)S(1)}, f32[512,384]{1,0:T(8,128)S(1)}) custom-call(s32[18,256]{1,0:T(8,128)S(1)} %copy-done.16, bf16[18,256,256]{2,1,0:T(8,128)(2,1)S(1)} %copy-done.11, bf16[3,4608,128]{2,1,0:T(8,128)(2,1)S(1)} %copy-done.3, bf16[4608,512]{1,0:T(8,128)(2,1)S(1)} %copy-done), custom_call_target="tpu_custom_call" | custom-call | tf_op jit(solution)/shard_map/project/pallas_call | solution.py:184
  25.4 0.0 copy-start.9
  25.5 1.4 %copy-done.9 = bf16[18,256,256]{2,1,0:T(8,128)(2,1)} copy-done((bf16[18,256,256]{2,1,0:T(8,128)(2,1)}, bf16[18,256,256]{2,1,0:T(8,128)(2,1)S(1)}, u32[]{:S(2)}) %copy-start.9) | copy-done | bytes 2359320
  26.9 0.0 copy-start.15
  26.9 0.9 copy-done.15
  27.8 0.0 copy-start.17
  27.8 0.0 all-to-all-done.1
  27.8 4.4 %all-to-all-start = ((f32[8,64,384]{2,1,0:T(8,128)}), f32[8,64,384]{2,1,0:T(8,128)}, u32[]{:S(2)}, u32[]{:S(2)}) async-start(f32[8,64,384]{2,1,0:T(8,128)} %bitcast.18), calls=%async_computation | async-start | bytes 1572864 | tf_op jit(solution)/shard_map/all_to_all | solution.py:216
  32.1 1.7 %dynamic-slice_bitcast_fusion.joined_ref = f32[256,256]{1,0:T(8,128)} fusion(f32[7,256,256]{2,1,0:T(8,128)} %joined_ref.1, s32[]{:T(128)S(6)} %select_n.4), kind=kLoop, calls=%fused_computation.2 | loop fusion | bytes 524292 | tf_op jit(solution)/shard_map/jit(dynamic_index_in_dim)/squeeze | solution.py:225
  33.8 1.0 bitcast_reduce_fusion
  34.8 14.3 %all-gather = f32[16,32,256]{2,1,0:T(8,128)S(1)} all-gather(f32[2,32,256]{2,1,0:T(8,128)S(1)} %bitcast_reduce_fusion), channel_id=2, replica_groups=mesh['leaf'=4,'rows'=8] {'rows'}, dimensions={0}, use_global_device_ids=true | all-gather | bytes 589824 | tf_op jit(solution)/shard_map/all_gather | solution.py:211
  49.1 0.0 copy-start.6
  49.1 0.8 copy-done.6
  49.9 0.0 copy-start.5
  49.9 15.2 %all-gather.2 = f32[512,128]{1,0:T(8,128)} all-gather(f32[128,128]{1,0:T(8,128)S(1)} %slice.14), channel_id=4, replica_groups=mesh['leaf'=4,'rows'=8] {'leaf'}, dimensions={0}, use_global_device_ids=true | all-gather | bytes 327680 | tf_op jit(solution)/shard_map/all_gather | solution.py:214
  65.2 0.0 all-to-all-done.parts_ref
  65.2 0.0 copy-done.17
  65.2 0.0 copy-start.7
  65.2 1.0 copy-done.7
  66.2 0.0 copy-start.14
  66.2 0.9 copy-done.14
  67.2 2.3 %node.1 = (f32[2,64,128]{2,1,0:T(8,128)S(1)}, f32[64,256]{1,0:T(8,128)S(1)}) custom-call(f32[8,64,384]{2,1,0:T(8,128)} %all-to-all-done.parts_ref, f32[8,2,32,256]{3,2,1,0:T(8,128)S(1)} %bitcast.13, f32[256,256]{1,0:T(8,128)S(1)} %copy-done.14, s32[3,128]{1,0:T(4,128)S(1)} %copy-done.17), custom_call_target="tpu_custom_call" | custom-call | tf_op jit(solution)/shard_map/node/pallas_call | solution.py:217
  69.5 14.7 %all-gather.1 = f32[256,256]{1,0:T(8,128)S(1)} all-gather(f32[64,256]{1,0:T(8,128)S(1)} %get-tuple-element.10), channel_id=3, replica_groups=mesh['leaf'=4,'rows'=8] {'leaf'}, dimensions={0}, use_global_device_ids=true | all-gather | bytes 327680 | tf_op jit(solution)/shard_map/all_gather | solution.py:227
  84.2 0.0 copy-start.8
  84.2 1.5 %copy-done.8 = f32[7,256,256]{2,1,0:T(8,128)S(1)} copy-done((f32[7,256,256]{2,1,0:T(8,128)S(1)}, f32[7,256,256]{2,1,0:T(8,128)}, u32[]{:S(2)}) %copy-start.8) | copy-done | bytes 1835032
  85.7 0.0 copy-start.12
  85.7 0.9 copy-done.12
  86.7 0.0 copy-start.10
  86.7 2.1 %tree.1 = f32[8,64,384]{2,1,0:T(8,128)S(1)} custom-call(f32[4,64,256]{2,1,0:T(8,128)S(1)} %bitcast.16, f32[4,128,128]{2,1,0:T(8,128)S(1)} %bitcast.15, f32[2,64,128]{2,1,0:T(8,128)S(1)} %get-tuple-element.11.coef_ref, f32[7,256,256]{2,1,0:T(8,128)S(1)} %copy-done.8, s32[3,128]{1,0:T(4,128)S(1)} %copy-done.17, s32[1]{0:T(128)} %bitcast.8.leaf_ref), custom_call_target="tpu_custom_call" | custom-call | tf_op jit(solution)/shard_map/tree/pallas_call | solution.py:228
  88.7 15.1 %all_to_all.23 = f32[8,64,384]{2,1,0:T(8,128)S(1)} all-to-all(f32[8,64,384]{2,1,0:T(8,128)S(1)} %tree.1), channel_id=1, replica_groups=mesh['leaf'=4,'rows'=8] {'rows'}, dimensions={0} | all-to-all | bytes 1572864 | tf_op jit(solution)/shard_map/all_to_all | solution.py:235
  103.8 0.0 copy-done.5
  103.8 0.0 copy-done.10
  103.8 0.0 copy-start.1
  103.8 2.3 %copy-done.1 = bf16[4608,512]{1,0:T(8,128)(2,1)S(1)} copy-done((bf16[4608,512]{1,0:T(8,128)(2,1)S(1)}, bf16[4608,512]{1,0:T(8,128)(2,1)}, u32[]{:S(2)}) %copy-start.1) | copy-done | bytes 4718616
  106.2 7.8 %expand.1 = f32[4608,512]{1,0:T(8,128)} custom-call(f32[512,384]{1,0:T(8,128)S(1)} %bitcast.14, bf16[18,256,256]{2,1,0:T(8,128)(2,1)S(1)} %copy-done.10, bf16[4608,512]{1,0:T(8,128)(2,1)S(1)} %copy-done.1, bf16[3,4608,128]{2,1,0:T(8,128)(2,1)S(1)} %copy-done.5), custom_call_target="tpu_custom_call" | custom-call | tf_op jit(solution)/shard_map/expand/pallas_call | solution.py:237
  (2 shorter events, 0.0 us)
Async XLA Ops:
  0.0 2.0 %copy-start.2 = (bf16[3,4608,128]{2,1,0:T(8,128)(2,1)S(1)}, bf16[3,4608,128]{2,1,0:T(8,128)(2,1)}, u32[]{:S(2)}) copy-start(bf16[3,4608,128]{2,1,0:T(8,128)(2,1)} %right_ref.3) | copy-start | bytes 10616836
  2.0 2.0 %copy-start.4 = (bf16[3,4608,128]{2,1,0:T(8,128)(2,1)S(1)}, bf16[3,4608,128]{2,1,0:T(8,128)(2,1)}, u32[]{:S(2)}) copy-start(bf16[3,4608,128]{2,1,0:T(8,128)(2,1)} %left_ref.3) | copy-start | bytes 10616836
  4.0 7.7 %copy-start.3 = (bf16[3,4608,128]{2,1,0:T(8,128)(2,1)S(1)}, bf16[3,4608,128]{2,1,0:T(8,128)(2,1)}, u32[]{:S(2)}) copy-start(bf16[3,4608,128]{2,1,0:T(8,128)(2,1)} %right_ref.3) | copy-start | bytes 10616836
  5.8 0.7 copy-start.13
  6.5 21.3 %all-to-all-start.1 = ((f32[8,32,256]{2,1,0:T(8,128)}), f32[8,32,256]{2,1,0:T(8,128)}, u32[]{:S(2)}, u32[]{:S(2)}) async-start(f32[8,32,256]{2,1,0:T(8,128)} %bitcast.17), calls=%async_computation.1 | async-start | bytes 524288 | tf_op jit(solution)/shard_map/all_to_all | solution.py:210
  11.7 2.3 %copy-start = (bf16[4608,512]{1,0:T(8,128)(2,1)S(1)}, bf16[4608,512]{1,0:T(8,128)(2,1)}, u32[]{:S(2)}) copy-start(bf16[4608,512]{1,0:T(8,128)(2,1)} %rhs_ref.3) | copy-start | bytes 14155780
  14.0 1.7 %copy-start.11 = (bf16[18,256,256]{2,1,0:T(8,128)(2,1)S(1)}, bf16[18,256,256]{2,1,0:T(8,128)(2,1)}, u32[]{:S(2)}) copy-start(bf16[18,256,256]{2,1,0:T(8,128)(2,1)} %inv_ref.1) | copy-start | bytes 7077892
  15.7 0.7 copy-start.16
  25.4 1.4 %copy-start.9 = (bf16[18,256,256]{2,1,0:T(8,128)(2,1)}, bf16[18,256,256]{2,1,0:T(8,128)(2,1)S(1)}, u32[]{:S(2)}) copy-start(bf16[18,256,256]{2,1,0:T(8,128)(2,1)S(1)} %get-tuple-element.12.moved_ref) | copy-start | bytes 7077892
  26.9 0.9 copy-start.15
  27.8 37.4 %copy-start.17 = (s32[3,128]{1,0:T(4,128)S(1)}, s32[3,128]{1,0:T(4,128)}, u32[]{:S(2)}) copy-start(s32[3,128]{1,0:T(4,128)} %perm_ref.3) | copy-start | bytes 4612
  27.8 37.4 %all-to-all-start = ((f32[8,64,384]{2,1,0:T(8,128)}), f32[8,64,384]{2,1,0:T(8,128)}, u32[]{:S(2)}, u32[]{:S(2)}) async-start(f32[8,64,384]{2,1,0:T(8,128)} %bitcast.18), calls=%async_computation | async-start | bytes 1572864 | tf_op jit(solution)/shard_map/all_to_all | solution.py:216
  49.1 0.8 copy-start.6
  49.9 53.9 %copy-start.5 = (bf16[3,4608,128]{2,1,0:T(8,128)(2,1)S(1)}, bf16[3,4608,128]{2,1,0:T(8,128)(2,1)}, u32[]{:S(2)}) copy-start(bf16[3,4608,128]{2,1,0:T(8,128)(2,1)} %left_ref.3) | copy-start | bytes 10616836
  65.2 1.0 copy-start.7
  66.2 0.9 copy-start.14
  84.2 1.5 %copy-start.8 = (f32[7,256,256]{2,1,0:T(8,128)S(1)}, f32[7,256,256]{2,1,0:T(8,128)}, u32[]{:S(2)}) copy-start(f32[7,256,256]{2,1,0:T(8,128)} %joined_ref.1) | copy-start | bytes 5505028
  85.7 0.9 copy-start.12
  86.7 17.2 %copy-start.10 = (bf16[18,256,256]{2,1,0:T(8,128)(2,1)S(1)}, bf16[18,256,256]{2,1,0:T(8,128)(2,1)}, u32[]{:S(2)}) copy-start(bf16[18,256,256]{2,1,0:T(8,128)(2,1)} %copy-done.9) | copy-start | bytes 7077892
  103.8 2.3 %copy-start.1 = (bf16[4608,512]{1,0:T(8,128)(2,1)S(1)}, bf16[4608,512]{1,0:T(8,128)(2,1)}, u32[]{:S(2)}) copy-start(bf16[4608,512]{1,0:T(8,128)(2,1)} %rhs_ref.3) | copy-start | bytes 14155780

commit v2 on v1

v2 whole, which is shorter than its diff:
```python
import functools

import jax
import jax.numpy as jnp
from jax import lax
from jax.experimental import pallas as pl
from jax.experimental.pallas import tpu as pltpu
from jax.sharding import PartitionSpec as P

HIGHEST = lax.Precision.HIGHEST
MIB = 1 << 20
BOTH = ("leaf", "rows")


def dot(a, b, contract, exact=False):
    return lax.dot_general(
        a, b, ((contract[:1], contract[1:]), ((), ())),
        precision=HIGHEST if exact else None, preferred_element_type=jnp.float32,
    )


def halves(value):
    high_part = value.astype(jnp.bfloat16)
    low_part = (value - high_part.astype(jnp.float32)).astype(jnp.bfloat16)
    return high_part, low_part


def swap(value, axis, mask):
    count = lax.axis_size(axis)
    return lax.ppermute(value, axis, [(i, i ^ mask) for i in range(count)])


def blocks_per_step(nblocks, most):
    return max(size for size in range(1, most + 1) if nblocks % size == 0)


def below_pairs(levels, first=0):
    return [(level, below) for level in range(levels) for below in range(first, level)]


def gram_kernel(levels, right_ref, left_ref, keep_ref, send_ref, gram_ref):
    step = pl.program_id(0)
    rank = right_ref.shape[2]
    half = rank // 2

    @pl.when(step == 0)
    def _():
        gram_ref[...] = jnp.zeros_like(gram_ref)

    right = jnp.concatenate([right_ref[l] for l in range(1, levels)], axis=1)
    left = jnp.concatenate([left_ref[l] for l in range(levels - 1)], axis=1)
    gram_ref[...] += dot(right, left, (0, 0))

    @pl.when(step == pl.num_programs(0) - 1)
    def _():
        core = lax.axis_index("rows") % 2
        for spot, (level, below) in enumerate(below_pairs(levels)):
            lanes = pl.ds(spot * rank, rank)
            for ref, side in ((keep_ref, core), (send_ref, 1 - core)):
                rows = pl.ds(pl.multiple_of((level - 1) * rank + side * half, half), half)
                ref[:, lanes] = gram_ref[rows, pl.ds(below * rank, rank)]


def project_kernel(levels, per_step, width, order_ref, inv_ref, right_ref, rhs_ref,
                   moved_ref, keep_ref, send_ref, factor_ref, total_ref, flip_ref):
    step = pl.program_id(0)
    rank = right_ref.shape[2]
    kinds = levels * rank
    place = lax.broadcasted_iota(jnp.int32, (width, width), 0)
    for b in range(per_step):
        order = order_ref[pl.ds(step * per_step + b, 1), :]
        chosen = (place == order).astype(jnp.float32).astype(jnp.bfloat16)
        moved = dot(inv_ref[b], chosen, (1, 1)).astype(jnp.bfloat16)
        moved_ref[b] = moved
        rows = pl.ds(b * width, width)
        right = jnp.concatenate([right_ref[l, rows, :] for l in range(levels)], axis=1)
        high_part, low_part = halves(dot(right, moved, (0, 0)))
        factor_ref[:kinds, rows] = high_part
        factor_ref[kinds:, rows] = low_part
    term = dot(factor_ref[...], rhs_ref[...], (1, 0))

    @pl.when(step == 0)
    def _():
        total_ref[...] = term

    @pl.when(step > 0)
    def _():
        total_ref[...] += term

    @pl.when(step == pl.num_programs(0) - 1)
    def _():
        flip_ref[...] = (total_ref[:kinds] + total_ref[kinds:]).T
        me = lax.axis_index("rows")
        slots, share, _ = keep_ref.shape
        for slot in range(slots):
            for ref, owner in ((keep_ref, me ^ (2 * slot)), (send_ref, me ^ (2 * slot + 1))):
                ref[slot] = flip_ref[pl.ds(pl.multiple_of(owner * share, share), share), :]


def merge_kernel(keep_ref, got_ref, *out_refs):
    for slot, out_ref in enumerate(out_refs):
        out_ref[...] = keep_ref[slot] + got_ref[slot]


def prepare_kernel(index_ref, joined_ref, perm_ref, out_ref):
    rank = perm_ref.shape[1]
    spot = lax.broadcasted_iota(jnp.int32, (rank, rank), 0)
    chosen = (spot == perm_ref[pl.ds(pl.program_id(0), 1), :]).astype(jnp.float32)
    for side in range(2):
        lanes = pl.ds(side * rank, rank)
        out_ref[0, :, lanes] = dot(joined_ref[0, :, lanes], chosen, (1, 1), True)


def by_side(side, own, other):
    return jnp.where(side == 0, own, other), jnp.where(side == 0, other, own)


def pack_message(message_ref, pieces):
    row = 0
    for piece in pieces:
        message_ref[pl.ds(row, piece.shape[0]), :] = piece
        row += piece.shape[0]


def node_kernel(levels, rank, slots, *refs):
    part_refs = refs[:slots]
    gram_refs = refs[slots:slots + 4]
    joined_ref, own_ref, other_ref, message_ref = refs[slots + 4:]
    me = lax.axis_index("rows")
    core, side = me % 2, me // slots
    half = slots // 2
    sums = [sum(ref[...] for ref in part_refs[:half]), sum(ref[...] for ref in part_refs[half:])]
    picked = jnp.concatenate(by_side(side, sums[0][:, :rank], sums[1][:, :rank]), axis=1)
    coef = dot(picked, joined_ref[0], (1, 1), True)
    sides = by_side(side, coef[:, :rank], coef[:, rank:])
    own_ref[...] = sides[0]
    other_ref[...] = sides[1]
    mine, theirs, pair_mine, pair_theirs = (ref[...] for ref in gram_refs)
    grams = [jnp.concatenate(by_side(core, mine, pair_mine), axis=0),
             jnp.concatenate(by_side(core, theirs, pair_theirs), axis=0)]
    rest = sums[0] + sums[1]
    pairs = below_pairs(levels)
    spots = [spot for spot, (_, below) in enumerate(pairs) if below == 0]
    pieces = []
    for level in range(1, levels):
        value = rest[:, level * rank:(level + 1) * rank]
        lanes = slice(spots[level - 1] * rank, (spots[level - 1] + 1) * rank)
        for part, gram in zip(sides, grams):
            value = value - dot(part, gram[:, lanes], (1, 1), True)
        pieces.append(value)
    for spot, (_, below) in enumerate(pairs):
        if below > 0:
            lanes = slice(spot * rank, (spot + 1) * rank)
            pieces.append(grams[0][:, lanes] + grams[1][:, lanes])
    pack_message(message_ref, pieces)


def level_kernel(levels, level, share, sent_ref, got_ref, joined_ref, coef_ref, *message_ref):
    rank = sent_ref.shape[1]
    side = lax.axis_index("leaf") // 2 ** (level - 1) % 2
    more = levels - level
    values = []
    for ref in (sent_ref, got_ref):
        values.append([ref[pl.ds(i * share, share), :] for i in range(more)])
    picked = jnp.concatenate(by_side(side, values[0][0], values[1][0]), axis=1)
    coef = dot(picked, joined_ref[level], (1, 1), True)
    sides = by_side(side, coef[:, :rank], coef[:, rank:])
    coef_ref[...] = sides[0]
    if not message_ref:
        return
    pairs = below_pairs(levels, level)
    grams = []
    for ref in (sent_ref, got_ref):
        grams.append({pair: ref[pl.ds(more * share + spot * rank, rank), :] for spot, pair in enumerate(pairs)})
    pieces = []
    for upper in range(level + 1, levels):
        value = values[0][upper - level] + values[1][upper - level]
        for part, gram in zip(sides, grams):
            value = value - dot(part, gram[upper, level], (1, 1), True)
        pieces.append(value)
    for pair in pairs:
        if pair[1] > level:
            pieces.append(grams[0][pair] + grams[1][pair])
    pack_message(message_ref[0], pieces)


def pack_kernel(*refs):
    levels = len(refs) - 3
    other_ref, own_refs, own_out, other_out = refs[0], refs[1:-2], refs[-2], refs[-1]
    own = [ref[...] for ref in own_refs]
    own_out[...] = jnp.concatenate(own, axis=1)
    other_out[...] = jnp.concatenate([other_ref[...]] + own[1:], axis=1)


def expand_kernel(levels, per_step, width, slots, *refs):
    piece_refs = refs[:2 * slots]
    moved_ref, rhs_ref, left_ref, out_ref, flip_ref, factor_ref = refs[2 * slots:]
    share, kinds = piece_refs[0].shape

    @pl.when(pl.program_id(0) == 0)
    def _():
        me = lax.axis_index("rows")
        for slot in range(2 * slots):
            owner = me ^ slot
            flip_ref[pl.ds(pl.multiple_of(owner * share, share), share), :] = piece_refs[slot][...]
        high_part, low_part = halves(flip_ref[...].T)
        factor_ref[:kinds, :] = high_part
        factor_ref[kinds:, :] = low_part

    for b in range(per_step):
        rows = pl.ds(b * width, width)
        left = jnp.concatenate([left_ref[l, rows, :] for l in range(levels)] * 2, axis=1)
        out_ref[rows, :] = dot(moved_ref[b], rhs_ref[rows, :], (1, 0)) - dot(left, factor_ref[...], (1, 0))


def whole(shape):
    return pl.BlockSpec(shape, lambda *_: (0,) * len(shape))


def params(mib):
    return pltpu.CompilerParams(vmem_limit_bytes=mib * MIB)


def floats(*shape):
    return jax.ShapeDtypeStruct(shape, jnp.float32)


def per_device(rhs, leaf_order, leaf_inv, right_basis, left_basis, rank_perm, joined):
    levels, rows, rank = right_basis.shape
    nblocks, width, _ = leaf_inv.shape
    columns = rhs.shape[1]
    leaves = lax.axis_size("leaf")
    count = lax.axis_size("rows")
    leaf = lax.axis_index("leaf")
    slots = count // 2
    kinds = levels * rank
    size = kinds - rank
    share = columns // count
    gram_lanes = len(below_pairs(levels)) * rank

    per_step = blocks_per_step(nblocks, 6)
    steps = nblocks // per_step
    tile = per_step * width
    gram_keep, gram_send = pl.pallas_call(
        functools.partial(gram_kernel, levels),
        grid=(steps,),
        in_specs=[pl.BlockSpec((levels, tile, rank), lambda i: (0, i, 0))] * 2,
        out_specs=[whole((rank // 2, gram_lanes))] * 2,
        out_shape=[floats(rank // 2, gram_lanes)] * 2,
        scratch_shapes=[pltpu.VMEM((size, size), jnp.float32)],
        compiler_params=params(56),
        name="gram",
    )(right_basis, left_basis)

    gram_got = swap(gram_send, "rows", 1)

    per_step = blocks_per_step(nblocks, 3)
    steps = nblocks // per_step
    tile = per_step * width
    moved, keep, send = pl.pallas_call(
        functools.partial(project_kernel, levels, per_step, width),
        grid=(steps,),
        in_specs=[
            whole((nblocks, width)),
            pl.BlockSpec((per_step, width, width), lambda i: (i, 0, 0)),
            pl.BlockSpec((levels, tile, rank), lambda i: (0, i, 0)),
            pl.BlockSpec((tile, columns), lambda i: (i, 0)),
        ],
        out_specs=[pl.BlockSpec((per_step, width, width), lambda i: (i, 0, 0))]
        + [whole((slots, share, kinds))] * 2,
        out_shape=[jax.ShapeDtypeStruct((nblocks, width, width), jnp.bfloat16)]
        + [floats(slots, share, kinds)] * 2,
        scratch_shapes=[
            pltpu.VMEM((2 * kinds, tile), jnp.bfloat16),
            pltpu.VMEM((2 * kinds, columns), jnp.float32),
            pltpu.VMEM((columns, kinds), jnp.float32),
        ],
        compiler_params=params(56),
        name="project",
    )(leaf_order, leaf_inv, right_basis, rhs)

    got = swap(send, "rows", 1)
    merged = pl.pallas_call(
        merge_kernel, out_shape=[floats(share, kinds)] * slots, compiler_params=params(8), name="merge",
    )(keep, got)
    parts = [merged[0]] + [swap(merged[s], "rows", 2 * s) for s in range(1, slots)]

    gram = gram_keep + gram_got
    mask = 2
    while mask < slots:
        gram = gram + swap(gram, "rows", mask)
        mask *= 2
    gram_other = swap(gram, "rows", slots)
    grams = [gram, gram_other, swap(gram, "rows", 1), swap(gram_other, "rows", 1)]

    index = jnp.stack([2 * leaves - 2 * leaves // 2 ** l + leaf // 2 ** l for l in range(levels)])
    prepared = pl.pallas_call(
        prepare_kernel,
        grid_spec=pltpu.PrefetchScalarGridSpec(
            num_scalar_prefetch=1,
            grid=(levels,),
            in_specs=[
                pl.BlockSpec((1, 2 * rank, 2 * rank), lambda i, index: (index[i], 0, 0)),
                pl.BlockSpec((levels, rank), lambda i, index: (0, 0)),
            ],
            out_specs=pl.BlockSpec((1, 2 * rank, 2 * rank), lambda i, index: (i, 0, 0)),
        ),
        out_shape=floats(levels, 2 * rank, 2 * rank),
        compiler_params=params(8),
        name="prepare",
    )(index.astype(jnp.int32), joined, rank_perm)

    def message_shape(level):
        return floats((levels - level) * share + len(below_pairs(levels, level)) * rank, rank)

    own, other, message = pl.pallas_call(
        functools.partial(node_kernel, levels, rank, slots),
        out_shape=[floats(share, rank)] * 2 + [message_shape(1)],
        compiler_params=params(8),
        name="node",
    )(*parts, *grams, prepared)
    coefs = [own]
    for level in range(1, levels):
        last = level + 1 == levels
        arrived = swap(message, "leaf", 2 ** (level - 1))
        outs = pl.pallas_call(
            functools.partial(level_kernel, levels, level, share),
            out_shape=[floats(share, rank)] + ([] if last else [message_shape(level + 1)]),
            compiler_params=params(8),
            name=f"level{level}",
        )(message, arrived, prepared)
        coefs.append(outs[0])
        message = outs[-1]
    own_pack, other_pack = pl.pallas_call(
        pack_kernel, out_shape=[floats(share, kinds)] * 2, compiler_params=params(8), name="pack",
    )(other, *coefs)

    pieces = []
    for slot in range(slots):
        piece = own_pack if slot < slots // 2 else other_pack
        piece = swap(piece, "rows", 2 * slot) if slot > 0 else piece
        pieces += [piece, swap(piece, "rows", 1)]

    return pl.pallas_call(
        functools.partial(expand_kernel, levels, per_step, width, slots),
        grid=(steps,),
        in_specs=[whole((share, kinds))] * count + [
            pl.BlockSpec((per_step, width, width), lambda i: (i, 0, 0)),
            pl.BlockSpec((tile, columns), lambda i: (i, 0)),
            pl.BlockSpec((levels, tile, rank), lambda i: (0, i, 0)),
        ],
        out_specs=pl.BlockSpec((tile, columns), lambda i: (i, 0)),
        out_shape=floats(rows, columns),
        scratch_shapes=[
            pltpu.VMEM((columns, kinds), jnp.float32),
            pltpu.VMEM((2 * kinds, columns), jnp.bfloat16),
        ],
        compiler_params=params(24),
        name="expand",
    )(*pieces, moved, rhs, left_basis)


def solution(mesh):
    return jax.shard_map(
        per_device,
        mesh=mesh,
        in_specs=(
            P(("leaf", "rows"), None),
            P(("leaf", "rows"), None),
            P(("leaf", "rows"), None, None),
            P(None, ("leaf", "rows"), None),
            P(None, ("leaf", "rows"), None),
            P(),
            P(),
        ),
        out_specs=P(("leaf", "rows"), None),
        check_vma=False,
    )
```

time: 115 us -> 73.2 us (0.64)
  blocking collectives: 59.3 us -> 0 us
  waiting for transfers between devices: 0.01 us -> 20.8 us
  local copies, waits for them, and re-layouts: 21 us -> 2.51 us
  Pallas kernels: 23 us -> 31.3 us
  starting transfers between devices: 9.53 us -> 16.4 us
    all_gather x3 -> x0, blocking collectives: 44.3 us -> none  [the longest x1 15.2 us: per_device(): gram_leaves = lax.all_gather(gram_leaf, 'leaf', axis=0)]
    ppermute x0 -> x18, waiting for transfers between devices: none -> 20.8 us  [swap(): return lax.ppermute(value, axis, [(i, i ^ mask) for i in range(count)])]
    unnamed x36 -> x12, local copies, waits for them, and re-layouts: 19.3 us -> 2.51 us
    ppermute x0 -> x18, starting transfers between devices: none -> 16.4 us  [swap(): return lax.ppermute(value, axis, [(i, i ^ mask) for i in range(count)])]
    all_to_all x1 -> x0, blocking collectives: 15.1 us -> none  [per_device(): lax.all_to_all(coef_out, 'rows', 0, 0, tiled=True).reshape(columns, kinds)]
    all_to_all x2 -> x0, starting transfers between devices: 9.53 us -> none  [the longest x1 5.18 us: per_device(): lax.all_to_all(gram, 'rows', 0, 0, tiled=True)]
    pallas_call x1, Pallas kernels: 1.8 us -> 5.21 us  [per_device(): pl.pallas_call(functools.partial(gram_kernel, levels), grid=(steps,), in_...]
    pallas_call x1, Pallas kernels: 9.01 us -> 11.6 us  [per_device(): pl.pallas_call(functools.partial(project_kernel, levels, per_step, width)...]
  transfers between devices with their start and end apart: 2 -> 18, of which waited for: 0 -> 12; matrix products, arithmetic and copies ran while one was open for 2% -> 2% of each run, Pallas kernels for 8% -> 11%
where the time goes in v2:
time: 73.2 us; the launch traced here: 72.8 us
  Pallas kernels  31.3 us (43%)
  waiting for transfers between devices  20.8 us (28%)
  starting transfers between devices  16.4 us (22%)
  local copies, waits for them, and re-layouts  2.51 us (3%)
  other arithmetic  1.62 us (2%)
    ppermute x18, waiting for transfers between devices, swap(): return lax.ppermute(value, axis, [(i, i ^ mask) for i in range(count)])  20.8 us
    ppermute x18, starting transfers between devices, swap(): return lax.ppermute(value, axis, [(i, i ^ mask) for i in range(count)])  16.4 us
    pallas_call x1, Pallas kernels, per_device(): pl.pallas_call(functools.partial(project_kernel, levels, per_step, width)...  11.6 us
    pallas_call x1, Pallas kernels, per_device(): pl.pallas_call(functools.partial(expand_kernel, levels, per_step, width,...  7.95 us
    pallas_call x1, Pallas kernels, per_device(): pl.pallas_call(functools.partial(gram_kernel, levels), grid=(steps,), in_...  5.21 us
    unnamed x12, local copies, waits for them, and re-layouts  2.51 us
    pallas_call x1, Pallas kernels, per_device(): pl.pallas_call(functools.partial(node_kernel, levels, rank, slots), out_s...  2.22 us
    pallas_call x1, Pallas kernels, per_device(): pl.pallas_call(prepare_kernel, grid_spec=pltpu.PrefetchScalarGridSpec(num...  1.7 us
  transfers between devices with their start and end apart: 18, of which 12 were waited for; matrix products, arithmetic and copies ran while one was open for 2% of the time, Pallas kernels for 11%

profile of v2, /device:TPU:0, one launch (start us, length us, event | category | flops | bytes accessed | tf_op | source)
XLA Modules:
  0.0 72.8 jit_solution(1776279097027765028)
XLA Ops:
  0.0 11.6 %project.1 = (bf16[18,256,256]{2,1,0:T(8,128)(2,1)}, f32[4,64,384]{2,1,0:T(8,128)}, f32[4,64,384]{2,1,0:T(8,128)}) custom-call(s32[18,256]{1,0:T(8,128)} %order_ref.1, bf16[18,256,256]{2,1,0:T(8,128)(2,1)} %inv_ref.1, bf16[3,4608,128]{2,1,0:T(8,128)(2,1)} %right_ref.3, bf16[4608,512]{1,0:T(8,128)(2,1)} %refs_9_.1), custom_call_target="tpu_custom_call" | custom-call | tf_op jit(solution)/shard_map/project/pallas_call | solution.py:260
  11.6 0.0 copy-start.5
  11.6 0.5 collective-permute-start
  12.2 0.0 copy-start.1
  12.2 5.2 %gram.1 = (f32[64,384]{1,0:T(8,128)}, f32[64,384]{1,0:T(8,128)}) custom-call(bf16[3,4608,128]{2,1,0:T(8,128)(2,1)} %right_ref.3, bf16[3,4608,128]{2,1,0:T(8,128)(2,1)} %refs_10_.1), custom_call_target="tpu_custom_call" | custom-call | tf_op jit(solution)/shard_map/gram/pallas_call | solution.py:244
  17.4 0.0 collective-permute-start.4
  17.4 1.5 %collective-permute-done.4 = f32[64,384]{1,0:T(8,128)S(1)} collective-permute-done((f32[64,384]{1,0:T(8,128)}, f32[64,384]{1,0:T(8,128)S(1)}, u32[]{:S(2)}, u32[]{:S(2)}) %collective-permute-start.4) | collective-permute-done | bytes 98336 | tf_op jit(solution)/shard_map/ppermute | solution.py:30
  18.9 0.9 %add.12 = f32[64,384]{1,0:T(8,128)S(1)} add(f32[64,384]{1,0:T(8,128)} %get-tuple-element.27, f32[64,384]{1,0:T(8,128)S(1)} %collective-permute-done.4) | non-fusion elementwise | flops 24576 | bytes 294912 | tf_op jit(solution)/shard_map/add | solution.py:288
  19.8 2.7 %collective-permute-start.5 = (f32[64,384]{1,0:T(8,128)S(1)}, f32[64,384]{1,0:T(8,128)S(1)}, u32[]{:S(2)}, u32[]{:S(2)}) collective-permute-start(f32[64,384]{1,0:T(8,128)S(1)} %add.12), channel_id=1, source_target_pairs={{0,2},{1,3},{2,0},{3,1},{4,6},{5,7},{6,4},{7,5},{8,10},{9,11},{10,... | collective-permute-start | bytes 294920 | tf_op jit(solution)/shard_map/ppermute | solution.py:30
  22.5 3.3 %collective-permute-done.5 = f32[64,384]{1,0:T(8,128)S(1)} collective-permute-done((f32[64,384]{1,0:T(8,128)S(1)}, f32[64,384]{1,0:T(8,128)S(1)}, u32[]{:S(2)}, u32[]{:S(2)}) %collective-permute-start.5) | collective-permute-done | bytes 98336 | tf_op jit(solution)/shard_map/ppermute | solution.py:30
  25.8 0.6 add.13.refs_4_
  26.5 1.8 %collective-permute-start.6 = (f32[64,384]{1,0:T(8,128)}, f32[64,384]{1,0:T(8,128)}, u32[]{:S(2)}, u32[]{:S(2)}) collective-permute-start(f32[64,384]{1,0:T(8,128)} %add.13.refs_4_), channel_id=1, source_target_pairs={{0,4},{1,5},{2,6},{3,7},{4,0},{5,1},{6,2},{7,3},{8,12},{9,13},{10,... | collective-permute-start | bytes 294920 | tf_op jit(solution)/shard_map/ppermute | solution.py:30
  28.2 0.0 collective-permute-start.7
  28.2 3.2 %collective-permute-done.6.refs_5_ = f32[64,384]{1,0:T(8,128)} collective-permute-done((f32[64,384]{1,0:T(8,128)}, f32[64,384]{1,0:T(8,128)}, u32[]{:S(2)}, u32[]{:S(2)}) %collective-permute-start.6) | collective-permute-done | bytes 98336 | tf_op jit(solution)/shard_map/ppermute | solution.py:30
  31.4 0.0 collective-permute-start.8
  31.4 0.0 collective-permute-done.got_ref
  31.4 0.0 copy-start.4
  31.4 1.0 %copy-done.4 = f32[4,64,384]{2,1,0:T(8,128)S(1)} copy-done((f32[4,64,384]{2,1,0:T(8,128)S(1)}, f32[4,64,384]{2,1,0:T(8,128)}, u32[]{:S(2)}) %copy-start.4) | copy-done | bytes 393240
  32.4 0.0 copy-start
  32.4 0.0 copy-start.2
  32.4 1.2 %merge.1 = (f32[64,384]{1,0:T(8,128)S(1)}, f32[64,384]{1,0:T(8,128)S(1)}, f32[64,384]{1,0:T(8,128)S(1)}, f32[64,384]{1,0:T(8,128)S(1)}) custom-call(f32[4,64,384]{2,1,0:T(8,128)S(1)} %copy-done.4, f32[4,64,384]{2,1,0:T(8,128)} %collective-permute-done.got_ref), custom_call_target="tpu_custom_call" | custom-call | tf_op jit(solution)/shard_map/merge/pallas_call | solution.py:283
  33.6 1.8 %collective-permute-start.1 = (f32[64,384]{1,0:T(8,128)S(1)}, f32[64,384]{1,0:T(8,128)S(1)}, u32[]{:S(2)}, u32[]{:S(2)}) collective-permute-start(f32[64,384]{1,0:T(8,128)S(1)} %get-tuple-element.24), channel_id=1, source_target_pairs={{0,2},{1,3},{2,0},{3,1},{4,6},{5,7},{6,4},{7,5},{8,10},{9,11},{10,... | collective-permute-start | bytes 294920 | tf_op jit(solution)/shard_map/ppermute | solution.py:30
  35.4 1.5 %collective-permute-start.2 = (f32[64,384]{1,0:T(8,128)S(1)}, f32[64,384]{1,0:T(8,128)S(1)}, u32[]{:S(2)}, u32[]{:S(2)}) collective-permute-start(f32[64,384]{1,0:T(8,128)S(1)} %get-tuple-element.25), channel_id=1, source_target_pairs={{0,4},{1,5},{2,6},{3,7},{4,0},{5,1},{6,2},{7,3},{8,12},{9,13},{10,... | collective-permute-start | bytes 294920 | tf_op jit(solution)/shard_map/ppermute | solution.py:30
  36.9 0.2 collective-permute-start.3
  37.1 0.1 pad_add_fusion.index_ref
  37.2 0.0 copy-done.5
  37.2 0.0 copy-start.3
  37.2 1.5 %copy-done.3 = f32[7,256,256]{2,1,0:T(8,128)S(1)} copy-done((f32[7,256,256]{2,1,0:T(8,128)S(1)}, f32[7,256,256]{2,1,0:T(8,128)}, u32[]{:S(2)}) %copy-start.3) | copy-done | bytes 1835032
  38.7 1.7 %prepare.1.refs_8_.joined_ref = f32[3,256,256]{2,1,0:T(8,128)S(1)} custom-call(s32[3]{0:T(128)S(1)} %pad_add_fusion.index_ref, f32[7,256,256]{2,1,0:T(8,128)S(1)} %copy-done.3, s32[3,128]{1,0:T(4,128)S(1)} %copy-done.5), custom_call_target="tpu_custom_call" | custom-call | tf_op jit(solution)/shard_map/prepare/pallas_call | solution.py:297
  40.4 0.0 collective-permute-done.7.refs_6_
  40.4 0.0 collective-permute-done.8.refs_7_
  40.5 0.0 collective-permute-done.1.refs_1_
  40.5 1.0 %collective-permute-done.2.refs_2_ = f32[64,384]{1,0:T(8,128)S(1)} collective-permute-done((f32[64,384]{1,0:T(8,128)S(1)}, f32[64,384]{1,0:T(8,128)S(1)}, u32[]{:S(2)}, u32[]{:S(2)}) %collective-permute-start.2) | collective-permute-done | bytes 98336 | tf_op jit(solution)/shard_map/ppermute | solution.py:30
  41.5 1.0 %collective-permute-done.3.refs_3_ = f32[64,384]{1,0:T(8,128)S(1)} collective-permute-done((f32[64,384]{1,0:T(8,128)S(1)}, f32[64,384]{1,0:T(8,128)S(1)}, u32[]{:S(2)}, u32[]{:S(2)}) %collective-permute-start.3) | collective-permute-done | bytes 98336 | tf_op jit(solution)/shard_map/ppermute | solution.py:30
  42.5 2.2 %node.1 = (f32[64,128]{1,0:T(8,128)S(1)}, f32[64,128]{1,0:T(8,128)S(1)}, f32[256,128]{1,0:T(8,128)S(1)}) custom-call(f32[64,384]{1,0:T(8,128)S(1)} %get-tuple-element.23.refs_0_, f32[64,384]{1,0:T(8,128)S(1)} %collective-permute-done.1.refs_1_, f32[64,384]{1,0:T(8,128)S(1)} %collective-permute-done.2.refs_2_, f32[64,384]{1,0:T(8,128)S(1)} %collective-permute-done.3.refs_3_, ...), custom_call_target="tpu_custom_call" | custom-call | tf_op jit(solution)/shard_map/node/pallas_call | solution.py:316
  44.7 1.6 %collective-permute-start.9 = (f32[256,128]{1,0:T(8,128)S(1)}, f32[256,128]{1,0:T(8,128)S(1)}, u32[]{:S(2)}, u32[]{:S(2)}) collective-permute-start(f32[256,128]{1,0:T(8,128)S(1)} %get-tuple-element.31.sent_ref), channel_id=1, source_target_pairs={{0,8},{8,0},{16,24},{24,16},{1,9},{9,1},{17,25},{25,17},{2,10},{10... | collective-permute-start | bytes 393224 | tf_op jit(solution)/shard_map/ppermute | solution.py:30
  46.3 3.4 %collective-permute-done.9.got_ref = f32[256,128]{1,0:T(8,128)S(1)} collective-permute-done((f32[256,128]{1,0:T(8,128)S(1)}, f32[256,128]{1,0:T(8,128)S(1)}, u32[]{:S(2)}, u32[]{:S(2)}) %collective-permute-start.9) | collective-permute-done | bytes 131104 | tf_op jit(solution)/shard_map/ppermute | solution.py:30
  49.7 1.0 %level1.1 = (f32[64,128]{1,0:T(8,128)S(1)}, f32[64,128]{1,0:T(8,128)S(1)}) custom-call(f32[256,128]{1,0:T(8,128)S(1)} %get-tuple-element.31.sent_ref, f32[256,128]{1,0:T(8,128)S(1)} %collective-permute-done.9.got_ref, f32[3,256,256]{2,1,0:T(8,128)S(1)} %prepare.1.refs_8_.joined_ref), custom_call_target="tpu_custom_call" | custom-call | tf_op jit(solution)/shard_map/level1/pallas_call | solution.py:326
  50.7 2.6 %collective-permute-start.10 = (f32[64,128]{1,0:T(8,128)S(1)}, f32[64,128]{1,0:T(8,128)S(1)}, u32[]{:S(2)}, u32[]{:S(2)}) collective-permute-start(f32[64,128]{1,0:T(8,128)S(1)} %get-tuple-element.33.sent_ref), channel_id=1, source_target_pairs={{0,16},{8,24},{16,0},{24,8},{1,17},{9,25},{17,1},{25,9},{2,18},{10... | collective-permute-start | bytes 98312 | tf_op jit(solution)/shard_map/ppermute | solution.py:30
  53.4 2.2 %collective-permute-done.10.got_ref = f32[64,128]{1,0:T(8,128)S(1)} collective-permute-done((f32[64,128]{1,0:T(8,128)S(1)}, f32[64,128]{1,0:T(8,128)S(1)}, u32[]{:S(2)}, u32[]{:S(2)}) %collective-permute-start.10) | collective-permute-done | bytes 32800 | tf_op jit(solution)/shard_map/ppermute | solution.py:30
  55.6 0.4 level2.1.refs_3_
  56.0 1.5 %collective-permute-start.16 = (f32[64,384]{1,0:T(8,128)S(1)}, f32[64,384]{1,0:T(8,128)S(1)}, u32[]{:S(2)}, u32[]{:S(2)}) collective-permute-start(f32[64,384]{1,0:T(8,128)S(1)} %get-tuple-element.35), channel_id=1, source_target_pairs={{0,6},{1,7},{2,4},{3,5},{4,2},{5,3},{6,0},{7,1},{8,14},{9,15},{10,... | collective-permute-start | bytes 294920 | tf_op jit(solution)/shard_map/ppermute | solution.py:30
  57.5 1.4 %collective-permute-start.14 = (f32[64,384]{1,0:T(8,128)S(1)}, f32[64,384]{1,0:T(8,128)S(1)}, u32[]{:S(2)}, u32[]{:S(2)}) collective-permute-start(f32[64,384]{1,0:T(8,128)S(1)} %get-tuple-element.35), channel_id=1, source_target_pairs={{0,4},{1,5},{2,6},{3,7},{4,0},{5,1},{6,2},{7,3},{8,12},{9,13},{10,... | collective-permute-start | bytes 294920 | tf_op jit(solution)/shard_map/ppermute | solution.py:30
  58.9 0.7 collective-permute-start.12
  59.6 0.0 collective-permute-start.11
  59.6 2.1 %collective-permute-done.16.refs_6_ = f32[64,384]{1,0:T(8,128)S(1)} collective-permute-done((f32[64,384]{1,0:T(8,128)S(1)}, f32[64,384]{1,0:T(8,128)S(1)}, u32[]{:S(2)}, u32[]{:S(2)}) %collective-permute-start.16) | collective-permute-done | bytes 98336 | tf_op jit(solution)/shard_map/ppermute | solution.py:30
  61.6 0.0 collective-permute-start.17
  61.6 1.0 %collective-permute-done.14.refs_4_ = f32[64,384]{1,0:T(8,128)S(1)} collective-permute-done((f32[64,384]{1,0:T(8,128)S(1)}, f32[64,384]{1,0:T(8,128)S(1)}, u32[]{:S(2)}, u32[]{:S(2)}) %collective-permute-start.14) | collective-permute-done | bytes 98336 | tf_op jit(solution)/shard_map/ppermute | solution.py:30
  62.6 0.0 collective-permute-start.15
  62.6 0.9 %collective-permute-done.12.refs_2_ = f32[64,384]{1,0:T(8,128)S(1)} collective-permute-done((f32[64,384]{1,0:T(8,128)S(1)}, f32[64,384]{1,0:T(8,128)S(1)}, u32[]{:S(2)}, u32[]{:S(2)}) %collective-permute-start.12) | collective-permute-done | bytes 98336 | tf_op jit(solution)/shard_map/ppermute | solution.py:30
  63.5 0.0 collective-permute-start.13
  63.5 0.0 collective-permute-done.11.refs_1_
  63.5 0.0 collective-permute-done.17.refs_7_
  63.5 0.4 collective-permute-done.15.refs_5_
  63.9 0.9 %collective-permute-done.13.refs_3_ = f32[64,384]{1,0:T(8,128)S(1)} collective-permute-done((f32[64,384]{1,0:T(8,128)S(1)}, f32[64,384]{1,0:T(8,128)S(1)}, u32[]{:S(2)}, u32[]{:S(2)}) %collective-permute-start.13) | collective-permute-done | bytes 98336 | tf_op jit(solution)/shard_map/ppermute | solution.py:30
  64.8 0.0 copy-done.1
  64.8 0.0 copy-done
  64.8 0.0 copy-done.2
  64.8 7.9 %expand.1 = f32[4608,512]{1,0:T(8,128)} custom-call(f32[64,384]{1,0:T(8,128)S(1)} %get-tuple-element.34.refs_0_, f32[64,384]{1,0:T(8,128)S(1)} %collective-permute-done.11.refs_1_, f32[64,384]{1,0:T(8,128)S(1)} %collective-permute-done.12.refs_2_, f32[64,384]{1,0:T(8,128)S(1)} %collective-permute-done.13.refs_3_, ...), custom_call_target="tpu_custom_call" | custom-call | tf_op jit(solution)/shard_map/expand/pallas_call | solution.py:344
  (1 shorter events, 0.0 us)
Async XLA Ops:
  11.6 25.6 %copy-start.5 = (s32[3,128]{1,0:T(4,128)S(1)}, s32[3,128]{1,0:T(4,128)}, u32[]{:S(2)}) copy-start(s32[3,128]{1,0:T(4,128)} %perm_ref.1) | copy-start | bytes 4612
  11.6 19.8 %collective-permute-start = (f32[4,64,384]{2,1,0:T(8,128)}, f32[4,64,384]{2,1,0:T(8,128)}, u32[]{:S(2)}, u32[]{:S(2)}) collective-permute-start(f32[4,64,384]{2,1,0:T(8,128)} %get-tuple-element.22), channel_id=1, source_target_pairs={{0,1},{1,0},{2,3},{3,2},{4,5},{5,4},{6,7},{7,6},{8,9},{9,8},{10,11... | collective-permute-start | bytes 1179656 | tf_op jit(solution)/shard_map/ppermute | solution.py:30
  12.2 52.6 %copy-start.1 = (bf16[3,4608,128]{2,1,0:T(8,128)(2,1)S(1)}, bf16[3,4608,128]{2,1,0:T(8,128)(2,1)}, u32[]{:S(2)}) copy-start(bf16[3,4608,128]{2,1,0:T(8,128)(2,1)} %refs_10_.1) | copy-start | bytes 10616836
  17.4 1.5 %collective-permute-start.4 = (f32[64,384]{1,0:T(8,128)}, f32[64,384]{1,0:T(8,128)S(1)}, u32[]{:S(2)}, u32[]{:S(2)}) collective-permute-start(f32[64,384]{1,0:T(8,128)} %get-tuple-element.28), channel_id=1, source_target_pairs={{0,1},{1,0},{2,3},{3,2},{4,5},{5,4},{6,7},{7,6},{8,9},{9,8},{10,11... | collective-permute-start | bytes 294920 | tf_op jit(solution)/shard_map/ppermute | solution.py:30
  19.8 6.0 %collective-permute-start.5 = (f32[64,384]{1,0:T(8,128)S(1)}, f32[64,384]{1,0:T(8,128)S(1)}, u32[]{:S(2)}, u32[]{:S(2)}) collective-permute-start(f32[64,384]{1,0:T(8,128)S(1)} %add.12), channel_id=1, source_target_pairs={{0,2},{1,3},{2,0},{3,1},{4,6},{5,7},{6,4},{7,5},{8,10},{9,11},{10,... | collective-permute-start | bytes 294920 | tf_op jit(solution)/shard_map/ppermute | solution.py:30
  26.5 4.9 %collective-permute-start.6 = (f32[64,384]{1,0:T(8,128)}, f32[64,384]{1,0:T(8,128)}, u32[]{:S(2)}, u32[]{:S(2)}) collective-permute-start(f32[64,384]{1,0:T(8,128)} %add.13.refs_4_), channel_id=1, source_target_pairs={{0,4},{1,5},{2,6},{3,7},{4,0},{5,1},{6,2},{7,3},{8,12},{9,13},{10,... | collective-permute-start | bytes 294920 | tf_op jit(solution)/shard_map/ppermute | solution.py:30
  28.2 12.2 %collective-permute-start.7 = (f32[64,384]{1,0:T(8,128)}, f32[64,384]{1,0:T(8,128)S(1)}, u32[]{:S(2)}, u32[]{:S(2)}) collective-permute-start(f32[64,384]{1,0:T(8,128)} %add.13.refs_4_), channel_id=1, source_target_pairs={{0,1},{1,0},{2,3},{3,2},{4,5},{5,4},{6,7},{7,6},{8,9},{9,8},{10,11... | collective-permute-start | bytes 294920 | tf_op jit(solution)/shard_map/ppermute | solution.py:30
  31.4 9.1 %collective-permute-start.8 = (f32[64,384]{1,0:T(8,128)}, f32[64,384]{1,0:T(8,128)S(1)}, u32[]{:S(2)}, u32[]{:S(2)}) collective-permute-start(f32[64,384]{1,0:T(8,128)} %collective-permute-done.6.refs_5_), channel_id=1, source_target_pairs={{0,1},{1,0},{2,3},{3,2},{4,5},{5,4},{6,7},{7,6},{8,9},{9,8},{10,11... | collective-permute-start | bytes 294920 | tf_op jit(solution)/shard_map/ppermute | solution.py:30
  31.4 1.0 %copy-start.4 = (f32[4,64,384]{2,1,0:T(8,128)S(1)}, f32[4,64,384]{2,1,0:T(8,128)}, u32[]{:S(2)}) copy-start(f32[4,64,384]{2,1,0:T(8,128)} %get-tuple-element.21.keep_ref) | copy-start | bytes 1179652
  32.4 32.4 %copy-start = (bf16[4608,512]{1,0:T(8,128)(2,1)S(1)}, bf16[4608,512]{1,0:T(8,128)(2,1)}, u32[]{:S(2)}) copy-start(bf16[4608,512]{1,0:T(8,128)(2,1)} %refs_9_.1) | copy-start | bytes 14155780
  32.4 32.4 %copy-start.2 = (bf16[18,256,256]{2,1,0:T(8,128)(2,1)S(1)}, bf16[18,256,256]{2,1,0:T(8,128)(2,1)}, u32[]{:S(2)}) copy-start(bf16[18,256,256]{2,1,0:T(8,128)(2,1)} %get-tuple-element.36.refs_8_) | copy-start | bytes 7077892
  33.6 6.9 %collective-permute-start.1 = (f32[64,384]{1,0:T(8,128)S(1)}, f32[64,384]{1,0:T(8,128)S(1)}, u32[]{:S(2)}, u32[]{:S(2)}) collective-permute-start(f32[64,384]{1,0:T(8,128)S(1)} %get-tuple-element.24), channel_id=1, source_target_pairs={{0,2},{1,3},{2,0},{3,1},{4,6},{5,7},{6,4},{7,5},{8,10},{9,11},{10,... | collective-permute-start | bytes 294920 | tf_op jit(solution)/shard_map/ppermute | solution.py:30
  35.4 6.1 %collective-permute-start.2 = (f32[64,384]{1,0:T(8,128)S(1)}, f32[64,384]{1,0:T(8,128)S(1)}, u32[]{:S(2)}, u32[]{:S(2)}) collective-permute-start(f32[64,384]{1,0:T(8,128)S(1)} %get-tuple-element.25), channel_id=1, source_target_pairs={{0,4},{1,5},{2,6},{3,7},{4,0},{5,1},{6,2},{7,3},{8,12},{9,13},{10,... | collective-permute-start | bytes 294920 | tf_op jit(solution)/shard_map/ppermute | solution.py:30
  36.9 5.5 %collective-permute-start.3 = (f32[64,384]{1,0:T(8,128)S(1)}, f32[64,384]{1,0:T(8,128)S(1)}, u32[]{:S(2)}, u32[]{:S(2)}) collective-permute-start(f32[64,384]{1,0:T(8,128)S(1)} %get-tuple-element.26), channel_id=1, source_target_pairs={{0,6},{1,7},{2,4},{3,5},{4,2},{5,3},{6,0},{7,1},{8,14},{9,15},{10,... | collective-permute-start | bytes 294920 | tf_op jit(solution)/shard_map/ppermute | solution.py:30
  37.2 1.5 %copy-start.3 = (f32[7,256,256]{2,1,0:T(8,128)S(1)}, f32[7,256,256]{2,1,0:T(8,128)}, u32[]{:S(2)}) copy-start(f32[7,256,256]{2,1,0:T(8,128)} %joined_ref.1) | copy-start | bytes 5505028
  44.7 5.0 %collective-permute-start.9 = (f32[256,128]{1,0:T(8,128)S(1)}, f32[256,128]{1,0:T(8,128)S(1)}, u32[]{:S(2)}, u32[]{:S(2)}) collective-permute-start(f32[256,128]{1,0:T(8,128)S(1)} %get-tuple-element.31.sent_ref), channel_id=1, source_target_pairs={{0,8},{8,0},{16,24},{24,16},{1,9},{9,1},{17,25},{25,17},{2,10},{10... | collective-permute-start | bytes 393224 | tf_op jit(solution)/shard_map/ppermute | solution.py:30
  50.7 4.9 %collective-permute-start.10 = (f32[64,128]{1,0:T(8,128)S(1)}, f32[64,128]{1,0:T(8,128)S(1)}, u32[]{:S(2)}, u32[]{:S(2)}) collective-permute-start(f32[64,128]{1,0:T(8,128)S(1)} %get-tuple-element.33.sent_ref), channel_id=1, source_target_pairs={{0,16},{8,24},{16,0},{24,8},{1,17},{9,25},{17,1},{25,9},{2,18},{10... | collective-permute-start | bytes 98312 | tf_op jit(solution)/shard_map/ppermute | solution.py:30
  56.0 5.6 %collective-permute-start.16 = (f32[64,384]{1,0:T(8,128)S(1)}, f32[64,384]{1,0:T(8,128)S(1)}, u32[]{:S(2)}, u32[]{:S(2)}) collective-permute-start(f32[64,384]{1,0:T(8,128)S(1)} %get-tuple-element.35), channel_id=1, source_target_pairs={{0,6},{1,7},{2,4},{3,5},{4,2},{5,3},{6,0},{7,1},{8,14},{9,15},{10,... | collective-permute-start | bytes 294920 | tf_op jit(solution)/shard_map/ppermute | solution.py:30
  57.5 5.1 %collective-permute-start.14 = (f32[64,384]{1,0:T(8,128)S(1)}, f32[64,384]{1,0:T(8,128)S(1)}, u32[]{:S(2)}, u32[]{:S(2)}) collective-permute-start(f32[64,384]{1,0:T(8,128)S(1)} %get-tuple-element.35), channel_id=1, source_target_pairs={{0,4},{1,5},{2,6},{3,7},{4,0},{5,1},{6,2},{7,3},{8,12},{9,13},{10,... | collective-permute-start | bytes 294920 | tf_op jit(solution)/shard_map/ppermute | solution.py:30
  58.9 4.6 %collective-permute-start.12 = (f32[64,384]{1,0:T(8,128)S(1)}, f32[64,384]{1,0:T(8,128)S(1)}, u32[]{:S(2)}, u32[]{:S(2)}) collective-permute-start(f32[64,384]{1,0:T(8,128)S(1)} %get-tuple-element.34.refs_0_), channel_id=1, source_target_pairs={{0,2},{1,3},{2,0},{3,1},{4,6},{5,7},{6,4},{7,5},{8,10},{9,11},{10,... | collective-permute-start | bytes 294920 | tf_op jit(solution)/shard_map/ppermute | solution.py:30
  59.6 4.0 %collective-permute-start.11 = (f32[64,384]{1,0:T(8,128)S(1)}, f32[64,384]{1,0:T(8,128)S(1)}, u32[]{:S(2)}, u32[]{:S(2)}) collective-permute-start(f32[64,384]{1,0:T(8,128)S(1)} %get-tuple-element.34.refs_0_), channel_id=1, source_target_pairs={{0,1},{1,0},{2,3},{3,2},{4,5},{5,4},{6,7},{7,6},{8,9},{9,8},{10,11... | collective-permute-start | bytes 294920 | tf_op jit(solution)/shard_map/ppermute | solution.py:30
  61.6 1.9 %collective-permute-start.17 = (f32[64,384]{1,0:T(8,128)S(1)}, f32[64,384]{1,0:T(8,128)S(1)}, u32[]{:S(2)}, u32[]{:S(2)}) collective-permute-start(f32[64,384]{1,0:T(8,128)S(1)} %collective-permute-done.16.refs_6_), channel_id=1, source_target_pairs={{0,1},{1,0},{2,3},{3,2},{4,5},{5,4},{6,7},{7,6},{8,9},{9,8},{10,11... | collective-permute-start | bytes 294920 | tf_op jit(solution)/shard_map/ppermute | solution.py:30
  62.6 1.3 %collective-permute-start.15 = (f32[64,384]{1,0:T(8,128)S(1)}, f32[64,384]{1,0:T(8,128)S(1)}, u32[]{:S(2)}, u32[]{:S(2)}) collective-permute-start(f32[64,384]{1,0:T(8,128)S(1)} %collective-permute-done.14.refs_4_), channel_id=1, source_target_pairs={{0,1},{1,0},{2,3},{3,2},{4,5},{5,4},{6,7},{7,6},{8,9},{9,8},{10,11... | collective-permute-start | bytes 294920 | tf_op jit(solution)/shard_map/ppermute | solution.py:30
  63.5 1.3 %collective-permute-start.13 = (f32[64,384]{1,0:T(8,128)S(1)}, f32[64,384]{1,0:T(8,128)S(1)}, u32[]{:S(2)}, u32[]{:S(2)}) collective-permute-start(f32[64,384]{1,0:T(8,128)S(1)} %collective-permute-done.12.refs_2_), channel_id=1, source_target_pairs={{0,1},{1,0},{2,3},{3,2},{4,5},{5,4},{6,7},{7,6},{8,9},{9,8},{10,11... | collective-permute-start | bytes 294920 | tf_op jit(solution)/shard_map/ppermute | solution.py:30

commit v3 on v2

--- a/solution.py
+++ b/solution.py
@@ -38,63 +38,69 @@
     return [(level, below) for level in range(levels) for below in range(first, level)]
 
 
-def gram_kernel(levels, right_ref, left_ref, keep_ref, send_ref, gram_ref):
-    step = pl.program_id(0)
-    rank = right_ref.shape[2]
-    half = rank // 2
-
-    @pl.when(step == 0)
-    def _():
-        gram_ref[...] = jnp.zeros_like(gram_ref)
-
-    right = jnp.concatenate([right_ref[l] for l in range(1, levels)], axis=1)
-    left = jnp.concatenate([left_ref[l] for l in range(levels - 1)], axis=1)
-    gram_ref[...] += dot(right, left, (0, 0))
-
-    @pl.when(step == pl.num_programs(0) - 1)
-    def _():
-        core = lax.axis_index("rows") % 2
-        for spot, (level, below) in enumerate(below_pairs(levels)):
-            lanes = pl.ds(spot * rank, rank)
-            for ref, side in ((keep_ref, core), (send_ref, 1 - core)):
-                rows = pl.ds(pl.multiple_of((level - 1) * rank + side * half, half), half)
-                ref[:, lanes] = gram_ref[rows, pl.ds(below * rank, rank)]
-
-
-def project_kernel(levels, per_step, width, order_ref, inv_ref, right_ref, rhs_ref,
-                   moved_ref, keep_ref, send_ref, factor_ref, total_ref, flip_ref):
-    step = pl.program_id(0)
+def factor_kernel(levels, per_step, width, order_ref, inv_ref, right_ref, left_ref,
+                  factor_ref, moved_ref, keep_ref, send_ref,
+                  inv_buf, right_buf, left_buf, gram_ref, sems):
     rank = right_ref.shape[2]
     kinds = levels * rank
+    half = rank // 2
+    tile = per_step * width
+    steps = inv_ref.shape[0] // per_step
+
+    def copies(step):
+        rows = pl.ds(pl.multiple_of(step * tile, tile), tile)
+        blocks = pl.ds(step * per_step, per_step)
+        return (
+            pltpu.make_async_copy(right_ref.at[:, rows], right_buf.at[:, rows], sems.at[0, step]),
+            pltpu.make_async_copy(inv_ref.at[blocks], inv_buf.at[blocks], sems.at[1, step]),
+            pltpu.make_async_copy(left_ref.at[:levels - 1, rows], left_buf.at[:, rows], sems.at[2, step]),
+        )
+
+    for step in range(steps):
+        for copy in copies(step):
+            copy.start()
+    gram_ref[...] = jnp.zeros_like(gram_ref)
     place = lax.broadcasted_iota(jnp.int32, (width, width), 0)
-    for b in range(per_step):
-        order = order_ref[pl.ds(step * per_step + b, 1), :]
-        chosen = (place == order).astype(jnp.float32).astype(jnp.bfloat16)
-        moved = dot(inv_ref[b], chosen, (1, 1)).astype(jnp.bfloat16)
-        moved_ref[b] = moved
-        rows = pl.ds(b * width, width)
-        right = jnp.concatenate([right_ref[l, rows, :] for l in range(levels)], axis=1)
-        high_part, low_part = halves(dot(right, moved, (0, 0)))
-        factor_ref[:kinds, rows] = high_part
-        factor_ref[kinds:, rows] = low_part
-    term = dot(factor_ref[...], rhs_ref[...], (1, 0))
-
-    @pl.when(step == 0)
-    def _():
-        total_ref[...] = term
-
-    @pl.when(step > 0)
-    def _():
-        total_ref[...] += term
-
-    @pl.when(step == pl.num_programs(0) - 1)
-    def _():
-        flip_ref[...] = (total_ref[:kinds] + total_ref[kinds:]).T
-        me = lax.axis_index("rows")
-        slots, share, _ = keep_ref.shape
-        for slot in range(slots):
-            for ref, owner in ((keep_ref, me ^ (2 * slot)), (send_ref, me ^ (2 * slot + 1))):
-                ref[slot] = flip_ref[pl.ds(pl.multiple_of(owner * share, share), share), :]
+
+    def body(step, _):
+        for copy in copies(step):
+            copy.wait()
+        rows = pl.ds(pl.multiple_of(step * tile, tile), tile)
+        right = jnp.concatenate([right_buf[l, rows, :] for l in range(levels)], axis=1).T
+        left = jnp.concatenate([left_buf[l, rows, :] for l in range(levels - 1)], axis=1)
+        gram_ref[...] += dot(right[rank:], left, (1, 0))
+        for b in range(per_step):
+            block = step * per_step + b
+            chosen = (place == order_ref[pl.ds(block, 1), :]).astype(jnp.float32).astype(jnp.bfloat16)
+            moved = dot(inv_buf[block], chosen, (1, 1)).astype(jnp.bfloat16)
+            moved_ref[block] = moved
+            lanes = pl.ds(pl.multiple_of(block * width, width), width)
+            high_part, low_part = halves(dot(right[:, b * width:(b + 1) * width], moved, (1, 0)))
+            factor_ref[:kinds, lanes] = high_part
+            factor_ref[kinds:, lanes] = low_part
+        return 0
+
+    lax.fori_loop(0, steps, body, 0)
+    core = lax.axis_index("rows") % 2
+    for spot, (level, below) in enumerate(below_pairs(levels)):
+        lanes = pl.ds(spot * rank, rank)
+        for ref, side in ((keep_ref, core), (send_ref, 1 - core)):
+            rows = pl.ds(pl.multiple_of((level - 1) * rank + side * half, half), half)
+            ref[:, lanes] = gram_ref[rows, pl.ds(below * rank, rank)]
+
+
+def project_kernel(factor_ref, rhs_ref, keep_ref, send_ref, flip_ref):
+    kinds = factor_ref.shape[0] // 2
+    columns = rhs_ref.shape[1]
+    part = min(256, columns)
+    for begin in range(0, columns, part):
+        total = dot(factor_ref[...], rhs_ref[:, begin:begin + part], (1, 0))
+        flip_ref[begin:begin + part, :] = (total[:kinds] + total[kinds:]).T
+    me = lax.axis_index("rows")
+    slots, share, _ = keep_ref.shape
+    for slot in range(slots):
+        for ref, owner in ((keep_ref, me ^ (2 * slot)), (send_ref, me ^ (2 * slot + 1))):
+            ref[slot] = flip_ref[pl.ds(pl.multiple_of(owner * share, share), share), :]
 
 
 def merge_kernel(keep_ref, got_ref, *out_refs):
@@ -194,23 +200,37 @@
 
 def expand_kernel(levels, per_step, width, slots, *refs):
     piece_refs = refs[:2 * slots]
-    moved_ref, rhs_ref, left_ref, out_ref, flip_ref, factor_ref = refs[2 * slots:]
+    moved_ref, rhs_ref, left_ref, out_ref, flip_ref, factor_ref, out_buf, sems = refs[2 * slots:]
     share, kinds = piece_refs[0].shape
-
-    @pl.when(pl.program_id(0) == 0)
-    def _():
-        me = lax.axis_index("rows")
-        for slot in range(2 * slots):
-            owner = me ^ slot
-            flip_ref[pl.ds(pl.multiple_of(owner * share, share), share), :] = piece_refs[slot][...]
-        high_part, low_part = halves(flip_ref[...].T)
-        factor_ref[:kinds, :] = high_part
-        factor_ref[kinds:, :] = low_part
-
-    for b in range(per_step):
-        rows = pl.ds(b * width, width)
+    tile = per_step * width
+    steps = moved_ref.shape[0] // per_step
+    me = lax.axis_index("rows")
+    for slot in range(2 * slots):
+        owner = me ^ slot
+        flip_ref[pl.ds(pl.multiple_of(owner * share, share), share), :] = piece_refs[slot][...]
+    high_part, low_part = halves(flip_ref[...].T)
+    factor_ref[:kinds, :] = high_part
+    factor_ref[kinds:, :] = low_part
+
+    def copy(step):
+        rows = pl.ds(pl.multiple_of(step * tile, tile), tile)
+        return pltpu.make_async_copy(out_buf.at[rows], out_ref.at[rows], sems.at[step])
+
+    def body(step, _):
+        rows = pl.ds(pl.multiple_of(step * tile, tile), tile)
         left = jnp.concatenate([left_ref[l, rows, :] for l in range(levels)] * 2, axis=1)
-        out_ref[rows, :] = dot(moved_ref[b], rhs_ref[rows, :], (1, 0)) - dot(left, factor_ref[...], (1, 0))
+        update = dot(left, factor_ref[...], (1, 0))
+        for b in range(per_step):
+            block = step * per_step + b
+            rows = pl.ds(pl.multiple_of(block * width, width), width)
+            first = dot(moved_ref[block], rhs_ref[rows, :], (1, 0))
+            out_buf[rows, :] = first - update[b * width:(b + 1) * width]
+        copy(step).start()
+        return 0
+
+    lax.fori_loop(0, steps, body, 0)
+    for step in range(steps):
+        copy(step).wait()
 
 
 def whole(shape):
@@ -238,46 +258,34 @@
     share = columns // count
     gram_lanes = len(below_pairs(levels)) * rank
 
-    per_step = blocks_per_step(nblocks, 6)
-    steps = nblocks // per_step
-    tile = per_step * width
-    gram_keep, gram_send = pl.pallas_call(
-        functools.partial(gram_kernel, levels),
-        grid=(steps,),
-        in_specs=[pl.BlockSpec((levels, tile, rank), lambda i: (0, i, 0))] * 2,
-        out_specs=[whole((rank // 2, gram_lanes))] * 2,
-        out_shape=[floats(rank // 2, gram_lanes)] * 2,
-        scratch_shapes=[pltpu.VMEM((size, size), jnp.float32)],
-        compiler_params=params(56),
-        name="gram",
-    )(right_basis, left_basis)
+    per_step = blocks_per_step(nblocks, 3)
+    factors, moved, gram_keep, gram_send = pl.pallas_call(
+        functools.partial(factor_kernel, levels, per_step, width),
+        in_specs=[pl.BlockSpec()] + [pl.BlockSpec(memory_space=pl.ANY)] * 3,
+        out_shape=[
+            jax.ShapeDtypeStruct((2 * kinds, rows), jnp.bfloat16),
+            jax.ShapeDtypeStruct((nblocks, width, width), jnp.bfloat16),
+        ] + [floats(rank // 2, gram_lanes)] * 2,
+        scratch_shapes=[
+            pltpu.VMEM((nblocks, width, width), jnp.bfloat16),
+            pltpu.VMEM((levels, rows, rank), jnp.bfloat16),
+            pltpu.VMEM((levels - 1, rows, rank), jnp.bfloat16),
+            pltpu.VMEM((size, size), jnp.float32),
+            pltpu.SemaphoreType.DMA((3, nblocks // per_step)),
+        ],
+        compiler_params=params(32),
+        name="factor",
+    )(leaf_order, leaf_inv, right_basis, left_basis)
 
     gram_got = swap(gram_send, "rows", 1)
 
-    per_step = blocks_per_step(nblocks, 3)
-    steps = nblocks // per_step
-    tile = per_step * width
-    moved, keep, send = pl.pallas_call(
-        functools.partial(project_kernel, levels, per_step, width),
-        grid=(steps,),
-        in_specs=[
-            whole((nblocks, width)),
-            pl.BlockSpec((per_step, width, width), lambda i: (i, 0, 0)),
-            pl.BlockSpec((levels, tile, rank), lambda i: (0, i, 0)),
-            pl.BlockSpec((tile, columns), lambda i: (i, 0)),
-        ],
-        out_specs=[pl.BlockSpec((per_step, width, width), lambda i: (i, 0, 0))]
-        + [whole((slots, share, kinds))] * 2,
-        out_shape=[jax.ShapeDtypeStruct((nblocks, width, width), jnp.bfloat16)]
-        + [floats(slots, share, kinds)] * 2,
-        scratch_shapes=[
-            pltpu.VMEM((2 * kinds, tile), jnp.bfloat16),
-            pltpu.VMEM((2 * kinds, columns), jnp.float32),
-            pltpu.VMEM((columns, kinds), jnp.float32),
-        ],
-        compiler_params=params(56),
+    keep, send = pl.pallas_call(
+        project_kernel,
+        out_shape=[floats(slots, share, kinds)] * 2,
+        scratch_shapes=[pltpu.VMEM((columns, kinds), jnp.float32)],
+        compiler_params=params(24),
         name="project",
-    )(leaf_order, leaf_inv, right_basis, rhs)
+    )(factors, rhs)
 
     got = swap(send, "rows", 1)
     merged = pl.pallas_call(
@@ -341,21 +349,18 @@
         piece = swap(piece, "rows", 2 * slot) if slot > 0 else piece
         pieces += [piece, swap(piece, "rows", 1)]
 
+    per_step = blocks_per_step(nblocks, 2)
     return pl.pallas_call(
         functools.partial(expand_kernel, levels, per_step, width, slots),
-        grid=(steps,),
-        in_specs=[whole((share, kinds))] * count + [
-            pl.BlockSpec((per_step, width, width), lambda i: (i, 0, 0)),
-            pl.BlockSpec((tile, columns), lambda i: (i, 0)),
-            pl.BlockSpec((levels, tile, rank), lambda i: (0, i, 0)),
-        ],
-        out_specs=pl.BlockSpec((tile, columns), lambda i: (i, 0)),
+        out_specs=pl.BlockSpec(memory_space=pl.ANY),
         out_shape=floats(rows, columns),
         scratch_shapes=[
             pltpu.VMEM((columns, kinds), jnp.float32),
             pltpu.VMEM((2 * kinds, columns), jnp.bfloat16),
+            pltpu.VMEM((rows, columns), jnp.float32),
+            pltpu.SemaphoreType.DMA((nblocks // per_step,)),
         ],
-        compiler_params=params(24),
+        compiler_params=params(32),
         name="expand",
     )(*pieces, moved, rhs, left_basis)
 

time: 73.2 us -> 74.1 us (1.012)
  local copies, waits for them, and re-layouts: 2.51 us -> 10.1 us
  Pallas kernels: 31.3 us -> 25.7 us
  other arithmetic: 1.62 us -> 0.74 us
    unnamed x12 -> x26, local copies, waits for them, and re-layouts: 2.51 us -> 10.1 us
    pallas_call x2, Pallas kernels: 16.8 us -> 11.5 us  [the longest x1 6.69 us: per_device(): pl.pallas_call(functools.partial(factor_kernel, levels, per_step, width),...]
    add x1, other arithmetic: 0.91 us -> 0.01 us  [per_device(): gram = gram_keep + gram_got]
  transfers between devices with their start and end apart: 18 -> 18, of which waited for: 12 -> 12; matrix products, arithmetic and copies ran while one was open for 2% -> 1% of each run, Pallas kernels for 11% -> 4%
where the time goes in v3:
time: 74.1 us; the launch traced here: 73.8 us
  Pallas kernels  25.7 us (35%)
  waiting for transfers between devices  20.8 us (28%)
  starting transfers between devices  16.2 us (22%)
  local copies, waits for them, and re-layouts  10.1 us (14%)
    ppermute x18, waiting for transfers between devices, swap(): return lax.ppermute(value, axis, [(i, i ^ mask) for i in range(count)])  20.8 us
    ppermute x18, starting transfers between devices, swap(): return lax.ppermute(value, axis, [(i, i ^ mask) for i in range(count)])  16.2 us
    unnamed x26, local copies, waits for them, and re-layouts  10.1 us
    pallas_call x1, Pallas kernels, per_device(): pl.pallas_call(functools.partial(expand_kernel, levels, per_step, width,...  7.78 us
    pallas_call x1, Pallas kernels, per_device(): pl.pallas_call(functools.partial(factor_kernel, levels, per_step, width),...  6.69 us
    pallas_call x1, Pallas kernels, per_device(): pl.pallas_call(project_kernel, out_shape=[floats(slots, share, kinds)] *...  4.78 us
    pallas_call x1, Pallas kernels, per_device(): pl.pallas_call(functools.partial(node_kernel, levels, rank, slots), out_s...  2.22 us
    pallas_call x1, Pallas kernels, per_device(): pl.pallas_call(prepare_kernel, grid_spec=pltpu.PrefetchScalarGridSpec(num...  1.69 us
  transfers between devices with their start and end apart: 18, of which 12 were waited for; matrix products, arithmetic and copies ran while one was open for 1% of the time, Pallas kernels for 4%

profile of v3, /device:TPU:0, one launch (start us, length us, event | category | flops | bytes accessed | tf_op | source)
XLA Modules:
  0.0 73.8 jit_solution(15784013840615142718)
XLA Ops:
  0.0 0.0 copy-start
  0.0 0.0 copy-start.2
  0.0 2.1 %copy-done.2 = bf16[3,4608,128]{2,1,0:T(8,128)(2,1)S(1)} copy-done((bf16[3,4608,128]{2,1,0:T(8,128)(2,1)S(1)}, bf16[3,4608,128]{2,1,0:T(8,128)(2,1)}, u32[]{:S(2)}) %copy-start.2) | copy-done | bytes 3538968
  2.2 2.3 %copy-done.4 = bf16[3,4608,128]{2,1,0:T(8,128)(2,1)S(1)} copy-done((bf16[3,4608,128]{2,1,0:T(8,128)(2,1)S(1)}, bf16[3,4608,128]{2,1,0:T(8,128)(2,1)}, u32[]{:S(2)}) %copy-start.4) | copy-done | bytes 3538968
  4.5 1.7 %copy-done.7 = bf16[18,256,256]{2,1,0:T(8,128)(2,1)S(1)} copy-done((bf16[18,256,256]{2,1,0:T(8,128)(2,1)S(1)}, bf16[18,256,256]{2,1,0:T(8,128)(2,1)}, u32[]{:S(2)}) %copy-start.7) | copy-done | bytes 2359320
  6.1 0.7 copy-done.11
  6.9 6.7 %factor.1 = (bf16[768,4608]{1,0:T(8,128)(2,1)S(1)}, bf16[18,256,256]{2,1,0:T(8,128)(2,1)S(1)}, f32[64,384]{1,0:T(8,128)S(1)}, f32[64,384]{1,0:T(8,128)S(1)}) custom-call(s32[18,256]{1,0:T(8,128)S(1)} %copy-done.11, bf16[18,256,256]{2,1,0:T(8,128)(2,1)S(1)} %copy-done.7, bf16[3,4608,128]{2,1,0:T(8,128)(2,1)S(1)} %copy-done.4, bf16[3,4608,128]{2,1,0:T(8,128)(2,1)S(1)} %copy-done.2), custom_call_target="tpu_custom_call" | custom-call | tf_op jit(solution)/shard_map/factor/pallas_call | solution.py:262
  13.6 0.0 copy-start.5
  13.6 0.0 copy-done
  13.6 0.0 copy-start.12
  13.6 0.0 copy-start.3
  13.6 4.8 %project.1 = (f32[4,64,384]{2,1,0:T(8,128)S(1)}, f32[4,64,384]{2,1,0:T(8,128)}) custom-call(bf16[768,4608]{1,0:T(8,128)(2,1)S(1)} %get-tuple-element.22.factor_ref, bf16[4608,512]{1,0:T(8,128)(2,1)S(1)} %copy-done), custom_call_target="tpu_custom_call" | custom-call | tf_op jit(solution)/shard_map/project/pallas_call | solution.py:282
  18.4 0.0 copy-done.5
  18.4 0.7 %copy-done.9 = f32[4,64,384]{2,1,0:T(8,128)} copy-done((f32[4,64,384]{2,1,0:T(8,128)}, f32[4,64,384]{2,1,0:T(8,128)S(1)}, u32[]{:S(2)}) %copy-start.9) | copy-done | bytes 393240
  19.1 0.5 collective-permute-start
  19.6 0.1 collective-permute-start.4
  19.7 1.4 %collective-permute-done.4 = f32[64,384]{1,0:T(8,128)S(1)} collective-permute-done((f32[64,384]{1,0:T(8,128)S(1)}, f32[64,384]{1,0:T(8,128)S(1)}, u32[]{:S(2)}, u32[]{:S(2)}) %collective-permute-start.4) | collective-permute-done | bytes 98336 | tf_op jit(solution)/shard_map/ppermute | solution.py:30
  21.1 2.6 %collective-permute-start.5 = (f32[64,384]{1,0:T(8,128)S(1)}, f32[64,384]{1,0:T(8,128)S(1)}, u32[]{:S(2)}, u32[]{:S(2)}) collective-permute-start(f32[64,384]{1,0:T(8,128)S(1)} %add.12), channel_id=1, source_target_pairs={{0,2},{1,3},{2,0},{3,1},{4,6},{5,7},{6,4},{7,5},{8,10},{9,11},{10,... | collective-permute-start | bytes 294920 | tf_op jit(solution)/shard_map/ppermute | solution.py:30
  23.7 3.3 %collective-permute-done.5 = f32[64,384]{1,0:T(8,128)S(1)} collective-permute-done((f32[64,384]{1,0:T(8,128)S(1)}, f32[64,384]{1,0:T(8,128)S(1)}, u32[]{:S(2)}, u32[]{:S(2)}) %collective-permute-start.5) | collective-permute-done | bytes 98336 | tf_op jit(solution)/shard_map/ppermute | solution.py:30
  27.0 0.7 add.13.refs_4_
  27.6 1.8 %collective-permute-start.6 = (f32[64,384]{1,0:T(8,128)}, f32[64,384]{1,0:T(8,128)}, u32[]{:S(2)}, u32[]{:S(2)}) collective-permute-start(f32[64,384]{1,0:T(8,128)} %add.13.refs_4_), channel_id=1, source_target_pairs={{0,4},{1,5},{2,6},{3,7},{4,0},{5,1},{6,2},{7,3},{8,12},{9,13},{10,... | collective-permute-start | bytes 294920 | tf_op jit(solution)/shard_map/ppermute | solution.py:30
  29.4 0.0 collective-permute-start.7
  29.4 3.2 %collective-permute-done.6.refs_5_ = f32[64,384]{1,0:T(8,128)} collective-permute-done((f32[64,384]{1,0:T(8,128)}, f32[64,384]{1,0:T(8,128)}, u32[]{:S(2)}, u32[]{:S(2)}) %collective-permute-start.6) | collective-permute-done | bytes 98336 | tf_op jit(solution)/shard_map/ppermute | solution.py:30
  32.6 0.0 collective-permute-start.8
  32.6 0.0 collective-permute-done.got_ref
  32.6 1.0 %copy-done.10 = f32[4,64,384]{2,1,0:T(8,128)S(1)} copy-done((f32[4,64,384]{2,1,0:T(8,128)S(1)}, f32[4,64,384]{2,1,0:T(8,128)}, u32[]{:S(2)}) %copy-start.10) | copy-done | bytes 393240
  33.6 1.2 %merge.1 = (f32[64,384]{1,0:T(8,128)S(1)}, f32[64,384]{1,0:T(8,128)S(1)}, f32[64,384]{1,0:T(8,128)S(1)}, f32[64,384]{1,0:T(8,128)S(1)}) custom-call(f32[4,64,384]{2,1,0:T(8,128)S(1)} %copy-done.10, f32[4,64,384]{2,1,0:T(8,128)} %collective-permute-done.got_ref), custom_call_target="tpu_custom_call" | custom-call | tf_op jit(solution)/shard_map/merge/pallas_call | solution.py:291
  34.8 1.8 %collective-permute-start.1 = (f32[64,384]{1,0:T(8,128)S(1)}, f32[64,384]{1,0:T(8,128)S(1)}, u32[]{:S(2)}, u32[]{:S(2)}) collective-permute-start(f32[64,384]{1,0:T(8,128)S(1)} %get-tuple-element.26), channel_id=1, source_target_pairs={{0,2},{1,3},{2,0},{3,1},{4,6},{5,7},{6,4},{7,5},{8,10},{9,11},{10,... | collective-permute-start | bytes 294920 | tf_op jit(solution)/shard_map/ppermute | solution.py:30
  36.6 1.5 %collective-permute-start.2 = (f32[64,384]{1,0:T(8,128)S(1)}, f32[64,384]{1,0:T(8,128)S(1)}, u32[]{:S(2)}, u32[]{:S(2)}) collective-permute-start(f32[64,384]{1,0:T(8,128)S(1)} %get-tuple-element.27), channel_id=1, source_target_pairs={{0,4},{1,5},{2,6},{3,7},{4,0},{5,1},{6,2},{7,3},{8,12},{9,13},{10,... | collective-permute-start | bytes 294920 | tf_op jit(solution)/shard_map/ppermute | solution.py:30
  38.1 0.2 collective-permute-start.3
  38.3 0.1 pad_add_fusion.index_ref
  38.4 0.0 copy-done.12
  38.4 1.5 %copy-done.8 = f32[7,256,256]{2,1,0:T(8,128)S(1)} copy-done((f32[7,256,256]{2,1,0:T(8,128)S(1)}, f32[7,256,256]{2,1,0:T(8,128)}, u32[]{:S(2)}) %copy-start.8) | copy-done | bytes 1835032
  39.9 1.7 %prepare.1.refs_8_.joined_ref = f32[3,256,256]{2,1,0:T(8,128)S(1)} custom-call(s32[3]{0:T(128)S(1)} %pad_add_fusion.index_ref, f32[7,256,256]{2,1,0:T(8,128)S(1)} %copy-done.8, s32[3,128]{1,0:T(4,128)S(1)} %copy-done.12), custom_call_target="tpu_custom_call" | custom-call | tf_op jit(solution)/shard_map/prepare/pallas_call | solution.py:305
  41.6 0.0 collective-permute-done.7.refs_6_
  41.6 0.0 collective-permute-done.8.refs_7_
  41.6 0.0 collective-permute-done.1.refs_1_
  41.6 1.0 %collective-permute-done.2.refs_2_ = f32[64,384]{1,0:T(8,128)S(1)} collective-permute-done((f32[64,384]{1,0:T(8,128)S(1)}, f32[64,384]{1,0:T(8,128)S(1)}, u32[]{:S(2)}, u32[]{:S(2)}) %collective-permute-start.2) | collective-permute-done | bytes 98336 | tf_op jit(solution)/shard_map/ppermute | solution.py:30
  42.6 1.0 %collective-permute-done.3.refs_3_ = f32[64,384]{1,0:T(8,128)S(1)} collective-permute-done((f32[64,384]{1,0:T(8,128)S(1)}, f32[64,384]{1,0:T(8,128)S(1)}, u32[]{:S(2)}, u32[]{:S(2)}) %collective-permute-start.3) | collective-permute-done | bytes 98336 | tf_op jit(solution)/shard_map/ppermute | solution.py:30
  43.6 2.2 %node.1 = (f32[64,128]{1,0:T(8,128)S(1)}, f32[64,128]{1,0:T(8,128)S(1)}, f32[256,128]{1,0:T(8,128)S(1)}) custom-call(f32[64,384]{1,0:T(8,128)S(1)} %get-tuple-element.25.refs_0_, f32[64,384]{1,0:T(8,128)S(1)} %collective-permute-done.1.refs_1_, f32[64,384]{1,0:T(8,128)S(1)} %collective-permute-done.2.refs_2_, f32[64,384]{1,0:T(8,128)S(1)} %collective-permute-done.3.refs_3_, ...), custom_call_target="tpu_custom_call" | custom-call | tf_op jit(solution)/shard_map/node/pallas_call | solution.py:324
  45.9 1.6 %collective-permute-start.9 = (f32[256,128]{1,0:T(8,128)S(1)}, f32[256,128]{1,0:T(8,128)S(1)}, u32[]{:S(2)}, u32[]{:S(2)}) collective-permute-start(f32[256,128]{1,0:T(8,128)S(1)} %get-tuple-element.33.sent_ref), channel_id=1, source_target_pairs={{0,8},{8,0},{16,24},{24,16},{1,9},{9,1},{17,25},{25,17},{2,10},{10... | collective-permute-start | bytes 393224 | tf_op jit(solution)/shard_map/ppermute | solution.py:30
  47.5 3.4 %collective-permute-done.9.got_ref = f32[256,128]{1,0:T(8,128)S(1)} collective-permute-done((f32[256,128]{1,0:T(8,128)S(1)}, f32[256,128]{1,0:T(8,128)S(1)}, u32[]{:S(2)}, u32[]{:S(2)}) %collective-permute-start.9) | collective-permute-done | bytes 131104 | tf_op jit(solution)/shard_map/ppermute | solution.py:30
  50.9 1.0 %level1.1 = (f32[64,128]{1,0:T(8,128)S(1)}, f32[64,128]{1,0:T(8,128)S(1)}) custom-call(f32[256,128]{1,0:T(8,128)S(1)} %get-tuple-element.33.sent_ref, f32[256,128]{1,0:T(8,128)S(1)} %collective-permute-done.9.got_ref, f32[3,256,256]{2,1,0:T(8,128)S(1)} %prepare.1.refs_8_.joined_ref), custom_call_target="tpu_custom_call" | custom-call | tf_op jit(solution)/shard_map/level1/pallas_call | solution.py:334
  51.9 2.6 %collective-permute-start.10 = (f32[64,128]{1,0:T(8,128)S(1)}, f32[64,128]{1,0:T(8,128)S(1)}, u32[]{:S(2)}, u32[]{:S(2)}) collective-permute-start(f32[64,128]{1,0:T(8,128)S(1)} %get-tuple-element.35.sent_ref), channel_id=1, source_target_pairs={{0,16},{8,24},{16,0},{24,8},{1,17},{9,25},{17,1},{25,9},{2,18},{10... | collective-permute-start | bytes 98312 | tf_op jit(solution)/shard_map/ppermute | solution.py:30
  54.6 2.2 %collective-permute-done.10.got_ref = f32[64,128]{1,0:T(8,128)S(1)} collective-permute-done((f32[64,128]{1,0:T(8,128)S(1)}, f32[64,128]{1,0:T(8,128)S(1)}, u32[]{:S(2)}, u32[]{:S(2)}) %collective-permute-start.10) | collective-permute-done | bytes 32800 | tf_op jit(solution)/shard_map/ppermute | solution.py:30
  56.8 0.4 level2.1.refs_3_
  57.2 1.5 %collective-permute-start.16 = (f32[64,384]{1,0:T(8,128)S(1)}, f32[64,384]{1,0:T(8,128)S(1)}, u32[]{:S(2)}, u32[]{:S(2)}) collective-permute-start(f32[64,384]{1,0:T(8,128)S(1)} %get-tuple-element.37), channel_id=1, source_target_pairs={{0,6},{1,7},{2,4},{3,5},{4,2},{5,3},{6,0},{7,1},{8,14},{9,15},{10,... | collective-permute-start | bytes 294920 | tf_op jit(solution)/shard_map/ppermute | solution.py:30
  58.7 1.4 %collective-permute-start.14 = (f32[64,384]{1,0:T(8,128)S(1)}, f32[64,384]{1,0:T(8,128)S(1)}, u32[]{:S(2)}, u32[]{:S(2)}) collective-permute-start(f32[64,384]{1,0:T(8,128)S(1)} %get-tuple-element.37), channel_id=1, source_target_pairs={{0,4},{1,5},{2,6},{3,7},{4,0},{5,1},{6,2},{7,3},{8,12},{9,13},{10,... | collective-permute-start | bytes 294920 | tf_op jit(solution)/shard_map/ppermute | solution.py:30
  60.1 0.7 collective-permute-start.12
  60.7 0.0 collective-permute-start.11
  60.7 2.1 %collective-permute-done.16.refs_6_ = f32[64,384]{1,0:T(8,128)S(1)} collective-permute-done((f32[64,384]{1,0:T(8,128)S(1)}, f32[64,384]{1,0:T(8,128)S(1)}, u32[]{:S(2)}, u32[]{:S(2)}) %collective-permute-start.16) | collective-permute-done | bytes 98336 | tf_op jit(solution)/shard_map/ppermute | solution.py:30
  62.8 0.0 collective-permute-start.17
  62.8 1.0 %collective-permute-done.14.refs_4_ = f32[64,384]{1,0:T(8,128)S(1)} collective-permute-done((f32[64,384]{1,0:T(8,128)S(1)}, f32[64,384]{1,0:T(8,128)S(1)}, u32[]{:S(2)}, u32[]{:S(2)}) %collective-permute-start.14) | collective-permute-done | bytes 98336 | tf_op jit(solution)/shard_map/ppermute | solution.py:30
  63.8 0.0 collective-permute-start.15
  63.8 0.9 %collective-permute-done.12.refs_2_ = f32[64,384]{1,0:T(8,128)S(1)} collective-permute-done((f32[64,384]{1,0:T(8,128)S(1)}, f32[64,384]{1,0:T(8,128)S(1)}, u32[]{:S(2)}, u32[]{:S(2)}) %collective-permute-start.12) | collective-permute-done | bytes 98336 | tf_op jit(solution)/shard_map/ppermute | solution.py:30
  64.7 0.0 collective-permute-start.13
  64.7 0.0 collective-permute-done.11.refs_1_
  64.7 0.0 collective-permute-done.17.refs_7_
  64.7 0.4 collective-permute-done.15.refs_5_
  65.1 0.9 %collective-permute-done.13.refs_3_ = f32[64,384]{1,0:T(8,128)S(1)} collective-permute-done((f32[64,384]{1,0:T(8,128)S(1)}, f32[64,384]{1,0:T(8,128)S(1)}, u32[]{:S(2)}, u32[]{:S(2)}) %collective-permute-start.13) | collective-permute-done | bytes 98336 | tf_op jit(solution)/shard_map/ppermute | solution.py:30
  66.0 0.0 copy-done.3
  66.0 0.0 copy-done.1
  66.0 0.0 copy-done.6
  66.0 7.8 %expand.1 = f32[4608,512]{1,0:T(8,128)} custom-call(f32[64,384]{1,0:T(8,128)S(1)} %get-tuple-element.36.refs_0_, f32[64,384]{1,0:T(8,128)S(1)} %collective-permute-done.11.refs_1_, f32[64,384]{1,0:T(8,128)S(1)} %collective-permute-done.12.refs_2_, f32[64,384]{1,0:T(8,128)S(1)} %collective-permute-done.13.refs_3_, ...), custom_call_target="tpu_custom_call" | custom-call | tf_op jit(solution)/shard_map/expand/pallas_call | solution.py:353
  (10 shorter events, 0.0 us)
Async XLA Ops:
  0.0 13.6 %copy-start = (bf16[4608,512]{1,0:T(8,128)(2,1)S(1)}, bf16[4608,512]{1,0:T(8,128)(2,1)}, u32[]{:S(2)}) copy-start(bf16[4608,512]{1,0:T(8,128)(2,1)} %refs_9_.1) | copy-start | bytes 14155780
  0.0 2.2 %copy-start.2 = (bf16[3,4608,128]{2,1,0:T(8,128)(2,1)S(1)}, bf16[3,4608,128]{2,1,0:T(8,128)(2,1)}, u32[]{:S(2)}) copy-start(bf16[3,4608,128]{2,1,0:T(8,128)(2,1)} %refs_10_.1) | copy-start | bytes 10616836
  2.2 2.3 %copy-start.4 = (bf16[3,4608,128]{2,1,0:T(8,128)(2,1)S(1)}, bf16[3,4608,128]{2,1,0:T(8,128)(2,1)}, u32[]{:S(2)}) copy-start(bf16[3,4608,128]{2,1,0:T(8,128)(2,1)} %right_ref.1) | copy-start | bytes 10616836
  4.5 1.7 %copy-start.7 = (bf16[18,256,256]{2,1,0:T(8,128)(2,1)S(1)}, bf16[18,256,256]{2,1,0:T(8,128)(2,1)}, u32[]{:S(2)}) copy-start(bf16[18,256,256]{2,1,0:T(8,128)(2,1)} %inv_ref.1) | copy-start | bytes 7077892
  6.1 0.7 copy-start.11
  13.6 4.8 %copy-start.5 = (bf16[18,256,256]{2,1,0:T(8,128)(2,1)}, bf16[18,256,256]{2,1,0:T(8,128)(2,1)S(1)}, u32[]{:S(2)}) copy-start(bf16[18,256,256]{2,1,0:T(8,128)(2,1)S(1)} %get-tuple-element.38.refs_8_) | copy-start | bytes 7077892
  13.6 24.8 %copy-start.12 = (s32[3,128]{1,0:T(4,128)S(1)}, s32[3,128]{1,0:T(4,128)}, u32[]{:S(2)}) copy-start(s32[3,128]{1,0:T(4,128)} %perm_ref.1) | copy-start | bytes 4612
  13.6 52.4 %copy-start.3 = (bf16[3,4608,128]{2,1,0:T(8,128)(2,1)S(1)}, bf16[3,4608,128]{2,1,0:T(8,128)(2,1)}, u32[]{:S(2)}) copy-start(bf16[3,4608,128]{2,1,0:T(8,128)(2,1)} %refs_10_.1) | copy-start | bytes 10616836
  18.4 0.8 %copy-start.9 = (f32[4,64,384]{2,1,0:T(8,128)}, f32[4,64,384]{2,1,0:T(8,128)S(1)}, u32[]{:S(2)}) copy-start(f32[4,64,384]{2,1,0:T(8,128)S(1)} %get-tuple-element.23.keep_ref) | copy-start | bytes 1179652
  19.1 13.4 %collective-permute-start = (f32[4,64,384]{2,1,0:T(8,128)}, f32[4,64,384]{2,1,0:T(8,128)}, u32[]{:S(2)}, u32[]{:S(2)}) collective-permute-start(f32[4,64,384]{2,1,0:T(8,128)} %get-tuple-element.24), channel_id=1, source_target_pairs={{0,1},{1,0},{2,3},{3,2},{4,5},{5,4},{6,7},{7,6},{8,9},{9,8},{10,11... | collective-permute-start | bytes 1179656 | tf_op jit(solution)/shard_map/ppermute | solution.py:30
  19.6 1.5 %collective-permute-start.4 = (f32[64,384]{1,0:T(8,128)S(1)}, f32[64,384]{1,0:T(8,128)S(1)}, u32[]{:S(2)}, u32[]{:S(2)}) collective-permute-start(f32[64,384]{1,0:T(8,128)S(1)} %get-tuple-element.30), channel_id=1, source_target_pairs={{0,1},{1,0},{2,3},{3,2},{4,5},{5,4},{6,7},{7,6},{8,9},{9,8},{10,11... | collective-permute-start | bytes 294920 | tf_op jit(solution)/shard_map/ppermute | solution.py:30
  21.1 5.9 %collective-permute-start.5 = (f32[64,384]{1,0:T(8,128)S(1)}, f32[64,384]{1,0:T(8,128)S(1)}, u32[]{:S(2)}, u32[]{:S(2)}) collective-permute-start(f32[64,384]{1,0:T(8,128)S(1)} %add.12), channel_id=1, source_target_pairs={{0,2},{1,3},{2,0},{3,1},{4,6},{5,7},{6,4},{7,5},{8,10},{9,11},{10,... | collective-permute-start | bytes 294920 | tf_op jit(solution)/shard_map/ppermute | solution.py:30
  27.6 4.9 %collective-permute-start.6 = (f32[64,384]{1,0:T(8,128)}, f32[64,384]{1,0:T(8,128)}, u32[]{:S(2)}, u32[]{:S(2)}) collective-permute-start(f32[64,384]{1,0:T(8,128)} %add.13.refs_4_), channel_id=1, source_target_pairs={{0,4},{1,5},{2,6},{3,7},{4,0},{5,1},{6,2},{7,3},{8,12},{9,13},{10,... | collective-permute-start | bytes 294920 | tf_op jit(solution)/shard_map/ppermute | solution.py:30
  29.4 12.2 %collective-permute-start.7 = (f32[64,384]{1,0:T(8,128)}, f32[64,384]{1,0:T(8,128)S(1)}, u32[]{:S(2)}, u32[]{:S(2)}) collective-permute-start(f32[64,384]{1,0:T(8,128)} %add.13.refs_4_), channel_id=1, source_target_pairs={{0,1},{1,0},{2,3},{3,2},{4,5},{5,4},{6,7},{7,6},{8,9},{9,8},{10,11... | collective-permute-start | bytes 294920 | tf_op jit(solution)/shard_map/ppermute | solution.py:30
  32.6 9.0 %collective-permute-start.8 = (f32[64,384]{1,0:T(8,128)}, f32[64,384]{1,0:T(8,128)S(1)}, u32[]{:S(2)}, u32[]{:S(2)}) collective-permute-start(f32[64,384]{1,0:T(8,128)} %collective-permute-done.6.refs_5_), channel_id=1, source_target_pairs={{0,1},{1,0},{2,3},{3,2},{4,5},{5,4},{6,7},{7,6},{8,9},{9,8},{10,11... | collective-permute-start | bytes 294920 | tf_op jit(solution)/shard_map/ppermute | solution.py:30
  32.6 1.0 %copy-start.10 = (f32[4,64,384]{2,1,0:T(8,128)S(1)}, f32[4,64,384]{2,1,0:T(8,128)}, u32[]{:S(2)}) copy-start(f32[4,64,384]{2,1,0:T(8,128)} %copy-done.9) | copy-start | bytes 1179652
  33.6 32.4 %copy-start.1 = (bf16[4608,512]{1,0:T(8,128)(2,1)S(1)}, bf16[4608,512]{1,0:T(8,128)(2,1)}, u32[]{:S(2)}) copy-start(bf16[4608,512]{1,0:T(8,128)(2,1)} %refs_9_.1) | copy-start | bytes 14155780
  33.6 32.4 %copy-start.6 = (bf16[18,256,256]{2,1,0:T(8,128)(2,1)S(1)}, bf16[18,256,256]{2,1,0:T(8,128)(2,1)}, u32[]{:S(2)}) copy-start(bf16[18,256,256]{2,1,0:T(8,128)(2,1)} %copy-done.5) | copy-start | bytes 7077892
  34.8 6.9 %collective-permute-start.1 = (f32[64,384]{1,0:T(8,128)S(1)}, f32[64,384]{1,0:T(8,128)S(1)}, u32[]{:S(2)}, u32[]{:S(2)}) collective-permute-start(f32[64,384]{1,0:T(8,128)S(1)} %get-tuple-element.26), channel_id=1, source_target_pairs={{0,2},{1,3},{2,0},{3,1},{4,6},{5,7},{6,4},{7,5},{8,10},{9,11},{10,... | collective-permute-start | bytes 294920 | tf_op jit(solution)/shard_map/ppermute | solution.py:30
  36.6 6.1 %collective-permute-start.2 = (f32[64,384]{1,0:T(8,128)S(1)}, f32[64,384]{1,0:T(8,128)S(1)}, u32[]{:S(2)}, u32[]{:S(2)}) collective-permute-start(f32[64,384]{1,0:T(8,128)S(1)} %get-tuple-element.27), channel_id=1, source_target_pairs={{0,4},{1,5},{2,6},{3,7},{4,0},{5,1},{6,2},{7,3},{8,12},{9,13},{10,... | collective-permute-start | bytes 294920 | tf_op jit(solution)/shard_map/ppermute | solution.py:30
  38.1 5.5 %collective-permute-start.3 = (f32[64,384]{1,0:T(8,128)S(1)}, f32[64,384]{1,0:T(8,128)S(1)}, u32[]{:S(2)}, u32[]{:S(2)}) collective-permute-start(f32[64,384]{1,0:T(8,128)S(1)} %get-tuple-element.28), channel_id=1, source_target_pairs={{0,6},{1,7},{2,4},{3,5},{4,2},{5,3},{6,0},{7,1},{8,14},{9,15},{10,... | collective-permute-start | bytes 294920 | tf_op jit(solution)/shard_map/ppermute | solution.py:30
  38.4 1.5 %copy-start.8 = (f32[7,256,256]{2,1,0:T(8,128)S(1)}, f32[7,256,256]{2,1,0:T(8,128)}, u32[]{:S(2)}) copy-start(f32[7,256,256]{2,1,0:T(8,128)} %joined_ref.1) | copy-start | bytes 5505028
  45.9 5.0 %collective-permute-start.9 = (f32[256,128]{1,0:T(8,128)S(1)}, f32[256,128]{1,0:T(8,128)S(1)}, u32[]{:S(2)}, u32[]{:S(2)}) collective-permute-start(f32[256,128]{1,0:T(8,128)S(1)} %get-tuple-element.33.sent_ref), channel_id=1, source_target_pairs={{0,8},{8,0},{16,24},{24,16},{1,9},{9,1},{17,25},{25,17},{2,10},{10... | collective-permute-start | bytes 393224 | tf_op jit(solution)/shard_map/ppermute | solution.py:30
  51.9 4.9 %collective-permute-start.10 = (f32[64,128]{1,0:T(8,128)S(1)}, f32[64,128]{1,0:T(8,128)S(1)}, u32[]{:S(2)}, u32[]{:S(2)}) collective-permute-start(f32[64,128]{1,0:T(8,128)S(1)} %get-tuple-element.35.sent_ref), channel_id=1, source_target_pairs={{0,16},{8,24},{16,0},{24,8},{1,17},{9,25},{17,1},{25,9},{2,18},{10... | collective-permute-start | bytes 98312 | tf_op jit(solution)/shard_map/ppermute | solution.py:30
  57.2 5.6 %collective-permute-start.16 = (f32[64,384]{1,0:T(8,128)S(1)}, f32[64,384]{1,0:T(8,128)S(1)}, u32[]{:S(2)}, u32[]{:S(2)}) collective-permute-start(f32[64,384]{1,0:T(8,128)S(1)} %get-tuple-element.37), channel_id=1, source_target_pairs={{0,6},{1,7},{2,4},{3,5},{4,2},{5,3},{6,0},{7,1},{8,14},{9,15},{10,... | collective-permute-start | bytes 294920 | tf_op jit(solution)/shard_map/ppermute | solution.py:30
  58.7 5.1 %collective-permute-start.14 = (f32[64,384]{1,0:T(8,128)S(1)}, f32[64,384]{1,0:T(8,128)S(1)}, u32[]{:S(2)}, u32[]{:S(2)}) collective-permute-start(f32[64,384]{1,0:T(8,128)S(1)} %get-tuple-element.37), channel_id=1, source_target_pairs={{0,4},{1,5},{2,6},{3,7},{4,0},{5,1},{6,2},{7,3},{8,12},{9,13},{10,... | collective-permute-start | bytes 294920 | tf_op jit(solution)/shard_map/ppermute | solution.py:30
  60.1 4.6 %collective-permute-start.12 = (f32[64,384]{1,0:T(8,128)S(1)}, f32[64,384]{1,0:T(8,128)S(1)}, u32[]{:S(2)}, u32[]{:S(2)}) collective-permute-start(f32[64,384]{1,0:T(8,128)S(1)} %get-tuple-element.36.refs_0_), channel_id=1, source_target_pairs={{0,2},{1,3},{2,0},{3,1},{4,6},{5,7},{6,4},{7,5},{8,10},{9,11},{10,... | collective-permute-start | bytes 294920 | tf_op jit(solution)/shard_map/ppermute | solution.py:30
  60.7 4.0 %collective-permute-start.11 = (f32[64,384]{1,0:T(8,128)S(1)}, f32[64,384]{1,0:T(8,128)S(1)}, u32[]{:S(2)}, u32[]{:S(2)}) collective-permute-start(f32[64,384]{1,0:T(8,128)S(1)} %get-tuple-element.36.refs_0_), channel_id=1, source_target_pairs={{0,1},{1,0},{2,3},{3,2},{4,5},{5,4},{6,7},{7,6},{8,9},{9,8},{10,11... | collective-permute-start | bytes 294920 | tf_op jit(solution)/shard_map/ppermute | solution.py:30
  62.8 1.9 %collective-permute-start.17 = (f32[64,384]{1,0:T(8,128)S(1)}, f32[64,384]{1,0:T(8,128)S(1)}, u32[]{:S(2)}, u32[]{:S(2)}) collective-permute-start(f32[64,384]{1,0:T(8,128)S(1)} %collective-permute-done.16.refs_6_), channel_id=1, source_target_pairs={{0,1},{1,0},{2,3},{3,2},{4,5},{5,4},{6,7},{7,6},{8,9},{9,8},{10,11... | collective-permute-start | bytes 294920 | tf_op jit(solution)/shard_map/ppermute | solution.py:30
  63.8 1.3 %collective-permute-start.15 = (f32[64,384]{1,0:T(8,128)S(1)}, f32[64,384]{1,0:T(8,128)S(1)}, u32[]{:S(2)}, u32[]{:S(2)}) collective-permute-start(f32[64,384]{1,0:T(8,128)S(1)} %collective-permute-done.14.refs_4_), channel_id=1, source_target_pairs={{0,1},{1,0},{2,3},{3,2},{4,5},{5,4},{6,7},{7,6},{8,9},{9,8},{10,11... | collective-permute-start | bytes 294920 | tf_op jit(solution)/shard_map/ppermute | solution.py:30
  64.7 1.3 %collective-permute-start.13 = (f32[64,384]{1,0:T(8,128)S(1)}, f32[64,384]{1,0:T(8,128)S(1)}, u32[]{:S(2)}, u32[]{:S(2)}) collective-permute-start(f32[64,384]{1,0:T(8,128)S(1)} %collective-permute-done.12.refs_2_), channel_id=1, source_target_pairs={{0,1},{1,0},{2,3},{3,2},{4,5},{5,4},{6,7},{7,6},{8,9},{9,8},{10,11... | collective-permute-start | bytes 294920 | tf_op jit(solution)/shard_map/ppermute | solution.py:30

commit v4 on v3

v4 whole, which is shorter than its diff:
```python
import functools

import jax
import jax.numpy as jnp
from jax import lax
from jax.experimental import pallas as pl
from jax.experimental.pallas import tpu as pltpu
from jax.sharding import PartitionSpec as P

HIGHEST = lax.Precision.HIGHEST
MIB = 1 << 20


def dot(a, b, contract, exact=False):
    return lax.dot_general(
        a, b, ((contract[:1], contract[1:]), ((), ())),
        precision=HIGHEST if exact else None, preferred_element_type=jnp.float32,
    )


def halves(value):
    high_part = value.astype(jnp.bfloat16)
    low_part = (value - high_part.astype(jnp.float32)).astype(jnp.bfloat16)
    return high_part, low_part


def swap(value, axis, mask):
    count = lax.axis_size(axis)
    return lax.ppermute(value, axis, [(i, i ^ mask) for i in range(count)])


def blocks_per_step(nblocks, most):
    return max(size for size in range(1, most + 1) if nblocks % size == 0)


def below_pairs(levels, first=0):
    return [(level, below) for level in range(levels) for below in range(first, level)]


def gram_kernel(levels, per_step, width, right_ref, left_ref, flip_ref, keep_ref, send_ref,
                right_buf, left_buf, gram_ref, sems):
    rank = right_ref.shape[2]
    half = rank // 2
    tile = per_step * width
    steps = right_ref.shape[1] // tile

    def copies(step):
        rows = pl.ds(pl.multiple_of(step * tile, tile), tile)
        return (
            pltpu.make_async_copy(right_ref.at[:, rows], right_buf.at[:, rows], sems.at[0, step]),
            pltpu.make_async_copy(left_ref.at[:levels - 1, rows], left_buf.at[:, rows], sems.at[1, step]),
        )

    for step in range(steps):
        for copy in copies(step):
            copy.start()
    gram_ref[...] = jnp.zeros_like(gram_ref)

    def body(step, _):
        for copy in copies(step):
            copy.wait()
        rows = pl.ds(pl.multiple_of(step * tile, tile), tile)
        right = jnp.concatenate([right_buf[l, rows, :] for l in range(levels)], axis=1).T
        flip_ref[:, rows] = right
        left = jnp.concatenate([left_buf[l, rows, :] for l in range(levels - 1)], axis=1)
        gram_ref[...] += dot(right[rank:], left, (1, 0))
        return 0

    lax.fori_loop(0, steps, body, 0)
    core = lax.axis_index("rows") % 2
    for spot, (level, below) in enumerate(below_pairs(levels)):
        lanes = pl.ds(spot * rank, rank)
        for ref, side in ((keep_ref, core), (send_ref, 1 - core)):
            rows = pl.ds(pl.multiple_of((level - 1) * rank + side * half, half), half)
            ref[:, lanes] = gram_ref[rows, pl.ds(below * rank, rank)]


def factor_kernel(per_step, width, order_ref, inv_ref, flip_ref, factor_ref, moved_ref):
    kinds = flip_ref.shape[0]
    place = lax.broadcasted_iota(jnp.int32, (width, width), 0)

    def body(step, _):
        blocks = [step * per_step + b for b in range(per_step)]
        chosen = [(place == order_ref[pl.ds(block, 1), :]).astype(jnp.float32).astype(jnp.bfloat16)
                  for block in blocks]
        moved = [dot(inv_ref[block], pick, (1, 1)).astype(jnp.bfloat16) for block, pick in zip(blocks, chosen)]
        for block, inverse in zip(blocks, moved):
            moved_ref[block] = inverse
            lanes = pl.ds(pl.multiple_of(block * width, width), width)
            high_part, low_part = halves(dot(flip_ref[:, lanes], inverse, (1, 0)))
            factor_ref[:kinds, lanes] = high_part
            factor_ref[kinds:, lanes] = low_part
        return 0

    lax.fori_loop(0, inv_ref.shape[0] // per_step, body, 0)


def project_kernel(half, factor_ref, rhs_ref, *refs):
    kinds = factor_ref.shape[0] // 2
    keep_ref, send_ref, total_ref = refs[-3:]
    spots, share, _ = keep_ref.shape
    part = total_ref.shape[0]
    total = dot(factor_ref[...], rhs_ref[:, half * part:(half + 1) * part], (1, 0))
    total_ref[...] = (total[:kinds] + total[kinds:]).T
    core = lax.axis_index("rows") % 2
    for spot in range(spots):
        for ref, owner in ((keep_ref, 2 * spot + core), (send_ref, 2 * spot + 1 - core)):
            ref[spot] = total_ref[pl.ds(pl.multiple_of(owner * share, share), share), :]
    if len(refs) > 3:
        mine_ref, got_ref, gram_ref = refs[:-3][0], refs[:-3][1], refs[:-3][2]
        gram_ref[...] = mine_ref[...] + got_ref[...]


def merge_kernel(keep_a, got_a, keep_b, got_b, mine_ref, got_ref, gram_ref, *out_refs):
    chip = lax.axis_index("rows") // 2
    slots = len(out_refs)
    for slot, out_ref in enumerate(out_refs):
        owner = chip ^ slot
        spot = owner % (slots // 2)
        first = keep_a[spot] + got_a[spot]
        second = keep_b[spot] + got_b[spot]
        out_ref[...] = jnp.where(owner < slots // 2, first, second)
    gram_ref[...] = mine_ref[...] + got_ref[...]


def prepare_kernel(levels, joined_ref, perm_ref, out_ref, joined_buf, sems):
    rank = perm_ref.shape[1]
    leaves = lax.axis_size("leaf")
    leaf = lax.axis_index("leaf")
    copies = []
    for level in range(levels):
        node = 2 * leaves - 2 * leaves // 2 ** level + leaf // 2 ** level
        copies.append(pltpu.make_async_copy(joined_ref.at[node], joined_buf.at[level], sems.at[level]))
        copies[-1].start()
    spot = lax.broadcasted_iota(jnp.int32, (rank, rank), 0)
    for level in range(levels):
        copies[level].wait()
        chosen = (spot == perm_ref[level:level + 1, :]).astype(jnp.float32)
        for side in range(2):
            lanes = pl.ds(side * rank, rank)
            out_ref[level, :, lanes] = dot(joined_buf[level, :, lanes], chosen, (1, 1), True)


def by_side(side, own, other):
    return jnp.where(side == 0, own, other), jnp.where(side == 0, other, own)


def pack_message(message_ref, pieces):
    row = 0
    for piece in pieces:
        message_ref[pl.ds(row, piece.shape[0]), :] = piece
        row += piece.shape[0]


def node_kernel(rank, slots, *refs):
    part_refs = refs[:slots]
    joined_ref, own_ref, other_ref, rest_ref = refs[slots:]
    side = lax.axis_index("rows") // slots
    half = slots // 2
    sums = [sum(ref[...] for ref in part_refs[:half]), sum(ref[...] for ref in part_refs[half:])]
    picked = jnp.concatenate(by_side(side, sums[0][:, :rank], sums[1][:, :rank]), axis=1)
    coef = dot(picked, joined_ref[0], (1, 1), True)
    own_ref[...], other_ref[...] = by_side(side, coef[:, :rank], coef[:, rank:])
    rest_ref[...] = (sums[0] + sums[1])[:, rank:]


def correct_kernel(levels, rank, own_ref, other_ref, rest_ref, mine_ref, theirs_ref, pair_mine_ref,
                   pair_theirs_ref, message_ref):
    core = lax.axis_index("rows") % 2
    grams = [jnp.concatenate(by_side(core, mine_ref[...], pair_mine_ref[...]), axis=0),
             jnp.concatenate(by_side(core, theirs_ref[...], pair_theirs_ref[...]), axis=0)]
    sides = [own_ref[...], other_ref[...]]
    pairs = below_pairs(levels)
    spots = [spot for spot, (_, below) in enumerate(pairs) if below == 0]
    pieces = []
    for level in range(1, levels):
        value = rest_ref[:, (level - 1) * rank:level * rank]
        lanes = slice(spots[level - 1] * rank, (spots[level - 1] + 1) * rank)
        for part, gram in zip(sides, grams):
            value = value - dot(part, gram[:, lanes], (1, 1), True)
        pieces.append(value)
    for spot, (_, below) in enumerate(pairs):
        if below > 0:
            lanes = slice(spot * rank, (spot + 1) * rank)
            pieces.append(grams[0][:, lanes] + grams[1][:, lanes])
    pack_message(message_ref, pieces)


def level_kernel(levels, level, share, sent_ref, got_ref, joined_ref, coef_ref, *message_ref):
    rank = sent_ref.shape[1]
    side = lax.axis_index("leaf") // 2 ** (level - 1) % 2
    more = levels - level
    values = []
    for ref in (sent_ref, got_ref):
        values.append([ref[pl.ds(i * share, share), :] for i in range(more)])
    picked = jnp.concatenate(by_side(side, values[0][0], values[1][0]), axis=1)
    coef = dot(picked, joined_ref[level], (1, 1), True)
    sides = by_side(side, coef[:, :rank], coef[:, rank:])
    coef_ref[...] = sides[0]
    if not message_ref:
        return
    pairs = below_pairs(levels, level)
    grams = []
    for ref in (sent_ref, got_ref):
        grams.append({pair: ref[pl.ds(more * share + spot * rank, rank), :] for spot, pair in enumerate(pairs)})
    pieces = []
    for upper in range(level + 1, levels):
        value = values[0][upper - level] + values[1][upper - level]
        for part, gram in zip(sides, grams):
            value = value - dot(part, gram[upper, level], (1, 1), True)
        pieces.append(value)
    for pair in pairs:
        if pair[1] > level:
            pieces.append(grams[0][pair] + grams[1][pair])
    pack_message(message_ref[0], pieces)


def pack_kernel(*refs):
    levels = len(refs) - 3
    other_ref, own_refs, own_out, other_out = refs[0], refs[1:-2], refs[-2], refs[-1]
    own = [ref[...] for ref in own_refs]
    own_out[...] = jnp.concatenate(own, axis=1)
    other_out[...] = jnp.concatenate([other_ref[...]] + own[1:], axis=1)


def expand_kernel(levels, per_step, width, slots, *refs):
    piece_refs = refs[:2 * slots]
    moved_ref, rhs_ref, left_ref, out_ref, flip_ref, factor_ref, out_buf, sems = refs[2 * slots:]
    share, kinds = piece_refs[0].shape
    tile = per_step * width
    steps = moved_ref.shape[0] // per_step
    me = lax.axis_index("rows")
    for slot in range(2 * slots):
        owner = me ^ slot
        flip_ref[pl.ds(pl.multiple_of(owner * share, share), share), :] = piece_refs[slot][...]
    high_part, low_part = halves(flip_ref[...].T)
    factor_ref[:kinds, :] = high_part
    factor_ref[kinds:, :] = low_part

    def copy(step):
        rows = pl.ds(pl.multiple_of(step * tile, tile), tile)
        return pltpu.make_async_copy(out_buf.at[rows], out_ref.at[rows], sems.at[step])

    def body(step, _):
        rows = pl.ds(pl.multiple_of(step * tile, tile), tile)
        left = jnp.concatenate([left_ref[l, rows, :] for l in range(levels)] * 2, axis=1)
        update = dot(left, factor_ref[...], (1, 0))
        for b in range(per_step):
            block = step * per_step + b
            rows = pl.ds(pl.multiple_of(block * width, width), width)
            first = dot(moved_ref[block], rhs_ref[rows, :], (1, 0))
            out_buf[rows, :] = first - update[b * width:(b + 1) * width]
        copy(step).start()
        return 0

    lax.fori_loop(0, steps, body, 0)
    for step in range(steps):
        copy(step).wait()


def settings(mib, micros):
    return dict(
        compiler_params=pltpu.CompilerParams(vmem_limit_bytes=mib * MIB),
        cost_estimate=pl.CostEstimate(flops=int(micros * 1.1e9), bytes_accessed=0, transcendentals=0),
    )


def floats(*shape):
    return jax.ShapeDtypeStruct(shape, jnp.float32)


def per_device(rhs, leaf_order, leaf_inv, right_basis, left_basis, rank_perm, joined):
    levels, rows, rank = right_basis.shape
    nblocks, width, _ = leaf_inv.shape
    columns = rhs.shape[1]
    leaves = lax.axis_size("leaf")
    count = lax.axis_size("rows")
    slots = count // 2
    kinds = levels * rank
    size = kinds - rank
    share = columns // count
    gram_lanes = len(below_pairs(levels)) * rank

    per_step = blocks_per_step(nblocks, 3)
    flipped, gram_keep, gram_send = pl.pallas_call(
        functools.partial(gram_kernel, levels, per_step, width),
        in_specs=[pl.BlockSpec(memory_space=pltpu.HBM)] * 2,
        out_shape=[jax.ShapeDtypeStruct((kinds, rows), jnp.bfloat16)] + [floats(rank // 2, gram_lanes)] * 2,
        scratch_shapes=[
            pltpu.VMEM((levels, rows, rank), jnp.bfloat16),
            pltpu.VMEM((levels - 1, rows, rank), jnp.bfloat16),
            pltpu.VMEM((size, size), jnp.float32),
            pltpu.SemaphoreType.DMA((2, nblocks // per_step)),
        ],
        name="gram",
        **settings(24, 3),
    )(pltpu.with_memory_space_constraint(right_basis, pltpu.HBM),
      pltpu.with_memory_space_constraint(left_basis, pltpu.HBM))
    gram_got = swap(gram_send, "rows", 1)

    factors, moved = pl.pallas_call(
        functools.partial(factor_kernel, per_step, width),
        out_shape=[
            jax.ShapeDtypeStruct((2 * kinds, rows), jnp.bfloat16),
            jax.ShapeDtypeStruct((nblocks, width, width), jnp.bfloat16),
        ],
        name="factor",
        **settings(24, 4),
    )(leaf_order, leaf_inv, flipped)

    def project(half, *grams):
        return pl.pallas_call(
            functools.partial(project_kernel, half),
            out_shape=[floats(rank // 2, gram_lanes)] * (len(grams) // 2) + [floats(slots // 2, share, kinds)] * 2,
            scratch_shapes=[pltpu.VMEM((columns // 2, kinds), jnp.float32)],
            name="project",
            **settings(24, 2.4),
        )(factors, rhs, *grams)

    gram, keep_a, send_a = project(0, gram_keep, gram_got)
    got_a = swap(send_a, "rows", 1)
    mask = 2
    while 2 * mask < slots:
        gram = gram + swap(gram, "rows", mask)
        mask *= 2
    gram_got = swap(gram, "rows", mask)
    keep_b, send_b = project(1)
    got_b = swap(send_b, "rows", 1)
    gram, *merged = pl.pallas_call(
        merge_kernel,
        out_shape=[floats(rank // 2, gram_lanes)] + [floats(share, kinds)] * slots,
        name="merge",
        **settings(8, 1),
    )(keep_a, got_a, keep_b, got_b, gram, gram_got)
    parts = [merged[0]] + [swap(merged[s], "rows", 2 * s) for s in range(1, slots)]
    gram_other = swap(gram, "rows", slots)
    grams = [gram, gram_other, swap(gram, "rows", 1), swap(gram_other, "rows", 1)]

    prepared = pl.pallas_call(
        functools.partial(prepare_kernel, levels),
        in_specs=[pl.BlockSpec(memory_space=pltpu.HBM), pl.BlockSpec()],
        out_shape=floats(levels, 2 * rank, 2 * rank),
        scratch_shapes=[pltpu.VMEM((levels, 2 * rank, 2 * rank), jnp.float32), pltpu.SemaphoreType.DMA((levels,))],
        name="prepare",
        **settings(8, 2),
    )(pltpu.with_memory_space_constraint(joined, pltpu.HBM), rank_perm)

    def message_shape(level):
        return floats((levels - level) * share + len(below_pairs(levels, level)) * rank, rank)

    own, other, rest = pl.pallas_call(
        functools.partial(node_kernel, rank, slots),
        out_shape=[floats(share, rank)] * 2 + [floats(share, size)],
        name="node",
        **settings(8, 1),
    )(*parts, prepared)
    message = pl.pallas_call(
        functools.partial(correct_kernel, levels, rank),
        out_shape=message_shape(1),
        name="correct",
        **settings(8, 1),
    )(own, other, rest, *grams)
    coefs = [own]
    for level in range(1, levels):
        last = level + 1 == levels
        arrived = swap(message, "leaf", 2 ** (level - 1))
        outs = pl.pallas_call(
            functools.partial(level_kernel, levels, level, share),
            out_shape=[floats(share, rank)] + ([] if last else [message_shape(level + 1)]),
            name=f"level{level}",
            **settings(8, 0.7),
        )(message, arrived, prepared)
        coefs.append(outs[0])
        message = outs[-1]
    own_pack, other_pack = pl.pallas_call(
        pack_kernel, out_shape=[floats(share, kinds)] * 2, name="pack", **settings(8, 0.2),
    )(other, *coefs)

    pieces = []
    for slot in range(slots):
        piece = own_pack if slot < slots // 2 else other_pack
        piece = swap(piece, "rows", 2 * slot) if slot > 0 else piece
        pieces += [piece, swap(piece, "rows", 1)]

    per_step = blocks_per_step(nblocks, 2)
    return pl.pallas_call(
        functools.partial(expand_kernel, levels, per_step, width, slots),
        out_specs=pl.BlockSpec(memory_space=pl.ANY),
        out_shape=floats(rows, columns),
        scratch_shapes=[
            pltpu.VMEM((columns, kinds), jnp.float32),
            pltpu.VMEM((2 * kinds, columns), jnp.bfloat16),
            pltpu.VMEM((rows, columns), jnp.float32),
            pltpu.SemaphoreType.DMA((nblocks // per_step,)),
        ],
        name="expand",
        **settings(32, 7),
    )(*pieces, moved, rhs, left_basis)


def solution(mesh):
    return jax.shard_map(
        per_device,
        mesh=mesh,
        in_specs=(
            P(("leaf", "rows"), None),
            P(("leaf", "rows"), None),
            P(("leaf", "rows"), None, None),
            P(None, ("leaf", "rows"), None),
            P(None, ("leaf", "rows"), None),
            P(),
            P(),
        ),
        out_specs=P(("leaf", "rows"), None),
        check_vma=False,
    )
```

time: 74.1 us -> 59.5 us (0.80)
  local copies, waits for them, and re-layouts: 10.1 us -> 0.03 us
  Pallas kernels: 25.7 us -> 23.5 us
  waiting for transfers between devices: 20.8 us -> 18.6 us
  starting transfers between devices: 16.2 us -> 17.2 us
    unnamed x26 -> x12, local copies, waits for them, and re-layouts: 10.1 us -> 0.03 us
    pallas_call x6 -> x9, Pallas kernels: 16.6 us -> 14.3 us  [the longest x2 4.21 us: project(): pl.pallas_call(functools.partial(project_kernel, half), out_shape=[floats...]
    ppermute x18 -> x19, waiting for transfers between devices: 20.8 us -> 18.6 us  [swap(): return lax.ppermute(value, axis, [(i, i ^ mask) for i in range(count)])]
    ppermute x18 -> x19, starting transfers between devices: 16.2 us -> 17.2 us  [swap(): return lax.ppermute(value, axis, [(i, i ^ mask) for i in range(count)])]
  transfers between devices with their start and end apart: 18 -> 19, of which waited for: 12 -> 9; matrix products, arithmetic and copies ran while one was open for 1% -> 0% of each run, Pallas kernels for 4% -> 17%
where the time goes in v4:
time: 59.5 us; the launch traced here: 59.4 us
  Pallas kernels  23.5 us (39%)
  waiting for transfers between devices  18.6 us (31%)
  starting transfers between devices  17.2 us (29%)
    ppermute x19, waiting for transfers between devices, swap(): return lax.ppermute(value, axis, [(i, i ^ mask) for i in range(count)])  18.6 us
    ppermute x19, starting transfers between devices, swap(): return lax.ppermute(value, axis, [(i, i ^ mask) for i in range(count)])  17.2 us
    pallas_call x1, Pallas kernels, per_device(): pl.pallas_call(functools.partial(expand_kernel, levels, per_step, width,...  7.77 us
    pallas_call x2, Pallas kernels, project(): pl.pallas_call(functools.partial(project_kernel, half), out_shape=[floats...  4.21 us
    pallas_call x1, Pallas kernels, per_device(): pl.pallas_call(functools.partial(factor_kernel, per_step, width), out_sha...  3.59 us
    pallas_call x1, Pallas kernels, per_device(): pl.pallas_call(functools.partial(gram_kernel, levels, per_step, width), i...  3.34 us
    pallas_call x1, Pallas kernels, per_device(): pl.pallas_call(functools.partial(prepare_kernel, levels), in_specs=[pl.Bl...  2.1 us
    pallas_call x2, Pallas kernels, per_device(): pl.pallas_call(functools.partial(level_kernel, levels, level, share), out...  1.38 us
  transfers between devices with their start and end apart: 19, of which 9 were waited for; matrix products, arithmetic and copies ran while one was open for 0% of the time, Pallas kernels for 17%

profile of v4, /device:TPU:0, one launch (start us, length us, event | category | flops | bytes accessed | tf_op | source)
XLA Modules:
  0.0 59.4 jit_solution(13913413589616021220)
XLA Ops:
  0.0 0.0 copy-start.2
  0.0 0.0 copy-start.1
  0.0 0.0 slice-start
  0.0 3.3 %gram.1 = (bf16[384,4608]{1,0:T(8,128)(2,1)S(1)}, f32[64,384]{1,0:T(8,128)S(1)}, f32[64,384]{1,0:T(8,128)S(1)}) custom-call(bf16[3,4608,128]{2,1,0:T(8,128)(2,1)} %right_ref.1, bf16[3,4608,128]{2,1,0:T(8,128)(2,1)} %refs_10_.1), custom_call_target="tpu_custom_call" | custom-call | flops 3300000000 | tf_op jit(solution)/shard_map/gram/pallas_call | solution.py:285
  3.4 0.5 collective-permute-start
  3.9 0.0 copy-done.2
  3.9 0.0 copy-done.1
  3.9 0.0 slice-start.1
  3.9 3.6 %factor.1 = (bf16[768,4608]{1,0:T(8,128)(2,1)S(1)}, bf16[18,256,256]{2,1,0:T(8,128)(2,1)S(1)}) custom-call(s32[18,256]{1,0:T(8,128)S(1)} %copy-done.2, bf16[18,256,256]{2,1,0:T(8,128)(2,1)S(1)} %copy-done.1, bf16[384,4608]{1,0:T(8,128)(2,1)S(1)} %get-tuple-element.27.flip_ref), custom_call_target="tpu_custom_call" | custom-call | flops 4400000000 | tf_op jit(solution)/shard_map/factor/pallas_call | solution.py:301
  7.5 0.0 slice-done
  7.5 0.0 slice-done.1
  7.5 2.1 %project.3 = (f32[2,64,384]{2,1,0:T(8,128)S(1)}, f32[2,64,384]{2,1,0:T(8,128)S(1)}) custom-call(bf16[768,4608]{1,0:T(8,128)(2,1)S(1)} %get-tuple-element.28.factor_ref, bf16[4608,512]{1,0:T(8,128)(2,1)S(1)} %bitcast.1), custom_call_target="tpu_custom_call" | custom-call | flops 2640000000 | tf_op jit(solution)/shard_map/project/pallas_call | solution.py:312
  9.6 0.1 collective-permute-start.2
  9.7 0.0 collective-permute-done.refs_1_
  9.7 2.1 %project.2 = (f32[64,384]{1,0:T(8,128)S(1)}, f32[2,64,384]{2,1,0:T(8,128)S(1)}, f32[2,64,384]{2,1,0:T(8,128)S(1)}) custom-call(bf16[768,4608]{1,0:T(8,128)(2,1)S(1)} %get-tuple-element.28.factor_ref, bf16[4608,512]{1,0:T(8,128)(2,1)S(1)} %bitcast.1, f32[64,384]{1,0:T(8,128)S(1)} %get-tuple-element.29.refs_0_, f32[64,384]{1,0:T(8,128)S(1)} %collective-permute-done.refs_1_), custom_call_target="tpu_custom_call" | custom-call | flops 2640000000 | tf_op jit(solution)/shard_map/project/pallas_call | solution.py:312
  11.8 0.0 copy-start.3
  11.9 0.5 collective-permute-start.1
  12.4 2.6 %collective-permute-start.3 = (f32[64,384]{1,0:T(8,128)S(1)}, f32[64,384]{1,0:T(8,128)S(1)}, u32[]{:S(2)}, u32[]{:S(2)}) collective-permute-start(f32[64,384]{1,0:T(8,128)S(1)} %get-tuple-element.35.mine_ref), channel_id=1, source_target_pairs={{0,2},{1,3},{2,0},{3,1},{4,6},{5,7},{6,4},{7,5},{8,10},{9,11},{10,... | collective-permute-start | bytes 294920 | tf_op jit(solution)/shard_map/ppermute | solution.py:29
  15.0 3.4 %collective-permute-done.3.got_ref = f32[64,384]{1,0:T(8,128)S(1)} collective-permute-done((f32[64,384]{1,0:T(8,128)S(1)}, f32[64,384]{1,0:T(8,128)S(1)}, u32[]{:S(2)}, u32[]{:S(2)}) %collective-permute-start.3) | collective-permute-done | bytes 98336 | tf_op jit(solution)/shard_map/ppermute | solution.py:29
  18.3 0.0 collective-permute-done.2.got_b
  18.3 0.0 collective-permute-done.1.got_a
  18.3 0.1 merge.1
  18.4 1.8 %collective-permute-start.4 = (f32[64,384]{1,0:T(8,128)S(1)}, f32[64,384]{1,0:T(8,128)S(1)}, u32[]{:S(2)}, u32[]{:S(2)}) collective-permute-start(f32[64,384]{1,0:T(8,128)S(1)} %get-tuple-element.37), channel_id=1, source_target_pairs={{0,2},{1,3},{2,0},{3,1},{4,6},{5,7},{6,4},{7,5},{8,10},{9,11},{10,... | collective-permute-start | bytes 294920 | tf_op jit(solution)/shard_map/ppermute | solution.py:29
  20.3 1.5 %collective-permute-start.5 = (f32[64,384]{1,0:T(8,128)S(1)}, f32[64,384]{1,0:T(8,128)S(1)}, u32[]{:S(2)}, u32[]{:S(2)}) collective-permute-start(f32[64,384]{1,0:T(8,128)S(1)} %get-tuple-element.38), channel_id=1, source_target_pairs={{0,4},{1,5},{2,6},{3,7},{4,0},{5,1},{6,2},{7,3},{8,12},{9,13},{10,... | collective-permute-start | bytes 294920 | tf_op jit(solution)/shard_map/ppermute | solution.py:29
  21.8 0.2 collective-permute-start.6
  22.0 1.8 %collective-permute-start.7 = (f32[64,384]{1,0:T(8,128)S(1)}, f32[64,384]{1,0:T(8,128)S(1)}, u32[]{:S(2)}, u32[]{:S(2)}) collective-permute-start(f32[64,384]{1,0:T(8,128)S(1)} %get-tuple-element.43.mine_ref), channel_id=1, source_target_pairs={{0,4},{1,5},{2,6},{3,7},{4,0},{5,1},{6,2},{7,3},{8,12},{9,13},{10,... | collective-permute-start | bytes 294920 | tf_op jit(solution)/shard_map/ppermute | solution.py:29
  23.8 0.0 copy-done.3
  23.8 2.1 %prepare.1.refs_4_.joined_ref = f32[3,256,256]{2,1,0:T(8,128)S(1)} custom-call(f32[7,256,256]{2,1,0:T(8,128)} %joined_ref.1, s32[3,128]{1,0:T(4,128)S(1)} %copy-done.3), custom_call_target="tpu_custom_call" | custom-call | flops 2200000000 | tf_op jit(solution)/shard_map/prepare/pallas_call | solution.py:339
  25.9 0.1 collective-permute-start.8
  26.0 2.9 %collective-permute-done.7.theirs_ref = f32[64,384]{1,0:T(8,128)S(1)} collective-permute-done((f32[64,384]{1,0:T(8,128)S(1)}, f32[64,384]{1,0:T(8,128)S(1)}, u32[]{:S(2)}, u32[]{:S(2)}) %collective-permute-start.7) | collective-permute-done | bytes 98336 | tf_op jit(solution)/shard_map/ppermute | solution.py:29
  28.9 0.0 collective-permute-start.9
  28.9 0.0 collective-permute-done.4.refs_1_
  28.9 0.0 collective-permute-done.5.refs_2_
  28.9 0.0 collective-permute-done.6.refs_3_
  28.9 0.4 node.1
  29.3 0.0 collective-permute-done.8.pair_mine_ref
  29.3 0.9 %collective-permute-done.9.pair_theirs_ref = f32[64,384]{1,0:T(8,128)S(1)} collective-permute-done((f32[64,384]{1,0:T(8,128)S(1)}, f32[64,384]{1,0:T(8,128)S(1)}, u32[]{:S(2)}, u32[]{:S(2)}) %collective-permute-start.9) | collective-permute-done | bytes 98336 | tf_op jit(solution)/shard_map/ppermute | solution.py:29
  30.2 0.6 %correct.1.sent_ref = f32[256,128]{1,0:T(8,128)S(1)} custom-call(f32[64,128]{1,0:T(8,128)S(1)} %get-tuple-element.41.own_ref.refs_1_, f32[64,128]{1,0:T(8,128)S(1)} %get-tuple-element.40.other_ref.refs_0_, f32[64,256]{1,0:T(8,128)S(1)} %get-tuple-element.42.rest_ref, f32[64,384]{1,0:T(8,128)S(1)} %get-tuple-element.43.mine_ref, ...), custom_call_target="tpu_custom_call" | custom-call | flops 1100000000 | tf_op jit(solution)/shard_map/correct/pallas_call | solution.py:357
  30.8 0.0 copy-start
  30.8 1.7 %collective-permute-start.10 = (f32[256,128]{1,0:T(8,128)S(1)}, f32[256,128]{1,0:T(8,128)S(1)}, u32[]{:S(2)}, u32[]{:S(2)}) collective-permute-start(f32[256,128]{1,0:T(8,128)S(1)} %correct.1.sent_ref), channel_id=1, source_target_pairs={{0,8},{8,0},{16,24},{24,16},{1,9},{9,1},{17,25},{25,17},{2,10},{10... | collective-permute-start | bytes 393224 | tf_op jit(solution)/shard_map/ppermute | solution.py:29
  32.5 3.9 %collective-permute-done.10.got_ref = f32[256,128]{1,0:T(8,128)S(1)} collective-permute-done((f32[256,128]{1,0:T(8,128)S(1)}, f32[256,128]{1,0:T(8,128)S(1)}, u32[]{:S(2)}, u32[]{:S(2)}) %collective-permute-start.10) | collective-permute-done | bytes 131104 | tf_op jit(solution)/shard_map/ppermute | solution.py:29
  36.4 1.0 %level1.1 = (f32[64,128]{1,0:T(8,128)S(1)}, f32[64,128]{1,0:T(8,128)S(1)}) custom-call(f32[256,128]{1,0:T(8,128)S(1)} %correct.1.sent_ref, f32[256,128]{1,0:T(8,128)S(1)} %collective-permute-done.10.got_ref, f32[3,256,256]{2,1,0:T(8,128)S(1)} %prepare.1.refs_4_.joined_ref), custom_call_target="tpu_custom_call" | custom-call | flops 770000000 | tf_op jit(solution)/shard_map/level1/pallas_call | solution.py:367
  37.4 2.7 %collective-permute-start.11 = (f32[64,128]{1,0:T(8,128)S(1)}, f32[64,128]{1,0:T(8,128)S(1)}, u32[]{:S(2)}, u32[]{:S(2)}) collective-permute-start(f32[64,128]{1,0:T(8,128)S(1)} %get-tuple-element.45.sent_ref), channel_id=1, source_target_pairs={{0,16},{8,24},{16,0},{24,8},{1,17},{9,25},{17,1},{25,9},{2,18},{10... | collective-permute-start | bytes 98312 | tf_op jit(solution)/shard_map/ppermute | solution.py:29
  40.2 2.1 %collective-permute-done.11.got_ref = f32[64,128]{1,0:T(8,128)S(1)} collective-permute-done((f32[64,128]{1,0:T(8,128)S(1)}, f32[64,128]{1,0:T(8,128)S(1)}, u32[]{:S(2)}, u32[]{:S(2)}) %collective-permute-start.11) | collective-permute-done | bytes 32800 | tf_op jit(solution)/shard_map/ppermute | solution.py:29
  42.3 0.4 level2.1.refs_3_
  42.7 0.7 %collective-permute-start.13 = (f32[64,384]{1,0:T(8,128)S(1)}, f32[64,384]{1,0:T(8,128)S(1)}, u32[]{:S(2)}, u32[]{:S(2)}) collective-permute-start(f32[64,384]{1,0:T(8,128)S(1)} %get-tuple-element.46.refs_0_), channel_id=1, source_target_pairs={{0,2},{1,3},{2,0},{3,1},{4,6},{5,7},{6,4},{7,5},{8,10},{9,11},{10,... | collective-permute-start | bytes 294920 | tf_op jit(solution)/shard_map/ppermute | solution.py:29
  43.4 1.4 %collective-permute-start.15 = (f32[64,384]{1,0:T(8,128)S(1)}, f32[64,384]{1,0:T(8,128)S(1)}, u32[]{:S(2)}, u32[]{:S(2)}) collective-permute-start(f32[64,384]{1,0:T(8,128)S(1)} %get-tuple-element.47), channel_id=1, source_target_pairs={{0,4},{1,5},{2,6},{3,7},{4,0},{5,1},{6,2},{7,3},{8,12},{9,13},{10,... | collective-permute-start | bytes 294920 | tf_op jit(solution)/shard_map/ppermute | solution.py:29
  44.8 1.5 %collective-permute-start.17 = (f32[64,384]{1,0:T(8,128)S(1)}, f32[64,384]{1,0:T(8,128)S(1)}, u32[]{:S(2)}, u32[]{:S(2)}) collective-permute-start(f32[64,384]{1,0:T(8,128)S(1)} %get-tuple-element.47), channel_id=1, source_target_pairs={{0,6},{1,7},{2,4},{3,5},{4,2},{5,3},{6,0},{7,1},{8,14},{9,15},{10,... | collective-permute-start | bytes 294920 | tf_op jit(solution)/shard_map/ppermute | solution.py:29
  46.2 0.0 collective-permute-start.12
  46.3 1.1 %collective-permute-done.13.refs_2_ = f32[64,384]{1,0:T(8,128)S(1)} collective-permute-done((f32[64,384]{1,0:T(8,128)S(1)}, f32[64,384]{1,0:T(8,128)S(1)}, u32[]{:S(2)}, u32[]{:S(2)}) %collective-permute-start.13) | collective-permute-done | bytes 98336 | tf_op jit(solution)/shard_map/ppermute | solution.py:29
  47.4 0.0 collective-permute-start.14
  47.4 0.6 %collective-permute-done.15.refs_4_ = f32[64,384]{1,0:T(8,128)S(1)} collective-permute-done((f32[64,384]{1,0:T(8,128)S(1)}, f32[64,384]{1,0:T(8,128)S(1)}, u32[]{:S(2)}, u32[]{:S(2)}) %collective-permute-start.15) | collective-permute-done | bytes 98336 | tf_op jit(solution)/shard_map/ppermute | solution.py:29
  48.0 0.0 collective-permute-start.16
  48.0 2.3 %collective-permute-done.17.refs_6_ = f32[64,384]{1,0:T(8,128)S(1)} collective-permute-done((f32[64,384]{1,0:T(8,128)S(1)}, f32[64,384]{1,0:T(8,128)S(1)}, u32[]{:S(2)}, u32[]{:S(2)}) %collective-permute-start.17) | collective-permute-done | bytes 98336 | tf_op jit(solution)/shard_map/ppermute | solution.py:29
  50.3 0.0 collective-permute-start.18
  50.3 0.0 collective-permute-done.12.refs_1_
  50.3 0.0 collective-permute-done.14.refs_3_
  50.3 0.0 collective-permute-done.16.refs_5_
  50.3 1.3 %collective-permute-done.18.refs_7_ = f32[64,384]{1,0:T(8,128)S(1)} collective-permute-done((f32[64,384]{1,0:T(8,128)S(1)}, f32[64,384]{1,0:T(8,128)S(1)}, u32[]{:S(2)}, u32[]{:S(2)}) %collective-permute-start.18) | collective-permute-done | bytes 98336 | tf_op jit(solution)/shard_map/ppermute | solution.py:29
  51.6 0.0 copy-done
  51.6 7.8 %expand.1 = f32[4608,512]{1,0:T(8,128)} custom-call(f32[64,384]{1,0:T(8,128)S(1)} %get-tuple-element.46.refs_0_, f32[64,384]{1,0:T(8,128)S(1)} %collective-permute-done.12.refs_1_, f32[64,384]{1,0:T(8,128)S(1)} %collective-permute-done.13.refs_2_, f32[64,384]{1,0:T(8,128)S(1)} %collective-permute-done.14.refs_3_, ...), custom_call_target="tpu_custom_call" | custom-call | flops 7699999744 | tf_op jit(solution)/shard_map/expand/pallas_call | solution.py:386
  (2 shorter events, 0.0 us)
Async XLA Ops:
  0.0 3.9 %copy-start.2 = (s32[18,256]{1,0:T(8,128)S(1)}, s32[18,256]{1,0:T(8,128)}, u32[]{:S(2)}) copy-start(s32[18,256]{1,0:T(8,128)} %order_ref.1) | copy-start | bytes 55300
  0.0 3.9 %copy-start.1 = (bf16[18,256,256]{2,1,0:T(8,128)(2,1)S(1)}, bf16[18,256,256]{2,1,0:T(8,128)(2,1)}, u32[]{:S(2)}) copy-start(bf16[18,256,256]{2,1,0:T(8,128)(2,1)} %inv_ref.1) | copy-start | bytes 7077892
  0.0 7.5 %slice-start = ((s8[4718592]{0:T(1024)(128)(4,1)}), s8[4194304]{0:T(1024)(128)(4,1)S(1)}, s32[]{:S(2)}) async-start(s8[4718592]{0:T(1024)(128)(4,1)} %bitcast), calls=%async_computation | async-start | bytes 8388608
  3.4 6.4 %collective-permute-start = (f32[64,384]{1,0:T(8,128)S(1)}, f32[64,384]{1,0:T(8,128)S(1)}, u32[]{:S(2)}, u32[]{:S(2)}) collective-permute-start(f32[64,384]{1,0:T(8,128)S(1)} %get-tuple-element.30), channel_id=1, source_target_pairs={{0,1},{1,0},{2,3},{3,2},{4,5},{5,4},{6,7},{7,6},{8,9},{9,8},{10,11... | collective-permute-start | bytes 294920 | tf_op jit(solution)/shard_map/ppermute | solution.py:29
  3.9 3.6 %slice-start.1 = ((s8[4718592]{0:T(1024)(128)(4,1)}), s8[524288]{0:T(1024)(128)(4,1)S(1)}, s32[]{:S(2)}) async-start(s8[4718592]{0:T(1024)(128)(4,1)} %bitcast), calls=%async_computation.1 | async-start | bytes 1048576
  9.6 8.7 %collective-permute-start.2 = (f32[2,64,384]{2,1,0:T(8,128)S(1)}, f32[2,64,384]{2,1,0:T(8,128)S(1)}, u32[]{:S(2)}, u32[]{:S(2)}) collective-permute-start(f32[2,64,384]{2,1,0:T(8,128)S(1)} %get-tuple-element.34), channel_id=1, source_target_pairs={{0,1},{1,0},{2,3},{3,2},{4,5},{5,4},{6,7},{7,6},{8,9},{9,8},{10,11... | collective-permute-start | bytes 589832 | tf_op jit(solution)/shard_map/ppermute | solution.py:29
  11.8 11.9 %copy-start.3 = (s32[3,128]{1,0:T(4,128)S(1)}, s32[3,128]{1,0:T(4,128)}, u32[]{:S(2)}) copy-start(s32[3,128]{1,0:T(4,128)} %perm_ref.1) | copy-start | bytes 4612
  11.9 6.5 %collective-permute-start.1 = (f32[2,64,384]{2,1,0:T(8,128)S(1)}, f32[2,64,384]{2,1,0:T(8,128)S(1)}, u32[]{:S(2)}, u32[]{:S(2)}) collective-permute-start(f32[2,64,384]{2,1,0:T(8,128)S(1)} %get-tuple-element.32), channel_id=1, source_target_pairs={{0,1},{1,0},{2,3},{3,2},{4,5},{5,4},{6,7},{7,6},{8,9},{9,8},{10,11... | collective-permute-start | bytes 589832 | tf_op jit(solution)/shard_map/ppermute | solution.py:29
  12.4 6.0 %collective-permute-start.3 = (f32[64,384]{1,0:T(8,128)S(1)}, f32[64,384]{1,0:T(8,128)S(1)}, u32[]{:S(2)}, u32[]{:S(2)}) collective-permute-start(f32[64,384]{1,0:T(8,128)S(1)} %get-tuple-element.35.mine_ref), channel_id=1, source_target_pairs={{0,2},{1,3},{2,0},{3,1},{4,6},{5,7},{6,4},{7,5},{8,10},{9,11},{10,... | collective-permute-start | bytes 294920 | tf_op jit(solution)/shard_map/ppermute | solution.py:29
  18.4 10.4 %collective-permute-start.4 = (f32[64,384]{1,0:T(8,128)S(1)}, f32[64,384]{1,0:T(8,128)S(1)}, u32[]{:S(2)}, u32[]{:S(2)}) collective-permute-start(f32[64,384]{1,0:T(8,128)S(1)} %get-tuple-element.37), channel_id=1, source_target_pairs={{0,2},{1,3},{2,0},{3,1},{4,6},{5,7},{6,4},{7,5},{8,10},{9,11},{10,... | collective-permute-start | bytes 294920 | tf_op jit(solution)/shard_map/ppermute | solution.py:29
  20.3 8.6 %collective-permute-start.5 = (f32[64,384]{1,0:T(8,128)S(1)}, f32[64,384]{1,0:T(8,128)S(1)}, u32[]{:S(2)}, u32[]{:S(2)}) collective-permute-start(f32[64,384]{1,0:T(8,128)S(1)} %get-tuple-element.38), channel_id=1, source_target_pairs={{0,4},{1,5},{2,6},{3,7},{4,0},{5,1},{6,2},{7,3},{8,12},{9,13},{10,... | collective-permute-start | bytes 294920 | tf_op jit(solution)/shard_map/ppermute | solution.py:29
  21.8 7.1 %collective-permute-start.6 = (f32[64,384]{1,0:T(8,128)S(1)}, f32[64,384]{1,0:T(8,128)S(1)}, u32[]{:S(2)}, u32[]{:S(2)}) collective-permute-start(f32[64,384]{1,0:T(8,128)S(1)} %get-tuple-element.39), channel_id=1, source_target_pairs={{0,6},{1,7},{2,4},{3,5},{4,2},{5,3},{6,0},{7,1},{8,14},{9,15},{10,... | collective-permute-start | bytes 294920 | tf_op jit(solution)/shard_map/ppermute | solution.py:29
  22.0 6.9 %collective-permute-start.7 = (f32[64,384]{1,0:T(8,128)S(1)}, f32[64,384]{1,0:T(8,128)S(1)}, u32[]{:S(2)}, u32[]{:S(2)}) collective-permute-start(f32[64,384]{1,0:T(8,128)S(1)} %get-tuple-element.43.mine_ref), channel_id=1, source_target_pairs={{0,4},{1,5},{2,6},{3,7},{4,0},{5,1},{6,2},{7,3},{8,12},{9,13},{10,... | collective-permute-start | bytes 294920 | tf_op jit(solution)/shard_map/ppermute | solution.py:29
  25.9 3.4 %collective-permute-start.8 = (f32[64,384]{1,0:T(8,128)S(1)}, f32[64,384]{1,0:T(8,128)S(1)}, u32[]{:S(2)}, u32[]{:S(2)}) collective-permute-start(f32[64,384]{1,0:T(8,128)S(1)} %get-tuple-element.43.mine_ref), channel_id=1, source_target_pairs={{0,1},{1,0},{2,3},{3,2},{4,5},{5,4},{6,7},{7,6},{8,9},{9,8},{10,11... | collective-permute-start | bytes 294920 | tf_op jit(solution)/shard_map/ppermute | solution.py:29
  28.9 1.3 %collective-permute-start.9 = (f32[64,384]{1,0:T(8,128)S(1)}, f32[64,384]{1,0:T(8,128)S(1)}, u32[]{:S(2)}, u32[]{:S(2)}) collective-permute-start(f32[64,384]{1,0:T(8,128)S(1)} %collective-permute-done.7.theirs_ref), channel_id=1, source_target_pairs={{0,1},{1,0},{2,3},{3,2},{4,5},{5,4},{6,7},{7,6},{8,9},{9,8},{10,11... | collective-permute-start | bytes 294920 | tf_op jit(solution)/shard_map/ppermute | solution.py:29
  30.8 20.8 %copy-start = (bf16[3,4608,128]{2,1,0:T(8,128)(2,1)S(1)}, bf16[3,4608,128]{2,1,0:T(8,128)(2,1)}, u32[]{:S(2)}) copy-start(bf16[3,4608,128]{2,1,0:T(8,128)(2,1)} %refs_10_.1) | copy-start | bytes 10616836
  30.8 5.6 %collective-permute-start.10 = (f32[256,128]{1,0:T(8,128)S(1)}, f32[256,128]{1,0:T(8,128)S(1)}, u32[]{:S(2)}, u32[]{:S(2)}) collective-permute-start(f32[256,128]{1,0:T(8,128)S(1)} %correct.1.sent_ref), channel_id=1, source_target_pairs={{0,8},{8,0},{16,24},{24,16},{1,9},{9,1},{17,25},{25,17},{2,10},{10... | collective-permute-start | bytes 393224 | tf_op jit(solution)/shard_map/ppermute | solution.py:29
  37.4 4.9 %collective-permute-start.11 = (f32[64,128]{1,0:T(8,128)S(1)}, f32[64,128]{1,0:T(8,128)S(1)}, u32[]{:S(2)}, u32[]{:S(2)}) collective-permute-start(f32[64,128]{1,0:T(8,128)S(1)} %get-tuple-element.45.sent_ref), channel_id=1, source_target_pairs={{0,16},{8,24},{16,0},{24,8},{1,17},{9,25},{17,1},{25,9},{2,18},{10... | collective-permute-start | bytes 98312 | tf_op jit(solution)/shard_map/ppermute | solution.py:29
  42.7 4.7 %collective-permute-start.13 = (f32[64,384]{1,0:T(8,128)S(1)}, f32[64,384]{1,0:T(8,128)S(1)}, u32[]{:S(2)}, u32[]{:S(2)}) collective-permute-start(f32[64,384]{1,0:T(8,128)S(1)} %get-tuple-element.46.refs_0_), channel_id=1, source_target_pairs={{0,2},{1,3},{2,0},{3,1},{4,6},{5,7},{6,4},{7,5},{8,10},{9,11},{10,... | collective-permute-start | bytes 294920 | tf_op jit(solution)/shard_map/ppermute | solution.py:29
  43.4 4.6 %collective-permute-start.15 = (f32[64,384]{1,0:T(8,128)S(1)}, f32[64,384]{1,0:T(8,128)S(1)}, u32[]{:S(2)}, u32[]{:S(2)}) collective-permute-start(f32[64,384]{1,0:T(8,128)S(1)} %get-tuple-element.47), channel_id=1, source_target_pairs={{0,4},{1,5},{2,6},{3,7},{4,0},{5,1},{6,2},{7,3},{8,12},{9,13},{10,... | collective-permute-start | bytes 294920 | tf_op jit(solution)/shard_map/ppermute | solution.py:29
  44.8 5.5 %collective-permute-start.17 = (f32[64,384]{1,0:T(8,128)S(1)}, f32[64,384]{1,0:T(8,128)S(1)}, u32[]{:S(2)}, u32[]{:S(2)}) collective-permute-start(f32[64,384]{1,0:T(8,128)S(1)} %get-tuple-element.47), channel_id=1, source_target_pairs={{0,6},{1,7},{2,4},{3,5},{4,2},{5,3},{6,0},{7,1},{8,14},{9,15},{10,... | collective-permute-start | bytes 294920 | tf_op jit(solution)/shard_map/ppermute | solution.py:29
  46.2 4.0 %collective-permute-start.12 = (f32[64,384]{1,0:T(8,128)S(1)}, f32[64,384]{1,0:T(8,128)S(1)}, u32[]{:S(2)}, u32[]{:S(2)}) collective-permute-start(f32[64,384]{1,0:T(8,128)S(1)} %get-tuple-element.46.refs_0_), channel_id=1, source_target_pairs={{0,1},{1,0},{2,3},{3,2},{4,5},{5,4},{6,7},{7,6},{8,9},{9,8},{10,11... | collective-permute-start | bytes 294920 | tf_op jit(solution)/shard_map/ppermute | solution.py:29
  47.4 2.9 %collective-permute-start.14 = (f32[64,384]{1,0:T(8,128)S(1)}, f32[64,384]{1,0:T(8,128)S(1)}, u32[]{:S(2)}, u32[]{:S(2)}) collective-permute-start(f32[64,384]{1,0:T(8,128)S(1)} %collective-permute-done.13.refs_2_), channel_id=1, source_target_pairs={{0,1},{1,0},{2,3},{3,2},{4,5},{5,4},{6,7},{7,6},{8,9},{9,8},{10,11... | collective-permute-start | bytes 294920 | tf_op jit(solution)/shard_map/ppermute | solution.py:29
  48.0 2.3 %collective-permute-start.16 = (f32[64,384]{1,0:T(8,128)S(1)}, f32[64,384]{1,0:T(8,128)S(1)}, u32[]{:S(2)}, u32[]{:S(2)}) collective-permute-start(f32[64,384]{1,0:T(8,128)S(1)} %collective-permute-done.15.refs_4_), channel_id=1, source_target_pairs={{0,1},{1,0},{2,3},{3,2},{4,5},{5,4},{6,7},{7,6},{8,9},{9,8},{10,11... | collective-permute-start | bytes 294920 | tf_op jit(solution)/shard_map/ppermute | solution.py:29
  50.3 1.3 %collective-permute-start.18 = (f32[64,384]{1,0:T(8,128)S(1)}, f32[64,384]{1,0:T(8,128)S(1)}, u32[]{:S(2)}, u32[]{:S(2)}) collective-permute-start(f32[64,384]{1,0:T(8,128)S(1)} %collective-permute-done.17.refs_6_), channel_id=1, source_target_pairs={{0,1},{1,0},{2,3},{3,2},{4,5},{5,4},{6,7},{7,6},{8,9},{9,8},{10,11... | collective-permute-start | bytes 294920 | tf_op jit(solution)/shard_map/ppermute | solution.py:29

commit v5 on v4

--- a/solution.py
+++ b/solution.py
@@ -75,52 +75,70 @@
             ref[:, lanes] = gram_ref[rows, pl.ds(below * rank, rank)]
 
 
-def factor_kernel(per_step, width, order_ref, inv_ref, flip_ref, factor_ref, moved_ref):
+def permute_kernel(per_step, width, order_ref, inv_ref, moved_ref):
+    place = lax.broadcasted_iota(jnp.int32, (width, width), 0)
+
+    def body(step, _):
+        for b in range(per_step):
+            block = step * per_step + b
+            chosen = (place == order_ref[pl.ds(block, 1), :]).astype(jnp.float32).astype(jnp.bfloat16)
+            moved_ref[block] = dot(inv_ref[block], chosen, (1, 1)).astype(jnp.bfloat16)
+        return 0
+
+    lax.fori_loop(0, inv_ref.shape[0] // per_step, body, 0)
+
+
+def weigh_kernel(per_step, width, moved_ref, flip_ref, after_ref, factor_ref):
     kinds = flip_ref.shape[0]
-    place = lax.broadcasted_iota(jnp.int32, (width, width), 0)
 
     def body(step, _):
-        blocks = [step * per_step + b for b in range(per_step)]
-        chosen = [(place == order_ref[pl.ds(block, 1), :]).astype(jnp.float32).astype(jnp.bfloat16)
-                  for block in blocks]
-        moved = [dot(inv_ref[block], pick, (1, 1)).astype(jnp.bfloat16) for block, pick in zip(blocks, chosen)]
-        for block, inverse in zip(blocks, moved):
-            moved_ref[block] = inverse
+        for b in range(per_step):
+            block = step * per_step + b
             lanes = pl.ds(pl.multiple_of(block * width, width), width)
-            high_part, low_part = halves(dot(flip_ref[:, lanes], inverse, (1, 0)))
+            high_part, low_part = halves(dot(flip_ref[:, lanes], moved_ref[block], (1, 0)))
             factor_ref[:kinds, lanes] = high_part
             factor_ref[kinds:, lanes] = low_part
         return 0
 
-    lax.fori_loop(0, inv_ref.shape[0] // per_step, body, 0)
-
-
-def project_kernel(half, factor_ref, rhs_ref, *refs):
+    lax.fori_loop(0, moved_ref.shape[0] // per_step, body, 0)
+
+
+def solve_kernel(per_step, width, moved_ref, rhs_ref, after_ref, out_ref):
+    def body(step, _):
+        for b in range(per_step):
+            block = step * per_step + b
+            rows = pl.ds(pl.multiple_of(block * width, width), width)
+            out_ref[rows, :] = dot(moved_ref[block], rhs_ref[rows, :], (1, 0))
+        return 0
+
+    lax.fori_loop(0, moved_ref.shape[0] // per_step, body, 0)
+
+
+def half_lanes(far, me, count, part):
+    side = me // (count // 2)
+    return pl.ds(pl.multiple_of((1 - side if far else side) * part, part), part)
+
+
+def project_kernel(far, factor_ref, rhs_ref, after_ref, keep_ref, send_ref, total_ref):
     kinds = factor_ref.shape[0] // 2
-    keep_ref, send_ref, total_ref = refs[-3:]
-    spots, share, _ = keep_ref.shape
+    slots, share, _ = keep_ref.shape
     part = total_ref.shape[0]
-    total = dot(factor_ref[...], rhs_ref[:, half * part:(half + 1) * part], (1, 0))
+    me = lax.axis_index("rows")
+    total = dot(factor_ref[...], rhs_ref[:, half_lanes(far, me, 4 * slots, part)], (1, 0))
     total_ref[...] = (total[:kinds] + total[kinds:]).T
-    core = lax.axis_index("rows") % 2
-    for spot in range(spots):
-        for ref, owner in ((keep_ref, 2 * spot + core), (send_ref, 2 * spot + 1 - core)):
-            ref[spot] = total_ref[pl.ds(pl.multiple_of(owner * share, share), share), :]
-    if len(refs) > 3:
-        mine_ref, got_ref, gram_ref = refs[:-3][0], refs[:-3][1], refs[:-3][2]
-        gram_ref[...] = mine_ref[...] + got_ref[...]
-
-
-def merge_kernel(keep_a, got_a, keep_b, got_b, mine_ref, got_ref, gram_ref, *out_refs):
-    chip = lax.axis_index("rows") // 2
-    slots = len(out_refs)
+    for slot in range(slots):
+        for ref, mask in ((keep_ref, 2 * slot), (send_ref, 2 * slot + 1)):
+            owner = (me ^ mask) % (2 * slots)
+            ref[slot] = total_ref[pl.ds(pl.multiple_of(owner * share, share), share), :]
+
+
+def merge_kernel(keep_ref, got_ref, *out_refs):
     for slot, out_ref in enumerate(out_refs):
-        owner = chip ^ slot
-        spot = owner % (slots // 2)
-        first = keep_a[spot] + got_a[spot]
-        second = keep_b[spot] + got_b[spot]
-        out_ref[...] = jnp.where(owner < slots // 2, first, second)
-    gram_ref[...] = mine_ref[...] + got_ref[...]
+        out_ref[...] = keep_ref[slot] + got_ref[slot]
+
+
+def add_kernel(mine_ref, got_ref, out_ref):
+    out_ref[...] = mine_ref[...] + got_ref[...]
 
 
 def prepare_kernel(levels, joined_ref, perm_ref, out_ref, joined_buf, sems):
@@ -169,20 +187,15 @@
     core = lax.axis_index("rows") % 2
     grams = [jnp.concatenate(by_side(core, mine_ref[...], pair_mine_ref[...]), axis=0),
              jnp.concatenate(by_side(core, theirs_ref[...], pair_theirs_ref[...]), axis=0)]
-    sides = [own_ref[...], other_ref[...]]
     pairs = below_pairs(levels)
-    spots = [spot for spot, (_, below) in enumerate(pairs) if below == 0]
-    pieces = []
-    for level in range(1, levels):
-        value = rest_ref[:, (level - 1) * rank:level * rank]
-        lanes = slice(spots[level - 1] * rank, (spots[level - 1] + 1) * rank)
-        for part, gram in zip(sides, grams):
-            value = value - dot(part, gram[:, lanes], (1, 1), True)
-        pieces.append(value)
-    for spot, (_, below) in enumerate(pairs):
-        if below > 0:
-            lanes = slice(spot * rank, (spot + 1) * rank)
-            pieces.append(grams[0][:, lanes] + grams[1][:, lanes])
+    lanes = {pair: slice(spot * rank, (spot + 1) * rank) for spot, pair in enumerate(pairs)}
+    joint = jnp.concatenate(
+        [jnp.concatenate([gram[:, lanes[level, 0]] for gram in grams], axis=1) for level in range(1, levels)], axis=0)
+    rest = rest_ref[...] - dot(jnp.concatenate([own_ref[...], other_ref[...]], axis=1), joint, (1, 1), True)
+    pieces = [rest[:, level * rank:(level + 1) * rank] for level in range(levels - 1)]
+    for pair in pairs:
+        if pair[1] > 0:
+            pieces.append(grams[0][:, lanes[pair]] + grams[1][:, lanes[pair]])
     pack_message(message_ref, pieces)
 
 
@@ -203,12 +216,12 @@
     grams = []
     for ref in (sent_ref, got_ref):
         grams.append({pair: ref[pl.ds(more * share + spot * rank, rank), :] for spot, pair in enumerate(pairs)})
-    pieces = []
-    for upper in range(level + 1, levels):
-        value = values[0][upper - level] + values[1][upper - level]
-        for part, gram in zip(sides, grams):
-            value = value - dot(part, gram[upper, level], (1, 1), True)
-        pieces.append(value)
+    uppers = list(range(level + 1, levels))
+    joint = jnp.concatenate(
+        [jnp.concatenate([gram[upper, level] for gram in grams], axis=1) for upper in uppers], axis=0)
+    change = dot(jnp.concatenate(sides, axis=1), joint, (1, 1), True)
+    pieces = [values[0][upper - level] + values[1][upper - level] - change[:, i * rank:(i + 1) * rank]
+              for i, upper in enumerate(uppers)]
     for pair in pairs:
         if pair[1] > level:
             pieces.append(grams[0][pair] + grams[1][pair])
@@ -223,15 +236,17 @@
     other_out[...] = jnp.concatenate([other_ref[...]] + own[1:], axis=1)
 
 
-def expand_kernel(levels, per_step, width, slots, *refs):
+def expand_kernel(far, levels, per_step, width, slots, *refs):
     piece_refs = refs[:2 * slots]
-    moved_ref, rhs_ref, left_ref, out_ref, flip_ref, factor_ref, out_buf, sems = refs[2 * slots:]
+    first_ref, left_ref = refs[2 * slots:2 * slots + 2]
+    out_ref, flip_ref, factor_ref, out_buf, sems = refs[-5:]
     share, kinds = piece_refs[0].shape
     tile = per_step * width
-    steps = moved_ref.shape[0] // per_step
+    steps = out_buf.shape[0] // tile
     me = lax.axis_index("rows")
+    lanes = half_lanes(far, me, 4 * slots, out_buf.shape[1])
     for slot in range(2 * slots):
-        owner = me ^ slot
+        owner = (me ^ slot) % (2 * slots)
         flip_ref[pl.ds(pl.multiple_of(owner * share, share), share), :] = piece_refs[slot][...]
     high_part, low_part = halves(flip_ref[...].T)
     factor_ref[:kinds, :] = high_part
@@ -239,17 +254,12 @@
 
     def copy(step):
         rows = pl.ds(pl.multiple_of(step * tile, tile), tile)
-        return pltpu.make_async_copy(out_buf.at[rows], out_ref.at[rows], sems.at[step])
+        return pltpu.make_async_copy(out_buf.at[rows], out_ref.at[rows, lanes], sems.at[step])
 
     def body(step, _):
         rows = pl.ds(pl.multiple_of(step * tile, tile), tile)
         left = jnp.concatenate([left_ref[l, rows, :] for l in range(levels)] * 2, axis=1)
-        update = dot(left, factor_ref[...], (1, 0))
-        for b in range(per_step):
-            block = step * per_step + b
-            rows = pl.ds(pl.multiple_of(block * width, width), width)
-            first = dot(moved_ref[block], rhs_ref[rows, :], (1, 0))
-            out_buf[rows, :] = first - update[b * width:(b + 1) * width]
+        out_buf[rows, :] = first_ref[rows, lanes] - dot(left, factor_ref[...], (1, 0))
         copy(step).start()
         return 0
 
@@ -298,43 +308,59 @@
       pltpu.with_memory_space_constraint(left_basis, pltpu.HBM))
     gram_got = swap(gram_send, "rows", 1)
 
-    factors, moved = pl.pallas_call(
-        functools.partial(factor_kernel, per_step, width),
-        out_shape=[
-            jax.ShapeDtypeStruct((2 * kinds, rows), jnp.bfloat16),
-            jax.ShapeDtypeStruct((nblocks, width, width), jnp.bfloat16),
-        ],
-        name="factor",
-        **settings(24, 4),
-    )(leaf_order, leaf_inv, flipped)
-
-    def project(half, *grams):
+    moved = pl.pallas_call(
+        functools.partial(permute_kernel, per_step, width),
+        out_shape=jax.ShapeDtypeStruct((nblocks, width, width), jnp.bfloat16),
+        name="permute",
+        **settings(8, 1.5),
+    )(leaf_order, leaf_inv)
+
+    def add(mine, got):
         return pl.pallas_call(
-            functools.partial(project_kernel, half),
-            out_shape=[floats(rank // 2, gram_lanes)] * (len(grams) // 2) + [floats(slots // 2, share, kinds)] * 2,
+            add_kernel, out_shape=floats(*mine.shape), name="add", **settings(8, 0.1),
+        )(mine, got)
+
+    gram = add(gram_keep, gram_got)
+    factors = pl.pallas_call(
+        functools.partial(weigh_kernel, per_step, width),
+        out_shape=jax.ShapeDtypeStruct((2 * kinds, rows), jnp.bfloat16),
+        name="weigh",
+        **settings(8, 2.4),
+    )(moved, flipped, gram)
+
+    def project(far, after):
+        return pl.pallas_call(
+            functools.partial(project_kernel, far),
+            out_shape=[floats(slots // 2, share, kinds)] * 2,
             scratch_shapes=[pltpu.VMEM((columns // 2, kinds), jnp.float32)],
-            name="project",
-            **settings(24, 2.4),
-        )(factors, rhs, *grams)
-
-    gram, keep_a, send_a = project(0, gram_keep, gram_got)
-    got_a = swap(send_a, "rows", 1)
+            name="project_far" if far else "project_near",
+            **settings(12, 2.1),
+        )(factors, rhs, after)
+
+    def merge(keep, got):
+        return pl.pallas_call(
+            merge_kernel, out_shape=[floats(share, kinds)] * (slots // 2), name="merge", **settings(8, 0.1),
+        )(keep, got)
+
+    keep_far, send_far = project(True, gram)
+    got_far = swap(send_far, "rows", 1)
     mask = 2
-    while 2 * mask < slots:
-        gram = gram + swap(gram, "rows", mask)
+    while mask < slots:
+        gram = add(gram, swap(gram, "rows", mask))
         mask *= 2
-    gram_got = swap(gram, "rows", mask)
-    keep_b, send_b = project(1)
-    got_b = swap(send_b, "rows", 1)
-    gram, *merged = pl.pallas_call(
-        merge_kernel,
-        out_shape=[floats(rank // 2, gram_lanes)] + [floats(share, kinds)] * slots,
-        name="merge",
-        **settings(8, 1),
-    )(keep_a, got_a, keep_b, got_b, gram, gram_got)
+    keep_near, send_near = project(False, gram)
+    got_near = swap(send_near, "rows", 1)
+    merged = [None] * (slots // 2) + list(merge(keep_far, got_far))
+    merged[:slots // 2] = merge(keep_near, got_near)
     parts = [merged[0]] + [swap(merged[s], "rows", 2 * s) for s in range(1, slots)]
     gram_other = swap(gram, "rows", slots)
     grams = [gram, gram_other, swap(gram, "rows", 1), swap(gram_other, "rows", 1)]
+    first = pl.pallas_call(
+        functools.partial(solve_kernel, per_step, width),
+        out_shape=floats(rows, columns),
+        name="solve",
+        **settings(8, 1.7),
+    )(moved, rhs, merged[0])
 
     prepared = pl.pallas_call(
         functools.partial(prepare_kernel, levels),
@@ -382,20 +408,27 @@
         piece = swap(piece, "rows", 2 * slot) if slot > 0 else piece
         pieces += [piece, swap(piece, "rows", 1)]
 
-    per_step = blocks_per_step(nblocks, 2)
-    return pl.pallas_call(
-        functools.partial(expand_kernel, levels, per_step, width, slots),
-        out_specs=pl.BlockSpec(memory_space=pl.ANY),
-        out_shape=floats(rows, columns),
-        scratch_shapes=[
-            pltpu.VMEM((columns, kinds), jnp.float32),
-            pltpu.VMEM((2 * kinds, columns), jnp.bfloat16),
-            pltpu.VMEM((rows, columns), jnp.float32),
-            pltpu.SemaphoreType.DMA((nblocks // per_step,)),
-        ],
-        name="expand",
-        **settings(32, 7),
-    )(*pieces, moved, rhs, left_basis)
+    def expand(far, *extra):
+        begin = count // 2 if far else 0
+        operands = (*pieces[begin:begin + count // 2], first, left_basis, *extra)
+        inner = [pl.BlockSpec()] * (count // 2 + 2) + [pl.BlockSpec(memory_space=pl.ANY)] * len(extra)
+        return pl.pallas_call(
+            functools.partial(expand_kernel, far, levels, per_step, width, slots // 2),
+            in_specs=inner,
+            out_specs=pl.BlockSpec(memory_space=pl.ANY),
+            out_shape=floats(rows, columns),
+            scratch_shapes=[
+                pltpu.VMEM((columns // 2, kinds), jnp.float32),
+                pltpu.VMEM((2 * kinds, columns // 2), jnp.bfloat16),
+                pltpu.VMEM((rows, columns // 2), jnp.float32),
+                pltpu.SemaphoreType.DMA((nblocks // per_step,)),
+            ],
+            input_output_aliases={len(operands) - 1: 0} if extra else {},
+            name="expand_far" if far else "expand_near",
+            **settings(14, 2.6),
+        )(*operands)
+
+    return expand(True, expand(False))
 
 
 def solution(mesh):

time: 59.5 us -> 52.7 us (0.89)
  waiting for transfers between devices: 18.6 us -> 8.44 us
  Pallas kernels: 23.5 us -> 25.9 us
  starting transfers between devices: 17.2 us -> 18 us
    ppermute x19, waiting for transfers between devices: 18.6 us -> 8.44 us  [swap(): return lax.ppermute(value, axis, [(i, i ^ mask) for i in range(count)])]
    pallas_call x5 -> x11, Pallas kernels: 15.7 us -> 18.5 us  [the longest x2 8.06 us: expand(): pl.pallas_call(functools.partial(expand_kernel, far, levels, per_step, wi...]
    ppermute x19, starting transfers between devices: 17.2 us -> 18 us  [swap(): return lax.ppermute(value, axis, [(i, i ^ mask) for i in range(count)])]
  transfers between devices with their start and end apart: 19 -> 19, of which waited for: 9 -> 5; matrix products, arithmetic and copies ran while one was open for 0% -> 0% of each run, Pallas kernels for 17% -> 32%
where the time goes in v5:
time: 52.7 us; the launch traced here: 52.5 us
  Pallas kernels  25.9 us (49%)
  starting transfers between devices  18 us (34%)
  waiting for transfers between devices  8.44 us (16%)
    ppermute x19, starting transfers between devices, swap(): return lax.ppermute(value, axis, [(i, i ^ mask) for i in range(count)])  18 us
    ppermute x19, waiting for transfers between devices, swap(): return lax.ppermute(value, axis, [(i, i ^ mask) for i in range(count)])  8.44 us
    pallas_call x2, Pallas kernels, expand(): pl.pallas_call(functools.partial(expand_kernel, far, levels, per_step, wi...  8.06 us
    pallas_call x2, Pallas kernels, project(): pl.pallas_call(functools.partial(project_kernel, far), out_shape=[floats(...  4.21 us
    pallas_call x1, Pallas kernels, per_device(): pl.pallas_call(functools.partial(gram_kernel, levels, per_step, width), i...  3.34 us
    pallas_call x1, Pallas kernels, per_device(): pl.pallas_call(functools.partial(solve_kernel, per_step, width), out_shap...  2.22 us
    pallas_call x1, Pallas kernels, per_device(): pl.pallas_call(functools.partial(weigh_kernel, per_step, width), out_shap...  2.12 us
    pallas_call x1, Pallas kernels, per_device(): pl.pallas_call(functools.partial(prepare_kernel, levels), in_specs=[pl.Bl...  2.1 us
  transfers between devices with their start and end apart: 19, of which 5 were waited for; matrix products, arithmetic and copies ran while one was open for 0% of the time, Pallas kernels for 32%

profile of v5, /device:TPU:0, one launch (start us, length us, event | category | flops | bytes accessed | tf_op | source)
XLA Modules:
  0.0 52.5 jit_solution(11360731808516973504)
XLA Ops:
  0.0 0.0 copy-start.1
  0.0 0.0 copy-start.2
  0.0 3.3 %gram.1 = (bf16[384,4608]{1,0:T(8,128)(2,1)S(1)}, f32[64,384]{1,0:T(8,128)S(1)}, f32[64,384]{1,0:T(8,128)S(1)}) custom-call(bf16[3,4608,128]{2,1,0:T(8,128)(2,1)} %right_ref.1, bf16[3,4608,128]{2,1,0:T(8,128)(2,1)} %refs_5_.3), custom_call_target="tpu_custom_call" | custom-call | flops 3300000000 | tf_op jit(solution)/shard_map/gram/pallas_call | solution.py:295
  3.4 0.5 collective-permute-start
  3.9 0.0 copy-done.1
  3.9 0.0 copy-done.2
  3.9 1.9 %permute.1.moved_ref = bf16[18,256,256]{2,1,0:T(8,128)(2,1)S(1)} custom-call(s32[18,256]{1,0:T(8,128)S(1)} %copy-done.2, bf16[18,256,256]{2,1,0:T(8,128)(2,1)S(1)} %copy-done.1), custom_call_target="tpu_custom_call" | custom-call | flops 1650000000 | tf_op jit(solution)/shard_map/permute/pallas_call | solution.py:311
  5.7 0.0 collective-permute-done.got_ref
  5.8 0.0 slice-start
  5.8 2.6 %collective-permute-start.1 = (f32[64,384]{1,0:T(8,128)S(1)}, f32[64,384]{1,0:T(8,128)S(1)}, u32[]{:S(2)}, u32[]{:S(2)}) collective-permute-start(f32[64,384]{1,0:T(8,128)S(1)} %add.2.after_ref.mine_ref), channel_id=1, source_target_pairs={{0,2},{1,3},{2,0},{3,1},{4,6},{5,7},{6,4},{7,5},{8,10},{9,11},{10,... | collective-permute-start | bytes 294920 | tf_op jit(solution)/shard_map/ppermute | solution.py:29
  8.4 0.0 slice-start.1
  8.4 2.1 %weigh.1.factor_ref = bf16[768,4608]{1,0:T(8,128)(2,1)S(1)} custom-call(bf16[18,256,256]{2,1,0:T(8,128)(2,1)S(1)} %permute.1.moved_ref, bf16[384,4608]{1,0:T(8,128)(2,1)S(1)} %get-tuple-element.23.flip_ref, f32[64,384]{1,0:T(8,128)S(1)} %add.2.after_ref.mine_ref), custom_call_target="tpu_custom_call" | custom-call | flops 2640000000 | tf_op jit(solution)/shard_map/weigh/pallas_call | solution.py:324
  10.5 0.0 slice-done
  10.5 0.0 slice-done.1
  10.5 2.1 %project_far.1 = (f32[2,64,384]{2,1,0:T(8,128)S(1)}, f32[2,64,384]{2,1,0:T(8,128)S(1)}) custom-call(bf16[768,4608]{1,0:T(8,128)(2,1)S(1)} %weigh.1.factor_ref, bf16[4608,512]{1,0:T(8,128)(2,1)S(1)} %bitcast.1, f32[64,384]{1,0:T(8,128)S(1)} %add.2.after_ref.mine_ref), custom_call_target="tpu_custom_call" | custom-call | flops 2310000128 | tf_op jit(solution)/shard_map/project_far/pallas_call | solution.py:332
  12.7 0.3 collective-permute-start.4
  12.9 0.0 collective-permute-done.1.got_ref
  12.9 0.0 copy-start.3
  13.0 2.1 %project_near.1 = (f32[2,64,384]{2,1,0:T(8,128)S(1)}, f32[2,64,384]{2,1,0:T(8,128)S(1)}) custom-call(bf16[768,4608]{1,0:T(8,128)(2,1)S(1)} %weigh.1.factor_ref, bf16[4608,512]{1,0:T(8,128)(2,1)S(1)} %bitcast.1, f32[64,384]{1,0:T(8,128)S(1)} %add.3.after_ref.mine_ref), custom_call_target="tpu_custom_call" | custom-call | flops 2310000128 | tf_op jit(solution)/shard_map/project_near/pallas_call | solution.py:332
  15.1 0.4 collective-permute-start.2
  15.4 1.5 %collective-permute-start.7 = (f32[64,384]{1,0:T(8,128)S(1)}, f32[64,384]{1,0:T(8,128)S(1)}, u32[]{:S(2)}, u32[]{:S(2)}) collective-permute-start(f32[64,384]{1,0:T(8,128)S(1)} %add.3.after_ref.mine_ref), channel_id=1, source_target_pairs={{0,4},{1,5},{2,6},{3,7},{4,0},{5,1},{6,2},{7,3},{8,12},{9,13},{10,... | collective-permute-start | bytes 294920 | tf_op jit(solution)/shard_map/ppermute | solution.py:29
  17.0 0.0 collective-permute-done.4.got_ref
  17.0 0.6 %collective-permute-start.5 = (f32[64,384]{1,0:T(8,128)S(1)}, f32[64,384]{1,0:T(8,128)S(1)}, u32[]{:S(2)}, u32[]{:S(2)}) collective-permute-start(f32[64,384]{1,0:T(8,128)S(1)} %get-tuple-element.32), channel_id=1, source_target_pairs={{0,4},{1,5},{2,6},{3,7},{4,0},{5,1},{6,2},{7,3},{8,12},{9,13},{10,... | collective-permute-start | bytes 294920 | tf_op jit(solution)/shard_map/ppermute | solution.py:29
  17.6 1.5 %collective-permute-start.6 = (f32[64,384]{1,0:T(8,128)S(1)}, f32[64,384]{1,0:T(8,128)S(1)}, u32[]{:S(2)}, u32[]{:S(2)}) collective-permute-start(f32[64,384]{1,0:T(8,128)S(1)} %get-tuple-element.33), channel_id=1, source_target_pairs={{0,6},{1,7},{2,4},{3,5},{4,2},{5,3},{6,0},{7,1},{8,14},{9,15},{10,... | collective-permute-start | bytes 294920 | tf_op jit(solution)/shard_map/ppermute | solution.py:29
  19.1 0.0 collective-permute-done.2.got_ref
  19.1 1.5 %collective-permute-start.3 = (f32[64,384]{1,0:T(8,128)S(1)}, f32[64,384]{1,0:T(8,128)S(1)}, u32[]{:S(2)}, u32[]{:S(2)}) collective-permute-start(f32[64,384]{1,0:T(8,128)S(1)} %get-tuple-element.29), channel_id=1, source_target_pairs={{0,2},{1,3},{2,0},{3,1},{4,6},{5,7},{6,4},{7,5},{8,10},{9,11},{10,... | collective-permute-start | bytes 294920 | tf_op jit(solution)/shard_map/ppermute | solution.py:29
  20.6 0.0 copy-done.3
  20.6 2.1 %prepare.1.refs_4_.joined_ref = f32[3,256,256]{2,1,0:T(8,128)S(1)} custom-call(f32[7,256,256]{2,1,0:T(8,128)} %joined_ref.1, s32[3,128]{1,0:T(4,128)S(1)} %copy-done.3), custom_call_target="tpu_custom_call" | custom-call | flops 2200000000 | tf_op jit(solution)/shard_map/prepare/pallas_call | solution.py:365
  22.7 0.1 collective-permute-start.8
  22.8 0.0 collective-permute-done.7.theirs_ref
  22.8 0.5 collective-permute-start.9
  23.3 1.2 %collective-permute-done.5.refs_2_ = f32[64,384]{1,0:T(8,128)S(1)} collective-permute-done((f32[64,384]{1,0:T(8,128)S(1)}, f32[64,384]{1,0:T(8,128)S(1)}, u32[]{:S(2)}, u32[]{:S(2)}) %collective-permute-start.5) | collective-permute-done | bytes 98336 | tf_op jit(solution)/shard_map/ppermute | solution.py:29
  24.6 0.0 collective-permute-done.6.refs_3_
  24.6 0.4 collective-permute-done.3.refs_1_
  25.0 0.4 node.1
  25.4 0.0 collective-permute-done.8.pair_mine_ref
  25.4 0.0 collective-permute-done.9.pair_theirs_ref
  25.4 0.4 correct.1.sent_ref
  25.8 1.6 %collective-permute-start.10 = (f32[256,128]{1,0:T(8,128)S(1)}, f32[256,128]{1,0:T(8,128)S(1)}, u32[]{:S(2)}, u32[]{:S(2)}) collective-permute-start(f32[256,128]{1,0:T(8,128)S(1)} %correct.1.sent_ref), channel_id=1, source_target_pairs={{0,8},{8,0},{16,24},{24,16},{1,9},{9,1},{17,25},{25,17},{2,10},{10... | collective-permute-start | bytes 393224 | tf_op jit(solution)/shard_map/ppermute | solution.py:29
  27.4 3.4 %collective-permute-done.10.got_ref = f32[256,128]{1,0:T(8,128)S(1)} collective-permute-done((f32[256,128]{1,0:T(8,128)S(1)}, f32[256,128]{1,0:T(8,128)S(1)}, u32[]{:S(2)}, u32[]{:S(2)}) %collective-permute-start.10) | collective-permute-done | bytes 131104 | tf_op jit(solution)/shard_map/ppermute | solution.py:29
  30.8 0.8 %level1.1 = (f32[64,128]{1,0:T(8,128)S(1)}, f32[64,128]{1,0:T(8,128)S(1)}) custom-call(f32[256,128]{1,0:T(8,128)S(1)} %correct.1.sent_ref, f32[256,128]{1,0:T(8,128)S(1)} %collective-permute-done.10.got_ref, f32[3,256,256]{2,1,0:T(8,128)S(1)} %prepare.1.refs_4_.joined_ref), custom_call_target="tpu_custom_call" | custom-call | flops 770000000 | tf_op jit(solution)/shard_map/level1/pallas_call | solution.py:393
  31.6 2.7 %collective-permute-start.11 = (f32[64,128]{1,0:T(8,128)S(1)}, f32[64,128]{1,0:T(8,128)S(1)}, u32[]{:S(2)}, u32[]{:S(2)}) collective-permute-start(f32[64,128]{1,0:T(8,128)S(1)} %get-tuple-element.38.sent_ref), channel_id=1, source_target_pairs={{0,16},{8,24},{16,0},{24,8},{1,17},{9,25},{17,1},{25,9},{2,18},{10... | collective-permute-start | bytes 98312 | tf_op jit(solution)/shard_map/ppermute | solution.py:29
  34.2 2.2 %collective-permute-done.11.got_ref = f32[64,128]{1,0:T(8,128)S(1)} collective-permute-done((f32[64,128]{1,0:T(8,128)S(1)}, f32[64,128]{1,0:T(8,128)S(1)}, u32[]{:S(2)}, u32[]{:S(2)}) %collective-permute-start.11) | collective-permute-done | bytes 32800 | tf_op jit(solution)/shard_map/ppermute | solution.py:29
  36.5 0.4 level2.1.refs_3_
  36.9 0.8 %collective-permute-start.17 = (f32[64,384]{1,0:T(8,128)S(1)}, f32[64,384]{1,0:T(8,128)S(1)}, u32[]{:S(2)}, u32[]{:S(2)}) collective-permute-start(f32[64,384]{1,0:T(8,128)S(1)} %get-tuple-element.40.refs_0_), channel_id=1, source_target_pairs={{0,2},{1,3},{2,0},{3,1},{4,6},{5,7},{6,4},{7,5},{8,10},{9,11},{10,... | collective-permute-start | bytes 294920 | tf_op jit(solution)/shard_map/ppermute | solution.py:29
  37.7 0.0 copy-start
  37.7 1.8 %collective-permute-start.14 = (f32[64,384]{1,0:T(8,128)S(1)}, f32[64,384]{1,0:T(8,128)S(1)}, u32[]{:S(2)}, u32[]{:S(2)}) collective-permute-start(f32[64,384]{1,0:T(8,128)S(1)} %get-tuple-element.39), channel_id=1, source_target_pairs={{0,6},{1,7},{2,4},{3,5},{4,2},{5,3},{6,0},{7,1},{8,14},{9,15},{10,... | collective-permute-start | bytes 294920 | tf_op jit(solution)/shard_map/ppermute | solution.py:29
  39.5 1.0 %collective-permute-start.12 = (f32[64,384]{1,0:T(8,128)S(1)}, f32[64,384]{1,0:T(8,128)S(1)}, u32[]{:S(2)}, u32[]{:S(2)}) collective-permute-start(f32[64,384]{1,0:T(8,128)S(1)} %get-tuple-element.39), channel_id=1, source_target_pairs={{0,4},{1,5},{2,6},{3,7},{4,0},{5,1},{6,2},{7,3},{8,12},{9,13},{10,... | collective-permute-start | bytes 294920 | tf_op jit(solution)/shard_map/ppermute | solution.py:29
  40.4 0.0 collective-permute-start.16
  40.4 1.1 %collective-permute-done.17.refs_2_ = f32[64,384]{1,0:T(8,128)S(1)} collective-permute-done((f32[64,384]{1,0:T(8,128)S(1)}, f32[64,384]{1,0:T(8,128)S(1)}, u32[]{:S(2)}, u32[]{:S(2)}) %collective-permute-start.17) | collective-permute-done | bytes 98336 | tf_op jit(solution)/shard_map/ppermute | solution.py:29
  41.5 0.0 collective-permute-start.18
  41.5 2.2 %solve.1.refs_4_ = f32[4608,512]{1,0:T(8,128)S(1)} custom-call(bf16[18,256,256]{2,1,0:T(8,128)(2,1)S(1)} %permute.1.moved_ref, bf16[4608,512]{1,0:T(8,128)(2,1)S(1)} %bitcast.1, f32[64,384]{1,0:T(8,128)S(1)} %get-tuple-element.28.refs_0_.after_ref), custom_call_target="tpu_custom_call" | custom-call | flops 1870000000 | tf_op jit(solution)/shard_map/solve/pallas_call | solution.py:358
  43.8 0.0 collective-permute-done.14.refs_2_
  43.8 0.6 %collective-permute-start.15 = (f32[64,384]{1,0:T(8,128)S(1)}, f32[64,384]{1,0:T(8,128)S(1)}, u32[]{:S(2)}, u32[]{:S(2)}) collective-permute-start(f32[64,384]{1,0:T(8,128)S(1)} %collective-permute-done.14.refs_2_), channel_id=1, source_target_pairs={{0,1},{1,0},{2,3},{3,2},{4,5},{5,4},{6,7},{7,6},{8,9},{9,8},{10,11... | collective-permute-start | bytes 294920 | tf_op jit(solution)/shard_map/ppermute | solution.py:29
  44.4 0.0 collective-permute-done.12.refs_0_
  44.4 0.1 collective-permute-start.13
  44.4 0.0 collective-permute-done.16.refs_1_
  44.4 0.0 collective-permute-done.18.refs_3_
  44.5 0.0 copy-done
  44.5 4.0 %expand_near.1.refs_6_ = f32[4608,512]{1,0:T(8,128)} custom-call(f32[64,384]{1,0:T(8,128)S(1)} %get-tuple-element.40.refs_0_, f32[64,384]{1,0:T(8,128)S(1)} %collective-permute-done.16.refs_1_, f32[64,384]{1,0:T(8,128)S(1)} %collective-permute-done.17.refs_2_, f32[64,384]{1,0:T(8,128)S(1)} %collective-permute-done.18.refs_3_, f32[4608,512]{1,0:T(8,128)S(1)} %solve.1.refs_4_, ...), custom_call_target="tpu_custom_call" | custom-call | flops 2860000000 | tf_op jit(solution)/shard_map/expand_near/pallas_call | solution.py:415
  48.5 0.0 collective-permute-done.15.refs_3_
  48.5 0.0 collective-permute-done.13.refs_1_
  48.5 4.0 %expand_far.1 = f32[4608,512]{1,0:T(8,128)} custom-call(f32[64,384]{1,0:T(8,128)S(1)} %collective-permute-done.12.refs_0_, f32[64,384]{1,0:T(8,128)S(1)} %collective-permute-done.13.refs_1_, f32[64,384]{1,0:T(8,128)S(1)} %collective-permute-done.14.refs_2_, f32[64,384]{1,0:T(8,128)S(1)} %collective-permute-done.15.refs_3_, ...), custom_call_target="tpu_custom_call", output_to_operand_aliasing={{}: (6, {})} | custom-call | flops 2860000000 | tf_op jit(solution)/shard_map/expand_far/pallas_call | solution.py:415
  (6 shorter events, 0.1 us)
Async XLA Ops:
  0.0 3.9 %copy-start.1 = (bf16[18,256,256]{2,1,0:T(8,128)(2,1)S(1)}, bf16[18,256,256]{2,1,0:T(8,128)(2,1)}, u32[]{:S(2)}) copy-start(bf16[18,256,256]{2,1,0:T(8,128)(2,1)} %inv_ref.1) | copy-start | bytes 7077892
  0.0 3.9 %copy-start.2 = (s32[18,256]{1,0:T(8,128)S(1)}, s32[18,256]{1,0:T(8,128)}, u32[]{:S(2)}) copy-start(s32[18,256]{1,0:T(8,128)} %order_ref.1) | copy-start | bytes 55300
  3.4 2.4 %collective-permute-start = (f32[64,384]{1,0:T(8,128)S(1)}, f32[64,384]{1,0:T(8,128)S(1)}, u32[]{:S(2)}, u32[]{:S(2)}) collective-permute-start(f32[64,384]{1,0:T(8,128)S(1)} %get-tuple-element.25), channel_id=1, source_target_pairs={{0,1},{1,0},{2,3},{3,2},{4,5},{5,4},{6,7},{7,6},{8,9},{9,8},{10,11... | collective-permute-start | bytes 294920 | tf_op jit(solution)/shard_map/ppermute | solution.py:29
  5.8 4.8 %slice-start = ((s8[4718592]{0:T(1024)(128)(4,1)}), s8[4194304]{0:T(1024)(128)(4,1)S(1)}, s32[]{:S(2)}) async-start(s8[4718592]{0:T(1024)(128)(4,1)} %bitcast), calls=%async_computation | async-start | bytes 8388608
  5.8 7.1 %collective-permute-start.1 = (f32[64,384]{1,0:T(8,128)S(1)}, f32[64,384]{1,0:T(8,128)S(1)}, u32[]{:S(2)}, u32[]{:S(2)}) collective-permute-start(f32[64,384]{1,0:T(8,128)S(1)} %add.2.after_ref.mine_ref), channel_id=1, source_target_pairs={{0,2},{1,3},{2,0},{3,1},{4,6},{5,7},{6,4},{7,5},{8,10},{9,11},{10,... | collective-permute-start | bytes 294920 | tf_op jit(solution)/shard_map/ppermute | solution.py:29
  8.4 2.1 %slice-start.1 = ((s8[4718592]{0:T(1024)(128)(4,1)}), s8[524288]{0:T(1024)(128)(4,1)S(1)}, s32[]{:S(2)}) async-start(s8[4718592]{0:T(1024)(128)(4,1)} %bitcast), calls=%async_computation.1 | async-start | bytes 1048576
  12.7 4.3 %collective-permute-start.4 = (f32[2,64,384]{2,1,0:T(8,128)S(1)}, f32[2,64,384]{2,1,0:T(8,128)S(1)}, u32[]{:S(2)}, u32[]{:S(2)}) collective-permute-start(f32[2,64,384]{2,1,0:T(8,128)S(1)} %get-tuple-element.31), channel_id=1, source_target_pairs={{0,1},{1,0},{2,3},{3,2},{4,5},{5,4},{6,7},{7,6},{8,9},{9,8},{10,11... | collective-permute-start | bytes 589832 | tf_op jit(solution)/shard_map/ppermute | solution.py:29
  12.9 7.7 %copy-start.3 = (s32[3,128]{1,0:T(4,128)S(1)}, s32[3,128]{1,0:T(4,128)}, u32[]{:S(2)}) copy-start(s32[3,128]{1,0:T(4,128)} %perm_ref.1) | copy-start | bytes 4612
  15.1 4.0 %collective-permute-start.2 = (f32[2,64,384]{2,1,0:T(8,128)S(1)}, f32[2,64,384]{2,1,0:T(8,128)S(1)}, u32[]{:S(2)}, u32[]{:S(2)}) collective-permute-start(f32[2,64,384]{2,1,0:T(8,128)S(1)} %get-tuple-element.27), channel_id=1, source_target_pairs={{0,1},{1,0},{2,3},{3,2},{4,5},{5,4},{6,7},{7,6},{8,9},{9,8},{10,11... | collective-permute-start | bytes 589832 | tf_op jit(solution)/shard_map/ppermute | solution.py:29
  15.4 7.4 %collective-permute-start.7 = (f32[64,384]{1,0:T(8,128)S(1)}, f32[64,384]{1,0:T(8,128)S(1)}, u32[]{:S(2)}, u32[]{:S(2)}) collective-permute-start(f32[64,384]{1,0:T(8,128)S(1)} %add.3.after_ref.mine_ref), channel_id=1, source_target_pairs={{0,4},{1,5},{2,6},{3,7},{4,0},{5,1},{6,2},{7,3},{8,12},{9,13},{10,... | collective-permute-start | bytes 294920 | tf_op jit(solution)/shard_map/ppermute | solution.py:29
  17.0 7.6 %collective-permute-start.5 = (f32[64,384]{1,0:T(8,128)S(1)}, f32[64,384]{1,0:T(8,128)S(1)}, u32[]{:S(2)}, u32[]{:S(2)}) collective-permute-start(f32[64,384]{1,0:T(8,128)S(1)} %get-tuple-element.32), channel_id=1, source_target_pairs={{0,4},{1,5},{2,6},{3,7},{4,0},{5,1},{6,2},{7,3},{8,12},{9,13},{10,... | collective-permute-start | bytes 294920 | tf_op jit(solution)/shard_map/ppermute | solution.py:29
  17.6 7.0 %collective-permute-start.6 = (f32[64,384]{1,0:T(8,128)S(1)}, f32[64,384]{1,0:T(8,128)S(1)}, u32[]{:S(2)}, u32[]{:S(2)}) collective-permute-start(f32[64,384]{1,0:T(8,128)S(1)} %get-tuple-element.33), channel_id=1, source_target_pairs={{0,6},{1,7},{2,4},{3,5},{4,2},{5,3},{6,0},{7,1},{8,14},{9,15},{10,... | collective-permute-start | bytes 294920 | tf_op jit(solution)/shard_map/ppermute | solution.py:29
  19.1 5.9 %collective-permute-start.3 = (f32[64,384]{1,0:T(8,128)S(1)}, f32[64,384]{1,0:T(8,128)S(1)}, u32[]{:S(2)}, u32[]{:S(2)}) collective-permute-start(f32[64,384]{1,0:T(8,128)S(1)} %get-tuple-element.29), channel_id=1, source_target_pairs={{0,2},{1,3},{2,0},{3,1},{4,6},{5,7},{6,4},{7,5},{8,10},{9,11},{10,... | collective-permute-start | bytes 294920 | tf_op jit(solution)/shard_map/ppermute | solution.py:29
  22.7 2.6 %collective-permute-start.8 = (f32[64,384]{1,0:T(8,128)S(1)}, f32[64,384]{1,0:T(8,128)S(1)}, u32[]{:S(2)}, u32[]{:S(2)}) collective-permute-start(f32[64,384]{1,0:T(8,128)S(1)} %add.3.after_ref.mine_ref), channel_id=1, source_target_pairs={{0,1},{1,0},{2,3},{3,2},{4,5},{5,4},{6,7},{7,6},{8,9},{9,8},{10,11... | collective-permute-start | bytes 294920 | tf_op jit(solution)/shard_map/ppermute | solution.py:29
  22.8 2.6 %collective-permute-start.9 = (f32[64,384]{1,0:T(8,128)S(1)}, f32[64,384]{1,0:T(8,128)S(1)}, u32[]{:S(2)}, u32[]{:S(2)}) collective-permute-start(f32[64,384]{1,0:T(8,128)S(1)} %collective-permute-done.7.theirs_ref), channel_id=1, source_target_pairs={{0,1},{1,0},{2,3},{3,2},{4,5},{5,4},{6,7},{7,6},{8,9},{9,8},{10,11... | collective-permute-start | bytes 294920 | tf_op jit(solution)/shard_map/ppermute | solution.py:29
  25.8 5.0 %collective-permute-start.10 = (f32[256,128]{1,0:T(8,128)S(1)}, f32[256,128]{1,0:T(8,128)S(1)}, u32[]{:S(2)}, u32[]{:S(2)}) collective-permute-start(f32[256,128]{1,0:T(8,128)S(1)} %correct.1.sent_ref), channel_id=1, source_target_pairs={{0,8},{8,0},{16,24},{24,16},{1,9},{9,1},{17,25},{25,17},{2,10},{10... | collective-permute-start | bytes 393224 | tf_op jit(solution)/shard_map/ppermute | solution.py:29
  31.6 4.9 %collective-permute-start.11 = (f32[64,128]{1,0:T(8,128)S(1)}, f32[64,128]{1,0:T(8,128)S(1)}, u32[]{:S(2)}, u32[]{:S(2)}) collective-permute-start(f32[64,128]{1,0:T(8,128)S(1)} %get-tuple-element.38.sent_ref), channel_id=1, source_target_pairs={{0,16},{8,24},{16,0},{24,8},{1,17},{9,25},{17,1},{25,9},{2,18},{10... | collective-permute-start | bytes 98312 | tf_op jit(solution)/shard_map/ppermute | solution.py:29
  36.9 4.7 %collective-permute-start.17 = (f32[64,384]{1,0:T(8,128)S(1)}, f32[64,384]{1,0:T(8,128)S(1)}, u32[]{:S(2)}, u32[]{:S(2)}) collective-permute-start(f32[64,384]{1,0:T(8,128)S(1)} %get-tuple-element.40.refs_0_), channel_id=1, source_target_pairs={{0,2},{1,3},{2,0},{3,1},{4,6},{5,7},{6,4},{7,5},{8,10},{9,11},{10,... | collective-permute-start | bytes 294920 | tf_op jit(solution)/shard_map/ppermute | solution.py:29
  37.7 6.8 %copy-start = (bf16[3,4608,128]{2,1,0:T(8,128)(2,1)S(1)}, bf16[3,4608,128]{2,1,0:T(8,128)(2,1)}, u32[]{:S(2)}) copy-start(bf16[3,4608,128]{2,1,0:T(8,128)(2,1)} %refs_5_.3) | copy-start | bytes 10616836
  37.7 6.1 %collective-permute-start.14 = (f32[64,384]{1,0:T(8,128)S(1)}, f32[64,384]{1,0:T(8,128)S(1)}, u32[]{:S(2)}, u32[]{:S(2)}) collective-permute-start(f32[64,384]{1,0:T(8,128)S(1)} %get-tuple-element.39), channel_id=1, source_target_pairs={{0,6},{1,7},{2,4},{3,5},{4,2},{5,3},{6,0},{7,1},{8,14},{9,15},{10,... | collective-permute-start | bytes 294920 | tf_op jit(solution)/shard_map/ppermute | solution.py:29
  39.5 4.9 %collective-permute-start.12 = (f32[64,384]{1,0:T(8,128)S(1)}, f32[64,384]{1,0:T(8,128)S(1)}, u32[]{:S(2)}, u32[]{:S(2)}) collective-permute-start(f32[64,384]{1,0:T(8,128)S(1)} %get-tuple-element.39), channel_id=1, source_target_pairs={{0,4},{1,5},{2,6},{3,7},{4,0},{5,1},{6,2},{7,3},{8,12},{9,13},{10,... | collective-permute-start | bytes 294920 | tf_op jit(solution)/shard_map/ppermute | solution.py:29
  40.4 4.0 %collective-permute-start.16 = (f32[64,384]{1,0:T(8,128)S(1)}, f32[64,384]{1,0:T(8,128)S(1)}, u32[]{:S(2)}, u32[]{:S(2)}) collective-permute-start(f32[64,384]{1,0:T(8,128)S(1)} %get-tuple-element.40.refs_0_), channel_id=1, source_target_pairs={{0,1},{1,0},{2,3},{3,2},{4,5},{5,4},{6,7},{7,6},{8,9},{9,8},{10,11... | collective-permute-start | bytes 294920 | tf_op jit(solution)/shard_map/ppermute | solution.py:29
  41.5 2.9 %collective-permute-start.18 = (f32[64,384]{1,0:T(8,128)S(1)}, f32[64,384]{1,0:T(8,128)S(1)}, u32[]{:S(2)}, u32[]{:S(2)}) collective-permute-start(f32[64,384]{1,0:T(8,128)S(1)} %collective-permute-done.17.refs_2_), channel_id=1, source_target_pairs={{0,1},{1,0},{2,3},{3,2},{4,5},{5,4},{6,7},{7,6},{8,9},{9,8},{10,11... | collective-permute-start | bytes 294920 | tf_op jit(solution)/shard_map/ppermute | solution.py:29
  43.8 4.7 %collective-permute-start.15 = (f32[64,384]{1,0:T(8,128)S(1)}, f32[64,384]{1,0:T(8,128)S(1)}, u32[]{:S(2)}, u32[]{:S(2)}) collective-permute-start(f32[64,384]{1,0:T(8,128)S(1)} %collective-permute-done.14.refs_2_), channel_id=1, source_target_pairs={{0,1},{1,0},{2,3},{3,2},{4,5},{5,4},{6,7},{7,6},{8,9},{9,8},{10,11... | collective-permute-start | bytes 294920 | tf_op jit(solution)/shard_map/ppermute | solution.py:29
  44.4 4.1 %collective-permute-start.13 = (f32[64,384]{1,0:T(8,128)S(1)}, f32[64,384]{1,0:T(8,128)S(1)}, u32[]{:S(2)}, u32[]{:S(2)}) collective-permute-start(f32[64,384]{1,0:T(8,128)S(1)} %collective-permute-done.12.refs_0_), channel_id=1, source_target_pairs={{0,1},{1,0},{2,3},{3,2},{4,5},{5,4},{6,7},{7,6},{8,9},{9,8},{10,11... | collective-permute-start | bytes 294920 | tf_op jit(solution)/shard_map/ppermute | solution.py:29

commit v6 on v5

--- a/solution.py
+++ b/solution.py
@@ -52,8 +52,8 @@
         )
 
     for step in range(steps):
-        for copy in copies(step):
-            copy.start()
+        for priority, copy in enumerate(copies(step)):
+            copy.start(priority=priority)
     gram_ref[...] = jnp.zeros_like(gram_ref)
 
     def body(step, _):
@@ -199,7 +199,7 @@
     pack_message(message_ref, pieces)
 
 
-def level_kernel(levels, level, share, sent_ref, got_ref, joined_ref, coef_ref, *message_ref):
+def level_kernel(levels, level, share, sent_ref, got_ref, joined_ref, after_ref, coef_ref, *message_ref):
     rank = sent_ref.shape[1]
     side = lax.axis_index("leaf") // 2 ** (level - 1) % 2
     more = levels - level
@@ -253,17 +253,14 @@
     factor_ref[kinds:, :] = low_part
 
     def copy(step):
-        rows = pl.ds(pl.multiple_of(step * tile, tile), tile)
+        rows = pl.ds(step * tile, tile)
         return pltpu.make_async_copy(out_buf.at[rows], out_ref.at[rows, lanes], sems.at[step])
 
-    def body(step, _):
-        rows = pl.ds(pl.multiple_of(step * tile, tile), tile)
+    for step in range(steps):
+        rows = pl.ds(step * tile, tile)
         left = jnp.concatenate([left_ref[l, rows, :] for l in range(levels)] * 2, axis=1)
         out_buf[rows, :] = first_ref[rows, lanes] - dot(left, factor_ref[...], (1, 0))
-        copy(step).start()
-        return 0
-
-    lax.fori_loop(0, steps, body, 0)
+        copy(step).start(priority=step % 2)
     for step in range(steps):
         copy(step).wait()
 
@@ -309,7 +306,7 @@
     gram_got = swap(gram_send, "rows", 1)
 
     moved = pl.pallas_call(
-        functools.partial(permute_kernel, per_step, width),
+        functools.partial(permute_kernel, blocks_per_step(nblocks, 6), width),
         out_shape=jax.ShapeDtypeStruct((nblocks, width, width), jnp.bfloat16),
         name="permute",
         **settings(8, 1.5),
@@ -389,24 +386,20 @@
     coefs = [own]
     for level in range(1, levels):
         last = level + 1 == levels
-        arrived = swap(message, "leaf", 2 ** (level - 1))
+        arrived = swap(message, "leaf", 2 ** level - 1)
         outs = pl.pallas_call(
             functools.partial(level_kernel, levels, level, share),
             out_shape=[floats(share, rank)] + ([] if last else [message_shape(level + 1)]),
             name=f"level{level}",
             **settings(8, 0.7),
-        )(message, arrived, prepared)
+        )(message, arrived, prepared, first)
         coefs.append(outs[0])
         message = outs[-1]
     own_pack, other_pack = pl.pallas_call(
         pack_kernel, out_shape=[floats(share, kinds)] * 2, name="pack", **settings(8, 0.2),
     )(other, *coefs)
 
-    pieces = []
-    for slot in range(slots):
-        piece = own_pack if slot < slots // 2 else other_pack
-        piece = swap(piece, "rows", 2 * slot) if slot > 0 else piece
-        pieces += [piece, swap(piece, "rows", 1)]
+    steps = nblocks // per_step
 
     def expand(far, *extra):
         begin = count // 2 if far else 0
@@ -421,13 +414,18 @@
                 pltpu.VMEM((columns // 2, kinds), jnp.float32),
                 pltpu.VMEM((2 * kinds, columns // 2), jnp.bfloat16),
                 pltpu.VMEM((rows, columns // 2), jnp.float32),
-                pltpu.SemaphoreType.DMA((nblocks // per_step,)),
+                pltpu.SemaphoreType.DMA((steps,)),
             ],
             input_output_aliases={len(operands) - 1: 0} if extra else {},
             name="expand_far" if far else "expand_near",
             **settings(14, 2.6),
         )(*operands)
 
+    pieces = []
+    for slot in range(slots):
+        piece = own_pack if slot < slots // 2 else other_pack
+        piece = swap(piece, "rows", 2 * slot) if slot > 0 else piece
+        pieces += [piece, swap(piece, "rows", 1)]
     return expand(True, expand(False))
 
 

time: 52.7 us -> 52.8 us (level)
  Pallas kernels: 25.9 us -> 25.2 us
    pallas_call x2, Pallas kernels: 8.06 us -> 7.13 us  [expand(): pl.pallas_call(functools.partial(expand_kernel, far, levels, per_step, wi...]
    pallas_call x1, Pallas kernels: 3.34 us -> 4.23 us  [per_device(): pl.pallas_call(functools.partial(gram_kernel, levels, per_step, width), i...]
    pallas_call x1, Pallas kernels: 1.85 us -> 1.24 us  [per_device(): pl.pallas_call(functools.partial(permute_kernel, blocks_per_step(nblocks,...]
  transfers between devices with their start and end apart: 19 -> 19, of which waited for: 5 -> 7; matrix products, arithmetic and copies ran while one was open for 0% -> 0% of each run, Pallas kernels for 32% -> 30%
where the time goes in v6:
time: 52.8 us; the launch traced here: 52.6 us
  Pallas kernels  25.2 us (48%)
  starting transfers between devices  18.3 us (35%)
  waiting for transfers between devices  8.8 us (17%)
    ppermute x19, starting transfers between devices, swap(): return lax.ppermute(value, axis, [(i, i ^ mask) for i in range(count)])  18.3 us
    ppermute x19, waiting for transfers between devices, swap(): return lax.ppermute(value, axis, [(i, i ^ mask) for i in range(count)])  8.8 us
    pallas_call x2, Pallas kernels, expand(): pl.pallas_call(functools.partial(expand_kernel, far, levels, per_step, wi...  7.13 us
    pallas_call x1, Pallas kernels, per_device(): pl.pallas_call(functools.partial(gram_kernel, levels, per_step, width), i...  4.23 us
    pallas_call x2, Pallas kernels, project(): pl.pallas_call(functools.partial(project_kernel, far), out_shape=[floats(...  4.2 us
    pallas_call x1, Pallas kernels, per_device(): pl.pallas_call(functools.partial(solve_kernel, per_step, width), out_shap...  2.22 us
    pallas_call x1, Pallas kernels, per_device(): pl.pallas_call(functools.partial(weigh_kernel, per_step, width), out_shap...  2.12 us
    pallas_call x1, Pallas kernels, per_device(): pl.pallas_call(functools.partial(prepare_kernel, levels), in_specs=[pl.Bl...  2.11 us
  transfers between devices with their start and end apart: 19, of which 7 were waited for; matrix products, arithmetic and copies ran while one was open for 0% of the time, Pallas kernels for 30%

profile of v6, /device:TPU:0, one launch (start us, length us, event | category | flops | bytes accessed | tf_op | source)
XLA Modules:
  0.0 52.6 jit_solution(14906590214671927884)
XLA Ops:
  0.0 0.0 copy-start.1
  0.0 0.0 copy-start.2
  0.0 4.2 %gram.1 = (bf16[384,4608]{1,0:T(8,128)(2,1)S(1)}, f32[64,384]{1,0:T(8,128)S(1)}, f32[64,384]{1,0:T(8,128)S(1)}) custom-call(bf16[3,4608,128]{2,1,0:T(8,128)(2,1)} %right_ref.1, bf16[3,4608,128]{2,1,0:T(8,128)(2,1)} %refs_5_.3), custom_call_target="tpu_custom_call" | custom-call | flops 3300000000 | tf_op jit(solution)/shard_map/gram/pallas_call | solution.py:292
  4.2 0.5 collective-permute-start
  4.8 0.0 copy-done.1
  4.8 0.0 copy-done.2
  4.8 1.2 %permute.1.moved_ref = bf16[18,256,256]{2,1,0:T(8,128)(2,1)S(1)} custom-call(s32[18,256]{1,0:T(8,128)S(1)} %copy-done.2, bf16[18,256,256]{2,1,0:T(8,128)(2,1)S(1)} %copy-done.1), custom_call_target="tpu_custom_call" | custom-call | flops 1650000000 | tf_op jit(solution)/shard_map/permute/pallas_call | solution.py:308
  6.0 0.0 collective-permute-done.got_ref
  6.0 0.0 slice-start
  6.1 2.6 %collective-permute-start.1 = (f32[64,384]{1,0:T(8,128)S(1)}, f32[64,384]{1,0:T(8,128)S(1)}, u32[]{:S(2)}, u32[]{:S(2)}) collective-permute-start(f32[64,384]{1,0:T(8,128)S(1)} %add.2.after_ref.mine_ref), channel_id=1, source_target_pairs={{0,2},{1,3},{2,0},{3,1},{4,6},{5,7},{6,4},{7,5},{8,10},{9,11},{10,... | collective-permute-start | bytes 294920 | tf_op jit(solution)/shard_map/ppermute | solution.py:29
  8.6 0.0 slice-start.1
  8.6 2.1 %weigh.1.factor_ref = bf16[768,4608]{1,0:T(8,128)(2,1)S(1)} custom-call(bf16[18,256,256]{2,1,0:T(8,128)(2,1)S(1)} %permute.1.moved_ref, bf16[384,4608]{1,0:T(8,128)(2,1)S(1)} %get-tuple-element.23.flip_ref, f32[64,384]{1,0:T(8,128)S(1)} %add.2.after_ref.mine_ref), custom_call_target="tpu_custom_call" | custom-call | flops 2640000000 | tf_op jit(solution)/shard_map/weigh/pallas_call | solution.py:321
  10.8 0.0 slice-done
  10.8 0.0 slice-done.1
  10.8 2.1 %project_far.1 = (f32[2,64,384]{2,1,0:T(8,128)S(1)}, f32[2,64,384]{2,1,0:T(8,128)S(1)}) custom-call(bf16[768,4608]{1,0:T(8,128)(2,1)S(1)} %weigh.1.factor_ref, bf16[4608,512]{1,0:T(8,128)(2,1)S(1)} %bitcast.1, f32[64,384]{1,0:T(8,128)S(1)} %add.2.after_ref.mine_ref), custom_call_target="tpu_custom_call" | custom-call | flops 2310000128 | tf_op jit(solution)/shard_map/project_far/pallas_call | solution.py:329
  12.9 0.3 collective-permute-start.4
  13.2 0.0 collective-permute-done.1.got_ref
  13.2 0.0 copy-start.3
  13.2 2.1 %project_near.1 = (f32[2,64,384]{2,1,0:T(8,128)S(1)}, f32[2,64,384]{2,1,0:T(8,128)S(1)}) custom-call(bf16[768,4608]{1,0:T(8,128)(2,1)S(1)} %weigh.1.factor_ref, bf16[4608,512]{1,0:T(8,128)(2,1)S(1)} %bitcast.1, f32[64,384]{1,0:T(8,128)S(1)} %add.3.after_ref.mine_ref), custom_call_target="tpu_custom_call" | custom-call | flops 2310000128 | tf_op jit(solution)/shard_map/project_near/pallas_call | solution.py:329
  15.3 0.4 collective-permute-start.2
  15.7 1.5 %collective-permute-start.7 = (f32[64,384]{1,0:T(8,128)S(1)}, f32[64,384]{1,0:T(8,128)S(1)}, u32[]{:S(2)}, u32[]{:S(2)}) collective-permute-start(f32[64,384]{1,0:T(8,128)S(1)} %add.3.after_ref.mine_ref), channel_id=1, source_target_pairs={{0,4},{1,5},{2,6},{3,7},{4,0},{5,1},{6,2},{7,3},{8,12},{9,13},{10,... | collective-permute-start | bytes 294920 | tf_op jit(solution)/shard_map/ppermute | solution.py:29
  17.2 0.0 collective-permute-done.4.got_ref
  17.2 0.6 %collective-permute-start.5 = (f32[64,384]{1,0:T(8,128)S(1)}, f32[64,384]{1,0:T(8,128)S(1)}, u32[]{:S(2)}, u32[]{:S(2)}) collective-permute-start(f32[64,384]{1,0:T(8,128)S(1)} %get-tuple-element.32), channel_id=1, source_target_pairs={{0,4},{1,5},{2,6},{3,7},{4,0},{5,1},{6,2},{7,3},{8,12},{9,13},{10,... | collective-permute-start | bytes 294920 | tf_op jit(solution)/shard_map/ppermute | solution.py:29
  17.8 1.5 %collective-permute-start.6 = (f32[64,384]{1,0:T(8,128)S(1)}, f32[64,384]{1,0:T(8,128)S(1)}, u32[]{:S(2)}, u32[]{:S(2)}) collective-permute-start(f32[64,384]{1,0:T(8,128)S(1)} %get-tuple-element.33), channel_id=1, source_target_pairs={{0,6},{1,7},{2,4},{3,5},{4,2},{5,3},{6,0},{7,1},{8,14},{9,15},{10,... | collective-permute-start | bytes 294920 | tf_op jit(solution)/shard_map/ppermute | solution.py:29
  19.3 0.0 collective-permute-done.2.got_ref
  19.3 1.6 %collective-permute-start.3 = (f32[64,384]{1,0:T(8,128)S(1)}, f32[64,384]{1,0:T(8,128)S(1)}, u32[]{:S(2)}, u32[]{:S(2)}) collective-permute-start(f32[64,384]{1,0:T(8,128)S(1)} %get-tuple-element.29), channel_id=1, source_target_pairs={{0,2},{1,3},{2,0},{3,1},{4,6},{5,7},{6,4},{7,5},{8,10},{9,11},{10,... | collective-permute-start | bytes 294920 | tf_op jit(solution)/shard_map/ppermute | solution.py:29
  20.9 0.0 copy-done.3
  20.9 2.1 %prepare.1.refs_4_.joined_ref = f32[3,256,256]{2,1,0:T(8,128)S(1)} custom-call(f32[7,256,256]{2,1,0:T(8,128)} %joined_ref.1, s32[3,128]{1,0:T(4,128)S(1)} %copy-done.3), custom_call_target="tpu_custom_call" | custom-call | flops 2200000000 | tf_op jit(solution)/shard_map/prepare/pallas_call | solution.py:362
  23.0 0.1 collective-permute-start.8
  23.1 0.0 collective-permute-done.7.theirs_ref
  23.1 0.5 collective-permute-start.9
  23.6 1.2 %collective-permute-done.5.refs_2_ = f32[64,384]{1,0:T(8,128)S(1)} collective-permute-done((f32[64,384]{1,0:T(8,128)S(1)}, f32[64,384]{1,0:T(8,128)S(1)}, u32[]{:S(2)}, u32[]{:S(2)}) %collective-permute-start.5) | collective-permute-done | bytes 98336 | tf_op jit(solution)/shard_map/ppermute | solution.py:29
  24.8 0.0 collective-permute-done.6.refs_3_
  24.8 0.5 collective-permute-done.3.refs_1_
  25.3 0.4 node.1
  25.6 0.0 collective-permute-done.8.pair_mine_ref
  25.7 0.0 collective-permute-done.9.pair_theirs_ref
  25.7 0.4 correct.1.sent_ref
  26.1 1.6 %collective-permute-start.10 = (f32[256,128]{1,0:T(8,128)S(1)}, f32[256,128]{1,0:T(8,128)S(1)}, u32[]{:S(2)}, u32[]{:S(2)}) collective-permute-start(f32[256,128]{1,0:T(8,128)S(1)} %correct.1.sent_ref), channel_id=1, source_target_pairs={{0,8},{8,0},{16,24},{24,16},{1,9},{9,1},{17,25},{25,17},{2,10},{10... | collective-permute-start | bytes 393224 | tf_op jit(solution)/shard_map/ppermute | solution.py:29
  27.7 2.2 %solve.1.after_ref.refs_4_ = f32[4608,512]{1,0:T(8,128)S(1)} custom-call(bf16[18,256,256]{2,1,0:T(8,128)(2,1)S(1)} %permute.1.moved_ref, bf16[4608,512]{1,0:T(8,128)(2,1)S(1)} %bitcast.1, f32[64,384]{1,0:T(8,128)S(1)} %get-tuple-element.28.refs_0_.after_ref), custom_call_target="tpu_custom_call" | custom-call | flops 1870000000 | tf_op jit(solution)/shard_map/solve/pallas_call | solution.py:355
  29.9 1.2 %collective-permute-done.10.got_ref = f32[256,128]{1,0:T(8,128)S(1)} collective-permute-done((f32[256,128]{1,0:T(8,128)S(1)}, f32[256,128]{1,0:T(8,128)S(1)}, u32[]{:S(2)}, u32[]{:S(2)}) %collective-permute-start.10) | collective-permute-done | bytes 131104 | tf_op jit(solution)/shard_map/ppermute | solution.py:29
  31.1 0.8 %level1.1 = (f32[64,128]{1,0:T(8,128)S(1)}, f32[64,128]{1,0:T(8,128)S(1)}) custom-call(f32[256,128]{1,0:T(8,128)S(1)} %correct.1.sent_ref, f32[256,128]{1,0:T(8,128)S(1)} %collective-permute-done.10.got_ref, f32[3,256,256]{2,1,0:T(8,128)S(1)} %prepare.1.refs_4_.joined_ref, f32[4608,512]{1,0:T(8,128)S(1)} %solve.1.after_ref.refs_4_), custom_call_target="tpu_custom_call" | custom-call | flops 770000000 | tf_op jit(solution)/shard_map/level1/pallas_call | solution.py:390
  31.9 0.0 copy-start
  31.9 3.7 %collective-permute-start.11 = (f32[64,128]{1,0:T(8,128)S(1)}, f32[64,128]{1,0:T(8,128)S(1)}, u32[]{:S(2)}, u32[]{:S(2)}) collective-permute-start(f32[64,128]{1,0:T(8,128)S(1)} %get-tuple-element.38.sent_ref), channel_id=1, source_target_pairs={{0,24},{8,16},{16,8},{24,0},{1,25},{9,17},{17,9},{25,1},{2,26},{10... | collective-permute-start | bytes 98312 | tf_op jit(solution)/shard_map/ppermute | solution.py:29
  35.5 2.1 %collective-permute-done.11.got_ref = f32[64,128]{1,0:T(8,128)S(1)} collective-permute-done((f32[64,128]{1,0:T(8,128)S(1)}, f32[64,128]{1,0:T(8,128)S(1)}, u32[]{:S(2)}, u32[]{:S(2)}) %collective-permute-start.11) | collective-permute-done | bytes 32800 | tf_op jit(solution)/shard_map/ppermute | solution.py:29
  37.6 0.4 level2.1.refs_3_
  38.0 0.8 %collective-permute-start.17 = (f32[64,384]{1,0:T(8,128)S(1)}, f32[64,384]{1,0:T(8,128)S(1)}, u32[]{:S(2)}, u32[]{:S(2)}) collective-permute-start(f32[64,384]{1,0:T(8,128)S(1)} %get-tuple-element.40.refs_0_), channel_id=1, source_target_pairs={{0,2},{1,3},{2,0},{3,1},{4,6},{5,7},{6,4},{7,5},{8,10},{9,11},{10,... | collective-permute-start | bytes 294920 | tf_op jit(solution)/shard_map/ppermute | solution.py:29
  38.8 1.8 %collective-permute-start.14 = (f32[64,384]{1,0:T(8,128)S(1)}, f32[64,384]{1,0:T(8,128)S(1)}, u32[]{:S(2)}, u32[]{:S(2)}) collective-permute-start(f32[64,384]{1,0:T(8,128)S(1)} %get-tuple-element.39), channel_id=1, source_target_pairs={{0,6},{1,7},{2,4},{3,5},{4,2},{5,3},{6,0},{7,1},{8,14},{9,15},{10,... | collective-permute-start | bytes 294920 | tf_op jit(solution)/shard_map/ppermute | solution.py:29
  40.6 1.0 %collective-permute-start.12 = (f32[64,384]{1,0:T(8,128)S(1)}, f32[64,384]{1,0:T(8,128)S(1)}, u32[]{:S(2)}, u32[]{:S(2)}) collective-permute-start(f32[64,384]{1,0:T(8,128)S(1)} %get-tuple-element.39), channel_id=1, source_target_pairs={{0,4},{1,5},{2,6},{3,7},{4,0},{5,1},{6,2},{7,3},{8,12},{9,13},{10,... | collective-permute-start | bytes 294920 | tf_op jit(solution)/shard_map/ppermute | solution.py:29
  41.6 0.0 collective-permute-start.16
  41.6 1.1 %collective-permute-done.17.refs_2_ = f32[64,384]{1,0:T(8,128)S(1)} collective-permute-done((f32[64,384]{1,0:T(8,128)S(1)}, f32[64,384]{1,0:T(8,128)S(1)}, u32[]{:S(2)}, u32[]{:S(2)}) %collective-permute-start.17) | collective-permute-done | bytes 98336 | tf_op jit(solution)/shard_map/ppermute | solution.py:29
  42.7 0.0 collective-permute-start.18
  42.7 1.6 %collective-permute-done.14.refs_2_ = f32[64,384]{1,0:T(8,128)S(1)} collective-permute-done((f32[64,384]{1,0:T(8,128)S(1)}, f32[64,384]{1,0:T(8,128)S(1)}, u32[]{:S(2)}, u32[]{:S(2)}) %collective-permute-start.14) | collective-permute-done | bytes 98336 | tf_op jit(solution)/shard_map/ppermute | solution.py:29
  44.4 0.0 collective-permute-start.15
  44.4 1.0 %collective-permute-done.12.refs_0_ = f32[64,384]{1,0:T(8,128)S(1)} collective-permute-done((f32[64,384]{1,0:T(8,128)S(1)}, f32[64,384]{1,0:T(8,128)S(1)}, u32[]{:S(2)}, u32[]{:S(2)}) %collective-permute-start.12) | collective-permute-done | bytes 98336 | tf_op jit(solution)/shard_map/ppermute | solution.py:29
  45.4 0.0 collective-permute-start.13
  45.4 0.0 collective-permute-done.16.refs_1_
  45.4 0.0 collective-permute-done.18.refs_3_
  45.4 0.0 copy-done
  45.4 3.5 %expand_near.1.refs_6_ = f32[4608,512]{1,0:T(8,128)} custom-call(f32[64,384]{1,0:T(8,128)S(1)} %get-tuple-element.40.refs_0_, f32[64,384]{1,0:T(8,128)S(1)} %collective-permute-done.16.refs_1_, f32[64,384]{1,0:T(8,128)S(1)} %collective-permute-done.17.refs_2_, f32[64,384]{1,0:T(8,128)S(1)} %collective-permute-done.18.refs_3_, ...), custom_call_target="tpu_custom_call" | custom-call | flops 2860000000 | tf_op jit(solution)/shard_map/expand_near/pallas_call | solution.py:408
  49.0 0.0 collective-permute-done.15.refs_3_
  49.0 0.0 collective-permute-done.13.refs_1_
  49.0 3.6 %expand_far.1 = f32[4608,512]{1,0:T(8,128)} custom-call(f32[64,384]{1,0:T(8,128)S(1)} %collective-permute-done.12.refs_0_, f32[64,384]{1,0:T(8,128)S(1)} %collective-permute-done.13.refs_1_, f32[64,384]{1,0:T(8,128)S(1)} %collective-permute-done.14.refs_2_, f32[64,384]{1,0:T(8,128)S(1)} %collective-permute-done.15.refs_3_, ...), custom_call_target="tpu_custom_call", output_to_operand_aliasing={{}: (6, {})} | custom-call | flops 2860000000 | tf_op jit(solution)/shard_map/expand_far/pallas_call | solution.py:408
  (6 shorter events, 0.1 us)
Async XLA Ops:
  0.0 4.8 %copy-start.1 = (bf16[18,256,256]{2,1,0:T(8,128)(2,1)S(1)}, bf16[18,256,256]{2,1,0:T(8,128)(2,1)}, u32[]{:S(2)}) copy-start(bf16[18,256,256]{2,1,0:T(8,128)(2,1)} %inv_ref.1) | copy-start | bytes 7077892
  0.0 4.8 %copy-start.2 = (s32[18,256]{1,0:T(8,128)S(1)}, s32[18,256]{1,0:T(8,128)}, u32[]{:S(2)}) copy-start(s32[18,256]{1,0:T(8,128)} %order_ref.1) | copy-start | bytes 55300
  4.2 1.8 %collective-permute-start = (f32[64,384]{1,0:T(8,128)S(1)}, f32[64,384]{1,0:T(8,128)S(1)}, u32[]{:S(2)}, u32[]{:S(2)}) collective-permute-start(f32[64,384]{1,0:T(8,128)S(1)} %get-tuple-element.25), channel_id=1, source_target_pairs={{0,1},{1,0},{2,3},{3,2},{4,5},{5,4},{6,7},{7,6},{8,9},{9,8},{10,11... | collective-permute-start | bytes 294920 | tf_op jit(solution)/shard_map/ppermute | solution.py:29
  6.0 4.8 %slice-start = ((s8[4718592]{0:T(1024)(128)(4,1)}), s8[4194304]{0:T(1024)(128)(4,1)S(1)}, s32[]{:S(2)}) async-start(s8[4718592]{0:T(1024)(128)(4,1)} %bitcast), calls=%async_computation | async-start | bytes 8388608
  6.1 7.1 %collective-permute-start.1 = (f32[64,384]{1,0:T(8,128)S(1)}, f32[64,384]{1,0:T(8,128)S(1)}, u32[]{:S(2)}, u32[]{:S(2)}) collective-permute-start(f32[64,384]{1,0:T(8,128)S(1)} %add.2.after_ref.mine_ref), channel_id=1, source_target_pairs={{0,2},{1,3},{2,0},{3,1},{4,6},{5,7},{6,4},{7,5},{8,10},{9,11},{10,... | collective-permute-start | bytes 294920 | tf_op jit(solution)/shard_map/ppermute | solution.py:29
  8.6 2.1 %slice-start.1 = ((s8[4718592]{0:T(1024)(128)(4,1)}), s8[524288]{0:T(1024)(128)(4,1)S(1)}, s32[]{:S(2)}) async-start(s8[4718592]{0:T(1024)(128)(4,1)} %bitcast), calls=%async_computation.1 | async-start | bytes 1048576
  12.9 4.3 %collective-permute-start.4 = (f32[2,64,384]{2,1,0:T(8,128)S(1)}, f32[2,64,384]{2,1,0:T(8,128)S(1)}, u32[]{:S(2)}, u32[]{:S(2)}) collective-permute-start(f32[2,64,384]{2,1,0:T(8,128)S(1)} %get-tuple-element.31), channel_id=1, source_target_pairs={{0,1},{1,0},{2,3},{3,2},{4,5},{5,4},{6,7},{7,6},{8,9},{9,8},{10,11... | collective-permute-start | bytes 589832 | tf_op jit(solution)/shard_map/ppermute | solution.py:29
  13.2 7.7 %copy-start.3 = (s32[3,128]{1,0:T(4,128)S(1)}, s32[3,128]{1,0:T(4,128)}, u32[]{:S(2)}) copy-start(s32[3,128]{1,0:T(4,128)} %perm_ref.1) | copy-start | bytes 4612
  15.3 4.0 %collective-permute-start.2 = (f32[2,64,384]{2,1,0:T(8,128)S(1)}, f32[2,64,384]{2,1,0:T(8,128)S(1)}, u32[]{:S(2)}, u32[]{:S(2)}) collective-permute-start(f32[2,64,384]{2,1,0:T(8,128)S(1)} %get-tuple-element.27), channel_id=1, source_target_pairs={{0,1},{1,0},{2,3},{3,2},{4,5},{5,4},{6,7},{7,6},{8,9},{9,8},{10,11... | collective-permute-start | bytes 589832 | tf_op jit(solution)/shard_map/ppermute | solution.py:29
  15.7 7.4 %collective-permute-start.7 = (f32[64,384]{1,0:T(8,128)S(1)}, f32[64,384]{1,0:T(8,128)S(1)}, u32[]{:S(2)}, u32[]{:S(2)}) collective-permute-start(f32[64,384]{1,0:T(8,128)S(1)} %add.3.after_ref.mine_ref), channel_id=1, source_target_pairs={{0,4},{1,5},{2,6},{3,7},{4,0},{5,1},{6,2},{7,3},{8,12},{9,13},{10,... | collective-permute-start | bytes 294920 | tf_op jit(solution)/shard_map/ppermute | solution.py:29
  17.2 7.6 %collective-permute-start.5 = (f32[64,384]{1,0:T(8,128)S(1)}, f32[64,384]{1,0:T(8,128)S(1)}, u32[]{:S(2)}, u32[]{:S(2)}) collective-permute-start(f32[64,384]{1,0:T(8,128)S(1)} %get-tuple-element.32), channel_id=1, source_target_pairs={{0,4},{1,5},{2,6},{3,7},{4,0},{5,1},{6,2},{7,3},{8,12},{9,13},{10,... | collective-permute-start | bytes 294920 | tf_op jit(solution)/shard_map/ppermute | solution.py:29
  17.8 7.0 %collective-permute-start.6 = (f32[64,384]{1,0:T(8,128)S(1)}, f32[64,384]{1,0:T(8,128)S(1)}, u32[]{:S(2)}, u32[]{:S(2)}) collective-permute-start(f32[64,384]{1,0:T(8,128)S(1)} %get-tuple-element.33), channel_id=1, source_target_pairs={{0,6},{1,7},{2,4},{3,5},{4,2},{5,3},{6,0},{7,1},{8,14},{9,15},{10,... | collective-permute-start | bytes 294920 | tf_op jit(solution)/shard_map/ppermute | solution.py:29
  19.3 5.9 %collective-permute-start.3 = (f32[64,384]{1,0:T(8,128)S(1)}, f32[64,384]{1,0:T(8,128)S(1)}, u32[]{:S(2)}, u32[]{:S(2)}) collective-permute-start(f32[64,384]{1,0:T(8,128)S(1)} %get-tuple-element.29), channel_id=1, source_target_pairs={{0,2},{1,3},{2,0},{3,1},{4,6},{5,7},{6,4},{7,5},{8,10},{9,11},{10,... | collective-permute-start | bytes 294920 | tf_op jit(solution)/shard_map/ppermute | solution.py:29
  23.0 2.6 %collective-permute-start.8 = (f32[64,384]{1,0:T(8,128)S(1)}, f32[64,384]{1,0:T(8,128)S(1)}, u32[]{:S(2)}, u32[]{:S(2)}) collective-permute-start(f32[64,384]{1,0:T(8,128)S(1)} %add.3.after_ref.mine_ref), channel_id=1, source_target_pairs={{0,1},{1,0},{2,3},{3,2},{4,5},{5,4},{6,7},{7,6},{8,9},{9,8},{10,11... | collective-permute-start | bytes 294920 | tf_op jit(solution)/shard_map/ppermute | solution.py:29
  23.1 2.6 %collective-permute-start.9 = (f32[64,384]{1,0:T(8,128)S(1)}, f32[64,384]{1,0:T(8,128)S(1)}, u32[]{:S(2)}, u32[]{:S(2)}) collective-permute-start(f32[64,384]{1,0:T(8,128)S(1)} %collective-permute-done.7.theirs_ref), channel_id=1, source_target_pairs={{0,1},{1,0},{2,3},{3,2},{4,5},{5,4},{6,7},{7,6},{8,9},{9,8},{10,11... | collective-permute-start | bytes 294920 | tf_op jit(solution)/shard_map/ppermute | solution.py:29
  26.1 5.0 %collective-permute-start.10 = (f32[256,128]{1,0:T(8,128)S(1)}, f32[256,128]{1,0:T(8,128)S(1)}, u32[]{:S(2)}, u32[]{:S(2)}) collective-permute-start(f32[256,128]{1,0:T(8,128)S(1)} %correct.1.sent_ref), channel_id=1, source_target_pairs={{0,8},{8,0},{16,24},{24,16},{1,9},{9,1},{17,25},{25,17},{2,10},{10... | collective-permute-start | bytes 393224 | tf_op jit(solution)/shard_map/ppermute | solution.py:29
  31.9 13.6 %copy-start = (bf16[3,4608,128]{2,1,0:T(8,128)(2,1)S(1)}, bf16[3,4608,128]{2,1,0:T(8,128)(2,1)}, u32[]{:S(2)}) copy-start(bf16[3,4608,128]{2,1,0:T(8,128)(2,1)} %refs_5_.3) | copy-start | bytes 10616836
  31.9 5.8 %collective-permute-start.11 = (f32[64,128]{1,0:T(8,128)S(1)}, f32[64,128]{1,0:T(8,128)S(1)}, u32[]{:S(2)}, u32[]{:S(2)}) collective-permute-start(f32[64,128]{1,0:T(8,128)S(1)} %get-tuple-element.38.sent_ref), channel_id=1, source_target_pairs={{0,24},{8,16},{16,8},{24,0},{1,25},{9,17},{17,9},{25,1},{2,26},{10... | collective-permute-start | bytes 98312 | tf_op jit(solution)/shard_map/ppermute | solution.py:29
  38.0 4.7 %collective-permute-start.17 = (f32[64,384]{1,0:T(8,128)S(1)}, f32[64,384]{1,0:T(8,128)S(1)}, u32[]{:S(2)}, u32[]{:S(2)}) collective-permute-start(f32[64,384]{1,0:T(8,128)S(1)} %get-tuple-element.40.refs_0_), channel_id=1, source_target_pairs={{0,2},{1,3},{2,0},{3,1},{4,6},{5,7},{6,4},{7,5},{8,10},{9,11},{10,... | collective-permute-start | bytes 294920 | tf_op jit(solution)/shard_map/ppermute | solution.py:29
  38.8 5.5 %collective-permute-start.14 = (f32[64,384]{1,0:T(8,128)S(1)}, f32[64,384]{1,0:T(8,128)S(1)}, u32[]{:S(2)}, u32[]{:S(2)}) collective-permute-start(f32[64,384]{1,0:T(8,128)S(1)} %get-tuple-element.39), channel_id=1, source_target_pairs={{0,6},{1,7},{2,4},{3,5},{4,2},{5,3},{6,0},{7,1},{8,14},{9,15},{10,... | collective-permute-start | bytes 294920 | tf_op jit(solution)/shard_map/ppermute | solution.py:29
  40.6 4.8 %collective-permute-start.12 = (f32[64,384]{1,0:T(8,128)S(1)}, f32[64,384]{1,0:T(8,128)S(1)}, u32[]{:S(2)}, u32[]{:S(2)}) collective-permute-start(f32[64,384]{1,0:T(8,128)S(1)} %get-tuple-element.39), channel_id=1, source_target_pairs={{0,4},{1,5},{2,6},{3,7},{4,0},{5,1},{6,2},{7,3},{8,12},{9,13},{10,... | collective-permute-start | bytes 294920 | tf_op jit(solution)/shard_map/ppermute | solution.py:29
  41.6 3.8 %collective-permute-start.16 = (f32[64,384]{1,0:T(8,128)S(1)}, f32[64,384]{1,0:T(8,128)S(1)}, u32[]{:S(2)}, u32[]{:S(2)}) collective-permute-start(f32[64,384]{1,0:T(8,128)S(1)} %get-tuple-element.40.refs_0_), channel_id=1, source_target_pairs={{0,1},{1,0},{2,3},{3,2},{4,5},{5,4},{6,7},{7,6},{8,9},{9,8},{10,11... | collective-permute-start | bytes 294920 | tf_op jit(solution)/shard_map/ppermute | solution.py:29
  42.7 2.7 %collective-permute-start.18 = (f32[64,384]{1,0:T(8,128)S(1)}, f32[64,384]{1,0:T(8,128)S(1)}, u32[]{:S(2)}, u32[]{:S(2)}) collective-permute-start(f32[64,384]{1,0:T(8,128)S(1)} %collective-permute-done.17.refs_2_), channel_id=1, source_target_pairs={{0,1},{1,0},{2,3},{3,2},{4,5},{5,4},{6,7},{7,6},{8,9},{9,8},{10,11... | collective-permute-start | bytes 294920 | tf_op jit(solution)/shard_map/ppermute | solution.py:29
  44.4 4.6 %collective-permute-start.15 = (f32[64,384]{1,0:T(8,128)S(1)}, f32[64,384]{1,0:T(8,128)S(1)}, u32[]{:S(2)}, u32[]{:S(2)}) collective-permute-start(f32[64,384]{1,0:T(8,128)S(1)} %collective-permute-done.14.refs_2_), channel_id=1, source_target_pairs={{0,1},{1,0},{2,3},{3,2},{4,5},{5,4},{6,7},{7,6},{8,9},{9,8},{10,11... | collective-permute-start | bytes 294920 | tf_op jit(solution)/shard_map/ppermute | solution.py:29
  45.4 3.6 %collective-permute-start.13 = (f32[64,384]{1,0:T(8,128)S(1)}, f32[64,384]{1,0:T(8,128)S(1)}, u32[]{:S(2)}, u32[]{:S(2)}) collective-permute-start(f32[64,384]{1,0:T(8,128)S(1)} %collective-permute-done.12.refs_0_), channel_id=1, source_target_pairs={{0,1},{1,0},{2,3},{3,2},{4,5},{5,4},{6,7},{7,6},{8,9},{9,8},{10,11... | collective-permute-start | bytes 294920 | tf_op jit(solution)/shard_map/ppermute | solution.py:29

commit v7 on v6

--- a/solution.py
+++ b/solution.py
@@ -52,8 +52,8 @@
         )
 
     for step in range(steps):
-        for priority, copy in enumerate(copies(step)):
-            copy.start(priority=priority)
+        for copy in copies(step):
+            copy.start()
     gram_ref[...] = jnp.zeros_like(gram_ref)
 
     def body(step, _):
@@ -114,27 +114,21 @@
     lax.fori_loop(0, moved_ref.shape[0] // per_step, body, 0)
 
 
-def half_lanes(far, me, count, part):
-    side = me // (count // 2)
-    return pl.ds(pl.multiple_of((1 - side if far else side) * part, part), part)
-
-
-def project_kernel(far, factor_ref, rhs_ref, after_ref, keep_ref, send_ref, total_ref):
-    kinds = factor_ref.shape[0] // 2
-    slots, share, _ = keep_ref.shape
-    part = total_ref.shape[0]
-    me = lax.axis_index("rows")
-    total = dot(factor_ref[...], rhs_ref[:, half_lanes(far, me, 4 * slots, part)], (1, 0))
-    total_ref[...] = (total[:kinds] + total[kinds:]).T
-    for slot in range(slots):
-        for ref, mask in ((keep_ref, 2 * slot), (send_ref, 2 * slot + 1)):
-            owner = (me ^ mask) % (2 * slots)
-            ref[slot] = total_ref[pl.ds(pl.multiple_of(owner * share, share), share), :]
-
-
-def merge_kernel(keep_ref, got_ref, *out_refs):
+def project_kernel(other, factor_ref, rhs_ref, after_ref, out_ref):
+    kinds, part = out_ref.shape
+    core = lax.axis_index("rows") % 2
+    lanes = pl.ds(pl.multiple_of((1 - core if other else core) * part, part), part)
+    total = dot(factor_ref[...], rhs_ref[:, lanes], (1, 0))
+    out_ref[...] = total[:kinds] + total[kinds:]
+
+
+def merge_kernel(keep_ref, got_ref, *refs):
+    out_refs, flip_ref = refs[:-1], refs[-1]
+    share = out_refs[0].shape[0]
+    chip = lax.axis_index("rows") // 2
+    flip_ref[...] = (keep_ref[...] + got_ref[...]).T
     for slot, out_ref in enumerate(out_refs):
-        out_ref[...] = keep_ref[slot] + got_ref[slot]
+        out_ref[...] = flip_ref[pl.ds(pl.multiple_of((chip ^ slot) * share, share), share), :]
 
 
 def add_kernel(mine_ref, got_ref, out_ref):
@@ -229,40 +223,33 @@
 
 
 def pack_kernel(*refs):
-    levels = len(refs) - 3
     other_ref, own_refs, own_out, other_out = refs[0], refs[1:-2], refs[-2], refs[-1]
     own = [ref[...] for ref in own_refs]
     own_out[...] = jnp.concatenate(own, axis=1)
     other_out[...] = jnp.concatenate([other_ref[...]] + own[1:], axis=1)
 
 
-def expand_kernel(far, levels, per_step, width, slots, *refs):
-    piece_refs = refs[:2 * slots]
-    first_ref, left_ref = refs[2 * slots:2 * slots + 2]
-    out_ref, flip_ref, factor_ref, out_buf, sems = refs[-5:]
+def expand_kernel(levels, tile, count, *refs):
+    piece_refs = refs[:count]
+    first_ref, left_ref, out_ref, flip_ref, factor_ref, out_buf, sems = refs[count:]
     share, kinds = piece_refs[0].shape
-    tile = per_step * width
-    steps = out_buf.shape[0] // tile
     me = lax.axis_index("rows")
-    lanes = half_lanes(far, me, 4 * slots, out_buf.shape[1])
-    for slot in range(2 * slots):
-        owner = (me ^ slot) % (2 * slots)
-        flip_ref[pl.ds(pl.multiple_of(owner * share, share), share), :] = piece_refs[slot][...]
+    for slot, ref in enumerate(piece_refs):
+        owner = me ^ slot
+        row = (owner % 2 * (count // 2) + owner // 2) * share
+        flip_ref[pl.ds(pl.multiple_of(row, share), share), :] = ref[...]
     high_part, low_part = halves(flip_ref[...].T)
     factor_ref[:kinds, :] = high_part
     factor_ref[kinds:, :] = low_part
-
-    def copy(step):
-        rows = pl.ds(step * tile, tile)
-        return pltpu.make_async_copy(out_buf.at[rows], out_ref.at[rows, lanes], sems.at[step])
-
-    for step in range(steps):
+    copies = []
+    for step in range(out_buf.shape[0] // tile):
         rows = pl.ds(step * tile, tile)
         left = jnp.concatenate([left_ref[l, rows, :] for l in range(levels)] * 2, axis=1)
-        out_buf[rows, :] = first_ref[rows, lanes] - dot(left, factor_ref[...], (1, 0))
-        copy(step).start(priority=step % 2)
-    for step in range(steps):
-        copy(step).wait()
+        out_buf[rows, :] = first_ref[rows, :] - dot(left, factor_ref[...], (1, 0))
+        copies.append(pltpu.make_async_copy(out_buf.at[rows], out_ref.at[rows], sems.at[step]))
+        copies[-1].start(priority=step % 2)
+    for copy in copies:
+        copy.wait()
 
 
 def settings(mib, micros):
@@ -325,30 +312,28 @@
         **settings(8, 2.4),
     )(moved, flipped, gram)
 
-    def project(far, after):
+    def project(other, after):
         return pl.pallas_call(
-            functools.partial(project_kernel, far),
-            out_shape=[floats(slots // 2, share, kinds)] * 2,
-            scratch_shapes=[pltpu.VMEM((columns // 2, kinds), jnp.float32)],
-            name="project_far" if far else "project_near",
-            **settings(12, 2.1),
+            functools.partial(project_kernel, other),
+            out_shape=floats(kinds, columns // 2),
+            name="project_other" if other else "project_own",
+            **settings(12, 1 if other else 8),
         )(factors, rhs, after)
 
-    def merge(keep, got):
-        return pl.pallas_call(
-            merge_kernel, out_shape=[floats(share, kinds)] * (slots // 2), name="merge", **settings(8, 0.1),
-        )(keep, got)
-
-    keep_far, send_far = project(True, gram)
-    got_far = swap(send_far, "rows", 1)
+    send = project(True, gram)
+    got = swap(send, "rows", 1)
     mask = 2
     while mask < slots:
         gram = add(gram, swap(gram, "rows", mask))
         mask *= 2
-    keep_near, send_near = project(False, gram)
-    got_near = swap(send_near, "rows", 1)
-    merged = [None] * (slots // 2) + list(merge(keep_far, got_far))
-    merged[:slots // 2] = merge(keep_near, got_near)
+    keep = project(False, gram)
+    merged = pl.pallas_call(
+        merge_kernel,
+        out_shape=[floats(share, kinds)] * slots,
+        scratch_shapes=[pltpu.VMEM((columns // 2, kinds), jnp.float32)],
+        name="merge",
+        **settings(8, 0.4),
+    )(keep, got)
     parts = [merged[0]] + [swap(merged[s], "rows", 2 * s) for s in range(1, slots)]
     gram_other = swap(gram, "rows", slots)
     grams = [gram, gram_other, swap(gram, "rows", 1), swap(gram_other, "rows", 1)]
@@ -386,7 +371,7 @@
     coefs = [own]
     for level in range(1, levels):
         last = level + 1 == levels
-        arrived = swap(message, "leaf", 2 ** level - 1)
+        arrived = swap(message, "leaf", 2 ** (level - 1))
         outs = pl.pallas_call(
             functools.partial(level_kernel, levels, level, share),
             out_shape=[floats(share, rank)] + ([] if last else [message_shape(level + 1)]),
@@ -395,38 +380,28 @@
         )(message, arrived, prepared, first)
         coefs.append(outs[0])
         message = outs[-1]
-    own_pack, other_pack = pl.pallas_call(
-        pack_kernel, out_shape=[floats(share, kinds)] * 2, name="pack", **settings(8, 0.2),
+
+    packs = pl.pallas_call(
+        pack_kernel, out_shape=[floats(share, kinds)] * 2, name="pack", **settings(8, 0.1),
     )(other, *coefs)
-
-    steps = nblocks // per_step
-
-    def expand(far, *extra):
-        begin = count // 2 if far else 0
-        operands = (*pieces[begin:begin + count // 2], first, left_basis, *extra)
-        inner = [pl.BlockSpec()] * (count // 2 + 2) + [pl.BlockSpec(memory_space=pl.ANY)] * len(extra)
-        return pl.pallas_call(
-            functools.partial(expand_kernel, far, levels, per_step, width, slots // 2),
-            in_specs=inner,
-            out_specs=pl.BlockSpec(memory_space=pl.ANY),
-            out_shape=floats(rows, columns),
-            scratch_shapes=[
-                pltpu.VMEM((columns // 2, kinds), jnp.float32),
-                pltpu.VMEM((2 * kinds, columns // 2), jnp.bfloat16),
-                pltpu.VMEM((rows, columns // 2), jnp.float32),
-                pltpu.SemaphoreType.DMA((steps,)),
-            ],
-            input_output_aliases={len(operands) - 1: 0} if extra else {},
-            name="expand_far" if far else "expand_near",
-            **settings(14, 2.6),
-        )(*operands)
-
     pieces = []
     for slot in range(slots):
-        piece = own_pack if slot < slots // 2 else other_pack
+        piece = packs[0 if slot < slots // 2 else 1]
         piece = swap(piece, "rows", 2 * slot) if slot > 0 else piece
         pieces += [piece, swap(piece, "rows", 1)]
-    return expand(True, expand(False))
+    return pl.pallas_call(
+        functools.partial(expand_kernel, levels, per_step * width, count),
+        out_specs=pl.BlockSpec(memory_space=pl.ANY),
+        out_shape=floats(rows, columns),
+        scratch_shapes=[
+            pltpu.VMEM((columns, kinds), jnp.float32),
+            pltpu.VMEM((2 * kinds, columns), jnp.bfloat16),
+            pltpu.VMEM((rows, columns), jnp.float32),
+            pltpu.SemaphoreType.DMA((nblocks // per_step,)),
+        ],
+        name="expand",
+        **settings(16, 5),
+    )(*pieces, first, left_basis)
 
 
 def solution(mesh):

time: 52.8 us -> 49.5 us (0.938)
  Pallas kernels: 25.2 us -> 22.4 us
  starting transfers between devices: 18.3 us -> 17 us
  waiting for transfers between devices: 8.8 us -> 9.73 us
    pallas_call x6 -> x4, Pallas kernels: 11.4 us -> 9.47 us  [the longest x1 5.26 us: per_device(): pl.pallas_call(functools.partial(expand_kernel, levels, per_step * width,...]
    ppermute x19 -> x18, starting transfers between devices: 18.3 us -> 17 us  [swap(): return lax.ppermute(value, axis, [(i, i ^ mask) for i in range(count)])]
    ppermute x19 -> x18, waiting for transfers between devices: 8.8 us -> 9.73 us  [swap(): return lax.ppermute(value, axis, [(i, i ^ mask) for i in range(count)])]
    pallas_call x1, Pallas kernels: 4.23 us -> 3.34 us  [per_device(): pl.pallas_call(functools.partial(gram_kernel, levels, per_step, width), i...]
  transfers between devices with their start and end apart: 19 -> 18, of which waited for: 7 -> 8; matrix products, arithmetic and copies ran while one was open for 0% -> 0% of each run, Pallas kernels for 30% -> 25%
where the time goes in v7:
time: 49.5 us; the launch traced here: 49.4 us
  Pallas kernels  22.4 us (45%)
  starting transfers between devices  17 us (34%)
  waiting for transfers between devices  9.73 us (20%)
    ppermute x18, starting transfers between devices, swap(): return lax.ppermute(value, axis, [(i, i ^ mask) for i in range(count)])  17 us
    ppermute x18, waiting for transfers between devices, swap(): return lax.ppermute(value, axis, [(i, i ^ mask) for i in range(count)])  9.73 us
    pallas_call x1, Pallas kernels, per_device(): pl.pallas_call(functools.partial(expand_kernel, levels, per_step * width,...  5.26 us
    pallas_call x2, Pallas kernels, project(): pl.pallas_call(functools.partial(project_kernel, other), out_shape=floats...  3.99 us
    pallas_call x1, Pallas kernels, per_device(): pl.pallas_call(functools.partial(gram_kernel, levels, per_step, width), i...  3.34 us
    pallas_call x1, Pallas kernels, per_device(): pl.pallas_call(functools.partial(solve_kernel, per_step, width), out_shap...  2.22 us
    pallas_call x1, Pallas kernels, per_device(): pl.pallas_call(functools.partial(weigh_kernel, per_step, width), out_shap...  2.12 us
    pallas_call x1, Pallas kernels, per_device(): pl.pallas_call(functools.partial(prepare_kernel, levels), in_specs=[pl.Bl...  2.1 us
  transfers between devices with their start and end apart: 18, of which 8 were waited for; matrix products, arithmetic and copies ran while one was open for 0% of the time, Pallas kernels for 25%

profile of v7, /device:TPU:0, one launch (start us, length us, event | category | flops | bytes accessed | tf_op | source)
XLA Modules:
  0.0 49.4 jit_solution(6791227305010978983)
XLA Ops:
  0.0 0.0 copy-start.1
  0.0 0.0 copy-start.2
  0.0 3.3 %gram.1 = (bf16[384,4608]{1,0:T(8,128)(2,1)S(1)}, f32[64,384]{1,0:T(8,128)S(1)}, f32[64,384]{1,0:T(8,128)S(1)}) custom-call(bf16[3,4608,128]{2,1,0:T(8,128)(2,1)} %right_ref.1, bf16[3,4608,128]{2,1,0:T(8,128)(2,1)} %refs_9_.1), custom_call_target="tpu_custom_call" | custom-call | flops 3300000000 | tf_op jit(solution)/shard_map/gram/pallas_call | solution.py:279
  3.4 0.5 %collective-permute-start = (f32[64,384]{1,0:T(8,128)S(1)}, f32[64,384]{1,0:T(8,128)S(1)}, u32[]{:S(2)}, u32[]{:S(2)}) collective-permute-start(f32[64,384]{1,0:T(8,128)S(1)} %get-tuple-element.21), channel_id=1, source_target_pairs={{0,1},{1,0},{2,3},{3,2},{4,5},{5,4},{6,7},{7,6},{8,9},{9,8},{10,11... | collective-permute-start | bytes 294920 | tf_op jit(solution)/shard_map/ppermute | solution.py:29
  3.9 0.0 copy-done.1
  3.9 0.0 copy-done.2
  3.9 1.2 %permute.1.moved_ref = bf16[18,256,256]{2,1,0:T(8,128)(2,1)S(1)} custom-call(s32[18,256]{1,0:T(8,128)S(1)} %copy-done.2, bf16[18,256,256]{2,1,0:T(8,128)(2,1)S(1)} %copy-done.1), custom_call_target="tpu_custom_call" | custom-call | flops 1650000000 | tf_op jit(solution)/shard_map/permute/pallas_call | solution.py:295
  5.1 0.0 collective-permute-done.got_ref
  5.1 0.0 slice-start
  5.2 2.6 %collective-permute-start.1 = (f32[64,384]{1,0:T(8,128)S(1)}, f32[64,384]{1,0:T(8,128)S(1)}, u32[]{:S(2)}, u32[]{:S(2)}) collective-permute-start(f32[64,384]{1,0:T(8,128)S(1)} %add.2.after_ref.mine_ref), channel_id=1, source_target_pairs={{0,2},{1,3},{2,0},{3,1},{4,6},{5,7},{6,4},{7,5},{8,10},{9,11},{10,... | collective-permute-start | bytes 294920 | tf_op jit(solution)/shard_map/ppermute | solution.py:29
  7.8 0.0 slice-start.1
  7.8 2.1 %weigh.1.factor_ref = bf16[768,4608]{1,0:T(8,128)(2,1)S(1)} custom-call(bf16[18,256,256]{2,1,0:T(8,128)(2,1)S(1)} %permute.1.moved_ref, bf16[384,4608]{1,0:T(8,128)(2,1)S(1)} %get-tuple-element.19.flip_ref, f32[64,384]{1,0:T(8,128)S(1)} %add.2.after_ref.mine_ref), custom_call_target="tpu_custom_call" | custom-call | flops 2640000000 | tf_op jit(solution)/shard_map/weigh/pallas_call | solution.py:308
  9.9 0.0 slice-done
  9.9 0.0 slice-done.1
  9.9 2.0 %project_other.1 = f32[384,256]{1,0:T(8,128)S(1)} custom-call(bf16[768,4608]{1,0:T(8,128)(2,1)S(1)} %weigh.1.factor_ref, bf16[4608,512]{1,0:T(8,128)(2,1)S(1)} %bitcast.1, f32[64,384]{1,0:T(8,128)S(1)} %add.2.after_ref.mine_ref), custom_call_target="tpu_custom_call" | custom-call | flops 1100000000 | tf_op jit(solution)/shard_map/project_other/pallas_call | solution.py:316
  11.9 0.2 collective-permute-start.2
  12.2 0.0 collective-permute-done.1.got_ref
  12.2 0.0 copy-start.3
  12.2 1.6 %collective-permute-start.6 = (f32[64,384]{1,0:T(8,128)S(1)}, f32[64,384]{1,0:T(8,128)S(1)}, u32[]{:S(2)}, u32[]{:S(2)}) collective-permute-start(f32[64,384]{1,0:T(8,128)S(1)} %add.3.after_ref.mine_ref), channel_id=1, source_target_pairs={{0,4},{1,5},{2,6},{3,7},{4,0},{5,1},{6,2},{7,3},{8,12},{9,13},{10,... | collective-permute-start | bytes 294920 | tf_op jit(solution)/shard_map/ppermute | solution.py:29
  13.8 2.0 %project_own.1.keep_ref = f32[384,256]{1,0:T(8,128)S(1)} custom-call(bf16[768,4608]{1,0:T(8,128)(2,1)S(1)} %weigh.1.factor_ref, bf16[4608,512]{1,0:T(8,128)(2,1)S(1)} %bitcast.1, f32[64,384]{1,0:T(8,128)S(1)} %add.3.after_ref.mine_ref), custom_call_target="tpu_custom_call" | custom-call | flops 8800000000 | tf_op jit(solution)/shard_map/project_own/pallas_call | solution.py:316
  15.8 0.0 collective-permute-done.2.got_ref
  15.8 0.2 merge.1
  16.0 0.8 %collective-permute-start.3 = (f32[64,384]{1,0:T(8,128)S(1)}, f32[64,384]{1,0:T(8,128)S(1)}, u32[]{:S(2)}, u32[]{:S(2)}) collective-permute-start(f32[64,384]{1,0:T(8,128)S(1)} %get-tuple-element.23), channel_id=1, source_target_pairs={{0,2},{1,3},{2,0},{3,1},{4,6},{5,7},{6,4},{7,5},{8,10},{9,11},{10,... | collective-permute-start | bytes 294920 | tf_op jit(solution)/shard_map/ppermute | solution.py:29
  16.8 0.5 %collective-permute-start.4 = (f32[64,384]{1,0:T(8,128)S(1)}, f32[64,384]{1,0:T(8,128)S(1)}, u32[]{:S(2)}, u32[]{:S(2)}) collective-permute-start(f32[64,384]{1,0:T(8,128)S(1)} %get-tuple-element.24), channel_id=1, source_target_pairs={{0,4},{1,5},{2,6},{3,7},{4,0},{5,1},{6,2},{7,3},{8,12},{9,13},{10,... | collective-permute-start | bytes 294920 | tf_op jit(solution)/shard_map/ppermute | solution.py:29
  17.3 2.2 %collective-permute-start.5 = (f32[64,384]{1,0:T(8,128)S(1)}, f32[64,384]{1,0:T(8,128)S(1)}, u32[]{:S(2)}, u32[]{:S(2)}) collective-permute-start(f32[64,384]{1,0:T(8,128)S(1)} %get-tuple-element.25), channel_id=1, source_target_pairs={{0,6},{1,7},{2,4},{3,5},{4,2},{5,3},{6,0},{7,1},{8,14},{9,15},{10,... | collective-permute-start | bytes 294920 | tf_op jit(solution)/shard_map/ppermute | solution.py:29
  19.6 0.0 copy-done.3
  19.6 2.1 %prepare.1.refs_4_.joined_ref = f32[3,256,256]{2,1,0:T(8,128)S(1)} custom-call(f32[7,256,256]{2,1,0:T(8,128)} %joined_ref.1, s32[3,128]{1,0:T(4,128)S(1)} %copy-done.3), custom_call_target="tpu_custom_call" | custom-call | flops 2200000000 | tf_op jit(solution)/shard_map/prepare/pallas_call | solution.py:347
  21.7 0.1 collective-permute-start.7
  21.8 0.0 collective-permute-done.6.theirs_ref
  21.8 0.5 collective-permute-start.8
  22.3 0.0 collective-permute-done.3.refs_1_
  22.3 1.1 %collective-permute-done.4.refs_2_ = f32[64,384]{1,0:T(8,128)S(1)} collective-permute-done((f32[64,384]{1,0:T(8,128)S(1)}, f32[64,384]{1,0:T(8,128)S(1)}, u32[]{:S(2)}, u32[]{:S(2)}) %collective-permute-start.4) | collective-permute-done | bytes 98336 | tf_op jit(solution)/shard_map/ppermute | solution.py:29
  23.3 0.0 collective-permute-done.5.refs_3_
  23.3 0.4 node.1
  23.7 0.0 collective-permute-done.7.pair_mine_ref
  23.7 0.0 collective-permute-done.8.pair_theirs_ref
  23.7 0.4 correct.1.sent_ref
  24.1 1.7 %collective-permute-start.9 = (f32[256,128]{1,0:T(8,128)S(1)}, f32[256,128]{1,0:T(8,128)S(1)}, u32[]{:S(2)}, u32[]{:S(2)}) collective-permute-start(f32[256,128]{1,0:T(8,128)S(1)} %correct.1.sent_ref), channel_id=1, source_target_pairs={{0,8},{8,0},{16,24},{24,16},{1,9},{9,1},{17,25},{25,17},{2,10},{10... | collective-permute-start | bytes 393224 | tf_op jit(solution)/shard_map/ppermute | solution.py:29
  25.8 2.2 %solve.1.after_ref.refs_8_ = f32[4608,512]{1,0:T(8,128)S(1)} custom-call(bf16[18,256,256]{2,1,0:T(8,128)(2,1)S(1)} %permute.1.moved_ref, bf16[4608,512]{1,0:T(8,128)(2,1)S(1)} %bitcast.1, f32[64,384]{1,0:T(8,128)S(1)} %get-tuple-element.22.refs_0_.after_ref), custom_call_target="tpu_custom_call" | custom-call | flops 1870000000 | tf_op jit(solution)/shard_map/solve/pallas_call | solution.py:340
  28.0 1.4 %collective-permute-done.9.got_ref = f32[256,128]{1,0:T(8,128)S(1)} collective-permute-done((f32[256,128]{1,0:T(8,128)S(1)}, f32[256,128]{1,0:T(8,128)S(1)}, u32[]{:S(2)}, u32[]{:S(2)}) %collective-permute-start.9) | collective-permute-done | bytes 131104 | tf_op jit(solution)/shard_map/ppermute | solution.py:29
  29.4 0.8 %level1.1 = (f32[64,128]{1,0:T(8,128)S(1)}, f32[64,128]{1,0:T(8,128)S(1)}) custom-call(f32[256,128]{1,0:T(8,128)S(1)} %correct.1.sent_ref, f32[256,128]{1,0:T(8,128)S(1)} %collective-permute-done.9.got_ref, f32[3,256,256]{2,1,0:T(8,128)S(1)} %prepare.1.refs_4_.joined_ref, f32[4608,512]{1,0:T(8,128)S(1)} %solve.1.after_ref.refs_8_), custom_call_target="tpu_custom_call" | custom-call | flops 770000000 | tf_op jit(solution)/shard_map/level1/pallas_call | solution.py:375
  30.2 0.0 copy-start
  30.2 2.7 %collective-permute-start.10 = (f32[64,128]{1,0:T(8,128)S(1)}, f32[64,128]{1,0:T(8,128)S(1)}, u32[]{:S(2)}, u32[]{:S(2)}) collective-permute-start(f32[64,128]{1,0:T(8,128)S(1)} %get-tuple-element.30.sent_ref), channel_id=1, source_target_pairs={{0,16},{8,24},{16,0},{24,8},{1,17},{9,25},{17,1},{25,9},{2,18},{10... | collective-permute-start | bytes 98312 | tf_op jit(solution)/shard_map/ppermute | solution.py:29
  32.9 2.2 %collective-permute-done.10.got_ref = f32[64,128]{1,0:T(8,128)S(1)} collective-permute-done((f32[64,128]{1,0:T(8,128)S(1)}, f32[64,128]{1,0:T(8,128)S(1)}, u32[]{:S(2)}, u32[]{:S(2)}) %collective-permute-start.10) | collective-permute-done | bytes 32800 | tf_op jit(solution)/shard_map/ppermute | solution.py:29
  35.1 0.4 level2.1.refs_3_
  35.5 1.5 %collective-permute-start.16 = (f32[64,384]{1,0:T(8,128)S(1)}, f32[64,384]{1,0:T(8,128)S(1)}, u32[]{:S(2)}, u32[]{:S(2)}) collective-permute-start(f32[64,384]{1,0:T(8,128)S(1)} %get-tuple-element.32), channel_id=1, source_target_pairs={{0,6},{1,7},{2,4},{3,5},{4,2},{5,3},{6,0},{7,1},{8,14},{9,15},{10,... | collective-permute-start | bytes 294920 | tf_op jit(solution)/shard_map/ppermute | solution.py:29
  37.0 1.1 %collective-permute-start.14 = (f32[64,384]{1,0:T(8,128)S(1)}, f32[64,384]{1,0:T(8,128)S(1)}, u32[]{:S(2)}, u32[]{:S(2)}) collective-permute-start(f32[64,384]{1,0:T(8,128)S(1)} %get-tuple-element.32), channel_id=1, source_target_pairs={{0,4},{1,5},{2,6},{3,7},{4,0},{5,1},{6,2},{7,3},{8,12},{9,13},{10,... | collective-permute-start | bytes 294920 | tf_op jit(solution)/shard_map/ppermute | solution.py:29
  38.2 0.9 %collective-permute-start.12 = (f32[64,384]{1,0:T(8,128)S(1)}, f32[64,384]{1,0:T(8,128)S(1)}, u32[]{:S(2)}, u32[]{:S(2)}) collective-permute-start(f32[64,384]{1,0:T(8,128)S(1)} %get-tuple-element.31.refs_0_), channel_id=1, source_target_pairs={{0,2},{1,3},{2,0},{3,1},{4,6},{5,7},{6,4},{7,5},{8,10},{9,11},{10,... | collective-permute-start | bytes 294920 | tf_op jit(solution)/shard_map/ppermute | solution.py:29
  39.0 0.0 collective-permute-start.11
  39.0 2.1 %collective-permute-done.16.refs_6_ = f32[64,384]{1,0:T(8,128)S(1)} collective-permute-done((f32[64,384]{1,0:T(8,128)S(1)}, f32[64,384]{1,0:T(8,128)S(1)}, u32[]{:S(2)}, u32[]{:S(2)}) %collective-permute-start.16) | collective-permute-done | bytes 98336 | tf_op jit(solution)/shard_map/ppermute | solution.py:29
  41.1 0.0 collective-permute-start.17
  41.1 1.0 %collective-permute-done.14.refs_4_ = f32[64,384]{1,0:T(8,128)S(1)} collective-permute-done((f32[64,384]{1,0:T(8,128)S(1)}, f32[64,384]{1,0:T(8,128)S(1)}, u32[]{:S(2)}, u32[]{:S(2)}) %collective-permute-start.14) | collective-permute-done | bytes 98336 | tf_op jit(solution)/shard_map/ppermute | solution.py:29
  42.1 0.0 collective-permute-start.15
  42.1 0.7 %collective-permute-done.12.refs_2_ = f32[64,384]{1,0:T(8,128)S(1)} collective-permute-done((f32[64,384]{1,0:T(8,128)S(1)}, f32[64,384]{1,0:T(8,128)S(1)}, u32[]{:S(2)}, u32[]{:S(2)}) %collective-permute-start.12) | collective-permute-done | bytes 98336 | tf_op jit(solution)/shard_map/ppermute | solution.py:29
  42.8 0.0 collective-permute-start.13
  42.8 0.0 collective-permute-done.11.refs_1_
  42.8 0.0 collective-permute-done.17.refs_7_
  42.8 0.6 %collective-permute-done.15.refs_5_ = f32[64,384]{1,0:T(8,128)S(1)} collective-permute-done((f32[64,384]{1,0:T(8,128)S(1)}, f32[64,384]{1,0:T(8,128)S(1)}, u32[]{:S(2)}, u32[]{:S(2)}) %collective-permute-start.15) | collective-permute-done | bytes 98336 | tf_op jit(solution)/shard_map/ppermute | solution.py:29
  43.4 0.7 %collective-permute-done.13.refs_3_ = f32[64,384]{1,0:T(8,128)S(1)} collective-permute-done((f32[64,384]{1,0:T(8,128)S(1)}, f32[64,384]{1,0:T(8,128)S(1)}, u32[]{:S(2)}, u32[]{:S(2)}) %collective-permute-start.13) | collective-permute-done | bytes 98336 | tf_op jit(solution)/shard_map/ppermute | solution.py:29
  44.1 0.0 copy-done
  44.1 5.3 %expand.1 = f32[4608,512]{1,0:T(8,128)} custom-call(f32[64,384]{1,0:T(8,128)S(1)} %get-tuple-element.31.refs_0_, f32[64,384]{1,0:T(8,128)S(1)} %collective-permute-done.11.refs_1_, f32[64,384]{1,0:T(8,128)S(1)} %collective-permute-done.12.refs_2_, f32[64,384]{1,0:T(8,128)S(1)} %collective-permute-done.13.refs_3_, ...), custom_call_target="tpu_custom_call" | custom-call | flops 5500000256 | tf_op jit(solution)/shard_map/expand/pallas_call | solution.py:392
  (4 shorter events, 0.0 us)
Async XLA Ops:
  0.0 3.9 %copy-start.1 = (bf16[18,256,256]{2,1,0:T(8,128)(2,1)S(1)}, bf16[18,256,256]{2,1,0:T(8,128)(2,1)}, u32[]{:S(2)}) copy-start(bf16[18,256,256]{2,1,0:T(8,128)(2,1)} %inv_ref.1) | copy-start | bytes 7077892
  0.0 3.9 %copy-start.2 = (s32[18,256]{1,0:T(8,128)S(1)}, s32[18,256]{1,0:T(8,128)}, u32[]{:S(2)}) copy-start(s32[18,256]{1,0:T(8,128)} %order_ref.1) | copy-start | bytes 55300
  3.4 1.8 %collective-permute-start = (f32[64,384]{1,0:T(8,128)S(1)}, f32[64,384]{1,0:T(8,128)S(1)}, u32[]{:S(2)}, u32[]{:S(2)}) collective-permute-start(f32[64,384]{1,0:T(8,128)S(1)} %get-tuple-element.21), channel_id=1, source_target_pairs={{0,1},{1,0},{2,3},{3,2},{4,5},{5,4},{6,7},{7,6},{8,9},{9,8},{10,11... | collective-permute-start | bytes 294920 | tf_op jit(solution)/shard_map/ppermute | solution.py:29
  5.1 4.8 %slice-start = ((s8[4718592]{0:T(1024)(128)(4,1)}), s8[4194304]{0:T(1024)(128)(4,1)S(1)}, s32[]{:S(2)}) async-start(s8[4718592]{0:T(1024)(128)(4,1)} %bitcast), calls=%async_computation | async-start | bytes 8388608
  5.2 7.0 %collective-permute-start.1 = (f32[64,384]{1,0:T(8,128)S(1)}, f32[64,384]{1,0:T(8,128)S(1)}, u32[]{:S(2)}, u32[]{:S(2)}) collective-permute-start(f32[64,384]{1,0:T(8,128)S(1)} %add.2.after_ref.mine_ref), channel_id=1, source_target_pairs={{0,2},{1,3},{2,0},{3,1},{4,6},{5,7},{6,4},{7,5},{8,10},{9,11},{10,... | collective-permute-start | bytes 294920 | tf_op jit(solution)/shard_map/ppermute | solution.py:29
  7.8 2.1 %slice-start.1 = ((s8[4718592]{0:T(1024)(128)(4,1)}), s8[524288]{0:T(1024)(128)(4,1)S(1)}, s32[]{:S(2)}) async-start(s8[4718592]{0:T(1024)(128)(4,1)} %bitcast), calls=%async_computation.1 | async-start | bytes 1048576
  11.9 3.9 %collective-permute-start.2 = (f32[384,256]{1,0:T(8,128)S(1)}, f32[384,256]{1,0:T(8,128)S(1)}, u32[]{:S(2)}, u32[]{:S(2)}) collective-permute-start(f32[384,256]{1,0:T(8,128)S(1)} %project_other.1), channel_id=1, source_target_pairs={{0,1},{1,0},{2,3},{3,2},{4,5},{5,4},{6,7},{7,6},{8,9},{9,8},{10,11... | collective-permute-start | bytes 1179656 | tf_op jit(solution)/shard_map/ppermute | solution.py:29
  12.2 7.4 %copy-start.3 = (s32[3,128]{1,0:T(4,128)S(1)}, s32[3,128]{1,0:T(4,128)}, u32[]{:S(2)}) copy-start(s32[3,128]{1,0:T(4,128)} %perm_ref.1) | copy-start | bytes 4612
  12.2 9.6 %collective-permute-start.6 = (f32[64,384]{1,0:T(8,128)S(1)}, f32[64,384]{1,0:T(8,128)S(1)}, u32[]{:S(2)}, u32[]{:S(2)}) collective-permute-start(f32[64,384]{1,0:T(8,128)S(1)} %add.3.after_ref.mine_ref), channel_id=1, source_target_pairs={{0,4},{1,5},{2,6},{3,7},{4,0},{5,1},{6,2},{7,3},{8,12},{9,13},{10,... | collective-permute-start | bytes 294920 | tf_op jit(solution)/shard_map/ppermute | solution.py:29
  16.0 6.3 %collective-permute-start.3 = (f32[64,384]{1,0:T(8,128)S(1)}, f32[64,384]{1,0:T(8,128)S(1)}, u32[]{:S(2)}, u32[]{:S(2)}) collective-permute-start(f32[64,384]{1,0:T(8,128)S(1)} %get-tuple-element.23), channel_id=1, source_target_pairs={{0,2},{1,3},{2,0},{3,1},{4,6},{5,7},{6,4},{7,5},{8,10},{9,11},{10,... | collective-permute-start | bytes 294920 | tf_op jit(solution)/shard_map/ppermute | solution.py:29
  16.8 6.5 %collective-permute-start.4 = (f32[64,384]{1,0:T(8,128)S(1)}, f32[64,384]{1,0:T(8,128)S(1)}, u32[]{:S(2)}, u32[]{:S(2)}) collective-permute-start(f32[64,384]{1,0:T(8,128)S(1)} %get-tuple-element.24), channel_id=1, source_target_pairs={{0,4},{1,5},{2,6},{3,7},{4,0},{5,1},{6,2},{7,3},{8,12},{9,13},{10,... | collective-permute-start | bytes 294920 | tf_op jit(solution)/shard_map/ppermute | solution.py:29
  17.3 6.0 %collective-permute-start.5 = (f32[64,384]{1,0:T(8,128)S(1)}, f32[64,384]{1,0:T(8,128)S(1)}, u32[]{:S(2)}, u32[]{:S(2)}) collective-permute-start(f32[64,384]{1,0:T(8,128)S(1)} %get-tuple-element.25), channel_id=1, source_target_pairs={{0,6},{1,7},{2,4},{3,5},{4,2},{5,3},{6,0},{7,1},{8,14},{9,15},{10,... | collective-permute-start | bytes 294920 | tf_op jit(solution)/shard_map/ppermute | solution.py:29
  21.7 2.0 %collective-permute-start.7 = (f32[64,384]{1,0:T(8,128)S(1)}, f32[64,384]{1,0:T(8,128)S(1)}, u32[]{:S(2)}, u32[]{:S(2)}) collective-permute-start(f32[64,384]{1,0:T(8,128)S(1)} %add.3.after_ref.mine_ref), channel_id=1, source_target_pairs={{0,1},{1,0},{2,3},{3,2},{4,5},{5,4},{6,7},{7,6},{8,9},{9,8},{10,11... | collective-permute-start | bytes 294920 | tf_op jit(solution)/shard_map/ppermute | solution.py:29
  21.8 1.9 %collective-permute-start.8 = (f32[64,384]{1,0:T(8,128)S(1)}, f32[64,384]{1,0:T(8,128)S(1)}, u32[]{:S(2)}, u32[]{:S(2)}) collective-permute-start(f32[64,384]{1,0:T(8,128)S(1)} %collective-permute-done.6.theirs_ref), channel_id=1, source_target_pairs={{0,1},{1,0},{2,3},{3,2},{4,5},{5,4},{6,7},{7,6},{8,9},{9,8},{10,11... | collective-permute-start | bytes 294920 | tf_op jit(solution)/shard_map/ppermute | solution.py:29
  24.1 5.3 %collective-permute-start.9 = (f32[256,128]{1,0:T(8,128)S(1)}, f32[256,128]{1,0:T(8,128)S(1)}, u32[]{:S(2)}, u32[]{:S(2)}) collective-permute-start(f32[256,128]{1,0:T(8,128)S(1)} %correct.1.sent_ref), channel_id=1, source_target_pairs={{0,8},{8,0},{16,24},{24,16},{1,9},{9,1},{17,25},{25,17},{2,10},{10... | collective-permute-start | bytes 393224 | tf_op jit(solution)/shard_map/ppermute | solution.py:29
  30.2 13.9 %copy-start = (bf16[3,4608,128]{2,1,0:T(8,128)(2,1)S(1)}, bf16[3,4608,128]{2,1,0:T(8,128)(2,1)}, u32[]{:S(2)}) copy-start(bf16[3,4608,128]{2,1,0:T(8,128)(2,1)} %refs_9_.1) | copy-start | bytes 10616836
  30.2 4.9 %collective-permute-start.10 = (f32[64,128]{1,0:T(8,128)S(1)}, f32[64,128]{1,0:T(8,128)S(1)}, u32[]{:S(2)}, u32[]{:S(2)}) collective-permute-start(f32[64,128]{1,0:T(8,128)S(1)} %get-tuple-element.30.sent_ref), channel_id=1, source_target_pairs={{0,16},{8,24},{16,0},{24,8},{1,17},{9,25},{17,1},{25,9},{2,18},{10... | collective-permute-start | bytes 98312 | tf_op jit(solution)/shard_map/ppermute | solution.py:29
  35.5 5.6 %collective-permute-start.16 = (f32[64,384]{1,0:T(8,128)S(1)}, f32[64,384]{1,0:T(8,128)S(1)}, u32[]{:S(2)}, u32[]{:S(2)}) collective-permute-start(f32[64,384]{1,0:T(8,128)S(1)} %get-tuple-element.32), channel_id=1, source_target_pairs={{0,6},{1,7},{2,4},{3,5},{4,2},{5,3},{6,0},{7,1},{8,14},{9,15},{10,... | collective-permute-start | bytes 294920 | tf_op jit(solution)/shard_map/ppermute | solution.py:29
  37.0 5.1 %collective-permute-start.14 = (f32[64,384]{1,0:T(8,128)S(1)}, f32[64,384]{1,0:T(8,128)S(1)}, u32[]{:S(2)}, u32[]{:S(2)}) collective-permute-start(f32[64,384]{1,0:T(8,128)S(1)} %get-tuple-element.32), channel_id=1, source_target_pairs={{0,4},{1,5},{2,6},{3,7},{4,0},{5,1},{6,2},{7,3},{8,12},{9,13},{10,... | collective-permute-start | bytes 294920 | tf_op jit(solution)/shard_map/ppermute | solution.py:29
  38.2 4.6 %collective-permute-start.12 = (f32[64,384]{1,0:T(8,128)S(1)}, f32[64,384]{1,0:T(8,128)S(1)}, u32[]{:S(2)}, u32[]{:S(2)}) collective-permute-start(f32[64,384]{1,0:T(8,128)S(1)} %get-tuple-element.31.refs_0_), channel_id=1, source_target_pairs={{0,2},{1,3},{2,0},{3,1},{4,6},{5,7},{6,4},{7,5},{8,10},{9,11},{10,... | collective-permute-start | bytes 294920 | tf_op jit(solution)/shard_map/ppermute | solution.py:29
  39.0 3.8 %collective-permute-start.11 = (f32[64,384]{1,0:T(8,128)S(1)}, f32[64,384]{1,0:T(8,128)S(1)}, u32[]{:S(2)}, u32[]{:S(2)}) collective-permute-start(f32[64,384]{1,0:T(8,128)S(1)} %get-tuple-element.31.refs_0_), channel_id=1, source_target_pairs={{0,1},{1,0},{2,3},{3,2},{4,5},{5,4},{6,7},{7,6},{8,9},{9,8},{10,11... | collective-permute-start | bytes 294920 | tf_op jit(solution)/shard_map/ppermute | solution.py:29
  41.1 1.7 %collective-permute-start.17 = (f32[64,384]{1,0:T(8,128)S(1)}, f32[64,384]{1,0:T(8,128)S(1)}, u32[]{:S(2)}, u32[]{:S(2)}) collective-permute-start(f32[64,384]{1,0:T(8,128)S(1)} %collective-permute-done.16.refs_6_), channel_id=1, source_target_pairs={{0,1},{1,0},{2,3},{3,2},{4,5},{5,4},{6,7},{7,6},{8,9},{9,8},{10,11... | collective-permute-start | bytes 294920 | tf_op jit(solution)/shard_map/ppermute | solution.py:29
  42.1 1.3 %collective-permute-start.15 = (f32[64,384]{1,0:T(8,128)S(1)}, f32[64,384]{1,0:T(8,128)S(1)}, u32[]{:S(2)}, u32[]{:S(2)}) collective-permute-start(f32[64,384]{1,0:T(8,128)S(1)} %collective-permute-done.14.refs_4_), channel_id=1, source_target_pairs={{0,1},{1,0},{2,3},{3,2},{4,5},{5,4},{6,7},{7,6},{8,9},{9,8},{10,11... | collective-permute-start | bytes 294920 | tf_op jit(solution)/shard_map/ppermute | solution.py:29
  42.8 1.3 %collective-permute-start.13 = (f32[64,384]{1,0:T(8,128)S(1)}, f32[64,384]{1,0:T(8,128)S(1)}, u32[]{:S(2)}, u32[]{:S(2)}) collective-permute-start(f32[64,384]{1,0:T(8,128)S(1)} %collective-permute-done.12.refs_2_), channel_id=1, source_target_pairs={{0,1},{1,0},{2,3},{3,2},{4,5},{5,4},{6,7},{7,6},{8,9},{9,8},{10,11... | collective-permute-start | bytes 294920 | tf_op jit(solution)/shard_map/ppermute | solution.py:29

commit v8 on v7

--- a/solution.py
+++ b/solution.py
@@ -37,10 +37,9 @@
     return [(level, below) for level in range(levels) for below in range(first, level)]
 
 
-def gram_kernel(levels, per_step, width, right_ref, left_ref, flip_ref, keep_ref, send_ref,
+def gram_kernel(levels, per_step, width, right_ref, left_ref, flip_ref, out_ref,
                 right_buf, left_buf, gram_ref, sems):
     rank = right_ref.shape[2]
-    half = rank // 2
     tile = per_step * width
     steps = right_ref.shape[1] // tile
 
@@ -67,12 +66,9 @@
         return 0
 
     lax.fori_loop(0, steps, body, 0)
-    core = lax.axis_index("rows") % 2
     for spot, (level, below) in enumerate(below_pairs(levels)):
-        lanes = pl.ds(spot * rank, rank)
-        for ref, side in ((keep_ref, core), (send_ref, 1 - core)):
-            rows = pl.ds(pl.multiple_of((level - 1) * rank + side * half, half), half)
-            ref[:, lanes] = gram_ref[rows, pl.ds(below * rank, rank)]
+        rows = pl.ds((level - 1) * rank, rank)
+        out_ref[:, pl.ds(spot * rank, rank)] = gram_ref[rows, pl.ds(below * rank, rank)]
 
 
 def permute_kernel(per_step, width, order_ref, inv_ref, moved_ref):
@@ -103,7 +99,9 @@
     lax.fori_loop(0, moved_ref.shape[0] // per_step, body, 0)
 
 
-def solve_kernel(per_step, width, moved_ref, rhs_ref, after_ref, out_ref):
+def solve_kernel(per_step, width, moved_ref, rhs_ref, *refs):
+    out_ref = refs[-1]
+
     def body(step, _):
         for b in range(per_step):
             block = step * per_step + b
@@ -178,9 +176,7 @@
 
 def correct_kernel(levels, rank, own_ref, other_ref, rest_ref, mine_ref, theirs_ref, pair_mine_ref,
                    pair_theirs_ref, message_ref):
-    core = lax.axis_index("rows") % 2
-    grams = [jnp.concatenate(by_side(core, mine_ref[...], pair_mine_ref[...]), axis=0),
-             jnp.concatenate(by_side(core, theirs_ref[...], pair_theirs_ref[...]), axis=0)]
+    grams = [mine_ref[...] + pair_mine_ref[...], theirs_ref[...] + pair_theirs_ref[...]]
     pairs = below_pairs(levels)
     lanes = {pair: slice(spot * rank, (spot + 1) * rank) for spot, pair in enumerate(pairs)}
     joint = jnp.concatenate(
@@ -223,28 +219,44 @@
 
 
 def pack_kernel(*refs):
-    other_ref, own_refs, own_out, other_out = refs[0], refs[1:-2], refs[-2], refs[-1]
-    own = [ref[...] for ref in own_refs]
-    own_out[...] = jnp.concatenate(own, axis=1)
-    other_out[...] = jnp.concatenate([other_ref[...]] + own[1:], axis=1)
-
-
-def expand_kernel(levels, tile, count, *refs):
-    piece_refs = refs[:count]
-    first_ref, left_ref, out_ref, flip_ref, factor_ref, out_buf, sems = refs[count:]
-    share, kinds = piece_refs[0].shape
+    refs[-1][...] = jnp.concatenate([ref[...] for ref in refs[:-1]], axis=1)
+
+
+def stack_kernel(after_ref, *refs):
+    for slot, ref in enumerate(refs[:-1]):
+        refs[-1][slot] = ref[...]
+
+
+def split_factor(pieces, flip_ref, factor_ref):
+    share, kinds = pieces[0].shape
+    slots = len(pieces) // 2
     me = lax.axis_index("rows")
-    for slot, ref in enumerate(piece_refs):
-        owner = me ^ slot
-        row = (owner % 2 * (count // 2) + owner // 2) * share
+    for mask, ref in enumerate(pieces):
+        owner = me ^ mask
+        row = (owner % 2 * slots + owner // 2) * share
         flip_ref[pl.ds(pl.multiple_of(row, share), share), :] = ref[...]
     high_part, low_part = halves(flip_ref[...].T)
     factor_ref[:kinds, :] = high_part
     factor_ref[kinds:, :] = low_part
+
+
+def apply_kernel(tile, own_ref, pair_ref, first_ref, left_ref, out_ref, flip_ref, factor_ref):
+    pieces = [ref.at[slot] for slot in range(own_ref.shape[0]) for ref in (own_ref, pair_ref)]
+    split_factor(pieces, flip_ref, factor_ref)
+    for row in range(0, out_ref.shape[0], tile):
+        rows = pl.ds(row, tile)
+        left = jnp.concatenate([left_ref[0, rows, :]] * 2, axis=1)
+        out_ref[rows, :] = first_ref[rows, :] - dot(left, factor_ref[...], (1, 0))
+
+
+def expand_kernel(levels, tile, count, *refs):
+    piece_refs = refs[:count]
+    first_ref, left_ref, out_ref, flip_ref, factor_ref, out_buf, sems = refs[count:]
+    split_factor(piece_refs, flip_ref, factor_ref)
     copies = []
     for step in range(out_buf.shape[0] // tile):
         rows = pl.ds(step * tile, tile)
-        left = jnp.concatenate([left_ref[l, rows, :] for l in range(levels)] * 2, axis=1)
+        left = jnp.concatenate([left_ref[l, rows, :] for l in range(1, levels)] * 2, axis=1)
         out_buf[rows, :] = first_ref[rows, :] - dot(left, factor_ref[...], (1, 0))
         copies.append(pltpu.make_async_copy(out_buf.at[rows], out_ref.at[rows], sems.at[step]))
         copies[-1].start(priority=step % 2)
@@ -276,10 +288,10 @@
     gram_lanes = len(below_pairs(levels)) * rank
 
     per_step = blocks_per_step(nblocks, 3)
-    flipped, gram_keep, gram_send = pl.pallas_call(
+    flipped, gram = pl.pallas_call(
         functools.partial(gram_kernel, levels, per_step, width),
         in_specs=[pl.BlockSpec(memory_space=pltpu.HBM)] * 2,
-        out_shape=[jax.ShapeDtypeStruct((kinds, rows), jnp.bfloat16)] + [floats(rank // 2, gram_lanes)] * 2,
+        out_shape=[jax.ShapeDtypeStruct((kinds, rows), jnp.bfloat16), floats(rank, gram_lanes)],
         scratch_shapes=[
             pltpu.VMEM((levels, rows, rank), jnp.bfloat16),
             pltpu.VMEM((levels - 1, rows, rank), jnp.bfloat16),
@@ -290,7 +302,6 @@
         **settings(24, 3),
     )(pltpu.with_memory_space_constraint(right_basis, pltpu.HBM),
       pltpu.with_memory_space_constraint(left_basis, pltpu.HBM))
-    gram_got = swap(gram_send, "rows", 1)
 
     moved = pl.pallas_call(
         functools.partial(permute_kernel, blocks_per_step(nblocks, 6), width),
@@ -304,7 +315,6 @@
             add_kernel, out_shape=floats(*mine.shape), name="add", **settings(8, 0.1),
         )(mine, got)
 
-    gram = add(gram_keep, gram_got)
     factors = pl.pallas_call(
         functools.partial(weigh_kernel, per_step, width),
         out_shape=jax.ShapeDtypeStruct((2 * kinds, rows), jnp.bfloat16),
@@ -337,13 +347,6 @@
     parts = [merged[0]] + [swap(merged[s], "rows", 2 * s) for s in range(1, slots)]
     gram_other = swap(gram, "rows", slots)
     grams = [gram, gram_other, swap(gram, "rows", 1), swap(gram_other, "rows", 1)]
-    first = pl.pallas_call(
-        functools.partial(solve_kernel, per_step, width),
-        out_shape=floats(rows, columns),
-        name="solve",
-        **settings(8, 1.7),
-    )(moved, rhs, merged[0])
-
     prepared = pl.pallas_call(
         functools.partial(prepare_kernel, levels),
         in_specs=[pl.BlockSpec(memory_space=pltpu.HBM), pl.BlockSpec()],
@@ -368,7 +371,15 @@
         name="correct",
         **settings(8, 1),
     )(own, other, rest, *grams)
-    coefs = [own]
+    early = [own] + [swap(own if slot < slots // 2 else other, "rows", 2 * slot) for slot in range(1, slots)]
+    first = pl.pallas_call(
+        functools.partial(solve_kernel, per_step, width),
+        out_shape=floats(rows, columns),
+        name="solve",
+        **settings(8, 8),
+    )(moved, rhs, merged[0])
+
+    coefs = []
     for level in range(1, levels):
         last = level + 1 == levels
         arrived = swap(message, "leaf", 2 ** (level - 1))
@@ -376,32 +387,44 @@
             functools.partial(level_kernel, levels, level, share),
             out_shape=[floats(share, rank)] + ([] if last else [message_shape(level + 1)]),
             name=f"level{level}",
-            **settings(8, 0.7),
-        )(message, arrived, prepared, first)
+            **settings(8, 1 if last else 6),
+        )(message, arrived, prepared, first if last else arrived)
         coefs.append(outs[0])
         message = outs[-1]
-
-    packs = pl.pallas_call(
-        pack_kernel, out_shape=[floats(share, kinds)] * 2, name="pack", **settings(8, 0.1),
-    )(other, *coefs)
+    stack = pl.pallas_call(
+        stack_kernel, out_shape=floats(slots, share, rank), name="stack", **settings(8, 0.1),
+    )(first, *early)
+    second = pl.pallas_call(
+        functools.partial(apply_kernel, per_step * width),
+        out_shape=floats(rows, columns),
+        scratch_shapes=[
+            pltpu.VMEM((columns, rank), jnp.float32),
+            pltpu.VMEM((2 * rank, columns), jnp.bfloat16),
+        ],
+        name="apply",
+        **settings(8, 1.8),
+    )(stack, swap(stack, "rows", 1), first, left_basis)
+
+    pack = pl.pallas_call(
+        pack_kernel, out_shape=floats(share, size), name="pack", **settings(8, 0.1),
+    )(*coefs)
     pieces = []
     for slot in range(slots):
-        piece = packs[0 if slot < slots // 2 else 1]
-        piece = swap(piece, "rows", 2 * slot) if slot > 0 else piece
+        piece = swap(pack, "rows", 2 * slot) if slot > 0 else pack
         pieces += [piece, swap(piece, "rows", 1)]
     return pl.pallas_call(
         functools.partial(expand_kernel, levels, per_step * width, count),
         out_specs=pl.BlockSpec(memory_space=pl.ANY),
         out_shape=floats(rows, columns),
         scratch_shapes=[
-            pltpu.VMEM((columns, kinds), jnp.float32),
-            pltpu.VMEM((2 * kinds, columns), jnp.bfloat16),
+            pltpu.VMEM((columns, size), jnp.float32),
+            pltpu.VMEM((2 * size, columns), jnp.bfloat16),
             pltpu.VMEM((rows, columns), jnp.float32),
             pltpu.SemaphoreType.DMA((nblocks // per_step,)),
         ],
         name="expand",
         **settings(16, 5),
-    )(*pieces, first, left_basis)
+    )(*pieces, second, left_basis)
 
 
 def solution(mesh):

time: 49.5 us -> 49.5 us (level)
  waiting for transfers between devices: 9.73 us -> 5.2 us
  starting transfers between devices: 17 us -> 20.5 us
  Pallas kernels: 22.4 us -> 23.3 us
    ppermute x18 -> x21, waiting for transfers between devices: 9.73 us -> 5.2 us  [swap(): return lax.ppermute(value, axis, [(i, i ^ mask) for i in range(count)])]
    ppermute x18 -> x21, starting transfers between devices: 17 us -> 20.5 us  [swap(): return lax.ppermute(value, axis, [(i, i ^ mask) for i in range(count)])]
    pallas_call x1 -> x3, Pallas kernels: 0.02 us -> 1.59 us  [the longest x1 1.57 us: per_device(): pl.pallas_call(functools.partial(apply_kernel, per_step * width), out_sha...]
    pallas_call x1, Pallas kernels: 5.26 us -> 4.51 us  [per_device(): pl.pallas_call(functools.partial(expand_kernel, levels, per_step * width,...]
  transfers between devices with their start and end apart: 18 -> 21, of which waited for: 8 -> 4; matrix products, arithmetic and copies ran while one was open for 0% -> 0% of each run, Pallas kernels for 25% -> 30%
where the time goes in v8:
time: 49.5 us; the launch traced here: 49.3 us
  Pallas kernels  23.3 us (47%)
  starting transfers between devices  20.5 us (41%)
  waiting for transfers between devices  5.2 us (11%)
    ppermute x21, starting transfers between devices, swap(): return lax.ppermute(value, axis, [(i, i ^ mask) for i in range(count)])  20.5 us
    ppermute x21, waiting for transfers between devices, swap(): return lax.ppermute(value, axis, [(i, i ^ mask) for i in range(count)])  5.2 us
    pallas_call x1, Pallas kernels, per_device(): pl.pallas_call(functools.partial(expand_kernel, levels, per_step * width,...  4.51 us
    pallas_call x2, Pallas kernels, project(): pl.pallas_call(functools.partial(project_kernel, other), out_shape=floats...  3.99 us
    pallas_call x1, Pallas kernels, per_device(): pl.pallas_call(functools.partial(gram_kernel, levels, per_step, width), i...  3.34 us
    pallas_call x1, Pallas kernels, per_device(): pl.pallas_call(functools.partial(solve_kernel, per_step, width), out_shap...  2.22 us
    pallas_call x1, Pallas kernels, per_device(): pl.pallas_call(functools.partial(weigh_kernel, per_step, width), out_shap...  2.13 us
    pallas_call x1, Pallas kernels, per_device(): pl.pallas_call(functools.partial(prepare_kernel, levels), in_specs=[pl.Bl...  2.11 us
  transfers between devices with their start and end apart: 21, of which 4 were waited for; matrix products, arithmetic and copies ran while one was open for 0% of the time, Pallas kernels for 30%

profile of v8, /device:TPU:0, one launch (start us, length us, event | category | flops | bytes accessed | tf_op | source)
XLA Modules:
  0.0 49.3 jit_solution(10518508726744234949)
XLA Ops:
  0.0 3.3 %gram.1 = (bf16[384,4608]{1,0:T(8,128)(2,1)S(1)}, f32[128,384]{1,0:T(8,128)S(1)}) custom-call(bf16[3,4608,128]{2,1,0:T(8,128)(2,1)} %right_ref.1, bf16[3,4608,128]{2,1,0:T(8,128)(2,1)} %refs_9_.1), custom_call_target="tpu_custom_call" | custom-call | flops 3300000000 | tf_op jit(solution)/shard_map/gram/pallas_call | solution.py:291
  3.3 3.0 %collective-permute-start = (f32[128,384]{1,0:T(8,128)S(1)}, f32[128,384]{1,0:T(8,128)S(1)}, u32[]{:S(2)}, u32[]{:S(2)}) collective-permute-start(f32[128,384]{1,0:T(8,128)S(1)} %get-tuple-element.17.after_ref.mine_ref), channel_id=1, source_target_pairs={{0,2},{1,3},{2,0},{3,1},{4,6},{5,7},{6,4},{7,5},{8,10},{9,11},{10,... | collective-permute-start | bytes 589832 | tf_op jit(solution)/shard_map/ppermute | solution.py:29
  6.4 0.0 copy-done.1
  6.4 0.0 copy-done.2
  6.4 1.2 %permute.1.moved_ref = bf16[18,256,256]{2,1,0:T(8,128)(2,1)S(1)} custom-call(s32[18,256]{1,0:T(8,128)S(1)} %copy-done.2, bf16[18,256,256]{2,1,0:T(8,128)(2,1)S(1)} %copy-done.1), custom_call_target="tpu_custom_call" | custom-call | flops 1650000000 | tf_op jit(solution)/shard_map/permute/pallas_call | solution.py:306
  7.6 0.0 slice-start.1
  7.6 2.1 %weigh.1.factor_ref = bf16[768,4608]{1,0:T(8,128)(2,1)S(1)} custom-call(bf16[18,256,256]{2,1,0:T(8,128)(2,1)S(1)} %permute.1.moved_ref, bf16[384,4608]{1,0:T(8,128)(2,1)S(1)} %get-tuple-element.16.flip_ref, f32[128,384]{1,0:T(8,128)S(1)} %get-tuple-element.17.after_ref.mine_ref), custom_call_target="tpu_custom_call" | custom-call | flops 2640000000 | tf_op jit(solution)/shard_map/weigh/pallas_call | solution.py:318
  9.8 0.0 slice-done
  9.8 0.0 slice-done.1
  9.8 2.0 %project_other.1 = f32[384,256]{1,0:T(8,128)S(1)} custom-call(bf16[768,4608]{1,0:T(8,128)(2,1)S(1)} %weigh.1.factor_ref, bf16[4608,512]{1,0:T(8,128)(2,1)S(1)} %bitcast.1, f32[128,384]{1,0:T(8,128)S(1)} %get-tuple-element.17.after_ref.mine_ref), custom_call_target="tpu_custom_call" | custom-call | flops 1100000000 | tf_op jit(solution)/shard_map/project_other/pallas_call | solution.py:326
  11.8 0.1 collective-permute-start.1
  11.9 0.0 collective-permute-done.got_ref
  11.9 0.0 copy-start.3
  11.9 0.5 %collective-permute-start.6 = (f32[128,384]{1,0:T(8,128)S(1)}, f32[128,384]{1,0:T(8,128)S(1)}, u32[]{:S(2)}, u32[]{:S(2)}) collective-permute-start(f32[128,384]{1,0:T(8,128)S(1)} %add.1.after_ref.mine_ref), channel_id=1, source_target_pairs={{0,1},{1,0},{2,3},{3,2},{4,5},{5,4},{6,7},{7,6},{8,9},{9,8},{10,11... | collective-permute-start | bytes 589832 | tf_op jit(solution)/shard_map/ppermute | solution.py:29
  12.5 1.5 %collective-permute-start.5 = (f32[128,384]{1,0:T(8,128)S(1)}, f32[128,384]{1,0:T(8,128)S(1)}, u32[]{:S(2)}, u32[]{:S(2)}) collective-permute-start(f32[128,384]{1,0:T(8,128)S(1)} %add.1.after_ref.mine_ref), channel_id=1, source_target_pairs={{0,4},{1,5},{2,6},{3,7},{4,0},{5,1},{6,2},{7,3},{8,12},{9,13},{10,... | collective-permute-start | bytes 589832 | tf_op jit(solution)/shard_map/ppermute | solution.py:29
  14.0 2.0 %project_own.1.keep_ref = f32[384,256]{1,0:T(8,128)S(1)} custom-call(bf16[768,4608]{1,0:T(8,128)(2,1)S(1)} %weigh.1.factor_ref, bf16[4608,512]{1,0:T(8,128)(2,1)S(1)} %bitcast.1, f32[128,384]{1,0:T(8,128)S(1)} %add.1.after_ref.mine_ref), custom_call_target="tpu_custom_call" | custom-call | flops 8800000000 | tf_op jit(solution)/shard_map/project_own/pallas_call | solution.py:326
  16.0 0.0 collective-permute-done.1.got_ref
  16.0 0.2 merge.1
  16.2 0.8 %collective-permute-start.2 = (f32[64,384]{1,0:T(8,128)S(1)}, f32[64,384]{1,0:T(8,128)S(1)}, u32[]{:S(2)}, u32[]{:S(2)}) collective-permute-start(f32[64,384]{1,0:T(8,128)S(1)} %get-tuple-element.19), channel_id=1, source_target_pairs={{0,2},{1,3},{2,0},{3,1},{4,6},{5,7},{6,4},{7,5},{8,10},{9,11},{10,... | collective-permute-start | bytes 294920 | tf_op jit(solution)/shard_map/ppermute | solution.py:29
  17.0 0.5 %collective-permute-start.3 = (f32[64,384]{1,0:T(8,128)S(1)}, f32[64,384]{1,0:T(8,128)S(1)}, u32[]{:S(2)}, u32[]{:S(2)}) collective-permute-start(f32[64,384]{1,0:T(8,128)S(1)} %get-tuple-element.20), channel_id=1, source_target_pairs={{0,4},{1,5},{2,6},{3,7},{4,0},{5,1},{6,2},{7,3},{8,12},{9,13},{10,... | collective-permute-start | bytes 294920 | tf_op jit(solution)/shard_map/ppermute | solution.py:29
  17.5 2.3 %collective-permute-start.4 = (f32[64,384]{1,0:T(8,128)S(1)}, f32[64,384]{1,0:T(8,128)S(1)}, u32[]{:S(2)}, u32[]{:S(2)}) collective-permute-start(f32[64,384]{1,0:T(8,128)S(1)} %get-tuple-element.21), channel_id=1, source_target_pairs={{0,6},{1,7},{2,4},{3,5},{4,2},{5,3},{6,0},{7,1},{8,14},{9,15},{10,... | collective-permute-start | bytes 294920 | tf_op jit(solution)/shard_map/ppermute | solution.py:29
  19.8 0.0 collective-permute-done.5.theirs_ref
  19.8 0.0 collective-permute-start.7
  19.8 0.0 copy-done.3
  19.8 2.1 %prepare.1.refs_4_.joined_ref = f32[3,256,256]{2,1,0:T(8,128)S(1)} custom-call(f32[7,256,256]{2,1,0:T(8,128)} %joined_ref.1, s32[3,128]{1,0:T(4,128)S(1)} %copy-done.3), custom_call_target="tpu_custom_call" | custom-call | flops 2200000000 | tf_op jit(solution)/shard_map/prepare/pallas_call | solution.py:350
  21.9 0.0 collective-permute-done.2.refs_1_
  21.9 1.8 %collective-permute-done.3.refs_2_ = f32[64,384]{1,0:T(8,128)S(1)} collective-permute-done((f32[64,384]{1,0:T(8,128)S(1)}, f32[64,384]{1,0:T(8,128)S(1)}, u32[]{:S(2)}, u32[]{:S(2)}) %collective-permute-start.3) | collective-permute-done | bytes 98336 | tf_op jit(solution)/shard_map/ppermute | solution.py:29
  23.7 0.0 collective-permute-done.4.refs_3_
  23.7 0.4 node.1
  24.1 0.0 collective-permute-done.6.pair_mine_ref
  24.1 0.0 collective-permute-done.7.pair_theirs_ref
  24.1 0.4 correct.1.sent_ref
  24.5 1.6 %collective-permute-start.8 = (f32[256,128]{1,0:T(8,128)S(1)}, f32[256,128]{1,0:T(8,128)S(1)}, u32[]{:S(2)}, u32[]{:S(2)}) collective-permute-start(f32[256,128]{1,0:T(8,128)S(1)} %correct.1.sent_ref), channel_id=1, source_target_pairs={{0,8},{8,0},{16,24},{24,16},{1,9},{9,1},{17,25},{25,17},{2,10},{10... | collective-permute-start | bytes 393224 | tf_op jit(solution)/shard_map/ppermute | solution.py:29
  26.1 1.2 %collective-permute-start.17 = (f32[64,128]{1,0:T(8,128)S(1)}, f32[64,128]{1,0:T(8,128)S(1)}, u32[]{:S(2)}, u32[]{:S(2)}) collective-permute-start(f32[64,128]{1,0:T(8,128)S(1)} %get-tuple-element.22.own_ref.refs_0_), channel_id=1, source_target_pairs={{0,2},{1,3},{2,0},{3,1},{4,6},{5,7},{6,4},{7,5},{8,10},{9,11},{10,... | collective-permute-start | bytes 98312 | tf_op jit(solution)/shard_map/ppermute | solution.py:29
  27.3 1.7 %collective-permute-start.19 = (f32[64,128]{1,0:T(8,128)S(1)}, f32[64,128]{1,0:T(8,128)S(1)}, u32[]{:S(2)}, u32[]{:S(2)}) collective-permute-start(f32[64,128]{1,0:T(8,128)S(1)} %get-tuple-element.23.other_ref), channel_id=1, source_target_pairs={{0,6},{1,7},{2,4},{3,5},{4,2},{5,3},{6,0},{7,1},{8,14},{9,15},{10,... | collective-permute-start | bytes 98312 | tf_op jit(solution)/shard_map/ppermute | solution.py:29
  29.0 0.6 %collective-permute-start.18 = (f32[64,128]{1,0:T(8,128)S(1)}, f32[64,128]{1,0:T(8,128)S(1)}, u32[]{:S(2)}, u32[]{:S(2)}) collective-permute-start(f32[64,128]{1,0:T(8,128)S(1)} %get-tuple-element.23.other_ref), channel_id=1, source_target_pairs={{0,4},{1,5},{2,6},{3,7},{4,0},{5,1},{6,2},{7,3},{8,12},{9,13},{10,... | collective-permute-start | bytes 98312 | tf_op jit(solution)/shard_map/ppermute | solution.py:29
  29.6 0.0 collective-permute-done.8.got_ref.after_ref
  29.6 0.8 %level1.1 = (f32[64,128]{1,0:T(8,128)S(1)}, f32[64,128]{1,0:T(8,128)S(1)}) custom-call(f32[256,128]{1,0:T(8,128)S(1)} %correct.1.sent_ref, f32[256,128]{1,0:T(8,128)S(1)} %collective-permute-done.8.got_ref.after_ref, f32[3,256,256]{2,1,0:T(8,128)S(1)} %prepare.1.refs_4_.joined_ref, f32[256,128]{1,0:T(8,128)S(1)} %collective-permute-done.8.got_ref.after_ref), custom_call_target="tpu_custom_call" | custom-call | flops 6600000000 | tf_op jit(solution)/shard_map/level1/pallas_call | solution.py:386
  30.4 2.7 %collective-permute-start.9 = (f32[64,128]{1,0:T(8,128)S(1)}, f32[64,128]{1,0:T(8,128)S(1)}, u32[]{:S(2)}, u32[]{:S(2)}) collective-permute-start(f32[64,128]{1,0:T(8,128)S(1)} %get-tuple-element.26.sent_ref), channel_id=1, source_target_pairs={{0,16},{8,24},{16,0},{24,8},{1,17},{9,25},{17,1},{25,9},{2,18},{10... | collective-permute-start | bytes 98312 | tf_op jit(solution)/shard_map/ppermute | solution.py:29
  33.0 2.2 %solve.1.after_ref.first_ref = f32[4608,512]{1,0:T(8,128)S(1)} custom-call(bf16[18,256,256]{2,1,0:T(8,128)(2,1)S(1)} %permute.1.moved_ref, bf16[4608,512]{1,0:T(8,128)(2,1)S(1)} %bitcast.1, f32[64,384]{1,0:T(8,128)S(1)} %get-tuple-element.18.refs_0_), custom_call_target="tpu_custom_call" | custom-call | flops 8800000000 | tf_op jit(solution)/shard_map/solve/pallas_call | solution.py:375
  35.3 0.0 collective-permute-done.17.refs_1_
  35.3 0.0 collective-permute-done.19.refs_3_
  35.3 0.0 collective-permute-done.18.refs_2_
  35.3 0.0 copy-start
  35.3 0.1 collective-permute-start.20
  35.4 0.0 collective-permute-done.9.got_ref
  35.4 0.4 level2.1.refs_1_
  35.8 2.0 %collective-permute-start.15 = (f32[64,256]{1,0:T(8,128)S(1)}, f32[64,256]{1,0:T(8,128)S(1)}, u32[]{:S(2)}, u32[]{:S(2)}) collective-permute-start(f32[64,256]{1,0:T(8,128)S(1)} %pack.1.refs_0_), channel_id=1, source_target_pairs={{0,6},{1,7},{2,4},{3,5},{4,2},{5,3},{6,0},{7,1},{8,14},{9,15},{10,... | collective-permute-start | bytes 196616 | tf_op jit(solution)/shard_map/ppermute | solution.py:29
  37.8 0.8 %collective-permute-start.13 = (f32[64,256]{1,0:T(8,128)S(1)}, f32[64,256]{1,0:T(8,128)S(1)}, u32[]{:S(2)}, u32[]{:S(2)}) collective-permute-start(f32[64,256]{1,0:T(8,128)S(1)} %pack.1.refs_0_), channel_id=1, source_target_pairs={{0,4},{1,5},{2,6},{3,7},{4,0},{5,1},{6,2},{7,3},{8,12},{9,13},{10,... | collective-permute-start | bytes 196616 | tf_op jit(solution)/shard_map/ppermute | solution.py:29
  38.5 0.8 %collective-permute-start.11 = (f32[64,256]{1,0:T(8,128)S(1)}, f32[64,256]{1,0:T(8,128)S(1)}, u32[]{:S(2)}, u32[]{:S(2)}) collective-permute-start(f32[64,256]{1,0:T(8,128)S(1)} %pack.1.refs_0_), channel_id=1, source_target_pairs={{0,2},{1,3},{2,0},{3,1},{4,6},{5,7},{6,4},{7,5},{8,10},{9,11},{10,... | collective-permute-start | bytes 196616 | tf_op jit(solution)/shard_map/ppermute | solution.py:29
  39.4 0.0 collective-permute-start.10
  39.4 2.0 %collective-permute-done.15.refs_6_ = f32[64,256]{1,0:T(8,128)S(1)} collective-permute-done((f32[64,256]{1,0:T(8,128)S(1)}, f32[64,256]{1,0:T(8,128)S(1)}, u32[]{:S(2)}, u32[]{:S(2)}) %collective-permute-start.15) | collective-permute-done | bytes 65568 | tf_op jit(solution)/shard_map/ppermute | solution.py:29
  41.3 0.0 collective-permute-start.16
  41.3 1.3 %collective-permute-done.13.refs_4_ = f32[64,256]{1,0:T(8,128)S(1)} collective-permute-done((f32[64,256]{1,0:T(8,128)S(1)}, f32[64,256]{1,0:T(8,128)S(1)}, u32[]{:S(2)}, u32[]{:S(2)}) %collective-permute-start.13) | collective-permute-done | bytes 65568 | tf_op jit(solution)/shard_map/ppermute | solution.py:29
  42.7 0.0 collective-permute-start.14
  42.7 0.1 collective-permute-done.11.refs_2_
  42.8 0.4 collective-permute-start.12
  43.2 0.0 collective-permute-done.20.pair_ref
  43.2 1.6 %apply.1.refs_8_ = f32[4608,512]{1,0:T(8,128)S(1)} custom-call(f32[4,64,128]{2,1,0:T(8,128)S(1)} %stack.1.own_ref, f32[4,64,128]{2,1,0:T(8,128)S(1)} %collective-permute-done.20.pair_ref, f32[4608,512]{1,0:T(8,128)S(1)} %solve.1.after_ref.first_ref, bf16[3,4608,128]{2,1,0:T(8,128)(2,1)S(1)} %copy-done), custom_call_target="tpu_custom_call" | custom-call | flops 1980000000 | tf_op jit(solution)/shard_map/apply/pallas_call | solution.py:397
  44.8 0.0 collective-permute-done.10.refs_1_
  44.8 0.0 collective-permute-done.16.refs_7_
  44.8 0.0 collective-permute-done.14.refs_5_
  44.8 0.0 collective-permute-done.12.refs_3_
  44.8 4.5 %expand.1 = f32[4608,512]{1,0:T(8,128)} custom-call(f32[64,256]{1,0:T(8,128)S(1)} %pack.1.refs_0_, f32[64,256]{1,0:T(8,128)S(1)} %collective-permute-done.10.refs_1_, f32[64,256]{1,0:T(8,128)S(1)} %collective-permute-done.11.refs_2_, f32[64,256]{1,0:T(8,128)S(1)} %collective-permute-done.12.refs_3_, f32[64,256]{1,0:T(8,128)S(1)} %collective-permute-done.13.refs_4_, ...), custom_call_target="tpu_custom_call" | custom-call | flops 5500000256 | tf_op jit(solution)/shard_map/expand/pallas_call | solution.py:415
  (8 shorter events, 0.0 us)
Async XLA Ops:
  0.0 6.4 %copy-start.1 = (bf16[18,256,256]{2,1,0:T(8,128)(2,1)S(1)}, bf16[18,256,256]{2,1,0:T(8,128)(2,1)}, u32[]{:S(2)}) copy-start(bf16[18,256,256]{2,1,0:T(8,128)(2,1)} %inv_ref.1) | copy-start | bytes 7077892
  0.0 6.4 %copy-start.2 = (s32[18,256]{1,0:T(8,128)S(1)}, s32[18,256]{1,0:T(8,128)}, u32[]{:S(2)}) copy-start(s32[18,256]{1,0:T(8,128)} %order_ref.1) | copy-start | bytes 55300
  3.3 8.5 %collective-permute-start = (f32[128,384]{1,0:T(8,128)S(1)}, f32[128,384]{1,0:T(8,128)S(1)}, u32[]{:S(2)}, u32[]{:S(2)}) collective-permute-start(f32[128,384]{1,0:T(8,128)S(1)} %get-tuple-element.17.after_ref.mine_ref), channel_id=1, source_target_pairs={{0,2},{1,3},{2,0},{3,1},{4,6},{5,7},{6,4},{7,5},{8,10},{9,11},{10,... | collective-permute-start | bytes 589832 | tf_op jit(solution)/shard_map/ppermute | solution.py:29
  6.4 3.4 %slice-start = ((s8[4718592]{0:T(1024)(128)(4,1)}), s8[4194304]{0:T(1024)(128)(4,1)S(1)}, s32[]{:S(2)}) async-start(s8[4718592]{0:T(1024)(128)(4,1)} %bitcast), calls=%async_computation | async-start | bytes 8388608
  7.6 2.2 %slice-start.1 = ((s8[4718592]{0:T(1024)(128)(4,1)}), s8[524288]{0:T(1024)(128)(4,1)S(1)}, s32[]{:S(2)}) async-start(s8[4718592]{0:T(1024)(128)(4,1)} %bitcast), calls=%async_computation.1 | async-start | bytes 1048576
  11.8 4.2 %collective-permute-start.1 = (f32[384,256]{1,0:T(8,128)S(1)}, f32[384,256]{1,0:T(8,128)S(1)}, u32[]{:S(2)}, u32[]{:S(2)}) collective-permute-start(f32[384,256]{1,0:T(8,128)S(1)} %project_other.1), channel_id=1, source_target_pairs={{0,1},{1,0},{2,3},{3,2},{4,5},{5,4},{6,7},{7,6},{8,9},{9,8},{10,11... | collective-permute-start | bytes 1179656 | tf_op jit(solution)/shard_map/ppermute | solution.py:29
  11.9 7.9 %copy-start.3 = (s32[3,128]{1,0:T(4,128)S(1)}, s32[3,128]{1,0:T(4,128)}, u32[]{:S(2)}) copy-start(s32[3,128]{1,0:T(4,128)} %perm_ref.1) | copy-start | bytes 4612
  11.9 12.2 %collective-permute-start.6 = (f32[128,384]{1,0:T(8,128)S(1)}, f32[128,384]{1,0:T(8,128)S(1)}, u32[]{:S(2)}, u32[]{:S(2)}) collective-permute-start(f32[128,384]{1,0:T(8,128)S(1)} %add.1.after_ref.mine_ref), channel_id=1, source_target_pairs={{0,1},{1,0},{2,3},{3,2},{4,5},{5,4},{6,7},{7,6},{8,9},{9,8},{10,11... | collective-permute-start | bytes 589832 | tf_op jit(solution)/shard_map/ppermute | solution.py:29
  12.5 7.3 %collective-permute-start.5 = (f32[128,384]{1,0:T(8,128)S(1)}, f32[128,384]{1,0:T(8,128)S(1)}, u32[]{:S(2)}, u32[]{:S(2)}) collective-permute-start(f32[128,384]{1,0:T(8,128)S(1)} %add.1.after_ref.mine_ref), channel_id=1, source_target_pairs={{0,4},{1,5},{2,6},{3,7},{4,0},{5,1},{6,2},{7,3},{8,12},{9,13},{10,... | collective-permute-start | bytes 589832 | tf_op jit(solution)/shard_map/ppermute | solution.py:29
  16.2 5.7 %collective-permute-start.2 = (f32[64,384]{1,0:T(8,128)S(1)}, f32[64,384]{1,0:T(8,128)S(1)}, u32[]{:S(2)}, u32[]{:S(2)}) collective-permute-start(f32[64,384]{1,0:T(8,128)S(1)} %get-tuple-element.19), channel_id=1, source_target_pairs={{0,2},{1,3},{2,0},{3,1},{4,6},{5,7},{6,4},{7,5},{8,10},{9,11},{10,... | collective-permute-start | bytes 294920 | tf_op jit(solution)/shard_map/ppermute | solution.py:29
  17.0 6.7 %collective-permute-start.3 = (f32[64,384]{1,0:T(8,128)S(1)}, f32[64,384]{1,0:T(8,128)S(1)}, u32[]{:S(2)}, u32[]{:S(2)}) collective-permute-start(f32[64,384]{1,0:T(8,128)S(1)} %get-tuple-element.20), channel_id=1, source_target_pairs={{0,4},{1,5},{2,6},{3,7},{4,0},{5,1},{6,2},{7,3},{8,12},{9,13},{10,... | collective-permute-start | bytes 294920 | tf_op jit(solution)/shard_map/ppermute | solution.py:29
  17.5 6.2 %collective-permute-start.4 = (f32[64,384]{1,0:T(8,128)S(1)}, f32[64,384]{1,0:T(8,128)S(1)}, u32[]{:S(2)}, u32[]{:S(2)}) collective-permute-start(f32[64,384]{1,0:T(8,128)S(1)} %get-tuple-element.21), channel_id=1, source_target_pairs={{0,6},{1,7},{2,4},{3,5},{4,2},{5,3},{6,0},{7,1},{8,14},{9,15},{10,... | collective-permute-start | bytes 294920 | tf_op jit(solution)/shard_map/ppermute | solution.py:29
  19.8 4.3 %collective-permute-start.7 = (f32[128,384]{1,0:T(8,128)S(1)}, f32[128,384]{1,0:T(8,128)S(1)}, u32[]{:S(2)}, u32[]{:S(2)}) collective-permute-start(f32[128,384]{1,0:T(8,128)S(1)} %collective-permute-done.5.theirs_ref), channel_id=1, source_target_pairs={{0,1},{1,0},{2,3},{3,2},{4,5},{5,4},{6,7},{7,6},{8,9},{9,8},{10,11... | collective-permute-start | bytes 589832 | tf_op jit(solution)/shard_map/ppermute | solution.py:29
  24.5 5.1 %collective-permute-start.8 = (f32[256,128]{1,0:T(8,128)S(1)}, f32[256,128]{1,0:T(8,128)S(1)}, u32[]{:S(2)}, u32[]{:S(2)}) collective-permute-start(f32[256,128]{1,0:T(8,128)S(1)} %correct.1.sent_ref), channel_id=1, source_target_pairs={{0,8},{8,0},{16,24},{24,16},{1,9},{9,1},{17,25},{25,17},{2,10},{10... | collective-permute-start | bytes 393224 | tf_op jit(solution)/shard_map/ppermute | solution.py:29
  26.1 9.2 %collective-permute-start.17 = (f32[64,128]{1,0:T(8,128)S(1)}, f32[64,128]{1,0:T(8,128)S(1)}, u32[]{:S(2)}, u32[]{:S(2)}) collective-permute-start(f32[64,128]{1,0:T(8,128)S(1)} %get-tuple-element.22.own_ref.refs_0_), channel_id=1, source_target_pairs={{0,2},{1,3},{2,0},{3,1},{4,6},{5,7},{6,4},{7,5},{8,10},{9,11},{10,... | collective-permute-start | bytes 98312 | tf_op jit(solution)/shard_map/ppermute | solution.py:29
  27.3 8.0 %collective-permute-start.19 = (f32[64,128]{1,0:T(8,128)S(1)}, f32[64,128]{1,0:T(8,128)S(1)}, u32[]{:S(2)}, u32[]{:S(2)}) collective-permute-start(f32[64,128]{1,0:T(8,128)S(1)} %get-tuple-element.23.other_ref), channel_id=1, source_target_pairs={{0,6},{1,7},{2,4},{3,5},{4,2},{5,3},{6,0},{7,1},{8,14},{9,15},{10,... | collective-permute-start | bytes 98312 | tf_op jit(solution)/shard_map/ppermute | solution.py:29
  29.0 6.3 %collective-permute-start.18 = (f32[64,128]{1,0:T(8,128)S(1)}, f32[64,128]{1,0:T(8,128)S(1)}, u32[]{:S(2)}, u32[]{:S(2)}) collective-permute-start(f32[64,128]{1,0:T(8,128)S(1)} %get-tuple-element.23.other_ref), channel_id=1, source_target_pairs={{0,4},{1,5},{2,6},{3,7},{4,0},{5,1},{6,2},{7,3},{8,12},{9,13},{10,... | collective-permute-start | bytes 98312 | tf_op jit(solution)/shard_map/ppermute | solution.py:29
  30.4 5.0 %collective-permute-start.9 = (f32[64,128]{1,0:T(8,128)S(1)}, f32[64,128]{1,0:T(8,128)S(1)}, u32[]{:S(2)}, u32[]{:S(2)}) collective-permute-start(f32[64,128]{1,0:T(8,128)S(1)} %get-tuple-element.26.sent_ref), channel_id=1, source_target_pairs={{0,16},{8,24},{16,0},{24,8},{1,17},{9,25},{17,1},{25,9},{2,18},{10... | collective-permute-start | bytes 98312 | tf_op jit(solution)/shard_map/ppermute | solution.py:29
  35.3 7.9 %copy-start = (bf16[3,4608,128]{2,1,0:T(8,128)(2,1)S(1)}, bf16[3,4608,128]{2,1,0:T(8,128)(2,1)}, u32[]{:S(2)}) copy-start(bf16[3,4608,128]{2,1,0:T(8,128)(2,1)} %refs_9_.1) | copy-start | bytes 10616836
  35.3 7.8 %collective-permute-start.20 = (f32[4,64,128]{2,1,0:T(8,128)S(1)}, f32[4,64,128]{2,1,0:T(8,128)S(1)}, u32[]{:S(2)}, u32[]{:S(2)}) collective-permute-start(f32[4,64,128]{2,1,0:T(8,128)S(1)} %stack.1.own_ref), channel_id=1, source_target_pairs={{0,1},{1,0},{2,3},{3,2},{4,5},{5,4},{6,7},{7,6},{8,9},{9,8},{10,11... | collective-permute-start | bytes 393224 | tf_op jit(solution)/shard_map/ppermute | solution.py:29
  35.8 5.5 %collective-permute-start.15 = (f32[64,256]{1,0:T(8,128)S(1)}, f32[64,256]{1,0:T(8,128)S(1)}, u32[]{:S(2)}, u32[]{:S(2)}) collective-permute-start(f32[64,256]{1,0:T(8,128)S(1)} %pack.1.refs_0_), channel_id=1, source_target_pairs={{0,6},{1,7},{2,4},{3,5},{4,2},{5,3},{6,0},{7,1},{8,14},{9,15},{10,... | collective-permute-start | bytes 196616 | tf_op jit(solution)/shard_map/ppermute | solution.py:29
  37.8 4.9 %collective-permute-start.13 = (f32[64,256]{1,0:T(8,128)S(1)}, f32[64,256]{1,0:T(8,128)S(1)}, u32[]{:S(2)}, u32[]{:S(2)}) collective-permute-start(f32[64,256]{1,0:T(8,128)S(1)} %pack.1.refs_0_), channel_id=1, source_target_pairs={{0,4},{1,5},{2,6},{3,7},{4,0},{5,1},{6,2},{7,3},{8,12},{9,13},{10,... | collective-permute-start | bytes 196616 | tf_op jit(solution)/shard_map/ppermute | solution.py:29
  38.5 4.3 %collective-permute-start.11 = (f32[64,256]{1,0:T(8,128)S(1)}, f32[64,256]{1,0:T(8,128)S(1)}, u32[]{:S(2)}, u32[]{:S(2)}) collective-permute-start(f32[64,256]{1,0:T(8,128)S(1)} %pack.1.refs_0_), channel_id=1, source_target_pairs={{0,2},{1,3},{2,0},{3,1},{4,6},{5,7},{6,4},{7,5},{8,10},{9,11},{10,... | collective-permute-start | bytes 196616 | tf_op jit(solution)/shard_map/ppermute | solution.py:29
  39.4 5.4 %collective-permute-start.10 = (f32[64,256]{1,0:T(8,128)S(1)}, f32[64,256]{1,0:T(8,128)S(1)}, u32[]{:S(2)}, u32[]{:S(2)}) collective-permute-start(f32[64,256]{1,0:T(8,128)S(1)} %pack.1.refs_0_), channel_id=1, source_target_pairs={{0,1},{1,0},{2,3},{3,2},{4,5},{5,4},{6,7},{7,6},{8,9},{9,8},{10,11... | collective-permute-start | bytes 196616 | tf_op jit(solution)/shard_map/ppermute | solution.py:29
  41.3 3.4 %collective-permute-start.16 = (f32[64,256]{1,0:T(8,128)S(1)}, f32[64,256]{1,0:T(8,128)S(1)}, u32[]{:S(2)}, u32[]{:S(2)}) collective-permute-start(f32[64,256]{1,0:T(8,128)S(1)} %collective-permute-done.15.refs_6_), channel_id=1, source_target_pairs={{0,1},{1,0},{2,3},{3,2},{4,5},{5,4},{6,7},{7,6},{8,9},{9,8},{10,11... | collective-permute-start | bytes 196616 | tf_op jit(solution)/shard_map/ppermute | solution.py:29
  42.7 2.1 %collective-permute-start.14 = (f32[64,256]{1,0:T(8,128)S(1)}, f32[64,256]{1,0:T(8,128)S(1)}, u32[]{:S(2)}, u32[]{:S(2)}) collective-permute-start(f32[64,256]{1,0:T(8,128)S(1)} %collective-permute-done.13.refs_4_), channel_id=1, source_target_pairs={{0,1},{1,0},{2,3},{3,2},{4,5},{5,4},{6,7},{7,6},{8,9},{9,8},{10,11... | collective-permute-start | bytes 196616 | tf_op jit(solution)/shard_map/ppermute | solution.py:29
  42.8 2.0 %collective-permute-start.12 = (f32[64,256]{1,0:T(8,128)S(1)}, f32[64,256]{1,0:T(8,128)S(1)}, u32[]{:S(2)}, u32[]{:S(2)}) collective-permute-start(f32[64,256]{1,0:T(8,128)S(1)} %collective-permute-done.11.refs_2_), channel_id=1, source_target_pairs={{0,1},{1,0},{2,3},{3,2},{4,5},{5,4},{6,7},{7,6},{8,9},{9,8},{10,11... | collective-permute-start | bytes 196616 | tf_op jit(solution)/shard_map/ppermute | solution.py:29

commit v9 on v8

--- a/solution.py
+++ b/solution.py
@@ -175,8 +175,9 @@
 
 
 def correct_kernel(levels, rank, own_ref, other_ref, rest_ref, mine_ref, theirs_ref, pair_mine_ref,
-                   pair_theirs_ref, message_ref):
+                   pair_theirs_ref, message_ref, share_ref):
     grams = [mine_ref[...] + pair_mine_ref[...], theirs_ref[...] + pair_theirs_ref[...]]
+    share_ref[...] = other_ref[...]
     pairs = below_pairs(levels)
     lanes = {pair: slice(spot * rank, (spot + 1) * rank) for spot, pair in enumerate(pairs)}
     joint = jnp.concatenate(
@@ -218,41 +219,39 @@
     pack_message(message_ref[0], pieces)
 
 
-def pack_kernel(*refs):
-    refs[-1][...] = jnp.concatenate([ref[...] for ref in refs[:-1]], axis=1)
-
-
-def stack_kernel(after_ref, *refs):
-    for slot, ref in enumerate(refs[:-1]):
-        refs[-1][slot] = ref[...]
-
-
-def split_factor(pieces, flip_ref, factor_ref):
-    share, kinds = pieces[0].shape
-    slots = len(pieces) // 2
+def stack_kernel(low_ref, high_ref, *refs):
+    held = low_ref.shape[0]
+    refs[-1][:held] = low_ref[...]
+    refs[-1][held:] = high_ref[...]
+
+
+def split_factor(masks, pairs, flip_ref, factor_ref):
+    slots, share, rank = pairs[0].shape
     me = lax.axis_index("rows")
-    for mask, ref in enumerate(pieces):
-        owner = me ^ mask
-        row = (owner % 2 * slots + owner // 2) * share
-        flip_ref[pl.ds(pl.multiple_of(row, share), share), :] = ref[...]
+    core, chip = me % 2, me // 2
+    for i, ref in enumerate(pairs):
+        side = core if i % 2 == 0 else 1 - core
+        for spot, mask in enumerate(masks):
+            row = (side * slots + (chip ^ mask)) * share
+            rows = pl.ds(pl.multiple_of(row, share), share)
+            flip_ref[rows, pl.ds(i // 2 * rank, rank)] = ref[spot]
     high_part, low_part = halves(flip_ref[...].T)
+    kinds = flip_ref.shape[1]
     factor_ref[:kinds, :] = high_part
     factor_ref[kinds:, :] = low_part
 
 
-def apply_kernel(tile, own_ref, pair_ref, first_ref, left_ref, out_ref, flip_ref, factor_ref):
-    pieces = [ref.at[slot] for slot in range(own_ref.shape[0]) for ref in (own_ref, pair_ref)]
-    split_factor(pieces, flip_ref, factor_ref)
+def apply_kernel(masks, tile, own_ref, pair_ref, first_ref, left_ref, out_ref, flip_ref, factor_ref):
+    split_factor(masks, (own_ref, pair_ref), flip_ref, factor_ref)
     for row in range(0, out_ref.shape[0], tile):
         rows = pl.ds(row, tile)
         left = jnp.concatenate([left_ref[0, rows, :]] * 2, axis=1)
         out_ref[rows, :] = first_ref[rows, :] - dot(left, factor_ref[...], (1, 0))
 
 
-def expand_kernel(levels, tile, count, *refs):
-    piece_refs = refs[:count]
-    first_ref, left_ref, out_ref, flip_ref, factor_ref, out_buf, sems = refs[count:]
-    split_factor(piece_refs, flip_ref, factor_ref)
+def expand_kernel(masks, levels, tile, *refs):
+    first_ref, left_ref, out_ref, flip_ref, factor_ref, out_buf, sems = refs[2 * levels - 2:]
+    split_factor(masks, refs[:2 * levels - 2], flip_ref, factor_ref)
     copies = []
     for step in range(out_buf.shape[0] // tile):
         rows = pl.ds(step * tile, tile)
@@ -365,21 +364,52 @@
         name="node",
         **settings(8, 1),
     )(*parts, prepared)
-    message = pl.pallas_call(
+    message, other = pl.pallas_call(
         functools.partial(correct_kernel, levels, rank),
-        out_shape=message_shape(1),
+        out_shape=[message_shape(1), floats(share, rank)],
         name="correct",
         **settings(8, 1),
     )(own, other, rest, *grams)
-    early = [own] + [swap(own if slot < slots // 2 else other, "rows", 2 * slot) for slot in range(1, slots)]
     first = pl.pallas_call(
         functools.partial(solve_kernel, per_step, width),
         out_shape=floats(rows, columns),
         name="solve",
-        **settings(8, 8),
+        **settings(8, 2),
     )(moved, rhs, merged[0])
 
-    coefs = []
+    bits = [slots] + [2 ** bit for bit in range(1, slots.bit_length() - 1)]
+    masks = [0]
+    for bit in bits:
+        masks += [mask ^ bit // 2 for mask in masks]
+
+    def stack(low, high, *after):
+        return pl.pallas_call(
+            stack_kernel,
+            out_shape=floats(low.shape[0] + high.shape[0], share, rank),
+            name="stack",
+            **settings(8, 0.1),
+        )(low, high, *after)
+
+    def gather(mine, sent, *after):
+        mine, sent = mine[None], sent[None]
+        for bit in bits:
+            mine = stack(mine, swap(sent, "rows", bit), *(after if bit == bits[-1] else ()))
+            sent = mine
+        return mine, swap(mine, "rows", 1)
+
+    early = gather(own, other)
+    second = pl.pallas_call(
+        functools.partial(apply_kernel, masks, per_step * width),
+        out_shape=floats(rows, columns),
+        scratch_shapes=[
+            pltpu.VMEM((columns, rank), jnp.float32),
+            pltpu.VMEM((2 * rank, columns), jnp.bfloat16),
+        ],
+        name="apply",
+        **settings(8, 1.8),
+    )(*early, first, left_basis)
+
+    pieces = []
     for level in range(1, levels):
         last = level + 1 == levels
         arrived = swap(message, "leaf", 2 ** (level - 1))
@@ -387,33 +417,13 @@
             functools.partial(level_kernel, levels, level, share),
             out_shape=[floats(share, rank)] + ([] if last else [message_shape(level + 1)]),
             name=f"level{level}",
-            **settings(8, 1 if last else 6),
-        )(message, arrived, prepared, first if last else arrived)
-        coefs.append(outs[0])
+            **settings(8, 8 if last else 8),
+        )(message, arrived, prepared, first)
+        pieces += gather(outs[0], outs[0], *((second,) if last else ()))
         message = outs[-1]
-    stack = pl.pallas_call(
-        stack_kernel, out_shape=floats(slots, share, rank), name="stack", **settings(8, 0.1),
-    )(first, *early)
-    second = pl.pallas_call(
-        functools.partial(apply_kernel, per_step * width),
-        out_shape=floats(rows, columns),
-        scratch_shapes=[
-            pltpu.VMEM((columns, rank), jnp.float32),
-            pltpu.VMEM((2 * rank, columns), jnp.bfloat16),
-        ],
-        name="apply",
-        **settings(8, 1.8),
-    )(stack, swap(stack, "rows", 1), first, left_basis)
-
-    pack = pl.pallas_call(
-        pack_kernel, out_shape=floats(share, size), name="pack", **settings(8, 0.1),
-    )(*coefs)
-    pieces = []
-    for slot in range(slots):
-        piece = swap(pack, "rows", 2 * slot) if slot > 0 else pack
-        pieces += [piece, swap(piece, "rows", 1)]
+
     return pl.pallas_call(
-        functools.partial(expand_kernel, levels, per_step * width, count),
+        functools.partial(expand_kernel, masks, levels, per_step * width),
         out_specs=pl.BlockSpec(memory_space=pl.ANY),
         out_shape=floats(rows, columns),
         scratch_shapes=[

time: 49.5 us -> 51.2 us (1.034)
  waiting for transfers between devices: 5.2 us -> 8.11 us
  starting transfers between devices: 20.5 us -> 19.4 us
    ppermute x21 -> x19, waiting for transfers between devices: 5.2 us -> 8.11 us  [swap(): return lax.ppermute(value, axis, [(i, i ^ mask) for i in range(count)])]
    ppermute x21 -> x19, starting transfers between devices: 20.5 us -> 19.4 us  [swap(): return lax.ppermute(value, axis, [(i, i ^ mask) for i in range(count)])]
    pallas_call x4 -> x8, Pallas kernels: 6.1 us -> 6.08 us  [the longest x1 4.48 us: per_device(): pl.pallas_call(functools.partial(expand_kernel, masks, levels, per_step *...]
  transfers between devices with their start and end apart: 21 -> 19, of which waited for: 4 -> 6; matrix products, arithmetic and copies ran while one was open for 0% -> 0% of each run, Pallas kernels for 30% -> 29%
where the time goes in v9:
time: 51.2 us; the launch traced here: 51.1 us
  Pallas kernels  23.2 us (45%)
  starting transfers between devices  19.4 us (38%)
  waiting for transfers between devices  8.11 us (16%)
    ppermute x19, starting transfers between devices, swap(): return lax.ppermute(value, axis, [(i, i ^ mask) for i in range(count)])  19.4 us
    ppermute x19, waiting for transfers between devices, swap(): return lax.ppermute(value, axis, [(i, i ^ mask) for i in range(count)])  8.11 us
    pallas_call x1, Pallas kernels, per_device(): pl.pallas_call(functools.partial(expand_kernel, masks, levels, per_step *...  4.48 us
    pallas_call x2, Pallas kernels, project(): pl.pallas_call(functools.partial(project_kernel, other), out_shape=floats...  3.99 us
    pallas_call x1, Pallas kernels, per_device(): pl.pallas_call(functools.partial(gram_kernel, levels, per_step, width), i...  3.34 us
    pallas_call x1, Pallas kernels, per_device(): pl.pallas_call(functools.partial(solve_kernel, per_step, width), out_shap...  2.22 us
    pallas_call x1, Pallas kernels, per_device(): pl.pallas_call(functools.partial(weigh_kernel, per_step, width), out_shap...  2.13 us
    pallas_call x1, Pallas kernels, per_device(): pl.pallas_call(functools.partial(prepare_kernel, levels), in_specs=[pl.Bl...  2.11 us
  transfers between devices with their start and end apart: 19, of which 6 were waited for; matrix products, arithmetic and copies ran while one was open for 0% of the time, Pallas kernels for 29%

profile of v9, /device:TPU:0, one launch (start us, length us, event | category | flops | bytes accessed | tf_op | source)
XLA Modules:
  0.0 51.1 jit_solution(5191737973175256680)
XLA Ops:
  0.0 0.0 copy-start.1
  0.0 0.0 copy-start.2
  0.0 3.3 %gram.1 = (bf16[384,4608]{1,0:T(8,128)(2,1)S(1)}, f32[128,384]{1,0:T(8,128)S(1)}) custom-call(bf16[3,4608,128]{2,1,0:T(8,128)(2,1)} %right_ref.1, bf16[3,4608,128]{2,1,0:T(8,128)(2,1)} %refs_5_.1), custom_call_target="tpu_custom_call" | custom-call | flops 3300000000 | tf_op jit(solution)/shard_map/gram/pallas_call | solution.py:290
  3.3 3.0 %collective-permute-start = (f32[128,384]{1,0:T(8,128)S(1)}, f32[128,384]{1,0:T(8,128)S(1)}, u32[]{:S(2)}, u32[]{:S(2)}) collective-permute-start(f32[128,384]{1,0:T(8,128)S(1)} %get-tuple-element.19.after_ref.mine_ref), channel_id=1, source_target_pairs={{0,2},{1,3},{2,0},{3,1},{4,6},{5,7},{6,4},{7,5},{8,10},{9,11},{10,... | collective-permute-start | bytes 589832 | tf_op jit(solution)/shard_map/ppermute | solution.py:29
  6.4 0.0 copy-done.1
  6.4 0.0 copy-done.2
  6.4 0.0 slice-start
  6.4 1.2 %permute.1.moved_ref = bf16[18,256,256]{2,1,0:T(8,128)(2,1)S(1)} custom-call(s32[18,256]{1,0:T(8,128)S(1)} %copy-done.2, bf16[18,256,256]{2,1,0:T(8,128)(2,1)S(1)} %copy-done.1), custom_call_target="tpu_custom_call" | custom-call | flops 1650000000 | tf_op jit(solution)/shard_map/permute/pallas_call | solution.py:305
  7.6 0.0 slice-start.1
  7.6 2.1 %weigh.1.factor_ref = bf16[768,4608]{1,0:T(8,128)(2,1)S(1)} custom-call(bf16[18,256,256]{2,1,0:T(8,128)(2,1)S(1)} %permute.1.moved_ref, bf16[384,4608]{1,0:T(8,128)(2,1)S(1)} %get-tuple-element.18.flip_ref, f32[128,384]{1,0:T(8,128)S(1)} %get-tuple-element.19.after_ref.mine_ref), custom_call_target="tpu_custom_call" | custom-call | flops 2640000000 | tf_op jit(solution)/shard_map/weigh/pallas_call | solution.py:317
  9.8 0.0 slice-done
  9.8 0.0 slice-done.1
  9.8 2.0 %project_other.1 = f32[384,256]{1,0:T(8,128)S(1)} custom-call(bf16[768,4608]{1,0:T(8,128)(2,1)S(1)} %weigh.1.factor_ref, bf16[4608,512]{1,0:T(8,128)(2,1)S(1)} %bitcast.5, f32[128,384]{1,0:T(8,128)S(1)} %get-tuple-element.19.after_ref.mine_ref), custom_call_target="tpu_custom_call" | custom-call | flops 1100000000 | tf_op jit(solution)/shard_map/project_other/pallas_call | solution.py:325
  11.8 0.1 collective-permute-start.1
  11.9 0.0 collective-permute-done.got_ref
  11.9 0.0 copy-start.3
  11.9 0.5 %collective-permute-start.6 = (f32[128,384]{1,0:T(8,128)S(1)}, f32[128,384]{1,0:T(8,128)S(1)}, u32[]{:S(2)}, u32[]{:S(2)}) collective-permute-start(f32[128,384]{1,0:T(8,128)S(1)} %add.1.after_ref.mine_ref), channel_id=1, source_target_pairs={{0,1},{1,0},{2,3},{3,2},{4,5},{5,4},{6,7},{7,6},{8,9},{9,8},{10,11... | collective-permute-start | bytes 589832 | tf_op jit(solution)/shard_map/ppermute | solution.py:29
  12.5 1.5 %collective-permute-start.5 = (f32[128,384]{1,0:T(8,128)S(1)}, f32[128,384]{1,0:T(8,128)S(1)}, u32[]{:S(2)}, u32[]{:S(2)}) collective-permute-start(f32[128,384]{1,0:T(8,128)S(1)} %add.1.after_ref.mine_ref), channel_id=1, source_target_pairs={{0,4},{1,5},{2,6},{3,7},{4,0},{5,1},{6,2},{7,3},{8,12},{9,13},{10,... | collective-permute-start | bytes 589832 | tf_op jit(solution)/shard_map/ppermute | solution.py:29
  14.0 2.0 %project_own.1.keep_ref = f32[384,256]{1,0:T(8,128)S(1)} custom-call(bf16[768,4608]{1,0:T(8,128)(2,1)S(1)} %weigh.1.factor_ref, bf16[4608,512]{1,0:T(8,128)(2,1)S(1)} %bitcast.5, f32[128,384]{1,0:T(8,128)S(1)} %add.1.after_ref.mine_ref), custom_call_target="tpu_custom_call" | custom-call | flops 8800000000 | tf_op jit(solution)/shard_map/project_own/pallas_call | solution.py:325
  16.0 0.0 collective-permute-done.1.got_ref
  16.0 0.2 merge.1
  16.2 0.8 %collective-permute-start.2 = (f32[64,384]{1,0:T(8,128)S(1)}, f32[64,384]{1,0:T(8,128)S(1)}, u32[]{:S(2)}, u32[]{:S(2)}) collective-permute-start(f32[64,384]{1,0:T(8,128)S(1)} %get-tuple-element.21), channel_id=1, source_target_pairs={{0,2},{1,3},{2,0},{3,1},{4,6},{5,7},{6,4},{7,5},{8,10},{9,11},{10,... | collective-permute-start | bytes 294920 | tf_op jit(solution)/shard_map/ppermute | solution.py:29
  17.0 0.5 collective-permute-start.3
  17.5 2.3 %collective-permute-start.4 = (f32[64,384]{1,0:T(8,128)S(1)}, f32[64,384]{1,0:T(8,128)S(1)}, u32[]{:S(2)}, u32[]{:S(2)}) collective-permute-start(f32[64,384]{1,0:T(8,128)S(1)} %get-tuple-element.23), channel_id=1, source_target_pairs={{0,6},{1,7},{2,4},{3,5},{4,2},{5,3},{6,0},{7,1},{8,14},{9,15},{10,... | collective-permute-start | bytes 294920 | tf_op jit(solution)/shard_map/ppermute | solution.py:29
  19.8 0.0 collective-permute-done.5.theirs_ref
  19.8 0.0 collective-permute-start.7
  19.8 0.0 copy-done.3
  19.8 2.1 %prepare.1.refs_4_.joined_ref = f32[3,256,256]{2,1,0:T(8,128)S(1)} custom-call(f32[7,256,256]{2,1,0:T(8,128)} %joined_ref.1, s32[3,128]{1,0:T(4,128)S(1)} %copy-done.3), custom_call_target="tpu_custom_call" | custom-call | flops 2200000000 | tf_op jit(solution)/shard_map/prepare/pallas_call | solution.py:349
  21.9 0.0 collective-permute-done.2.refs_1_
  21.9 1.8 %collective-permute-done.3.refs_2_ = f32[64,384]{1,0:T(8,128)S(1)} collective-permute-done((f32[64,384]{1,0:T(8,128)S(1)}, f32[64,384]{1,0:T(8,128)S(1)}, u32[]{:S(2)}, u32[]{:S(2)}) %collective-permute-start.3) | collective-permute-done | bytes 98336 | tf_op jit(solution)/shard_map/ppermute | solution.py:29
  23.7 0.0 collective-permute-done.4.refs_3_
  23.7 0.4 node.1
  24.1 0.0 collective-permute-done.6.pair_mine_ref
  24.1 0.0 collective-permute-done.7.pair_theirs_ref
  24.1 0.4 correct.1
  24.5 1.5 %collective-permute-start.15 = (f32[1,64,128]{2,1,0:T(8,128)S(1)}, f32[1,64,128]{2,1,0:T(8,128)S(1)}, u32[]{:S(2)}, u32[]{:S(2)}) collective-permute-start(f32[1,64,128]{2,1,0:T(8,128)S(1)} %bitcast.10), channel_id=1, source_target_pairs={{0,4},{1,5},{2,6},{3,7},{4,0},{5,1},{6,2},{7,3},{8,12},{9,13},{10,... | collective-permute-start | bytes 98312 | tf_op jit(solution)/shard_map/ppermute | solution.py:29
  25.9 1.6 %collective-permute-start.8 = (f32[256,128]{1,0:T(8,128)S(1)}, f32[256,128]{1,0:T(8,128)S(1)}, u32[]{:S(2)}, u32[]{:S(2)}) collective-permute-start(f32[256,128]{1,0:T(8,128)S(1)} %get-tuple-element.27.sent_ref), channel_id=1, source_target_pairs={{0,8},{8,0},{16,24},{24,16},{1,9},{9,1},{17,25},{25,17},{2,10},{10... | collective-permute-start | bytes 393224 | tf_op jit(solution)/shard_map/ppermute | solution.py:29
  27.5 2.2 %solve.1.after_ref.first_ref = f32[4608,512]{1,0:T(8,128)S(1)} custom-call(bf16[18,256,256]{2,1,0:T(8,128)(2,1)S(1)} %permute.1.moved_ref, bf16[4608,512]{1,0:T(8,128)(2,1)S(1)} %bitcast.5, f32[64,384]{1,0:T(8,128)S(1)} %get-tuple-element.20.refs_0_), custom_call_target="tpu_custom_call" | custom-call | flops 2200000000 | tf_op jit(solution)/shard_map/solve/pallas_call | solution.py:373
  29.7 0.0 collective-permute-done.15.high_ref
  29.8 1.1 %collective-permute-start.16 = (f32[2,64,128]{2,1,0:T(8,128)S(1)}, f32[2,64,128]{2,1,0:T(8,128)S(1)}, u32[]{:S(2)}, u32[]{:S(2)}) collective-permute-start(f32[2,64,128]{2,1,0:T(8,128)S(1)} %stack.9.low_ref), channel_id=1, source_target_pairs={{0,2},{1,3},{2,0},{3,1},{4,6},{5,7},{6,4},{7,5},{8,10},{9,11},{10,... | collective-permute-start | bytes 196616 | tf_op jit(solution)/shard_map/ppermute | solution.py:29
  30.9 0.0 collective-permute-done.8.got_ref
  30.9 0.8 %level1.1 = (f32[64,128]{1,0:T(8,128)S(1)}, f32[64,128]{1,0:T(8,128)S(1)}) custom-call(f32[256,128]{1,0:T(8,128)S(1)} %get-tuple-element.27.sent_ref, f32[256,128]{1,0:T(8,128)S(1)} %collective-permute-done.8.got_ref, f32[3,256,256]{2,1,0:T(8,128)S(1)} %prepare.1.refs_4_.joined_ref, f32[4608,512]{1,0:T(8,128)S(1)} %solve.1.after_ref.first_ref), custom_call_target="tpu_custom_call" | custom-call | flops 8800000000 | tf_op jit(solution)/shard_map/level1/pallas_call | solution.py:416
  31.7 2.6 %collective-permute-start.12 = (f32[64,128]{1,0:T(8,128)S(1)}, f32[64,128]{1,0:T(8,128)S(1)}, u32[]{:S(2)}, u32[]{:S(2)}) collective-permute-start(f32[64,128]{1,0:T(8,128)S(1)} %get-tuple-element.29.sent_ref), channel_id=1, source_target_pairs={{0,16},{8,24},{16,0},{24,8},{1,17},{9,25},{17,1},{25,9},{2,18},{10... | collective-permute-start | bytes 98312 | tf_op jit(solution)/shard_map/ppermute | solution.py:29
  34.3 0.0 collective-permute-done.16.high_ref
  34.3 0.1 collective-permute-start.17
  34.4 0.0 copy-start
  34.4 0.8 %collective-permute-start.9 = (f32[1,64,128]{2,1,0:T(8,128)S(1)}, f32[1,64,128]{2,1,0:T(8,128)S(1)}, u32[]{:S(2)}, u32[]{:S(2)}) collective-permute-start(f32[1,64,128]{2,1,0:T(8,128)S(1)} %bitcast.6), channel_id=1, source_target_pairs={{0,4},{1,5},{2,6},{3,7},{4,0},{5,1},{6,2},{7,3},{8,12},{9,13},{10,... | collective-permute-start | bytes 98312 | tf_op jit(solution)/shard_map/ppermute | solution.py:29
  35.3 1.3 %collective-permute-done.12.got_ref = f32[64,128]{1,0:T(8,128)S(1)} collective-permute-done((f32[64,128]{1,0:T(8,128)S(1)}, f32[64,128]{1,0:T(8,128)S(1)}, u32[]{:S(2)}, u32[]{:S(2)}) %collective-permute-start.12) | collective-permute-done | bytes 32800 | tf_op jit(solution)/shard_map/ppermute | solution.py:29
  36.6 0.4 level2.1
  36.9 0.8 %collective-permute-start.13 = (f32[1,64,128]{2,1,0:T(8,128)S(1)}, f32[1,64,128]{2,1,0:T(8,128)S(1)}, u32[]{:S(2)}, u32[]{:S(2)}) collective-permute-start(f32[1,64,128]{2,1,0:T(8,128)S(1)} %bitcast.8), channel_id=1, source_target_pairs={{0,4},{1,5},{2,6},{3,7},{4,0},{5,1},{6,2},{7,3},{8,12},{9,13},{10,... | collective-permute-start | bytes 98312 | tf_op jit(solution)/shard_map/ppermute | solution.py:29
  37.7 0.7 %collective-permute-done.9.high_ref = f32[1,64,128]{2,1,0:T(8,128)S(1)} collective-permute-done((f32[1,64,128]{2,1,0:T(8,128)S(1)}, f32[1,64,128]{2,1,0:T(8,128)S(1)}, u32[]{:S(2)}, u32[]{:S(2)}) %collective-permute-start.9) | collective-permute-done | bytes 32800 | tf_op jit(solution)/shard_map/ppermute | solution.py:29
  38.4 1.1 %collective-permute-start.10 = (f32[2,64,128]{2,1,0:T(8,128)S(1)}, f32[2,64,128]{2,1,0:T(8,128)S(1)}, u32[]{:S(2)}, u32[]{:S(2)}) collective-permute-start(f32[2,64,128]{2,1,0:T(8,128)S(1)} %stack.6.low_ref), channel_id=1, source_target_pairs={{0,2},{1,3},{2,0},{3,1},{4,6},{5,7},{6,4},{7,5},{8,10},{9,11},{10,... | collective-permute-start | bytes 196616 | tf_op jit(solution)/shard_map/ppermute | solution.py:29
  39.5 1.4 %collective-permute-done.13.high_ref = f32[1,64,128]{2,1,0:T(8,128)S(1)} collective-permute-done((f32[1,64,128]{2,1,0:T(8,128)S(1)}, f32[1,64,128]{2,1,0:T(8,128)S(1)}, u32[]{:S(2)}, u32[]{:S(2)}) %collective-permute-start.13) | collective-permute-done | bytes 32800 | tf_op jit(solution)/shard_map/ppermute | solution.py:29
  40.9 1.1 %collective-permute-start.14 = (f32[2,64,128]{2,1,0:T(8,128)S(1)}, f32[2,64,128]{2,1,0:T(8,128)S(1)}, u32[]{:S(2)}, u32[]{:S(2)}) collective-permute-start(f32[2,64,128]{2,1,0:T(8,128)S(1)} %stack.8.low_ref), channel_id=1, source_target_pairs={{0,2},{1,3},{2,0},{3,1},{4,6},{5,7},{6,4},{7,5},{8,10},{9,11},{10,... | collective-permute-start | bytes 196616 | tf_op jit(solution)/shard_map/ppermute | solution.py:29
  42.0 0.0 collective-permute-done.17.pair_ref
  42.0 0.0 copy-done
  42.0 1.5 %apply.1.refs_0_.refs_4_ = f32[4608,512]{1,0:T(8,128)S(1)} custom-call(f32[4,64,128]{2,1,0:T(8,128)S(1)} %stack.10.own_ref, f32[4,64,128]{2,1,0:T(8,128)S(1)} %collective-permute-done.17.pair_ref, f32[4608,512]{1,0:T(8,128)S(1)} %solve.1.after_ref.first_ref, bf16[3,4608,128]{2,1,0:T(8,128)(2,1)S(1)} %copy-done), custom_call_target="tpu_custom_call" | custom-call | flops 1980000000 | tf_op jit(solution)/shard_map/apply/pallas_call | solution.py:401
  43.5 0.0 collective-permute-done.10.high_ref
  43.6 0.1 collective-permute-start.11
  43.6 1.5 %collective-permute-done.14.high_ref = f32[2,64,128]{2,1,0:T(8,128)S(1)} collective-permute-done((f32[2,64,128]{2,1,0:T(8,128)S(1)}, f32[2,64,128]{2,1,0:T(8,128)S(1)}, u32[]{:S(2)}, u32[]{:S(2)}) %collective-permute-start.14) | collective-permute-done | bytes 65568 | tf_op jit(solution)/shard_map/ppermute | solution.py:29
  45.2 0.1 collective-permute-start.18
  45.3 0.0 collective-permute-done.11.refs_1_
  45.3 1.3 %collective-permute-done.18.refs_3_ = f32[4,64,128]{2,1,0:T(8,128)S(1)} collective-permute-done((f32[4,64,128]{2,1,0:T(8,128)S(1)}, f32[4,64,128]{2,1,0:T(8,128)S(1)}, u32[]{:S(2)}, u32[]{:S(2)}) %collective-permute-start.18) | collective-permute-done | bytes 131104 | tf_op jit(solution)/shard_map/ppermute | solution.py:29
  46.6 4.5 %expand.1 = f32[4608,512]{1,0:T(8,128)} custom-call(f32[4,64,128]{2,1,0:T(8,128)S(1)} %stack.7.refs_0_, f32[4,64,128]{2,1,0:T(8,128)S(1)} %collective-permute-done.11.refs_1_, f32[4,64,128]{2,1,0:T(8,128)S(1)} %stack.11.refs_2_, f32[4,64,128]{2,1,0:T(8,128)S(1)} %collective-permute-done.18.refs_3_, f32[4608,512]{1,0:T(8,128)S(1)} %apply.1.refs_0_.refs_4_, ...), custom_call_target="tpu_custom_call" | custom-call | flops 5500000256 | tf_op jit(solution)/shard_map/expand/pallas_call | solution.py:425
  (8 shorter events, 0.1 us)
Async XLA Ops:
  0.0 6.4 %copy-start.1 = (bf16[18,256,256]{2,1,0:T(8,128)(2,1)S(1)}, bf16[18,256,256]{2,1,0:T(8,128)(2,1)}, u32[]{:S(2)}) copy-start(bf16[18,256,256]{2,1,0:T(8,128)(2,1)} %inv_ref.1) | copy-start | bytes 7077892
  0.0 6.4 %copy-start.2 = (s32[18,256]{1,0:T(8,128)S(1)}, s32[18,256]{1,0:T(8,128)}, u32[]{:S(2)}) copy-start(s32[18,256]{1,0:T(8,128)} %order_ref.1) | copy-start | bytes 55300
  3.3 8.5 %collective-permute-start = (f32[128,384]{1,0:T(8,128)S(1)}, f32[128,384]{1,0:T(8,128)S(1)}, u32[]{:S(2)}, u32[]{:S(2)}) collective-permute-start(f32[128,384]{1,0:T(8,128)S(1)} %get-tuple-element.19.after_ref.mine_ref), channel_id=1, source_target_pairs={{0,2},{1,3},{2,0},{3,1},{4,6},{5,7},{6,4},{7,5},{8,10},{9,11},{10,... | collective-permute-start | bytes 589832 | tf_op jit(solution)/shard_map/ppermute | solution.py:29
  6.4 3.4 %slice-start = ((s8[4718592]{0:T(1024)(128)(4,1)}), s8[4194304]{0:T(1024)(128)(4,1)S(1)}, s32[]{:S(2)}) async-start(s8[4718592]{0:T(1024)(128)(4,1)} %bitcast.4), calls=%async_computation | async-start | bytes 8388608
  7.6 2.2 %slice-start.1 = ((s8[4718592]{0:T(1024)(128)(4,1)}), s8[524288]{0:T(1024)(128)(4,1)S(1)}, s32[]{:S(2)}) async-start(s8[4718592]{0:T(1024)(128)(4,1)} %bitcast.4), calls=%async_computation.1 | async-start | bytes 1048576
  11.8 4.2 %collective-permute-start.1 = (f32[384,256]{1,0:T(8,128)S(1)}, f32[384,256]{1,0:T(8,128)S(1)}, u32[]{:S(2)}, u32[]{:S(2)}) collective-permute-start(f32[384,256]{1,0:T(8,128)S(1)} %project_other.1), channel_id=1, source_target_pairs={{0,1},{1,0},{2,3},{3,2},{4,5},{5,4},{6,7},{7,6},{8,9},{9,8},{10,11... | collective-permute-start | bytes 1179656 | tf_op jit(solution)/shard_map/ppermute | solution.py:29
  11.9 7.9 %copy-start.3 = (s32[3,128]{1,0:T(4,128)S(1)}, s32[3,128]{1,0:T(4,128)}, u32[]{:S(2)}) copy-start(s32[3,128]{1,0:T(4,128)} %perm_ref.1) | copy-start | bytes 4612
  11.9 12.2 %collective-permute-start.6 = (f32[128,384]{1,0:T(8,128)S(1)}, f32[128,384]{1,0:T(8,128)S(1)}, u32[]{:S(2)}, u32[]{:S(2)}) collective-permute-start(f32[128,384]{1,0:T(8,128)S(1)} %add.1.after_ref.mine_ref), channel_id=1, source_target_pairs={{0,1},{1,0},{2,3},{3,2},{4,5},{5,4},{6,7},{7,6},{8,9},{9,8},{10,11... | collective-permute-start | bytes 589832 | tf_op jit(solution)/shard_map/ppermute | solution.py:29
  12.5 7.3 %collective-permute-start.5 = (f32[128,384]{1,0:T(8,128)S(1)}, f32[128,384]{1,0:T(8,128)S(1)}, u32[]{:S(2)}, u32[]{:S(2)}) collective-permute-start(f32[128,384]{1,0:T(8,128)S(1)} %add.1.after_ref.mine_ref), channel_id=1, source_target_pairs={{0,4},{1,5},{2,6},{3,7},{4,0},{5,1},{6,2},{7,3},{8,12},{9,13},{10,... | collective-permute-start | bytes 589832 | tf_op jit(solution)/shard_map/ppermute | solution.py:29
  16.2 5.7 %collective-permute-start.2 = (f32[64,384]{1,0:T(8,128)S(1)}, f32[64,384]{1,0:T(8,128)S(1)}, u32[]{:S(2)}, u32[]{:S(2)}) collective-permute-start(f32[64,384]{1,0:T(8,128)S(1)} %get-tuple-element.21), channel_id=1, source_target_pairs={{0,2},{1,3},{2,0},{3,1},{4,6},{5,7},{6,4},{7,5},{8,10},{9,11},{10,... | collective-permute-start | bytes 294920 | tf_op jit(solution)/shard_map/ppermute | solution.py:29
  17.0 6.7 %collective-permute-start.3 = (f32[64,384]{1,0:T(8,128)S(1)}, f32[64,384]{1,0:T(8,128)S(1)}, u32[]{:S(2)}, u32[]{:S(2)}) collective-permute-start(f32[64,384]{1,0:T(8,128)S(1)} %get-tuple-element.22), channel_id=1, source_target_pairs={{0,4},{1,5},{2,6},{3,7},{4,0},{5,1},{6,2},{7,3},{8,12},{9,13},{10,... | collective-permute-start | bytes 294920 | tf_op jit(solution)/shard_map/ppermute | solution.py:29
  17.5 6.2 %collective-permute-start.4 = (f32[64,384]{1,0:T(8,128)S(1)}, f32[64,384]{1,0:T(8,128)S(1)}, u32[]{:S(2)}, u32[]{:S(2)}) collective-permute-start(f32[64,384]{1,0:T(8,128)S(1)} %get-tuple-element.23), channel_id=1, source_target_pairs={{0,6},{1,7},{2,4},{3,5},{4,2},{5,3},{6,0},{7,1},{8,14},{9,15},{10,... | collective-permute-start | bytes 294920 | tf_op jit(solution)/shard_map/ppermute | solution.py:29
  19.8 4.3 %collective-permute-start.7 = (f32[128,384]{1,0:T(8,128)S(1)}, f32[128,384]{1,0:T(8,128)S(1)}, u32[]{:S(2)}, u32[]{:S(2)}) collective-permute-start(f32[128,384]{1,0:T(8,128)S(1)} %collective-permute-done.5.theirs_ref), channel_id=1, source_target_pairs={{0,1},{1,0},{2,3},{3,2},{4,5},{5,4},{6,7},{7,6},{8,9},{9,8},{10,11... | collective-permute-start | bytes 589832 | tf_op jit(solution)/shard_map/ppermute | solution.py:29
  24.5 5.3 %collective-permute-start.15 = (f32[1,64,128]{2,1,0:T(8,128)S(1)}, f32[1,64,128]{2,1,0:T(8,128)S(1)}, u32[]{:S(2)}, u32[]{:S(2)}) collective-permute-start(f32[1,64,128]{2,1,0:T(8,128)S(1)} %bitcast.10), channel_id=1, source_target_pairs={{0,4},{1,5},{2,6},{3,7},{4,0},{5,1},{6,2},{7,3},{8,12},{9,13},{10,... | collective-permute-start | bytes 98312 | tf_op jit(solution)/shard_map/ppermute | solution.py:29
  25.9 5.0 %collective-permute-start.8 = (f32[256,128]{1,0:T(8,128)S(1)}, f32[256,128]{1,0:T(8,128)S(1)}, u32[]{:S(2)}, u32[]{:S(2)}) collective-permute-start(f32[256,128]{1,0:T(8,128)S(1)} %get-tuple-element.27.sent_ref), channel_id=1, source_target_pairs={{0,8},{8,0},{16,24},{24,16},{1,9},{9,1},{17,25},{25,17},{2,10},{10... | collective-permute-start | bytes 393224 | tf_op jit(solution)/shard_map/ppermute | solution.py:29
  29.8 4.6 %collective-permute-start.16 = (f32[2,64,128]{2,1,0:T(8,128)S(1)}, f32[2,64,128]{2,1,0:T(8,128)S(1)}, u32[]{:S(2)}, u32[]{:S(2)}) collective-permute-start(f32[2,64,128]{2,1,0:T(8,128)S(1)} %stack.9.low_ref), channel_id=1, source_target_pairs={{0,2},{1,3},{2,0},{3,1},{4,6},{5,7},{6,4},{7,5},{8,10},{9,11},{10,... | collective-permute-start | bytes 196616 | tf_op jit(solution)/shard_map/ppermute | solution.py:29
  31.7 4.9 %collective-permute-start.12 = (f32[64,128]{1,0:T(8,128)S(1)}, f32[64,128]{1,0:T(8,128)S(1)}, u32[]{:S(2)}, u32[]{:S(2)}) collective-permute-start(f32[64,128]{1,0:T(8,128)S(1)} %get-tuple-element.29.sent_ref), channel_id=1, source_target_pairs={{0,16},{8,24},{16,0},{24,8},{1,17},{9,25},{17,1},{25,9},{2,18},{10... | collective-permute-start | bytes 98312 | tf_op jit(solution)/shard_map/ppermute | solution.py:29
  34.3 7.6 %collective-permute-start.17 = (f32[4,64,128]{2,1,0:T(8,128)S(1)}, f32[4,64,128]{2,1,0:T(8,128)S(1)}, u32[]{:S(2)}, u32[]{:S(2)}) collective-permute-start(f32[4,64,128]{2,1,0:T(8,128)S(1)} %stack.10.own_ref), channel_id=1, source_target_pairs={{0,1},{1,0},{2,3},{3,2},{4,5},{5,4},{6,7},{7,6},{8,9},{9,8},{10,11... | collective-permute-start | bytes 393224 | tf_op jit(solution)/shard_map/ppermute | solution.py:29
  34.4 7.5 %copy-start = (bf16[3,4608,128]{2,1,0:T(8,128)(2,1)S(1)}, bf16[3,4608,128]{2,1,0:T(8,128)(2,1)}, u32[]{:S(2)}) copy-start(bf16[3,4608,128]{2,1,0:T(8,128)(2,1)} %refs_5_.1) | copy-start | bytes 10616836
  34.4 4.0 %collective-permute-start.9 = (f32[1,64,128]{2,1,0:T(8,128)S(1)}, f32[1,64,128]{2,1,0:T(8,128)S(1)}, u32[]{:S(2)}, u32[]{:S(2)}) collective-permute-start(f32[1,64,128]{2,1,0:T(8,128)S(1)} %bitcast.6), channel_id=1, source_target_pairs={{0,4},{1,5},{2,6},{3,7},{4,0},{5,1},{6,2},{7,3},{8,12},{9,13},{10,... | collective-permute-start | bytes 98312 | tf_op jit(solution)/shard_map/ppermute | solution.py:29
  36.9 4.0 %collective-permute-start.13 = (f32[1,64,128]{2,1,0:T(8,128)S(1)}, f32[1,64,128]{2,1,0:T(8,128)S(1)}, u32[]{:S(2)}, u32[]{:S(2)}) collective-permute-start(f32[1,64,128]{2,1,0:T(8,128)S(1)} %bitcast.8), channel_id=1, source_target_pairs={{0,4},{1,5},{2,6},{3,7},{4,0},{5,1},{6,2},{7,3},{8,12},{9,13},{10,... | collective-permute-start | bytes 98312 | tf_op jit(solution)/shard_map/ppermute | solution.py:29
  38.4 5.1 %collective-permute-start.10 = (f32[2,64,128]{2,1,0:T(8,128)S(1)}, f32[2,64,128]{2,1,0:T(8,128)S(1)}, u32[]{:S(2)}, u32[]{:S(2)}) collective-permute-start(f32[2,64,128]{2,1,0:T(8,128)S(1)} %stack.6.low_ref), channel_id=1, source_target_pairs={{0,2},{1,3},{2,0},{3,1},{4,6},{5,7},{6,4},{7,5},{8,10},{9,11},{10,... | collective-permute-start | bytes 196616 | tf_op jit(solution)/shard_map/ppermute | solution.py:29
  40.9 4.3 %collective-permute-start.14 = (f32[2,64,128]{2,1,0:T(8,128)S(1)}, f32[2,64,128]{2,1,0:T(8,128)S(1)}, u32[]{:S(2)}, u32[]{:S(2)}) collective-permute-start(f32[2,64,128]{2,1,0:T(8,128)S(1)} %stack.8.low_ref), channel_id=1, source_target_pairs={{0,2},{1,3},{2,0},{3,1},{4,6},{5,7},{6,4},{7,5},{8,10},{9,11},{10,... | collective-permute-start | bytes 196616 | tf_op jit(solution)/shard_map/ppermute | solution.py:29
  43.6 1.7 %collective-permute-start.11 = (f32[4,64,128]{2,1,0:T(8,128)S(1)}, f32[4,64,128]{2,1,0:T(8,128)S(1)}, u32[]{:S(2)}, u32[]{:S(2)}) collective-permute-start(f32[4,64,128]{2,1,0:T(8,128)S(1)} %stack.7.refs_0_), channel_id=1, source_target_pairs={{0,1},{1,0},{2,3},{3,2},{4,5},{5,4},{6,7},{7,6},{8,9},{9,8},{10,11... | collective-permute-start | bytes 393224 | tf_op jit(solution)/shard_map/ppermute | solution.py:29
  45.2 1.4 %collective-permute-start.18 = (f32[4,64,128]{2,1,0:T(8,128)S(1)}, f32[4,64,128]{2,1,0:T(8,128)S(1)}, u32[]{:S(2)}, u32[]{:S(2)}) collective-permute-start(f32[4,64,128]{2,1,0:T(8,128)S(1)} %stack.11.refs_2_), channel_id=1, source_target_pairs={{0,1},{1,0},{2,3},{3,2},{4,5},{5,4},{6,7},{7,6},{8,9},{9,8},{10,11... | collective-permute-start | bytes 393224 | tf_op jit(solution)/shard_map/ppermute | solution.py:29

commit v10 on v8

--- a/solution.py
+++ b/solution.py
@@ -37,51 +37,45 @@
     return [(level, below) for level in range(levels) for below in range(first, level)]
 
 
-def gram_kernel(levels, per_step, width, right_ref, left_ref, flip_ref, out_ref,
-                right_buf, left_buf, gram_ref, sems):
+def gram_kernel(levels, per_step, width, order_ref, inv_ref, right_ref, left_ref,
+                moved_ref, flip_ref, out_ref, order_buf, inv_buf, right_buf, left_buf, gram_ref, order_sem, sems):
     rank = right_ref.shape[2]
     tile = per_step * width
     steps = right_ref.shape[1] // tile
-
-    def copies(step):
-        rows = pl.ds(pl.multiple_of(step * tile, tile), tile)
-        return (
+    place = lax.broadcasted_iota(jnp.int32, (width, width), 0)
+    order_copy = pltpu.make_async_copy(order_ref, order_buf, order_sem)
+    copies = []
+    for step in range(steps):
+        rows = pl.ds(step * tile, tile)
+        blocks = pl.ds(step * per_step, per_step)
+        copies.append((
             pltpu.make_async_copy(right_ref.at[:, rows], right_buf.at[:, rows], sems.at[0, step]),
             pltpu.make_async_copy(left_ref.at[:levels - 1, rows], left_buf.at[:, rows], sems.at[1, step]),
-        )
-
+            pltpu.make_async_copy(inv_ref.at[blocks], inv_buf.at[blocks], sems.at[2, step]),
+        ))
+        for copy in copies[-1]:
+            copy.start()
+        if step == 0:
+            order_copy.start()
+    gram_ref[...] = jnp.zeros_like(gram_ref)
     for step in range(steps):
-        for copy in copies(step):
-            copy.start()
-    gram_ref[...] = jnp.zeros_like(gram_ref)
-
-    def body(step, _):
-        for copy in copies(step):
-            copy.wait()
-        rows = pl.ds(pl.multiple_of(step * tile, tile), tile)
+        rows = pl.ds(step * tile, tile)
+        copies[step][0].wait()
+        copies[step][1].wait()
         right = jnp.concatenate([right_buf[l, rows, :] for l in range(levels)], axis=1).T
         flip_ref[:, rows] = right
         left = jnp.concatenate([left_buf[l, rows, :] for l in range(levels - 1)], axis=1)
         gram_ref[...] += dot(right[rank:], left, (1, 0))
-        return 0
-
-    lax.fori_loop(0, steps, body, 0)
+        copies[step][2].wait()
+        if step == 0:
+            order_copy.wait()
+        for b in range(per_step):
+            block = step * per_step + b
+            chosen = (place == order_buf[block:block + 1, :]).astype(jnp.float32).astype(jnp.bfloat16)
+            moved_ref[block] = dot(inv_buf[block], chosen, (1, 1)).astype(jnp.bfloat16)
     for spot, (level, below) in enumerate(below_pairs(levels)):
         rows = pl.ds((level - 1) * rank, rank)
         out_ref[:, pl.ds(spot * rank, rank)] = gram_ref[rows, pl.ds(below * rank, rank)]
-
-
-def permute_kernel(per_step, width, order_ref, inv_ref, moved_ref):
-    place = lax.broadcasted_iota(jnp.int32, (width, width), 0)
-
-    def body(step, _):
-        for b in range(per_step):
-            block = step * per_step + b
-            chosen = (place == order_ref[pl.ds(block, 1), :]).astype(jnp.float32).astype(jnp.bfloat16)
-            moved_ref[block] = dot(inv_ref[block], chosen, (1, 1)).astype(jnp.bfloat16)
-        return 0
-
-    lax.fori_loop(0, inv_ref.shape[0] // per_step, body, 0)
 
 
 def weigh_kernel(per_step, width, moved_ref, flip_ref, after_ref, factor_ref):
@@ -227,6 +221,10 @@
         refs[-1][slot] = ref[...]
 
 
+def relay_kernel(after_ref, ref, out_ref):
+    out_ref[...] = ref[...]
+
+
 def split_factor(pieces, flip_ref, factor_ref):
     share, kinds = pieces[0].shape
     slots = len(pieces) // 2
@@ -288,27 +286,26 @@
     gram_lanes = len(below_pairs(levels)) * rank
 
     per_step = blocks_per_step(nblocks, 3)
-    flipped, gram = pl.pallas_call(
+    moved, flipped, gram = pl.pallas_call(
         functools.partial(gram_kernel, levels, per_step, width),
-        in_specs=[pl.BlockSpec(memory_space=pltpu.HBM)] * 2,
-        out_shape=[jax.ShapeDtypeStruct((kinds, rows), jnp.bfloat16), floats(rank, gram_lanes)],
+        in_specs=[pl.BlockSpec(memory_space=pltpu.HBM)] * 4,
+        out_shape=[
+            jax.ShapeDtypeStruct((nblocks, width, width), jnp.bfloat16),
+            jax.ShapeDtypeStruct((kinds, rows), jnp.bfloat16),
+            floats(rank, gram_lanes),
+        ],
         scratch_shapes=[
+            pltpu.VMEM((nblocks, width), jnp.int32),
+            pltpu.VMEM((nblocks, width, width), jnp.bfloat16),
             pltpu.VMEM((levels, rows, rank), jnp.bfloat16),
             pltpu.VMEM((levels - 1, rows, rank), jnp.bfloat16),
             pltpu.VMEM((size, size), jnp.float32),
-            pltpu.SemaphoreType.DMA((2, nblocks // per_step)),
+            pltpu.SemaphoreType.DMA,
+            pltpu.SemaphoreType.DMA((3, nblocks // per_step)),
         ],
         name="gram",
-        **settings(24, 3),
-    )(pltpu.with_memory_space_constraint(right_basis, pltpu.HBM),
-      pltpu.with_memory_space_constraint(left_basis, pltpu.HBM))
-
-    moved = pl.pallas_call(
-        functools.partial(permute_kernel, blocks_per_step(nblocks, 6), width),
-        out_shape=jax.ShapeDtypeStruct((nblocks, width, width), jnp.bfloat16),
-        name="permute",
-        **settings(8, 1.5),
-    )(leaf_order, leaf_inv)
+        **settings(24, 4),
+    )(*(pltpu.with_memory_space_constraint(x, pltpu.HBM) for x in (leaf_order, leaf_inv, right_basis, left_basis)))
 
     def add(mine, got):
         return pl.pallas_call(
@@ -316,7 +313,7 @@
         )(mine, got)
 
     factors = pl.pallas_call(
-        functools.partial(weigh_kernel, per_step, width),
+        functools.partial(weigh_kernel, blocks_per_step(nblocks, 9), width),
         out_shape=jax.ShapeDtypeStruct((2 * kinds, rows), jnp.bfloat16),
         name="weigh",
         **settings(8, 2.4),
@@ -411,6 +408,10 @@
     pieces = []
     for slot in range(slots):
         piece = swap(pack, "rows", 2 * slot) if slot > 0 else pack
+        if slot == slots - 1:
+            piece = pl.pallas_call(
+                relay_kernel, out_shape=floats(share, size), name="relay", **settings(8, 0.1),
+            )(second, piece)
         pieces += [piece, swap(piece, "rows", 1)]
     return pl.pallas_call(
         functools.partial(expand_kernel, levels, per_step * width, count),

time: 49.5 us -> 52.8 us (1.067)
  Pallas kernels: 23.3 us -> 25.1 us
  local copies, waits for them, and re-layouts: 0.03 us -> 0.74 us
  waiting for transfers between devices: 5.2 us -> 5.81 us
    pallas_call x1, Pallas kernels: 3.34 us -> 7 us  [per_device(): pl.pallas_call(functools.partial(gram_kernel, levels, per_step, width), i...]
    pallas_call x2, Pallas kernels: 3.37 us -> 1.61 us  [the longest x1 1.6 us: per_device(): pl.pallas_call(functools.partial(weigh_kernel, blocks_per_step(nblocks, 9...]
    unnamed x12 -> x6, local copies, waits for them, and re-layouts: 0.03 us -> 0.74 us
    ppermute x21, waiting for transfers between devices: 5.2 us -> 5.81 us  [swap(): return lax.ppermute(value, axis, [(i, i ^ mask) for i in range(count)])]
  transfers between devices with their start and end apart: 21 -> 21, of which waited for: 4 -> 4; matrix products, arithmetic and copies ran while one was open for 0% -> 0% of each run, Pallas kernels for 30% -> 25%
where the time goes in v10:
time: 52.8 us; the launch traced here: 52.7 us
  Pallas kernels  25.1 us (48%)
  starting transfers between devices  20.6 us (39%)
  waiting for transfers between devices  5.81 us (11%)
  local copies, waits for them, and re-layouts  0.74 us (1%)
    ppermute x21, starting transfers between devices, swap(): return lax.ppermute(value, axis, [(i, i ^ mask) for i in range(count)])  20.6 us
    pallas_call x1, Pallas kernels, per_device(): pl.pallas_call(functools.partial(gram_kernel, levels, per_step, width), i...  7 us
    ppermute x21, waiting for transfers between devices, swap(): return lax.ppermute(value, axis, [(i, i ^ mask) for i in range(count)])  5.81 us
    pallas_call x1, Pallas kernels, per_device(): pl.pallas_call(functools.partial(expand_kernel, levels, per_step * width,...  4.5 us
    pallas_call x2, Pallas kernels, project(): pl.pallas_call(functools.partial(project_kernel, other), out_shape=floats...  3.98 us
    pallas_call x1, Pallas kernels, per_device(): pl.pallas_call(functools.partial(solve_kernel, per_step, width), out_shap...  2.22 us
    pallas_call x1, Pallas kernels, per_device(): pl.pallas_call(functools.partial(prepare_kernel, levels), in_specs=[pl.Bl...  2.11 us
    pallas_call x1, Pallas kernels, per_device(): pl.pallas_call(functools.partial(weigh_kernel, blocks_per_step(nblocks, 9...  1.6 us
  transfers between devices with their start and end apart: 21, of which 4 were waited for; matrix products, arithmetic and copies ran while one was open for 0% of the time, Pallas kernels for 25%

profile of v10, /device:TPU:0, one launch (start us, length us, event | category | flops | bytes accessed | tf_op | source)
XLA Modules:
  0.0 52.7 jit_solution(18054977896218472728)
XLA Ops:
  0.0 7.0 %gram.1 = (bf16[18,256,256]{2,1,0:T(8,128)(2,1)S(1)}, bf16[384,4608]{1,0:T(8,128)(2,1)S(1)}, f32[128,384]{1,0:T(8,128)S(1)}) custom-call(s32[18,256]{1,0:T(8,128)} %order_ref.1, bf16[18,256,256]{2,1,0:T(8,128)(2,1)} %inv_ref.1, bf16[3,4608,128]{2,1,0:T(8,128)(2,1)} %right_ref.1, bf16[3,4608,128]{2,1,0:T(8,128)(2,1)} %refs_9_.1), custom_call_target="tpu_custom_call" | custom-call | flops 4400000000 | tf_op jit(solution)/shard_map/gram/pallas_call | solution.py:289
  7.0 3.0 %collective-permute-start = (f32[128,384]{1,0:T(8,128)S(1)}, f32[128,384]{1,0:T(8,128)S(1)}, u32[]{:S(2)}, u32[]{:S(2)}) collective-permute-start(f32[128,384]{1,0:T(8,128)S(1)} %get-tuple-element.19.after_ref.mine_ref), channel_id=1, source_target_pairs={{0,2},{1,3},{2,0},{3,1},{4,6},{5,7},{6,4},{7,5},{8,10},{9,11},{10,... | collective-permute-start | bytes 589832 | tf_op jit(solution)/shard_map/ppermute | solution.py:29
  10.0 0.0 copy-start.1
  10.0 1.6 %weigh.1.factor_ref = bf16[768,4608]{1,0:T(8,128)(2,1)S(1)} custom-call(bf16[18,256,256]{2,1,0:T(8,128)(2,1)S(1)} %get-tuple-element.17.moved_ref, bf16[384,4608]{1,0:T(8,128)(2,1)S(1)} %get-tuple-element.18.flip_ref, f32[128,384]{1,0:T(8,128)S(1)} %get-tuple-element.19.after_ref.mine_ref), custom_call_target="tpu_custom_call" | custom-call | flops 2640000000 | tf_op jit(solution)/shard_map/weigh/pallas_call | solution.py:315
  11.6 0.7 %copy-done.1 = bf16[4608,512]{1,0:T(8,128)(2,1)S(1)} copy-done((bf16[4608,512]{1,0:T(8,128)(2,1)S(1)}, bf16[4608,512]{1,0:T(8,128)(2,1)}, u32[]{:S(2)}) %copy-start.1) | copy-done | bytes 4718616
  12.4 2.0 %project_other.1 = f32[384,256]{1,0:T(8,128)S(1)} custom-call(bf16[768,4608]{1,0:T(8,128)(2,1)S(1)} %weigh.1.factor_ref, bf16[4608,512]{1,0:T(8,128)(2,1)S(1)} %copy-done.1, f32[128,384]{1,0:T(8,128)S(1)} %get-tuple-element.19.after_ref.mine_ref), custom_call_target="tpu_custom_call" | custom-call | flops 1100000000 | tf_op jit(solution)/shard_map/project_other/pallas_call | solution.py:323
  14.4 0.1 collective-permute-start.1
  14.4 0.5 collective-permute-done.got_ref
  14.9 0.0 copy-start.2
  15.0 1.8 %collective-permute-start.5 = (f32[128,384]{1,0:T(8,128)S(1)}, f32[128,384]{1,0:T(8,128)S(1)}, u32[]{:S(2)}, u32[]{:S(2)}) collective-permute-start(f32[128,384]{1,0:T(8,128)S(1)} %add.1.after_ref.mine_ref), channel_id=1, source_target_pairs={{0,4},{1,5},{2,6},{3,7},{4,0},{5,1},{6,2},{7,3},{8,12},{9,13},{10,... | collective-permute-start | bytes 589832 | tf_op jit(solution)/shard_map/ppermute | solution.py:29
  16.8 2.0 %project_own.1.keep_ref = f32[384,256]{1,0:T(8,128)S(1)} custom-call(bf16[768,4608]{1,0:T(8,128)(2,1)S(1)} %weigh.1.factor_ref, bf16[4608,512]{1,0:T(8,128)(2,1)S(1)} %copy-done.1, f32[128,384]{1,0:T(8,128)S(1)} %add.1.after_ref.mine_ref), custom_call_target="tpu_custom_call" | custom-call | flops 8800000000 | tf_op jit(solution)/shard_map/project_own/pallas_call | solution.py:323
  18.8 0.1 collective-permute-start.6
  18.9 0.0 collective-permute-done.1.got_ref
  18.9 0.2 merge.1
  19.1 1.6 %collective-permute-start.2 = (f32[64,384]{1,0:T(8,128)S(1)}, f32[64,384]{1,0:T(8,128)S(1)}, u32[]{:S(2)}, u32[]{:S(2)}) collective-permute-start(f32[64,384]{1,0:T(8,128)S(1)} %get-tuple-element.21), channel_id=1, source_target_pairs={{0,2},{1,3},{2,0},{3,1},{4,6},{5,7},{6,4},{7,5},{8,10},{9,11},{10,... | collective-permute-start | bytes 294920 | tf_op jit(solution)/shard_map/ppermute | solution.py:29
  20.6 0.5 collective-permute-start.3
  21.1 1.5 %collective-permute-start.4 = (f32[64,384]{1,0:T(8,128)S(1)}, f32[64,384]{1,0:T(8,128)S(1)}, u32[]{:S(2)}, u32[]{:S(2)}) collective-permute-start(f32[64,384]{1,0:T(8,128)S(1)} %get-tuple-element.23), channel_id=1, source_target_pairs={{0,6},{1,7},{2,4},{3,5},{4,2},{5,3},{6,0},{7,1},{8,14},{9,15},{10,... | collective-permute-start | bytes 294920 | tf_op jit(solution)/shard_map/ppermute | solution.py:29
  22.6 0.0 collective-permute-done.5.theirs_ref
  22.6 0.0 collective-permute-start.7
  22.6 0.0 copy-done.2
  22.6 2.1 %prepare.1.refs_4_.joined_ref = f32[3,256,256]{2,1,0:T(8,128)S(1)} custom-call(f32[7,256,256]{2,1,0:T(8,128)} %joined_ref.1, s32[3,128]{1,0:T(4,128)S(1)} %copy-done.2), custom_call_target="tpu_custom_call" | custom-call | flops 2200000000 | tf_op jit(solution)/shard_map/prepare/pallas_call | solution.py:347
  24.8 0.0 collective-permute-done.2.refs_1_
  24.8 2.9 %collective-permute-done.3.refs_2_ = f32[64,384]{1,0:T(8,128)S(1)} collective-permute-done((f32[64,384]{1,0:T(8,128)S(1)}, f32[64,384]{1,0:T(8,128)S(1)}, u32[]{:S(2)}, u32[]{:S(2)}) %collective-permute-start.3) | collective-permute-done | bytes 98336 | tf_op jit(solution)/shard_map/ppermute | solution.py:29
  27.6 0.0 collective-permute-done.4.refs_3_
  27.7 0.4 node.1
  28.0 0.0 collective-permute-done.6.pair_mine_ref
  28.0 0.0 collective-permute-done.7.pair_theirs_ref
  28.0 0.4 correct.1.sent_ref
  28.4 1.6 %collective-permute-start.8 = (f32[256,128]{1,0:T(8,128)S(1)}, f32[256,128]{1,0:T(8,128)S(1)}, u32[]{:S(2)}, u32[]{:S(2)}) collective-permute-start(f32[256,128]{1,0:T(8,128)S(1)} %correct.1.sent_ref), channel_id=1, source_target_pairs={{0,8},{8,0},{16,24},{24,16},{1,9},{9,1},{17,25},{25,17},{2,10},{10... | collective-permute-start | bytes 393224 | tf_op jit(solution)/shard_map/ppermute | solution.py:29
  30.1 0.5 %collective-permute-start.15 = (f32[64,128]{1,0:T(8,128)S(1)}, f32[64,128]{1,0:T(8,128)S(1)}, u32[]{:S(2)}, u32[]{:S(2)}) collective-permute-start(f32[64,128]{1,0:T(8,128)S(1)} %get-tuple-element.24.own_ref.refs_0_), channel_id=1, source_target_pairs={{0,2},{1,3},{2,0},{3,1},{4,6},{5,7},{6,4},{7,5},{8,10},{9,11},{10,... | collective-permute-start | bytes 98312 | tf_op jit(solution)/shard_map/ppermute | solution.py:29
  30.6 1.2 %collective-permute-start.16 = (f32[64,128]{1,0:T(8,128)S(1)}, f32[64,128]{1,0:T(8,128)S(1)}, u32[]{:S(2)}, u32[]{:S(2)}) collective-permute-start(f32[64,128]{1,0:T(8,128)S(1)} %get-tuple-element.25.other_ref), channel_id=1, source_target_pairs={{0,4},{1,5},{2,6},{3,7},{4,0},{5,1},{6,2},{7,3},{8,12},{9,13},{10,... | collective-permute-start | bytes 98312 | tf_op jit(solution)/shard_map/ppermute | solution.py:29
  31.8 1.7 %collective-permute-start.17 = (f32[64,128]{1,0:T(8,128)S(1)}, f32[64,128]{1,0:T(8,128)S(1)}, u32[]{:S(2)}, u32[]{:S(2)}) collective-permute-start(f32[64,128]{1,0:T(8,128)S(1)} %get-tuple-element.25.other_ref), channel_id=1, source_target_pairs={{0,6},{1,7},{2,4},{3,5},{4,2},{5,3},{6,0},{7,1},{8,14},{9,15},{10,... | collective-permute-start | bytes 98312 | tf_op jit(solution)/shard_map/ppermute | solution.py:29
  33.5 0.0 collective-permute-done.8.got_ref.after_ref
  33.5 0.8 %level1.1 = (f32[64,128]{1,0:T(8,128)S(1)}, f32[64,128]{1,0:T(8,128)S(1)}) custom-call(f32[256,128]{1,0:T(8,128)S(1)} %correct.1.sent_ref, f32[256,128]{1,0:T(8,128)S(1)} %collective-permute-done.8.got_ref.after_ref, f32[3,256,256]{2,1,0:T(8,128)S(1)} %prepare.1.refs_4_.joined_ref, f32[256,128]{1,0:T(8,128)S(1)} %collective-permute-done.8.got_ref.after_ref), custom_call_target="tpu_custom_call" | custom-call | flops 6600000000 | tf_op jit(solution)/shard_map/level1/pallas_call | solution.py:383
  34.3 2.7 %collective-permute-start.9 = (f32[64,128]{1,0:T(8,128)S(1)}, f32[64,128]{1,0:T(8,128)S(1)}, u32[]{:S(2)}, u32[]{:S(2)}) collective-permute-start(f32[64,128]{1,0:T(8,128)S(1)} %get-tuple-element.28.sent_ref), channel_id=1, source_target_pairs={{0,16},{8,24},{16,0},{24,8},{1,17},{9,25},{17,1},{25,9},{2,18},{10... | collective-permute-start | bytes 98312 | tf_op jit(solution)/shard_map/ppermute | solution.py:29
  37.0 2.2 %solve.1.after_ref.first_ref = f32[4608,512]{1,0:T(8,128)S(1)} custom-call(bf16[18,256,256]{2,1,0:T(8,128)(2,1)S(1)} %get-tuple-element.17.moved_ref, bf16[4608,512]{1,0:T(8,128)(2,1)S(1)} %copy-done.1, f32[64,384]{1,0:T(8,128)S(1)} %get-tuple-element.20.refs_0_), custom_call_target="tpu_custom_call" | custom-call | flops 8800000000 | tf_op jit(solution)/shard_map/solve/pallas_call | solution.py:372
  39.2 0.0 collective-permute-done.15.refs_1_
  39.2 0.0 collective-permute-done.16.refs_2_
  39.2 0.0 collective-permute-done.17.refs_3_
  39.3 0.0 copy-start
  39.3 0.1 collective-permute-start.18
  39.3 0.0 collective-permute-done.9.got_ref
  39.4 0.4 level2.1.refs_1_
  39.7 0.6 %collective-permute-start.11 = (f32[64,256]{1,0:T(8,128)S(1)}, f32[64,256]{1,0:T(8,128)S(1)}, u32[]{:S(2)}, u32[]{:S(2)}) collective-permute-start(f32[64,256]{1,0:T(8,128)S(1)} %pack.1.refs_0_), channel_id=1, source_target_pairs={{0,2},{1,3},{2,0},{3,1},{4,6},{5,7},{6,4},{7,5},{8,10},{9,11},{10,... | collective-permute-start | bytes 196616 | tf_op jit(solution)/shard_map/ppermute | solution.py:29
  40.3 1.2 %collective-permute-start.13 = (f32[64,256]{1,0:T(8,128)S(1)}, f32[64,256]{1,0:T(8,128)S(1)}, u32[]{:S(2)}, u32[]{:S(2)}) collective-permute-start(f32[64,256]{1,0:T(8,128)S(1)} %pack.1.refs_0_), channel_id=1, source_target_pairs={{0,4},{1,5},{2,6},{3,7},{4,0},{5,1},{6,2},{7,3},{8,12},{9,13},{10,... | collective-permute-start | bytes 196616 | tf_op jit(solution)/shard_map/ppermute | solution.py:29
  41.6 1.7 %collective-permute-start.19 = (f32[64,256]{1,0:T(8,128)S(1)}, f32[64,256]{1,0:T(8,128)S(1)}, u32[]{:S(2)}, u32[]{:S(2)}) collective-permute-start(f32[64,256]{1,0:T(8,128)S(1)} %pack.1.refs_0_), channel_id=1, source_target_pairs={{0,6},{1,7},{2,4},{3,5},{4,2},{5,3},{6,0},{7,1},{8,14},{9,15},{10,... | collective-permute-start | bytes 196616 | tf_op jit(solution)/shard_map/ppermute | solution.py:29
  43.3 0.0 collective-permute-done.18.pair_ref
  43.3 0.0 copy-done
  43.3 1.6 %apply.1.after_ref.refs_8_ = f32[4608,512]{1,0:T(8,128)S(1)} custom-call(f32[4,64,128]{2,1,0:T(8,128)S(1)} %stack.1.own_ref, f32[4,64,128]{2,1,0:T(8,128)S(1)} %collective-permute-done.18.pair_ref, f32[4608,512]{1,0:T(8,128)S(1)} %solve.1.after_ref.first_ref, bf16[3,4608,128]{2,1,0:T(8,128)(2,1)S(1)} %copy-done), custom_call_target="tpu_custom_call" | custom-call | flops 1980000000 | tf_op jit(solution)/shard_map/apply/pallas_call | solution.py:394
  44.9 0.1 collective-permute-start.10
  45.0 0.0 collective-permute-done.11.refs_2_
  45.0 0.5 collective-permute-start.12
  45.5 0.0 collective-permute-done.13.refs_4_
  45.5 0.1 collective-permute-start.14
  45.6 1.2 %collective-permute-done.19.ref = f32[64,256]{1,0:T(8,128)S(1)} collective-permute-done((f32[64,256]{1,0:T(8,128)S(1)}, f32[64,256]{1,0:T(8,128)S(1)}, u32[]{:S(2)}, u32[]{:S(2)}) %collective-permute-start.19) | collective-permute-done | bytes 65568 | tf_op jit(solution)/shard_map/ppermute | solution.py:29
  46.8 0.0 collective-permute-start.20
  46.8 0.0 collective-permute-done.10.refs_1_
  46.8 0.0 collective-permute-done.12.refs_3_
  46.8 0.0 collective-permute-done.14.refs_5_
  46.8 1.2 %collective-permute-done.20.refs_7_ = f32[64,256]{1,0:T(8,128)S(1)} collective-permute-done((f32[64,256]{1,0:T(8,128)S(1)}, f32[64,256]{1,0:T(8,128)S(1)}, u32[]{:S(2)}, u32[]{:S(2)}) %collective-permute-start.20) | collective-permute-done | bytes 65568 | tf_op jit(solution)/shard_map/ppermute | solution.py:29
  48.0 4.5 %expand.1 = f32[4608,512]{1,0:T(8,128)} custom-call(f32[64,256]{1,0:T(8,128)S(1)} %pack.1.refs_0_, f32[64,256]{1,0:T(8,128)S(1)} %collective-permute-done.10.refs_1_, f32[64,256]{1,0:T(8,128)S(1)} %collective-permute-done.11.refs_2_, f32[64,256]{1,0:T(8,128)S(1)} %collective-permute-done.12.refs_3_, f32[64,256]{1,0:T(8,128)S(1)} %collective-permute-done.13.refs_4_, ...), custom_call_target="tpu_custom_call" | custom-call | flops 5500000256 | tf_op jit(solution)/shard_map/expand/pallas_call | solution.py:416
  (4 shorter events, 0.0 us)
Async XLA Ops:
  7.0 7.9 %collective-permute-start = (f32[128,384]{1,0:T(8,128)S(1)}, f32[128,384]{1,0:T(8,128)S(1)}, u32[]{:S(2)}, u32[]{:S(2)}) collective-permute-start(f32[128,384]{1,0:T(8,128)S(1)} %get-tuple-element.19.after_ref.mine_ref), channel_id=1, source_target_pairs={{0,2},{1,3},{2,0},{3,1},{4,6},{5,7},{6,4},{7,5},{8,10},{9,11},{10,... | collective-permute-start | bytes 589832 | tf_op jit(solution)/shard_map/ppermute | solution.py:29
  10.0 2.3 %copy-start.1 = (bf16[4608,512]{1,0:T(8,128)(2,1)S(1)}, bf16[4608,512]{1,0:T(8,128)(2,1)}, u32[]{:S(2)}) copy-start(bf16[4608,512]{1,0:T(8,128)(2,1)} %rhs_ref.5) | copy-start | bytes 14155780
  14.4 4.5 %collective-permute-start.1 = (f32[384,256]{1,0:T(8,128)S(1)}, f32[384,256]{1,0:T(8,128)S(1)}, u32[]{:S(2)}, u32[]{:S(2)}) collective-permute-start(f32[384,256]{1,0:T(8,128)S(1)} %project_other.1), channel_id=1, source_target_pairs={{0,1},{1,0},{2,3},{3,2},{4,5},{5,4},{6,7},{7,6},{8,9},{9,8},{10,11... | collective-permute-start | bytes 1179656 | tf_op jit(solution)/shard_map/ppermute | solution.py:29
  14.9 7.7 %copy-start.2 = (s32[3,128]{1,0:T(4,128)S(1)}, s32[3,128]{1,0:T(4,128)}, u32[]{:S(2)}) copy-start(s32[3,128]{1,0:T(4,128)} %perm_ref.1) | copy-start | bytes 4612
  15.0 7.7 %collective-permute-start.5 = (f32[128,384]{1,0:T(8,128)S(1)}, f32[128,384]{1,0:T(8,128)S(1)}, u32[]{:S(2)}, u32[]{:S(2)}) collective-permute-start(f32[128,384]{1,0:T(8,128)S(1)} %add.1.after_ref.mine_ref), channel_id=1, source_target_pairs={{0,4},{1,5},{2,6},{3,7},{4,0},{5,1},{6,2},{7,3},{8,12},{9,13},{10,... | collective-permute-start | bytes 589832 | tf_op jit(solution)/shard_map/ppermute | solution.py:29
  18.8 9.2 %collective-permute-start.6 = (f32[128,384]{1,0:T(8,128)S(1)}, f32[128,384]{1,0:T(8,128)S(1)}, u32[]{:S(2)}, u32[]{:S(2)}) collective-permute-start(f32[128,384]{1,0:T(8,128)S(1)} %add.1.after_ref.mine_ref), channel_id=1, source_target_pairs={{0,1},{1,0},{2,3},{3,2},{4,5},{5,4},{6,7},{7,6},{8,9},{9,8},{10,11... | collective-permute-start | bytes 589832 | tf_op jit(solution)/shard_map/ppermute | solution.py:29
  19.1 5.7 %collective-permute-start.2 = (f32[64,384]{1,0:T(8,128)S(1)}, f32[64,384]{1,0:T(8,128)S(1)}, u32[]{:S(2)}, u32[]{:S(2)}) collective-permute-start(f32[64,384]{1,0:T(8,128)S(1)} %get-tuple-element.21), channel_id=1, source_target_pairs={{0,2},{1,3},{2,0},{3,1},{4,6},{5,7},{6,4},{7,5},{8,10},{9,11},{10,... | collective-permute-start | bytes 294920 | tf_op jit(solution)/shard_map/ppermute | solution.py:29
  20.6 7.0 %collective-permute-start.3 = (f32[64,384]{1,0:T(8,128)S(1)}, f32[64,384]{1,0:T(8,128)S(1)}, u32[]{:S(2)}, u32[]{:S(2)}) collective-permute-start(f32[64,384]{1,0:T(8,128)S(1)} %get-tuple-element.22), channel_id=1, source_target_pairs={{0,4},{1,5},{2,6},{3,7},{4,0},{5,1},{6,2},{7,3},{8,12},{9,13},{10,... | collective-permute-start | bytes 294920 | tf_op jit(solution)/shard_map/ppermute | solution.py:29
  21.1 6.5 %collective-permute-start.4 = (f32[64,384]{1,0:T(8,128)S(1)}, f32[64,384]{1,0:T(8,128)S(1)}, u32[]{:S(2)}, u32[]{:S(2)}) collective-permute-start(f32[64,384]{1,0:T(8,128)S(1)} %get-tuple-element.23), channel_id=1, source_target_pairs={{0,6},{1,7},{2,4},{3,5},{4,2},{5,3},{6,0},{7,1},{8,14},{9,15},{10,... | collective-permute-start | bytes 294920 | tf_op jit(solution)/shard_map/ppermute | solution.py:29
  22.6 5.4 %collective-permute-start.7 = (f32[128,384]{1,0:T(8,128)S(1)}, f32[128,384]{1,0:T(8,128)S(1)}, u32[]{:S(2)}, u32[]{:S(2)}) collective-permute-start(f32[128,384]{1,0:T(8,128)S(1)} %collective-permute-done.5.theirs_ref), channel_id=1, source_target_pairs={{0,1},{1,0},{2,3},{3,2},{4,5},{5,4},{6,7},{7,6},{8,9},{9,8},{10,11... | collective-permute-start | bytes 589832 | tf_op jit(solution)/shard_map/ppermute | solution.py:29
  28.4 5.1 %collective-permute-start.8 = (f32[256,128]{1,0:T(8,128)S(1)}, f32[256,128]{1,0:T(8,128)S(1)}, u32[]{:S(2)}, u32[]{:S(2)}) collective-permute-start(f32[256,128]{1,0:T(8,128)S(1)} %correct.1.sent_ref), channel_id=1, source_target_pairs={{0,8},{8,0},{16,24},{24,16},{1,9},{9,1},{17,25},{25,17},{2,10},{10... | collective-permute-start | bytes 393224 | tf_op jit(solution)/shard_map/ppermute | solution.py:29
  30.1 9.2 %collective-permute-start.15 = (f32[64,128]{1,0:T(8,128)S(1)}, f32[64,128]{1,0:T(8,128)S(1)}, u32[]{:S(2)}, u32[]{:S(2)}) collective-permute-start(f32[64,128]{1,0:T(8,128)S(1)} %get-tuple-element.24.own_ref.refs_0_), channel_id=1, source_target_pairs={{0,2},{1,3},{2,0},{3,1},{4,6},{5,7},{6,4},{7,5},{8,10},{9,11},{10,... | collective-permute-start | bytes 98312 | tf_op jit(solution)/shard_map/ppermute | solution.py:29
  30.6 8.6 %collective-permute-start.16 = (f32[64,128]{1,0:T(8,128)S(1)}, f32[64,128]{1,0:T(8,128)S(1)}, u32[]{:S(2)}, u32[]{:S(2)}) collective-permute-start(f32[64,128]{1,0:T(8,128)S(1)} %get-tuple-element.25.other_ref), channel_id=1, source_target_pairs={{0,4},{1,5},{2,6},{3,7},{4,0},{5,1},{6,2},{7,3},{8,12},{9,13},{10,... | collective-permute-start | bytes 98312 | tf_op jit(solution)/shard_map/ppermute | solution.py:29
  31.8 7.4 %collective-permute-start.17 = (f32[64,128]{1,0:T(8,128)S(1)}, f32[64,128]{1,0:T(8,128)S(1)}, u32[]{:S(2)}, u32[]{:S(2)}) collective-permute-start(f32[64,128]{1,0:T(8,128)S(1)} %get-tuple-element.25.other_ref), channel_id=1, source_target_pairs={{0,6},{1,7},{2,4},{3,5},{4,2},{5,3},{6,0},{7,1},{8,14},{9,15},{10,... | collective-permute-start | bytes 98312 | tf_op jit(solution)/shard_map/ppermute | solution.py:29
  34.3 5.0 %collective-permute-start.9 = (f32[64,128]{1,0:T(8,128)S(1)}, f32[64,128]{1,0:T(8,128)S(1)}, u32[]{:S(2)}, u32[]{:S(2)}) collective-permute-start(f32[64,128]{1,0:T(8,128)S(1)} %get-tuple-element.28.sent_ref), channel_id=1, source_target_pairs={{0,16},{8,24},{16,0},{24,8},{1,17},{9,25},{17,1},{25,9},{2,18},{10... | collective-permute-start | bytes 98312 | tf_op jit(solution)/shard_map/ppermute | solution.py:29
  39.3 4.0 %copy-start = (bf16[3,4608,128]{2,1,0:T(8,128)(2,1)S(1)}, bf16[3,4608,128]{2,1,0:T(8,128)(2,1)}, u32[]{:S(2)}) copy-start(bf16[3,4608,128]{2,1,0:T(8,128)(2,1)} %refs_9_.1) | copy-start | bytes 10616836
  39.3 4.0 %collective-permute-start.18 = (f32[4,64,128]{2,1,0:T(8,128)S(1)}, f32[4,64,128]{2,1,0:T(8,128)S(1)}, u32[]{:S(2)}, u32[]{:S(2)}) collective-permute-start(f32[4,64,128]{2,1,0:T(8,128)S(1)} %stack.1.own_ref), channel_id=1, source_target_pairs={{0,1},{1,0},{2,3},{3,2},{4,5},{5,4},{6,7},{7,6},{8,9},{9,8},{10,11... | collective-permute-start | bytes 393224 | tf_op jit(solution)/shard_map/ppermute | solution.py:29
  39.7 5.2 %collective-permute-start.11 = (f32[64,256]{1,0:T(8,128)S(1)}, f32[64,256]{1,0:T(8,128)S(1)}, u32[]{:S(2)}, u32[]{:S(2)}) collective-permute-start(f32[64,256]{1,0:T(8,128)S(1)} %pack.1.refs_0_), channel_id=1, source_target_pairs={{0,2},{1,3},{2,0},{3,1},{4,6},{5,7},{6,4},{7,5},{8,10},{9,11},{10,... | collective-permute-start | bytes 196616 | tf_op jit(solution)/shard_map/ppermute | solution.py:29
  40.3 5.1 %collective-permute-start.13 = (f32[64,256]{1,0:T(8,128)S(1)}, f32[64,256]{1,0:T(8,128)S(1)}, u32[]{:S(2)}, u32[]{:S(2)}) collective-permute-start(f32[64,256]{1,0:T(8,128)S(1)} %pack.1.refs_0_), channel_id=1, source_target_pairs={{0,4},{1,5},{2,6},{3,7},{4,0},{5,1},{6,2},{7,3},{8,12},{9,13},{10,... | collective-permute-start | bytes 196616 | tf_op jit(solution)/shard_map/ppermute | solution.py:29
  41.6 5.2 %collective-permute-start.19 = (f32[64,256]{1,0:T(8,128)S(1)}, f32[64,256]{1,0:T(8,128)S(1)}, u32[]{:S(2)}, u32[]{:S(2)}) collective-permute-start(f32[64,256]{1,0:T(8,128)S(1)} %pack.1.refs_0_), channel_id=1, source_target_pairs={{0,6},{1,7},{2,4},{3,5},{4,2},{5,3},{6,0},{7,1},{8,14},{9,15},{10,... | collective-permute-start | bytes 196616 | tf_op jit(solution)/shard_map/ppermute | solution.py:29
  44.9 1.9 %collective-permute-start.10 = (f32[64,256]{1,0:T(8,128)S(1)}, f32[64,256]{1,0:T(8,128)S(1)}, u32[]{:S(2)}, u32[]{:S(2)}) collective-permute-start(f32[64,256]{1,0:T(8,128)S(1)} %pack.1.refs_0_), channel_id=1, source_target_pairs={{0,1},{1,0},{2,3},{3,2},{4,5},{5,4},{6,7},{7,6},{8,9},{9,8},{10,11... | collective-permute-start | bytes 196616 | tf_op jit(solution)/shard_map/ppermute | solution.py:29
  45.0 1.8 %collective-permute-start.12 = (f32[64,256]{1,0:T(8,128)S(1)}, f32[64,256]{1,0:T(8,128)S(1)}, u32[]{:S(2)}, u32[]{:S(2)}) collective-permute-start(f32[64,256]{1,0:T(8,128)S(1)} %collective-permute-done.11.refs_2_), channel_id=1, source_target_pairs={{0,1},{1,0},{2,3},{3,2},{4,5},{5,4},{6,7},{7,6},{8,9},{9,8},{10,11... | collective-permute-start | bytes 196616 | tf_op jit(solution)/shard_map/ppermute | solution.py:29
  45.5 1.3 %collective-permute-start.14 = (f32[64,256]{1,0:T(8,128)S(1)}, f32[64,256]{1,0:T(8,128)S(1)}, u32[]{:S(2)}, u32[]{:S(2)}) collective-permute-start(f32[64,256]{1,0:T(8,128)S(1)} %collective-permute-done.13.refs_4_), channel_id=1, source_target_pairs={{0,1},{1,0},{2,3},{3,2},{4,5},{5,4},{6,7},{7,6},{8,9},{9,8},{10,11... | collective-permute-start | bytes 196616 | tf_op jit(solution)/shard_map/ppermute | solution.py:29
  46.8 1.3 %collective-permute-start.20 = (f32[64,256]{1,0:T(8,128)S(1)}, f32[64,256]{1,0:T(8,128)S(1)}, u32[]{:S(2)}, u32[]{:S(2)}) collective-permute-start(f32[64,256]{1,0:T(8,128)S(1)} %relay.1.refs_6_), channel_id=1, source_target_pairs={{0,1},{1,0},{2,3},{3,2},{4,5},{5,4},{6,7},{7,6},{8,9},{9,8},{10,11... | collective-permute-start | bytes 196616 | tf_op jit(solution)/shard_map/ppermute | solution.py:29

commit v11 on v10

--- a/solution.py
+++ b/solution.py
@@ -53,8 +53,8 @@
             pltpu.make_async_copy(left_ref.at[:levels - 1, rows], left_buf.at[:, rows], sems.at[1, step]),
             pltpu.make_async_copy(inv_ref.at[blocks], inv_buf.at[blocks], sems.at[2, step]),
         ))
-        for copy in copies[-1]:
-            copy.start()
+        for index, copy in enumerate(copies[-1]):
+            copy.start(priority=(step + (index > 0)) % 2)
         if step == 0:
             order_copy.start()
     gram_ref[...] = jnp.zeros_like(gram_ref)
@@ -316,7 +316,7 @@
         functools.partial(weigh_kernel, blocks_per_step(nblocks, 9), width),
         out_shape=jax.ShapeDtypeStruct((2 * kinds, rows), jnp.bfloat16),
         name="weigh",
-        **settings(8, 2.4),
+        **settings(8, 0.3),
     )(moved, flipped, gram)
 
     def project(other, after):

time: 52.8 us -> 52.2 us (0.989)
  Pallas kernels: 25.1 us -> 24.5 us
    pallas_call x1, Pallas kernels: 7 us -> 6.41 us  [per_device(): pl.pallas_call(functools.partial(gram_kernel, levels, per_step, width), i...]
where the time goes in v11:
time: 52.2 us; the launch traced here: 52.1 us
  Pallas kernels  24.5 us (47%)
  starting transfers between devices  20.6 us (39%)
  waiting for transfers between devices  5.83 us (11%)
  local copies, waits for them, and re-layouts  0.74 us (1%)
    ppermute x21, starting transfers between devices, swap(): return lax.ppermute(value, axis, [(i, i ^ mask) for i in range(count)])  20.6 us
    pallas_call x1, Pallas kernels, per_device(): pl.pallas_call(functools.partial(gram_kernel, levels, per_step, width), i...  6.41 us
    ppermute x21, waiting for transfers between devices, swap(): return lax.ppermute(value, axis, [(i, i ^ mask) for i in range(count)])  5.83 us
    pallas_call x1, Pallas kernels, per_device(): pl.pallas_call(functools.partial(expand_kernel, levels, per_step * width,...  4.5 us
    pallas_call x2, Pallas kernels, project(): pl.pallas_call(functools.partial(project_kernel, other), out_shape=floats...  3.98 us
    pallas_call x1, Pallas kernels, per_device(): pl.pallas_call(functools.partial(solve_kernel, per_step, width), out_shap...  2.22 us
    pallas_call x1, Pallas kernels, per_device(): pl.pallas_call(functools.partial(prepare_kernel, levels), in_specs=[pl.Bl...  2.11 us
    pallas_call x1, Pallas kernels, per_device(): pl.pallas_call(functools.partial(weigh_kernel, blocks_per_step(nblocks, 9...  1.6 us
  transfers between devices with their start and end apart: 21, of which 4 were waited for; matrix products, arithmetic and copies ran while one was open for 0% of the time, Pallas kernels for 25%

profile of v11, /device:TPU:0, one launch (start us, length us, event | category | flops | bytes accessed | tf_op | source)
XLA Modules:
  0.0 52.1 jit_solution(16338076800465099706)
XLA Ops:
  0.0 6.4 %gram.1 = (bf16[18,256,256]{2,1,0:T(8,128)(2,1)S(1)}, bf16[384,4608]{1,0:T(8,128)(2,1)S(1)}, f32[128,384]{1,0:T(8,128)S(1)}) custom-call(s32[18,256]{1,0:T(8,128)} %order_ref.1, bf16[18,256,256]{2,1,0:T(8,128)(2,1)} %inv_ref.1, bf16[3,4608,128]{2,1,0:T(8,128)(2,1)} %right_ref.1, bf16[3,4608,128]{2,1,0:T(8,128)(2,1)} %refs_9_.1), custom_call_target="tpu_custom_call" | custom-call | flops 4400000000 | tf_op jit(solution)/shard_map/gram/pallas_call | solution.py:289
  6.4 3.0 %collective-permute-start = (f32[128,384]{1,0:T(8,128)S(1)}, f32[128,384]{1,0:T(8,128)S(1)}, u32[]{:S(2)}, u32[]{:S(2)}) collective-permute-start(f32[128,384]{1,0:T(8,128)S(1)} %get-tuple-element.19.after_ref.mine_ref), channel_id=1, source_target_pairs={{0,2},{1,3},{2,0},{3,1},{4,6},{5,7},{6,4},{7,5},{8,10},{9,11},{10,... | collective-permute-start | bytes 589832 | tf_op jit(solution)/shard_map/ppermute | solution.py:29
  9.4 0.0 copy-start.1
  9.4 1.6 %weigh.1.factor_ref = bf16[768,4608]{1,0:T(8,128)(2,1)S(1)} custom-call(bf16[18,256,256]{2,1,0:T(8,128)(2,1)S(1)} %get-tuple-element.17.moved_ref, bf16[384,4608]{1,0:T(8,128)(2,1)S(1)} %get-tuple-element.18.flip_ref, f32[128,384]{1,0:T(8,128)S(1)} %get-tuple-element.19.after_ref.mine_ref), custom_call_target="tpu_custom_call" | custom-call | flops 330000000 | tf_op jit(solution)/shard_map/weigh/pallas_call | solution.py:315
  11.0 0.7 %copy-done.1 = bf16[4608,512]{1,0:T(8,128)(2,1)S(1)} copy-done((bf16[4608,512]{1,0:T(8,128)(2,1)S(1)}, bf16[4608,512]{1,0:T(8,128)(2,1)}, u32[]{:S(2)}) %copy-start.1) | copy-done | bytes 4718616
  11.8 2.0 %project_other.1 = f32[384,256]{1,0:T(8,128)S(1)} custom-call(bf16[768,4608]{1,0:T(8,128)(2,1)S(1)} %weigh.1.factor_ref, bf16[4608,512]{1,0:T(8,128)(2,1)S(1)} %copy-done.1, f32[128,384]{1,0:T(8,128)S(1)} %get-tuple-element.19.after_ref.mine_ref), custom_call_target="tpu_custom_call" | custom-call | flops 1100000000 | tf_op jit(solution)/shard_map/project_other/pallas_call | solution.py:323
  13.8 0.1 collective-permute-start.1
  13.8 0.5 collective-permute-done.got_ref
  14.4 0.0 copy-start.2
  14.4 1.8 %collective-permute-start.5 = (f32[128,384]{1,0:T(8,128)S(1)}, f32[128,384]{1,0:T(8,128)S(1)}, u32[]{:S(2)}, u32[]{:S(2)}) collective-permute-start(f32[128,384]{1,0:T(8,128)S(1)} %add.1.after_ref.mine_ref), channel_id=1, source_target_pairs={{0,4},{1,5},{2,6},{3,7},{4,0},{5,1},{6,2},{7,3},{8,12},{9,13},{10,... | collective-permute-start | bytes 589832 | tf_op jit(solution)/shard_map/ppermute | solution.py:29
  16.2 2.0 %project_own.1.keep_ref = f32[384,256]{1,0:T(8,128)S(1)} custom-call(bf16[768,4608]{1,0:T(8,128)(2,1)S(1)} %weigh.1.factor_ref, bf16[4608,512]{1,0:T(8,128)(2,1)S(1)} %copy-done.1, f32[128,384]{1,0:T(8,128)S(1)} %add.1.after_ref.mine_ref), custom_call_target="tpu_custom_call" | custom-call | flops 8800000000 | tf_op jit(solution)/shard_map/project_own/pallas_call | solution.py:323
  18.2 0.1 collective-permute-start.6
  18.3 0.0 collective-permute-done.1.got_ref
  18.3 0.2 merge.1
  18.5 1.6 %collective-permute-start.2 = (f32[64,384]{1,0:T(8,128)S(1)}, f32[64,384]{1,0:T(8,128)S(1)}, u32[]{:S(2)}, u32[]{:S(2)}) collective-permute-start(f32[64,384]{1,0:T(8,128)S(1)} %get-tuple-element.21), channel_id=1, source_target_pairs={{0,2},{1,3},{2,0},{3,1},{4,6},{5,7},{6,4},{7,5},{8,10},{9,11},{10,... | collective-permute-start | bytes 294920 | tf_op jit(solution)/shard_map/ppermute | solution.py:29
  20.0 0.5 collective-permute-start.3
  20.5 1.5 %collective-permute-start.4 = (f32[64,384]{1,0:T(8,128)S(1)}, f32[64,384]{1,0:T(8,128)S(1)}, u32[]{:S(2)}, u32[]{:S(2)}) collective-permute-start(f32[64,384]{1,0:T(8,128)S(1)} %get-tuple-element.23), channel_id=1, source_target_pairs={{0,6},{1,7},{2,4},{3,5},{4,2},{5,3},{6,0},{7,1},{8,14},{9,15},{10,... | collective-permute-start | bytes 294920 | tf_op jit(solution)/shard_map/ppermute | solution.py:29
  22.0 0.0 collective-permute-done.5.theirs_ref
  22.0 0.0 collective-permute-start.7
  22.0 0.0 copy-done.2
  22.1 2.1 %prepare.1.refs_4_.joined_ref = f32[3,256,256]{2,1,0:T(8,128)S(1)} custom-call(f32[7,256,256]{2,1,0:T(8,128)} %joined_ref.1, s32[3,128]{1,0:T(4,128)S(1)} %copy-done.2), custom_call_target="tpu_custom_call" | custom-call | flops 2200000000 | tf_op jit(solution)/shard_map/prepare/pallas_call | solution.py:347
  24.2 0.0 collective-permute-done.2.refs_1_
  24.2 2.9 %collective-permute-done.3.refs_2_ = f32[64,384]{1,0:T(8,128)S(1)} collective-permute-done((f32[64,384]{1,0:T(8,128)S(1)}, f32[64,384]{1,0:T(8,128)S(1)}, u32[]{:S(2)}, u32[]{:S(2)}) %collective-permute-start.3) | collective-permute-done | bytes 98336 | tf_op jit(solution)/shard_map/ppermute | solution.py:29
  27.1 0.0 collective-permute-done.4.refs_3_
  27.1 0.4 node.1
  27.4 0.0 collective-permute-done.6.pair_mine_ref
  27.4 0.0 collective-permute-done.7.pair_theirs_ref
  27.5 0.4 correct.1.sent_ref
  27.8 1.6 %collective-permute-start.8 = (f32[256,128]{1,0:T(8,128)S(1)}, f32[256,128]{1,0:T(8,128)S(1)}, u32[]{:S(2)}, u32[]{:S(2)}) collective-permute-start(f32[256,128]{1,0:T(8,128)S(1)} %correct.1.sent_ref), channel_id=1, source_target_pairs={{0,8},{8,0},{16,24},{24,16},{1,9},{9,1},{17,25},{25,17},{2,10},{10... | collective-permute-start | bytes 393224 | tf_op jit(solution)/shard_map/ppermute | solution.py:29
  29.5 0.5 %collective-permute-start.15 = (f32[64,128]{1,0:T(8,128)S(1)}, f32[64,128]{1,0:T(8,128)S(1)}, u32[]{:S(2)}, u32[]{:S(2)}) collective-permute-start(f32[64,128]{1,0:T(8,128)S(1)} %get-tuple-element.24.own_ref.refs_0_), channel_id=1, source_target_pairs={{0,2},{1,3},{2,0},{3,1},{4,6},{5,7},{6,4},{7,5},{8,10},{9,11},{10,... | collective-permute-start | bytes 98312 | tf_op jit(solution)/shard_map/ppermute | solution.py:29
  30.0 1.2 %collective-permute-start.16 = (f32[64,128]{1,0:T(8,128)S(1)}, f32[64,128]{1,0:T(8,128)S(1)}, u32[]{:S(2)}, u32[]{:S(2)}) collective-permute-start(f32[64,128]{1,0:T(8,128)S(1)} %get-tuple-element.25.other_ref), channel_id=1, source_target_pairs={{0,4},{1,5},{2,6},{3,7},{4,0},{5,1},{6,2},{7,3},{8,12},{9,13},{10,... | collective-permute-start | bytes 98312 | tf_op jit(solution)/shard_map/ppermute | solution.py:29
  31.2 1.7 %collective-permute-start.17 = (f32[64,128]{1,0:T(8,128)S(1)}, f32[64,128]{1,0:T(8,128)S(1)}, u32[]{:S(2)}, u32[]{:S(2)}) collective-permute-start(f32[64,128]{1,0:T(8,128)S(1)} %get-tuple-element.25.other_ref), channel_id=1, source_target_pairs={{0,6},{1,7},{2,4},{3,5},{4,2},{5,3},{6,0},{7,1},{8,14},{9,15},{10,... | collective-permute-start | bytes 98312 | tf_op jit(solution)/shard_map/ppermute | solution.py:29
  33.0 0.0 collective-permute-done.8.got_ref.after_ref
  33.0 0.8 %level1.1 = (f32[64,128]{1,0:T(8,128)S(1)}, f32[64,128]{1,0:T(8,128)S(1)}) custom-call(f32[256,128]{1,0:T(8,128)S(1)} %correct.1.sent_ref, f32[256,128]{1,0:T(8,128)S(1)} %collective-permute-done.8.got_ref.after_ref, f32[3,256,256]{2,1,0:T(8,128)S(1)} %prepare.1.refs_4_.joined_ref, f32[256,128]{1,0:T(8,128)S(1)} %collective-permute-done.8.got_ref.after_ref), custom_call_target="tpu_custom_call" | custom-call | flops 6600000000 | tf_op jit(solution)/shard_map/level1/pallas_call | solution.py:383
  33.7 2.6 %collective-permute-start.9 = (f32[64,128]{1,0:T(8,128)S(1)}, f32[64,128]{1,0:T(8,128)S(1)}, u32[]{:S(2)}, u32[]{:S(2)}) collective-permute-start(f32[64,128]{1,0:T(8,128)S(1)} %get-tuple-element.28.sent_ref), channel_id=1, source_target_pairs={{0,16},{8,24},{16,0},{24,8},{1,17},{9,25},{17,1},{25,9},{2,18},{10... | collective-permute-start | bytes 98312 | tf_op jit(solution)/shard_map/ppermute | solution.py:29
  36.4 2.2 %solve.1.after_ref.first_ref = f32[4608,512]{1,0:T(8,128)S(1)} custom-call(bf16[18,256,256]{2,1,0:T(8,128)(2,1)S(1)} %get-tuple-element.17.moved_ref, bf16[4608,512]{1,0:T(8,128)(2,1)S(1)} %copy-done.1, f32[64,384]{1,0:T(8,128)S(1)} %get-tuple-element.20.refs_0_), custom_call_target="tpu_custom_call" | custom-call | flops 8800000000 | tf_op jit(solution)/shard_map/solve/pallas_call | solution.py:372
  38.6 0.0 collective-permute-done.15.refs_1_
  38.6 0.0 collective-permute-done.16.refs_2_
  38.6 0.0 collective-permute-done.17.refs_3_
  38.7 0.0 copy-start
  38.7 0.1 collective-permute-start.18
  38.7 0.0 collective-permute-done.9.got_ref
  38.8 0.4 level2.1.refs_1_
  39.1 0.6 %collective-permute-start.11 = (f32[64,256]{1,0:T(8,128)S(1)}, f32[64,256]{1,0:T(8,128)S(1)}, u32[]{:S(2)}, u32[]{:S(2)}) collective-permute-start(f32[64,256]{1,0:T(8,128)S(1)} %pack.1.refs_0_), channel_id=1, source_target_pairs={{0,2},{1,3},{2,0},{3,1},{4,6},{5,7},{6,4},{7,5},{8,10},{9,11},{10,... | collective-permute-start | bytes 196616 | tf_op jit(solution)/shard_map/ppermute | solution.py:29
  39.7 1.2 %collective-permute-start.13 = (f32[64,256]{1,0:T(8,128)S(1)}, f32[64,256]{1,0:T(8,128)S(1)}, u32[]{:S(2)}, u32[]{:S(2)}) collective-permute-start(f32[64,256]{1,0:T(8,128)S(1)} %pack.1.refs_0_), channel_id=1, source_target_pairs={{0,4},{1,5},{2,6},{3,7},{4,0},{5,1},{6,2},{7,3},{8,12},{9,13},{10,... | collective-permute-start | bytes 196616 | tf_op jit(solution)/shard_map/ppermute | solution.py:29
  41.0 1.7 %collective-permute-start.19 = (f32[64,256]{1,0:T(8,128)S(1)}, f32[64,256]{1,0:T(8,128)S(1)}, u32[]{:S(2)}, u32[]{:S(2)}) collective-permute-start(f32[64,256]{1,0:T(8,128)S(1)} %pack.1.refs_0_), channel_id=1, source_target_pairs={{0,6},{1,7},{2,4},{3,5},{4,2},{5,3},{6,0},{7,1},{8,14},{9,15},{10,... | collective-permute-start | bytes 196616 | tf_op jit(solution)/shard_map/ppermute | solution.py:29
  42.7 0.0 collective-permute-done.18.pair_ref
  42.7 0.0 copy-done
  42.7 1.6 %apply.1.after_ref.refs_8_ = f32[4608,512]{1,0:T(8,128)S(1)} custom-call(f32[4,64,128]{2,1,0:T(8,128)S(1)} %stack.1.own_ref, f32[4,64,128]{2,1,0:T(8,128)S(1)} %collective-permute-done.18.pair_ref, f32[4608,512]{1,0:T(8,128)S(1)} %solve.1.after_ref.first_ref, bf16[3,4608,128]{2,1,0:T(8,128)(2,1)S(1)} %copy-done), custom_call_target="tpu_custom_call" | custom-call | flops 1980000000 | tf_op jit(solution)/shard_map/apply/pallas_call | solution.py:394
  44.3 0.1 collective-permute-start.10
  44.4 0.0 collective-permute-done.11.refs_2_
  44.4 0.5 collective-permute-start.12
  44.9 0.0 collective-permute-done.13.refs_4_
  44.9 0.1 collective-permute-start.14
  45.0 1.2 %collective-permute-done.19.ref = f32[64,256]{1,0:T(8,128)S(1)} collective-permute-done((f32[64,256]{1,0:T(8,128)S(1)}, f32[64,256]{1,0:T(8,128)S(1)}, u32[]{:S(2)}, u32[]{:S(2)}) %collective-permute-start.19) | collective-permute-done | bytes 65568 | tf_op jit(solution)/shard_map/ppermute | solution.py:29
  46.2 0.0 collective-permute-start.20
  46.2 0.0 collective-permute-done.10.refs_1_
  46.2 0.0 collective-permute-done.12.refs_3_
  46.2 0.0 collective-permute-done.14.refs_5_
  46.2 1.2 %collective-permute-done.20.refs_7_ = f32[64,256]{1,0:T(8,128)S(1)} collective-permute-done((f32[64,256]{1,0:T(8,128)S(1)}, f32[64,256]{1,0:T(8,128)S(1)}, u32[]{:S(2)}, u32[]{:S(2)}) %collective-permute-start.20) | collective-permute-done | bytes 65568 | tf_op jit(solution)/shard_map/ppermute | solution.py:29
  47.4 4.5 %expand.1 = f32[4608,512]{1,0:T(8,128)} custom-call(f32[64,256]{1,0:T(8,128)S(1)} %pack.1.refs_0_, f32[64,256]{1,0:T(8,128)S(1)} %collective-permute-done.10.refs_1_, f32[64,256]{1,0:T(8,128)S(1)} %collective-permute-done.11.refs_2_, f32[64,256]{1,0:T(8,128)S(1)} %collective-permute-done.12.refs_3_, f32[64,256]{1,0:T(8,128)S(1)} %collective-permute-done.13.refs_4_, ...), custom_call_target="tpu_custom_call" | custom-call | flops 5500000256 | tf_op jit(solution)/shard_map/expand/pallas_call | solution.py:416
  (4 shorter events, 0.0 us)
Async XLA Ops:
  6.4 7.9 %collective-permute-start = (f32[128,384]{1,0:T(8,128)S(1)}, f32[128,384]{1,0:T(8,128)S(1)}, u32[]{:S(2)}, u32[]{:S(2)}) collective-permute-start(f32[128,384]{1,0:T(8,128)S(1)} %get-tuple-element.19.after_ref.mine_ref), channel_id=1, source_target_pairs={{0,2},{1,3},{2,0},{3,1},{4,6},{5,7},{6,4},{7,5},{8,10},{9,11},{10,... | collective-permute-start | bytes 589832 | tf_op jit(solution)/shard_map/ppermute | solution.py:29
  9.4 2.3 %copy-start.1 = (bf16[4608,512]{1,0:T(8,128)(2,1)S(1)}, bf16[4608,512]{1,0:T(8,128)(2,1)}, u32[]{:S(2)}) copy-start(bf16[4608,512]{1,0:T(8,128)(2,1)} %rhs_ref.5) | copy-start | bytes 14155780
  13.8 4.5 %collective-permute-start.1 = (f32[384,256]{1,0:T(8,128)S(1)}, f32[384,256]{1,0:T(8,128)S(1)}, u32[]{:S(2)}, u32[]{:S(2)}) collective-permute-start(f32[384,256]{1,0:T(8,128)S(1)} %project_other.1), channel_id=1, source_target_pairs={{0,1},{1,0},{2,3},{3,2},{4,5},{5,4},{6,7},{7,6},{8,9},{9,8},{10,11... | collective-permute-start | bytes 1179656 | tf_op jit(solution)/shard_map/ppermute | solution.py:29
  14.4 7.7 %copy-start.2 = (s32[3,128]{1,0:T(4,128)S(1)}, s32[3,128]{1,0:T(4,128)}, u32[]{:S(2)}) copy-start(s32[3,128]{1,0:T(4,128)} %perm_ref.1) | copy-start | bytes 4612
  14.4 7.7 %collective-permute-start.5 = (f32[128,384]{1,0:T(8,128)S(1)}, f32[128,384]{1,0:T(8,128)S(1)}, u32[]{:S(2)}, u32[]{:S(2)}) collective-permute-start(f32[128,384]{1,0:T(8,128)S(1)} %add.1.after_ref.mine_ref), channel_id=1, source_target_pairs={{0,4},{1,5},{2,6},{3,7},{4,0},{5,1},{6,2},{7,3},{8,12},{9,13},{10,... | collective-permute-start | bytes 589832 | tf_op jit(solution)/shard_map/ppermute | solution.py:29
  18.2 9.2 %collective-permute-start.6 = (f32[128,384]{1,0:T(8,128)S(1)}, f32[128,384]{1,0:T(8,128)S(1)}, u32[]{:S(2)}, u32[]{:S(2)}) collective-permute-start(f32[128,384]{1,0:T(8,128)S(1)} %add.1.after_ref.mine_ref), channel_id=1, source_target_pairs={{0,1},{1,0},{2,3},{3,2},{4,5},{5,4},{6,7},{7,6},{8,9},{9,8},{10,11... | collective-permute-start | bytes 589832 | tf_op jit(solution)/shard_map/ppermute | solution.py:29
  18.5 5.7 %collective-permute-start.2 = (f32[64,384]{1,0:T(8,128)S(1)}, f32[64,384]{1,0:T(8,128)S(1)}, u32[]{:S(2)}, u32[]{:S(2)}) collective-permute-start(f32[64,384]{1,0:T(8,128)S(1)} %get-tuple-element.21), channel_id=1, source_target_pairs={{0,2},{1,3},{2,0},{3,1},{4,6},{5,7},{6,4},{7,5},{8,10},{9,11},{10,... | collective-permute-start | bytes 294920 | tf_op jit(solution)/shard_map/ppermute | solution.py:29
  20.0 7.0 %collective-permute-start.3 = (f32[64,384]{1,0:T(8,128)S(1)}, f32[64,384]{1,0:T(8,128)S(1)}, u32[]{:S(2)}, u32[]{:S(2)}) collective-permute-start(f32[64,384]{1,0:T(8,128)S(1)} %get-tuple-element.22), channel_id=1, source_target_pairs={{0,4},{1,5},{2,6},{3,7},{4,0},{5,1},{6,2},{7,3},{8,12},{9,13},{10,... | collective-permute-start | bytes 294920 | tf_op jit(solution)/shard_map/ppermute | solution.py:29
  20.5 6.5 %collective-permute-start.4 = (f32[64,384]{1,0:T(8,128)S(1)}, f32[64,384]{1,0:T(8,128)S(1)}, u32[]{:S(2)}, u32[]{:S(2)}) collective-permute-start(f32[64,384]{1,0:T(8,128)S(1)} %get-tuple-element.23), channel_id=1, source_target_pairs={{0,6},{1,7},{2,4},{3,5},{4,2},{5,3},{6,0},{7,1},{8,14},{9,15},{10,... | collective-permute-start | bytes 294920 | tf_op jit(solution)/shard_map/ppermute | solution.py:29
  22.0 5.4 %collective-permute-start.7 = (f32[128,384]{1,0:T(8,128)S(1)}, f32[128,384]{1,0:T(8,128)S(1)}, u32[]{:S(2)}, u32[]{:S(2)}) collective-permute-start(f32[128,384]{1,0:T(8,128)S(1)} %collective-permute-done.5.theirs_ref), channel_id=1, source_target_pairs={{0,1},{1,0},{2,3},{3,2},{4,5},{5,4},{6,7},{7,6},{8,9},{9,8},{10,11... | collective-permute-start | bytes 589832 | tf_op jit(solution)/shard_map/ppermute | solution.py:29
  27.8 5.1 %collective-permute-start.8 = (f32[256,128]{1,0:T(8,128)S(1)}, f32[256,128]{1,0:T(8,128)S(1)}, u32[]{:S(2)}, u32[]{:S(2)}) collective-permute-start(f32[256,128]{1,0:T(8,128)S(1)} %correct.1.sent_ref), channel_id=1, source_target_pairs={{0,8},{8,0},{16,24},{24,16},{1,9},{9,1},{17,25},{25,17},{2,10},{10... | collective-permute-start | bytes 393224 | tf_op jit(solution)/shard_map/ppermute | solution.py:29
  29.5 9.1 %collective-permute-start.15 = (f32[64,128]{1,0:T(8,128)S(1)}, f32[64,128]{1,0:T(8,128)S(1)}, u32[]{:S(2)}, u32[]{:S(2)}) collective-permute-start(f32[64,128]{1,0:T(8,128)S(1)} %get-tuple-element.24.own_ref.refs_0_), channel_id=1, source_target_pairs={{0,2},{1,3},{2,0},{3,1},{4,6},{5,7},{6,4},{7,5},{8,10},{9,11},{10,... | collective-permute-start | bytes 98312 | tf_op jit(solution)/shard_map/ppermute | solution.py:29
  30.0 8.6 %collective-permute-start.16 = (f32[64,128]{1,0:T(8,128)S(1)}, f32[64,128]{1,0:T(8,128)S(1)}, u32[]{:S(2)}, u32[]{:S(2)}) collective-permute-start(f32[64,128]{1,0:T(8,128)S(1)} %get-tuple-element.25.other_ref), channel_id=1, source_target_pairs={{0,4},{1,5},{2,6},{3,7},{4,0},{5,1},{6,2},{7,3},{8,12},{9,13},{10,... | collective-permute-start | bytes 98312 | tf_op jit(solution)/shard_map/ppermute | solution.py:29
  31.2 7.4 %collective-permute-start.17 = (f32[64,128]{1,0:T(8,128)S(1)}, f32[64,128]{1,0:T(8,128)S(1)}, u32[]{:S(2)}, u32[]{:S(2)}) collective-permute-start(f32[64,128]{1,0:T(8,128)S(1)} %get-tuple-element.25.other_ref), channel_id=1, source_target_pairs={{0,6},{1,7},{2,4},{3,5},{4,2},{5,3},{6,0},{7,1},{8,14},{9,15},{10,... | collective-permute-start | bytes 98312 | tf_op jit(solution)/shard_map/ppermute | solution.py:29
  33.7 5.0 %collective-permute-start.9 = (f32[64,128]{1,0:T(8,128)S(1)}, f32[64,128]{1,0:T(8,128)S(1)}, u32[]{:S(2)}, u32[]{:S(2)}) collective-permute-start(f32[64,128]{1,0:T(8,128)S(1)} %get-tuple-element.28.sent_ref), channel_id=1, source_target_pairs={{0,16},{8,24},{16,0},{24,8},{1,17},{9,25},{17,1},{25,9},{2,18},{10... | collective-permute-start | bytes 98312 | tf_op jit(solution)/shard_map/ppermute | solution.py:29
  38.7 4.0 %copy-start = (bf16[3,4608,128]{2,1,0:T(8,128)(2,1)S(1)}, bf16[3,4608,128]{2,1,0:T(8,128)(2,1)}, u32[]{:S(2)}) copy-start(bf16[3,4608,128]{2,1,0:T(8,128)(2,1)} %refs_9_.1) | copy-start | bytes 10616836
  38.7 4.0 %collective-permute-start.18 = (f32[4,64,128]{2,1,0:T(8,128)S(1)}, f32[4,64,128]{2,1,0:T(8,128)S(1)}, u32[]{:S(2)}, u32[]{:S(2)}) collective-permute-start(f32[4,64,128]{2,1,0:T(8,128)S(1)} %stack.1.own_ref), channel_id=1, source_target_pairs={{0,1},{1,0},{2,3},{3,2},{4,5},{5,4},{6,7},{7,6},{8,9},{9,8},{10,11... | collective-permute-start | bytes 393224 | tf_op jit(solution)/shard_map/ppermute | solution.py:29
  39.1 5.2 %collective-permute-start.11 = (f32[64,256]{1,0:T(8,128)S(1)}, f32[64,256]{1,0:T(8,128)S(1)}, u32[]{:S(2)}, u32[]{:S(2)}) collective-permute-start(f32[64,256]{1,0:T(8,128)S(1)} %pack.1.refs_0_), channel_id=1, source_target_pairs={{0,2},{1,3},{2,0},{3,1},{4,6},{5,7},{6,4},{7,5},{8,10},{9,11},{10,... | collective-permute-start | bytes 196616 | tf_op jit(solution)/shard_map/ppermute | solution.py:29
  39.7 5.1 %collective-permute-start.13 = (f32[64,256]{1,0:T(8,128)S(1)}, f32[64,256]{1,0:T(8,128)S(1)}, u32[]{:S(2)}, u32[]{:S(2)}) collective-permute-start(f32[64,256]{1,0:T(8,128)S(1)} %pack.1.refs_0_), channel_id=1, source_target_pairs={{0,4},{1,5},{2,6},{3,7},{4,0},{5,1},{6,2},{7,3},{8,12},{9,13},{10,... | collective-permute-start | bytes 196616 | tf_op jit(solution)/shard_map/ppermute | solution.py:29
  41.0 5.2 %collective-permute-start.19 = (f32[64,256]{1,0:T(8,128)S(1)}, f32[64,256]{1,0:T(8,128)S(1)}, u32[]{:S(2)}, u32[]{:S(2)}) collective-permute-start(f32[64,256]{1,0:T(8,128)S(1)} %pack.1.refs_0_), channel_id=1, source_target_pairs={{0,6},{1,7},{2,4},{3,5},{4,2},{5,3},{6,0},{7,1},{8,14},{9,15},{10,... | collective-permute-start | bytes 196616 | tf_op jit(solution)/shard_map/ppermute | solution.py:29
  44.3 1.9 %collective-permute-start.10 = (f32[64,256]{1,0:T(8,128)S(1)}, f32[64,256]{1,0:T(8,128)S(1)}, u32[]{:S(2)}, u32[]{:S(2)}) collective-permute-start(f32[64,256]{1,0:T(8,128)S(1)} %pack.1.refs_0_), channel_id=1, source_target_pairs={{0,1},{1,0},{2,3},{3,2},{4,5},{5,4},{6,7},{7,6},{8,9},{9,8},{10,11... | collective-permute-start | bytes 196616 | tf_op jit(solution)/shard_map/ppermute | solution.py:29
  44.4 1.8 %collective-permute-start.12 = (f32[64,256]{1,0:T(8,128)S(1)}, f32[64,256]{1,0:T(8,128)S(1)}, u32[]{:S(2)}, u32[]{:S(2)}) collective-permute-start(f32[64,256]{1,0:T(8,128)S(1)} %collective-permute-done.11.refs_2_), channel_id=1, source_target_pairs={{0,1},{1,0},{2,3},{3,2},{4,5},{5,4},{6,7},{7,6},{8,9},{9,8},{10,11... | collective-permute-start | bytes 196616 | tf_op jit(solution)/shard_map/ppermute | solution.py:29
  44.9 1.3 %collective-permute-start.14 = (f32[64,256]{1,0:T(8,128)S(1)}, f32[64,256]{1,0:T(8,128)S(1)}, u32[]{:S(2)}, u32[]{:S(2)}) collective-permute-start(f32[64,256]{1,0:T(8,128)S(1)} %collective-permute-done.13.refs_4_), channel_id=1, source_target_pairs={{0,1},{1,0},{2,3},{3,2},{4,5},{5,4},{6,7},{7,6},{8,9},{9,8},{10,11... | collective-permute-start | bytes 196616 | tf_op jit(solution)/shard_map/ppermute | solution.py:29
  46.2 1.3 %collective-permute-start.20 = (f32[64,256]{1,0:T(8,128)S(1)}, f32[64,256]{1,0:T(8,128)S(1)}, u32[]{:S(2)}, u32[]{:S(2)}) collective-permute-start(f32[64,256]{1,0:T(8,128)S(1)} %relay.1.refs_6_), channel_id=1, source_target_pairs={{0,1},{1,0},{2,3},{3,2},{4,5},{5,4},{6,7},{7,6},{8,9},{9,8},{10,11... | collective-permute-start | bytes 196616 | tf_op jit(solution)/shard_map/ppermute | solution.py:29

commit v12 on v8

--- a/solution.py
+++ b/solution.py
@@ -227,6 +227,10 @@
         refs[-1][slot] = ref[...]
 
 
+def relay_kernel(after_ref, ref, out_ref):
+    out_ref[...] = ref[...]
+
+
 def split_factor(pieces, flip_ref, factor_ref):
     share, kinds = pieces[0].shape
     slots = len(pieces) // 2
@@ -304,7 +308,7 @@
       pltpu.with_memory_space_constraint(left_basis, pltpu.HBM))
 
     moved = pl.pallas_call(
-        functools.partial(permute_kernel, blocks_per_step(nblocks, 6), width),
+        functools.partial(permute_kernel, blocks_per_step(nblocks, 9), width),
         out_shape=jax.ShapeDtypeStruct((nblocks, width, width), jnp.bfloat16),
         name="permute",
         **settings(8, 1.5),
@@ -316,7 +320,7 @@
         )(mine, got)
 
     factors = pl.pallas_call(
-        functools.partial(weigh_kernel, per_step, width),
+        functools.partial(weigh_kernel, blocks_per_step(nblocks, 9), width),
         out_shape=jax.ShapeDtypeStruct((2 * kinds, rows), jnp.bfloat16),
         name="weigh",
         **settings(8, 2.4),
@@ -411,6 +415,10 @@
     pieces = []
     for slot in range(slots):
         piece = swap(pack, "rows", 2 * slot) if slot > 0 else pack
+        if slot == slots - 1:
+            piece = pl.pallas_call(
+                relay_kernel, out_shape=floats(share, size), name="relay", **settings(8, 0.1),
+            )(second, piece)
         pieces += [piece, swap(piece, "rows", 1)]
     return pl.pallas_call(
         functools.partial(expand_kernel, levels, per_step * width, count),

time: 49.5 us -> 49 us (0.990)
  Pallas kernels: 23.3 us -> 22.5 us
    pallas_call x1 -> x2, Pallas kernels: 2.13 us -> 1.61 us  [the longest x1 1.6 us: per_device(): pl.pallas_call(functools.partial(weigh_kernel, blocks_per_step(nblocks, 9...]
  transfers between devices with their start and end apart: 21 -> 21, of which waited for: 4 -> 4; matrix products, arithmetic and copies ran while one was open for 0% -> 0% of each run, Pallas kernels for 30% -> 29%
where the time goes in v12:
time: 49 us; the launch traced here: 48.9 us
  Pallas kernels  22.5 us (46%)
  starting transfers between devices  20.6 us (42%)
  waiting for transfers between devices  5.44 us (11%)
    ppermute x21, starting transfers between devices, swap(): return lax.ppermute(value, axis, [(i, i ^ mask) for i in range(count)])  20.6 us
    ppermute x21, waiting for transfers between devices, swap(): return lax.ppermute(value, axis, [(i, i ^ mask) for i in range(count)])  5.44 us
    pallas_call x1, Pallas kernels, per_device(): pl.pallas_call(functools.partial(expand_kernel, levels, per_step * width,...  4.5 us
    pallas_call x2, Pallas kernels, project(): pl.pallas_call(functools.partial(project_kernel, other), out_shape=floats...  3.99 us
    pallas_call x1, Pallas kernels, per_device(): pl.pallas_call(functools.partial(gram_kernel, levels, per_step, width), i...  3.34 us
    pallas_call x1, Pallas kernels, per_device(): pl.pallas_call(functools.partial(solve_kernel, per_step, width), out_shap...  2.22 us
    pallas_call x1, Pallas kernels, per_device(): pl.pallas_call(functools.partial(prepare_kernel, levels), in_specs=[pl.Bl...  2.11 us
    pallas_call x1, Pallas kernels, per_device(): pl.pallas_call(functools.partial(weigh_kernel, blocks_per_step(nblocks, 9...  1.6 us
  transfers between devices with their start and end apart: 21, of which 4 were waited for; matrix products, arithmetic and copies ran while one was open for 0% of the time, Pallas kernels for 29%

profile of v12, /device:TPU:0, one launch (start us, length us, event | category | flops | bytes accessed | tf_op | source)
XLA Modules:
  0.0 48.9 jit_solution(6893184730405815453)
XLA Ops:
  0.0 3.3 %gram.1 = (bf16[384,4608]{1,0:T(8,128)(2,1)S(1)}, f32[128,384]{1,0:T(8,128)S(1)}) custom-call(bf16[3,4608,128]{2,1,0:T(8,128)(2,1)} %right_ref.1, bf16[3,4608,128]{2,1,0:T(8,128)(2,1)} %refs_9_.1), custom_call_target="tpu_custom_call" | custom-call | flops 3300000000 | tf_op jit(solution)/shard_map/gram/pallas_call | solution.py:295
  3.3 3.0 %collective-permute-start = (f32[128,384]{1,0:T(8,128)S(1)}, f32[128,384]{1,0:T(8,128)S(1)}, u32[]{:S(2)}, u32[]{:S(2)}) collective-permute-start(f32[128,384]{1,0:T(8,128)S(1)} %get-tuple-element.17.after_ref.mine_ref), channel_id=1, source_target_pairs={{0,2},{1,3},{2,0},{3,1},{4,6},{5,7},{6,4},{7,5},{8,10},{9,11},{10,... | collective-permute-start | bytes 589832 | tf_op jit(solution)/shard_map/ppermute | solution.py:29
  6.4 0.0 copy-done.2
  6.4 0.0 copy-done.1
  6.4 1.0 %permute.1.moved_ref = bf16[18,256,256]{2,1,0:T(8,128)(2,1)S(1)} custom-call(s32[18,256]{1,0:T(8,128)S(1)} %copy-done.2, bf16[18,256,256]{2,1,0:T(8,128)(2,1)S(1)} %copy-done.1), custom_call_target="tpu_custom_call" | custom-call | flops 1650000000 | tf_op jit(solution)/shard_map/permute/pallas_call | solution.py:310
  7.4 0.0 slice-start.1
  7.4 1.6 %weigh.1.factor_ref = bf16[768,4608]{1,0:T(8,128)(2,1)S(1)} custom-call(bf16[18,256,256]{2,1,0:T(8,128)(2,1)S(1)} %permute.1.moved_ref, bf16[384,4608]{1,0:T(8,128)(2,1)S(1)} %get-tuple-element.16.flip_ref, f32[128,384]{1,0:T(8,128)S(1)} %get-tuple-element.17.after_ref.mine_ref), custom_call_target="tpu_custom_call" | custom-call | flops 2640000000 | tf_op jit(solution)/shard_map/weigh/pallas_call | solution.py:322
  9.0 0.0 slice-done
  9.0 0.0 slice-done.1
  9.0 2.0 %project_other.1 = f32[384,256]{1,0:T(8,128)S(1)} custom-call(bf16[768,4608]{1,0:T(8,128)(2,1)S(1)} %weigh.1.factor_ref, bf16[4608,512]{1,0:T(8,128)(2,1)S(1)} %bitcast.1, f32[128,384]{1,0:T(8,128)S(1)} %get-tuple-element.17.after_ref.mine_ref), custom_call_target="tpu_custom_call" | custom-call | flops 1100000000 | tf_op jit(solution)/shard_map/project_other/pallas_call | solution.py:330
  11.1 0.1 collective-permute-start.1
  11.1 0.1 collective-permute-done.got_ref
  11.3 0.0 copy-start.3
  11.3 1.8 %collective-permute-start.5 = (f32[128,384]{1,0:T(8,128)S(1)}, f32[128,384]{1,0:T(8,128)S(1)}, u32[]{:S(2)}, u32[]{:S(2)}) collective-permute-start(f32[128,384]{1,0:T(8,128)S(1)} %add.1.after_ref.mine_ref), channel_id=1, source_target_pairs={{0,4},{1,5},{2,6},{3,7},{4,0},{5,1},{6,2},{7,3},{8,12},{9,13},{10,... | collective-permute-start | bytes 589832 | tf_op jit(solution)/shard_map/ppermute | solution.py:29
  13.1 2.0 %project_own.1.keep_ref = f32[384,256]{1,0:T(8,128)S(1)} custom-call(bf16[768,4608]{1,0:T(8,128)(2,1)S(1)} %weigh.1.factor_ref, bf16[4608,512]{1,0:T(8,128)(2,1)S(1)} %bitcast.1, f32[128,384]{1,0:T(8,128)S(1)} %add.1.after_ref.mine_ref), custom_call_target="tpu_custom_call" | custom-call | flops 8800000000 | tf_op jit(solution)/shard_map/project_own/pallas_call | solution.py:330
  15.1 0.1 collective-permute-start.6
  15.2 0.0 collective-permute-done.1.got_ref
  15.2 0.2 merge.1
  15.4 1.6 %collective-permute-start.2 = (f32[64,384]{1,0:T(8,128)S(1)}, f32[64,384]{1,0:T(8,128)S(1)}, u32[]{:S(2)}, u32[]{:S(2)}) collective-permute-start(f32[64,384]{1,0:T(8,128)S(1)} %get-tuple-element.19), channel_id=1, source_target_pairs={{0,2},{1,3},{2,0},{3,1},{4,6},{5,7},{6,4},{7,5},{8,10},{9,11},{10,... | collective-permute-start | bytes 294920 | tf_op jit(solution)/shard_map/ppermute | solution.py:29
  17.0 0.5 %collective-permute-start.3 = (f32[64,384]{1,0:T(8,128)S(1)}, f32[64,384]{1,0:T(8,128)S(1)}, u32[]{:S(2)}, u32[]{:S(2)}) collective-permute-start(f32[64,384]{1,0:T(8,128)S(1)} %get-tuple-element.20), channel_id=1, source_target_pairs={{0,4},{1,5},{2,6},{3,7},{4,0},{5,1},{6,2},{7,3},{8,12},{9,13},{10,... | collective-permute-start | bytes 294920 | tf_op jit(solution)/shard_map/ppermute | solution.py:29
  17.5 1.5 %collective-permute-start.4 = (f32[64,384]{1,0:T(8,128)S(1)}, f32[64,384]{1,0:T(8,128)S(1)}, u32[]{:S(2)}, u32[]{:S(2)}) collective-permute-start(f32[64,384]{1,0:T(8,128)S(1)} %get-tuple-element.21), channel_id=1, source_target_pairs={{0,6},{1,7},{2,4},{3,5},{4,2},{5,3},{6,0},{7,1},{8,14},{9,15},{10,... | collective-permute-start | bytes 294920 | tf_op jit(solution)/shard_map/ppermute | solution.py:29
  19.0 0.0 collective-permute-done.5.theirs_ref
  19.0 0.0 collective-permute-start.7
  19.0 0.0 copy-done.3
  19.0 2.1 %prepare.1.refs_4_.joined_ref = f32[3,256,256]{2,1,0:T(8,128)S(1)} custom-call(f32[7,256,256]{2,1,0:T(8,128)} %joined_ref.1, s32[3,128]{1,0:T(4,128)S(1)} %copy-done.3), custom_call_target="tpu_custom_call" | custom-call | flops 2200000000 | tf_op jit(solution)/shard_map/prepare/pallas_call | solution.py:354
  21.1 0.0 collective-permute-done.2.refs_1_
  21.1 2.9 %collective-permute-done.3.refs_2_ = f32[64,384]{1,0:T(8,128)S(1)} collective-permute-done((f32[64,384]{1,0:T(8,128)S(1)}, f32[64,384]{1,0:T(8,128)S(1)}, u32[]{:S(2)}, u32[]{:S(2)}) %collective-permute-start.3) | collective-permute-done | bytes 98336 | tf_op jit(solution)/shard_map/ppermute | solution.py:29
  24.0 0.0 collective-permute-done.4.refs_3_
  24.0 0.4 node.1
  24.4 0.0 collective-permute-done.6.pair_mine_ref
  24.4 0.0 collective-permute-done.7.pair_theirs_ref
  24.4 0.4 correct.1.sent_ref
  24.8 1.6 %collective-permute-start.8 = (f32[256,128]{1,0:T(8,128)S(1)}, f32[256,128]{1,0:T(8,128)S(1)}, u32[]{:S(2)}, u32[]{:S(2)}) collective-permute-start(f32[256,128]{1,0:T(8,128)S(1)} %correct.1.sent_ref), channel_id=1, source_target_pairs={{0,8},{8,0},{16,24},{24,16},{1,9},{9,1},{17,25},{25,17},{2,10},{10... | collective-permute-start | bytes 393224 | tf_op jit(solution)/shard_map/ppermute | solution.py:29
  26.4 0.5 %collective-permute-start.15 = (f32[64,128]{1,0:T(8,128)S(1)}, f32[64,128]{1,0:T(8,128)S(1)}, u32[]{:S(2)}, u32[]{:S(2)}) collective-permute-start(f32[64,128]{1,0:T(8,128)S(1)} %get-tuple-element.22.own_ref.refs_0_), channel_id=1, source_target_pairs={{0,2},{1,3},{2,0},{3,1},{4,6},{5,7},{6,4},{7,5},{8,10},{9,11},{10,... | collective-permute-start | bytes 98312 | tf_op jit(solution)/shard_map/ppermute | solution.py:29
  26.9 1.2 %collective-permute-start.16 = (f32[64,128]{1,0:T(8,128)S(1)}, f32[64,128]{1,0:T(8,128)S(1)}, u32[]{:S(2)}, u32[]{:S(2)}) collective-permute-start(f32[64,128]{1,0:T(8,128)S(1)} %get-tuple-element.23.other_ref), channel_id=1, source_target_pairs={{0,4},{1,5},{2,6},{3,7},{4,0},{5,1},{6,2},{7,3},{8,12},{9,13},{10,... | collective-permute-start | bytes 98312 | tf_op jit(solution)/shard_map/ppermute | solution.py:29
  28.1 1.8 %collective-permute-start.17 = (f32[64,128]{1,0:T(8,128)S(1)}, f32[64,128]{1,0:T(8,128)S(1)}, u32[]{:S(2)}, u32[]{:S(2)}) collective-permute-start(f32[64,128]{1,0:T(8,128)S(1)} %get-tuple-element.23.other_ref), channel_id=1, source_target_pairs={{0,6},{1,7},{2,4},{3,5},{4,2},{5,3},{6,0},{7,1},{8,14},{9,15},{10,... | collective-permute-start | bytes 98312 | tf_op jit(solution)/shard_map/ppermute | solution.py:29
  29.9 0.0 collective-permute-done.8.got_ref.after_ref
  29.9 0.8 %level1.1 = (f32[64,128]{1,0:T(8,128)S(1)}, f32[64,128]{1,0:T(8,128)S(1)}) custom-call(f32[256,128]{1,0:T(8,128)S(1)} %correct.1.sent_ref, f32[256,128]{1,0:T(8,128)S(1)} %collective-permute-done.8.got_ref.after_ref, f32[3,256,256]{2,1,0:T(8,128)S(1)} %prepare.1.refs_4_.joined_ref, f32[256,128]{1,0:T(8,128)S(1)} %collective-permute-done.8.got_ref.after_ref), custom_call_target="tpu_custom_call" | custom-call | flops 6600000000 | tf_op jit(solution)/shard_map/level1/pallas_call | solution.py:390
  30.7 2.7 %collective-permute-start.9 = (f32[64,128]{1,0:T(8,128)S(1)}, f32[64,128]{1,0:T(8,128)S(1)}, u32[]{:S(2)}, u32[]{:S(2)}) collective-permute-start(f32[64,128]{1,0:T(8,128)S(1)} %get-tuple-element.26.sent_ref), channel_id=1, source_target_pairs={{0,16},{8,24},{16,0},{24,8},{1,17},{9,25},{17,1},{25,9},{2,18},{10... | collective-permute-start | bytes 98312 | tf_op jit(solution)/shard_map/ppermute | solution.py:29
  33.3 2.2 %solve.1.after_ref.first_ref = f32[4608,512]{1,0:T(8,128)S(1)} custom-call(bf16[18,256,256]{2,1,0:T(8,128)(2,1)S(1)} %permute.1.moved_ref, bf16[4608,512]{1,0:T(8,128)(2,1)S(1)} %bitcast.1, f32[64,384]{1,0:T(8,128)S(1)} %get-tuple-element.18.refs_0_), custom_call_target="tpu_custom_call" | custom-call | flops 8800000000 | tf_op jit(solution)/shard_map/solve/pallas_call | solution.py:379
  35.6 0.0 collective-permute-done.15.refs_1_
  35.6 0.0 collective-permute-done.16.refs_2_
  35.6 0.0 collective-permute-done.17.refs_3_
  35.6 0.0 copy-start
  35.6 0.1 collective-permute-start.18
  35.7 0.0 collective-permute-done.9.got_ref
  35.7 0.4 level2.1.refs_1_
  36.1 0.6 %collective-permute-start.11 = (f32[64,256]{1,0:T(8,128)S(1)}, f32[64,256]{1,0:T(8,128)S(1)}, u32[]{:S(2)}, u32[]{:S(2)}) collective-permute-start(f32[64,256]{1,0:T(8,128)S(1)} %pack.1.refs_0_), channel_id=1, source_target_pairs={{0,2},{1,3},{2,0},{3,1},{4,6},{5,7},{6,4},{7,5},{8,10},{9,11},{10,... | collective-permute-start | bytes 196616 | tf_op jit(solution)/shard_map/ppermute | solution.py:29
  36.7 1.2 %collective-permute-start.13 = (f32[64,256]{1,0:T(8,128)S(1)}, f32[64,256]{1,0:T(8,128)S(1)}, u32[]{:S(2)}, u32[]{:S(2)}) collective-permute-start(f32[64,256]{1,0:T(8,128)S(1)} %pack.1.refs_0_), channel_id=1, source_target_pairs={{0,4},{1,5},{2,6},{3,7},{4,0},{5,1},{6,2},{7,3},{8,12},{9,13},{10,... | collective-permute-start | bytes 196616 | tf_op jit(solution)/shard_map/ppermute | solution.py:29
  37.9 1.7 %collective-permute-start.19 = (f32[64,256]{1,0:T(8,128)S(1)}, f32[64,256]{1,0:T(8,128)S(1)}, u32[]{:S(2)}, u32[]{:S(2)}) collective-permute-start(f32[64,256]{1,0:T(8,128)S(1)} %pack.1.refs_0_), channel_id=1, source_target_pairs={{0,6},{1,7},{2,4},{3,5},{4,2},{5,3},{6,0},{7,1},{8,14},{9,15},{10,... | collective-permute-start | bytes 196616 | tf_op jit(solution)/shard_map/ppermute | solution.py:29
  39.6 0.0 collective-permute-done.18.pair_ref
  39.6 1.6 %apply.1.after_ref.refs_8_ = f32[4608,512]{1,0:T(8,128)S(1)} custom-call(f32[4,64,128]{2,1,0:T(8,128)S(1)} %stack.1.own_ref, f32[4,64,128]{2,1,0:T(8,128)S(1)} %collective-permute-done.18.pair_ref, f32[4608,512]{1,0:T(8,128)S(1)} %solve.1.after_ref.first_ref, bf16[3,4608,128]{2,1,0:T(8,128)(2,1)S(1)} %copy-done), custom_call_target="tpu_custom_call" | custom-call | flops 1980000000 | tf_op jit(solution)/shard_map/apply/pallas_call | solution.py:401
  41.2 0.1 collective-permute-start.10
  41.3 0.0 collective-permute-done.11.refs_2_
  41.3 0.5 %collective-permute-start.12 = (f32[64,256]{1,0:T(8,128)S(1)}, f32[64,256]{1,0:T(8,128)S(1)}, u32[]{:S(2)}, u32[]{:S(2)}) collective-permute-start(f32[64,256]{1,0:T(8,128)S(1)} %collective-permute-done.11.refs_2_), channel_id=1, source_target_pairs={{0,1},{1,0},{2,3},{3,2},{4,5},{5,4},{6,7},{7,6},{8,9},{9,8},{10,11... | collective-permute-start | bytes 196616 | tf_op jit(solution)/shard_map/ppermute | solution.py:29
  41.8 0.0 collective-permute-done.13.refs_4_
  41.8 0.1 collective-permute-start.14
  41.9 1.2 %collective-permute-done.19.ref = f32[64,256]{1,0:T(8,128)S(1)} collective-permute-done((f32[64,256]{1,0:T(8,128)S(1)}, f32[64,256]{1,0:T(8,128)S(1)}, u32[]{:S(2)}, u32[]{:S(2)}) %collective-permute-start.19) | collective-permute-done | bytes 65568 | tf_op jit(solution)/shard_map/ppermute | solution.py:29
  43.1 0.0 collective-permute-start.20
  43.1 0.0 collective-permute-done.10.refs_1_
  43.1 0.0 collective-permute-done.12.refs_3_
  43.1 0.0 collective-permute-done.14.refs_5_
  43.1 1.2 %collective-permute-done.20.refs_7_ = f32[64,256]{1,0:T(8,128)S(1)} collective-permute-done((f32[64,256]{1,0:T(8,128)S(1)}, f32[64,256]{1,0:T(8,128)S(1)}, u32[]{:S(2)}, u32[]{:S(2)}) %collective-permute-start.20) | collective-permute-done | bytes 65568 | tf_op jit(solution)/shard_map/ppermute | solution.py:29
  44.4 4.5 %expand.1 = f32[4608,512]{1,0:T(8,128)} custom-call(f32[64,256]{1,0:T(8,128)S(1)} %pack.1.refs_0_, f32[64,256]{1,0:T(8,128)S(1)} %collective-permute-done.10.refs_1_, f32[64,256]{1,0:T(8,128)S(1)} %collective-permute-done.11.refs_2_, f32[64,256]{1,0:T(8,128)S(1)} %collective-permute-done.12.refs_3_, f32[64,256]{1,0:T(8,128)S(1)} %collective-permute-done.13.refs_4_, ...), custom_call_target="tpu_custom_call" | custom-call | flops 5500000256 | tf_op jit(solution)/shard_map/expand/pallas_call | solution.py:423
  (9 shorter events, 0.1 us)
Async XLA Ops:
  0.0 6.4 %copy-start.2 = (s32[18,256]{1,0:T(8,128)S(1)}, s32[18,256]{1,0:T(8,128)}, u32[]{:S(2)}) copy-start(s32[18,256]{1,0:T(8,128)} %order_ref.1) | copy-start | bytes 55300
  0.0 6.4 %copy-start.1 = (bf16[18,256,256]{2,1,0:T(8,128)(2,1)S(1)}, bf16[18,256,256]{2,1,0:T(8,128)(2,1)}, u32[]{:S(2)}) copy-start(bf16[18,256,256]{2,1,0:T(8,128)(2,1)} %inv_ref.1) | copy-start | bytes 7077892
  3.3 7.9 %collective-permute-start = (f32[128,384]{1,0:T(8,128)S(1)}, f32[128,384]{1,0:T(8,128)S(1)}, u32[]{:S(2)}, u32[]{:S(2)}) collective-permute-start(f32[128,384]{1,0:T(8,128)S(1)} %get-tuple-element.17.after_ref.mine_ref), channel_id=1, source_target_pairs={{0,2},{1,3},{2,0},{3,1},{4,6},{5,7},{6,4},{7,5},{8,10},{9,11},{10,... | collective-permute-start | bytes 589832 | tf_op jit(solution)/shard_map/ppermute | solution.py:29
  6.4 2.7 %slice-start = ((s8[4718592]{0:T(1024)(128)(4,1)}), s8[4194304]{0:T(1024)(128)(4,1)S(1)}, s32[]{:S(2)}) async-start(s8[4718592]{0:T(1024)(128)(4,1)} %bitcast), calls=%async_computation | async-start | bytes 8388608
  7.4 1.6 %slice-start.1 = ((s8[4718592]{0:T(1024)(128)(4,1)}), s8[524288]{0:T(1024)(128)(4,1)S(1)}, s32[]{:S(2)}) async-start(s8[4718592]{0:T(1024)(128)(4,1)} %bitcast), calls=%async_computation.1 | async-start | bytes 1048576
  11.1 4.1 %collective-permute-start.1 = (f32[384,256]{1,0:T(8,128)S(1)}, f32[384,256]{1,0:T(8,128)S(1)}, u32[]{:S(2)}, u32[]{:S(2)}) collective-permute-start(f32[384,256]{1,0:T(8,128)S(1)} %project_other.1), channel_id=1, source_target_pairs={{0,1},{1,0},{2,3},{3,2},{4,5},{5,4},{6,7},{7,6},{8,9},{9,8},{10,11... | collective-permute-start | bytes 1179656 | tf_op jit(solution)/shard_map/ppermute | solution.py:29
  11.3 7.7 %copy-start.3 = (s32[3,128]{1,0:T(4,128)S(1)}, s32[3,128]{1,0:T(4,128)}, u32[]{:S(2)}) copy-start(s32[3,128]{1,0:T(4,128)} %perm_ref.1) | copy-start | bytes 4612
  11.3 7.7 %collective-permute-start.5 = (f32[128,384]{1,0:T(8,128)S(1)}, f32[128,384]{1,0:T(8,128)S(1)}, u32[]{:S(2)}, u32[]{:S(2)}) collective-permute-start(f32[128,384]{1,0:T(8,128)S(1)} %add.1.after_ref.mine_ref), channel_id=1, source_target_pairs={{0,4},{1,5},{2,6},{3,7},{4,0},{5,1},{6,2},{7,3},{8,12},{9,13},{10,... | collective-permute-start | bytes 589832 | tf_op jit(solution)/shard_map/ppermute | solution.py:29
  15.1 9.3 %collective-permute-start.6 = (f32[128,384]{1,0:T(8,128)S(1)}, f32[128,384]{1,0:T(8,128)S(1)}, u32[]{:S(2)}, u32[]{:S(2)}) collective-permute-start(f32[128,384]{1,0:T(8,128)S(1)} %add.1.after_ref.mine_ref), channel_id=1, source_target_pairs={{0,1},{1,0},{2,3},{3,2},{4,5},{5,4},{6,7},{7,6},{8,9},{9,8},{10,11... | collective-permute-start | bytes 589832 | tf_op jit(solution)/shard_map/ppermute | solution.py:29
  15.4 5.7 %collective-permute-start.2 = (f32[64,384]{1,0:T(8,128)S(1)}, f32[64,384]{1,0:T(8,128)S(1)}, u32[]{:S(2)}, u32[]{:S(2)}) collective-permute-start(f32[64,384]{1,0:T(8,128)S(1)} %get-tuple-element.19), channel_id=1, source_target_pairs={{0,2},{1,3},{2,0},{3,1},{4,6},{5,7},{6,4},{7,5},{8,10},{9,11},{10,... | collective-permute-start | bytes 294920 | tf_op jit(solution)/shard_map/ppermute | solution.py:29
  17.0 7.0 %collective-permute-start.3 = (f32[64,384]{1,0:T(8,128)S(1)}, f32[64,384]{1,0:T(8,128)S(1)}, u32[]{:S(2)}, u32[]{:S(2)}) collective-permute-start(f32[64,384]{1,0:T(8,128)S(1)} %get-tuple-element.20), channel_id=1, source_target_pairs={{0,4},{1,5},{2,6},{3,7},{4,0},{5,1},{6,2},{7,3},{8,12},{9,13},{10,... | collective-permute-start | bytes 294920 | tf_op jit(solution)/shard_map/ppermute | solution.py:29
  17.5 6.5 %collective-permute-start.4 = (f32[64,384]{1,0:T(8,128)S(1)}, f32[64,384]{1,0:T(8,128)S(1)}, u32[]{:S(2)}, u32[]{:S(2)}) collective-permute-start(f32[64,384]{1,0:T(8,128)S(1)} %get-tuple-element.21), channel_id=1, source_target_pairs={{0,6},{1,7},{2,4},{3,5},{4,2},{5,3},{6,0},{7,1},{8,14},{9,15},{10,... | collective-permute-start | bytes 294920 | tf_op jit(solution)/shard_map/ppermute | solution.py:29
  19.0 5.4 %collective-permute-start.7 = (f32[128,384]{1,0:T(8,128)S(1)}, f32[128,384]{1,0:T(8,128)S(1)}, u32[]{:S(2)}, u32[]{:S(2)}) collective-permute-start(f32[128,384]{1,0:T(8,128)S(1)} %collective-permute-done.5.theirs_ref), channel_id=1, source_target_pairs={{0,1},{1,0},{2,3},{3,2},{4,5},{5,4},{6,7},{7,6},{8,9},{9,8},{10,11... | collective-permute-start | bytes 589832 | tf_op jit(solution)/shard_map/ppermute | solution.py:29
  24.8 5.1 %collective-permute-start.8 = (f32[256,128]{1,0:T(8,128)S(1)}, f32[256,128]{1,0:T(8,128)S(1)}, u32[]{:S(2)}, u32[]{:S(2)}) collective-permute-start(f32[256,128]{1,0:T(8,128)S(1)} %correct.1.sent_ref), channel_id=1, source_target_pairs={{0,8},{8,0},{16,24},{24,16},{1,9},{9,1},{17,25},{25,17},{2,10},{10... | collective-permute-start | bytes 393224 | tf_op jit(solution)/shard_map/ppermute | solution.py:29
  26.4 9.2 %collective-permute-start.15 = (f32[64,128]{1,0:T(8,128)S(1)}, f32[64,128]{1,0:T(8,128)S(1)}, u32[]{:S(2)}, u32[]{:S(2)}) collective-permute-start(f32[64,128]{1,0:T(8,128)S(1)} %get-tuple-element.22.own_ref.refs_0_), channel_id=1, source_target_pairs={{0,2},{1,3},{2,0},{3,1},{4,6},{5,7},{6,4},{7,5},{8,10},{9,11},{10,... | collective-permute-start | bytes 98312 | tf_op jit(solution)/shard_map/ppermute | solution.py:29
  26.9 8.6 %collective-permute-start.16 = (f32[64,128]{1,0:T(8,128)S(1)}, f32[64,128]{1,0:T(8,128)S(1)}, u32[]{:S(2)}, u32[]{:S(2)}) collective-permute-start(f32[64,128]{1,0:T(8,128)S(1)} %get-tuple-element.23.other_ref), channel_id=1, source_target_pairs={{0,4},{1,5},{2,6},{3,7},{4,0},{5,1},{6,2},{7,3},{8,12},{9,13},{10,... | collective-permute-start | bytes 98312 | tf_op jit(solution)/shard_map/ppermute | solution.py:29
  28.1 7.4 %collective-permute-start.17 = (f32[64,128]{1,0:T(8,128)S(1)}, f32[64,128]{1,0:T(8,128)S(1)}, u32[]{:S(2)}, u32[]{:S(2)}) collective-permute-start(f32[64,128]{1,0:T(8,128)S(1)} %get-tuple-element.23.other_ref), channel_id=1, source_target_pairs={{0,6},{1,7},{2,4},{3,5},{4,2},{5,3},{6,0},{7,1},{8,14},{9,15},{10,... | collective-permute-start | bytes 98312 | tf_op jit(solution)/shard_map/ppermute | solution.py:29
  30.7 5.0 %collective-permute-start.9 = (f32[64,128]{1,0:T(8,128)S(1)}, f32[64,128]{1,0:T(8,128)S(1)}, u32[]{:S(2)}, u32[]{:S(2)}) collective-permute-start(f32[64,128]{1,0:T(8,128)S(1)} %get-tuple-element.26.sent_ref), channel_id=1, source_target_pairs={{0,16},{8,24},{16,0},{24,8},{1,17},{9,25},{17,1},{25,9},{2,18},{10... | collective-permute-start | bytes 98312 | tf_op jit(solution)/shard_map/ppermute | solution.py:29
  35.6 4.0 %copy-start = (bf16[3,4608,128]{2,1,0:T(8,128)(2,1)S(1)}, bf16[3,4608,128]{2,1,0:T(8,128)(2,1)}, u32[]{:S(2)}) copy-start(bf16[3,4608,128]{2,1,0:T(8,128)(2,1)} %refs_9_.1) | copy-start | bytes 10616836
  35.6 4.0 %collective-permute-start.18 = (f32[4,64,128]{2,1,0:T(8,128)S(1)}, f32[4,64,128]{2,1,0:T(8,128)S(1)}, u32[]{:S(2)}, u32[]{:S(2)}) collective-permute-start(f32[4,64,128]{2,1,0:T(8,128)S(1)} %stack.1.own_ref), channel_id=1, source_target_pairs={{0,1},{1,0},{2,3},{3,2},{4,5},{5,4},{6,7},{7,6},{8,9},{9,8},{10,11... | collective-permute-start | bytes 393224 | tf_op jit(solution)/shard_map/ppermute | solution.py:29
  36.1 5.2 %collective-permute-start.11 = (f32[64,256]{1,0:T(8,128)S(1)}, f32[64,256]{1,0:T(8,128)S(1)}, u32[]{:S(2)}, u32[]{:S(2)}) collective-permute-start(f32[64,256]{1,0:T(8,128)S(1)} %pack.1.refs_0_), channel_id=1, source_target_pairs={{0,2},{1,3},{2,0},{3,1},{4,6},{5,7},{6,4},{7,5},{8,10},{9,11},{10,... | collective-permute-start | bytes 196616 | tf_op jit(solution)/shard_map/ppermute | solution.py:29
  36.7 5.1 %collective-permute-start.13 = (f32[64,256]{1,0:T(8,128)S(1)}, f32[64,256]{1,0:T(8,128)S(1)}, u32[]{:S(2)}, u32[]{:S(2)}) collective-permute-start(f32[64,256]{1,0:T(8,128)S(1)} %pack.1.refs_0_), channel_id=1, source_target_pairs={{0,4},{1,5},{2,6},{3,7},{4,0},{5,1},{6,2},{7,3},{8,12},{9,13},{10,... | collective-permute-start | bytes 196616 | tf_op jit(solution)/shard_map/ppermute | solution.py:29
  37.9 5.2 %collective-permute-start.19 = (f32[64,256]{1,0:T(8,128)S(1)}, f32[64,256]{1,0:T(8,128)S(1)}, u32[]{:S(2)}, u32[]{:S(2)}) collective-permute-start(f32[64,256]{1,0:T(8,128)S(1)} %pack.1.refs_0_), channel_id=1, source_target_pairs={{0,6},{1,7},{2,4},{3,5},{4,2},{5,3},{6,0},{7,1},{8,14},{9,15},{10,... | collective-permute-start | bytes 196616 | tf_op jit(solution)/shard_map/ppermute | solution.py:29
  41.2 1.9 %collective-permute-start.10 = (f32[64,256]{1,0:T(8,128)S(1)}, f32[64,256]{1,0:T(8,128)S(1)}, u32[]{:S(2)}, u32[]{:S(2)}) collective-permute-start(f32[64,256]{1,0:T(8,128)S(1)} %pack.1.refs_0_), channel_id=1, source_target_pairs={{0,1},{1,0},{2,3},{3,2},{4,5},{5,4},{6,7},{7,6},{8,9},{9,8},{10,11... | collective-permute-start | bytes 196616 | tf_op jit(solution)/shard_map/ppermute | solution.py:29
  41.3 1.8 %collective-permute-start.12 = (f32[64,256]{1,0:T(8,128)S(1)}, f32[64,256]{1,0:T(8,128)S(1)}, u32[]{:S(2)}, u32[]{:S(2)}) collective-permute-start(f32[64,256]{1,0:T(8,128)S(1)} %collective-permute-done.11.refs_2_), channel_id=1, source_target_pairs={{0,1},{1,0},{2,3},{3,2},{4,5},{5,4},{6,7},{7,6},{8,9},{9,8},{10,11... | collective-permute-start | bytes 196616 | tf_op jit(solution)/shard_map/ppermute | solution.py:29
  41.8 1.3 %collective-permute-start.14 = (f32[64,256]{1,0:T(8,128)S(1)}, f32[64,256]{1,0:T(8,128)S(1)}, u32[]{:S(2)}, u32[]{:S(2)}) collective-permute-start(f32[64,256]{1,0:T(8,128)S(1)} %collective-permute-done.13.refs_4_), channel_id=1, source_target_pairs={{0,1},{1,0},{2,3},{3,2},{4,5},{5,4},{6,7},{7,6},{8,9},{9,8},{10,11... | collective-permute-start | bytes 196616 | tf_op jit(solution)/shard_map/ppermute | solution.py:29
  43.1 1.3 %collective-permute-start.20 = (f32[64,256]{1,0:T(8,128)S(1)}, f32[64,256]{1,0:T(8,128)S(1)}, u32[]{:S(2)}, u32[]{:S(2)}) collective-permute-start(f32[64,256]{1,0:T(8,128)S(1)} %relay.1.refs_6_), channel_id=1, source_target_pairs={{0,1},{1,0},{2,3},{3,2},{4,5},{5,4},{6,7},{7,6},{8,9},{9,8},{10,11... | collective-permute-start | bytes 196616 | tf_op jit(solution)/shard_map/ppermute | solution.py:29

commit v13 on v12

--- a/solution.py
+++ b/solution.py
@@ -37,9 +37,10 @@
     return [(level, below) for level in range(levels) for below in range(first, level)]
 
 
-def gram_kernel(levels, per_step, width, right_ref, left_ref, flip_ref, out_ref,
+def gram_kernel(levels, per_step, width, right_ref, left_ref, flip_ref, keep_ref, send_ref,
                 right_buf, left_buf, gram_ref, sems):
     rank = right_ref.shape[2]
+    half = rank // 2
     tile = per_step * width
     steps = right_ref.shape[1] // tile
 
@@ -66,9 +67,12 @@
         return 0
 
     lax.fori_loop(0, steps, body, 0)
+    core = lax.axis_index("rows") % 2
     for spot, (level, below) in enumerate(below_pairs(levels)):
-        rows = pl.ds((level - 1) * rank, rank)
-        out_ref[:, pl.ds(spot * rank, rank)] = gram_ref[rows, pl.ds(below * rank, rank)]
+        lanes = pl.ds(spot * rank, rank)
+        for ref, side in ((keep_ref, core), (send_ref, 1 - core)):
+            rows = pl.ds(pl.multiple_of((level - 1) * rank + side * half, half), half)
+            ref[:, lanes] = gram_ref[rows, pl.ds(below * rank, rank)]
 
 
 def permute_kernel(per_step, width, order_ref, inv_ref, moved_ref):
@@ -176,7 +180,9 @@
 
 def correct_kernel(levels, rank, own_ref, other_ref, rest_ref, mine_ref, theirs_ref, pair_mine_ref,
                    pair_theirs_ref, message_ref):
-    grams = [mine_ref[...] + pair_mine_ref[...], theirs_ref[...] + pair_theirs_ref[...]]
+    core = lax.axis_index("rows") % 2
+    grams = [jnp.concatenate(by_side(core, mine_ref[...], pair_mine_ref[...]), axis=0),
+             jnp.concatenate(by_side(core, theirs_ref[...], pair_theirs_ref[...]), axis=0)]
     pairs = below_pairs(levels)
     lanes = {pair: slice(spot * rank, (spot + 1) * rank) for spot, pair in enumerate(pairs)}
     joint = jnp.concatenate(
@@ -292,10 +298,10 @@
     gram_lanes = len(below_pairs(levels)) * rank
 
     per_step = blocks_per_step(nblocks, 3)
-    flipped, gram = pl.pallas_call(
+    flipped, gram_keep, gram_send = pl.pallas_call(
         functools.partial(gram_kernel, levels, per_step, width),
         in_specs=[pl.BlockSpec(memory_space=pltpu.HBM)] * 2,
-        out_shape=[jax.ShapeDtypeStruct((kinds, rows), jnp.bfloat16), floats(rank, gram_lanes)],
+        out_shape=[jax.ShapeDtypeStruct((kinds, rows), jnp.bfloat16)] + [floats(rank // 2, gram_lanes)] * 2,
         scratch_shapes=[
             pltpu.VMEM((levels, rows, rank), jnp.bfloat16),
             pltpu.VMEM((levels - 1, rows, rank), jnp.bfloat16),
@@ -307,6 +313,7 @@
     )(pltpu.with_memory_space_constraint(right_basis, pltpu.HBM),
       pltpu.with_memory_space_constraint(left_basis, pltpu.HBM))
 
+    gram_got = swap(gram_send, "rows", 1)
     moved = pl.pallas_call(
         functools.partial(permute_kernel, blocks_per_step(nblocks, 9), width),
         out_shape=jax.ShapeDtypeStruct((nblocks, width, width), jnp.bfloat16),
@@ -319,6 +326,7 @@
             add_kernel, out_shape=floats(*mine.shape), name="add", **settings(8, 0.1),
         )(mine, got)
 
+    gram = add(gram_keep, gram_got)
     factors = pl.pallas_call(
         functools.partial(weigh_kernel, blocks_per_step(nblocks, 9), width),
         out_shape=jax.ShapeDtypeStruct((2 * kinds, rows), jnp.bfloat16),
@@ -331,7 +339,7 @@
             functools.partial(project_kernel, other),
             out_shape=floats(kinds, columns // 2),
             name="project_other" if other else "project_own",
-            **settings(12, 1 if other else 8),
+            **settings(12, 1 if other else 4),
         )(factors, rhs, after)
 
     send = project(True, gram)

time: 49 us -> 48.7 us (level)
  waiting for transfers between devices: 5.44 us -> 4.58 us
  starting transfers between devices: 20.6 us -> 21.1 us
    ppermute x21 -> x22, waiting for transfers between devices: 5.44 us -> 4.58 us  [swap(): return lax.ppermute(value, axis, [(i, i ^ mask) for i in range(count)])]
    ppermute x21 -> x22, starting transfers between devices: 20.6 us -> 21.1 us  [swap(): return lax.ppermute(value, axis, [(i, i ^ mask) for i in range(count)])]
  transfers between devices with their start and end apart: 21 -> 22, of which waited for: 4 -> 5; matrix products, arithmetic and copies ran while one was open for 0% -> 0% of each run, Pallas kernels for 29% -> 29%
where the time goes in v13:
time: 48.7 us; the launch traced here: 48.6 us
  Pallas kernels  22.5 us (46%)
  starting transfers between devices  21.1 us (43%)
  waiting for transfers between devices  4.58 us (9%)
    ppermute x22, starting transfers between devices, swap(): return lax.ppermute(value, axis, [(i, i ^ mask) for i in range(count)])  21.1 us
    ppermute x22, waiting for transfers between devices, swap(): return lax.ppermute(value, axis, [(i, i ^ mask) for i in range(count)])  4.58 us
    pallas_call x1, Pallas kernels, per_device(): pl.pallas_call(functools.partial(expand_kernel, levels, per_step * width,...  4.5 us
    pallas_call x2, Pallas kernels, project(): pl.pallas_call(functools.partial(project_kernel, other), out_shape=floats...  3.99 us
    pallas_call x1, Pallas kernels, per_device(): pl.pallas_call(functools.partial(gram_kernel, levels, per_step, width), i...  3.34 us
    pallas_call x1, Pallas kernels, per_device(): pl.pallas_call(functools.partial(solve_kernel, per_step, width), out_shap...  2.22 us
    pallas_call x1, Pallas kernels, per_device(): pl.pallas_call(functools.partial(prepare_kernel, levels), in_specs=[pl.Bl...  2.1 us
    pallas_call x1, Pallas kernels, per_device(): pl.pallas_call(functools.partial(weigh_kernel, blocks_per_step(nblocks, 9...  1.6 us
  transfers between devices with their start and end apart: 22, of which 5 were waited for; matrix products, arithmetic and copies ran while one was open for 0% of the time, Pallas kernels for 29%

profile of v13, /device:TPU:0, one launch (start us, length us, event | category | flops | bytes accessed | tf_op | source)
XLA Modules:
  0.0 48.6 jit_solution(3062307700576971333)
XLA Ops:
  0.0 3.3 %gram.1 = (bf16[384,4608]{1,0:T(8,128)(2,1)S(1)}, f32[64,384]{1,0:T(8,128)S(1)}, f32[64,384]{1,0:T(8,128)S(1)}) custom-call(bf16[3,4608,128]{2,1,0:T(8,128)(2,1)} %right_ref.1, bf16[3,4608,128]{2,1,0:T(8,128)(2,1)} %refs_9_.1), custom_call_target="tpu_custom_call" | custom-call | flops 3300000000 | tf_op jit(solution)/shard_map/gram/pallas_call | solution.py:301
  3.4 0.5 %collective-permute-start = (f32[64,384]{1,0:T(8,128)S(1)}, f32[64,384]{1,0:T(8,128)S(1)}, u32[]{:S(2)}, u32[]{:S(2)}) collective-permute-start(f32[64,384]{1,0:T(8,128)S(1)} %get-tuple-element.19), channel_id=1, source_target_pairs={{0,1},{1,0},{2,3},{3,2},{4,5},{5,4},{6,7},{7,6},{8,9},{9,8},{10,11... | collective-permute-start | bytes 294920 | tf_op jit(solution)/shard_map/ppermute | solution.py:29
  3.9 0.0 copy-done.2
  3.9 0.0 copy-done.1
  3.9 1.0 %permute.1.moved_ref = bf16[18,256,256]{2,1,0:T(8,128)(2,1)S(1)} custom-call(s32[18,256]{1,0:T(8,128)S(1)} %copy-done.2, bf16[18,256,256]{2,1,0:T(8,128)(2,1)S(1)} %copy-done.1), custom_call_target="tpu_custom_call" | custom-call | flops 1650000000 | tf_op jit(solution)/shard_map/permute/pallas_call | solution.py:317
  4.9 0.0 collective-permute-done.got_ref
  4.9 0.0 slice-start
  5.0 2.8 %collective-permute-start.1 = (f32[64,384]{1,0:T(8,128)S(1)}, f32[64,384]{1,0:T(8,128)S(1)}, u32[]{:S(2)}, u32[]{:S(2)}) collective-permute-start(f32[64,384]{1,0:T(8,128)S(1)} %add.2.after_ref.mine_ref), channel_id=1, source_target_pairs={{0,2},{1,3},{2,0},{3,1},{4,6},{5,7},{6,4},{7,5},{8,10},{9,11},{10,... | collective-permute-start | bytes 294920 | tf_op jit(solution)/shard_map/ppermute | solution.py:29
  7.7 1.6 %weigh.1.factor_ref = bf16[768,4608]{1,0:T(8,128)(2,1)S(1)} custom-call(bf16[18,256,256]{2,1,0:T(8,128)(2,1)S(1)} %permute.1.moved_ref, bf16[384,4608]{1,0:T(8,128)(2,1)S(1)} %get-tuple-element.17.flip_ref, f32[64,384]{1,0:T(8,128)S(1)} %add.2.after_ref.mine_ref), custom_call_target="tpu_custom_call" | custom-call | flops 2640000000 | tf_op jit(solution)/shard_map/weigh/pallas_call | solution.py:330
  9.4 2.0 %project_other.1 = f32[384,256]{1,0:T(8,128)S(1)} custom-call(bf16[768,4608]{1,0:T(8,128)(2,1)S(1)} %weigh.1.factor_ref, bf16[4608,512]{1,0:T(8,128)(2,1)S(1)} %bitcast.1, f32[64,384]{1,0:T(8,128)S(1)} %add.2.after_ref.mine_ref), custom_call_target="tpu_custom_call" | custom-call | flops 1100000000 | tf_op jit(solution)/shard_map/project_other/pallas_call | solution.py:338
  11.4 0.1 collective-permute-start.2
  11.5 0.0 collective-permute-done.1.got_ref
  11.5 0.0 copy-start.3
  11.5 1.6 %collective-permute-start.6 = (f32[64,384]{1,0:T(8,128)S(1)}, f32[64,384]{1,0:T(8,128)S(1)}, u32[]{:S(2)}, u32[]{:S(2)}) collective-permute-start(f32[64,384]{1,0:T(8,128)S(1)} %add.3.after_ref.mine_ref), channel_id=1, source_target_pairs={{0,4},{1,5},{2,6},{3,7},{4,0},{5,1},{6,2},{7,3},{8,12},{9,13},{10,... | collective-permute-start | bytes 294920 | tf_op jit(solution)/shard_map/ppermute | solution.py:29
  13.1 2.0 %project_own.1.keep_ref = f32[384,256]{1,0:T(8,128)S(1)} custom-call(bf16[768,4608]{1,0:T(8,128)(2,1)S(1)} %weigh.1.factor_ref, bf16[4608,512]{1,0:T(8,128)(2,1)S(1)} %bitcast.1, f32[64,384]{1,0:T(8,128)S(1)} %add.3.after_ref.mine_ref), custom_call_target="tpu_custom_call" | custom-call | flops 4400000000 | tf_op jit(solution)/shard_map/project_own/pallas_call | solution.py:338
  15.1 0.0 collective-permute-done.2.got_ref
  15.1 0.2 merge.1
  15.3 1.3 %collective-permute-start.3 = (f32[64,384]{1,0:T(8,128)S(1)}, f32[64,384]{1,0:T(8,128)S(1)}, u32[]{:S(2)}, u32[]{:S(2)}) collective-permute-start(f32[64,384]{1,0:T(8,128)S(1)} %get-tuple-element.21), channel_id=1, source_target_pairs={{0,2},{1,3},{2,0},{3,1},{4,6},{5,7},{6,4},{7,5},{8,10},{9,11},{10,... | collective-permute-start | bytes 294920 | tf_op jit(solution)/shard_map/ppermute | solution.py:29
  16.6 0.5 %collective-permute-start.4 = (f32[64,384]{1,0:T(8,128)S(1)}, f32[64,384]{1,0:T(8,128)S(1)}, u32[]{:S(2)}, u32[]{:S(2)}) collective-permute-start(f32[64,384]{1,0:T(8,128)S(1)} %get-tuple-element.22), channel_id=1, source_target_pairs={{0,4},{1,5},{2,6},{3,7},{4,0},{5,1},{6,2},{7,3},{8,12},{9,13},{10,... | collective-permute-start | bytes 294920 | tf_op jit(solution)/shard_map/ppermute | solution.py:29
  17.1 1.8 %collective-permute-start.5 = (f32[64,384]{1,0:T(8,128)S(1)}, f32[64,384]{1,0:T(8,128)S(1)}, u32[]{:S(2)}, u32[]{:S(2)}) collective-permute-start(f32[64,384]{1,0:T(8,128)S(1)} %get-tuple-element.23), channel_id=1, source_target_pairs={{0,6},{1,7},{2,4},{3,5},{4,2},{5,3},{6,0},{7,1},{8,14},{9,15},{10,... | collective-permute-start | bytes 294920 | tf_op jit(solution)/shard_map/ppermute | solution.py:29
  18.9 0.0 copy-done.3
  18.9 2.1 %prepare.1.refs_4_.joined_ref = f32[3,256,256]{2,1,0:T(8,128)S(1)} custom-call(f32[7,256,256]{2,1,0:T(8,128)} %joined_ref.1, s32[3,128]{1,0:T(4,128)S(1)} %copy-done.3), custom_call_target="tpu_custom_call" | custom-call | flops 2200000000 | tf_op jit(solution)/shard_map/prepare/pallas_call | solution.py:362
  21.0 0.1 collective-permute-start.7
  21.1 0.0 collective-permute-done.6.theirs_ref
  21.1 0.5 %collective-permute-start.8 = (f32[64,384]{1,0:T(8,128)S(1)}, f32[64,384]{1,0:T(8,128)S(1)}, u32[]{:S(2)}, u32[]{:S(2)}) collective-permute-start(f32[64,384]{1,0:T(8,128)S(1)} %collective-permute-done.6.theirs_ref), channel_id=1, source_target_pairs={{0,1},{1,0},{2,3},{3,2},{4,5},{5,4},{6,7},{7,6},{8,9},{9,8},{10,11... | collective-permute-start | bytes 294920 | tf_op jit(solution)/shard_map/ppermute | solution.py:29
  21.6 0.0 collective-permute-done.3.refs_1_
  21.6 1.5 %collective-permute-done.4.refs_2_ = f32[64,384]{1,0:T(8,128)S(1)} collective-permute-done((f32[64,384]{1,0:T(8,128)S(1)}, f32[64,384]{1,0:T(8,128)S(1)}, u32[]{:S(2)}, u32[]{:S(2)}) %collective-permute-start.4) | collective-permute-done | bytes 98336 | tf_op jit(solution)/shard_map/ppermute | solution.py:29
  23.1 0.0 collective-permute-done.5.refs_3_
  23.1 0.4 node.1
  23.4 0.0 collective-permute-done.7.pair_mine_ref
  23.4 0.0 collective-permute-done.8.pair_theirs_ref
  23.5 0.4 correct.1.sent_ref
  23.8 1.7 %collective-permute-start.9 = (f32[256,128]{1,0:T(8,128)S(1)}, f32[256,128]{1,0:T(8,128)S(1)}, u32[]{:S(2)}, u32[]{:S(2)}) collective-permute-start(f32[256,128]{1,0:T(8,128)S(1)} %correct.1.sent_ref), channel_id=1, source_target_pairs={{0,8},{8,0},{16,24},{24,16},{1,9},{9,1},{17,25},{25,17},{2,10},{10... | collective-permute-start | bytes 393224 | tf_op jit(solution)/shard_map/ppermute | solution.py:29
  25.5 1.0 %collective-permute-start.16 = (f32[64,128]{1,0:T(8,128)S(1)}, f32[64,128]{1,0:T(8,128)S(1)}, u32[]{:S(2)}, u32[]{:S(2)}) collective-permute-start(f32[64,128]{1,0:T(8,128)S(1)} %get-tuple-element.24.own_ref.refs_0_), channel_id=1, source_target_pairs={{0,2},{1,3},{2,0},{3,1},{4,6},{5,7},{6,4},{7,5},{8,10},{9,11},{10,... | collective-permute-start | bytes 98312 | tf_op jit(solution)/shard_map/ppermute | solution.py:29
  26.6 0.8 %collective-permute-start.17 = (f32[64,128]{1,0:T(8,128)S(1)}, f32[64,128]{1,0:T(8,128)S(1)}, u32[]{:S(2)}, u32[]{:S(2)}) collective-permute-start(f32[64,128]{1,0:T(8,128)S(1)} %get-tuple-element.25.other_ref), channel_id=1, source_target_pairs={{0,4},{1,5},{2,6},{3,7},{4,0},{5,1},{6,2},{7,3},{8,12},{9,13},{10,... | collective-permute-start | bytes 98312 | tf_op jit(solution)/shard_map/ppermute | solution.py:29
  27.4 1.7 %collective-permute-start.18 = (f32[64,128]{1,0:T(8,128)S(1)}, f32[64,128]{1,0:T(8,128)S(1)}, u32[]{:S(2)}, u32[]{:S(2)}) collective-permute-start(f32[64,128]{1,0:T(8,128)S(1)} %get-tuple-element.25.other_ref), channel_id=1, source_target_pairs={{0,6},{1,7},{2,4},{3,5},{4,2},{5,3},{6,0},{7,1},{8,14},{9,15},{10,... | collective-permute-start | bytes 98312 | tf_op jit(solution)/shard_map/ppermute | solution.py:29
  29.0 0.0 collective-permute-done.9.got_ref.after_ref
  29.0 0.8 %level1.1 = (f32[64,128]{1,0:T(8,128)S(1)}, f32[64,128]{1,0:T(8,128)S(1)}) custom-call(f32[256,128]{1,0:T(8,128)S(1)} %correct.1.sent_ref, f32[256,128]{1,0:T(8,128)S(1)} %collective-permute-done.9.got_ref.after_ref, f32[3,256,256]{2,1,0:T(8,128)S(1)} %prepare.1.refs_4_.joined_ref, f32[256,128]{1,0:T(8,128)S(1)} %collective-permute-done.9.got_ref.after_ref), custom_call_target="tpu_custom_call" | custom-call | flops 6600000000 | tf_op jit(solution)/shard_map/level1/pallas_call | solution.py:398
  29.8 2.7 %collective-permute-start.10 = (f32[64,128]{1,0:T(8,128)S(1)}, f32[64,128]{1,0:T(8,128)S(1)}, u32[]{:S(2)}, u32[]{:S(2)}) collective-permute-start(f32[64,128]{1,0:T(8,128)S(1)} %get-tuple-element.28.sent_ref), channel_id=1, source_target_pairs={{0,16},{8,24},{16,0},{24,8},{1,17},{9,25},{17,1},{25,9},{2,18},{10... | collective-permute-start | bytes 98312 | tf_op jit(solution)/shard_map/ppermute | solution.py:29
  32.5 2.2 %solve.1.after_ref.first_ref = f32[4608,512]{1,0:T(8,128)S(1)} custom-call(bf16[18,256,256]{2,1,0:T(8,128)(2,1)S(1)} %permute.1.moved_ref, bf16[4608,512]{1,0:T(8,128)(2,1)S(1)} %bitcast.1, f32[64,384]{1,0:T(8,128)S(1)} %get-tuple-element.20.refs_0_), custom_call_target="tpu_custom_call" | custom-call | flops 8800000000 | tf_op jit(solution)/shard_map/solve/pallas_call | solution.py:387
  34.7 0.0 collective-permute-done.16.refs_1_
  34.7 0.0 collective-permute-done.17.refs_2_
  34.7 0.0 collective-permute-done.18.refs_3_
  34.8 0.0 copy-start
  34.8 0.1 collective-permute-start.19
  34.8 0.0 collective-permute-done.10.got_ref
  34.9 0.4 level2.1.refs_1_
  35.2 0.6 %collective-permute-start.11 = (f32[64,256]{1,0:T(8,128)S(1)}, f32[64,256]{1,0:T(8,128)S(1)}, u32[]{:S(2)}, u32[]{:S(2)}) collective-permute-start(f32[64,256]{1,0:T(8,128)S(1)} %pack.1.refs_0_), channel_id=1, source_target_pairs={{0,1},{1,0},{2,3},{3,2},{4,5},{5,4},{6,7},{7,6},{8,9},{9,8},{10,11... | collective-permute-start | bytes 196616 | tf_op jit(solution)/shard_map/ppermute | solution.py:29
  35.8 1.0 %collective-permute-start.12 = (f32[64,256]{1,0:T(8,128)S(1)}, f32[64,256]{1,0:T(8,128)S(1)}, u32[]{:S(2)}, u32[]{:S(2)}) collective-permute-start(f32[64,256]{1,0:T(8,128)S(1)} %pack.1.refs_0_), channel_id=1, source_target_pairs={{0,2},{1,3},{2,0},{3,1},{4,6},{5,7},{6,4},{7,5},{8,10},{9,11},{10,... | collective-permute-start | bytes 196616 | tf_op jit(solution)/shard_map/ppermute | solution.py:29
  36.8 0.8 %collective-permute-start.14 = (f32[64,256]{1,0:T(8,128)S(1)}, f32[64,256]{1,0:T(8,128)S(1)}, u32[]{:S(2)}, u32[]{:S(2)}) collective-permute-start(f32[64,256]{1,0:T(8,128)S(1)} %pack.1.refs_0_), channel_id=1, source_target_pairs={{0,4},{1,5},{2,6},{3,7},{4,0},{5,1},{6,2},{7,3},{8,12},{9,13},{10,... | collective-permute-start | bytes 196616 | tf_op jit(solution)/shard_map/ppermute | solution.py:29
  37.6 1.7 %collective-permute-start.20 = (f32[64,256]{1,0:T(8,128)S(1)}, f32[64,256]{1,0:T(8,128)S(1)}, u32[]{:S(2)}, u32[]{:S(2)}) collective-permute-start(f32[64,256]{1,0:T(8,128)S(1)} %pack.1.refs_0_), channel_id=1, source_target_pairs={{0,6},{1,7},{2,4},{3,5},{4,2},{5,3},{6,0},{7,1},{8,14},{9,15},{10,... | collective-permute-start | bytes 196616 | tf_op jit(solution)/shard_map/ppermute | solution.py:29
  39.3 0.0 collective-permute-done.19.pair_ref
  39.3 1.6 %apply.1.after_ref.refs_8_ = f32[4608,512]{1,0:T(8,128)S(1)} custom-call(f32[4,64,128]{2,1,0:T(8,128)S(1)} %stack.1.own_ref, f32[4,64,128]{2,1,0:T(8,128)S(1)} %collective-permute-done.19.pair_ref, f32[4608,512]{1,0:T(8,128)S(1)} %solve.1.after_ref.first_ref, bf16[3,4608,128]{2,1,0:T(8,128)(2,1)S(1)} %copy-done), custom_call_target="tpu_custom_call" | custom-call | flops 1980000000 | tf_op jit(solution)/shard_map/apply/pallas_call | solution.py:409
  40.9 0.0 collective-permute-done.12.refs_2_
  40.9 0.1 collective-permute-start.13
  41.0 0.8 %collective-permute-done.14.refs_4_ = f32[64,256]{1,0:T(8,128)S(1)} collective-permute-done((f32[64,256]{1,0:T(8,128)S(1)}, f32[64,256]{1,0:T(8,128)S(1)}, u32[]{:S(2)}, u32[]{:S(2)}) %collective-permute-start.14) | collective-permute-done | bytes 65568 | tf_op jit(solution)/shard_map/ppermute | solution.py:29
  41.8 0.0 collective-permute-start.15
  41.8 1.0 %collective-permute-done.20.ref = f32[64,256]{1,0:T(8,128)S(1)} collective-permute-done((f32[64,256]{1,0:T(8,128)S(1)}, f32[64,256]{1,0:T(8,128)S(1)}, u32[]{:S(2)}, u32[]{:S(2)}) %collective-permute-start.20) | collective-permute-done | bytes 65568 | tf_op jit(solution)/shard_map/ppermute | solution.py:29
  42.8 0.0 collective-permute-start.21
  42.8 0.0 collective-permute-done.11.refs_1_
  42.8 0.0 collective-permute-done.13.refs_3_
  42.8 0.2 collective-permute-done.15.refs_5_
  43.1 1.0 %collective-permute-done.21.refs_7_ = f32[64,256]{1,0:T(8,128)S(1)} collective-permute-done((f32[64,256]{1,0:T(8,128)S(1)}, f32[64,256]{1,0:T(8,128)S(1)}, u32[]{:S(2)}, u32[]{:S(2)}) %collective-permute-start.21) | collective-permute-done | bytes 65568 | tf_op jit(solution)/shard_map/ppermute | solution.py:29
  44.1 4.5 %expand.1 = f32[4608,512]{1,0:T(8,128)} custom-call(f32[64,256]{1,0:T(8,128)S(1)} %pack.1.refs_0_, f32[64,256]{1,0:T(8,128)S(1)} %collective-permute-done.11.refs_1_, f32[64,256]{1,0:T(8,128)S(1)} %collective-permute-done.12.refs_2_, f32[64,256]{1,0:T(8,128)S(1)} %collective-permute-done.13.refs_3_, f32[64,256]{1,0:T(8,128)S(1)} %collective-permute-done.14.refs_4_, ...), custom_call_target="tpu_custom_call" | custom-call | flops 5500000256 | tf_op jit(solution)/shard_map/expand/pallas_call | solution.py:431
  (12 shorter events, 0.1 us)
Async XLA Ops:
  0.0 3.9 %copy-start.2 = (s32[18,256]{1,0:T(8,128)S(1)}, s32[18,256]{1,0:T(8,128)}, u32[]{:S(2)}) copy-start(s32[18,256]{1,0:T(8,128)} %order_ref.1) | copy-start | bytes 55300
  0.0 3.9 %copy-start.1 = (bf16[18,256,256]{2,1,0:T(8,128)(2,1)S(1)}, bf16[18,256,256]{2,1,0:T(8,128)(2,1)}, u32[]{:S(2)}) copy-start(bf16[18,256,256]{2,1,0:T(8,128)(2,1)} %inv_ref.1) | copy-start | bytes 7077892
  3.4 1.6 %collective-permute-start = (f32[64,384]{1,0:T(8,128)S(1)}, f32[64,384]{1,0:T(8,128)S(1)}, u32[]{:S(2)}, u32[]{:S(2)}) collective-permute-start(f32[64,384]{1,0:T(8,128)S(1)} %get-tuple-element.19), channel_id=1, source_target_pairs={{0,1},{1,0},{2,3},{3,2},{4,5},{5,4},{6,7},{7,6},{8,9},{9,8},{10,11... | collective-permute-start | bytes 294920 | tf_op jit(solution)/shard_map/ppermute | solution.py:29
  4.9 4.4 %slice-start = ((s8[4718592]{0:T(1024)(128)(4,1)}), s8[4194304]{0:T(1024)(128)(4,1)S(1)}, s32[]{:S(2)}) async-start(s8[4718592]{0:T(1024)(128)(4,1)} %bitcast), calls=%async_computation | async-start | bytes 8388608
  5.0 6.5 %collective-permute-start.1 = (f32[64,384]{1,0:T(8,128)S(1)}, f32[64,384]{1,0:T(8,128)S(1)}, u32[]{:S(2)}, u32[]{:S(2)}) collective-permute-start(f32[64,384]{1,0:T(8,128)S(1)} %add.2.after_ref.mine_ref), channel_id=1, source_target_pairs={{0,2},{1,3},{2,0},{3,1},{4,6},{5,7},{6,4},{7,5},{8,10},{9,11},{10,... | collective-permute-start | bytes 294920 | tf_op jit(solution)/shard_map/ppermute | solution.py:29
  7.7 1.6 %slice-start.1 = ((s8[4718592]{0:T(1024)(128)(4,1)}), s8[524288]{0:T(1024)(128)(4,1)S(1)}, s32[]{:S(2)}) async-start(s8[4718592]{0:T(1024)(128)(4,1)} %bitcast), calls=%async_computation.1 | async-start | bytes 1048576
  11.4 3.7 %collective-permute-start.2 = (f32[384,256]{1,0:T(8,128)S(1)}, f32[384,256]{1,0:T(8,128)S(1)}, u32[]{:S(2)}, u32[]{:S(2)}) collective-permute-start(f32[384,256]{1,0:T(8,128)S(1)} %project_other.1), channel_id=1, source_target_pairs={{0,1},{1,0},{2,3},{3,2},{4,5},{5,4},{6,7},{7,6},{8,9},{9,8},{10,11... | collective-permute-start | bytes 1179656 | tf_op jit(solution)/shard_map/ppermute | solution.py:29
  11.5 7.4 %copy-start.3 = (s32[3,128]{1,0:T(4,128)S(1)}, s32[3,128]{1,0:T(4,128)}, u32[]{:S(2)}) copy-start(s32[3,128]{1,0:T(4,128)} %perm_ref.1) | copy-start | bytes 4612
  11.5 9.6 %collective-permute-start.6 = (f32[64,384]{1,0:T(8,128)S(1)}, f32[64,384]{1,0:T(8,128)S(1)}, u32[]{:S(2)}, u32[]{:S(2)}) collective-permute-start(f32[64,384]{1,0:T(8,128)S(1)} %add.3.after_ref.mine_ref), channel_id=1, source_target_pairs={{0,4},{1,5},{2,6},{3,7},{4,0},{5,1},{6,2},{7,3},{8,12},{9,13},{10,... | collective-permute-start | bytes 294920 | tf_op jit(solution)/shard_map/ppermute | solution.py:29
  15.3 6.2 %collective-permute-start.3 = (f32[64,384]{1,0:T(8,128)S(1)}, f32[64,384]{1,0:T(8,128)S(1)}, u32[]{:S(2)}, u32[]{:S(2)}) collective-permute-start(f32[64,384]{1,0:T(8,128)S(1)} %get-tuple-element.21), channel_id=1, source_target_pairs={{0,2},{1,3},{2,0},{3,1},{4,6},{5,7},{6,4},{7,5},{8,10},{9,11},{10,... | collective-permute-start | bytes 294920 | tf_op jit(solution)/shard_map/ppermute | solution.py:29
  16.6 6.4 %collective-permute-start.4 = (f32[64,384]{1,0:T(8,128)S(1)}, f32[64,384]{1,0:T(8,128)S(1)}, u32[]{:S(2)}, u32[]{:S(2)}) collective-permute-start(f32[64,384]{1,0:T(8,128)S(1)} %get-tuple-element.22), channel_id=1, source_target_pairs={{0,4},{1,5},{2,6},{3,7},{4,0},{5,1},{6,2},{7,3},{8,12},{9,13},{10,... | collective-permute-start | bytes 294920 | tf_op jit(solution)/shard_map/ppermute | solution.py:29
  17.1 5.9 %collective-permute-start.5 = (f32[64,384]{1,0:T(8,128)S(1)}, f32[64,384]{1,0:T(8,128)S(1)}, u32[]{:S(2)}, u32[]{:S(2)}) collective-permute-start(f32[64,384]{1,0:T(8,128)S(1)} %get-tuple-element.23), channel_id=1, source_target_pairs={{0,6},{1,7},{2,4},{3,5},{4,2},{5,3},{6,0},{7,1},{8,14},{9,15},{10,... | collective-permute-start | bytes 294920 | tf_op jit(solution)/shard_map/ppermute | solution.py:29
  21.0 2.4 %collective-permute-start.7 = (f32[64,384]{1,0:T(8,128)S(1)}, f32[64,384]{1,0:T(8,128)S(1)}, u32[]{:S(2)}, u32[]{:S(2)}) collective-permute-start(f32[64,384]{1,0:T(8,128)S(1)} %add.3.after_ref.mine_ref), channel_id=1, source_target_pairs={{0,1},{1,0},{2,3},{3,2},{4,5},{5,4},{6,7},{7,6},{8,9},{9,8},{10,11... | collective-permute-start | bytes 294920 | tf_op jit(solution)/shard_map/ppermute | solution.py:29
  21.1 2.4 %collective-permute-start.8 = (f32[64,384]{1,0:T(8,128)S(1)}, f32[64,384]{1,0:T(8,128)S(1)}, u32[]{:S(2)}, u32[]{:S(2)}) collective-permute-start(f32[64,384]{1,0:T(8,128)S(1)} %collective-permute-done.6.theirs_ref), channel_id=1, source_target_pairs={{0,1},{1,0},{2,3},{3,2},{4,5},{5,4},{6,7},{7,6},{8,9},{9,8},{10,11... | collective-permute-start | bytes 294920 | tf_op jit(solution)/shard_map/ppermute | solution.py:29
  23.8 5.2 %collective-permute-start.9 = (f32[256,128]{1,0:T(8,128)S(1)}, f32[256,128]{1,0:T(8,128)S(1)}, u32[]{:S(2)}, u32[]{:S(2)}) collective-permute-start(f32[256,128]{1,0:T(8,128)S(1)} %correct.1.sent_ref), channel_id=1, source_target_pairs={{0,8},{8,0},{16,24},{24,16},{1,9},{9,1},{17,25},{25,17},{2,10},{10... | collective-permute-start | bytes 393224 | tf_op jit(solution)/shard_map/ppermute | solution.py:29
  25.5 9.2 %collective-permute-start.16 = (f32[64,128]{1,0:T(8,128)S(1)}, f32[64,128]{1,0:T(8,128)S(1)}, u32[]{:S(2)}, u32[]{:S(2)}) collective-permute-start(f32[64,128]{1,0:T(8,128)S(1)} %get-tuple-element.24.own_ref.refs_0_), channel_id=1, source_target_pairs={{0,2},{1,3},{2,0},{3,1},{4,6},{5,7},{6,4},{7,5},{8,10},{9,11},{10,... | collective-permute-start | bytes 98312 | tf_op jit(solution)/shard_map/ppermute | solution.py:29
  26.6 8.1 %collective-permute-start.17 = (f32[64,128]{1,0:T(8,128)S(1)}, f32[64,128]{1,0:T(8,128)S(1)}, u32[]{:S(2)}, u32[]{:S(2)}) collective-permute-start(f32[64,128]{1,0:T(8,128)S(1)} %get-tuple-element.25.other_ref), channel_id=1, source_target_pairs={{0,4},{1,5},{2,6},{3,7},{4,0},{5,1},{6,2},{7,3},{8,12},{9,13},{10,... | collective-permute-start | bytes 98312 | tf_op jit(solution)/shard_map/ppermute | solution.py:29
  27.4 7.3 %collective-permute-start.18 = (f32[64,128]{1,0:T(8,128)S(1)}, f32[64,128]{1,0:T(8,128)S(1)}, u32[]{:S(2)}, u32[]{:S(2)}) collective-permute-start(f32[64,128]{1,0:T(8,128)S(1)} %get-tuple-element.25.other_ref), channel_id=1, source_target_pairs={{0,6},{1,7},{2,4},{3,5},{4,2},{5,3},{6,0},{7,1},{8,14},{9,15},{10,... | collective-permute-start | bytes 98312 | tf_op jit(solution)/shard_map/ppermute | solution.py:29
  29.8 5.0 %collective-permute-start.10 = (f32[64,128]{1,0:T(8,128)S(1)}, f32[64,128]{1,0:T(8,128)S(1)}, u32[]{:S(2)}, u32[]{:S(2)}) collective-permute-start(f32[64,128]{1,0:T(8,128)S(1)} %get-tuple-element.28.sent_ref), channel_id=1, source_target_pairs={{0,16},{8,24},{16,0},{24,8},{1,17},{9,25},{17,1},{25,9},{2,18},{10... | collective-permute-start | bytes 98312 | tf_op jit(solution)/shard_map/ppermute | solution.py:29
  34.8 4.5 %copy-start = (bf16[3,4608,128]{2,1,0:T(8,128)(2,1)S(1)}, bf16[3,4608,128]{2,1,0:T(8,128)(2,1)}, u32[]{:S(2)}) copy-start(bf16[3,4608,128]{2,1,0:T(8,128)(2,1)} %refs_9_.1) | copy-start | bytes 10616836
  34.8 4.5 %collective-permute-start.19 = (f32[4,64,128]{2,1,0:T(8,128)S(1)}, f32[4,64,128]{2,1,0:T(8,128)S(1)}, u32[]{:S(2)}, u32[]{:S(2)}) collective-permute-start(f32[4,64,128]{2,1,0:T(8,128)S(1)} %stack.1.own_ref), channel_id=1, source_target_pairs={{0,1},{1,0},{2,3},{3,2},{4,5},{5,4},{6,7},{7,6},{8,9},{9,8},{10,11... | collective-permute-start | bytes 393224 | tf_op jit(solution)/shard_map/ppermute | solution.py:29
  35.2 7.6 %collective-permute-start.11 = (f32[64,256]{1,0:T(8,128)S(1)}, f32[64,256]{1,0:T(8,128)S(1)}, u32[]{:S(2)}, u32[]{:S(2)}) collective-permute-start(f32[64,256]{1,0:T(8,128)S(1)} %pack.1.refs_0_), channel_id=1, source_target_pairs={{0,1},{1,0},{2,3},{3,2},{4,5},{5,4},{6,7},{7,6},{8,9},{9,8},{10,11... | collective-permute-start | bytes 196616 | tf_op jit(solution)/shard_map/ppermute | solution.py:29
  35.8 5.1 %collective-permute-start.12 = (f32[64,256]{1,0:T(8,128)S(1)}, f32[64,256]{1,0:T(8,128)S(1)}, u32[]{:S(2)}, u32[]{:S(2)}) collective-permute-start(f32[64,256]{1,0:T(8,128)S(1)} %pack.1.refs_0_), channel_id=1, source_target_pairs={{0,2},{1,3},{2,0},{3,1},{4,6},{5,7},{6,4},{7,5},{8,10},{9,11},{10,... | collective-permute-start | bytes 196616 | tf_op jit(solution)/shard_map/ppermute | solution.py:29
  36.8 5.0 %collective-permute-start.14 = (f32[64,256]{1,0:T(8,128)S(1)}, f32[64,256]{1,0:T(8,128)S(1)}, u32[]{:S(2)}, u32[]{:S(2)}) collective-permute-start(f32[64,256]{1,0:T(8,128)S(1)} %pack.1.refs_0_), channel_id=1, source_target_pairs={{0,4},{1,5},{2,6},{3,7},{4,0},{5,1},{6,2},{7,3},{8,12},{9,13},{10,... | collective-permute-start | bytes 196616 | tf_op jit(solution)/shard_map/ppermute | solution.py:29
  37.6 5.2 %collective-permute-start.20 = (f32[64,256]{1,0:T(8,128)S(1)}, f32[64,256]{1,0:T(8,128)S(1)}, u32[]{:S(2)}, u32[]{:S(2)}) collective-permute-start(f32[64,256]{1,0:T(8,128)S(1)} %pack.1.refs_0_), channel_id=1, source_target_pairs={{0,6},{1,7},{2,4},{3,5},{4,2},{5,3},{6,0},{7,1},{8,14},{9,15},{10,... | collective-permute-start | bytes 196616 | tf_op jit(solution)/shard_map/ppermute | solution.py:29
  40.9 1.9 %collective-permute-start.13 = (f32[64,256]{1,0:T(8,128)S(1)}, f32[64,256]{1,0:T(8,128)S(1)}, u32[]{:S(2)}, u32[]{:S(2)}) collective-permute-start(f32[64,256]{1,0:T(8,128)S(1)} %collective-permute-done.12.refs_2_), channel_id=1, source_target_pairs={{0,1},{1,0},{2,3},{3,2},{4,5},{5,4},{6,7},{7,6},{8,9},{9,8},{10,11... | collective-permute-start | bytes 196616 | tf_op jit(solution)/shard_map/ppermute | solution.py:29
  41.8 1.3 %collective-permute-start.15 = (f32[64,256]{1,0:T(8,128)S(1)}, f32[64,256]{1,0:T(8,128)S(1)}, u32[]{:S(2)}, u32[]{:S(2)}) collective-permute-start(f32[64,256]{1,0:T(8,128)S(1)} %collective-permute-done.14.refs_4_), channel_id=1, source_target_pairs={{0,1},{1,0},{2,3},{3,2},{4,5},{5,4},{6,7},{7,6},{8,9},{9,8},{10,11... | collective-permute-start | bytes 196616 | tf_op jit(solution)/shard_map/ppermute | solution.py:29
  42.8 1.3 %collective-permute-start.21 = (f32[64,256]{1,0:T(8,128)S(1)}, f32[64,256]{1,0:T(8,128)S(1)}, u32[]{:S(2)}, u32[]{:S(2)}) collective-permute-start(f32[64,256]{1,0:T(8,128)S(1)} %relay.1.refs_6_), channel_id=1, source_target_pairs={{0,1},{1,0},{2,3},{3,2},{4,5},{5,4},{6,7},{7,6},{8,9},{9,8},{10,11... | collective-permute-start | bytes 196616 | tf_op jit(solution)/shard_map/ppermute | solution.py:29

commit v14 on v13

--- a/solution.py
+++ b/solution.py
@@ -88,19 +88,39 @@
     lax.fori_loop(0, inv_ref.shape[0] // per_step, body, 0)
 
 
-def weigh_kernel(per_step, width, moved_ref, flip_ref, after_ref, factor_ref):
-    kinds = flip_ref.shape[0]
-
-    def body(step, _):
-        for b in range(per_step):
-            block = step * per_step + b
-            lanes = pl.ds(pl.multiple_of(block * width, width), width)
-            high_part, low_part = halves(dot(flip_ref[:, lanes], moved_ref[block], (1, 0)))
-            factor_ref[:kinds, lanes] = high_part
-            factor_ref[kinds:, lanes] = low_part
-        return 0
-
-    lax.fori_loop(0, moved_ref.shape[0] // per_step, body, 0)
+def other_lanes(part, other=True):
+    core = lax.axis_index("rows") % 2
+    return pl.ds(pl.multiple_of((1 - core if other else core) * part, part), part)
+
+
+def weigh_kernel(per_step, width, moved_ref, flip_ref, after_ref, rhs_ref,
+                 factor_ref, rhs_out, out_ref, total_ref, sems):
+    kinds, part = out_ref.shape
+    tile = per_step * width
+    steps = rhs_out.shape[0] // tile
+    lanes = other_lanes(part)
+    copies = []
+    for step in range(steps):
+        rows = pl.ds(step * tile, tile)
+        copies.append(pltpu.make_async_copy(rhs_ref.at[rows], rhs_out.at[rows], sems.at[step]))
+        copies[-1].start(priority=step % 2)
+
+    def weigh(step):
+        for block in range(step * per_step, (step + 1) * per_step):
+            spot = pl.ds(block * width, width)
+            high_part, low_part = halves(dot(flip_ref[:, spot], moved_ref[block], (1, 0)))
+            factor_ref[:kinds, spot] = high_part
+            factor_ref[kinds:, spot] = low_part
+
+    weigh(0)
+    for step in range(steps):
+        if step + 1 < steps:
+            weigh(step + 1)
+        copies[step].wait()
+        rows = pl.ds(step * tile, tile)
+        term = dot(factor_ref[:, rows], rhs_out[rows, lanes], (1, 0))
+        total_ref[...] = term if step == 0 else total_ref[...] + term
+    out_ref[...] = total_ref[:kinds] + total_ref[kinds:]
 
 
 def solve_kernel(per_step, width, moved_ref, rhs_ref, *refs):
@@ -116,11 +136,9 @@
     lax.fori_loop(0, moved_ref.shape[0] // per_step, body, 0)
 
 
-def project_kernel(other, factor_ref, rhs_ref, after_ref, out_ref):
+def project_kernel(factor_ref, rhs_ref, after_ref, out_ref):
     kinds, part = out_ref.shape
-    core = lax.axis_index("rows") % 2
-    lanes = pl.ds(pl.multiple_of((1 - core if other else core) * part, part), part)
-    total = dot(factor_ref[...], rhs_ref[:, lanes], (1, 0))
+    total = dot(factor_ref[...], rhs_ref[:, other_lanes(part, False)], (1, 0))
     out_ref[...] = total[:kinds] + total[kinds:]
 
 
@@ -327,28 +345,29 @@
         )(mine, got)
 
     gram = add(gram_keep, gram_got)
-    factors = pl.pallas_call(
-        functools.partial(weigh_kernel, blocks_per_step(nblocks, 9), width),
-        out_shape=jax.ShapeDtypeStruct((2 * kinds, rows), jnp.bfloat16),
+    factors, rhs, send = pl.pallas_call(
+        functools.partial(weigh_kernel, per_step, width),
+        in_specs=[pl.BlockSpec()] * 3 + [pl.BlockSpec(memory_space=pltpu.HBM)],
+        out_shape=[
+            jax.ShapeDtypeStruct((2 * kinds, rows), jnp.bfloat16),
+            jax.ShapeDtypeStruct((rows, columns), jnp.bfloat16),
+            floats(kinds, columns // 2),
+        ],
+        scratch_shapes=[
+            pltpu.VMEM((2 * kinds, columns // 2), jnp.float32),
+            pltpu.SemaphoreType.DMA((nblocks // per_step,)),
+        ],
         name="weigh",
-        **settings(8, 2.4),
-    )(moved, flipped, gram)
-
-    def project(other, after):
-        return pl.pallas_call(
-            functools.partial(project_kernel, other),
-            out_shape=floats(kinds, columns // 2),
-            name="project_other" if other else "project_own",
-            **settings(12, 1 if other else 4),
-        )(factors, rhs, after)
-
-    send = project(True, gram)
+        **settings(12, 2),
+    )(moved, flipped, gram, pltpu.with_memory_space_constraint(rhs, pltpu.HBM))
     got = swap(send, "rows", 1)
     mask = 2
     while mask < slots:
         gram = add(gram, swap(gram, "rows", mask))
         mask *= 2
-    keep = project(False, gram)
+    keep = pl.pallas_call(
+        project_kernel, out_shape=floats(kinds, columns // 2), name="project", **settings(12, 4),
+    )(factors, rhs, gram)
     merged = pl.pallas_call(
         merge_kernel,
         out_shape=[floats(share, kinds)] * slots,
@@ -423,7 +442,7 @@
     pieces = []
     for slot in range(slots):
         piece = swap(pack, "rows", 2 * slot) if slot > 0 else pack
-        if slot == slots - 1:
+        if slot in (0, slots - 1):
             piece = pl.pallas_call(
                 relay_kernel, out_shape=floats(share, size), name="relay", **settings(8, 0.1),
             )(second, piece)

time: 48.7 us -> 50.4 us (1.035)
  Pallas kernels: 22.5 us -> 25.2 us
  waiting for transfers between devices: 4.58 us -> 4.01 us
    pallas_call x3 -> x2, Pallas kernels: 5.59 us -> 8.04 us  [the longest x1 6.05 us: per_device(): pl.pallas_call(functools.partial(weigh_kernel, per_step, width), in_specs...]
    ppermute x22, waiting for transfers between devices: 4.58 us -> 4.01 us  [swap(): return lax.ppermute(value, axis, [(i, i ^ mask) for i in range(count)])]
  transfers between devices with their start and end apart: 22 -> 22, of which waited for: 5 -> 8; matrix products, arithmetic and copies ran while one was open for 0% -> 0% of each run, Pallas kernels for 29% -> 34%
where the time goes in v14:
time: 50.4 us; the launch traced here: 50.3 us
  Pallas kernels  25.2 us (50%)
  starting transfers between devices  20.7 us (41%)
  waiting for transfers between devices  4.01 us (8%)
    ppermute x22, starting transfers between devices, swap(): return lax.ppermute(value, axis, [(i, i ^ mask) for i in range(count)])  20.7 us
    pallas_call x1, Pallas kernels, per_device(): pl.pallas_call(functools.partial(weigh_kernel, per_step, width), in_specs...  6.05 us
    pallas_call x1, Pallas kernels, per_device(): pl.pallas_call(functools.partial(expand_kernel, levels, per_step * width,...  4.5 us
    ppermute x22, waiting for transfers between devices, swap(): return lax.ppermute(value, axis, [(i, i ^ mask) for i in range(count)])  4.01 us
    pallas_call x1, Pallas kernels, per_device(): pl.pallas_call(functools.partial(gram_kernel, levels, per_step, width), i...  3.34 us
    pallas_call x1, Pallas kernels, per_device(): pl.pallas_call(functools.partial(solve_kernel, per_step, width), out_shap...  2.4 us
    pallas_call x1, Pallas kernels, per_device(): pl.pallas_call(functools.partial(prepare_kernel, levels), in_specs=[pl.Bl...  2.11 us
    pallas_call x1, Pallas kernels, per_device(): pl.pallas_call(project_kernel, out_shape=floats(kinds, columns // 2), nam...  1.99 us
  transfers between devices with their start and end apart: 22, of which 8 were waited for; matrix products, arithmetic and copies ran while one was open for 0% of the time, Pallas kernels for 34%

profile of v14, /device:TPU:0, one launch (start us, length us, event | category | flops | bytes accessed | tf_op | source)
XLA Modules:
  0.0 50.3 jit_solution(13035477462258721174)
XLA Ops:
  0.0 0.0 copy-start.2
  0.0 0.0 copy-start.1
  0.0 3.3 %gram.1 = (bf16[384,4608]{1,0:T(8,128)(2,1)S(1)}, f32[64,384]{1,0:T(8,128)S(1)}, f32[64,384]{1,0:T(8,128)S(1)}) custom-call(bf16[3,4608,128]{2,1,0:T(8,128)(2,1)} %right_ref.1, bf16[3,4608,128]{2,1,0:T(8,128)(2,1)} %refs_9_.1), custom_call_target="tpu_custom_call" | custom-call | flops 3300000000 | tf_op jit(solution)/shard_map/gram/pallas_call | solution.py:319
  3.4 0.5 %collective-permute-start = (f32[64,384]{1,0:T(8,128)S(1)}, f32[64,384]{1,0:T(8,128)S(1)}, u32[]{:S(2)}, u32[]{:S(2)}) collective-permute-start(f32[64,384]{1,0:T(8,128)S(1)} %get-tuple-element.22), channel_id=1, source_target_pairs={{0,1},{1,0},{2,3},{3,2},{4,5},{5,4},{6,7},{7,6},{8,9},{9,8},{10,11... | collective-permute-start | bytes 294920 | tf_op jit(solution)/shard_map/ppermute | solution.py:29
  3.9 0.0 copy-done.2
  3.9 0.0 copy-done.1
  3.9 1.0 %permute.1.moved_ref = bf16[18,256,256]{2,1,0:T(8,128)(2,1)S(1)} custom-call(s32[18,256]{1,0:T(8,128)S(1)} %copy-done.2, bf16[18,256,256]{2,1,0:T(8,128)(2,1)S(1)} %copy-done.1), custom_call_target="tpu_custom_call" | custom-call | flops 1650000000 | tf_op jit(solution)/shard_map/permute/pallas_call | solution.py:335
  4.9 0.0 collective-permute-done.got_ref
  4.9 2.8 %collective-permute-start.1 = (f32[64,384]{1,0:T(8,128)S(1)}, f32[64,384]{1,0:T(8,128)S(1)}, u32[]{:S(2)}, u32[]{:S(2)}) collective-permute-start(f32[64,384]{1,0:T(8,128)S(1)} %add.2.after_ref.mine_ref), channel_id=1, source_target_pairs={{0,2},{1,3},{2,0},{3,1},{4,6},{5,7},{6,4},{7,5},{8,10},{9,11},{10,... | collective-permute-start | bytes 294920 | tf_op jit(solution)/shard_map/ppermute | solution.py:29
  7.7 6.1 %weigh.1 = (bf16[768,4608]{1,0:T(8,128)(2,1)S(1)}, bf16[4608,512]{1,0:T(8,128)(2,1)S(1)}, f32[384,256]{1,0:T(8,128)S(1)}) custom-call(bf16[18,256,256]{2,1,0:T(8,128)(2,1)S(1)} %permute.1.moved_ref, bf16[384,4608]{1,0:T(8,128)(2,1)S(1)} %get-tuple-element.20.flip_ref, f32[64,384]{1,0:T(8,128)S(1)} %add.2.after_ref.mine_ref, bf16[4608,512]{1,0:T(8,128)(2,1)} %rhs_ref.1), custom_call_target="tpu_custom_call" | custom-call | flops 2200000000 | tf_op jit(solution)/shard_map/weigh/pallas_call | solution.py:348
  13.8 0.1 collective-permute-start.2
  13.9 0.0 collective-permute-done.1.got_ref
  13.9 1.6 %collective-permute-start.10 = (f32[64,384]{1,0:T(8,128)S(1)}, f32[64,384]{1,0:T(8,128)S(1)}, u32[]{:S(2)}, u32[]{:S(2)}) collective-permute-start(f32[64,384]{1,0:T(8,128)S(1)} %add.3.after_ref.mine_ref), channel_id=1, source_target_pairs={{0,4},{1,5},{2,6},{3,7},{4,0},{5,1},{6,2},{7,3},{8,12},{9,13},{10,... | collective-permute-start | bytes 294920 | tf_op jit(solution)/shard_map/ppermute | solution.py:29
  15.5 2.0 %project.1.keep_ref = f32[384,256]{1,0:T(8,128)S(1)} custom-call(bf16[768,4608]{1,0:T(8,128)(2,1)S(1)} %get-tuple-element.24.factor_ref, bf16[4608,512]{1,0:T(8,128)(2,1)S(1)} %get-tuple-element.23.rhs_ref, f32[64,384]{1,0:T(8,128)S(1)} %add.3.after_ref.mine_ref), custom_call_target="tpu_custom_call" | custom-call | flops 4400000000 | tf_op jit(solution)/shard_map/project/pallas_call | solution.py:368
  17.5 0.0 collective-permute-done.2.got_ref
  17.5 0.2 merge.1
  17.7 0.6 %collective-permute-start.3 = (f32[64,384]{1,0:T(8,128)S(1)}, f32[64,384]{1,0:T(8,128)S(1)}, u32[]{:S(2)}, u32[]{:S(2)}) collective-permute-start(f32[64,384]{1,0:T(8,128)S(1)} %get-tuple-element.27), channel_id=1, source_target_pairs={{0,2},{1,3},{2,0},{3,1},{4,6},{5,7},{6,4},{7,5},{8,10},{9,11},{10,... | collective-permute-start | bytes 294920 | tf_op jit(solution)/shard_map/ppermute | solution.py:29
  18.3 0.2 collective-permute-start.4
  18.5 2.7 %collective-permute-start.5 = (f32[64,384]{1,0:T(8,128)S(1)}, f32[64,384]{1,0:T(8,128)S(1)}, u32[]{:S(2)}, u32[]{:S(2)}) collective-permute-start(f32[64,384]{1,0:T(8,128)S(1)} %get-tuple-element.29), channel_id=1, source_target_pairs={{0,6},{1,7},{2,4},{3,5},{4,2},{5,3},{6,0},{7,1},{8,14},{9,15},{10,... | collective-permute-start | bytes 294920 | tf_op jit(solution)/shard_map/ppermute | solution.py:29
  21.3 0.0 copy-done.3
  21.3 2.1 %prepare.1.refs_4_.joined_ref = f32[3,256,256]{2,1,0:T(8,128)S(1)} custom-call(f32[7,256,256]{2,1,0:T(8,128)} %joined_ref.1, s32[3,128]{1,0:T(4,128)S(1)} %copy-done.3), custom_call_target="tpu_custom_call" | custom-call | flops 2200000000 | tf_op jit(solution)/shard_map/prepare/pallas_call | solution.py:381
  23.4 0.1 collective-permute-start.11
  23.5 0.0 collective-permute-done.10.theirs_ref
  23.5 0.5 collective-permute-start.12
  24.0 0.0 collective-permute-done.3.refs_1_
  24.0 1.1 %collective-permute-done.4.refs_2_ = f32[64,384]{1,0:T(8,128)S(1)} collective-permute-done((f32[64,384]{1,0:T(8,128)S(1)}, f32[64,384]{1,0:T(8,128)S(1)}, u32[]{:S(2)}, u32[]{:S(2)}) %collective-permute-start.4) | collective-permute-done | bytes 98336 | tf_op jit(solution)/shard_map/ppermute | solution.py:29
  25.1 0.0 collective-permute-done.5.refs_3_
  25.1 0.4 node.1
  25.4 0.0 collective-permute-done.11.pair_mine_ref
  25.4 0.0 collective-permute-done.12.pair_theirs_ref
  25.5 0.4 correct.1.sent_ref
  25.8 1.6 %collective-permute-start.13 = (f32[256,128]{1,0:T(8,128)S(1)}, f32[256,128]{1,0:T(8,128)S(1)}, u32[]{:S(2)}, u32[]{:S(2)}) collective-permute-start(f32[256,128]{1,0:T(8,128)S(1)} %correct.1.sent_ref), channel_id=1, source_target_pairs={{0,8},{8,0},{16,24},{24,16},{1,9},{9,1},{17,25},{25,17},{2,10},{10... | collective-permute-start | bytes 393224 | tf_op jit(solution)/shard_map/ppermute | solution.py:29
  27.5 1.5 %collective-permute-start.6 = (f32[64,128]{1,0:T(8,128)S(1)}, f32[64,128]{1,0:T(8,128)S(1)}, u32[]{:S(2)}, u32[]{:S(2)}) collective-permute-start(f32[64,128]{1,0:T(8,128)S(1)} %get-tuple-element.30.refs_0_.own_ref), channel_id=1, source_target_pairs={{0,2},{1,3},{2,0},{3,1},{4,6},{5,7},{6,4},{7,5},{8,10},{9,11},{10,... | collective-permute-start | bytes 98312 | tf_op jit(solution)/shard_map/ppermute | solution.py:29
  29.0 0.8 %collective-permute-start.7 = (f32[64,128]{1,0:T(8,128)S(1)}, f32[64,128]{1,0:T(8,128)S(1)}, u32[]{:S(2)}, u32[]{:S(2)}) collective-permute-start(f32[64,128]{1,0:T(8,128)S(1)} %get-tuple-element.31.other_ref), channel_id=1, source_target_pairs={{0,4},{1,5},{2,6},{3,7},{4,0},{5,1},{6,2},{7,3},{8,12},{9,13},{10,... | collective-permute-start | bytes 98312 | tf_op jit(solution)/shard_map/ppermute | solution.py:29
  29.8 1.2 %collective-permute-start.8 = (f32[64,128]{1,0:T(8,128)S(1)}, f32[64,128]{1,0:T(8,128)S(1)}, u32[]{:S(2)}, u32[]{:S(2)}) collective-permute-start(f32[64,128]{1,0:T(8,128)S(1)} %get-tuple-element.31.other_ref), channel_id=1, source_target_pairs={{0,6},{1,7},{2,4},{3,5},{4,2},{5,3},{6,0},{7,1},{8,14},{9,15},{10,... | collective-permute-start | bytes 98312 | tf_op jit(solution)/shard_map/ppermute | solution.py:29
  31.0 0.1 collective-permute-done.13.got_ref.after_ref
  31.1 0.8 %level1.1 = (f32[64,128]{1,0:T(8,128)S(1)}, f32[64,128]{1,0:T(8,128)S(1)}) custom-call(f32[256,128]{1,0:T(8,128)S(1)} %correct.1.sent_ref, f32[256,128]{1,0:T(8,128)S(1)} %collective-permute-done.13.got_ref.after_ref, f32[3,256,256]{2,1,0:T(8,128)S(1)} %prepare.1.refs_4_.joined_ref, f32[256,128]{1,0:T(8,128)S(1)} %collective-permute-done.13.got_ref.after_ref), custom_call_target="tpu_custom_call" | custom-call | flops 6600000000 | tf_op jit(solution)/shard_map/level1/pallas_call | solution.py:417
  31.9 2.6 %collective-permute-start.14 = (f32[64,128]{1,0:T(8,128)S(1)}, f32[64,128]{1,0:T(8,128)S(1)}, u32[]{:S(2)}, u32[]{:S(2)}) collective-permute-start(f32[64,128]{1,0:T(8,128)S(1)} %get-tuple-element.34.sent_ref), channel_id=1, source_target_pairs={{0,16},{8,24},{16,0},{24,8},{1,17},{9,25},{17,1},{25,9},{2,18},{10... | collective-permute-start | bytes 98312 | tf_op jit(solution)/shard_map/ppermute | solution.py:29
  34.5 2.4 %solve.1.after_ref.first_ref = f32[4608,512]{1,0:T(8,128)S(1)} custom-call(bf16[18,256,256]{2,1,0:T(8,128)(2,1)S(1)} %permute.1.moved_ref, bf16[4608,512]{1,0:T(8,128)(2,1)S(1)} %get-tuple-element.23.rhs_ref, f32[64,384]{1,0:T(8,128)S(1)} %get-tuple-element.26.refs_0_), custom_call_target="tpu_custom_call" | custom-call | flops 8800000000 | tf_op jit(solution)/shard_map/solve/pallas_call | solution.py:406
  37.0 0.0 collective-permute-done.6.refs_1_
  37.0 0.0 collective-permute-done.7.refs_2_
  37.0 0.0 collective-permute-done.8.refs_3_
  37.0 0.0 copy-start
  37.0 0.1 collective-permute-start.9
  37.1 0.0 collective-permute-done.14.got_ref
  37.1 0.4 level2.1.refs_1_
  37.5 1.6 %collective-permute-start.20 = (f32[64,256]{1,0:T(8,128)S(1)}, f32[64,256]{1,0:T(8,128)S(1)}, u32[]{:S(2)}, u32[]{:S(2)}) collective-permute-start(f32[64,256]{1,0:T(8,128)S(1)} %pack.1.ref), channel_id=1, source_target_pairs={{0,6},{1,7},{2,4},{3,5},{4,2},{5,3},{6,0},{7,1},{8,14},{9,15},{10,... | collective-permute-start | bytes 196616 | tf_op jit(solution)/shard_map/ppermute | solution.py:29
  39.1 0.9 %collective-permute-start.16 = (f32[64,256]{1,0:T(8,128)S(1)}, f32[64,256]{1,0:T(8,128)S(1)}, u32[]{:S(2)}, u32[]{:S(2)}) collective-permute-start(f32[64,256]{1,0:T(8,128)S(1)} %pack.1.ref), channel_id=1, source_target_pairs={{0,2},{1,3},{2,0},{3,1},{4,6},{5,7},{6,4},{7,5},{8,10},{9,11},{10,... | collective-permute-start | bytes 196616 | tf_op jit(solution)/shard_map/ppermute | solution.py:29
  40.1 1.0 %collective-permute-start.18 = (f32[64,256]{1,0:T(8,128)S(1)}, f32[64,256]{1,0:T(8,128)S(1)}, u32[]{:S(2)}, u32[]{:S(2)}) collective-permute-start(f32[64,256]{1,0:T(8,128)S(1)} %pack.1.ref), channel_id=1, source_target_pairs={{0,4},{1,5},{2,6},{3,7},{4,0},{5,1},{6,2},{7,3},{8,12},{9,13},{10,... | collective-permute-start | bytes 196616 | tf_op jit(solution)/shard_map/ppermute | solution.py:29
  41.0 0.0 collective-permute-done.9.pair_ref
  41.0 0.0 copy-done
  41.0 1.6 %apply.1.after_ref.refs_8_ = f32[4608,512]{1,0:T(8,128)S(1)} custom-call(f32[4,64,128]{2,1,0:T(8,128)S(1)} %stack.1.own_ref, f32[4,64,128]{2,1,0:T(8,128)S(1)} %collective-permute-done.9.pair_ref, f32[4608,512]{1,0:T(8,128)S(1)} %solve.1.after_ref.first_ref, bf16[3,4608,128]{2,1,0:T(8,128)(2,1)S(1)} %copy-done), custom_call_target="tpu_custom_call" | custom-call | flops 1980000000 | tf_op jit(solution)/shard_map/apply/pallas_call | solution.py:428
  42.6 0.1 collective-permute-start.15
  42.7 0.6 %collective-permute-done.20.ref = f32[64,256]{1,0:T(8,128)S(1)} collective-permute-done((f32[64,256]{1,0:T(8,128)S(1)}, f32[64,256]{1,0:T(8,128)S(1)}, u32[]{:S(2)}, u32[]{:S(2)}) %collective-permute-start.20) | collective-permute-done | bytes 65568 | tf_op jit(solution)/shard_map/ppermute | solution.py:29
  43.3 0.0 collective-permute-start.21
  43.3 0.6 %collective-permute-done.16.refs_2_ = f32[64,256]{1,0:T(8,128)S(1)} collective-permute-done((f32[64,256]{1,0:T(8,128)S(1)}, f32[64,256]{1,0:T(8,128)S(1)}, u32[]{:S(2)}, u32[]{:S(2)}) %collective-permute-start.16) | collective-permute-done | bytes 65568 | tf_op jit(solution)/shard_map/ppermute | solution.py:29
  43.9 0.0 collective-permute-start.17
  43.9 0.4 collective-permute-done.18.refs_4_
  44.3 0.1 collective-permute-start.19
  44.5 0.0 collective-permute-done.15.refs_1_
  44.5 0.1 collective-permute-done.21.refs_7_
  44.6 0.6 %collective-permute-done.17.refs_3_ = f32[64,256]{1,0:T(8,128)S(1)} collective-permute-done((f32[64,256]{1,0:T(8,128)S(1)}, f32[64,256]{1,0:T(8,128)S(1)}, u32[]{:S(2)}, u32[]{:S(2)}) %collective-permute-start.17) | collective-permute-done | bytes 65568 | tf_op jit(solution)/shard_map/ppermute | solution.py:29
  45.2 0.4 collective-permute-done.19.refs_5_
  45.6 4.5 %expand.1 = f32[4608,512]{1,0:T(8,128)} custom-call(f32[64,256]{1,0:T(8,128)S(1)} %relay.2.refs_0_, f32[64,256]{1,0:T(8,128)S(1)} %collective-permute-done.15.refs_1_, f32[64,256]{1,0:T(8,128)S(1)} %collective-permute-done.16.refs_2_, f32[64,256]{1,0:T(8,128)S(1)} %collective-permute-done.17.refs_3_, f32[64,256]{1,0:T(8,128)S(1)} %collective-permute-done.18.refs_4_, ...), custom_call_target="tpu_custom_call" | custom-call | flops 5500000256 | tf_op jit(solution)/shard_map/expand/pallas_call | solution.py:450
  (7 shorter events, 0.1 us)
Async XLA Ops:
  0.0 3.9 %copy-start.2 = (s32[18,256]{1,0:T(8,128)S(1)}, s32[18,256]{1,0:T(8,128)}, u32[]{:S(2)}) copy-start(s32[18,256]{1,0:T(8,128)} %order_ref.1) | copy-start | bytes 55300
  0.0 3.9 %copy-start.1 = (bf16[18,256,256]{2,1,0:T(8,128)(2,1)S(1)}, bf16[18,256,256]{2,1,0:T(8,128)(2,1)}, u32[]{:S(2)}) copy-start(bf16[18,256,256]{2,1,0:T(8,128)(2,1)} %inv_ref.1) | copy-start | bytes 7077892
  3.4 1.6 %collective-permute-start = (f32[64,384]{1,0:T(8,128)S(1)}, f32[64,384]{1,0:T(8,128)S(1)}, u32[]{:S(2)}, u32[]{:S(2)}) collective-permute-start(f32[64,384]{1,0:T(8,128)S(1)} %get-tuple-element.22), channel_id=1, source_target_pairs={{0,1},{1,0},{2,3},{3,2},{4,5},{5,4},{6,7},{7,6},{8,9},{9,8},{10,11... | collective-permute-start | bytes 294920 | tf_op jit(solution)/shard_map/ppermute | solution.py:29
  4.9 8.9 %collective-permute-start.1 = (f32[64,384]{1,0:T(8,128)S(1)}, f32[64,384]{1,0:T(8,128)S(1)}, u32[]{:S(2)}, u32[]{:S(2)}) collective-permute-start(f32[64,384]{1,0:T(8,128)S(1)} %add.2.after_ref.mine_ref), channel_id=1, source_target_pairs={{0,2},{1,3},{2,0},{3,1},{4,6},{5,7},{6,4},{7,5},{8,10},{9,11},{10,... | collective-permute-start | bytes 294920 | tf_op jit(solution)/shard_map/ppermute | solution.py:29
  13.8 3.7 %collective-permute-start.2 = (f32[384,256]{1,0:T(8,128)S(1)}, f32[384,256]{1,0:T(8,128)S(1)}, u32[]{:S(2)}, u32[]{:S(2)}) collective-permute-start(f32[384,256]{1,0:T(8,128)S(1)} %get-tuple-element.25), channel_id=1, source_target_pairs={{0,1},{1,0},{2,3},{3,2},{4,5},{5,4},{6,7},{7,6},{8,9},{9,8},{10,11... | collective-permute-start | bytes 1179656 | tf_op jit(solution)/shard_map/ppermute | solution.py:29
  13.9 9.6 %collective-permute-start.10 = (f32[64,384]{1,0:T(8,128)S(1)}, f32[64,384]{1,0:T(8,128)S(1)}, u32[]{:S(2)}, u32[]{:S(2)}) collective-permute-start(f32[64,384]{1,0:T(8,128)S(1)} %add.3.after_ref.mine_ref), channel_id=1, source_target_pairs={{0,4},{1,5},{2,6},{3,7},{4,0},{5,1},{6,2},{7,3},{8,12},{9,13},{10,... | collective-permute-start | bytes 294920 | tf_op jit(solution)/shard_map/ppermute | solution.py:29
  15.5 5.8 %copy-start.3 = (s32[3,128]{1,0:T(4,128)S(1)}, s32[3,128]{1,0:T(4,128)}, u32[]{:S(2)}) copy-start(s32[3,128]{1,0:T(4,128)} %perm_ref.1) | copy-start | bytes 4612
  17.7 6.3 %collective-permute-start.3 = (f32[64,384]{1,0:T(8,128)S(1)}, f32[64,384]{1,0:T(8,128)S(1)}, u32[]{:S(2)}, u32[]{:S(2)}) collective-permute-start(f32[64,384]{1,0:T(8,128)S(1)} %get-tuple-element.27), channel_id=1, source_target_pairs={{0,2},{1,3},{2,0},{3,1},{4,6},{5,7},{6,4},{7,5},{8,10},{9,11},{10,... | collective-permute-start | bytes 294920 | tf_op jit(solution)/shard_map/ppermute | solution.py:29
  18.3 6.7 %collective-permute-start.4 = (f32[64,384]{1,0:T(8,128)S(1)}, f32[64,384]{1,0:T(8,128)S(1)}, u32[]{:S(2)}, u32[]{:S(2)}) collective-permute-start(f32[64,384]{1,0:T(8,128)S(1)} %get-tuple-element.28), channel_id=1, source_target_pairs={{0,4},{1,5},{2,6},{3,7},{4,0},{5,1},{6,2},{7,3},{8,12},{9,13},{10,... | collective-permute-start | bytes 294920 | tf_op jit(solution)/shard_map/ppermute | solution.py:29
  18.5 6.5 %collective-permute-start.5 = (f32[64,384]{1,0:T(8,128)S(1)}, f32[64,384]{1,0:T(8,128)S(1)}, u32[]{:S(2)}, u32[]{:S(2)}) collective-permute-start(f32[64,384]{1,0:T(8,128)S(1)} %get-tuple-element.29), channel_id=1, source_target_pairs={{0,6},{1,7},{2,4},{3,5},{4,2},{5,3},{6,0},{7,1},{8,14},{9,15},{10,... | collective-permute-start | bytes 294920 | tf_op jit(solution)/shard_map/ppermute | solution.py:29
  23.4 2.0 %collective-permute-start.11 = (f32[64,384]{1,0:T(8,128)S(1)}, f32[64,384]{1,0:T(8,128)S(1)}, u32[]{:S(2)}, u32[]{:S(2)}) collective-permute-start(f32[64,384]{1,0:T(8,128)S(1)} %add.3.after_ref.mine_ref), channel_id=1, source_target_pairs={{0,1},{1,0},{2,3},{3,2},{4,5},{5,4},{6,7},{7,6},{8,9},{9,8},{10,11... | collective-permute-start | bytes 294920 | tf_op jit(solution)/shard_map/ppermute | solution.py:29
  23.5 2.0 %collective-permute-start.12 = (f32[64,384]{1,0:T(8,128)S(1)}, f32[64,384]{1,0:T(8,128)S(1)}, u32[]{:S(2)}, u32[]{:S(2)}) collective-permute-start(f32[64,384]{1,0:T(8,128)S(1)} %collective-permute-done.10.theirs_ref), channel_id=1, source_target_pairs={{0,1},{1,0},{2,3},{3,2},{4,5},{5,4},{6,7},{7,6},{8,9},{9,8},{10,11... | collective-permute-start | bytes 294920 | tf_op jit(solution)/shard_map/ppermute | solution.py:29
  25.8 5.3 %collective-permute-start.13 = (f32[256,128]{1,0:T(8,128)S(1)}, f32[256,128]{1,0:T(8,128)S(1)}, u32[]{:S(2)}, u32[]{:S(2)}) collective-permute-start(f32[256,128]{1,0:T(8,128)S(1)} %correct.1.sent_ref), channel_id=1, source_target_pairs={{0,8},{8,0},{16,24},{24,16},{1,9},{9,1},{17,25},{25,17},{2,10},{10... | collective-permute-start | bytes 393224 | tf_op jit(solution)/shard_map/ppermute | solution.py:29
  27.5 9.5 %collective-permute-start.6 = (f32[64,128]{1,0:T(8,128)S(1)}, f32[64,128]{1,0:T(8,128)S(1)}, u32[]{:S(2)}, u32[]{:S(2)}) collective-permute-start(f32[64,128]{1,0:T(8,128)S(1)} %get-tuple-element.30.refs_0_.own_ref), channel_id=1, source_target_pairs={{0,2},{1,3},{2,0},{3,1},{4,6},{5,7},{6,4},{7,5},{8,10},{9,11},{10,... | collective-permute-start | bytes 98312 | tf_op jit(solution)/shard_map/ppermute | solution.py:29
  29.0 8.0 %collective-permute-start.7 = (f32[64,128]{1,0:T(8,128)S(1)}, f32[64,128]{1,0:T(8,128)S(1)}, u32[]{:S(2)}, u32[]{:S(2)}) collective-permute-start(f32[64,128]{1,0:T(8,128)S(1)} %get-tuple-element.31.other_ref), channel_id=1, source_target_pairs={{0,4},{1,5},{2,6},{3,7},{4,0},{5,1},{6,2},{7,3},{8,12},{9,13},{10,... | collective-permute-start | bytes 98312 | tf_op jit(solution)/shard_map/ppermute | solution.py:29
  29.8 7.2 %collective-permute-start.8 = (f32[64,128]{1,0:T(8,128)S(1)}, f32[64,128]{1,0:T(8,128)S(1)}, u32[]{:S(2)}, u32[]{:S(2)}) collective-permute-start(f32[64,128]{1,0:T(8,128)S(1)} %get-tuple-element.31.other_ref), channel_id=1, source_target_pairs={{0,6},{1,7},{2,4},{3,5},{4,2},{5,3},{6,0},{7,1},{8,14},{9,15},{10,... | collective-permute-start | bytes 98312 | tf_op jit(solution)/shard_map/ppermute | solution.py:29
  31.9 5.2 %collective-permute-start.14 = (f32[64,128]{1,0:T(8,128)S(1)}, f32[64,128]{1,0:T(8,128)S(1)}, u32[]{:S(2)}, u32[]{:S(2)}) collective-permute-start(f32[64,128]{1,0:T(8,128)S(1)} %get-tuple-element.34.sent_ref), channel_id=1, source_target_pairs={{0,16},{8,24},{16,0},{24,8},{1,17},{9,25},{17,1},{25,9},{2,18},{10... | collective-permute-start | bytes 98312 | tf_op jit(solution)/shard_map/ppermute | solution.py:29
  37.0 4.0 %copy-start = (bf16[3,4608,128]{2,1,0:T(8,128)(2,1)S(1)}, bf16[3,4608,128]{2,1,0:T(8,128)(2,1)}, u32[]{:S(2)}) copy-start(bf16[3,4608,128]{2,1,0:T(8,128)(2,1)} %refs_9_.1) | copy-start | bytes 10616836
  37.0 4.0 %collective-permute-start.9 = (f32[4,64,128]{2,1,0:T(8,128)S(1)}, f32[4,64,128]{2,1,0:T(8,128)S(1)}, u32[]{:S(2)}, u32[]{:S(2)}) collective-permute-start(f32[4,64,128]{2,1,0:T(8,128)S(1)} %stack.1.own_ref), channel_id=1, source_target_pairs={{0,1},{1,0},{2,3},{3,2},{4,5},{5,4},{6,7},{7,6},{8,9},{9,8},{10,11... | collective-permute-start | bytes 393224 | tf_op jit(solution)/shard_map/ppermute | solution.py:29
  37.5 5.8 %collective-permute-start.20 = (f32[64,256]{1,0:T(8,128)S(1)}, f32[64,256]{1,0:T(8,128)S(1)}, u32[]{:S(2)}, u32[]{:S(2)}) collective-permute-start(f32[64,256]{1,0:T(8,128)S(1)} %pack.1.ref), channel_id=1, source_target_pairs={{0,6},{1,7},{2,4},{3,5},{4,2},{5,3},{6,0},{7,1},{8,14},{9,15},{10,... | collective-permute-start | bytes 196616 | tf_op jit(solution)/shard_map/ppermute | solution.py:29
  39.1 4.8 %collective-permute-start.16 = (f32[64,256]{1,0:T(8,128)S(1)}, f32[64,256]{1,0:T(8,128)S(1)}, u32[]{:S(2)}, u32[]{:S(2)}) collective-permute-start(f32[64,256]{1,0:T(8,128)S(1)} %pack.1.ref), channel_id=1, source_target_pairs={{0,2},{1,3},{2,0},{3,1},{4,6},{5,7},{6,4},{7,5},{8,10},{9,11},{10,... | collective-permute-start | bytes 196616 | tf_op jit(solution)/shard_map/ppermute | solution.py:29
  40.1 4.3 %collective-permute-start.18 = (f32[64,256]{1,0:T(8,128)S(1)}, f32[64,256]{1,0:T(8,128)S(1)}, u32[]{:S(2)}, u32[]{:S(2)}) collective-permute-start(f32[64,256]{1,0:T(8,128)S(1)} %pack.1.ref), channel_id=1, source_target_pairs={{0,4},{1,5},{2,6},{3,7},{4,0},{5,1},{6,2},{7,3},{8,12},{9,13},{10,... | collective-permute-start | bytes 196616 | tf_op jit(solution)/shard_map/ppermute | solution.py:29
  42.6 1.8 %collective-permute-start.15 = (f32[64,256]{1,0:T(8,128)S(1)}, f32[64,256]{1,0:T(8,128)S(1)}, u32[]{:S(2)}, u32[]{:S(2)}) collective-permute-start(f32[64,256]{1,0:T(8,128)S(1)} %relay.2.refs_0_), channel_id=1, source_target_pairs={{0,1},{1,0},{2,3},{3,2},{4,5},{5,4},{6,7},{7,6},{8,9},{9,8},{10,11... | collective-permute-start | bytes 196616 | tf_op jit(solution)/shard_map/ppermute | solution.py:29
  43.3 1.3 %collective-permute-start.21 = (f32[64,256]{1,0:T(8,128)S(1)}, f32[64,256]{1,0:T(8,128)S(1)}, u32[]{:S(2)}, u32[]{:S(2)}) collective-permute-start(f32[64,256]{1,0:T(8,128)S(1)} %relay.3.refs_6_), channel_id=1, source_target_pairs={{0,1},{1,0},{2,3},{3,2},{4,5},{5,4},{6,7},{7,6},{8,9},{9,8},{10,11... | collective-permute-start | bytes 196616 | tf_op jit(solution)/shard_map/ppermute | solution.py:29
  43.9 1.3 %collective-permute-start.17 = (f32[64,256]{1,0:T(8,128)S(1)}, f32[64,256]{1,0:T(8,128)S(1)}, u32[]{:S(2)}, u32[]{:S(2)}) collective-permute-start(f32[64,256]{1,0:T(8,128)S(1)} %collective-permute-done.16.refs_2_), channel_id=1, source_target_pairs={{0,1},{1,0},{2,3},{3,2},{4,5},{5,4},{6,7},{7,6},{8,9},{9,8},{10,11... | collective-permute-start | bytes 196616 | tf_op jit(solution)/shard_map/ppermute | solution.py:29
  44.3 1.3 %collective-permute-start.19 = (f32[64,256]{1,0:T(8,128)S(1)}, f32[64,256]{1,0:T(8,128)S(1)}, u32[]{:S(2)}, u32[]{:S(2)}) collective-permute-start(f32[64,256]{1,0:T(8,128)S(1)} %collective-permute-done.18.refs_4_), channel_id=1, source_target_pairs={{0,1},{1,0},{2,3},{3,2},{4,5},{5,4},{6,7},{7,6},{8,9},{9,8},{10,11... | collective-permute-start | bytes 196616 | tf_op jit(solution)/shard_map/ppermute | solution.py:29

commit v15 on v13

--- a/solution.py
+++ b/solution.py
@@ -423,20 +423,20 @@
     pieces = []
     for slot in range(slots):
         piece = swap(pack, "rows", 2 * slot) if slot > 0 else pack
-        if slot == slots - 1:
+        if slot in (0, slots - 1):
             piece = pl.pallas_call(
                 relay_kernel, out_shape=floats(share, size), name="relay", **settings(8, 0.1),
             )(second, piece)
         pieces += [piece, swap(piece, "rows", 1)]
     return pl.pallas_call(
-        functools.partial(expand_kernel, levels, per_step * width, count),
+        functools.partial(expand_kernel, levels, width, count),
         out_specs=pl.BlockSpec(memory_space=pl.ANY),
         out_shape=floats(rows, columns),
         scratch_shapes=[
             pltpu.VMEM((columns, size), jnp.float32),
             pltpu.VMEM((2 * size, columns), jnp.bfloat16),
             pltpu.VMEM((rows, columns), jnp.float32),
-            pltpu.SemaphoreType.DMA((nblocks // per_step,)),
+            pltpu.SemaphoreType.DMA((nblocks,)),
         ],
         name="expand",
         **settings(16, 5),

time: 48.7 us -> 47.8 us (0.982)
  transfers between devices with their start and end apart: 22 -> 22, of which waited for: 5 -> 7; matrix products, arithmetic and copies ran while one was open for 0% -> 0% of each run, Pallas kernels for 29% -> 30%
where the time goes in v15:
time: 47.8 us; the launch traced here: 47.7 us
  Pallas kernels  22.3 us (47%)
  starting transfers between devices  20.7 us (43%)
  waiting for transfers between devices  4.32 us (9%)
    ppermute x22, starting transfers between devices, swap(): return lax.ppermute(value, axis, [(i, i ^ mask) for i in range(count)])  20.7 us
    ppermute x22, waiting for transfers between devices, swap(): return lax.ppermute(value, axis, [(i, i ^ mask) for i in range(count)])  4.32 us
    pallas_call x1, Pallas kernels, per_device(): pl.pallas_call(functools.partial(expand_kernel, levels, width, count), ou...  4.28 us
    pallas_call x2, Pallas kernels, project(): pl.pallas_call(functools.partial(project_kernel, other), out_shape=floats...  3.99 us
    pallas_call x1, Pallas kernels, per_device(): pl.pallas_call(functools.partial(gram_kernel, levels, per_step, width), i...  3.34 us
    pallas_call x1, Pallas kernels, per_device(): pl.pallas_call(functools.partial(solve_kernel, per_step, width), out_shap...  2.22 us
    pallas_call x1, Pallas kernels, per_device(): pl.pallas_call(functools.partial(prepare_kernel, levels), in_specs=[pl.Bl...  2.1 us
    pallas_call x1, Pallas kernels, per_device(): pl.pallas_call(functools.partial(weigh_kernel, blocks_per_step(nblocks, 9...  1.6 us
  transfers between devices with their start and end apart: 22, of which 7 were waited for; matrix products, arithmetic and copies ran while one was open for 0% of the time, Pallas kernels for 30%

profile of v15, /device:TPU:0, one launch (start us, length us, event | category | flops | bytes accessed | tf_op | source)
XLA Modules:
  0.0 47.7 jit_solution(13754085973083683920)
XLA Ops:
  0.0 3.3 %gram.1 = (bf16[384,4608]{1,0:T(8,128)(2,1)S(1)}, f32[64,384]{1,0:T(8,128)S(1)}, f32[64,384]{1,0:T(8,128)S(1)}) custom-call(bf16[3,4608,128]{2,1,0:T(8,128)(2,1)} %right_ref.1, bf16[3,4608,128]{2,1,0:T(8,128)(2,1)} %refs_9_.1), custom_call_target="tpu_custom_call" | custom-call | flops 3300000000 | tf_op jit(solution)/shard_map/gram/pallas_call | solution.py:301
  3.4 0.5 %collective-permute-start = (f32[64,384]{1,0:T(8,128)S(1)}, f32[64,384]{1,0:T(8,128)S(1)}, u32[]{:S(2)}, u32[]{:S(2)}) collective-permute-start(f32[64,384]{1,0:T(8,128)S(1)} %get-tuple-element.19), channel_id=1, source_target_pairs={{0,1},{1,0},{2,3},{3,2},{4,5},{5,4},{6,7},{7,6},{8,9},{9,8},{10,11... | collective-permute-start | bytes 294920 | tf_op jit(solution)/shard_map/ppermute | solution.py:29
  3.9 0.0 copy-done.2
  3.9 0.0 copy-done.1
  3.9 1.0 %permute.1.moved_ref = bf16[18,256,256]{2,1,0:T(8,128)(2,1)S(1)} custom-call(s32[18,256]{1,0:T(8,128)S(1)} %copy-done.2, bf16[18,256,256]{2,1,0:T(8,128)(2,1)S(1)} %copy-done.1), custom_call_target="tpu_custom_call" | custom-call | flops 1650000000 | tf_op jit(solution)/shard_map/permute/pallas_call | solution.py:317
  4.9 0.0 collective-permute-done.got_ref
  4.9 0.0 slice-start
  5.0 2.8 %collective-permute-start.1 = (f32[64,384]{1,0:T(8,128)S(1)}, f32[64,384]{1,0:T(8,128)S(1)}, u32[]{:S(2)}, u32[]{:S(2)}) collective-permute-start(f32[64,384]{1,0:T(8,128)S(1)} %add.2.after_ref.mine_ref), channel_id=1, source_target_pairs={{0,2},{1,3},{2,0},{3,1},{4,6},{5,7},{6,4},{7,5},{8,10},{9,11},{10,... | collective-permute-start | bytes 294920 | tf_op jit(solution)/shard_map/ppermute | solution.py:29
  7.7 1.6 %weigh.1.factor_ref = bf16[768,4608]{1,0:T(8,128)(2,1)S(1)} custom-call(bf16[18,256,256]{2,1,0:T(8,128)(2,1)S(1)} %permute.1.moved_ref, bf16[384,4608]{1,0:T(8,128)(2,1)S(1)} %get-tuple-element.17.flip_ref, f32[64,384]{1,0:T(8,128)S(1)} %add.2.after_ref.mine_ref), custom_call_target="tpu_custom_call" | custom-call | flops 2640000000 | tf_op jit(solution)/shard_map/weigh/pallas_call | solution.py:330
  9.4 0.0 slice-done
  9.4 2.0 %project_other.1 = f32[384,256]{1,0:T(8,128)S(1)} custom-call(bf16[768,4608]{1,0:T(8,128)(2,1)S(1)} %weigh.1.factor_ref, bf16[4608,512]{1,0:T(8,128)(2,1)S(1)} %bitcast.1, f32[64,384]{1,0:T(8,128)S(1)} %add.2.after_ref.mine_ref), custom_call_target="tpu_custom_call" | custom-call | flops 1100000000 | tf_op jit(solution)/shard_map/project_other/pallas_call | solution.py:338
  11.4 0.1 collective-permute-start.2
  11.5 0.0 collective-permute-done.1.got_ref
  11.5 0.0 copy-start.3
  11.5 1.6 %collective-permute-start.10 = (f32[64,384]{1,0:T(8,128)S(1)}, f32[64,384]{1,0:T(8,128)S(1)}, u32[]{:S(2)}, u32[]{:S(2)}) collective-permute-start(f32[64,384]{1,0:T(8,128)S(1)} %add.3.after_ref.mine_ref), channel_id=1, source_target_pairs={{0,4},{1,5},{2,6},{3,7},{4,0},{5,1},{6,2},{7,3},{8,12},{9,13},{10,... | collective-permute-start | bytes 294920 | tf_op jit(solution)/shard_map/ppermute | solution.py:29
  13.1 2.0 %project_own.1.keep_ref = f32[384,256]{1,0:T(8,128)S(1)} custom-call(bf16[768,4608]{1,0:T(8,128)(2,1)S(1)} %weigh.1.factor_ref, bf16[4608,512]{1,0:T(8,128)(2,1)S(1)} %bitcast.1, f32[64,384]{1,0:T(8,128)S(1)} %add.3.after_ref.mine_ref), custom_call_target="tpu_custom_call" | custom-call | flops 4400000000 | tf_op jit(solution)/shard_map/project_own/pallas_call | solution.py:338
  15.1 0.0 collective-permute-done.2.got_ref
  15.1 0.2 merge.1
  15.3 1.3 %collective-permute-start.3 = (f32[64,384]{1,0:T(8,128)S(1)}, f32[64,384]{1,0:T(8,128)S(1)}, u32[]{:S(2)}, u32[]{:S(2)}) collective-permute-start(f32[64,384]{1,0:T(8,128)S(1)} %get-tuple-element.21), channel_id=1, source_target_pairs={{0,2},{1,3},{2,0},{3,1},{4,6},{5,7},{6,4},{7,5},{8,10},{9,11},{10,... | collective-permute-start | bytes 294920 | tf_op jit(solution)/shard_map/ppermute | solution.py:29
  16.6 0.5 %collective-permute-start.4 = (f32[64,384]{1,0:T(8,128)S(1)}, f32[64,384]{1,0:T(8,128)S(1)}, u32[]{:S(2)}, u32[]{:S(2)}) collective-permute-start(f32[64,384]{1,0:T(8,128)S(1)} %get-tuple-element.22), channel_id=1, source_target_pairs={{0,4},{1,5},{2,6},{3,7},{4,0},{5,1},{6,2},{7,3},{8,12},{9,13},{10,... | collective-permute-start | bytes 294920 | tf_op jit(solution)/shard_map/ppermute | solution.py:29
  17.1 1.8 %collective-permute-start.5 = (f32[64,384]{1,0:T(8,128)S(1)}, f32[64,384]{1,0:T(8,128)S(1)}, u32[]{:S(2)}, u32[]{:S(2)}) collective-permute-start(f32[64,384]{1,0:T(8,128)S(1)} %get-tuple-element.23), channel_id=1, source_target_pairs={{0,6},{1,7},{2,4},{3,5},{4,2},{5,3},{6,0},{7,1},{8,14},{9,15},{10,... | collective-permute-start | bytes 294920 | tf_op jit(solution)/shard_map/ppermute | solution.py:29
  18.9 2.1 %prepare.1.refs_4_.joined_ref = f32[3,256,256]{2,1,0:T(8,128)S(1)} custom-call(f32[7,256,256]{2,1,0:T(8,128)} %joined_ref.1, s32[3,128]{1,0:T(4,128)S(1)} %copy-done.3), custom_call_target="tpu_custom_call" | custom-call | flops 2200000000 | tf_op jit(solution)/shard_map/prepare/pallas_call | solution.py:362
  21.0 0.1 collective-permute-start.11
  21.1 0.0 collective-permute-done.10.theirs_ref
  21.1 0.5 %collective-permute-start.12 = (f32[64,384]{1,0:T(8,128)S(1)}, f32[64,384]{1,0:T(8,128)S(1)}, u32[]{:S(2)}, u32[]{:S(2)}) collective-permute-start(f32[64,384]{1,0:T(8,128)S(1)} %collective-permute-done.10.theirs_ref), channel_id=1, source_target_pairs={{0,1},{1,0},{2,3},{3,2},{4,5},{5,4},{6,7},{7,6},{8,9},{9,8},{10,11... | collective-permute-start | bytes 294920 | tf_op jit(solution)/shard_map/ppermute | solution.py:29
  21.6 0.0 collective-permute-done.3.refs_1_
  21.6 1.5 %collective-permute-done.4.refs_2_ = f32[64,384]{1,0:T(8,128)S(1)} collective-permute-done((f32[64,384]{1,0:T(8,128)S(1)}, f32[64,384]{1,0:T(8,128)S(1)}, u32[]{:S(2)}, u32[]{:S(2)}) %collective-permute-start.4) | collective-permute-done | bytes 98336 | tf_op jit(solution)/shard_map/ppermute | solution.py:29
  23.1 0.0 collective-permute-done.5.refs_3_
  23.1 0.4 node.1
  23.4 0.0 collective-permute-done.11.pair_mine_ref
  23.4 0.0 collective-permute-done.12.pair_theirs_ref
  23.5 0.4 correct.1.sent_ref
  23.8 1.7 %collective-permute-start.13 = (f32[256,128]{1,0:T(8,128)S(1)}, f32[256,128]{1,0:T(8,128)S(1)}, u32[]{:S(2)}, u32[]{:S(2)}) collective-permute-start(f32[256,128]{1,0:T(8,128)S(1)} %correct.1.sent_ref), channel_id=1, source_target_pairs={{0,8},{8,0},{16,24},{24,16},{1,9},{9,1},{17,25},{25,17},{2,10},{10... | collective-permute-start | bytes 393224 | tf_op jit(solution)/shard_map/ppermute | solution.py:29
  25.5 1.0 %collective-permute-start.6 = (f32[64,128]{1,0:T(8,128)S(1)}, f32[64,128]{1,0:T(8,128)S(1)}, u32[]{:S(2)}, u32[]{:S(2)}) collective-permute-start(f32[64,128]{1,0:T(8,128)S(1)} %get-tuple-element.24.refs_0_.own_ref), channel_id=1, source_target_pairs={{0,2},{1,3},{2,0},{3,1},{4,6},{5,7},{6,4},{7,5},{8,10},{9,11},{10,... | collective-permute-start | bytes 98312 | tf_op jit(solution)/shard_map/ppermute | solution.py:29
  26.6 0.8 %collective-permute-start.7 = (f32[64,128]{1,0:T(8,128)S(1)}, f32[64,128]{1,0:T(8,128)S(1)}, u32[]{:S(2)}, u32[]{:S(2)}) collective-permute-start(f32[64,128]{1,0:T(8,128)S(1)} %get-tuple-element.25.other_ref), channel_id=1, source_target_pairs={{0,4},{1,5},{2,6},{3,7},{4,0},{5,1},{6,2},{7,3},{8,12},{9,13},{10,... | collective-permute-start | bytes 98312 | tf_op jit(solution)/shard_map/ppermute | solution.py:29
  27.4 1.7 %collective-permute-start.8 = (f32[64,128]{1,0:T(8,128)S(1)}, f32[64,128]{1,0:T(8,128)S(1)}, u32[]{:S(2)}, u32[]{:S(2)}) collective-permute-start(f32[64,128]{1,0:T(8,128)S(1)} %get-tuple-element.25.other_ref), channel_id=1, source_target_pairs={{0,6},{1,7},{2,4},{3,5},{4,2},{5,3},{6,0},{7,1},{8,14},{9,15},{10,... | collective-permute-start | bytes 98312 | tf_op jit(solution)/shard_map/ppermute | solution.py:29
  29.0 0.0 collective-permute-done.13.got_ref.after_ref
  29.0 0.8 %level1.1 = (f32[64,128]{1,0:T(8,128)S(1)}, f32[64,128]{1,0:T(8,128)S(1)}) custom-call(f32[256,128]{1,0:T(8,128)S(1)} %correct.1.sent_ref, f32[256,128]{1,0:T(8,128)S(1)} %collective-permute-done.13.got_ref.after_ref, f32[3,256,256]{2,1,0:T(8,128)S(1)} %prepare.1.refs_4_.joined_ref, f32[256,128]{1,0:T(8,128)S(1)} %collective-permute-done.13.got_ref.after_ref), custom_call_target="tpu_custom_call" | custom-call | flops 6600000000 | tf_op jit(solution)/shard_map/level1/pallas_call | solution.py:398
  29.8 2.7 %collective-permute-start.14 = (f32[64,128]{1,0:T(8,128)S(1)}, f32[64,128]{1,0:T(8,128)S(1)}, u32[]{:S(2)}, u32[]{:S(2)}) collective-permute-start(f32[64,128]{1,0:T(8,128)S(1)} %get-tuple-element.28.sent_ref), channel_id=1, source_target_pairs={{0,16},{8,24},{16,0},{24,8},{1,17},{9,25},{17,1},{25,9},{2,18},{10... | collective-permute-start | bytes 98312 | tf_op jit(solution)/shard_map/ppermute | solution.py:29
  32.5 2.2 %solve.1.after_ref.first_ref = f32[4608,512]{1,0:T(8,128)S(1)} custom-call(bf16[18,256,256]{2,1,0:T(8,128)(2,1)S(1)} %permute.1.moved_ref, bf16[4608,512]{1,0:T(8,128)(2,1)S(1)} %bitcast.1, f32[64,384]{1,0:T(8,128)S(1)} %get-tuple-element.20.refs_0_), custom_call_target="tpu_custom_call" | custom-call | flops 8800000000 | tf_op jit(solution)/shard_map/solve/pallas_call | solution.py:387
  34.7 0.0 collective-permute-done.6.refs_1_
  34.7 0.0 collective-permute-done.7.refs_2_
  34.7 0.0 collective-permute-done.8.refs_3_
  34.8 0.0 copy-start
  34.8 0.1 collective-permute-start.9
  34.8 0.0 collective-permute-done.14.got_ref
  34.9 0.4 level2.1.refs_1_
  35.2 1.3 %collective-permute-start.20 = (f32[64,256]{1,0:T(8,128)S(1)}, f32[64,256]{1,0:T(8,128)S(1)}, u32[]{:S(2)}, u32[]{:S(2)}) collective-permute-start(f32[64,256]{1,0:T(8,128)S(1)} %pack.1.ref), channel_id=1, source_target_pairs={{0,6},{1,7},{2,4},{3,5},{4,2},{5,3},{6,0},{7,1},{8,14},{9,15},{10,... | collective-permute-start | bytes 196616 | tf_op jit(solution)/shard_map/ppermute | solution.py:29
  36.6 1.2 %collective-permute-start.16 = (f32[64,256]{1,0:T(8,128)S(1)}, f32[64,256]{1,0:T(8,128)S(1)}, u32[]{:S(2)}, u32[]{:S(2)}) collective-permute-start(f32[64,256]{1,0:T(8,128)S(1)} %pack.1.ref), channel_id=1, source_target_pairs={{0,2},{1,3},{2,0},{3,1},{4,6},{5,7},{6,4},{7,5},{8,10},{9,11},{10,... | collective-permute-start | bytes 196616 | tf_op jit(solution)/shard_map/ppermute | solution.py:29
  37.8 1.0 %collective-permute-start.18 = (f32[64,256]{1,0:T(8,128)S(1)}, f32[64,256]{1,0:T(8,128)S(1)}, u32[]{:S(2)}, u32[]{:S(2)}) collective-permute-start(f32[64,256]{1,0:T(8,128)S(1)} %pack.1.ref), channel_id=1, source_target_pairs={{0,4},{1,5},{2,6},{3,7},{4,0},{5,1},{6,2},{7,3},{8,12},{9,13},{10,... | collective-permute-start | bytes 196616 | tf_op jit(solution)/shard_map/ppermute | solution.py:29
  38.8 0.0 collective-permute-done.9.pair_ref
  38.8 1.6 %apply.1.after_ref.refs_8_ = f32[4608,512]{1,0:T(8,128)S(1)} custom-call(f32[4,64,128]{2,1,0:T(8,128)S(1)} %stack.1.own_ref, f32[4,64,128]{2,1,0:T(8,128)S(1)} %collective-permute-done.9.pair_ref, f32[4608,512]{1,0:T(8,128)S(1)} %solve.1.after_ref.first_ref, bf16[3,4608,128]{2,1,0:T(8,128)(2,1)S(1)} %copy-done), custom_call_target="tpu_custom_call" | custom-call | flops 1980000000 | tf_op jit(solution)/shard_map/apply/pallas_call | solution.py:409
  40.4 0.1 collective-permute-start.15
  40.5 0.6 %collective-permute-done.20.ref = f32[64,256]{1,0:T(8,128)S(1)} collective-permute-done((f32[64,256]{1,0:T(8,128)S(1)}, f32[64,256]{1,0:T(8,128)S(1)}, u32[]{:S(2)}, u32[]{:S(2)}) %collective-permute-start.20) | collective-permute-done | bytes 65568 | tf_op jit(solution)/shard_map/ppermute | solution.py:29
  41.1 0.0 collective-permute-start.21
  41.1 0.6 %collective-permute-done.16.refs_2_ = f32[64,256]{1,0:T(8,128)S(1)} collective-permute-done((f32[64,256]{1,0:T(8,128)S(1)}, f32[64,256]{1,0:T(8,128)S(1)}, u32[]{:S(2)}, u32[]{:S(2)}) %collective-permute-start.16) | collective-permute-done | bytes 65568 | tf_op jit(solution)/shard_map/ppermute | solution.py:29
  41.7 0.0 collective-permute-start.17
  41.7 0.4 collective-permute-done.18.refs_4_
  42.1 0.1 collective-permute-start.19
  42.2 0.0 collective-permute-done.15.refs_1_
  42.2 0.2 collective-permute-done.21.refs_7_
  42.4 0.6 %collective-permute-done.17.refs_3_ = f32[64,256]{1,0:T(8,128)S(1)} collective-permute-done((f32[64,256]{1,0:T(8,128)S(1)}, f32[64,256]{1,0:T(8,128)S(1)}, u32[]{:S(2)}, u32[]{:S(2)}) %collective-permute-start.17) | collective-permute-done | bytes 65568 | tf_op jit(solution)/shard_map/ppermute | solution.py:29
  42.9 0.4 collective-permute-done.19.refs_5_
  43.4 4.3 %expand.1 = f32[4608,512]{1,0:T(8,128)} custom-call(f32[64,256]{1,0:T(8,128)S(1)} %relay.2.refs_0_, f32[64,256]{1,0:T(8,128)S(1)} %collective-permute-done.15.refs_1_, f32[64,256]{1,0:T(8,128)S(1)} %collective-permute-done.16.refs_2_, f32[64,256]{1,0:T(8,128)S(1)} %collective-permute-done.17.refs_3_, f32[64,256]{1,0:T(8,128)S(1)} %collective-permute-done.18.refs_4_, ...), custom_call_target="tpu_custom_call" | custom-call | flops 5500000256 | tf_op jit(solution)/shard_map/expand/pallas_call | solution.py:431
  (13 shorter events, 0.1 us)
Async XLA Ops:
  0.0 3.9 %copy-start.2 = (s32[18,256]{1,0:T(8,128)S(1)}, s32[18,256]{1,0:T(8,128)}, u32[]{:S(2)}) copy-start(s32[18,256]{1,0:T(8,128)} %order_ref.1) | copy-start | bytes 55300
  0.0 3.9 %copy-start.1 = (bf16[18,256,256]{2,1,0:T(8,128)(2,1)S(1)}, bf16[18,256,256]{2,1,0:T(8,128)(2,1)}, u32[]{:S(2)}) copy-start(bf16[18,256,256]{2,1,0:T(8,128)(2,1)} %inv_ref.1) | copy-start | bytes 7077892
  3.4 1.6 %collective-permute-start = (f32[64,384]{1,0:T(8,128)S(1)}, f32[64,384]{1,0:T(8,128)S(1)}, u32[]{:S(2)}, u32[]{:S(2)}) collective-permute-start(f32[64,384]{1,0:T(8,128)S(1)} %get-tuple-element.19), channel_id=1, source_target_pairs={{0,1},{1,0},{2,3},{3,2},{4,5},{5,4},{6,7},{7,6},{8,9},{9,8},{10,11... | collective-permute-start | bytes 294920 | tf_op jit(solution)/shard_map/ppermute | solution.py:29
  4.9 4.4 %slice-start = ((s8[4718592]{0:T(1024)(128)(4,1)}), s8[4194304]{0:T(1024)(128)(4,1)S(1)}, s32[]{:S(2)}) async-start(s8[4718592]{0:T(1024)(128)(4,1)} %bitcast), calls=%async_computation | async-start | bytes 8388608
  5.0 6.5 %collective-permute-start.1 = (f32[64,384]{1,0:T(8,128)S(1)}, f32[64,384]{1,0:T(8,128)S(1)}, u32[]{:S(2)}, u32[]{:S(2)}) collective-permute-start(f32[64,384]{1,0:T(8,128)S(1)} %add.2.after_ref.mine_ref), channel_id=1, source_target_pairs={{0,2},{1,3},{2,0},{3,1},{4,6},{5,7},{6,4},{7,5},{8,10},{9,11},{10,... | collective-permute-start | bytes 294920 | tf_op jit(solution)/shard_map/ppermute | solution.py:29
  7.7 1.6 %slice-start.1 = ((s8[4718592]{0:T(1024)(128)(4,1)}), s8[524288]{0:T(1024)(128)(4,1)S(1)}, s32[]{:S(2)}) async-start(s8[4718592]{0:T(1024)(128)(4,1)} %bitcast), calls=%async_computation.1 | async-start | bytes 1048576
  11.4 3.7 %collective-permute-start.2 = (f32[384,256]{1,0:T(8,128)S(1)}, f32[384,256]{1,0:T(8,128)S(1)}, u32[]{:S(2)}, u32[]{:S(2)}) collective-permute-start(f32[384,256]{1,0:T(8,128)S(1)} %project_other.1), channel_id=1, source_target_pairs={{0,1},{1,0},{2,3},{3,2},{4,5},{5,4},{6,7},{7,6},{8,9},{9,8},{10,11... | collective-permute-start | bytes 1179656 | tf_op jit(solution)/shard_map/ppermute | solution.py:29
  11.5 7.4 %copy-start.3 = (s32[3,128]{1,0:T(4,128)S(1)}, s32[3,128]{1,0:T(4,128)}, u32[]{:S(2)}) copy-start(s32[3,128]{1,0:T(4,128)} %perm_ref.1) | copy-start | bytes 4612
  11.5 9.6 %collective-permute-start.10 = (f32[64,384]{1,0:T(8,128)S(1)}, f32[64,384]{1,0:T(8,128)S(1)}, u32[]{:S(2)}, u32[]{:S(2)}) collective-permute-start(f32[64,384]{1,0:T(8,128)S(1)} %add.3.after_ref.mine_ref), channel_id=1, source_target_pairs={{0,4},{1,5},{2,6},{3,7},{4,0},{5,1},{6,2},{7,3},{8,12},{9,13},{10,... | collective-permute-start | bytes 294920 | tf_op jit(solution)/shard_map/ppermute | solution.py:29
  15.3 6.2 %collective-permute-start.3 = (f32[64,384]{1,0:T(8,128)S(1)}, f32[64,384]{1,0:T(8,128)S(1)}, u32[]{:S(2)}, u32[]{:S(2)}) collective-permute-start(f32[64,384]{1,0:T(8,128)S(1)} %get-tuple-element.21), channel_id=1, source_target_pairs={{0,2},{1,3},{2,0},{3,1},{4,6},{5,7},{6,4},{7,5},{8,10},{9,11},{10,... | collective-permute-start | bytes 294920 | tf_op jit(solution)/shard_map/ppermute | solution.py:29
  16.6 6.4 %collective-permute-start.4 = (f32[64,384]{1,0:T(8,128)S(1)}, f32[64,384]{1,0:T(8,128)S(1)}, u32[]{:S(2)}, u32[]{:S(2)}) collective-permute-start(f32[64,384]{1,0:T(8,128)S(1)} %get-tuple-element.22), channel_id=1, source_target_pairs={{0,4},{1,5},{2,6},{3,7},{4,0},{5,1},{6,2},{7,3},{8,12},{9,13},{10,... | collective-permute-start | bytes 294920 | tf_op jit(solution)/shard_map/ppermute | solution.py:29
  17.1 5.9 %collective-permute-start.5 = (f32[64,384]{1,0:T(8,128)S(1)}, f32[64,384]{1,0:T(8,128)S(1)}, u32[]{:S(2)}, u32[]{:S(2)}) collective-permute-start(f32[64,384]{1,0:T(8,128)S(1)} %get-tuple-element.23), channel_id=1, source_target_pairs={{0,6},{1,7},{2,4},{3,5},{4,2},{5,3},{6,0},{7,1},{8,14},{9,15},{10,... | collective-permute-start | bytes 294920 | tf_op jit(solution)/shard_map/ppermute | solution.py:29
  21.0 2.4 %collective-permute-start.11 = (f32[64,384]{1,0:T(8,128)S(1)}, f32[64,384]{1,0:T(8,128)S(1)}, u32[]{:S(2)}, u32[]{:S(2)}) collective-permute-start(f32[64,384]{1,0:T(8,128)S(1)} %add.3.after_ref.mine_ref), channel_id=1, source_target_pairs={{0,1},{1,0},{2,3},{3,2},{4,5},{5,4},{6,7},{7,6},{8,9},{9,8},{10,11... | collective-permute-start | bytes 294920 | tf_op jit(solution)/shard_map/ppermute | solution.py:29
  21.1 2.4 %collective-permute-start.12 = (f32[64,384]{1,0:T(8,128)S(1)}, f32[64,384]{1,0:T(8,128)S(1)}, u32[]{:S(2)}, u32[]{:S(2)}) collective-permute-start(f32[64,384]{1,0:T(8,128)S(1)} %collective-permute-done.10.theirs_ref), channel_id=1, source_target_pairs={{0,1},{1,0},{2,3},{3,2},{4,5},{5,4},{6,7},{7,6},{8,9},{9,8},{10,11... | collective-permute-start | bytes 294920 | tf_op jit(solution)/shard_map/ppermute | solution.py:29
  23.8 5.2 %collective-permute-start.13 = (f32[256,128]{1,0:T(8,128)S(1)}, f32[256,128]{1,0:T(8,128)S(1)}, u32[]{:S(2)}, u32[]{:S(2)}) collective-permute-start(f32[256,128]{1,0:T(8,128)S(1)} %correct.1.sent_ref), channel_id=1, source_target_pairs={{0,8},{8,0},{16,24},{24,16},{1,9},{9,1},{17,25},{25,17},{2,10},{10... | collective-permute-start | bytes 393224 | tf_op jit(solution)/shard_map/ppermute | solution.py:29
  25.5 9.2 %collective-permute-start.6 = (f32[64,128]{1,0:T(8,128)S(1)}, f32[64,128]{1,0:T(8,128)S(1)}, u32[]{:S(2)}, u32[]{:S(2)}) collective-permute-start(f32[64,128]{1,0:T(8,128)S(1)} %get-tuple-element.24.refs_0_.own_ref), channel_id=1, source_target_pairs={{0,2},{1,3},{2,0},{3,1},{4,6},{5,7},{6,4},{7,5},{8,10},{9,11},{10,... | collective-permute-start | bytes 98312 | tf_op jit(solution)/shard_map/ppermute | solution.py:29
  26.6 8.1 %collective-permute-start.7 = (f32[64,128]{1,0:T(8,128)S(1)}, f32[64,128]{1,0:T(8,128)S(1)}, u32[]{:S(2)}, u32[]{:S(2)}) collective-permute-start(f32[64,128]{1,0:T(8,128)S(1)} %get-tuple-element.25.other_ref), channel_id=1, source_target_pairs={{0,4},{1,5},{2,6},{3,7},{4,0},{5,1},{6,2},{7,3},{8,12},{9,13},{10,... | collective-permute-start | bytes 98312 | tf_op jit(solution)/shard_map/ppermute | solution.py:29
  27.4 7.3 %collective-permute-start.8 = (f32[64,128]{1,0:T(8,128)S(1)}, f32[64,128]{1,0:T(8,128)S(1)}, u32[]{:S(2)}, u32[]{:S(2)}) collective-permute-start(f32[64,128]{1,0:T(8,128)S(1)} %get-tuple-element.25.other_ref), channel_id=1, source_target_pairs={{0,6},{1,7},{2,4},{3,5},{4,2},{5,3},{6,0},{7,1},{8,14},{9,15},{10,... | collective-permute-start | bytes 98312 | tf_op jit(solution)/shard_map/ppermute | solution.py:29
  29.8 5.0 %collective-permute-start.14 = (f32[64,128]{1,0:T(8,128)S(1)}, f32[64,128]{1,0:T(8,128)S(1)}, u32[]{:S(2)}, u32[]{:S(2)}) collective-permute-start(f32[64,128]{1,0:T(8,128)S(1)} %get-tuple-element.28.sent_ref), channel_id=1, source_target_pairs={{0,16},{8,24},{16,0},{24,8},{1,17},{9,25},{17,1},{25,9},{2,18},{10... | collective-permute-start | bytes 98312 | tf_op jit(solution)/shard_map/ppermute | solution.py:29
  34.8 4.0 %copy-start = (bf16[3,4608,128]{2,1,0:T(8,128)(2,1)S(1)}, bf16[3,4608,128]{2,1,0:T(8,128)(2,1)}, u32[]{:S(2)}) copy-start(bf16[3,4608,128]{2,1,0:T(8,128)(2,1)} %refs_9_.1) | copy-start | bytes 10616836
  34.8 4.0 %collective-permute-start.9 = (f32[4,64,128]{2,1,0:T(8,128)S(1)}, f32[4,64,128]{2,1,0:T(8,128)S(1)}, u32[]{:S(2)}, u32[]{:S(2)}) collective-permute-start(f32[4,64,128]{2,1,0:T(8,128)S(1)} %stack.1.own_ref), channel_id=1, source_target_pairs={{0,1},{1,0},{2,3},{3,2},{4,5},{5,4},{6,7},{7,6},{8,9},{9,8},{10,11... | collective-permute-start | bytes 393224 | tf_op jit(solution)/shard_map/ppermute | solution.py:29
  35.2 5.9 %collective-permute-start.20 = (f32[64,256]{1,0:T(8,128)S(1)}, f32[64,256]{1,0:T(8,128)S(1)}, u32[]{:S(2)}, u32[]{:S(2)}) collective-permute-start(f32[64,256]{1,0:T(8,128)S(1)} %pack.1.ref), channel_id=1, source_target_pairs={{0,6},{1,7},{2,4},{3,5},{4,2},{5,3},{6,0},{7,1},{8,14},{9,15},{10,... | collective-permute-start | bytes 196616 | tf_op jit(solution)/shard_map/ppermute | solution.py:29
  36.6 5.1 %collective-permute-start.16 = (f32[64,256]{1,0:T(8,128)S(1)}, f32[64,256]{1,0:T(8,128)S(1)}, u32[]{:S(2)}, u32[]{:S(2)}) collective-permute-start(f32[64,256]{1,0:T(8,128)S(1)} %pack.1.ref), channel_id=1, source_target_pairs={{0,2},{1,3},{2,0},{3,1},{4,6},{5,7},{6,4},{7,5},{8,10},{9,11},{10,... | collective-permute-start | bytes 196616 | tf_op jit(solution)/shard_map/ppermute | solution.py:29
  37.8 4.3 %collective-permute-start.18 = (f32[64,256]{1,0:T(8,128)S(1)}, f32[64,256]{1,0:T(8,128)S(1)}, u32[]{:S(2)}, u32[]{:S(2)}) collective-permute-start(f32[64,256]{1,0:T(8,128)S(1)} %pack.1.ref), channel_id=1, source_target_pairs={{0,4},{1,5},{2,6},{3,7},{4,0},{5,1},{6,2},{7,3},{8,12},{9,13},{10,... | collective-permute-start | bytes 196616 | tf_op jit(solution)/shard_map/ppermute | solution.py:29
  40.4 1.8 %collective-permute-start.15 = (f32[64,256]{1,0:T(8,128)S(1)}, f32[64,256]{1,0:T(8,128)S(1)}, u32[]{:S(2)}, u32[]{:S(2)}) collective-permute-start(f32[64,256]{1,0:T(8,128)S(1)} %relay.2.refs_0_), channel_id=1, source_target_pairs={{0,1},{1,0},{2,3},{3,2},{4,5},{5,4},{6,7},{7,6},{8,9},{9,8},{10,11... | collective-permute-start | bytes 196616 | tf_op jit(solution)/shard_map/ppermute | solution.py:29
  41.1 1.3 %collective-permute-start.21 = (f32[64,256]{1,0:T(8,128)S(1)}, f32[64,256]{1,0:T(8,128)S(1)}, u32[]{:S(2)}, u32[]{:S(2)}) collective-permute-start(f32[64,256]{1,0:T(8,128)S(1)} %relay.3.refs_6_), channel_id=1, source_target_pairs={{0,1},{1,0},{2,3},{3,2},{4,5},{5,4},{6,7},{7,6},{8,9},{9,8},{10,11... | collective-permute-start | bytes 196616 | tf_op jit(solution)/shard_map/ppermute | solution.py:29
  41.7 1.3 %collective-permute-start.17 = (f32[64,256]{1,0:T(8,128)S(1)}, f32[64,256]{1,0:T(8,128)S(1)}, u32[]{:S(2)}, u32[]{:S(2)}) collective-permute-start(f32[64,256]{1,0:T(8,128)S(1)} %collective-permute-done.16.refs_2_), channel_id=1, source_target_pairs={{0,1},{1,0},{2,3},{3,2},{4,5},{5,4},{6,7},{7,6},{8,9},{9,8},{10,11... | collective-permute-start | bytes 196616 | tf_op jit(solution)/shard_map/ppermute | solution.py:29
  42.1 1.3 %collective-permute-start.19 = (f32[64,256]{1,0:T(8,128)S(1)}, f32[64,256]{1,0:T(8,128)S(1)}, u32[]{:S(2)}, u32[]{:S(2)}) collective-permute-start(f32[64,256]{1,0:T(8,128)S(1)} %collective-permute-done.18.refs_4_), channel_id=1, source_target_pairs={{0,1},{1,0},{2,3},{3,2},{4,5},{5,4},{6,7},{7,6},{8,9},{9,8},{10,11... | collective-permute-start | bytes 196616 | tf_op jit(solution)/shard_map/ppermute | solution.py:29

commit v16 on v15

--- a/solution.py
+++ b/solution.py
@@ -7,21 +7,27 @@
 from jax.experimental.pallas import tpu as pltpu
 from jax.sharding import PartitionSpec as P
 
-HIGHEST = lax.Precision.HIGHEST
 MIB = 1 << 20
 
 
-def dot(a, b, contract, exact=False):
-    return lax.dot_general(
-        a, b, ((contract[:1], contract[1:]), ((), ())),
-        precision=HIGHEST if exact else None, preferred_element_type=jnp.float32,
-    )
+def dot(a, b, contract):
+    return lax.dot_general(a, b, ((contract[:1], contract[1:]), ((), ())), preferred_element_type=jnp.float32)
 
 
 def halves(value):
     high_part = value.astype(jnp.bfloat16)
     low_part = (value - high_part.astype(jnp.float32)).astype(jnp.bfloat16)
     return high_part, low_part
+
+
+def left_stack(value):
+    high_part, low_part = halves(value)
+    return jnp.concatenate([high_part, high_part, low_part], axis=1)
+
+
+def right_stack(value):
+    high_part, low_part = halves(value)
+    return jnp.concatenate([high_part, low_part, high_part], axis=1)
 
 
 def swap(value, axis, mask):
@@ -149,10 +155,12 @@
     spot = lax.broadcasted_iota(jnp.int32, (rank, rank), 0)
     for level in range(levels):
         copies[level].wait()
-        chosen = (spot == perm_ref[level:level + 1, :]).astype(jnp.float32)
-        for side in range(2):
-            lanes = pl.ds(side * rank, rank)
-            out_ref[level, :, lanes] = dot(joined_buf[level, :, lanes], chosen, (1, 1), True)
+        chosen = (spot == perm_ref[level:level + 1, :]).astype(jnp.float32).astype(jnp.bfloat16)
+        high_part, low_part = halves(joined_buf[level])
+        for place, part in enumerate((high_part, low_part, high_part)):
+            for side in range(2):
+                moved = dot(chosen, part[:, side * rank:(side + 1) * rank], (1, 1)).astype(jnp.bfloat16)
+                out_ref[level, pl.ds((2 * place + side) * rank, rank), :] = moved
 
 
 def by_side(side, own, other):
@@ -173,7 +181,7 @@
     half = slots // 2
     sums = [sum(ref[...] for ref in part_refs[:half]), sum(ref[...] for ref in part_refs[half:])]
     picked = jnp.concatenate(by_side(side, sums[0][:, :rank], sums[1][:, :rank]), axis=1)
-    coef = dot(picked, joined_ref[0], (1, 1), True)
+    coef = dot(left_stack(picked), joined_ref[0], (1, 0))
     own_ref[...], other_ref[...] = by_side(side, coef[:, :rank], coef[:, rank:])
     rest_ref[...] = (sums[0] + sums[1])[:, rank:]
 
@@ -187,7 +195,8 @@
     lanes = {pair: slice(spot * rank, (spot + 1) * rank) for spot, pair in enumerate(pairs)}
     joint = jnp.concatenate(
         [jnp.concatenate([gram[:, lanes[level, 0]] for gram in grams], axis=1) for level in range(1, levels)], axis=0)
-    rest = rest_ref[...] - dot(jnp.concatenate([own_ref[...], other_ref[...]], axis=1), joint, (1, 1), True)
+    pair = jnp.concatenate([own_ref[...], other_ref[...]], axis=1)
+    rest = rest_ref[...] - dot(left_stack(pair), right_stack(joint), (1, 1))
     pieces = [rest[:, level * rank:(level + 1) * rank] for level in range(levels - 1)]
     for pair in pairs:
         if pair[1] > 0:
@@ -203,7 +212,7 @@
     for ref in (sent_ref, got_ref):
         values.append([ref[pl.ds(i * share, share), :] for i in range(more)])
     picked = jnp.concatenate(by_side(side, values[0][0], values[1][0]), axis=1)
-    coef = dot(picked, joined_ref[level], (1, 1), True)
+    coef = dot(left_stack(picked), joined_ref[level], (1, 0))
     sides = by_side(side, coef[:, :rank], coef[:, rank:])
     coef_ref[...] = sides[0]
     if not message_ref:
@@ -215,7 +224,7 @@
     uppers = list(range(level + 1, levels))
     joint = jnp.concatenate(
         [jnp.concatenate([gram[upper, level] for gram in grams], axis=1) for upper in uppers], axis=0)
-    change = dot(jnp.concatenate(sides, axis=1), joint, (1, 1), True)
+    change = dot(left_stack(jnp.concatenate(sides, axis=1)), right_stack(joint), (1, 1))
     pieces = [values[0][upper - level] + values[1][upper - level] - change[:, i * rank:(i + 1) * rank]
               for i, upper in enumerate(uppers)]
     for pair in pairs:
@@ -362,7 +371,7 @@
     prepared = pl.pallas_call(
         functools.partial(prepare_kernel, levels),
         in_specs=[pl.BlockSpec(memory_space=pltpu.HBM), pl.BlockSpec()],
-        out_shape=floats(levels, 2 * rank, 2 * rank),
+        out_shape=jax.ShapeDtypeStruct((levels, 6 * rank, 2 * rank), jnp.bfloat16),
         scratch_shapes=[pltpu.VMEM((levels, 2 * rank, 2 * rank), jnp.float32), pltpu.SemaphoreType.DMA((levels,))],
         name="prepare",
         **settings(8, 2),

time: 47.8 us -> 47 us (0.983)
  Pallas kernels: 22.3 us -> 21.1 us
    pallas_call x2, Pallas kernels: 1.14 us -> 0.6 us  [per_device(): pl.pallas_call(functools.partial(level_kernel, levels, level, share), out...]
  transfers between devices with their start and end apart: 22 -> 22, of which waited for: 7 -> 7; matrix products, arithmetic and copies ran while one was open for 0% -> 0% of each run, Pallas kernels for 30% -> 28%
where the time goes in v16:
time: 47 us; the launch traced here: 46.8 us
  Pallas kernels  21.1 us (45%)
  starting transfers between devices  20.7 us (44%)
  waiting for transfers between devices  4.74 us (10%)
    ppermute x22, starting transfers between devices, swap(): return lax.ppermute(value, axis, [(i, i ^ mask) for i in range(count)])  20.7 us
    ppermute x22, waiting for transfers between devices, swap(): return lax.ppermute(value, axis, [(i, i ^ mask) for i in range(count)])  4.74 us
    pallas_call x1, Pallas kernels, per_device(): pl.pallas_call(functools.partial(expand_kernel, levels, width, count), ou...  4.28 us
    pallas_call x2, Pallas kernels, project(): pl.pallas_call(functools.partial(project_kernel, other), out_shape=floats...  3.99 us
    pallas_call x1, Pallas kernels, per_device(): pl.pallas_call(functools.partial(gram_kernel, levels, per_step, width), i...  3.34 us
    pallas_call x1, Pallas kernels, per_device(): pl.pallas_call(functools.partial(solve_kernel, per_step, width), out_shap...  2.22 us
    pallas_call x1, Pallas kernels, per_device(): pl.pallas_call(functools.partial(prepare_kernel, levels), in_specs=[pl.Bl...  1.68 us
    pallas_call x1, Pallas kernels, per_device(): pl.pallas_call(functools.partial(weigh_kernel, blocks_per_step(nblocks, 9...  1.6 us
  transfers between devices with their start and end apart: 22, of which 7 were waited for; matrix products, arithmetic and copies ran while one was open for 0% of the time, Pallas kernels for 28%

profile of v16, /device:TPU:0, one launch (start us, length us, event | category | flops | bytes accessed | tf_op | source)
XLA Modules:
  0.0 46.8 jit_solution(4310691642194191742)
XLA Ops:
  0.0 3.3 %gram.1 = (bf16[384,4608]{1,0:T(8,128)(2,1)S(1)}, f32[64,384]{1,0:T(8,128)S(1)}, f32[64,384]{1,0:T(8,128)S(1)}) custom-call(bf16[3,4608,128]{2,1,0:T(8,128)(2,1)} %right_ref.1, bf16[3,4608,128]{2,1,0:T(8,128)(2,1)} %refs_9_.1), custom_call_target="tpu_custom_call" | custom-call | flops 3300000000 | tf_op jit(solution)/shard_map/gram/pallas_call | solution.py:310
  3.4 0.5 %collective-permute-start = (f32[64,384]{1,0:T(8,128)S(1)}, f32[64,384]{1,0:T(8,128)S(1)}, u32[]{:S(2)}, u32[]{:S(2)}) collective-permute-start(f32[64,384]{1,0:T(8,128)S(1)} %get-tuple-element.19), channel_id=1, source_target_pairs={{0,1},{1,0},{2,3},{3,2},{4,5},{5,4},{6,7},{7,6},{8,9},{9,8},{10,11... | collective-permute-start | bytes 294920 | tf_op jit(solution)/shard_map/ppermute | solution.py:35
  3.9 0.0 copy-done.2
  3.9 0.0 copy-done.1
  3.9 1.0 %permute.1.moved_ref = bf16[18,256,256]{2,1,0:T(8,128)(2,1)S(1)} custom-call(s32[18,256]{1,0:T(8,128)S(1)} %copy-done.2, bf16[18,256,256]{2,1,0:T(8,128)(2,1)S(1)} %copy-done.1), custom_call_target="tpu_custom_call" | custom-call | flops 1650000000 | tf_op jit(solution)/shard_map/permute/pallas_call | solution.py:326
  4.9 0.0 collective-permute-done.got_ref
  4.9 0.0 slice-start
  5.0 2.8 %collective-permute-start.1 = (f32[64,384]{1,0:T(8,128)S(1)}, f32[64,384]{1,0:T(8,128)S(1)}, u32[]{:S(2)}, u32[]{:S(2)}) collective-permute-start(f32[64,384]{1,0:T(8,128)S(1)} %add.2.after_ref.mine_ref), channel_id=1, source_target_pairs={{0,2},{1,3},{2,0},{3,1},{4,6},{5,7},{6,4},{7,5},{8,10},{9,11},{10,... | collective-permute-start | bytes 294920 | tf_op jit(solution)/shard_map/ppermute | solution.py:35
  7.7 1.6 %weigh.1.factor_ref = bf16[768,4608]{1,0:T(8,128)(2,1)S(1)} custom-call(bf16[18,256,256]{2,1,0:T(8,128)(2,1)S(1)} %permute.1.moved_ref, bf16[384,4608]{1,0:T(8,128)(2,1)S(1)} %get-tuple-element.17.flip_ref, f32[64,384]{1,0:T(8,128)S(1)} %add.2.after_ref.mine_ref), custom_call_target="tpu_custom_call" | custom-call | flops 2640000000 | tf_op jit(solution)/shard_map/weigh/pallas_call | solution.py:339
  9.4 0.0 slice-done
  9.4 2.0 %project_other.1 = f32[384,256]{1,0:T(8,128)S(1)} custom-call(bf16[768,4608]{1,0:T(8,128)(2,1)S(1)} %weigh.1.factor_ref, bf16[4608,512]{1,0:T(8,128)(2,1)S(1)} %bitcast.1, f32[64,384]{1,0:T(8,128)S(1)} %add.2.after_ref.mine_ref), custom_call_target="tpu_custom_call" | custom-call | flops 1100000000 | tf_op jit(solution)/shard_map/project_other/pallas_call | solution.py:347
  11.4 0.1 collective-permute-start.2
  11.5 0.0 collective-permute-done.1.got_ref
  11.5 0.0 copy-start.3
  11.5 1.6 %collective-permute-start.10 = (f32[64,384]{1,0:T(8,128)S(1)}, f32[64,384]{1,0:T(8,128)S(1)}, u32[]{:S(2)}, u32[]{:S(2)}) collective-permute-start(f32[64,384]{1,0:T(8,128)S(1)} %add.3.after_ref.mine_ref), channel_id=1, source_target_pairs={{0,4},{1,5},{2,6},{3,7},{4,0},{5,1},{6,2},{7,3},{8,12},{9,13},{10,... | collective-permute-start | bytes 294920 | tf_op jit(solution)/shard_map/ppermute | solution.py:35
  13.1 2.0 %project_own.1.keep_ref = f32[384,256]{1,0:T(8,128)S(1)} custom-call(bf16[768,4608]{1,0:T(8,128)(2,1)S(1)} %weigh.1.factor_ref, bf16[4608,512]{1,0:T(8,128)(2,1)S(1)} %bitcast.1, f32[64,384]{1,0:T(8,128)S(1)} %add.3.after_ref.mine_ref), custom_call_target="tpu_custom_call" | custom-call | flops 4400000000 | tf_op jit(solution)/shard_map/project_own/pallas_call | solution.py:347
  15.1 0.0 collective-permute-done.2.got_ref
  15.1 0.2 merge.1
  15.3 1.3 %collective-permute-start.3 = (f32[64,384]{1,0:T(8,128)S(1)}, f32[64,384]{1,0:T(8,128)S(1)}, u32[]{:S(2)}, u32[]{:S(2)}) collective-permute-start(f32[64,384]{1,0:T(8,128)S(1)} %get-tuple-element.21), channel_id=1, source_target_pairs={{0,2},{1,3},{2,0},{3,1},{4,6},{5,7},{6,4},{7,5},{8,10},{9,11},{10,... | collective-permute-start | bytes 294920 | tf_op jit(solution)/shard_map/ppermute | solution.py:35
  16.6 0.5 %collective-permute-start.4 = (f32[64,384]{1,0:T(8,128)S(1)}, f32[64,384]{1,0:T(8,128)S(1)}, u32[]{:S(2)}, u32[]{:S(2)}) collective-permute-start(f32[64,384]{1,0:T(8,128)S(1)} %get-tuple-element.22), channel_id=1, source_target_pairs={{0,4},{1,5},{2,6},{3,7},{4,0},{5,1},{6,2},{7,3},{8,12},{9,13},{10,... | collective-permute-start | bytes 294920 | tf_op jit(solution)/shard_map/ppermute | solution.py:35
  17.1 1.8 %collective-permute-start.5 = (f32[64,384]{1,0:T(8,128)S(1)}, f32[64,384]{1,0:T(8,128)S(1)}, u32[]{:S(2)}, u32[]{:S(2)}) collective-permute-start(f32[64,384]{1,0:T(8,128)S(1)} %get-tuple-element.23), channel_id=1, source_target_pairs={{0,6},{1,7},{2,4},{3,5},{4,2},{5,3},{6,0},{7,1},{8,14},{9,15},{10,... | collective-permute-start | bytes 294920 | tf_op jit(solution)/shard_map/ppermute | solution.py:35
  18.9 1.7 %prepare.1.refs_4_.joined_ref = bf16[3,768,256]{2,1,0:T(8,128)(2,1)S(1)} custom-call(f32[7,256,256]{2,1,0:T(8,128)} %joined_ref.1, s32[3,128]{1,0:T(4,128)S(1)} %copy-done.3), custom_call_target="tpu_custom_call" | custom-call | flops 2200000000 | tf_op jit(solution)/shard_map/prepare/pallas_call | solution.py:371
  20.6 0.1 collective-permute-start.11
  20.6 0.0 collective-permute-done.10.theirs_ref
  20.6 0.5 %collective-permute-start.12 = (f32[64,384]{1,0:T(8,128)S(1)}, f32[64,384]{1,0:T(8,128)S(1)}, u32[]{:S(2)}, u32[]{:S(2)}) collective-permute-start(f32[64,384]{1,0:T(8,128)S(1)} %collective-permute-done.10.theirs_ref), channel_id=1, source_target_pairs={{0,1},{1,0},{2,3},{3,2},{4,5},{5,4},{6,7},{7,6},{8,9},{9,8},{10,11... | collective-permute-start | bytes 294920 | tf_op jit(solution)/shard_map/ppermute | solution.py:35
  21.1 0.0 collective-permute-done.3.refs_1_
  21.1 1.9 %collective-permute-done.4.refs_2_ = f32[64,384]{1,0:T(8,128)S(1)} collective-permute-done((f32[64,384]{1,0:T(8,128)S(1)}, f32[64,384]{1,0:T(8,128)S(1)}, u32[]{:S(2)}, u32[]{:S(2)}) %collective-permute-start.4) | collective-permute-done | bytes 98336 | tf_op jit(solution)/shard_map/ppermute | solution.py:35
  23.0 0.0 collective-permute-done.5.refs_3_
  23.0 0.2 node.1
  23.2 0.0 collective-permute-done.11.pair_mine_ref
  23.2 0.0 collective-permute-done.12.pair_theirs_ref
  23.3 0.3 correct.1.sent_ref
  23.6 1.7 %collective-permute-start.13 = (f32[256,128]{1,0:T(8,128)S(1)}, f32[256,128]{1,0:T(8,128)S(1)}, u32[]{:S(2)}, u32[]{:S(2)}) collective-permute-start(f32[256,128]{1,0:T(8,128)S(1)} %correct.1.sent_ref), channel_id=1, source_target_pairs={{0,8},{8,0},{16,24},{24,16},{1,9},{9,1},{17,25},{25,17},{2,10},{10... | collective-permute-start | bytes 393224 | tf_op jit(solution)/shard_map/ppermute | solution.py:35
  25.3 1.0 %collective-permute-start.6 = (f32[64,128]{1,0:T(8,128)S(1)}, f32[64,128]{1,0:T(8,128)S(1)}, u32[]{:S(2)}, u32[]{:S(2)}) collective-permute-start(f32[64,128]{1,0:T(8,128)S(1)} %get-tuple-element.24.refs_0_.own_ref), channel_id=1, source_target_pairs={{0,2},{1,3},{2,0},{3,1},{4,6},{5,7},{6,4},{7,5},{8,10},{9,11},{10,... | collective-permute-start | bytes 98312 | tf_op jit(solution)/shard_map/ppermute | solution.py:35
  26.3 0.8 %collective-permute-start.7 = (f32[64,128]{1,0:T(8,128)S(1)}, f32[64,128]{1,0:T(8,128)S(1)}, u32[]{:S(2)}, u32[]{:S(2)}) collective-permute-start(f32[64,128]{1,0:T(8,128)S(1)} %get-tuple-element.25.other_ref), channel_id=1, source_target_pairs={{0,4},{1,5},{2,6},{3,7},{4,0},{5,1},{6,2},{7,3},{8,12},{9,13},{10,... | collective-permute-start | bytes 98312 | tf_op jit(solution)/shard_map/ppermute | solution.py:35
  27.1 1.7 %collective-permute-start.8 = (f32[64,128]{1,0:T(8,128)S(1)}, f32[64,128]{1,0:T(8,128)S(1)}, u32[]{:S(2)}, u32[]{:S(2)}) collective-permute-start(f32[64,128]{1,0:T(8,128)S(1)} %get-tuple-element.25.other_ref), channel_id=1, source_target_pairs={{0,6},{1,7},{2,4},{3,5},{4,2},{5,3},{6,0},{7,1},{8,14},{9,15},{10,... | collective-permute-start | bytes 98312 | tf_op jit(solution)/shard_map/ppermute | solution.py:35
  28.8 0.0 collective-permute-done.13.got_ref.after_ref
  28.8 0.4 level1.1
  29.2 2.7 %collective-permute-start.14 = (f32[64,128]{1,0:T(8,128)S(1)}, f32[64,128]{1,0:T(8,128)S(1)}, u32[]{:S(2)}, u32[]{:S(2)}) collective-permute-start(f32[64,128]{1,0:T(8,128)S(1)} %get-tuple-element.28.sent_ref), channel_id=1, source_target_pairs={{0,16},{8,24},{16,0},{24,8},{1,17},{9,25},{17,1},{25,9},{2,18},{10... | collective-permute-start | bytes 98312 | tf_op jit(solution)/shard_map/ppermute | solution.py:35
  31.8 2.2 %solve.1.after_ref.first_ref = f32[4608,512]{1,0:T(8,128)S(1)} custom-call(bf16[18,256,256]{2,1,0:T(8,128)(2,1)S(1)} %permute.1.moved_ref, bf16[4608,512]{1,0:T(8,128)(2,1)S(1)} %bitcast.1, f32[64,384]{1,0:T(8,128)S(1)} %get-tuple-element.20.refs_0_), custom_call_target="tpu_custom_call" | custom-call | flops 8800000000 | tf_op jit(solution)/shard_map/solve/pallas_call | solution.py:396
  34.1 0.0 collective-permute-done.6.refs_1_
  34.1 0.0 collective-permute-done.7.refs_2_
  34.1 0.0 collective-permute-done.8.refs_3_
  34.1 0.0 copy-start
  34.1 0.1 collective-permute-start.9
  34.2 0.0 collective-permute-done.14.got_ref
  34.2 0.2 level2.1.refs_1_
  34.4 1.3 %collective-permute-start.20 = (f32[64,256]{1,0:T(8,128)S(1)}, f32[64,256]{1,0:T(8,128)S(1)}, u32[]{:S(2)}, u32[]{:S(2)}) collective-permute-start(f32[64,256]{1,0:T(8,128)S(1)} %pack.1.ref), channel_id=1, source_target_pairs={{0,6},{1,7},{2,4},{3,5},{4,2},{5,3},{6,0},{7,1},{8,14},{9,15},{10,... | collective-permute-start | bytes 196616 | tf_op jit(solution)/shard_map/ppermute | solution.py:35
  35.8 1.2 %collective-permute-start.16 = (f32[64,256]{1,0:T(8,128)S(1)}, f32[64,256]{1,0:T(8,128)S(1)}, u32[]{:S(2)}, u32[]{:S(2)}) collective-permute-start(f32[64,256]{1,0:T(8,128)S(1)} %pack.1.ref), channel_id=1, source_target_pairs={{0,2},{1,3},{2,0},{3,1},{4,6},{5,7},{6,4},{7,5},{8,10},{9,11},{10,... | collective-permute-start | bytes 196616 | tf_op jit(solution)/shard_map/ppermute | solution.py:35
  37.0 1.0 %collective-permute-start.18 = (f32[64,256]{1,0:T(8,128)S(1)}, f32[64,256]{1,0:T(8,128)S(1)}, u32[]{:S(2)}, u32[]{:S(2)}) collective-permute-start(f32[64,256]{1,0:T(8,128)S(1)} %pack.1.ref), channel_id=1, source_target_pairs={{0,4},{1,5},{2,6},{3,7},{4,0},{5,1},{6,2},{7,3},{8,12},{9,13},{10,... | collective-permute-start | bytes 196616 | tf_op jit(solution)/shard_map/ppermute | solution.py:35
  38.0 0.0 collective-permute-done.9.pair_ref
  38.0 1.6 %apply.1.after_ref.refs_8_ = f32[4608,512]{1,0:T(8,128)S(1)} custom-call(f32[4,64,128]{2,1,0:T(8,128)S(1)} %stack.1.own_ref, f32[4,64,128]{2,1,0:T(8,128)S(1)} %collective-permute-done.9.pair_ref, f32[4608,512]{1,0:T(8,128)S(1)} %solve.1.after_ref.first_ref, bf16[3,4608,128]{2,1,0:T(8,128)(2,1)S(1)} %copy-done), custom_call_target="tpu_custom_call" | custom-call | flops 1980000000 | tf_op jit(solution)/shard_map/apply/pallas_call | solution.py:418
  39.6 0.1 collective-permute-start.15
  39.7 0.6 %collective-permute-done.20.ref = f32[64,256]{1,0:T(8,128)S(1)} collective-permute-done((f32[64,256]{1,0:T(8,128)S(1)}, f32[64,256]{1,0:T(8,128)S(1)}, u32[]{:S(2)}, u32[]{:S(2)}) %collective-permute-start.20) | collective-permute-done | bytes 65568 | tf_op jit(solution)/shard_map/ppermute | solution.py:35
  40.3 0.0 collective-permute-start.21
  40.3 0.6 %collective-permute-done.16.refs_2_ = f32[64,256]{1,0:T(8,128)S(1)} collective-permute-done((f32[64,256]{1,0:T(8,128)S(1)}, f32[64,256]{1,0:T(8,128)S(1)}, u32[]{:S(2)}, u32[]{:S(2)}) %collective-permute-start.16) | collective-permute-done | bytes 65568 | tf_op jit(solution)/shard_map/ppermute | solution.py:35
  40.9 0.0 collective-permute-start.17
  40.9 0.4 collective-permute-done.18.refs_4_
  41.3 0.1 collective-permute-start.19
  41.4 0.0 collective-permute-done.15.refs_1_
  41.4 0.2 collective-permute-done.21.refs_7_
  41.5 0.6 %collective-permute-done.17.refs_3_ = f32[64,256]{1,0:T(8,128)S(1)} collective-permute-done((f32[64,256]{1,0:T(8,128)S(1)}, f32[64,256]{1,0:T(8,128)S(1)}, u32[]{:S(2)}, u32[]{:S(2)}) %collective-permute-start.17) | collective-permute-done | bytes 65568 | tf_op jit(solution)/shard_map/ppermute | solution.py:35
  42.1 0.4 collective-permute-done.19.refs_5_
  42.6 4.3 %expand.1 = f32[4608,512]{1,0:T(8,128)} custom-call(f32[64,256]{1,0:T(8,128)S(1)} %relay.2.refs_0_, f32[64,256]{1,0:T(8,128)S(1)} %collective-permute-done.15.refs_1_, f32[64,256]{1,0:T(8,128)S(1)} %collective-permute-done.16.refs_2_, f32[64,256]{1,0:T(8,128)S(1)} %collective-permute-done.17.refs_3_, f32[64,256]{1,0:T(8,128)S(1)} %collective-permute-done.18.refs_4_, ...), custom_call_target="tpu_custom_call" | custom-call | flops 5500000256 | tf_op jit(solution)/shard_map/expand/pallas_call | solution.py:440
  (13 shorter events, 0.1 us)
Async XLA Ops:
  0.0 3.9 %copy-start.2 = (s32[18,256]{1,0:T(8,128)S(1)}, s32[18,256]{1,0:T(8,128)}, u32[]{:S(2)}) copy-start(s32[18,256]{1,0:T(8,128)} %order_ref.1) | copy-start | bytes 55300
  0.0 3.9 %copy-start.1 = (bf16[18,256,256]{2,1,0:T(8,128)(2,1)S(1)}, bf16[18,256,256]{2,1,0:T(8,128)(2,1)}, u32[]{:S(2)}) copy-start(bf16[18,256,256]{2,1,0:T(8,128)(2,1)} %inv_ref.1) | copy-start | bytes 7077892
  3.4 1.6 %collective-permute-start = (f32[64,384]{1,0:T(8,128)S(1)}, f32[64,384]{1,0:T(8,128)S(1)}, u32[]{:S(2)}, u32[]{:S(2)}) collective-permute-start(f32[64,384]{1,0:T(8,128)S(1)} %get-tuple-element.19), channel_id=1, source_target_pairs={{0,1},{1,0},{2,3},{3,2},{4,5},{5,4},{6,7},{7,6},{8,9},{9,8},{10,11... | collective-permute-start | bytes 294920 | tf_op jit(solution)/shard_map/ppermute | solution.py:35
  4.9 4.4 %slice-start = ((s8[4718592]{0:T(1024)(128)(4,1)}), s8[4194304]{0:T(1024)(128)(4,1)S(1)}, s32[]{:S(2)}) async-start(s8[4718592]{0:T(1024)(128)(4,1)} %bitcast), calls=%async_computation | async-start | bytes 8388608
  5.0 6.5 %collective-permute-start.1 = (f32[64,384]{1,0:T(8,128)S(1)}, f32[64,384]{1,0:T(8,128)S(1)}, u32[]{:S(2)}, u32[]{:S(2)}) collective-permute-start(f32[64,384]{1,0:T(8,128)S(1)} %add.2.after_ref.mine_ref), channel_id=1, source_target_pairs={{0,2},{1,3},{2,0},{3,1},{4,6},{5,7},{6,4},{7,5},{8,10},{9,11},{10,... | collective-permute-start | bytes 294920 | tf_op jit(solution)/shard_map/ppermute | solution.py:35
  7.7 1.6 %slice-start.1 = ((s8[4718592]{0:T(1024)(128)(4,1)}), s8[524288]{0:T(1024)(128)(4,1)S(1)}, s32[]{:S(2)}) async-start(s8[4718592]{0:T(1024)(128)(4,1)} %bitcast), calls=%async_computation.1 | async-start | bytes 1048576
  11.4 3.7 %collective-permute-start.2 = (f32[384,256]{1,0:T(8,128)S(1)}, f32[384,256]{1,0:T(8,128)S(1)}, u32[]{:S(2)}, u32[]{:S(2)}) collective-permute-start(f32[384,256]{1,0:T(8,128)S(1)} %project_other.1), channel_id=1, source_target_pairs={{0,1},{1,0},{2,3},{3,2},{4,5},{5,4},{6,7},{7,6},{8,9},{9,8},{10,11... | collective-permute-start | bytes 1179656 | tf_op jit(solution)/shard_map/ppermute | solution.py:35
  11.5 7.4 %copy-start.3 = (s32[3,128]{1,0:T(4,128)S(1)}, s32[3,128]{1,0:T(4,128)}, u32[]{:S(2)}) copy-start(s32[3,128]{1,0:T(4,128)} %perm_ref.1) | copy-start | bytes 4612
  11.5 9.1 %collective-permute-start.10 = (f32[64,384]{1,0:T(8,128)S(1)}, f32[64,384]{1,0:T(8,128)S(1)}, u32[]{:S(2)}, u32[]{:S(2)}) collective-permute-start(f32[64,384]{1,0:T(8,128)S(1)} %add.3.after_ref.mine_ref), channel_id=1, source_target_pairs={{0,4},{1,5},{2,6},{3,7},{4,0},{5,1},{6,2},{7,3},{8,12},{9,13},{10,... | collective-permute-start | bytes 294920 | tf_op jit(solution)/shard_map/ppermute | solution.py:35
  15.3 5.8 %collective-permute-start.3 = (f32[64,384]{1,0:T(8,128)S(1)}, f32[64,384]{1,0:T(8,128)S(1)}, u32[]{:S(2)}, u32[]{:S(2)}) collective-permute-start(f32[64,384]{1,0:T(8,128)S(1)} %get-tuple-element.21), channel_id=1, source_target_pairs={{0,2},{1,3},{2,0},{3,1},{4,6},{5,7},{6,4},{7,5},{8,10},{9,11},{10,... | collective-permute-start | bytes 294920 | tf_op jit(solution)/shard_map/ppermute | solution.py:35
  16.6 6.4 %collective-permute-start.4 = (f32[64,384]{1,0:T(8,128)S(1)}, f32[64,384]{1,0:T(8,128)S(1)}, u32[]{:S(2)}, u32[]{:S(2)}) collective-permute-start(f32[64,384]{1,0:T(8,128)S(1)} %get-tuple-element.22), channel_id=1, source_target_pairs={{0,4},{1,5},{2,6},{3,7},{4,0},{5,1},{6,2},{7,3},{8,12},{9,13},{10,... | collective-permute-start | bytes 294920 | tf_op jit(solution)/shard_map/ppermute | solution.py:35
  17.1 5.9 %collective-permute-start.5 = (f32[64,384]{1,0:T(8,128)S(1)}, f32[64,384]{1,0:T(8,128)S(1)}, u32[]{:S(2)}, u32[]{:S(2)}) collective-permute-start(f32[64,384]{1,0:T(8,128)S(1)} %get-tuple-element.23), channel_id=1, source_target_pairs={{0,6},{1,7},{2,4},{3,5},{4,2},{5,3},{6,0},{7,1},{8,14},{9,15},{10,... | collective-permute-start | bytes 294920 | tf_op jit(solution)/shard_map/ppermute | solution.py:35
  20.6 2.7 %collective-permute-start.11 = (f32[64,384]{1,0:T(8,128)S(1)}, f32[64,384]{1,0:T(8,128)S(1)}, u32[]{:S(2)}, u32[]{:S(2)}) collective-permute-start(f32[64,384]{1,0:T(8,128)S(1)} %add.3.after_ref.mine_ref), channel_id=1, source_target_pairs={{0,1},{1,0},{2,3},{3,2},{4,5},{5,4},{6,7},{7,6},{8,9},{9,8},{10,11... | collective-permute-start | bytes 294920 | tf_op jit(solution)/shard_map/ppermute | solution.py:35
  20.6 2.6 %collective-permute-start.12 = (f32[64,384]{1,0:T(8,128)S(1)}, f32[64,384]{1,0:T(8,128)S(1)}, u32[]{:S(2)}, u32[]{:S(2)}) collective-permute-start(f32[64,384]{1,0:T(8,128)S(1)} %collective-permute-done.10.theirs_ref), channel_id=1, source_target_pairs={{0,1},{1,0},{2,3},{3,2},{4,5},{5,4},{6,7},{7,6},{8,9},{9,8},{10,11... | collective-permute-start | bytes 294920 | tf_op jit(solution)/shard_map/ppermute | solution.py:35
  23.6 5.2 %collective-permute-start.13 = (f32[256,128]{1,0:T(8,128)S(1)}, f32[256,128]{1,0:T(8,128)S(1)}, u32[]{:S(2)}, u32[]{:S(2)}) collective-permute-start(f32[256,128]{1,0:T(8,128)S(1)} %correct.1.sent_ref), channel_id=1, source_target_pairs={{0,8},{8,0},{16,24},{24,16},{1,9},{9,1},{17,25},{25,17},{2,10},{10... | collective-permute-start | bytes 393224 | tf_op jit(solution)/shard_map/ppermute | solution.py:35
  25.3 8.8 %collective-permute-start.6 = (f32[64,128]{1,0:T(8,128)S(1)}, f32[64,128]{1,0:T(8,128)S(1)}, u32[]{:S(2)}, u32[]{:S(2)}) collective-permute-start(f32[64,128]{1,0:T(8,128)S(1)} %get-tuple-element.24.refs_0_.own_ref), channel_id=1, source_target_pairs={{0,2},{1,3},{2,0},{3,1},{4,6},{5,7},{6,4},{7,5},{8,10},{9,11},{10,... | collective-permute-start | bytes 98312 | tf_op jit(solution)/shard_map/ppermute | solution.py:35
  26.3 7.8 %collective-permute-start.7 = (f32[64,128]{1,0:T(8,128)S(1)}, f32[64,128]{1,0:T(8,128)S(1)}, u32[]{:S(2)}, u32[]{:S(2)}) collective-permute-start(f32[64,128]{1,0:T(8,128)S(1)} %get-tuple-element.25.other_ref), channel_id=1, source_target_pairs={{0,4},{1,5},{2,6},{3,7},{4,0},{5,1},{6,2},{7,3},{8,12},{9,13},{10,... | collective-permute-start | bytes 98312 | tf_op jit(solution)/shard_map/ppermute | solution.py:35
  27.1 7.0 %collective-permute-start.8 = (f32[64,128]{1,0:T(8,128)S(1)}, f32[64,128]{1,0:T(8,128)S(1)}, u32[]{:S(2)}, u32[]{:S(2)}) collective-permute-start(f32[64,128]{1,0:T(8,128)S(1)} %get-tuple-element.25.other_ref), channel_id=1, source_target_pairs={{0,6},{1,7},{2,4},{3,5},{4,2},{5,3},{6,0},{7,1},{8,14},{9,15},{10,... | collective-permute-start | bytes 98312 | tf_op jit(solution)/shard_map/ppermute | solution.py:35
  29.2 5.0 %collective-permute-start.14 = (f32[64,128]{1,0:T(8,128)S(1)}, f32[64,128]{1,0:T(8,128)S(1)}, u32[]{:S(2)}, u32[]{:S(2)}) collective-permute-start(f32[64,128]{1,0:T(8,128)S(1)} %get-tuple-element.28.sent_ref), channel_id=1, source_target_pairs={{0,16},{8,24},{16,0},{24,8},{1,17},{9,25},{17,1},{25,9},{2,18},{10... | collective-permute-start | bytes 98312 | tf_op jit(solution)/shard_map/ppermute | solution.py:35
  34.1 3.9 %copy-start = (bf16[3,4608,128]{2,1,0:T(8,128)(2,1)S(1)}, bf16[3,4608,128]{2,1,0:T(8,128)(2,1)}, u32[]{:S(2)}) copy-start(bf16[3,4608,128]{2,1,0:T(8,128)(2,1)} %refs_9_.1) | copy-start | bytes 10616836
  34.1 3.9 %collective-permute-start.9 = (f32[4,64,128]{2,1,0:T(8,128)S(1)}, f32[4,64,128]{2,1,0:T(8,128)S(1)}, u32[]{:S(2)}, u32[]{:S(2)}) collective-permute-start(f32[4,64,128]{2,1,0:T(8,128)S(1)} %stack.1.own_ref), channel_id=1, source_target_pairs={{0,1},{1,0},{2,3},{3,2},{4,5},{5,4},{6,7},{7,6},{8,9},{9,8},{10,11... | collective-permute-start | bytes 393224 | tf_op jit(solution)/shard_map/ppermute | solution.py:35
  34.4 5.9 %collective-permute-start.20 = (f32[64,256]{1,0:T(8,128)S(1)}, f32[64,256]{1,0:T(8,128)S(1)}, u32[]{:S(2)}, u32[]{:S(2)}) collective-permute-start(f32[64,256]{1,0:T(8,128)S(1)} %pack.1.ref), channel_id=1, source_target_pairs={{0,6},{1,7},{2,4},{3,5},{4,2},{5,3},{6,0},{7,1},{8,14},{9,15},{10,... | collective-permute-start | bytes 196616 | tf_op jit(solution)/shard_map/ppermute | solution.py:35
  35.8 5.1 %collective-permute-start.16 = (f32[64,256]{1,0:T(8,128)S(1)}, f32[64,256]{1,0:T(8,128)S(1)}, u32[]{:S(2)}, u32[]{:S(2)}) collective-permute-start(f32[64,256]{1,0:T(8,128)S(1)} %pack.1.ref), channel_id=1, source_target_pairs={{0,2},{1,3},{2,0},{3,1},{4,6},{5,7},{6,4},{7,5},{8,10},{9,11},{10,... | collective-permute-start | bytes 196616 | tf_op jit(solution)/shard_map/ppermute | solution.py:35
  37.0 4.3 %collective-permute-start.18 = (f32[64,256]{1,0:T(8,128)S(1)}, f32[64,256]{1,0:T(8,128)S(1)}, u32[]{:S(2)}, u32[]{:S(2)}) collective-permute-start(f32[64,256]{1,0:T(8,128)S(1)} %pack.1.ref), channel_id=1, source_target_pairs={{0,4},{1,5},{2,6},{3,7},{4,0},{5,1},{6,2},{7,3},{8,12},{9,13},{10,... | collective-permute-start | bytes 196616 | tf_op jit(solution)/shard_map/ppermute | solution.py:35
  39.6 1.8 %collective-permute-start.15 = (f32[64,256]{1,0:T(8,128)S(1)}, f32[64,256]{1,0:T(8,128)S(1)}, u32[]{:S(2)}, u32[]{:S(2)}) collective-permute-start(f32[64,256]{1,0:T(8,128)S(1)} %relay.2.refs_0_), channel_id=1, source_target_pairs={{0,1},{1,0},{2,3},{3,2},{4,5},{5,4},{6,7},{7,6},{8,9},{9,8},{10,11... | collective-permute-start | bytes 196616 | tf_op jit(solution)/shard_map/ppermute | solution.py:35
  40.3 1.3 %collective-permute-start.21 = (f32[64,256]{1,0:T(8,128)S(1)}, f32[64,256]{1,0:T(8,128)S(1)}, u32[]{:S(2)}, u32[]{:S(2)}) collective-permute-start(f32[64,256]{1,0:T(8,128)S(1)} %relay.3.refs_6_), channel_id=1, source_target_pairs={{0,1},{1,0},{2,3},{3,2},{4,5},{5,4},{6,7},{7,6},{8,9},{9,8},{10,11... | collective-permute-start | bytes 196616 | tf_op jit(solution)/shard_map/ppermute | solution.py:35
  40.9 1.3 %collective-permute-start.17 = (f32[64,256]{1,0:T(8,128)S(1)}, f32[64,256]{1,0:T(8,128)S(1)}, u32[]{:S(2)}, u32[]{:S(2)}) collective-permute-start(f32[64,256]{1,0:T(8,128)S(1)} %collective-permute-done.16.refs_2_), channel_id=1, source_target_pairs={{0,1},{1,0},{2,3},{3,2},{4,5},{5,4},{6,7},{7,6},{8,9},{9,8},{10,11... | collective-permute-start | bytes 196616 | tf_op jit(solution)/shard_map/ppermute | solution.py:35
  41.3 1.3 %collective-permute-start.19 = (f32[64,256]{1,0:T(8,128)S(1)}, f32[64,256]{1,0:T(8,128)S(1)}, u32[]{:S(2)}, u32[]{:S(2)}) collective-permute-start(f32[64,256]{1,0:T(8,128)S(1)} %collective-permute-done.18.refs_4_), channel_id=1, source_target_pairs={{0,1},{1,0},{2,3},{3,2},{4,5},{5,4},{6,7},{7,6},{8,9},{9,8},{10,11... | collective-permute-start | bytes 196616 | tf_op jit(solution)/shard_map/ppermute | solution.py:35

commit v17 on v16

--- a/solution.py
+++ b/solution.py
@@ -380,6 +380,12 @@
     def message_shape(level):
         return floats((levels - level) * share + len(below_pairs(levels, level)) * rank, rank)
 
+    def relay(after, value):
+        return pl.pallas_call(
+            relay_kernel, out_shape=floats(*value.shape), name="relay", **settings(8, 0.1),
+        )(after, value)
+
+    parts[-1] = relay(prepared, parts[-1])
     own, other, rest = pl.pallas_call(
         functools.partial(node_kernel, rank, slots),
         out_shape=[floats(share, rank)] * 2 + [floats(share, size)],
@@ -433,9 +439,7 @@
     for slot in range(slots):
         piece = swap(pack, "rows", 2 * slot) if slot > 0 else pack
         if slot in (0, slots - 1):
-            piece = pl.pallas_call(
-                relay_kernel, out_shape=floats(share, size), name="relay", **settings(8, 0.1),
-            )(second, piece)
+            piece = relay(second, piece)
         pieces += [piece, swap(piece, "rows", 1)]
     return pl.pallas_call(
         functools.partial(expand_kernel, levels, width, count),

time: 47 us -> 47.4 us (level)
  transfers between devices with their start and end apart: 22 -> 22, of which waited for: 7 -> 9; matrix products, arithmetic and copies ran while one was open for 0% -> 0% of each run, Pallas kernels for 28% -> 28%
where the time goes in v17:
time: 47.4 us; the launch traced here: 47.3 us
  Pallas kernels  21.1 us (45%)
  starting transfers between devices  21 us (44%)
  waiting for transfers between devices  4.76 us (10%)
    ppermute x22, starting transfers between devices, swap(): return lax.ppermute(value, axis, [(i, i ^ mask) for i in range(count)])  21 us
    ppermute x22, waiting for transfers between devices, swap(): return lax.ppermute(value, axis, [(i, i ^ mask) for i in range(count)])  4.76 us
    pallas_call x1, Pallas kernels, per_device(): pl.pallas_call(functools.partial(expand_kernel, levels, width, count), ou...  4.28 us
    pallas_call x2, Pallas kernels, project(): pl.pallas_call(functools.partial(project_kernel, other), out_shape=floats...  3.99 us
    pallas_call x1, Pallas kernels, per_device(): pl.pallas_call(functools.partial(gram_kernel, levels, per_step, width), i...  3.34 us
    pallas_call x1, Pallas kernels, per_device(): pl.pallas_call(functools.partial(solve_kernel, per_step, width), out_shap...  2.22 us
    pallas_call x1, Pallas kernels, per_device(): pl.pallas_call(functools.partial(prepare_kernel, levels), in_specs=[pl.Bl...  1.68 us
    pallas_call x1, Pallas kernels, per_device(): pl.pallas_call(functools.partial(weigh_kernel, blocks_per_step(nblocks, 9...  1.6 us
  transfers between devices with their start and end apart: 22, of which 9 were waited for; matrix products, arithmetic and copies ran while one was open for 0% of the time, Pallas kernels for 28%

profile of v17, /device:TPU:0, one launch (start us, length us, event | category | flops | bytes accessed | tf_op | source)
XLA Modules:
  0.0 47.3 jit_solution(6860470303998987709)
XLA Ops:
  0.0 3.3 %gram.1 = (bf16[384,4608]{1,0:T(8,128)(2,1)S(1)}, f32[64,384]{1,0:T(8,128)S(1)}, f32[64,384]{1,0:T(8,128)S(1)}) custom-call(bf16[3,4608,128]{2,1,0:T(8,128)(2,1)} %right_ref.1, bf16[3,4608,128]{2,1,0:T(8,128)(2,1)} %refs_9_.1), custom_call_target="tpu_custom_call" | custom-call | flops 3300000000 | tf_op jit(solution)/shard_map/gram/pallas_call | solution.py:310
  3.4 0.5 %collective-permute-start = (f32[64,384]{1,0:T(8,128)S(1)}, f32[64,384]{1,0:T(8,128)S(1)}, u32[]{:S(2)}, u32[]{:S(2)}) collective-permute-start(f32[64,384]{1,0:T(8,128)S(1)} %get-tuple-element.19), channel_id=1, source_target_pairs={{0,1},{1,0},{2,3},{3,2},{4,5},{5,4},{6,7},{7,6},{8,9},{9,8},{10,11... | collective-permute-start | bytes 294920 | tf_op jit(solution)/shard_map/ppermute | solution.py:35
  3.9 0.0 copy-done.2
  3.9 0.0 copy-done.1
  3.9 1.0 %permute.1.moved_ref = bf16[18,256,256]{2,1,0:T(8,128)(2,1)S(1)} custom-call(s32[18,256]{1,0:T(8,128)S(1)} %copy-done.2, bf16[18,256,256]{2,1,0:T(8,128)(2,1)S(1)} %copy-done.1), custom_call_target="tpu_custom_call" | custom-call | flops 1650000000 | tf_op jit(solution)/shard_map/permute/pallas_call | solution.py:326
  4.9 0.0 collective-permute-done.got_ref
  4.9 0.0 slice-start
  5.0 2.8 %collective-permute-start.1 = (f32[64,384]{1,0:T(8,128)S(1)}, f32[64,384]{1,0:T(8,128)S(1)}, u32[]{:S(2)}, u32[]{:S(2)}) collective-permute-start(f32[64,384]{1,0:T(8,128)S(1)} %add.2.after_ref.mine_ref), channel_id=1, source_target_pairs={{0,2},{1,3},{2,0},{3,1},{4,6},{5,7},{6,4},{7,5},{8,10},{9,11},{10,... | collective-permute-start | bytes 294920 | tf_op jit(solution)/shard_map/ppermute | solution.py:35
  7.7 1.6 %weigh.1.factor_ref = bf16[768,4608]{1,0:T(8,128)(2,1)S(1)} custom-call(bf16[18,256,256]{2,1,0:T(8,128)(2,1)S(1)} %permute.1.moved_ref, bf16[384,4608]{1,0:T(8,128)(2,1)S(1)} %get-tuple-element.17.flip_ref, f32[64,384]{1,0:T(8,128)S(1)} %add.2.after_ref.mine_ref), custom_call_target="tpu_custom_call" | custom-call | flops 2640000000 | tf_op jit(solution)/shard_map/weigh/pallas_call | solution.py:339
  9.4 0.0 slice-done
  9.4 2.0 %project_other.1 = f32[384,256]{1,0:T(8,128)S(1)} custom-call(bf16[768,4608]{1,0:T(8,128)(2,1)S(1)} %weigh.1.factor_ref, bf16[4608,512]{1,0:T(8,128)(2,1)S(1)} %bitcast.1, f32[64,384]{1,0:T(8,128)S(1)} %add.2.after_ref.mine_ref), custom_call_target="tpu_custom_call" | custom-call | flops 1100000000 | tf_op jit(solution)/shard_map/project_other/pallas_call | solution.py:347
  11.4 0.1 collective-permute-start.2
  11.5 0.0 collective-permute-done.1.got_ref
  11.5 0.0 copy-start.3
  11.5 1.6 %collective-permute-start.10 = (f32[64,384]{1,0:T(8,128)S(1)}, f32[64,384]{1,0:T(8,128)S(1)}, u32[]{:S(2)}, u32[]{:S(2)}) collective-permute-start(f32[64,384]{1,0:T(8,128)S(1)} %add.3.after_ref.mine_ref), channel_id=1, source_target_pairs={{0,4},{1,5},{2,6},{3,7},{4,0},{5,1},{6,2},{7,3},{8,12},{9,13},{10,... | collective-permute-start | bytes 294920 | tf_op jit(solution)/shard_map/ppermute | solution.py:35
  13.1 2.0 %project_own.1.keep_ref = f32[384,256]{1,0:T(8,128)S(1)} custom-call(bf16[768,4608]{1,0:T(8,128)(2,1)S(1)} %weigh.1.factor_ref, bf16[4608,512]{1,0:T(8,128)(2,1)S(1)} %bitcast.1, f32[64,384]{1,0:T(8,128)S(1)} %add.3.after_ref.mine_ref), custom_call_target="tpu_custom_call" | custom-call | flops 4400000000 | tf_op jit(solution)/shard_map/project_own/pallas_call | solution.py:347
  15.1 0.0 collective-permute-done.2.got_ref
  15.1 0.2 merge.1
  15.3 1.2 %collective-permute-start.5 = (f32[64,384]{1,0:T(8,128)S(1)}, f32[64,384]{1,0:T(8,128)S(1)}, u32[]{:S(2)}, u32[]{:S(2)}) collective-permute-start(f32[64,384]{1,0:T(8,128)S(1)} %get-tuple-element.23), channel_id=1, source_target_pairs={{0,6},{1,7},{2,4},{3,5},{4,2},{5,3},{6,0},{7,1},{8,14},{9,15},{10,... | collective-permute-start | bytes 294920 | tf_op jit(solution)/shard_map/ppermute | solution.py:35
  16.6 0.8 %collective-permute-start.3 = (f32[64,384]{1,0:T(8,128)S(1)}, f32[64,384]{1,0:T(8,128)S(1)}, u32[]{:S(2)}, u32[]{:S(2)}) collective-permute-start(f32[64,384]{1,0:T(8,128)S(1)} %get-tuple-element.21), channel_id=1, source_target_pairs={{0,2},{1,3},{2,0},{3,1},{4,6},{5,7},{6,4},{7,5},{8,10},{9,11},{10,... | collective-permute-start | bytes 294920 | tf_op jit(solution)/shard_map/ppermute | solution.py:35
  17.4 1.5 %collective-permute-start.4 = (f32[64,384]{1,0:T(8,128)S(1)}, f32[64,384]{1,0:T(8,128)S(1)}, u32[]{:S(2)}, u32[]{:S(2)}) collective-permute-start(f32[64,384]{1,0:T(8,128)S(1)} %get-tuple-element.22), channel_id=1, source_target_pairs={{0,4},{1,5},{2,6},{3,7},{4,0},{5,1},{6,2},{7,3},{8,12},{9,13},{10,... | collective-permute-start | bytes 294920 | tf_op jit(solution)/shard_map/ppermute | solution.py:35
  18.9 1.7 %prepare.1.after_ref.refs_4_.joined_ref = bf16[3,768,256]{2,1,0:T(8,128)(2,1)S(1)} custom-call(f32[7,256,256]{2,1,0:T(8,128)} %joined_ref.1, s32[3,128]{1,0:T(4,128)S(1)} %copy-done.3), custom_call_target="tpu_custom_call" | custom-call | flops 2200000000 | tf_op jit(solution)/shard_map/prepare/pallas_call | solution.py:371
  20.6 0.1 collective-permute-start.11
  20.7 0.0 collective-permute-done.10.theirs_ref
  20.7 0.5 %collective-permute-start.12 = (f32[64,384]{1,0:T(8,128)S(1)}, f32[64,384]{1,0:T(8,128)S(1)}, u32[]{:S(2)}, u32[]{:S(2)}) collective-permute-start(f32[64,384]{1,0:T(8,128)S(1)} %collective-permute-done.10.theirs_ref), channel_id=1, source_target_pairs={{0,1},{1,0},{2,3},{3,2},{4,5},{5,4},{6,7},{7,6},{8,9},{9,8},{10,11... | collective-permute-start | bytes 294920 | tf_op jit(solution)/shard_map/ppermute | solution.py:35
  21.2 0.8 %collective-permute-done.5.ref = f32[64,384]{1,0:T(8,128)S(1)} collective-permute-done((f32[64,384]{1,0:T(8,128)S(1)}, f32[64,384]{1,0:T(8,128)S(1)}, u32[]{:S(2)}, u32[]{:S(2)}) %collective-permute-start.5) | collective-permute-done | bytes 98336 | tf_op jit(solution)/shard_map/ppermute | solution.py:35
  21.9 0.4 collective-permute-done.3.refs_1_
  22.4 1.0 %collective-permute-done.4.refs_2_ = f32[64,384]{1,0:T(8,128)S(1)} collective-permute-done((f32[64,384]{1,0:T(8,128)S(1)}, f32[64,384]{1,0:T(8,128)S(1)}, u32[]{:S(2)}, u32[]{:S(2)}) %collective-permute-start.4) | collective-permute-done | bytes 98336 | tf_op jit(solution)/shard_map/ppermute | solution.py:35
  23.3 0.2 node.1
  23.5 0.0 collective-permute-done.11.pair_mine_ref
  23.5 0.0 collective-permute-done.12.pair_theirs_ref
  23.5 0.3 correct.1.sent_ref
  23.8 1.6 %collective-permute-start.13 = (f32[256,128]{1,0:T(8,128)S(1)}, f32[256,128]{1,0:T(8,128)S(1)}, u32[]{:S(2)}, u32[]{:S(2)}) collective-permute-start(f32[256,128]{1,0:T(8,128)S(1)} %correct.1.sent_ref), channel_id=1, source_target_pairs={{0,8},{8,0},{16,24},{24,16},{1,9},{9,1},{17,25},{25,17},{2,10},{10... | collective-permute-start | bytes 393224 | tf_op jit(solution)/shard_map/ppermute | solution.py:35
  25.5 0.7 %collective-permute-start.6 = (f32[64,128]{1,0:T(8,128)S(1)}, f32[64,128]{1,0:T(8,128)S(1)}, u32[]{:S(2)}, u32[]{:S(2)}) collective-permute-start(f32[64,128]{1,0:T(8,128)S(1)} %get-tuple-element.24.refs_0_.own_ref), channel_id=1, source_target_pairs={{0,2},{1,3},{2,0},{3,1},{4,6},{5,7},{6,4},{7,5},{8,10},{9,11},{10,... | collective-permute-start | bytes 98312 | tf_op jit(solution)/shard_map/ppermute | solution.py:35
  26.2 0.9 %collective-permute-start.7 = (f32[64,128]{1,0:T(8,128)S(1)}, f32[64,128]{1,0:T(8,128)S(1)}, u32[]{:S(2)}, u32[]{:S(2)}) collective-permute-start(f32[64,128]{1,0:T(8,128)S(1)} %get-tuple-element.25.other_ref), channel_id=1, source_target_pairs={{0,4},{1,5},{2,6},{3,7},{4,0},{5,1},{6,2},{7,3},{8,12},{9,13},{10,... | collective-permute-start | bytes 98312 | tf_op jit(solution)/shard_map/ppermute | solution.py:35
  27.1 1.9 %collective-permute-start.8 = (f32[64,128]{1,0:T(8,128)S(1)}, f32[64,128]{1,0:T(8,128)S(1)}, u32[]{:S(2)}, u32[]{:S(2)}) collective-permute-start(f32[64,128]{1,0:T(8,128)S(1)} %get-tuple-element.25.other_ref), channel_id=1, source_target_pairs={{0,6},{1,7},{2,4},{3,5},{4,2},{5,3},{6,0},{7,1},{8,14},{9,15},{10,... | collective-permute-start | bytes 98312 | tf_op jit(solution)/shard_map/ppermute | solution.py:35
  29.0 0.2 collective-permute-done.13.got_ref.after_ref
  29.2 0.4 level1.1
  29.6 2.7 %collective-permute-start.14 = (f32[64,128]{1,0:T(8,128)S(1)}, f32[64,128]{1,0:T(8,128)S(1)}, u32[]{:S(2)}, u32[]{:S(2)}) collective-permute-start(f32[64,128]{1,0:T(8,128)S(1)} %get-tuple-element.28.sent_ref), channel_id=1, source_target_pairs={{0,16},{8,24},{16,0},{24,8},{1,17},{9,25},{17,1},{25,9},{2,18},{10... | collective-permute-start | bytes 98312 | tf_op jit(solution)/shard_map/ppermute | solution.py:35
  32.3 2.2 %solve.1.after_ref.first_ref = f32[4608,512]{1,0:T(8,128)S(1)} custom-call(bf16[18,256,256]{2,1,0:T(8,128)(2,1)S(1)} %permute.1.moved_ref, bf16[4608,512]{1,0:T(8,128)(2,1)S(1)} %bitcast.1, f32[64,384]{1,0:T(8,128)S(1)} %get-tuple-element.20.refs_0_), custom_call_target="tpu_custom_call" | custom-call | flops 8800000000 | tf_op jit(solution)/shard_map/solve/pallas_call | solution.py:402
  34.5 0.0 collective-permute-done.6.refs_1_
  34.5 0.0 collective-permute-done.7.refs_2_
  34.5 0.0 collective-permute-done.8.refs_3_
  34.6 0.0 copy-start
  34.6 0.1 collective-permute-start.9
  34.6 0.0 collective-permute-done.14.got_ref
  34.7 0.2 level2.1.refs_1_
  34.9 0.9 %collective-permute-start.20 = (f32[64,256]{1,0:T(8,128)S(1)}, f32[64,256]{1,0:T(8,128)S(1)}, u32[]{:S(2)}, u32[]{:S(2)}) collective-permute-start(f32[64,256]{1,0:T(8,128)S(1)} %pack.1.ref), channel_id=1, source_target_pairs={{0,6},{1,7},{2,4},{3,5},{4,2},{5,3},{6,0},{7,1},{8,14},{9,15},{10,... | collective-permute-start | bytes 196616 | tf_op jit(solution)/shard_map/ppermute | solution.py:35
  35.7 1.0 %collective-permute-start.16 = (f32[64,256]{1,0:T(8,128)S(1)}, f32[64,256]{1,0:T(8,128)S(1)}, u32[]{:S(2)}, u32[]{:S(2)}) collective-permute-start(f32[64,256]{1,0:T(8,128)S(1)} %pack.1.ref), channel_id=1, source_target_pairs={{0,2},{1,3},{2,0},{3,1},{4,6},{5,7},{6,4},{7,5},{8,10},{9,11},{10,... | collective-permute-start | bytes 196616 | tf_op jit(solution)/shard_map/ppermute | solution.py:35
  36.7 1.7 %collective-permute-start.18 = (f32[64,256]{1,0:T(8,128)S(1)}, f32[64,256]{1,0:T(8,128)S(1)}, u32[]{:S(2)}, u32[]{:S(2)}) collective-permute-start(f32[64,256]{1,0:T(8,128)S(1)} %pack.1.ref), channel_id=1, source_target_pairs={{0,4},{1,5},{2,6},{3,7},{4,0},{5,1},{6,2},{7,3},{8,12},{9,13},{10,... | collective-permute-start | bytes 196616 | tf_op jit(solution)/shard_map/ppermute | solution.py:35
  38.4 0.0 collective-permute-done.9.pair_ref
  38.4 1.6 %apply.1.after_ref.refs_8_ = f32[4608,512]{1,0:T(8,128)S(1)} custom-call(f32[4,64,128]{2,1,0:T(8,128)S(1)} %stack.1.own_ref, f32[4,64,128]{2,1,0:T(8,128)S(1)} %collective-permute-done.9.pair_ref, f32[4608,512]{1,0:T(8,128)S(1)} %solve.1.after_ref.first_ref, bf16[3,4608,128]{2,1,0:T(8,128)(2,1)S(1)} %copy-done), custom_call_target="tpu_custom_call" | custom-call | flops 1980000000 | tf_op jit(solution)/shard_map/apply/pallas_call | solution.py:424
  40.0 0.1 collective-permute-start.15
  40.1 0.6 %collective-permute-done.20.ref = f32[64,256]{1,0:T(8,128)S(1)} collective-permute-done((f32[64,256]{1,0:T(8,128)S(1)}, f32[64,256]{1,0:T(8,128)S(1)}, u32[]{:S(2)}, u32[]{:S(2)}) %collective-permute-start.20) | collective-permute-done | bytes 65568 | tf_op jit(solution)/shard_map/ppermute | solution.py:35
  40.7 0.0 collective-permute-start.21
  40.7 0.0 collective-permute-done.16.refs_2_
  40.7 0.5 %collective-permute-start.17 = (f32[64,256]{1,0:T(8,128)S(1)}, f32[64,256]{1,0:T(8,128)S(1)}, u32[]{:S(2)}, u32[]{:S(2)}) collective-permute-start(f32[64,256]{1,0:T(8,128)S(1)} %collective-permute-done.16.refs_2_), channel_id=1, source_target_pairs={{0,1},{1,0},{2,3},{3,2},{4,5},{5,4},{6,7},{7,6},{8,9},{9,8},{10,11... | collective-permute-start | bytes 196616 | tf_op jit(solution)/shard_map/ppermute | solution.py:35
  41.2 0.5 %collective-permute-done.18.refs_4_ = f32[64,256]{1,0:T(8,128)S(1)} collective-permute-done((f32[64,256]{1,0:T(8,128)S(1)}, f32[64,256]{1,0:T(8,128)S(1)}, u32[]{:S(2)}, u32[]{:S(2)}) %collective-permute-start.18) | collective-permute-done | bytes 65568 | tf_op jit(solution)/shard_map/ppermute | solution.py:35
  41.7 0.0 collective-permute-start.19
  41.7 0.0 collective-permute-done.15.refs_1_
  41.7 0.3 collective-permute-done.21.refs_7_
  42.0 0.2 collective-permute-done.17.refs_3_
  42.1 0.8 %collective-permute-done.19.refs_5_ = f32[64,256]{1,0:T(8,128)S(1)} collective-permute-done((f32[64,256]{1,0:T(8,128)S(1)}, f32[64,256]{1,0:T(8,128)S(1)}, u32[]{:S(2)}, u32[]{:S(2)}) %collective-permute-start.19) | collective-permute-done | bytes 65568 | tf_op jit(solution)/shard_map/ppermute | solution.py:35
  43.0 4.3 %expand.1 = f32[4608,512]{1,0:T(8,128)} custom-call(f32[64,256]{1,0:T(8,128)S(1)} %relay.4.refs_0_, f32[64,256]{1,0:T(8,128)S(1)} %collective-permute-done.15.refs_1_, f32[64,256]{1,0:T(8,128)S(1)} %collective-permute-done.16.refs_2_, f32[64,256]{1,0:T(8,128)S(1)} %collective-permute-done.17.refs_3_, f32[64,256]{1,0:T(8,128)S(1)} %collective-permute-done.18.refs_4_, ...), custom_call_target="tpu_custom_call" | custom-call | flops 5500000256 | tf_op jit(solution)/shard_map/expand/pallas_call | solution.py:444
  (14 shorter events, 0.1 us)
Async XLA Ops:
  0.0 3.9 %copy-start.2 = (s32[18,256]{1,0:T(8,128)S(1)}, s32[18,256]{1,0:T(8,128)}, u32[]{:S(2)}) copy-start(s32[18,256]{1,0:T(8,128)} %order_ref.1) | copy-start | bytes 55300
  0.0 3.9 %copy-start.1 = (bf16[18,256,256]{2,1,0:T(8,128)(2,1)S(1)}, bf16[18,256,256]{2,1,0:T(8,128)(2,1)}, u32[]{:S(2)}) copy-start(bf16[18,256,256]{2,1,0:T(8,128)(2,1)} %inv_ref.1) | copy-start | bytes 7077892
  3.4 1.6 %collective-permute-start = (f32[64,384]{1,0:T(8,128)S(1)}, f32[64,384]{1,0:T(8,128)S(1)}, u32[]{:S(2)}, u32[]{:S(2)}) collective-permute-start(f32[64,384]{1,0:T(8,128)S(1)} %get-tuple-element.19), channel_id=1, source_target_pairs={{0,1},{1,0},{2,3},{3,2},{4,5},{5,4},{6,7},{7,6},{8,9},{9,8},{10,11... | collective-permute-start | bytes 294920 | tf_op jit(solution)/shard_map/ppermute | solution.py:35
  4.9 4.4 %slice-start = ((s8[4718592]{0:T(1024)(128)(4,1)}), s8[4194304]{0:T(1024)(128)(4,1)S(1)}, s32[]{:S(2)}) async-start(s8[4718592]{0:T(1024)(128)(4,1)} %bitcast), calls=%async_computation | async-start | bytes 8388608
  5.0 6.5 %collective-permute-start.1 = (f32[64,384]{1,0:T(8,128)S(1)}, f32[64,384]{1,0:T(8,128)S(1)}, u32[]{:S(2)}, u32[]{:S(2)}) collective-permute-start(f32[64,384]{1,0:T(8,128)S(1)} %add.2.after_ref.mine_ref), channel_id=1, source_target_pairs={{0,2},{1,3},{2,0},{3,1},{4,6},{5,7},{6,4},{7,5},{8,10},{9,11},{10,... | collective-permute-start | bytes 294920 | tf_op jit(solution)/shard_map/ppermute | solution.py:35
  7.7 1.6 %slice-start.1 = ((s8[4718592]{0:T(1024)(128)(4,1)}), s8[524288]{0:T(1024)(128)(4,1)S(1)}, s32[]{:S(2)}) async-start(s8[4718592]{0:T(1024)(128)(4,1)} %bitcast), calls=%async_computation.1 | async-start | bytes 1048576
  11.4 3.7 %collective-permute-start.2 = (f32[384,256]{1,0:T(8,128)S(1)}, f32[384,256]{1,0:T(8,128)S(1)}, u32[]{:S(2)}, u32[]{:S(2)}) collective-permute-start(f32[384,256]{1,0:T(8,128)S(1)} %project_other.1), channel_id=1, source_target_pairs={{0,1},{1,0},{2,3},{3,2},{4,5},{5,4},{6,7},{7,6},{8,9},{9,8},{10,11... | collective-permute-start | bytes 1179656 | tf_op jit(solution)/shard_map/ppermute | solution.py:35
  11.5 7.4 %copy-start.3 = (s32[3,128]{1,0:T(4,128)S(1)}, s32[3,128]{1,0:T(4,128)}, u32[]{:S(2)}) copy-start(s32[3,128]{1,0:T(4,128)} %perm_ref.1) | copy-start | bytes 4612
  11.5 9.1 %collective-permute-start.10 = (f32[64,384]{1,0:T(8,128)S(1)}, f32[64,384]{1,0:T(8,128)S(1)}, u32[]{:S(2)}, u32[]{:S(2)}) collective-permute-start(f32[64,384]{1,0:T(8,128)S(1)} %add.3.after_ref.mine_ref), channel_id=1, source_target_pairs={{0,4},{1,5},{2,6},{3,7},{4,0},{5,1},{6,2},{7,3},{8,12},{9,13},{10,... | collective-permute-start | bytes 294920 | tf_op jit(solution)/shard_map/ppermute | solution.py:35
  15.3 6.6 %collective-permute-start.5 = (f32[64,384]{1,0:T(8,128)S(1)}, f32[64,384]{1,0:T(8,128)S(1)}, u32[]{:S(2)}, u32[]{:S(2)}) collective-permute-start(f32[64,384]{1,0:T(8,128)S(1)} %get-tuple-element.23), channel_id=1, source_target_pairs={{0,6},{1,7},{2,4},{3,5},{4,2},{5,3},{6,0},{7,1},{8,14},{9,15},{10,... | collective-permute-start | bytes 294920 | tf_op jit(solution)/shard_map/ppermute | solution.py:35
  16.6 5.8 %collective-permute-start.3 = (f32[64,384]{1,0:T(8,128)S(1)}, f32[64,384]{1,0:T(8,128)S(1)}, u32[]{:S(2)}, u32[]{:S(2)}) collective-permute-start(f32[64,384]{1,0:T(8,128)S(1)} %get-tuple-element.21), channel_id=1, source_target_pairs={{0,2},{1,3},{2,0},{3,1},{4,6},{5,7},{6,4},{7,5},{8,10},{9,11},{10,... | collective-permute-start | bytes 294920 | tf_op jit(solution)/shard_map/ppermute | solution.py:35
  17.4 5.9 %collective-permute-start.4 = (f32[64,384]{1,0:T(8,128)S(1)}, f32[64,384]{1,0:T(8,128)S(1)}, u32[]{:S(2)}, u32[]{:S(2)}) collective-permute-start(f32[64,384]{1,0:T(8,128)S(1)} %get-tuple-element.22), channel_id=1, source_target_pairs={{0,4},{1,5},{2,6},{3,7},{4,0},{5,1},{6,2},{7,3},{8,12},{9,13},{10,... | collective-permute-start | bytes 294920 | tf_op jit(solution)/shard_map/ppermute | solution.py:35
  20.6 2.9 %collective-permute-start.11 = (f32[64,384]{1,0:T(8,128)S(1)}, f32[64,384]{1,0:T(8,128)S(1)}, u32[]{:S(2)}, u32[]{:S(2)}) collective-permute-start(f32[64,384]{1,0:T(8,128)S(1)} %add.3.after_ref.mine_ref), channel_id=1, source_target_pairs={{0,1},{1,0},{2,3},{3,2},{4,5},{5,4},{6,7},{7,6},{8,9},{9,8},{10,11... | collective-permute-start | bytes 294920 | tf_op jit(solution)/shard_map/ppermute | solution.py:35
  20.7 2.9 %collective-permute-start.12 = (f32[64,384]{1,0:T(8,128)S(1)}, f32[64,384]{1,0:T(8,128)S(1)}, u32[]{:S(2)}, u32[]{:S(2)}) collective-permute-start(f32[64,384]{1,0:T(8,128)S(1)} %collective-permute-done.10.theirs_ref), channel_id=1, source_target_pairs={{0,1},{1,0},{2,3},{3,2},{4,5},{5,4},{6,7},{7,6},{8,9},{9,8},{10,11... | collective-permute-start | bytes 294920 | tf_op jit(solution)/shard_map/ppermute | solution.py:35
  23.8 5.4 %collective-permute-start.13 = (f32[256,128]{1,0:T(8,128)S(1)}, f32[256,128]{1,0:T(8,128)S(1)}, u32[]{:S(2)}, u32[]{:S(2)}) collective-permute-start(f32[256,128]{1,0:T(8,128)S(1)} %correct.1.sent_ref), channel_id=1, source_target_pairs={{0,8},{8,0},{16,24},{24,16},{1,9},{9,1},{17,25},{25,17},{2,10},{10... | collective-permute-start | bytes 393224 | tf_op jit(solution)/shard_map/ppermute | solution.py:35
  25.5 9.0 %collective-permute-start.6 = (f32[64,128]{1,0:T(8,128)S(1)}, f32[64,128]{1,0:T(8,128)S(1)}, u32[]{:S(2)}, u32[]{:S(2)}) collective-permute-start(f32[64,128]{1,0:T(8,128)S(1)} %get-tuple-element.24.refs_0_.own_ref), channel_id=1, source_target_pairs={{0,2},{1,3},{2,0},{3,1},{4,6},{5,7},{6,4},{7,5},{8,10},{9,11},{10,... | collective-permute-start | bytes 98312 | tf_op jit(solution)/shard_map/ppermute | solution.py:35
  26.2 8.3 %collective-permute-start.7 = (f32[64,128]{1,0:T(8,128)S(1)}, f32[64,128]{1,0:T(8,128)S(1)}, u32[]{:S(2)}, u32[]{:S(2)}) collective-permute-start(f32[64,128]{1,0:T(8,128)S(1)} %get-tuple-element.25.other_ref), channel_id=1, source_target_pairs={{0,4},{1,5},{2,6},{3,7},{4,0},{5,1},{6,2},{7,3},{8,12},{9,13},{10,... | collective-permute-start | bytes 98312 | tf_op jit(solution)/shard_map/ppermute | solution.py:35
  27.1 7.5 %collective-permute-start.8 = (f32[64,128]{1,0:T(8,128)S(1)}, f32[64,128]{1,0:T(8,128)S(1)}, u32[]{:S(2)}, u32[]{:S(2)}) collective-permute-start(f32[64,128]{1,0:T(8,128)S(1)} %get-tuple-element.25.other_ref), channel_id=1, source_target_pairs={{0,6},{1,7},{2,4},{3,5},{4,2},{5,3},{6,0},{7,1},{8,14},{9,15},{10,... | collective-permute-start | bytes 98312 | tf_op jit(solution)/shard_map/ppermute | solution.py:35
  29.6 5.0 %collective-permute-start.14 = (f32[64,128]{1,0:T(8,128)S(1)}, f32[64,128]{1,0:T(8,128)S(1)}, u32[]{:S(2)}, u32[]{:S(2)}) collective-permute-start(f32[64,128]{1,0:T(8,128)S(1)} %get-tuple-element.28.sent_ref), channel_id=1, source_target_pairs={{0,16},{8,24},{16,0},{24,8},{1,17},{9,25},{17,1},{25,9},{2,18},{10... | collective-permute-start | bytes 98312 | tf_op jit(solution)/shard_map/ppermute | solution.py:35
  34.6 3.9 %copy-start = (bf16[3,4608,128]{2,1,0:T(8,128)(2,1)S(1)}, bf16[3,4608,128]{2,1,0:T(8,128)(2,1)}, u32[]{:S(2)}) copy-start(bf16[3,4608,128]{2,1,0:T(8,128)(2,1)} %refs_9_.1) | copy-start | bytes 10616836
  34.6 3.9 %collective-permute-start.9 = (f32[4,64,128]{2,1,0:T(8,128)S(1)}, f32[4,64,128]{2,1,0:T(8,128)S(1)}, u32[]{:S(2)}, u32[]{:S(2)}) collective-permute-start(f32[4,64,128]{2,1,0:T(8,128)S(1)} %stack.1.own_ref), channel_id=1, source_target_pairs={{0,1},{1,0},{2,3},{3,2},{4,5},{5,4},{6,7},{7,6},{8,9},{9,8},{10,11... | collective-permute-start | bytes 393224 | tf_op jit(solution)/shard_map/ppermute | solution.py:35
  34.9 5.9 %collective-permute-start.20 = (f32[64,256]{1,0:T(8,128)S(1)}, f32[64,256]{1,0:T(8,128)S(1)}, u32[]{:S(2)}, u32[]{:S(2)}) collective-permute-start(f32[64,256]{1,0:T(8,128)S(1)} %pack.1.ref), channel_id=1, source_target_pairs={{0,6},{1,7},{2,4},{3,5},{4,2},{5,3},{6,0},{7,1},{8,14},{9,15},{10,... | collective-permute-start | bytes 196616 | tf_op jit(solution)/shard_map/ppermute | solution.py:35
  35.7 5.0 %collective-permute-start.16 = (f32[64,256]{1,0:T(8,128)S(1)}, f32[64,256]{1,0:T(8,128)S(1)}, u32[]{:S(2)}, u32[]{:S(2)}) collective-permute-start(f32[64,256]{1,0:T(8,128)S(1)} %pack.1.ref), channel_id=1, source_target_pairs={{0,2},{1,3},{2,0},{3,1},{4,6},{5,7},{6,4},{7,5},{8,10},{9,11},{10,... | collective-permute-start | bytes 196616 | tf_op jit(solution)/shard_map/ppermute | solution.py:35
  36.7 5.0 %collective-permute-start.18 = (f32[64,256]{1,0:T(8,128)S(1)}, f32[64,256]{1,0:T(8,128)S(1)}, u32[]{:S(2)}, u32[]{:S(2)}) collective-permute-start(f32[64,256]{1,0:T(8,128)S(1)} %pack.1.ref), channel_id=1, source_target_pairs={{0,4},{1,5},{2,6},{3,7},{4,0},{5,1},{6,2},{7,3},{8,12},{9,13},{10,... | collective-permute-start | bytes 196616 | tf_op jit(solution)/shard_map/ppermute | solution.py:35
  40.0 1.7 %collective-permute-start.15 = (f32[64,256]{1,0:T(8,128)S(1)}, f32[64,256]{1,0:T(8,128)S(1)}, u32[]{:S(2)}, u32[]{:S(2)}) collective-permute-start(f32[64,256]{1,0:T(8,128)S(1)} %relay.4.refs_0_), channel_id=1, source_target_pairs={{0,1},{1,0},{2,3},{3,2},{4,5},{5,4},{6,7},{7,6},{8,9},{9,8},{10,11... | collective-permute-start | bytes 196616 | tf_op jit(solution)/shard_map/ppermute | solution.py:35
  40.7 1.3 %collective-permute-start.21 = (f32[64,256]{1,0:T(8,128)S(1)}, f32[64,256]{1,0:T(8,128)S(1)}, u32[]{:S(2)}, u32[]{:S(2)}) collective-permute-start(f32[64,256]{1,0:T(8,128)S(1)} %relay.5.refs_6_), channel_id=1, source_target_pairs={{0,1},{1,0},{2,3},{3,2},{4,5},{5,4},{6,7},{7,6},{8,9},{9,8},{10,11... | collective-permute-start | bytes 196616 | tf_op jit(solution)/shard_map/ppermute | solution.py:35
  40.7 1.4 %collective-permute-start.17 = (f32[64,256]{1,0:T(8,128)S(1)}, f32[64,256]{1,0:T(8,128)S(1)}, u32[]{:S(2)}, u32[]{:S(2)}) collective-permute-start(f32[64,256]{1,0:T(8,128)S(1)} %collective-permute-done.16.refs_2_), channel_id=1, source_target_pairs={{0,1},{1,0},{2,3},{3,2},{4,5},{5,4},{6,7},{7,6},{8,9},{9,8},{10,11... | collective-permute-start | bytes 196616 | tf_op jit(solution)/shard_map/ppermute | solution.py:35
  41.7 1.3 %collective-permute-start.19 = (f32[64,256]{1,0:T(8,128)S(1)}, f32[64,256]{1,0:T(8,128)S(1)}, u32[]{:S(2)}, u32[]{:S(2)}) collective-permute-start(f32[64,256]{1,0:T(8,128)S(1)} %collective-permute-done.18.refs_4_), channel_id=1, source_target_pairs={{0,1},{1,0},{2,3},{3,2},{4,5},{5,4},{6,7},{7,6},{8,9},{9,8},{10,11... | collective-permute-start | bytes 196616 | tf_op jit(solution)/shard_map/ppermute | solution.py:35

commit v18 on v16

--- a/solution.py
+++ b/solution.py
@@ -268,17 +268,56 @@
         out_ref[rows, :] = first_ref[rows, :] - dot(left, factor_ref[...], (1, 0))
 
 
-def expand_kernel(levels, tile, count, *refs):
-    piece_refs = refs[:count]
-    first_ref, left_ref, out_ref, flip_ref, factor_ref, out_buf, sems = refs[count:]
-    split_factor(piece_refs, flip_ref, factor_ref)
+def half_factor(piece_refs, flip_ref):
+    share = piece_refs[0].shape[0]
+    chip = lax.axis_index("rows") // 2
+    for slot, ref in enumerate(piece_refs):
+        flip_ref[pl.ds(pl.multiple_of((chip ^ slot) * share, share), share), :] = ref[...]
+    return jnp.concatenate(halves(flip_ref[...].T), axis=0)
+
+
+def side_lanes(part, other):
+    core = lax.axis_index("rows") % 2
+    return pl.ds(pl.multiple_of((1 - core if other else core) * part, part), part)
+
+
+def left_rows(left_ref, rows):
+    return jnp.concatenate([left_ref[l, rows, :] for l in range(1, left_ref.shape[0])] * 2, axis=1)
+
+
+def expand_own_kernel(head, width, slots, *refs):
+    first_ref, left_ref, out_ref, factor_ref, flip_ref, out_buf, sems = refs[slots:]
+    lanes = side_lanes(out_buf.shape[1], False)
+    factor_ref[...] = half_factor(refs[:slots], flip_ref)
     copies = []
-    for step in range(out_buf.shape[0] // tile):
-        rows = pl.ds(step * tile, tile)
-        left = jnp.concatenate([left_ref[l, rows, :] for l in range(1, levels)] * 2, axis=1)
-        out_buf[rows, :] = first_ref[rows, :] - dot(left, factor_ref[...], (1, 0))
-        copies.append(pltpu.make_async_copy(out_buf.at[rows], out_ref.at[rows], sems.at[step]))
-        copies[-1].start(priority=step % 2)
+    for block in range(head):
+        rows = pl.ds(block * width, width)
+        out_buf[rows, :] = first_ref[rows, lanes] - dot(left_rows(left_ref, rows), factor_ref[...], (1, 0))
+        copies.append(pltpu.make_async_copy(out_buf.at[rows], out_ref.at[rows, lanes], sems.at[block]))
+        copies[-1].start(priority=block % 2)
+    for copy in copies:
+        copy.wait()
+
+
+def expand_rest_kernel(head, width, slots, *refs):
+    own_ref, first_ref, left_ref, _, out_ref, flip_ref, factor_ref, head_buf, out_buf, sems = refs[slots:]
+    part = own_ref.shape[1]
+    lanes = side_lanes(part, True)
+    other = half_factor(refs[:slots], flip_ref)
+    factor_ref[:, side_lanes(part, False)] = own_ref[...]
+    factor_ref[:, lanes] = other
+    copies = []
+    for block in range(sems.shape[0]):
+        rows = pl.ds(block * width, width)
+        left = left_rows(left_ref, rows)
+        if block < head:
+            head_buf[rows, :] = first_ref[rows, lanes] - dot(left, other, (1, 0))
+            copies.append(pltpu.make_async_copy(head_buf.at[rows], out_ref.at[rows, lanes], sems.at[block]))
+        else:
+            place = pl.ds((block - head) * width, width)
+            out_buf[place, :] = first_ref[rows, :] - dot(left, factor_ref[...], (1, 0))
+            copies.append(pltpu.make_async_copy(out_buf.at[place], out_ref.at[rows], sems.at[block]))
+        copies[-1].start(priority=block % 2)
     for copy in copies:
         copy.wait()
 
@@ -429,27 +468,47 @@
     pack = pl.pallas_call(
         pack_kernel, out_shape=floats(share, size), name="pack", **settings(8, 0.1),
     )(*coefs)
-    pieces = []
+    direct, swapped = [], []
     for slot in range(slots):
         piece = swap(pack, "rows", 2 * slot) if slot > 0 else pack
         if slot in (0, slots - 1):
             piece = pl.pallas_call(
                 relay_kernel, out_shape=floats(share, size), name="relay", **settings(8, 0.1),
             )(second, piece)
-        pieces += [piece, swap(piece, "rows", 1)]
+        direct.append(piece)
+        swapped.append(swap(piece, "rows", 1))
+
+    head = nblocks // 3
+    half = columns // 2
+    anywhere = pl.BlockSpec(memory_space=pl.ANY)
+    out, factor = pl.pallas_call(
+        functools.partial(expand_own_kernel, head, width, slots),
+        out_specs=[anywhere, pl.BlockSpec()],
+        out_shape=[floats(rows, columns), jax.ShapeDtypeStruct((2 * size, half), jnp.bfloat16)],
+        scratch_shapes=[
+            pltpu.VMEM((half, size), jnp.float32),
+            pltpu.VMEM((head * width, half), jnp.float32),
+            pltpu.SemaphoreType.DMA((head,)),
+        ],
+        name="expand_own",
+        **settings(8, 1.2),
+    )(*direct, second, left_basis)
     return pl.pallas_call(
-        functools.partial(expand_kernel, levels, width, count),
-        out_specs=pl.BlockSpec(memory_space=pl.ANY),
+        functools.partial(expand_rest_kernel, head, width, slots),
+        in_specs=[pl.BlockSpec()] * (slots + 3) + [anywhere],
+        out_specs=anywhere,
         out_shape=floats(rows, columns),
         scratch_shapes=[
-            pltpu.VMEM((columns, size), jnp.float32),
+            pltpu.VMEM((half, size), jnp.float32),
             pltpu.VMEM((2 * size, columns), jnp.bfloat16),
-            pltpu.VMEM((rows, columns), jnp.float32),
+            pltpu.VMEM((head * width, half), jnp.float32),
+            pltpu.VMEM((rows - head * width, columns), jnp.float32),
             pltpu.SemaphoreType.DMA((nblocks,)),
         ],
-        name="expand",
-        **settings(16, 5),
-    )(*pieces, second, left_basis)
+        input_output_aliases={slots + 3: 0},
+        name="expand_rest",
+        **settings(16, 4),
+    )(*swapped, factor, second, left_basis, out)
 
 
 def solution(mesh):

time: 47 us -> 47.3 us (level)
  waiting for transfers between devices: 4.74 us -> 3.36 us
  Pallas kernels: 21.1 us -> 22.1 us
  starting transfers between devices: 20.7 us -> 21.3 us
    ppermute x22, waiting for transfers between devices: 4.74 us -> 3.36 us  [swap(): return lax.ppermute(value, axis, [(i, i ^ mask) for i in range(count)])]
    pallas_call x1 -> x2, Pallas kernels: 4.28 us -> 5.35 us  [the longest x1 3.73 us: per_device(): pl.pallas_call(functools.partial(expand_rest_kernel, head, width, slots),...]
    ppermute x22, starting transfers between devices: 20.7 us -> 21.3 us  [swap(): return lax.ppermute(value, axis, [(i, i ^ mask) for i in range(count)])]
  transfers between devices with their start and end apart: 22 -> 22, of which waited for: 7 -> 3; matrix products, arithmetic and copies ran while one was open for 0% -> 0% of each run, Pallas kernels for 28% -> 31%
where the time goes in v18:
time: 47.3 us; the launch traced here: 47.2 us
  Pallas kernels  22.1 us (47%)
  starting transfers between devices  21.3 us (45%)
  waiting for transfers between devices  3.36 us (7%)
    ppermute x22, starting transfers between devices, swap(): return lax.ppermute(value, axis, [(i, i ^ mask) for i in range(count)])  21.3 us
    pallas_call x2, Pallas kernels, project(): pl.pallas_call(functools.partial(project_kernel, other), out_shape=floats...  3.99 us
    pallas_call x1, Pallas kernels, per_device(): pl.pallas_call(functools.partial(expand_rest_kernel, head, width, slots),...  3.73 us
    ppermute x22, waiting for transfers between devices, swap(): return lax.ppermute(value, axis, [(i, i ^ mask) for i in range(count)])  3.36 us
    pallas_call x1, Pallas kernels, per_device(): pl.pallas_call(functools.partial(gram_kernel, levels, per_step, width), i...  3.34 us
    pallas_call x1, Pallas kernels, per_device(): pl.pallas_call(functools.partial(solve_kernel, per_step, width), out_shap...  2.22 us
    pallas_call x1, Pallas kernels, per_device(): pl.pallas_call(functools.partial(prepare_kernel, levels), in_specs=[pl.Bl...  1.68 us
    pallas_call x1, Pallas kernels, per_device(): pl.pallas_call(functools.partial(expand_own_kernel, head, width, slots),...  1.62 us
  transfers between devices with their start and end apart: 22, of which 3 were waited for; matrix products, arithmetic and copies ran while one was open for 0% of the time, Pallas kernels for 31%

profile of v18, /device:TPU:0, one launch (start us, length us, event | category | flops | bytes accessed | tf_op | source)
XLA Modules:
  0.0 47.2 jit_solution(9427501516749942471)
XLA Ops:
  0.0 3.3 %gram.1 = (bf16[384,4608]{1,0:T(8,128)(2,1)S(1)}, f32[64,384]{1,0:T(8,128)S(1)}, f32[64,384]{1,0:T(8,128)S(1)}) custom-call(bf16[3,4608,128]{2,1,0:T(8,128)(2,1)} %right_ref.1, bf16[3,4608,128]{2,1,0:T(8,128)(2,1)} %refs_6_.1), custom_call_target="tpu_custom_call" | custom-call | flops 3300000000 | tf_op jit(solution)/shard_map/gram/pallas_call | solution.py:349
  3.4 0.5 %collective-permute-start = (f32[64,384]{1,0:T(8,128)S(1)}, f32[64,384]{1,0:T(8,128)S(1)}, u32[]{:S(2)}, u32[]{:S(2)}) collective-permute-start(f32[64,384]{1,0:T(8,128)S(1)} %get-tuple-element.21), channel_id=1, source_target_pairs={{0,1},{1,0},{2,3},{3,2},{4,5},{5,4},{6,7},{7,6},{8,9},{9,8},{10,11... | collective-permute-start | bytes 294920 | tf_op jit(solution)/shard_map/ppermute | solution.py:35
  3.9 0.0 copy-done.1
  3.9 0.0 copy-done.2
  3.9 1.0 %permute.1.moved_ref = bf16[18,256,256]{2,1,0:T(8,128)(2,1)S(1)} custom-call(s32[18,256]{1,0:T(8,128)S(1)} %copy-done.2, bf16[18,256,256]{2,1,0:T(8,128)(2,1)S(1)} %copy-done.1), custom_call_target="tpu_custom_call" | custom-call | flops 1650000000 | tf_op jit(solution)/shard_map/permute/pallas_call | solution.py:365
  4.9 0.0 collective-permute-done.got_ref
  4.9 0.0 slice-start
  5.0 2.8 %collective-permute-start.1 = (f32[64,384]{1,0:T(8,128)S(1)}, f32[64,384]{1,0:T(8,128)S(1)}, u32[]{:S(2)}, u32[]{:S(2)}) collective-permute-start(f32[64,384]{1,0:T(8,128)S(1)} %add.2.after_ref.mine_ref), channel_id=1, source_target_pairs={{0,2},{1,3},{2,0},{3,1},{4,6},{5,7},{6,4},{7,5},{8,10},{9,11},{10,... | collective-permute-start | bytes 294920 | tf_op jit(solution)/shard_map/ppermute | solution.py:35
  7.7 1.6 %weigh.1.factor_ref = bf16[768,4608]{1,0:T(8,128)(2,1)S(1)} custom-call(bf16[18,256,256]{2,1,0:T(8,128)(2,1)S(1)} %permute.1.moved_ref, bf16[384,4608]{1,0:T(8,128)(2,1)S(1)} %get-tuple-element.19.flip_ref, f32[64,384]{1,0:T(8,128)S(1)} %add.2.after_ref.mine_ref), custom_call_target="tpu_custom_call" | custom-call | flops 2640000000 | tf_op jit(solution)/shard_map/weigh/pallas_call | solution.py:378
  9.4 2.0 %project_other.1 = f32[384,256]{1,0:T(8,128)S(1)} custom-call(bf16[768,4608]{1,0:T(8,128)(2,1)S(1)} %weigh.1.factor_ref, bf16[4608,512]{1,0:T(8,128)(2,1)S(1)} %bitcast.1, f32[64,384]{1,0:T(8,128)S(1)} %add.2.after_ref.mine_ref), custom_call_target="tpu_custom_call" | custom-call | flops 1100000000 | tf_op jit(solution)/shard_map/project_other/pallas_call | solution.py:386
  11.4 0.1 collective-permute-start.2
  11.5 0.0 collective-permute-done.1.got_ref
  11.5 0.0 copy-start.3
  11.5 1.6 %collective-permute-start.10 = (f32[64,384]{1,0:T(8,128)S(1)}, f32[64,384]{1,0:T(8,128)S(1)}, u32[]{:S(2)}, u32[]{:S(2)}) collective-permute-start(f32[64,384]{1,0:T(8,128)S(1)} %add.3.after_ref.mine_ref), channel_id=1, source_target_pairs={{0,4},{1,5},{2,6},{3,7},{4,0},{5,1},{6,2},{7,3},{8,12},{9,13},{10,... | collective-permute-start | bytes 294920 | tf_op jit(solution)/shard_map/ppermute | solution.py:35
  13.1 2.0 %project_own.1.keep_ref = f32[384,256]{1,0:T(8,128)S(1)} custom-call(bf16[768,4608]{1,0:T(8,128)(2,1)S(1)} %weigh.1.factor_ref, bf16[4608,512]{1,0:T(8,128)(2,1)S(1)} %bitcast.1, f32[64,384]{1,0:T(8,128)S(1)} %add.3.after_ref.mine_ref), custom_call_target="tpu_custom_call" | custom-call | flops 4400000000 | tf_op jit(solution)/shard_map/project_own/pallas_call | solution.py:386
  15.1 0.0 collective-permute-done.2.got_ref
  15.1 0.2 merge.1
  15.3 1.3 %collective-permute-start.3 = (f32[64,384]{1,0:T(8,128)S(1)}, f32[64,384]{1,0:T(8,128)S(1)}, u32[]{:S(2)}, u32[]{:S(2)}) collective-permute-start(f32[64,384]{1,0:T(8,128)S(1)} %get-tuple-element.23), channel_id=1, source_target_pairs={{0,2},{1,3},{2,0},{3,1},{4,6},{5,7},{6,4},{7,5},{8,10},{9,11},{10,... | collective-permute-start | bytes 294920 | tf_op jit(solution)/shard_map/ppermute | solution.py:35
  16.6 0.5 %collective-permute-start.4 = (f32[64,384]{1,0:T(8,128)S(1)}, f32[64,384]{1,0:T(8,128)S(1)}, u32[]{:S(2)}, u32[]{:S(2)}) collective-permute-start(f32[64,384]{1,0:T(8,128)S(1)} %get-tuple-element.24), channel_id=1, source_target_pairs={{0,4},{1,5},{2,6},{3,7},{4,0},{5,1},{6,2},{7,3},{8,12},{9,13},{10,... | collective-permute-start | bytes 294920 | tf_op jit(solution)/shard_map/ppermute | solution.py:35
  17.1 1.8 %collective-permute-start.5 = (f32[64,384]{1,0:T(8,128)S(1)}, f32[64,384]{1,0:T(8,128)S(1)}, u32[]{:S(2)}, u32[]{:S(2)}) collective-permute-start(f32[64,384]{1,0:T(8,128)S(1)} %get-tuple-element.25), channel_id=1, source_target_pairs={{0,6},{1,7},{2,4},{3,5},{4,2},{5,3},{6,0},{7,1},{8,14},{9,15},{10,... | collective-permute-start | bytes 294920 | tf_op jit(solution)/shard_map/ppermute | solution.py:35
  18.9 1.7 %prepare.1.refs_4_.joined_ref = bf16[3,768,256]{2,1,0:T(8,128)(2,1)S(1)} custom-call(f32[7,256,256]{2,1,0:T(8,128)} %joined_ref.1, s32[3,128]{1,0:T(4,128)S(1)} %copy-done.3), custom_call_target="tpu_custom_call" | custom-call | flops 2200000000 | tf_op jit(solution)/shard_map/prepare/pallas_call | solution.py:410
  20.6 0.1 collective-permute-start.11
  20.6 0.0 collective-permute-done.10.theirs_ref
  20.6 0.5 %collective-permute-start.12 = (f32[64,384]{1,0:T(8,128)S(1)}, f32[64,384]{1,0:T(8,128)S(1)}, u32[]{:S(2)}, u32[]{:S(2)}) collective-permute-start(f32[64,384]{1,0:T(8,128)S(1)} %collective-permute-done.10.theirs_ref), channel_id=1, source_target_pairs={{0,1},{1,0},{2,3},{3,2},{4,5},{5,4},{6,7},{7,6},{8,9},{9,8},{10,11... | collective-permute-start | bytes 294920 | tf_op jit(solution)/shard_map/ppermute | solution.py:35
  21.1 0.0 collective-permute-done.3.refs_1_
  21.1 1.9 %collective-permute-done.4.refs_2_ = f32[64,384]{1,0:T(8,128)S(1)} collective-permute-done((f32[64,384]{1,0:T(8,128)S(1)}, f32[64,384]{1,0:T(8,128)S(1)}, u32[]{:S(2)}, u32[]{:S(2)}) %collective-permute-start.4) | collective-permute-done | bytes 98336 | tf_op jit(solution)/shard_map/ppermute | solution.py:35
  23.0 0.0 collective-permute-done.5.refs_3_
  23.0 0.2 node.1
  23.2 0.0 collective-permute-done.11.pair_mine_ref
  23.2 0.0 collective-permute-done.12.pair_theirs_ref
  23.3 0.3 correct.1.sent_ref
  23.6 1.7 %collective-permute-start.13 = (f32[256,128]{1,0:T(8,128)S(1)}, f32[256,128]{1,0:T(8,128)S(1)}, u32[]{:S(2)}, u32[]{:S(2)}) collective-permute-start(f32[256,128]{1,0:T(8,128)S(1)} %correct.1.sent_ref), channel_id=1, source_target_pairs={{0,8},{8,0},{16,24},{24,16},{1,9},{9,1},{17,25},{25,17},{2,10},{10... | collective-permute-start | bytes 393224 | tf_op jit(solution)/shard_map/ppermute | solution.py:35
  25.3 1.0 %collective-permute-start.6 = (f32[64,128]{1,0:T(8,128)S(1)}, f32[64,128]{1,0:T(8,128)S(1)}, u32[]{:S(2)}, u32[]{:S(2)}) collective-permute-start(f32[64,128]{1,0:T(8,128)S(1)} %get-tuple-element.26.refs_0_.own_ref), channel_id=1, source_target_pairs={{0,2},{1,3},{2,0},{3,1},{4,6},{5,7},{6,4},{7,5},{8,10},{9,11},{10,... | collective-permute-start | bytes 98312 | tf_op jit(solution)/shard_map/ppermute | solution.py:35
  26.3 1.5 %collective-permute-start.8 = (f32[64,128]{1,0:T(8,128)S(1)}, f32[64,128]{1,0:T(8,128)S(1)}, u32[]{:S(2)}, u32[]{:S(2)}) collective-permute-start(f32[64,128]{1,0:T(8,128)S(1)} %get-tuple-element.27.other_ref), channel_id=1, source_target_pairs={{0,6},{1,7},{2,4},{3,5},{4,2},{5,3},{6,0},{7,1},{8,14},{9,15},{10,... | collective-permute-start | bytes 98312 | tf_op jit(solution)/shard_map/ppermute | solution.py:35
  27.8 1.0 %collective-permute-start.7 = (f32[64,128]{1,0:T(8,128)S(1)}, f32[64,128]{1,0:T(8,128)S(1)}, u32[]{:S(2)}, u32[]{:S(2)}) collective-permute-start(f32[64,128]{1,0:T(8,128)S(1)} %get-tuple-element.27.other_ref), channel_id=1, source_target_pairs={{0,4},{1,5},{2,6},{3,7},{4,0},{5,1},{6,2},{7,3},{8,12},{9,13},{10,... | collective-permute-start | bytes 98312 | tf_op jit(solution)/shard_map/ppermute | solution.py:35
  28.8 0.0 collective-permute-done.13.got_ref.after_ref
  28.8 0.4 level1.1
  29.2 2.7 %collective-permute-start.14 = (f32[64,128]{1,0:T(8,128)S(1)}, f32[64,128]{1,0:T(8,128)S(1)}, u32[]{:S(2)}, u32[]{:S(2)}) collective-permute-start(f32[64,128]{1,0:T(8,128)S(1)} %get-tuple-element.30.sent_ref), channel_id=1, source_target_pairs={{0,16},{8,24},{16,0},{24,8},{1,17},{9,25},{17,1},{25,9},{2,18},{10... | collective-permute-start | bytes 98312 | tf_op jit(solution)/shard_map/ppermute | solution.py:35
  31.8 2.2 %solve.1.after_ref.first_ref = f32[4608,512]{1,0:T(8,128)S(1)} custom-call(bf16[18,256,256]{2,1,0:T(8,128)(2,1)S(1)} %permute.1.moved_ref, bf16[4608,512]{1,0:T(8,128)(2,1)S(1)} %bitcast.1, f32[64,384]{1,0:T(8,128)S(1)} %get-tuple-element.22.refs_0_), custom_call_target="tpu_custom_call" | custom-call | flops 8800000000 | tf_op jit(solution)/shard_map/solve/pallas_call | solution.py:435
  34.1 0.0 collective-permute-done.6.refs_1_
  34.1 0.0 collective-permute-done.8.refs_3_
  34.1 0.0 collective-permute-done.7.refs_2_
  34.1 0.0 copy-start
  34.1 0.1 collective-permute-start.9
  34.2 0.0 collective-permute-done.14.got_ref
  34.2 0.2 level2.1.refs_1_
  34.4 1.3 %collective-permute-start.20 = (f32[64,256]{1,0:T(8,128)S(1)}, f32[64,256]{1,0:T(8,128)S(1)}, u32[]{:S(2)}, u32[]{:S(2)}) collective-permute-start(f32[64,256]{1,0:T(8,128)S(1)} %pack.1.ref), channel_id=1, source_target_pairs={{0,6},{1,7},{2,4},{3,5},{4,2},{5,3},{6,0},{7,1},{8,14},{9,15},{10,... | collective-permute-start | bytes 196616 | tf_op jit(solution)/shard_map/ppermute | solution.py:35
  35.8 1.2 %collective-permute-start.18 = (f32[64,256]{1,0:T(8,128)S(1)}, f32[64,256]{1,0:T(8,128)S(1)}, u32[]{:S(2)}, u32[]{:S(2)}) collective-permute-start(f32[64,256]{1,0:T(8,128)S(1)} %pack.1.ref), channel_id=1, source_target_pairs={{0,4},{1,5},{2,6},{3,7},{4,0},{5,1},{6,2},{7,3},{8,12},{9,13},{10,... | collective-permute-start | bytes 196616 | tf_op jit(solution)/shard_map/ppermute | solution.py:35
  37.0 1.0 %collective-permute-start.16 = (f32[64,256]{1,0:T(8,128)S(1)}, f32[64,256]{1,0:T(8,128)S(1)}, u32[]{:S(2)}, u32[]{:S(2)}) collective-permute-start(f32[64,256]{1,0:T(8,128)S(1)} %pack.1.ref), channel_id=1, source_target_pairs={{0,2},{1,3},{2,0},{3,1},{4,6},{5,7},{6,4},{7,5},{8,10},{9,11},{10,... | collective-permute-start | bytes 196616 | tf_op jit(solution)/shard_map/ppermute | solution.py:35
  38.0 0.0 collective-permute-done.9.pair_ref
  38.0 1.6 %apply.1.after_ref.refs_4_.refs_5_ = f32[4608,512]{1,0:T(8,128)S(1)} custom-call(f32[4,64,128]{2,1,0:T(8,128)S(1)} %stack.1.own_ref, f32[4,64,128]{2,1,0:T(8,128)S(1)} %collective-permute-done.9.pair_ref, f32[4608,512]{1,0:T(8,128)S(1)} %solve.1.after_ref.first_ref, bf16[3,4608,128]{2,1,0:T(8,128)(2,1)S(1)} %copy-done), custom_call_target="tpu_custom_call" | custom-call | flops 1980000000 | tf_op jit(solution)/shard_map/apply/pallas_call | solution.py:457
  39.6 0.1 collective-permute-start.15
  39.7 0.4 collective-permute-done.20.ref
  40.0 0.2 collective-permute-start.21
  40.2 1.0 %collective-permute-done.18.refs_2_ = f32[64,256]{1,0:T(8,128)S(1)} collective-permute-done((f32[64,256]{1,0:T(8,128)S(1)}, f32[64,256]{1,0:T(8,128)S(1)}, u32[]{:S(2)}, u32[]{:S(2)}) %collective-permute-start.18) | collective-permute-done | bytes 65568 | tf_op jit(solution)/shard_map/ppermute | solution.py:35
  41.3 0.0 collective-permute-start.19
  41.3 0.0 collective-permute-done.16.refs_1_
  41.3 0.5 collective-permute-start.17
  41.8 1.6 %expand_own.1 = (f32[4608,512]{1,0:T(8,128)}, bf16[512,256]{1,0:T(8,128)(2,1)S(1)}) custom-call(f32[64,256]{1,0:T(8,128)S(1)} %relay.2.refs_0_, f32[64,256]{1,0:T(8,128)S(1)} %collective-permute-done.16.refs_1_, f32[64,256]{1,0:T(8,128)S(1)} %collective-permute-done.18.refs_2_, f32[64,256]{1,0:T(8,128)S(1)} %relay.3.refs_3_, ...), custom_call_target="tpu_custom_call" | custom-call | flops 1320000000 | tf_op jit(solution)/shard_map/expand_own/pallas_call | solution.py:484
  43.4 0.0 collective-permute-done.15.refs_0_
  43.4 0.0 collective-permute-done.19.refs_2_
  43.5 0.0 collective-permute-done.17.refs_1_
  43.5 0.0 collective-permute-done.21.refs_3_
  43.5 3.7 %expand_rest.1 = f32[4608,512]{1,0:T(8,128)} custom-call(f32[64,256]{1,0:T(8,128)S(1)} %collective-permute-done.15.refs_0_, f32[64,256]{1,0:T(8,128)S(1)} %collective-permute-done.17.refs_1_, f32[64,256]{1,0:T(8,128)S(1)} %collective-permute-done.19.refs_2_, f32[64,256]{1,0:T(8,128)S(1)} %collective-permute-done.21.refs_3_, ...), custom_call_target="tpu_custom_call", output_to_operand_aliasing={{}: (7, {})} | custom-call | flops 4400000000 | tf_op jit(solution)/shard_map/expand_rest/pallas_call | solution.py:496
  (14 shorter events, 0.1 us)
Async XLA Ops:
  0.0 3.9 %copy-start.1 = (bf16[18,256,256]{2,1,0:T(8,128)(2,1)S(1)}, bf16[18,256,256]{2,1,0:T(8,128)(2,1)}, u32[]{:S(2)}) copy-start(bf16[18,256,256]{2,1,0:T(8,128)(2,1)} %inv_ref.1) | copy-start | bytes 7077892
  0.0 3.9 %copy-start.2 = (s32[18,256]{1,0:T(8,128)S(1)}, s32[18,256]{1,0:T(8,128)}, u32[]{:S(2)}) copy-start(s32[18,256]{1,0:T(8,128)} %order_ref.1) | copy-start | bytes 55300
  3.4 1.6 %collective-permute-start = (f32[64,384]{1,0:T(8,128)S(1)}, f32[64,384]{1,0:T(8,128)S(1)}, u32[]{:S(2)}, u32[]{:S(2)}) collective-permute-start(f32[64,384]{1,0:T(8,128)S(1)} %get-tuple-element.21), channel_id=1, source_target_pairs={{0,1},{1,0},{2,3},{3,2},{4,5},{5,4},{6,7},{7,6},{8,9},{9,8},{10,11... | collective-permute-start | bytes 294920 | tf_op jit(solution)/shard_map/ppermute | solution.py:35
  4.9 4.4 %slice-start = ((s8[4718592]{0:T(1024)(128)(4,1)}), s8[4194304]{0:T(1024)(128)(4,1)S(1)}, s32[]{:S(2)}) async-start(s8[4718592]{0:T(1024)(128)(4,1)} %bitcast), calls=%async_computation | async-start | bytes 8388608
  5.0 6.5 %collective-permute-start.1 = (f32[64,384]{1,0:T(8,128)S(1)}, f32[64,384]{1,0:T(8,128)S(1)}, u32[]{:S(2)}, u32[]{:S(2)}) collective-permute-start(f32[64,384]{1,0:T(8,128)S(1)} %add.2.after_ref.mine_ref), channel_id=1, source_target_pairs={{0,2},{1,3},{2,0},{3,1},{4,6},{5,7},{6,4},{7,5},{8,10},{9,11},{10,... | collective-permute-start | bytes 294920 | tf_op jit(solution)/shard_map/ppermute | solution.py:35
  7.7 1.6 %slice-start.1 = ((s8[4718592]{0:T(1024)(128)(4,1)}), s8[524288]{0:T(1024)(128)(4,1)S(1)}, s32[]{:S(2)}) async-start(s8[4718592]{0:T(1024)(128)(4,1)} %bitcast), calls=%async_computation.1 | async-start | bytes 1048576
  11.4 3.7 %collective-permute-start.2 = (f32[384,256]{1,0:T(8,128)S(1)}, f32[384,256]{1,0:T(8,128)S(1)}, u32[]{:S(2)}, u32[]{:S(2)}) collective-permute-start(f32[384,256]{1,0:T(8,128)S(1)} %project_other.1), channel_id=1, source_target_pairs={{0,1},{1,0},{2,3},{3,2},{4,5},{5,4},{6,7},{7,6},{8,9},{9,8},{10,11... | collective-permute-start | bytes 1179656 | tf_op jit(solution)/shard_map/ppermute | solution.py:35
  11.5 7.4 %copy-start.3 = (s32[3,128]{1,0:T(4,128)S(1)}, s32[3,128]{1,0:T(4,128)}, u32[]{:S(2)}) copy-start(s32[3,128]{1,0:T(4,128)} %perm_ref.1) | copy-start | bytes 4612
  11.5 9.1 %collective-permute-start.10 = (f32[64,384]{1,0:T(8,128)S(1)}, f32[64,384]{1,0:T(8,128)S(1)}, u32[]{:S(2)}, u32[]{:S(2)}) collective-permute-start(f32[64,384]{1,0:T(8,128)S(1)} %add.3.after_ref.mine_ref), channel_id=1, source_target_pairs={{0,4},{1,5},{2,6},{3,7},{4,0},{5,1},{6,2},{7,3},{8,12},{9,13},{10,... | collective-permute-start | bytes 294920 | tf_op jit(solution)/shard_map/ppermute | solution.py:35
  15.3 5.8 %collective-permute-start.3 = (f32[64,384]{1,0:T(8,128)S(1)}, f32[64,384]{1,0:T(8,128)S(1)}, u32[]{:S(2)}, u32[]{:S(2)}) collective-permute-start(f32[64,384]{1,0:T(8,128)S(1)} %get-tuple-element.23), channel_id=1, source_target_pairs={{0,2},{1,3},{2,0},{3,1},{4,6},{5,7},{6,4},{7,5},{8,10},{9,11},{10,... | collective-permute-start | bytes 294920 | tf_op jit(solution)/shard_map/ppermute | solution.py:35
  16.6 6.4 %collective-permute-start.4 = (f32[64,384]{1,0:T(8,128)S(1)}, f32[64,384]{1,0:T(8,128)S(1)}, u32[]{:S(2)}, u32[]{:S(2)}) collective-permute-start(f32[64,384]{1,0:T(8,128)S(1)} %get-tuple-element.24), channel_id=1, source_target_pairs={{0,4},{1,5},{2,6},{3,7},{4,0},{5,1},{6,2},{7,3},{8,12},{9,13},{10,... | collective-permute-start | bytes 294920 | tf_op jit(solution)/shard_map/ppermute | solution.py:35
  17.1 5.9 %collective-permute-start.5 = (f32[64,384]{1,0:T(8,128)S(1)}, f32[64,384]{1,0:T(8,128)S(1)}, u32[]{:S(2)}, u32[]{:S(2)}) collective-permute-start(f32[64,384]{1,0:T(8,128)S(1)} %get-tuple-element.25), channel_id=1, source_target_pairs={{0,6},{1,7},{2,4},{3,5},{4,2},{5,3},{6,0},{7,1},{8,14},{9,15},{10,... | collective-permute-start | bytes 294920 | tf_op jit(solution)/shard_map/ppermute | solution.py:35
  20.6 2.7 %collective-permute-start.11 = (f32[64,384]{1,0:T(8,128)S(1)}, f32[64,384]{1,0:T(8,128)S(1)}, u32[]{:S(2)}, u32[]{:S(2)}) collective-permute-start(f32[64,384]{1,0:T(8,128)S(1)} %add.3.after_ref.mine_ref), channel_id=1, source_target_pairs={{0,1},{1,0},{2,3},{3,2},{4,5},{5,4},{6,7},{7,6},{8,9},{9,8},{10,11... | collective-permute-start | bytes 294920 | tf_op jit(solution)/shard_map/ppermute | solution.py:35
  20.6 2.6 %collective-permute-start.12 = (f32[64,384]{1,0:T(8,128)S(1)}, f32[64,384]{1,0:T(8,128)S(1)}, u32[]{:S(2)}, u32[]{:S(2)}) collective-permute-start(f32[64,384]{1,0:T(8,128)S(1)} %collective-permute-done.10.theirs_ref), channel_id=1, source_target_pairs={{0,1},{1,0},{2,3},{3,2},{4,5},{5,4},{6,7},{7,6},{8,9},{9,8},{10,11... | collective-permute-start | bytes 294920 | tf_op jit(solution)/shard_map/ppermute | solution.py:35
  23.6 5.2 %collective-permute-start.13 = (f32[256,128]{1,0:T(8,128)S(1)}, f32[256,128]{1,0:T(8,128)S(1)}, u32[]{:S(2)}, u32[]{:S(2)}) collective-permute-start(f32[256,128]{1,0:T(8,128)S(1)} %correct.1.sent_ref), channel_id=1, source_target_pairs={{0,8},{8,0},{16,24},{24,16},{1,9},{9,1},{17,25},{25,17},{2,10},{10... | collective-permute-start | bytes 393224 | tf_op jit(solution)/shard_map/ppermute | solution.py:35
  25.3 8.8 %collective-permute-start.6 = (f32[64,128]{1,0:T(8,128)S(1)}, f32[64,128]{1,0:T(8,128)S(1)}, u32[]{:S(2)}, u32[]{:S(2)}) collective-permute-start(f32[64,128]{1,0:T(8,128)S(1)} %get-tuple-element.26.refs_0_.own_ref), channel_id=1, source_target_pairs={{0,2},{1,3},{2,0},{3,1},{4,6},{5,7},{6,4},{7,5},{8,10},{9,11},{10,... | collective-permute-start | bytes 98312 | tf_op jit(solution)/shard_map/ppermute | solution.py:35
  26.3 7.8 %collective-permute-start.8 = (f32[64,128]{1,0:T(8,128)S(1)}, f32[64,128]{1,0:T(8,128)S(1)}, u32[]{:S(2)}, u32[]{:S(2)}) collective-permute-start(f32[64,128]{1,0:T(8,128)S(1)} %get-tuple-element.27.other_ref), channel_id=1, source_target_pairs={{0,6},{1,7},{2,4},{3,5},{4,2},{5,3},{6,0},{7,1},{8,14},{9,15},{10,... | collective-permute-start | bytes 98312 | tf_op jit(solution)/shard_map/ppermute | solution.py:35
  27.8 6.3 %collective-permute-start.7 = (f32[64,128]{1,0:T(8,128)S(1)}, f32[64,128]{1,0:T(8,128)S(1)}, u32[]{:S(2)}, u32[]{:S(2)}) collective-permute-start(f32[64,128]{1,0:T(8,128)S(1)} %get-tuple-element.27.other_ref), channel_id=1, source_target_pairs={{0,4},{1,5},{2,6},{3,7},{4,0},{5,1},{6,2},{7,3},{8,12},{9,13},{10,... | collective-permute-start | bytes 98312 | tf_op jit(solution)/shard_map/ppermute | solution.py:35
  29.2 5.0 %collective-permute-start.14 = (f32[64,128]{1,0:T(8,128)S(1)}, f32[64,128]{1,0:T(8,128)S(1)}, u32[]{:S(2)}, u32[]{:S(2)}) collective-permute-start(f32[64,128]{1,0:T(8,128)S(1)} %get-tuple-element.30.sent_ref), channel_id=1, source_target_pairs={{0,16},{8,24},{16,0},{24,8},{1,17},{9,25},{17,1},{25,9},{2,18},{10... | collective-permute-start | bytes 98312 | tf_op jit(solution)/shard_map/ppermute | solution.py:35
  34.1 3.9 %copy-start = (bf16[3,4608,128]{2,1,0:T(8,128)(2,1)S(1)}, bf16[3,4608,128]{2,1,0:T(8,128)(2,1)}, u32[]{:S(2)}) copy-start(bf16[3,4608,128]{2,1,0:T(8,128)(2,1)} %refs_6_.1) | copy-start | bytes 10616836
  34.1 3.9 %collective-permute-start.9 = (f32[4,64,128]{2,1,0:T(8,128)S(1)}, f32[4,64,128]{2,1,0:T(8,128)S(1)}, u32[]{:S(2)}, u32[]{:S(2)}) collective-permute-start(f32[4,64,128]{2,1,0:T(8,128)S(1)} %stack.1.own_ref), channel_id=1, source_target_pairs={{0,1},{1,0},{2,3},{3,2},{4,5},{5,4},{6,7},{7,6},{8,9},{9,8},{10,11... | collective-permute-start | bytes 393224 | tf_op jit(solution)/shard_map/ppermute | solution.py:35
  34.4 5.6 %collective-permute-start.20 = (f32[64,256]{1,0:T(8,128)S(1)}, f32[64,256]{1,0:T(8,128)S(1)}, u32[]{:S(2)}, u32[]{:S(2)}) collective-permute-start(f32[64,256]{1,0:T(8,128)S(1)} %pack.1.ref), channel_id=1, source_target_pairs={{0,6},{1,7},{2,4},{3,5},{4,2},{5,3},{6,0},{7,1},{8,14},{9,15},{10,... | collective-permute-start | bytes 196616 | tf_op jit(solution)/shard_map/ppermute | solution.py:35
  35.8 5.5 %collective-permute-start.18 = (f32[64,256]{1,0:T(8,128)S(1)}, f32[64,256]{1,0:T(8,128)S(1)}, u32[]{:S(2)}, u32[]{:S(2)}) collective-permute-start(f32[64,256]{1,0:T(8,128)S(1)} %pack.1.ref), channel_id=1, source_target_pairs={{0,4},{1,5},{2,6},{3,7},{4,0},{5,1},{6,2},{7,3},{8,12},{9,13},{10,... | collective-permute-start | bytes 196616 | tf_op jit(solution)/shard_map/ppermute | solution.py:35
  37.0 4.3 %collective-permute-start.16 = (f32[64,256]{1,0:T(8,128)S(1)}, f32[64,256]{1,0:T(8,128)S(1)}, u32[]{:S(2)}, u32[]{:S(2)}) collective-permute-start(f32[64,256]{1,0:T(8,128)S(1)} %pack.1.ref), channel_id=1, source_target_pairs={{0,2},{1,3},{2,0},{3,1},{4,6},{5,7},{6,4},{7,5},{8,10},{9,11},{10,... | collective-permute-start | bytes 196616 | tf_op jit(solution)/shard_map/ppermute | solution.py:35
  39.6 3.8 %collective-permute-start.15 = (f32[64,256]{1,0:T(8,128)S(1)}, f32[64,256]{1,0:T(8,128)S(1)}, u32[]{:S(2)}, u32[]{:S(2)}) collective-permute-start(f32[64,256]{1,0:T(8,128)S(1)} %relay.2.refs_0_), channel_id=1, source_target_pairs={{0,1},{1,0},{2,3},{3,2},{4,5},{5,4},{6,7},{7,6},{8,9},{9,8},{10,11... | collective-permute-start | bytes 196616 | tf_op jit(solution)/shard_map/ppermute | solution.py:35
  40.0 3.4 %collective-permute-start.21 = (f32[64,256]{1,0:T(8,128)S(1)}, f32[64,256]{1,0:T(8,128)S(1)}, u32[]{:S(2)}, u32[]{:S(2)}) collective-permute-start(f32[64,256]{1,0:T(8,128)S(1)} %relay.3.refs_3_), channel_id=1, source_target_pairs={{0,1},{1,0},{2,3},{3,2},{4,5},{5,4},{6,7},{7,6},{8,9},{9,8},{10,11... | collective-permute-start | bytes 196616 | tf_op jit(solution)/shard_map/ppermute | solution.py:35
  41.3 2.2 %collective-permute-start.19 = (f32[64,256]{1,0:T(8,128)S(1)}, f32[64,256]{1,0:T(8,128)S(1)}, u32[]{:S(2)}, u32[]{:S(2)}) collective-permute-start(f32[64,256]{1,0:T(8,128)S(1)} %collective-permute-done.18.refs_2_), channel_id=1, source_target_pairs={{0,1},{1,0},{2,3},{3,2},{4,5},{5,4},{6,7},{7,6},{8,9},{9,8},{10,11... | collective-permute-start | bytes 196616 | tf_op jit(solution)/shard_map/ppermute | solution.py:35
  41.3 2.1 %collective-permute-start.17 = (f32[64,256]{1,0:T(8,128)S(1)}, f32[64,256]{1,0:T(8,128)S(1)}, u32[]{:S(2)}, u32[]{:S(2)}) collective-permute-start(f32[64,256]{1,0:T(8,128)S(1)} %collective-permute-done.16.refs_1_), channel_id=1, source_target_pairs={{0,1},{1,0},{2,3},{3,2},{4,5},{5,4},{6,7},{7,6},{8,9},{9,8},{10,11... | collective-permute-start | bytes 196616 | tf_op jit(solution)/shard_map/ppermute | solution.py:35

commit v19 on v16

--- a/solution.py
+++ b/solution.py
@@ -143,7 +143,7 @@
     out_ref[...] = mine_ref[...] + got_ref[...]
 
 
-def prepare_kernel(levels, joined_ref, perm_ref, out_ref, joined_buf, sems):
+def prepare_kernel(levels, joined_ref, perm_ref, after_ref, out_ref, joined_buf, sems):
     rank = perm_ref.shape[1]
     leaves = lax.axis_size("leaf")
     leaf = lax.axis_index("leaf")
@@ -157,10 +157,12 @@
         copies[level].wait()
         chosen = (spot == perm_ref[level:level + 1, :]).astype(jnp.float32).astype(jnp.bfloat16)
         high_part, low_part = halves(joined_buf[level])
-        for place, part in enumerate((high_part, low_part, high_part)):
+        for place, part in enumerate((high_part, low_part)):
             for side in range(2):
                 moved = dot(chosen, part[:, side * rank:(side + 1) * rank], (1, 1)).astype(jnp.bfloat16)
                 out_ref[level, pl.ds((2 * place + side) * rank, rank), :] = moved
+                if place == 0:
+                    out_ref[level, pl.ds((4 + side) * rank, rank), :] = moved
 
 
 def by_side(side, own, other):
@@ -174,7 +176,7 @@
         row += piece.shape[0]
 
 
-def node_kernel(rank, slots, *refs):
+def node_kernel(rank, slots, after_ref, *refs):
     part_refs = refs[:slots]
     joined_ref, own_ref, other_ref, rest_ref = refs[slots:]
     side = lax.axis_index("rows") // slots
@@ -242,6 +244,10 @@
         refs[-1][slot] = ref[...]
 
 
+def join_kernel(after_ref, *refs):
+    refs[-1][...] = jnp.concatenate([ref[...] for ref in refs[:-1]], axis=1)
+
+
 def relay_kernel(after_ref, ref, out_ref):
     out_ref[...] = ref[...]
 
@@ -259,7 +265,7 @@
     factor_ref[kinds:, :] = low_part
 
 
-def apply_kernel(tile, own_ref, pair_ref, first_ref, left_ref, out_ref, flip_ref, factor_ref):
+def apply_kernel(tile, own_ref, pair_ref, first_ref, left_ref, after_ref, out_ref, flip_ref, factor_ref):
     pieces = [ref.at[slot] for slot in range(own_ref.shape[0]) for ref in (own_ref, pair_ref)]
     split_factor(pieces, flip_ref, factor_ref)
     for row in range(0, out_ref.shape[0], tile):
@@ -367,25 +373,35 @@
     )(keep, got)
     parts = [merged[0]] + [swap(merged[s], "rows", 2 * s) for s in range(1, slots)]
     gram_other = swap(gram, "rows", slots)
-    grams = [gram, gram_other, swap(gram, "rows", 1), swap(gram_other, "rows", 1)]
     prepared = pl.pallas_call(
         functools.partial(prepare_kernel, levels),
-        in_specs=[pl.BlockSpec(memory_space=pltpu.HBM), pl.BlockSpec()],
+        in_specs=[pl.BlockSpec(memory_space=pltpu.HBM), pl.BlockSpec(), pl.BlockSpec()],
         out_shape=jax.ShapeDtypeStruct((levels, 6 * rank, 2 * rank), jnp.bfloat16),
         scratch_shapes=[pltpu.VMEM((levels, 2 * rank, 2 * rank), jnp.float32), pltpu.SemaphoreType.DMA((levels,))],
         name="prepare",
         **settings(8, 2),
-    )(pltpu.with_memory_space_constraint(joined, pltpu.HBM), rank_perm)
+    )(pltpu.with_memory_space_constraint(joined, pltpu.HBM), rank_perm, merged[0])
 
     def message_shape(level):
         return floats((levels - level) * share + len(below_pairs(levels, level)) * rank, rank)
+
+    gram_other = pl.pallas_call(
+        relay_kernel, out_shape=floats(*gram.shape), name="relay", **settings(8, 0.1),
+    )(prepared, gram_other)
+    grams = [gram, gram_other, swap(gram, "rows", 1), swap(gram_other, "rows", 1)]
+    first = pl.pallas_call(
+        functools.partial(solve_kernel, per_step, width),
+        out_shape=floats(rows, columns),
+        name="solve",
+        **settings(8, 1),
+    )(moved, rhs, merged[0])
 
     own, other, rest = pl.pallas_call(
         functools.partial(node_kernel, rank, slots),
         out_shape=[floats(share, rank)] * 2 + [floats(share, size)],
         name="node",
         **settings(8, 1),
-    )(*parts, prepared)
+    )(first, *parts, prepared)
     message = pl.pallas_call(
         functools.partial(correct_kernel, levels, rank),
         out_shape=message_shape(1),
@@ -393,13 +409,6 @@
         **settings(8, 1),
     )(own, other, rest, *grams)
     early = [own] + [swap(own if slot < slots // 2 else other, "rows", 2 * slot) for slot in range(1, slots)]
-    first = pl.pallas_call(
-        functools.partial(solve_kernel, per_step, width),
-        out_shape=floats(rows, columns),
-        name="solve",
-        **settings(8, 8),
-    )(moved, rhs, merged[0])
-
     coefs = []
     for level in range(1, levels):
         last = level + 1 == levels
@@ -409,9 +418,11 @@
             out_shape=[floats(share, rank)] + ([] if last else [message_shape(level + 1)]),
             name=f"level{level}",
             **settings(8, 1 if last else 6),
-        )(message, arrived, prepared, first if last else arrived)
+        )(message, arrived, prepared, arrived)
         coefs.append(outs[0])
         message = outs[-1]
+    packed = coefs[0] if levels == 3 else jnp.concatenate(coefs[:-1], axis=1)
+    ahead = swap(packed, "rows", 2 * (slots - 1))
     stack = pl.pallas_call(
         stack_kernel, out_shape=floats(slots, share, rank), name="stack", **settings(8, 0.1),
     )(first, *early)
@@ -424,7 +435,7 @@
         ],
         name="apply",
         **settings(8, 1.8),
-    )(stack, swap(stack, "rows", 1), first, left_basis)
+    )(stack, swap(stack, "rows", 1), first, left_basis, ahead)
 
     pack = pl.pallas_call(
         pack_kernel, out_shape=floats(share, size), name="pack", **settings(8, 0.1),
@@ -432,7 +443,12 @@
     pieces = []
     for slot in range(slots):
         piece = swap(pack, "rows", 2 * slot) if slot > 0 else pack
-        if slot in (0, slots - 1):
+        if slot == slots - 1:
+            tail = swap(coefs[-1], "rows", 2 * slot)
+            piece = pl.pallas_call(
+                join_kernel, out_shape=floats(share, size), name="join", **settings(8, 0.1),
+            )(second, ahead, tail)
+        elif slot == 0:
             piece = pl.pallas_call(
                 relay_kernel, out_shape=floats(share, size), name="relay", **settings(8, 0.1),
             )(second, piece)

time: 47 us -> 47.1 us (level)
  starting transfers between devices: 20.7 us -> 22.4 us
  waiting for transfers between devices: 4.74 us -> 3.12 us
    ppermute x22 -> x23, starting transfers between devices: 20.7 us -> 22.4 us  [swap(): return lax.ppermute(value, axis, [(i, i ^ mask) for i in range(count)])]
    ppermute x22 -> x23, waiting for transfers between devices: 4.74 us -> 3.12 us  [swap(): return lax.ppermute(value, axis, [(i, i ^ mask) for i in range(count)])]
  transfers between devices with their start and end apart: 22 -> 23, of which waited for: 7 -> 8; matrix products, arithmetic and copies ran while one was open for 0% -> 0% of each run, Pallas kernels for 28% -> 28%
where the time goes in v19:
time: 47.1 us; the launch traced here: 47 us
  starting transfers between devices  22.4 us (48%)
  Pallas kernels  21.1 us (45%)
  waiting for transfers between devices  3.12 us (7%)
    ppermute x23, starting transfers between devices, swap(): return lax.ppermute(value, axis, [(i, i ^ mask) for i in range(count)])  22.4 us
    pallas_call x1, Pallas kernels, per_device(): pl.pallas_call(functools.partial(expand_kernel, levels, width, count), ou...  4.28 us
    pallas_call x2, Pallas kernels, project(): pl.pallas_call(functools.partial(project_kernel, other), out_shape=floats...  3.99 us
    pallas_call x1, Pallas kernels, per_device(): pl.pallas_call(functools.partial(gram_kernel, levels, per_step, width), i...  3.34 us
    ppermute x23, waiting for transfers between devices, swap(): return lax.ppermute(value, axis, [(i, i ^ mask) for i in range(count)])  3.12 us
    pallas_call x1, Pallas kernels, per_device(): pl.pallas_call(functools.partial(solve_kernel, per_step, width), out_shap...  2.23 us
    pallas_call x1, Pallas kernels, per_device(): pl.pallas_call(functools.partial(prepare_kernel, levels), in_specs=[pl.Bl...  1.69 us
    pallas_call x1, Pallas kernels, per_device(): pl.pallas_call(functools.partial(weigh_kernel, blocks_per_step(nblocks, 9...  1.6 us
  transfers between devices with their start and end apart: 23, of which 8 were waited for; matrix products, arithmetic and copies ran while one was open for 0% of the time, Pallas kernels for 28%

profile of v19, /device:TPU:0, one launch (start us, length us, event | category | flops | bytes accessed | tf_op | source)
XLA Modules:
  0.0 47.0 jit_solution(6883298646980466944)
XLA Ops:
  0.0 3.3 %gram.1 = (bf16[384,4608]{1,0:T(8,128)(2,1)S(1)}, f32[64,384]{1,0:T(8,128)S(1)}, f32[64,384]{1,0:T(8,128)S(1)}) custom-call(bf16[3,4608,128]{2,1,0:T(8,128)(2,1)} %right_ref.1, bf16[3,4608,128]{2,1,0:T(8,128)(2,1)} %refs_9_.1), custom_call_target="tpu_custom_call" | custom-call | flops 3300000000 | tf_op jit(solution)/shard_map/gram/pallas_call | solution.py:316
  3.4 0.5 %collective-permute-start = (f32[64,384]{1,0:T(8,128)S(1)}, f32[64,384]{1,0:T(8,128)S(1)}, u32[]{:S(2)}, u32[]{:S(2)}) collective-permute-start(f32[64,384]{1,0:T(8,128)S(1)} %get-tuple-element.19), channel_id=1, source_target_pairs={{0,1},{1,0},{2,3},{3,2},{4,5},{5,4},{6,7},{7,6},{8,9},{9,8},{10,11... | collective-permute-start | bytes 294920 | tf_op jit(solution)/shard_map/ppermute | solution.py:35
  3.9 0.0 copy-done.2
  3.9 1.0 %permute.1.moved_ref = bf16[18,256,256]{2,1,0:T(8,128)(2,1)S(1)} custom-call(s32[18,256]{1,0:T(8,128)S(1)} %copy-done.2, bf16[18,256,256]{2,1,0:T(8,128)(2,1)S(1)} %copy-done.1), custom_call_target="tpu_custom_call" | custom-call | flops 1650000000 | tf_op jit(solution)/shard_map/permute/pallas_call | solution.py:332
  4.9 0.0 collective-permute-done.got_ref
  4.9 0.0 slice-start
  5.0 2.8 %collective-permute-start.1 = (f32[64,384]{1,0:T(8,128)S(1)}, f32[64,384]{1,0:T(8,128)S(1)}, u32[]{:S(2)}, u32[]{:S(2)}) collective-permute-start(f32[64,384]{1,0:T(8,128)S(1)} %add.2.after_ref.mine_ref), channel_id=1, source_target_pairs={{0,2},{1,3},{2,0},{3,1},{4,6},{5,7},{6,4},{7,5},{8,10},{9,11},{10,... | collective-permute-start | bytes 294920 | tf_op jit(solution)/shard_map/ppermute | solution.py:35
  7.7 1.6 %weigh.1.factor_ref = bf16[768,4608]{1,0:T(8,128)(2,1)S(1)} custom-call(bf16[18,256,256]{2,1,0:T(8,128)(2,1)S(1)} %permute.1.moved_ref, bf16[384,4608]{1,0:T(8,128)(2,1)S(1)} %get-tuple-element.17.flip_ref, f32[64,384]{1,0:T(8,128)S(1)} %add.2.after_ref.mine_ref), custom_call_target="tpu_custom_call" | custom-call | flops 2640000000 | tf_op jit(solution)/shard_map/weigh/pallas_call | solution.py:345
  9.4 2.0 %project_other.1 = f32[384,256]{1,0:T(8,128)S(1)} custom-call(bf16[768,4608]{1,0:T(8,128)(2,1)S(1)} %weigh.1.factor_ref, bf16[4608,512]{1,0:T(8,128)(2,1)S(1)} %bitcast.1, f32[64,384]{1,0:T(8,128)S(1)} %add.2.after_ref.mine_ref), custom_call_target="tpu_custom_call" | custom-call | flops 1100000000 | tf_op jit(solution)/shard_map/project_other/pallas_call | solution.py:353
  11.4 0.1 collective-permute-start.2
  11.5 0.0 collective-permute-done.1.got_ref
  11.5 0.0 copy-start.3
  11.5 1.6 %collective-permute-start.10 = (f32[64,384]{1,0:T(8,128)S(1)}, f32[64,384]{1,0:T(8,128)S(1)}, u32[]{:S(2)}, u32[]{:S(2)}) collective-permute-start(f32[64,384]{1,0:T(8,128)S(1)} %add.3.after_ref.mine_ref), channel_id=1, source_target_pairs={{0,4},{1,5},{2,6},{3,7},{4,0},{5,1},{6,2},{7,3},{8,12},{9,13},{10,... | collective-permute-start | bytes 294920 | tf_op jit(solution)/shard_map/ppermute | solution.py:35
  13.1 0.2 collective-permute-start.11
  13.3 2.0 %project_own.1.keep_ref = f32[384,256]{1,0:T(8,128)S(1)} custom-call(bf16[768,4608]{1,0:T(8,128)(2,1)S(1)} %weigh.1.factor_ref, bf16[4608,512]{1,0:T(8,128)(2,1)S(1)} %bitcast.1, f32[64,384]{1,0:T(8,128)S(1)} %add.3.after_ref.mine_ref), custom_call_target="tpu_custom_call" | custom-call | flops 4400000000 | tf_op jit(solution)/shard_map/project_own/pallas_call | solution.py:353
  15.3 0.0 collective-permute-done.2.got_ref
  15.3 0.2 merge.1
  15.5 1.1 %collective-permute-start.3 = (f32[64,384]{1,0:T(8,128)S(1)}, f32[64,384]{1,0:T(8,128)S(1)}, u32[]{:S(2)}, u32[]{:S(2)}) collective-permute-start(f32[64,384]{1,0:T(8,128)S(1)} %get-tuple-element.21), channel_id=1, source_target_pairs={{0,2},{1,3},{2,0},{3,1},{4,6},{5,7},{6,4},{7,5},{8,10},{9,11},{10,... | collective-permute-start | bytes 294920 | tf_op jit(solution)/shard_map/ppermute | solution.py:35
  16.6 0.5 %collective-permute-start.4 = (f32[64,384]{1,0:T(8,128)S(1)}, f32[64,384]{1,0:T(8,128)S(1)}, u32[]{:S(2)}, u32[]{:S(2)}) collective-permute-start(f32[64,384]{1,0:T(8,128)S(1)} %get-tuple-element.22), channel_id=1, source_target_pairs={{0,4},{1,5},{2,6},{3,7},{4,0},{5,1},{6,2},{7,3},{8,12},{9,13},{10,... | collective-permute-start | bytes 294920 | tf_op jit(solution)/shard_map/ppermute | solution.py:35
  17.1 2.0 %collective-permute-start.5 = (f32[64,384]{1,0:T(8,128)S(1)}, f32[64,384]{1,0:T(8,128)S(1)}, u32[]{:S(2)}, u32[]{:S(2)}) collective-permute-start(f32[64,384]{1,0:T(8,128)S(1)} %get-tuple-element.23), channel_id=1, source_target_pairs={{0,6},{1,7},{2,4},{3,5},{4,2},{5,3},{6,0},{7,1},{8,14},{9,15},{10,... | collective-permute-start | bytes 294920 | tf_op jit(solution)/shard_map/ppermute | solution.py:35
  19.1 1.7 %prepare.1.refs_4_.after_ref.joined_ref = bf16[3,768,256]{2,1,0:T(8,128)(2,1)S(1)} custom-call(f32[7,256,256]{2,1,0:T(8,128)} %joined_ref.1, s32[3,128]{1,0:T(4,128)S(1)} %copy-done.3, f32[64,384]{1,0:T(8,128)S(1)} %get-tuple-element.20.refs_0_.after_ref), custom_call_target="tpu_custom_call" | custom-call | flops 2200000000 | tf_op jit(solution)/shard_map/prepare/pallas_call | solution.py:376
  20.8 0.0 collective-permute-done.10.ref
  20.8 0.1 collective-permute-start.12
  20.9 2.2 %solve.1.after_ref.first_ref = f32[4608,512]{1,0:T(8,128)S(1)} custom-call(bf16[18,256,256]{2,1,0:T(8,128)(2,1)S(1)} %permute.1.moved_ref, bf16[4608,512]{1,0:T(8,128)(2,1)S(1)} %bitcast.1, f32[64,384]{1,0:T(8,128)S(1)} %get-tuple-element.20.refs_0_.after_ref), custom_call_target="tpu_custom_call" | custom-call | flops 1100000000 | tf_op jit(solution)/shard_map/solve/pallas_call | solution.py:392
  23.1 0.0 collective-permute-done.3.refs_1_
  23.1 0.5 %collective-permute-done.4.refs_2_ = f32[64,384]{1,0:T(8,128)S(1)} collective-permute-done((f32[64,384]{1,0:T(8,128)S(1)}, f32[64,384]{1,0:T(8,128)S(1)}, u32[]{:S(2)}, u32[]{:S(2)}) %collective-permute-start.4) | collective-permute-done | bytes 98336 | tf_op jit(solution)/shard_map/ppermute | solution.py:35
  23.7 0.0 collective-permute-done.5.refs_3_
  23.7 0.2 node.1
  23.9 0.0 collective-permute-done.11.pair_mine_ref
  23.9 0.0 collective-permute-done.12.pair_theirs_ref
  23.9 0.3 correct.1.sent_ref
  24.2 1.6 %collective-permute-start.13 = (f32[256,128]{1,0:T(8,128)S(1)}, f32[256,128]{1,0:T(8,128)S(1)}, u32[]{:S(2)}, u32[]{:S(2)}) collective-permute-start(f32[256,128]{1,0:T(8,128)S(1)} %correct.1.sent_ref), channel_id=1, source_target_pairs={{0,8},{8,0},{16,24},{24,16},{1,9},{9,1},{17,25},{25,17},{2,10},{10... | collective-permute-start | bytes 393224 | tf_op jit(solution)/shard_map/ppermute | solution.py:35
  25.8 0.8 %collective-permute-start.6 = (f32[64,128]{1,0:T(8,128)S(1)}, f32[64,128]{1,0:T(8,128)S(1)}, u32[]{:S(2)}, u32[]{:S(2)}) collective-permute-start(f32[64,128]{1,0:T(8,128)S(1)} %get-tuple-element.24.refs_0_.own_ref), channel_id=1, source_target_pairs={{0,2},{1,3},{2,0},{3,1},{4,6},{5,7},{6,4},{7,5},{8,10},{9,11},{10,... | collective-permute-start | bytes 98312 | tf_op jit(solution)/shard_map/ppermute | solution.py:35
  26.6 0.9 %collective-permute-start.7 = (f32[64,128]{1,0:T(8,128)S(1)}, f32[64,128]{1,0:T(8,128)S(1)}, u32[]{:S(2)}, u32[]{:S(2)}) collective-permute-start(f32[64,128]{1,0:T(8,128)S(1)} %get-tuple-element.25.other_ref), channel_id=1, source_target_pairs={{0,4},{1,5},{2,6},{3,7},{4,0},{5,1},{6,2},{7,3},{8,12},{9,13},{10,... | collective-permute-start | bytes 98312 | tf_op jit(solution)/shard_map/ppermute | solution.py:35
  27.6 1.7 %collective-permute-start.8 = (f32[64,128]{1,0:T(8,128)S(1)}, f32[64,128]{1,0:T(8,128)S(1)}, u32[]{:S(2)}, u32[]{:S(2)}) collective-permute-start(f32[64,128]{1,0:T(8,128)S(1)} %get-tuple-element.25.other_ref), channel_id=1, source_target_pairs={{0,6},{1,7},{2,4},{3,5},{4,2},{5,3},{6,0},{7,1},{8,14},{9,15},{10,... | collective-permute-start | bytes 98312 | tf_op jit(solution)/shard_map/ppermute | solution.py:35
  29.3 0.3 collective-permute-done.13.got_ref.after_ref
  29.6 0.4 level1.1
  30.0 2.7 %collective-permute-start.15 = (f32[64,128]{1,0:T(8,128)S(1)}, f32[64,128]{1,0:T(8,128)S(1)}, u32[]{:S(2)}, u32[]{:S(2)}) collective-permute-start(f32[64,128]{1,0:T(8,128)S(1)} %get-tuple-element.28.sent_ref), channel_id=1, source_target_pairs={{0,16},{8,24},{16,0},{24,8},{1,17},{9,25},{17,1},{25,9},{2,18},{10... | collective-permute-start | bytes 98312 | tf_op jit(solution)/shard_map/ppermute | solution.py:35
  32.7 0.0 collective-permute-done.6.refs_1_
  32.7 0.0 collective-permute-done.7.refs_2_
  32.7 0.0 collective-permute-done.8.refs_3_
  32.7 0.0 copy-start
  32.7 0.1 collective-permute-start.9
  32.8 1.5 %collective-permute-start.14 = (f32[64,128]{1,0:T(8,128)S(1)}, f32[64,128]{1,0:T(8,128)S(1)}, u32[]{:S(2)}, u32[]{:S(2)}) collective-permute-start(f32[64,128]{1,0:T(8,128)S(1)} %get-tuple-element.27.refs_0_), channel_id=1, source_target_pairs={{0,6},{1,7},{2,4},{3,5},{4,2},{5,3},{6,0},{7,1},{8,14},{9,15},{10,... | collective-permute-start | bytes 98312 | tf_op jit(solution)/shard_map/ppermute | solution.py:35
  34.3 0.6 %collective-permute-done.15.got_ref.after_ref = f32[64,128]{1,0:T(8,128)S(1)} collective-permute-done((f32[64,128]{1,0:T(8,128)S(1)}, f32[64,128]{1,0:T(8,128)S(1)}, u32[]{:S(2)}, u32[]{:S(2)}) %collective-permute-start.15) | collective-permute-done | bytes 32800 | tf_op jit(solution)/shard_map/ppermute | solution.py:35
  34.9 0.2 level2.1.refs_1_
  35.1 1.0 %collective-permute-start.21 = (f32[64,128]{1,0:T(8,128)S(1)}, f32[64,128]{1,0:T(8,128)S(1)}, u32[]{:S(2)}, u32[]{:S(2)}) collective-permute-start(f32[64,128]{1,0:T(8,128)S(1)} %level2.1.refs_1_), channel_id=1, source_target_pairs={{0,6},{1,7},{2,4},{3,5},{4,2},{5,3},{6,0},{7,1},{8,14},{9,15},{10,... | collective-permute-start | bytes 98312 | tf_op jit(solution)/shard_map/ppermute | solution.py:35
  36.1 1.0 %collective-permute-start.17 = (f32[64,256]{1,0:T(8,128)S(1)}, f32[64,256]{1,0:T(8,128)S(1)}, u32[]{:S(2)}, u32[]{:S(2)}) collective-permute-start(f32[64,256]{1,0:T(8,128)S(1)} %pack.1.ref), channel_id=1, source_target_pairs={{0,2},{1,3},{2,0},{3,1},{4,6},{5,7},{6,4},{7,5},{8,10},{9,11},{10,... | collective-permute-start | bytes 196616 | tf_op jit(solution)/shard_map/ppermute | solution.py:35
  37.2 1.5 %collective-permute-start.19 = (f32[64,256]{1,0:T(8,128)S(1)}, f32[64,256]{1,0:T(8,128)S(1)}, u32[]{:S(2)}, u32[]{:S(2)}) collective-permute-start(f32[64,256]{1,0:T(8,128)S(1)} %pack.1.ref), channel_id=1, source_target_pairs={{0,4},{1,5},{2,6},{3,7},{4,0},{5,1},{6,2},{7,3},{8,12},{9,13},{10,... | collective-permute-start | bytes 196616 | tf_op jit(solution)/shard_map/ppermute | solution.py:35
  38.7 0.0 collective-permute-done.14.after_ref.refs_0_
  38.7 0.0 collective-permute-done.9.pair_ref
  38.7 1.6 %apply.1.after_ref.refs_8_ = f32[4608,512]{1,0:T(8,128)S(1)} custom-call(f32[4,64,128]{2,1,0:T(8,128)S(1)} %stack.1.own_ref, f32[4,64,128]{2,1,0:T(8,128)S(1)} %collective-permute-done.9.pair_ref, f32[4608,512]{1,0:T(8,128)S(1)} %solve.1.after_ref.first_ref, bf16[3,4608,128]{2,1,0:T(8,128)(2,1)S(1)} %copy-done, ...), custom_call_target="tpu_custom_call" | custom-call | flops 1980000000 | tf_op jit(solution)/shard_map/apply/pallas_call | solution.py:429
  40.3 0.1 collective-permute-start.16
  40.4 0.0 collective-permute-done.21.refs_1_
  40.4 0.5 %collective-permute-start.22 = (f32[64,256]{1,0:T(8,128)S(1)}, f32[64,256]{1,0:T(8,128)S(1)}, u32[]{:S(2)}, u32[]{:S(2)}) collective-permute-start(f32[64,256]{1,0:T(8,128)S(1)} %join.1.refs_6_), channel_id=1, source_target_pairs={{0,1},{1,0},{2,3},{3,2},{4,5},{5,4},{6,7},{7,6},{8,9},{9,8},{10,11... | collective-permute-start | bytes 196616 | tf_op jit(solution)/shard_map/ppermute | solution.py:35
  40.9 0.0 collective-permute-done.17.refs_2_
  40.9 0.1 collective-permute-start.18
  41.0 0.4 collective-permute-done.19.refs_4_
  41.4 0.0 collective-permute-start.20
  41.5 0.1 collective-permute-done.16.refs_1_
  41.6 0.2 collective-permute-done.22.refs_7_
  41.8 0.4 collective-permute-done.18.refs_3_
  42.2 0.5 %collective-permute-done.20.refs_5_ = f32[64,256]{1,0:T(8,128)S(1)} collective-permute-done((f32[64,256]{1,0:T(8,128)S(1)}, f32[64,256]{1,0:T(8,128)S(1)}, u32[]{:S(2)}, u32[]{:S(2)}) %collective-permute-start.20) | collective-permute-done | bytes 65568 | tf_op jit(solution)/shard_map/ppermute | solution.py:35
  42.7 4.3 %expand.1 = f32[4608,512]{1,0:T(8,128)} custom-call(f32[64,256]{1,0:T(8,128)S(1)} %relay.3.refs_0_, f32[64,256]{1,0:T(8,128)S(1)} %collective-permute-done.16.refs_1_, f32[64,256]{1,0:T(8,128)S(1)} %collective-permute-done.17.refs_2_, f32[64,256]{1,0:T(8,128)S(1)} %collective-permute-done.18.refs_3_, f32[64,256]{1,0:T(8,128)S(1)} %collective-permute-done.19.refs_4_, ...), custom_call_target="tpu_custom_call" | custom-call | flops 5500000256 | tf_op jit(solution)/shard_map/expand/pallas_call | solution.py:456
  (16 shorter events, 0.1 us)
Async XLA Ops:
  0.0 3.9 %copy-start.2 = (s32[18,256]{1,0:T(8,128)S(1)}, s32[18,256]{1,0:T(8,128)}, u32[]{:S(2)}) copy-start(s32[18,256]{1,0:T(8,128)} %order_ref.1) | copy-start | bytes 55300
  0.0 3.9 %copy-start.1 = (bf16[18,256,256]{2,1,0:T(8,128)(2,1)S(1)}, bf16[18,256,256]{2,1,0:T(8,128)(2,1)}, u32[]{:S(2)}) copy-start(bf16[18,256,256]{2,1,0:T(8,128)(2,1)} %inv_ref.1) | copy-start | bytes 7077892
  3.4 1.6 %collective-permute-start = (f32[64,384]{1,0:T(8,128)S(1)}, f32[64,384]{1,0:T(8,128)S(1)}, u32[]{:S(2)}, u32[]{:S(2)}) collective-permute-start(f32[64,384]{1,0:T(8,128)S(1)} %get-tuple-element.19), channel_id=1, source_target_pairs={{0,1},{1,0},{2,3},{3,2},{4,5},{5,4},{6,7},{7,6},{8,9},{9,8},{10,11... | collective-permute-start | bytes 294920 | tf_op jit(solution)/shard_map/ppermute | solution.py:35
  4.9 4.4 %slice-start = ((s8[4718592]{0:T(1024)(128)(4,1)}), s8[4194304]{0:T(1024)(128)(4,1)S(1)}, s32[]{:S(2)}) async-start(s8[4718592]{0:T(1024)(128)(4,1)} %bitcast), calls=%async_computation | async-start | bytes 8388608
  5.0 6.5 %collective-permute-start.1 = (f32[64,384]{1,0:T(8,128)S(1)}, f32[64,384]{1,0:T(8,128)S(1)}, u32[]{:S(2)}, u32[]{:S(2)}) collective-permute-start(f32[64,384]{1,0:T(8,128)S(1)} %add.2.after_ref.mine_ref), channel_id=1, source_target_pairs={{0,2},{1,3},{2,0},{3,1},{4,6},{5,7},{6,4},{7,5},{8,10},{9,11},{10,... | collective-permute-start | bytes 294920 | tf_op jit(solution)/shard_map/ppermute | solution.py:35
  7.7 1.6 %slice-start.1 = ((s8[4718592]{0:T(1024)(128)(4,1)}), s8[524288]{0:T(1024)(128)(4,1)S(1)}, s32[]{:S(2)}) async-start(s8[4718592]{0:T(1024)(128)(4,1)} %bitcast), calls=%async_computation.1 | async-start | bytes 1048576
  11.4 3.9 %collective-permute-start.2 = (f32[384,256]{1,0:T(8,128)S(1)}, f32[384,256]{1,0:T(8,128)S(1)}, u32[]{:S(2)}, u32[]{:S(2)}) collective-permute-start(f32[384,256]{1,0:T(8,128)S(1)} %project_other.1), channel_id=1, source_target_pairs={{0,1},{1,0},{2,3},{3,2},{4,5},{5,4},{6,7},{7,6},{8,9},{9,8},{10,11... | collective-permute-start | bytes 1179656 | tf_op jit(solution)/shard_map/ppermute | solution.py:35
  11.5 7.6 %copy-start.3 = (s32[3,128]{1,0:T(4,128)S(1)}, s32[3,128]{1,0:T(4,128)}, u32[]{:S(2)}) copy-start(s32[3,128]{1,0:T(4,128)} %perm_ref.1) | copy-start | bytes 4612
  11.5 9.2 %collective-permute-start.10 = (f32[64,384]{1,0:T(8,128)S(1)}, f32[64,384]{1,0:T(8,128)S(1)}, u32[]{:S(2)}, u32[]{:S(2)}) collective-permute-start(f32[64,384]{1,0:T(8,128)S(1)} %add.3.after_ref.mine_ref), channel_id=1, source_target_pairs={{0,4},{1,5},{2,6},{3,7},{4,0},{5,1},{6,2},{7,3},{8,12},{9,13},{10,... | collective-permute-start | bytes 294920 | tf_op jit(solution)/shard_map/ppermute | solution.py:35
  13.1 10.8 %collective-permute-start.11 = (f32[64,384]{1,0:T(8,128)S(1)}, f32[64,384]{1,0:T(8,128)S(1)}, u32[]{:S(2)}, u32[]{:S(2)}) collective-permute-start(f32[64,384]{1,0:T(8,128)S(1)} %add.3.after_ref.mine_ref), channel_id=1, source_target_pairs={{0,1},{1,0},{2,3},{3,2},{4,5},{5,4},{6,7},{7,6},{8,9},{9,8},{10,11... | collective-permute-start | bytes 294920 | tf_op jit(solution)/shard_map/ppermute | solution.py:35
  15.5 7.6 %collective-permute-start.3 = (f32[64,384]{1,0:T(8,128)S(1)}, f32[64,384]{1,0:T(8,128)S(1)}, u32[]{:S(2)}, u32[]{:S(2)}) collective-permute-start(f32[64,384]{1,0:T(8,128)S(1)} %get-tuple-element.21), channel_id=1, source_target_pairs={{0,2},{1,3},{2,0},{3,1},{4,6},{5,7},{6,4},{7,5},{8,10},{9,11},{10,... | collective-permute-start | bytes 294920 | tf_op jit(solution)/shard_map/ppermute | solution.py:35
  16.6 7.0 %collective-permute-start.4 = (f32[64,384]{1,0:T(8,128)S(1)}, f32[64,384]{1,0:T(8,128)S(1)}, u32[]{:S(2)}, u32[]{:S(2)}) collective-permute-start(f32[64,384]{1,0:T(8,128)S(1)} %get-tuple-element.22), channel_id=1, source_target_pairs={{0,4},{1,5},{2,6},{3,7},{4,0},{5,1},{6,2},{7,3},{8,12},{9,13},{10,... | collective-permute-start | bytes 294920 | tf_op jit(solution)/shard_map/ppermute | solution.py:35
  17.1 6.5 %collective-permute-start.5 = (f32[64,384]{1,0:T(8,128)S(1)}, f32[64,384]{1,0:T(8,128)S(1)}, u32[]{:S(2)}, u32[]{:S(2)}) collective-permute-start(f32[64,384]{1,0:T(8,128)S(1)} %get-tuple-element.23), channel_id=1, source_target_pairs={{0,6},{1,7},{2,4},{3,5},{4,2},{5,3},{6,0},{7,1},{8,14},{9,15},{10,... | collective-permute-start | bytes 294920 | tf_op jit(solution)/shard_map/ppermute | solution.py:35
  20.8 3.1 %collective-permute-start.12 = (f32[64,384]{1,0:T(8,128)S(1)}, f32[64,384]{1,0:T(8,128)S(1)}, u32[]{:S(2)}, u32[]{:S(2)}) collective-permute-start(f32[64,384]{1,0:T(8,128)S(1)} %relay.2.theirs_ref), channel_id=1, source_target_pairs={{0,1},{1,0},{2,3},{3,2},{4,5},{5,4},{6,7},{7,6},{8,9},{9,8},{10,11... | collective-permute-start | bytes 294920 | tf_op jit(solution)/shard_map/ppermute | solution.py:35
  24.2 5.4 %collective-permute-start.13 = (f32[256,128]{1,0:T(8,128)S(1)}, f32[256,128]{1,0:T(8,128)S(1)}, u32[]{:S(2)}, u32[]{:S(2)}) collective-permute-start(f32[256,128]{1,0:T(8,128)S(1)} %correct.1.sent_ref), channel_id=1, source_target_pairs={{0,8},{8,0},{16,24},{24,16},{1,9},{9,1},{17,25},{25,17},{2,10},{10... | collective-permute-start | bytes 393224 | tf_op jit(solution)/shard_map/ppermute | solution.py:35
  25.8 6.9 %collective-permute-start.6 = (f32[64,128]{1,0:T(8,128)S(1)}, f32[64,128]{1,0:T(8,128)S(1)}, u32[]{:S(2)}, u32[]{:S(2)}) collective-permute-start(f32[64,128]{1,0:T(8,128)S(1)} %get-tuple-element.24.refs_0_.own_ref), channel_id=1, source_target_pairs={{0,2},{1,3},{2,0},{3,1},{4,6},{5,7},{6,4},{7,5},{8,10},{9,11},{10,... | collective-permute-start | bytes 98312 | tf_op jit(solution)/shard_map/ppermute | solution.py:35
  26.6 6.1 %collective-permute-start.7 = (f32[64,128]{1,0:T(8,128)S(1)}, f32[64,128]{1,0:T(8,128)S(1)}, u32[]{:S(2)}, u32[]{:S(2)}) collective-permute-start(f32[64,128]{1,0:T(8,128)S(1)} %get-tuple-element.25.other_ref), channel_id=1, source_target_pairs={{0,4},{1,5},{2,6},{3,7},{4,0},{5,1},{6,2},{7,3},{8,12},{9,13},{10,... | collective-permute-start | bytes 98312 | tf_op jit(solution)/shard_map/ppermute | solution.py:35
  27.6 5.1 %collective-permute-start.8 = (f32[64,128]{1,0:T(8,128)S(1)}, f32[64,128]{1,0:T(8,128)S(1)}, u32[]{:S(2)}, u32[]{:S(2)}) collective-permute-start(f32[64,128]{1,0:T(8,128)S(1)} %get-tuple-element.25.other_ref), channel_id=1, source_target_pairs={{0,6},{1,7},{2,4},{3,5},{4,2},{5,3},{6,0},{7,1},{8,14},{9,15},{10,... | collective-permute-start | bytes 98312 | tf_op jit(solution)/shard_map/ppermute | solution.py:35
  30.0 4.9 %collective-permute-start.15 = (f32[64,128]{1,0:T(8,128)S(1)}, f32[64,128]{1,0:T(8,128)S(1)}, u32[]{:S(2)}, u32[]{:S(2)}) collective-permute-start(f32[64,128]{1,0:T(8,128)S(1)} %get-tuple-element.28.sent_ref), channel_id=1, source_target_pairs={{0,16},{8,24},{16,0},{24,8},{1,17},{9,25},{17,1},{25,9},{2,18},{10... | collective-permute-start | bytes 98312 | tf_op jit(solution)/shard_map/ppermute | solution.py:35
  32.7 6.0 %copy-start = (bf16[3,4608,128]{2,1,0:T(8,128)(2,1)S(1)}, bf16[3,4608,128]{2,1,0:T(8,128)(2,1)}, u32[]{:S(2)}) copy-start(bf16[3,4608,128]{2,1,0:T(8,128)(2,1)} %refs_9_.1) | copy-start | bytes 10616836
  32.7 5.9 %collective-permute-start.9 = (f32[4,64,128]{2,1,0:T(8,128)S(1)}, f32[4,64,128]{2,1,0:T(8,128)S(1)}, u32[]{:S(2)}, u32[]{:S(2)}) collective-permute-start(f32[4,64,128]{2,1,0:T(8,128)S(1)} %stack.1.own_ref), channel_id=1, source_target_pairs={{0,1},{1,0},{2,3},{3,2},{4,5},{5,4},{6,7},{7,6},{8,9},{9,8},{10,11... | collective-permute-start | bytes 393224 | tf_op jit(solution)/shard_map/ppermute | solution.py:35
  32.8 5.9 %collective-permute-start.14 = (f32[64,128]{1,0:T(8,128)S(1)}, f32[64,128]{1,0:T(8,128)S(1)}, u32[]{:S(2)}, u32[]{:S(2)}) collective-permute-start(f32[64,128]{1,0:T(8,128)S(1)} %get-tuple-element.27.refs_0_), channel_id=1, source_target_pairs={{0,6},{1,7},{2,4},{3,5},{4,2},{5,3},{6,0},{7,1},{8,14},{9,15},{10,... | collective-permute-start | bytes 98312 | tf_op jit(solution)/shard_map/ppermute | solution.py:35
  35.1 5.3 %collective-permute-start.21 = (f32[64,128]{1,0:T(8,128)S(1)}, f32[64,128]{1,0:T(8,128)S(1)}, u32[]{:S(2)}, u32[]{:S(2)}) collective-permute-start(f32[64,128]{1,0:T(8,128)S(1)} %level2.1.refs_1_), channel_id=1, source_target_pairs={{0,6},{1,7},{2,4},{3,5},{4,2},{5,3},{6,0},{7,1},{8,14},{9,15},{10,... | collective-permute-start | bytes 98312 | tf_op jit(solution)/shard_map/ppermute | solution.py:35
  36.1 4.8 %collective-permute-start.17 = (f32[64,256]{1,0:T(8,128)S(1)}, f32[64,256]{1,0:T(8,128)S(1)}, u32[]{:S(2)}, u32[]{:S(2)}) collective-permute-start(f32[64,256]{1,0:T(8,128)S(1)} %pack.1.ref), channel_id=1, source_target_pairs={{0,2},{1,3},{2,0},{3,1},{4,6},{5,7},{6,4},{7,5},{8,10},{9,11},{10,... | collective-permute-start | bytes 196616 | tf_op jit(solution)/shard_map/ppermute | solution.py:35
  37.2 4.3 %collective-permute-start.19 = (f32[64,256]{1,0:T(8,128)S(1)}, f32[64,256]{1,0:T(8,128)S(1)}, u32[]{:S(2)}, u32[]{:S(2)}) collective-permute-start(f32[64,256]{1,0:T(8,128)S(1)} %pack.1.ref), channel_id=1, source_target_pairs={{0,4},{1,5},{2,6},{3,7},{4,0},{5,1},{6,2},{7,3},{8,12},{9,13},{10,... | collective-permute-start | bytes 196616 | tf_op jit(solution)/shard_map/ppermute | solution.py:35
  40.3 1.3 %collective-permute-start.16 = (f32[64,256]{1,0:T(8,128)S(1)}, f32[64,256]{1,0:T(8,128)S(1)}, u32[]{:S(2)}, u32[]{:S(2)}) collective-permute-start(f32[64,256]{1,0:T(8,128)S(1)} %relay.3.refs_0_), channel_id=1, source_target_pairs={{0,1},{1,0},{2,3},{3,2},{4,5},{5,4},{6,7},{7,6},{8,9},{9,8},{10,11... | collective-permute-start | bytes 196616 | tf_op jit(solution)/shard_map/ppermute | solution.py:35
  40.4 1.5 %collective-permute-start.22 = (f32[64,256]{1,0:T(8,128)S(1)}, f32[64,256]{1,0:T(8,128)S(1)}, u32[]{:S(2)}, u32[]{:S(2)}) collective-permute-start(f32[64,256]{1,0:T(8,128)S(1)} %join.1.refs_6_), channel_id=1, source_target_pairs={{0,1},{1,0},{2,3},{3,2},{4,5},{5,4},{6,7},{7,6},{8,9},{9,8},{10,11... | collective-permute-start | bytes 196616 | tf_op jit(solution)/shard_map/ppermute | solution.py:35
  40.9 1.3 %collective-permute-start.18 = (f32[64,256]{1,0:T(8,128)S(1)}, f32[64,256]{1,0:T(8,128)S(1)}, u32[]{:S(2)}, u32[]{:S(2)}) collective-permute-start(f32[64,256]{1,0:T(8,128)S(1)} %collective-permute-done.17.refs_2_), channel_id=1, source_target_pairs={{0,1},{1,0},{2,3},{3,2},{4,5},{5,4},{6,7},{7,6},{8,9},{9,8},{10,11... | collective-permute-start | bytes 196616 | tf_op jit(solution)/shard_map/ppermute | solution.py:35
  41.4 1.3 %collective-permute-start.20 = (f32[64,256]{1,0:T(8,128)S(1)}, f32[64,256]{1,0:T(8,128)S(1)}, u32[]{:S(2)}, u32[]{:S(2)}) collective-permute-start(f32[64,256]{1,0:T(8,128)S(1)} %collective-permute-done.19.refs_4_), channel_id=1, source_target_pairs={{0,1},{1,0},{2,3},{3,2},{4,5},{5,4},{6,7},{7,6},{8,9},{9,8},{10,11... | collective-permute-start | bytes 196616 | tf_op jit(solution)/shard_map/ppermute | solution.py:35

commit v20 on v19

--- a/solution.py
+++ b/solution.py
@@ -330,7 +330,7 @@
 
     gram_got = swap(gram_send, "rows", 1)
     moved = pl.pallas_call(
-        functools.partial(permute_kernel, blocks_per_step(nblocks, 9), width),
+        functools.partial(permute_kernel, nblocks, width),
         out_shape=jax.ShapeDtypeStruct((nblocks, width, width), jnp.bfloat16),
         name="permute",
         **settings(8, 1.5),
@@ -343,7 +343,7 @@
 
     gram = add(gram_keep, gram_got)
     factors = pl.pallas_call(
-        functools.partial(weigh_kernel, blocks_per_step(nblocks, 9), width),
+        functools.partial(weigh_kernel, nblocks, width),
         out_shape=jax.ShapeDtypeStruct((2 * kinds, rows), jnp.bfloat16),
         name="weigh",
         **settings(8, 2.4),
@@ -379,7 +379,7 @@
         out_shape=jax.ShapeDtypeStruct((levels, 6 * rank, 2 * rank), jnp.bfloat16),
         scratch_shapes=[pltpu.VMEM((levels, 2 * rank, 2 * rank), jnp.float32), pltpu.SemaphoreType.DMA((levels,))],
         name="prepare",
-        **settings(8, 2),
+        **settings(8, 0.5),
     )(pltpu.with_memory_space_constraint(joined, pltpu.HBM), rank_perm, merged[0])
 
     def message_shape(level):
@@ -393,7 +393,7 @@
         functools.partial(solve_kernel, per_step, width),
         out_shape=floats(rows, columns),
         name="solve",
-        **settings(8, 1),
+        **settings(8, 0.1),
     )(moved, rhs, merged[0])
 
     own, other, rest = pl.pallas_call(

time: 47.1 us -> 47 us (level)
  Pallas kernels: 21.1 us -> 20.4 us
  starting transfers between devices: 22.4 us -> 23 us
    pallas_call x2, Pallas kernels: 2.64 us -> 1.91 us  [the longest x1 1.09 us: per_device(): pl.pallas_call(functools.partial(weigh_kernel, nblocks, width), out_shape...]
    ppermute x23, starting transfers between devices: 22.4 us -> 23 us  [swap(): return lax.ppermute(value, axis, [(i, i ^ mask) for i in range(count)])]
  transfers between devices with their start and end apart: 23 -> 23, of which waited for: 8 -> 6; matrix products, arithmetic and copies ran while one was open for 0% -> 0% of each run, Pallas kernels for 28% -> 27%
where the time goes in v20:
time: 47 us; the launch traced here: 46.8 us
  starting transfers between devices  23 us (49%)
  Pallas kernels  20.4 us (43%)
  waiting for transfers between devices  3.16 us (7%)
    ppermute x23, starting transfers between devices, swap(): return lax.ppermute(value, axis, [(i, i ^ mask) for i in range(count)])  23 us
    pallas_call x1, Pallas kernels, per_device(): pl.pallas_call(functools.partial(expand_kernel, levels, width, count), ou...  4.28 us
    pallas_call x2, Pallas kernels, project(): pl.pallas_call(functools.partial(project_kernel, other), out_shape=floats...  3.99 us
    pallas_call x1, Pallas kernels, per_device(): pl.pallas_call(functools.partial(gram_kernel, levels, per_step, width), i...  3.34 us
    ppermute x23, waiting for transfers between devices, swap(): return lax.ppermute(value, axis, [(i, i ^ mask) for i in range(count)])  3.16 us
    pallas_call x1, Pallas kernels, per_device(): pl.pallas_call(functools.partial(solve_kernel, per_step, width), out_shap...  2.22 us
    pallas_call x1, Pallas kernels, per_device(): pl.pallas_call(functools.partial(prepare_kernel, levels), in_specs=[pl.Bl...  1.68 us
    pallas_call x1, Pallas kernels, per_device(): pl.pallas_call(functools.partial(apply_kernel, per_step * width), out_sha...  1.58 us
  transfers between devices with their start and end apart: 23, of which 6 were waited for; matrix products, arithmetic and copies ran while one was open for 0% of the time, Pallas kernels for 27%

profile of v20, /device:TPU:0, one launch (start us, length us, event | category | flops | bytes accessed | tf_op | source)
XLA Modules:
  0.0 46.8 jit_solution(16629773921227750146)
XLA Ops:
  0.0 3.3 %gram.1 = (bf16[384,4608]{1,0:T(8,128)(2,1)S(1)}, f32[64,384]{1,0:T(8,128)S(1)}, f32[64,384]{1,0:T(8,128)S(1)}) custom-call(bf16[3,4608,128]{2,1,0:T(8,128)(2,1)} %right_ref.1, bf16[3,4608,128]{2,1,0:T(8,128)(2,1)} %refs_9_.1), custom_call_target="tpu_custom_call" | custom-call | flops 3300000000 | tf_op jit(solution)/shard_map/gram/pallas_call | solution.py:316
  3.4 0.5 %collective-permute-start = (f32[64,384]{1,0:T(8,128)S(1)}, f32[64,384]{1,0:T(8,128)S(1)}, u32[]{:S(2)}, u32[]{:S(2)}) collective-permute-start(f32[64,384]{1,0:T(8,128)S(1)} %get-tuple-element.19), channel_id=1, source_target_pairs={{0,1},{1,0},{2,3},{3,2},{4,5},{5,4},{6,7},{7,6},{8,9},{9,8},{10,11... | collective-permute-start | bytes 294920 | tf_op jit(solution)/shard_map/ppermute | solution.py:35
  3.9 0.0 copy-done.3
  3.9 0.0 copy-done.2
  3.9 0.8 %permute.1.moved_ref = bf16[18,256,256]{2,1,0:T(8,128)(2,1)S(1)} custom-call(s32[18,256]{1,0:T(8,128)S(1)} %copy-done.3, bf16[18,256,256]{2,1,0:T(8,128)(2,1)S(1)} %copy-done.2), custom_call_target="tpu_custom_call" | custom-call | flops 1650000000 | tf_op jit(solution)/shard_map/permute/pallas_call | solution.py:332
  4.7 0.1 collective-permute-done.got_ref
  4.8 2.9 %collective-permute-start.1 = (f32[64,384]{1,0:T(8,128)S(1)}, f32[64,384]{1,0:T(8,128)S(1)}, u32[]{:S(2)}, u32[]{:S(2)}) collective-permute-start(f32[64,384]{1,0:T(8,128)S(1)} %add.2.after_ref.mine_ref), channel_id=1, source_target_pairs={{0,2},{1,3},{2,0},{3,1},{4,6},{5,7},{6,4},{7,5},{8,10},{9,11},{10,... | collective-permute-start | bytes 294920 | tf_op jit(solution)/shard_map/ppermute | solution.py:35
  7.7 1.1 %weigh.1.factor_ref = bf16[768,4608]{1,0:T(8,128)(2,1)S(1)} custom-call(bf16[18,256,256]{2,1,0:T(8,128)(2,1)S(1)} %permute.1.moved_ref, bf16[384,4608]{1,0:T(8,128)(2,1)S(1)} %get-tuple-element.17.flip_ref, f32[64,384]{1,0:T(8,128)S(1)} %add.2.after_ref.mine_ref), custom_call_target="tpu_custom_call" | custom-call | flops 2640000000 | tf_op jit(solution)/shard_map/weigh/pallas_call | solution.py:345
  8.9 2.0 %project_other.1 = f32[384,256]{1,0:T(8,128)S(1)} custom-call(bf16[768,4608]{1,0:T(8,128)(2,1)S(1)} %weigh.1.factor_ref, bf16[4608,512]{1,0:T(8,128)(2,1)S(1)} %bitcast.1, f32[64,384]{1,0:T(8,128)S(1)} %add.2.after_ref.mine_ref), custom_call_target="tpu_custom_call" | custom-call | flops 1100000000 | tf_op jit(solution)/shard_map/project_other/pallas_call | solution.py:353
  10.9 0.1 collective-permute-start.2
  11.0 0.0 collective-permute-done.1.got_ref
  11.0 0.0 copy-start.1
  11.0 1.7 %collective-permute-start.10 = (f32[64,384]{1,0:T(8,128)S(1)}, f32[64,384]{1,0:T(8,128)S(1)}, u32[]{:S(2)}, u32[]{:S(2)}) collective-permute-start(f32[64,384]{1,0:T(8,128)S(1)} %add.3.after_ref.mine_ref), channel_id=1, source_target_pairs={{0,4},{1,5},{2,6},{3,7},{4,0},{5,1},{6,2},{7,3},{8,12},{9,13},{10,... | collective-permute-start | bytes 294920 | tf_op jit(solution)/shard_map/ppermute | solution.py:35
  12.7 2.0 %project_own.1.keep_ref = f32[384,256]{1,0:T(8,128)S(1)} custom-call(bf16[768,4608]{1,0:T(8,128)(2,1)S(1)} %weigh.1.factor_ref, bf16[4608,512]{1,0:T(8,128)(2,1)S(1)} %bitcast.1, f32[64,384]{1,0:T(8,128)S(1)} %add.3.after_ref.mine_ref), custom_call_target="tpu_custom_call" | custom-call | flops 4400000000 | tf_op jit(solution)/shard_map/project_own/pallas_call | solution.py:353
  14.7 0.0 collective-permute-done.2.got_ref
  14.7 0.2 merge.1
  14.9 1.6 %collective-permute-start.3 = (f32[64,384]{1,0:T(8,128)S(1)}, f32[64,384]{1,0:T(8,128)S(1)}, u32[]{:S(2)}, u32[]{:S(2)}) collective-permute-start(f32[64,384]{1,0:T(8,128)S(1)} %get-tuple-element.21), channel_id=1, source_target_pairs={{0,2},{1,3},{2,0},{3,1},{4,6},{5,7},{6,4},{7,5},{8,10},{9,11},{10,... | collective-permute-start | bytes 294920 | tf_op jit(solution)/shard_map/ppermute | solution.py:35
  16.5 0.5 %collective-permute-start.4 = (f32[64,384]{1,0:T(8,128)S(1)}, f32[64,384]{1,0:T(8,128)S(1)}, u32[]{:S(2)}, u32[]{:S(2)}) collective-permute-start(f32[64,384]{1,0:T(8,128)S(1)} %get-tuple-element.22), channel_id=1, source_target_pairs={{0,4},{1,5},{2,6},{3,7},{4,0},{5,1},{6,2},{7,3},{8,12},{9,13},{10,... | collective-permute-start | bytes 294920 | tf_op jit(solution)/shard_map/ppermute | solution.py:35
  17.0 1.5 %collective-permute-start.5 = (f32[64,384]{1,0:T(8,128)S(1)}, f32[64,384]{1,0:T(8,128)S(1)}, u32[]{:S(2)}, u32[]{:S(2)}) collective-permute-start(f32[64,384]{1,0:T(8,128)S(1)} %get-tuple-element.23), channel_id=1, source_target_pairs={{0,6},{1,7},{2,4},{3,5},{4,2},{5,3},{6,0},{7,1},{8,14},{9,15},{10,... | collective-permute-start | bytes 294920 | tf_op jit(solution)/shard_map/ppermute | solution.py:35
  18.5 0.0 collective-permute-start.11
  18.5 1.7 %prepare.1.refs_4_.after_ref.joined_ref = bf16[3,768,256]{2,1,0:T(8,128)(2,1)S(1)} custom-call(f32[7,256,256]{2,1,0:T(8,128)} %joined_ref.1, s32[3,128]{1,0:T(4,128)S(1)} %copy-done.1, f32[64,384]{1,0:T(8,128)S(1)} %get-tuple-element.20.refs_0_.after_ref), custom_call_target="tpu_custom_call" | custom-call | flops 550000000 | tf_op jit(solution)/shard_map/prepare/pallas_call | solution.py:376
  20.2 0.0 collective-permute-done.10.ref
  20.2 0.6 %collective-permute-start.12 = (f32[64,384]{1,0:T(8,128)S(1)}, f32[64,384]{1,0:T(8,128)S(1)}, u32[]{:S(2)}, u32[]{:S(2)}) collective-permute-start(f32[64,384]{1,0:T(8,128)S(1)} %relay.2.theirs_ref), channel_id=1, source_target_pairs={{0,1},{1,0},{2,3},{3,2},{4,5},{5,4},{6,7},{7,6},{8,9},{9,8},{10,11... | collective-permute-start | bytes 294920 | tf_op jit(solution)/shard_map/ppermute | solution.py:35
  20.8 2.2 %solve.1.after_ref.first_ref = f32[4608,512]{1,0:T(8,128)S(1)} custom-call(bf16[18,256,256]{2,1,0:T(8,128)(2,1)S(1)} %permute.1.moved_ref, bf16[4608,512]{1,0:T(8,128)(2,1)S(1)} %bitcast.1, f32[64,384]{1,0:T(8,128)S(1)} %get-tuple-element.20.refs_0_.after_ref), custom_call_target="tpu_custom_call" | custom-call | flops 110000000 | tf_op jit(solution)/shard_map/solve/pallas_call | solution.py:392
  23.0 0.0 collective-permute-done.3.refs_1_
  23.0 0.0 collective-permute-done.4.refs_2_
  23.0 0.0 collective-permute-done.5.refs_3_
  23.1 0.2 node.1
  23.3 0.0 collective-permute-done.11.pair_mine_ref
  23.3 0.0 collective-permute-done.12.pair_theirs_ref
  23.3 0.3 correct.1.sent_ref
  23.6 1.6 %collective-permute-start.13 = (f32[256,128]{1,0:T(8,128)S(1)}, f32[256,128]{1,0:T(8,128)S(1)}, u32[]{:S(2)}, u32[]{:S(2)}) collective-permute-start(f32[256,128]{1,0:T(8,128)S(1)} %correct.1.sent_ref), channel_id=1, source_target_pairs={{0,8},{8,0},{16,24},{24,16},{1,9},{9,1},{17,25},{25,17},{2,10},{10... | collective-permute-start | bytes 393224 | tf_op jit(solution)/shard_map/ppermute | solution.py:35
  25.2 1.5 %collective-permute-start.6 = (f32[64,128]{1,0:T(8,128)S(1)}, f32[64,128]{1,0:T(8,128)S(1)}, u32[]{:S(2)}, u32[]{:S(2)}) collective-permute-start(f32[64,128]{1,0:T(8,128)S(1)} %get-tuple-element.24.refs_0_.own_ref), channel_id=1, source_target_pairs={{0,2},{1,3},{2,0},{3,1},{4,6},{5,7},{6,4},{7,5},{8,10},{9,11},{10,... | collective-permute-start | bytes 98312 | tf_op jit(solution)/shard_map/ppermute | solution.py:35
  26.7 0.5 %collective-permute-start.7 = (f32[64,128]{1,0:T(8,128)S(1)}, f32[64,128]{1,0:T(8,128)S(1)}, u32[]{:S(2)}, u32[]{:S(2)}) collective-permute-start(f32[64,128]{1,0:T(8,128)S(1)} %get-tuple-element.25.other_ref), channel_id=1, source_target_pairs={{0,4},{1,5},{2,6},{3,7},{4,0},{5,1},{6,2},{7,3},{8,12},{9,13},{10,... | collective-permute-start | bytes 98312 | tf_op jit(solution)/shard_map/ppermute | solution.py:35
  27.2 1.5 %collective-permute-start.8 = (f32[64,128]{1,0:T(8,128)S(1)}, f32[64,128]{1,0:T(8,128)S(1)}, u32[]{:S(2)}, u32[]{:S(2)}) collective-permute-start(f32[64,128]{1,0:T(8,128)S(1)} %get-tuple-element.25.other_ref), channel_id=1, source_target_pairs={{0,6},{1,7},{2,4},{3,5},{4,2},{5,3},{6,0},{7,1},{8,14},{9,15},{10,... | collective-permute-start | bytes 98312 | tf_op jit(solution)/shard_map/ppermute | solution.py:35
  28.7 0.4 collective-permute-done.13.got_ref.after_ref
  29.1 0.4 level1.1
  29.5 2.7 %collective-permute-start.15 = (f32[64,128]{1,0:T(8,128)S(1)}, f32[64,128]{1,0:T(8,128)S(1)}, u32[]{:S(2)}, u32[]{:S(2)}) collective-permute-start(f32[64,128]{1,0:T(8,128)S(1)} %get-tuple-element.28.sent_ref), channel_id=1, source_target_pairs={{0,16},{8,24},{16,0},{24,8},{1,17},{9,25},{17,1},{25,9},{2,18},{10... | collective-permute-start | bytes 98312 | tf_op jit(solution)/shard_map/ppermute | solution.py:35
  32.1 0.0 collective-permute-done.6.refs_1_
  32.1 0.0 collective-permute-done.7.refs_2_
  32.1 0.0 collective-permute-done.8.refs_3_
  32.2 0.0 copy-start
  32.2 0.1 collective-permute-start.9
  32.3 1.5 %collective-permute-start.14 = (f32[64,128]{1,0:T(8,128)S(1)}, f32[64,128]{1,0:T(8,128)S(1)}, u32[]{:S(2)}, u32[]{:S(2)}) collective-permute-start(f32[64,128]{1,0:T(8,128)S(1)} %get-tuple-element.27.refs_0_), channel_id=1, source_target_pairs={{0,6},{1,7},{2,4},{3,5},{4,2},{5,3},{6,0},{7,1},{8,14},{9,15},{10,... | collective-permute-start | bytes 98312 | tf_op jit(solution)/shard_map/ppermute | solution.py:35
  33.8 0.6 %collective-permute-done.15.got_ref.after_ref = f32[64,128]{1,0:T(8,128)S(1)} collective-permute-done((f32[64,128]{1,0:T(8,128)S(1)}, f32[64,128]{1,0:T(8,128)S(1)}, u32[]{:S(2)}, u32[]{:S(2)}) %collective-permute-start.15) | collective-permute-done | bytes 32800 | tf_op jit(solution)/shard_map/ppermute | solution.py:35
  34.4 0.2 level2.1.refs_1_
  34.6 1.5 %collective-permute-start.21 = (f32[64,128]{1,0:T(8,128)S(1)}, f32[64,128]{1,0:T(8,128)S(1)}, u32[]{:S(2)}, u32[]{:S(2)}) collective-permute-start(f32[64,128]{1,0:T(8,128)S(1)} %level2.1.refs_1_), channel_id=1, source_target_pairs={{0,6},{1,7},{2,4},{3,5},{4,2},{5,3},{6,0},{7,1},{8,14},{9,15},{10,... | collective-permute-start | bytes 98312 | tf_op jit(solution)/shard_map/ppermute | solution.py:35
  36.1 0.9 %collective-permute-start.17 = (f32[64,256]{1,0:T(8,128)S(1)}, f32[64,256]{1,0:T(8,128)S(1)}, u32[]{:S(2)}, u32[]{:S(2)}) collective-permute-start(f32[64,256]{1,0:T(8,128)S(1)} %pack.1.ref), channel_id=1, source_target_pairs={{0,2},{1,3},{2,0},{3,1},{4,6},{5,7},{6,4},{7,5},{8,10},{9,11},{10,... | collective-permute-start | bytes 196616 | tf_op jit(solution)/shard_map/ppermute | solution.py:35
  37.0 1.1 %collective-permute-start.19 = (f32[64,256]{1,0:T(8,128)S(1)}, f32[64,256]{1,0:T(8,128)S(1)}, u32[]{:S(2)}, u32[]{:S(2)}) collective-permute-start(f32[64,256]{1,0:T(8,128)S(1)} %pack.1.ref), channel_id=1, source_target_pairs={{0,4},{1,5},{2,6},{3,7},{4,0},{5,1},{6,2},{7,3},{8,12},{9,13},{10,... | collective-permute-start | bytes 196616 | tf_op jit(solution)/shard_map/ppermute | solution.py:35
  38.1 0.0 collective-permute-done.14.after_ref.refs_0_
  38.1 0.0 collective-permute-done.9.pair_ref
  38.1 1.6 %apply.1.after_ref.refs_8_ = f32[4608,512]{1,0:T(8,128)S(1)} custom-call(f32[4,64,128]{2,1,0:T(8,128)S(1)} %stack.1.own_ref, f32[4,64,128]{2,1,0:T(8,128)S(1)} %collective-permute-done.9.pair_ref, f32[4608,512]{1,0:T(8,128)S(1)} %solve.1.after_ref.first_ref, bf16[3,4608,128]{2,1,0:T(8,128)(2,1)S(1)} %copy-done, ...), custom_call_target="tpu_custom_call" | custom-call | flops 1980000000 | tf_op jit(solution)/shard_map/apply/pallas_call | solution.py:429
  39.7 0.1 collective-permute-start.16
  39.8 0.0 collective-permute-done.21.refs_1_
  39.8 0.5 %collective-permute-start.22 = (f32[64,256]{1,0:T(8,128)S(1)}, f32[64,256]{1,0:T(8,128)S(1)}, u32[]{:S(2)}, u32[]{:S(2)}) collective-permute-start(f32[64,256]{1,0:T(8,128)S(1)} %join.1.refs_6_), channel_id=1, source_target_pairs={{0,1},{1,0},{2,3},{3,2},{4,5},{5,4},{6,7},{7,6},{8,9},{9,8},{10,11... | collective-permute-start | bytes 196616 | tf_op jit(solution)/shard_map/ppermute | solution.py:35
  40.4 0.0 collective-permute-done.17.refs_2_
  40.4 0.1 collective-permute-start.18
  40.5 0.8 %collective-permute-done.19.refs_4_ = f32[64,256]{1,0:T(8,128)S(1)} collective-permute-done((f32[64,256]{1,0:T(8,128)S(1)}, f32[64,256]{1,0:T(8,128)S(1)}, u32[]{:S(2)}, u32[]{:S(2)}) %collective-permute-start.19) | collective-permute-done | bytes 65568 | tf_op jit(solution)/shard_map/ppermute | solution.py:35
  41.3 0.0 collective-permute-start.20
  41.3 0.0 collective-permute-done.16.refs_1_
  41.3 0.0 collective-permute-done.22.refs_7_
  41.3 0.4 collective-permute-done.18.refs_3_
  41.6 0.9 %collective-permute-done.20.refs_5_ = f32[64,256]{1,0:T(8,128)S(1)} collective-permute-done((f32[64,256]{1,0:T(8,128)S(1)}, f32[64,256]{1,0:T(8,128)S(1)}, u32[]{:S(2)}, u32[]{:S(2)}) %collective-permute-start.20) | collective-permute-done | bytes 65568 | tf_op jit(solution)/shard_map/ppermute | solution.py:35
  42.5 4.3 %expand.1 = f32[4608,512]{1,0:T(8,128)} custom-call(f32[64,256]{1,0:T(8,128)S(1)} %relay.3.refs_0_, f32[64,256]{1,0:T(8,128)S(1)} %collective-permute-done.16.refs_1_, f32[64,256]{1,0:T(8,128)S(1)} %collective-permute-done.17.refs_2_, f32[64,256]{1,0:T(8,128)S(1)} %collective-permute-done.18.refs_3_, f32[64,256]{1,0:T(8,128)S(1)} %collective-permute-done.19.refs_4_, ...), custom_call_target="tpu_custom_call" | custom-call | flops 5500000256 | tf_op jit(solution)/shard_map/expand/pallas_call | solution.py:456
  (16 shorter events, 0.1 us)
Async XLA Ops:
  0.0 3.9 %copy-start.3 = (s32[18,256]{1,0:T(8,128)S(1)}, s32[18,256]{1,0:T(8,128)}, u32[]{:S(2)}) copy-start(s32[18,256]{1,0:T(8,128)} %order_ref.1) | copy-start | bytes 55300
  0.0 3.9 %copy-start.2 = (bf16[18,256,256]{2,1,0:T(8,128)(2,1)S(1)}, bf16[18,256,256]{2,1,0:T(8,128)(2,1)}, u32[]{:S(2)}) copy-start(bf16[18,256,256]{2,1,0:T(8,128)(2,1)} %inv_ref.1) | copy-start | bytes 7077892
  3.4 1.5 %collective-permute-start = (f32[64,384]{1,0:T(8,128)S(1)}, f32[64,384]{1,0:T(8,128)S(1)}, u32[]{:S(2)}, u32[]{:S(2)}) collective-permute-start(f32[64,384]{1,0:T(8,128)S(1)} %get-tuple-element.19), channel_id=1, source_target_pairs={{0,1},{1,0},{2,3},{3,2},{4,5},{5,4},{6,7},{7,6},{8,9},{9,8},{10,11... | collective-permute-start | bytes 294920 | tf_op jit(solution)/shard_map/ppermute | solution.py:35
  4.8 4.0 %slice-start = ((s8[4718592]{0:T(1024)(128)(4,1)}), s8[4194304]{0:T(1024)(128)(4,1)S(1)}, s32[]{:S(2)}) async-start(s8[4718592]{0:T(1024)(128)(4,1)} %bitcast), calls=%async_computation | async-start | bytes 8388608
  4.8 6.1 %collective-permute-start.1 = (f32[64,384]{1,0:T(8,128)S(1)}, f32[64,384]{1,0:T(8,128)S(1)}, u32[]{:S(2)}, u32[]{:S(2)}) collective-permute-start(f32[64,384]{1,0:T(8,128)S(1)} %add.2.after_ref.mine_ref), channel_id=1, source_target_pairs={{0,2},{1,3},{2,0},{3,1},{4,6},{5,7},{6,4},{7,5},{8,10},{9,11},{10,... | collective-permute-start | bytes 294920 | tf_op jit(solution)/shard_map/ppermute | solution.py:35
  7.7 1.1 %slice-start.1 = ((s8[4718592]{0:T(1024)(128)(4,1)}), s8[524288]{0:T(1024)(128)(4,1)S(1)}, s32[]{:S(2)}) async-start(s8[4718592]{0:T(1024)(128)(4,1)} %bitcast), calls=%async_computation.1 | async-start | bytes 1048576
  10.9 3.8 %collective-permute-start.2 = (f32[384,256]{1,0:T(8,128)S(1)}, f32[384,256]{1,0:T(8,128)S(1)}, u32[]{:S(2)}, u32[]{:S(2)}) collective-permute-start(f32[384,256]{1,0:T(8,128)S(1)} %project_other.1), channel_id=1, source_target_pairs={{0,1},{1,0},{2,3},{3,2},{4,5},{5,4},{6,7},{7,6},{8,9},{9,8},{10,11... | collective-permute-start | bytes 1179656 | tf_op jit(solution)/shard_map/ppermute | solution.py:35
  11.0 7.5 %copy-start.1 = (s32[3,128]{1,0:T(4,128)S(1)}, s32[3,128]{1,0:T(4,128)}, u32[]{:S(2)}) copy-start(s32[3,128]{1,0:T(4,128)} %perm_ref.1) | copy-start | bytes 4612
  11.0 9.2 %collective-permute-start.10 = (f32[64,384]{1,0:T(8,128)S(1)}, f32[64,384]{1,0:T(8,128)S(1)}, u32[]{:S(2)}, u32[]{:S(2)}) collective-permute-start(f32[64,384]{1,0:T(8,128)S(1)} %add.3.after_ref.mine_ref), channel_id=1, source_target_pairs={{0,4},{1,5},{2,6},{3,7},{4,0},{5,1},{6,2},{7,3},{8,12},{9,13},{10,... | collective-permute-start | bytes 294920 | tf_op jit(solution)/shard_map/ppermute | solution.py:35
  14.9 8.1 %collective-permute-start.3 = (f32[64,384]{1,0:T(8,128)S(1)}, f32[64,384]{1,0:T(8,128)S(1)}, u32[]{:S(2)}, u32[]{:S(2)}) collective-permute-start(f32[64,384]{1,0:T(8,128)S(1)} %get-tuple-element.21), channel_id=1, source_target_pairs={{0,2},{1,3},{2,0},{3,1},{4,6},{5,7},{6,4},{7,5},{8,10},{9,11},{10,... | collective-permute-start | bytes 294920 | tf_op jit(solution)/shard_map/ppermute | solution.py:35
  16.5 6.5 %collective-permute-start.4 = (f32[64,384]{1,0:T(8,128)S(1)}, f32[64,384]{1,0:T(8,128)S(1)}, u32[]{:S(2)}, u32[]{:S(2)}) collective-permute-start(f32[64,384]{1,0:T(8,128)S(1)} %get-tuple-element.22), channel_id=1, source_target_pairs={{0,4},{1,5},{2,6},{3,7},{4,0},{5,1},{6,2},{7,3},{8,12},{9,13},{10,... | collective-permute-start | bytes 294920 | tf_op jit(solution)/shard_map/ppermute | solution.py:35
  17.0 6.0 %collective-permute-start.5 = (f32[64,384]{1,0:T(8,128)S(1)}, f32[64,384]{1,0:T(8,128)S(1)}, u32[]{:S(2)}, u32[]{:S(2)}) collective-permute-start(f32[64,384]{1,0:T(8,128)S(1)} %get-tuple-element.23), channel_id=1, source_target_pairs={{0,6},{1,7},{2,4},{3,5},{4,2},{5,3},{6,0},{7,1},{8,14},{9,15},{10,... | collective-permute-start | bytes 294920 | tf_op jit(solution)/shard_map/ppermute | solution.py:35
  18.5 4.8 %collective-permute-start.11 = (f32[64,384]{1,0:T(8,128)S(1)}, f32[64,384]{1,0:T(8,128)S(1)}, u32[]{:S(2)}, u32[]{:S(2)}) collective-permute-start(f32[64,384]{1,0:T(8,128)S(1)} %add.3.after_ref.mine_ref), channel_id=1, source_target_pairs={{0,1},{1,0},{2,3},{3,2},{4,5},{5,4},{6,7},{7,6},{8,9},{9,8},{10,11... | collective-permute-start | bytes 294920 | tf_op jit(solution)/shard_map/ppermute | solution.py:35
  20.2 3.0 %collective-permute-start.12 = (f32[64,384]{1,0:T(8,128)S(1)}, f32[64,384]{1,0:T(8,128)S(1)}, u32[]{:S(2)}, u32[]{:S(2)}) collective-permute-start(f32[64,384]{1,0:T(8,128)S(1)} %relay.2.theirs_ref), channel_id=1, source_target_pairs={{0,1},{1,0},{2,3},{3,2},{4,5},{5,4},{6,7},{7,6},{8,9},{9,8},{10,11... | collective-permute-start | bytes 294920 | tf_op jit(solution)/shard_map/ppermute | solution.py:35
  23.6 5.5 %collective-permute-start.13 = (f32[256,128]{1,0:T(8,128)S(1)}, f32[256,128]{1,0:T(8,128)S(1)}, u32[]{:S(2)}, u32[]{:S(2)}) collective-permute-start(f32[256,128]{1,0:T(8,128)S(1)} %correct.1.sent_ref), channel_id=1, source_target_pairs={{0,8},{8,0},{16,24},{24,16},{1,9},{9,1},{17,25},{25,17},{2,10},{10... | collective-permute-start | bytes 393224 | tf_op jit(solution)/shard_map/ppermute | solution.py:35
  25.2 6.9 %collective-permute-start.6 = (f32[64,128]{1,0:T(8,128)S(1)}, f32[64,128]{1,0:T(8,128)S(1)}, u32[]{:S(2)}, u32[]{:S(2)}) collective-permute-start(f32[64,128]{1,0:T(8,128)S(1)} %get-tuple-element.24.refs_0_.own_ref), channel_id=1, source_target_pairs={{0,2},{1,3},{2,0},{3,1},{4,6},{5,7},{6,4},{7,5},{8,10},{9,11},{10,... | collective-permute-start | bytes 98312 | tf_op jit(solution)/shard_map/ppermute | solution.py:35
  26.7 5.4 %collective-permute-start.7 = (f32[64,128]{1,0:T(8,128)S(1)}, f32[64,128]{1,0:T(8,128)S(1)}, u32[]{:S(2)}, u32[]{:S(2)}) collective-permute-start(f32[64,128]{1,0:T(8,128)S(1)} %get-tuple-element.25.other_ref), channel_id=1, source_target_pairs={{0,4},{1,5},{2,6},{3,7},{4,0},{5,1},{6,2},{7,3},{8,12},{9,13},{10,... | collective-permute-start | bytes 98312 | tf_op jit(solution)/shard_map/ppermute | solution.py:35
  27.2 4.9 %collective-permute-start.8 = (f32[64,128]{1,0:T(8,128)S(1)}, f32[64,128]{1,0:T(8,128)S(1)}, u32[]{:S(2)}, u32[]{:S(2)}) collective-permute-start(f32[64,128]{1,0:T(8,128)S(1)} %get-tuple-element.25.other_ref), channel_id=1, source_target_pairs={{0,6},{1,7},{2,4},{3,5},{4,2},{5,3},{6,0},{7,1},{8,14},{9,15},{10,... | collective-permute-start | bytes 98312 | tf_op jit(solution)/shard_map/ppermute | solution.py:35
  29.5 4.9 %collective-permute-start.15 = (f32[64,128]{1,0:T(8,128)S(1)}, f32[64,128]{1,0:T(8,128)S(1)}, u32[]{:S(2)}, u32[]{:S(2)}) collective-permute-start(f32[64,128]{1,0:T(8,128)S(1)} %get-tuple-element.28.sent_ref), channel_id=1, source_target_pairs={{0,16},{8,24},{16,0},{24,8},{1,17},{9,25},{17,1},{25,9},{2,18},{10... | collective-permute-start | bytes 98312 | tf_op jit(solution)/shard_map/ppermute | solution.py:35
  32.2 6.0 %copy-start = (bf16[3,4608,128]{2,1,0:T(8,128)(2,1)S(1)}, bf16[3,4608,128]{2,1,0:T(8,128)(2,1)}, u32[]{:S(2)}) copy-start(bf16[3,4608,128]{2,1,0:T(8,128)(2,1)} %refs_9_.1) | copy-start | bytes 10616836
  32.2 5.9 %collective-permute-start.9 = (f32[4,64,128]{2,1,0:T(8,128)S(1)}, f32[4,64,128]{2,1,0:T(8,128)S(1)}, u32[]{:S(2)}, u32[]{:S(2)}) collective-permute-start(f32[4,64,128]{2,1,0:T(8,128)S(1)} %stack.1.own_ref), channel_id=1, source_target_pairs={{0,1},{1,0},{2,3},{3,2},{4,5},{5,4},{6,7},{7,6},{8,9},{9,8},{10,11... | collective-permute-start | bytes 393224 | tf_op jit(solution)/shard_map/ppermute | solution.py:35
  32.3 5.9 %collective-permute-start.14 = (f32[64,128]{1,0:T(8,128)S(1)}, f32[64,128]{1,0:T(8,128)S(1)}, u32[]{:S(2)}, u32[]{:S(2)}) collective-permute-start(f32[64,128]{1,0:T(8,128)S(1)} %get-tuple-element.27.refs_0_), channel_id=1, source_target_pairs={{0,6},{1,7},{2,4},{3,5},{4,2},{5,3},{6,0},{7,1},{8,14},{9,15},{10,... | collective-permute-start | bytes 98312 | tf_op jit(solution)/shard_map/ppermute | solution.py:35
  34.6 5.3 %collective-permute-start.21 = (f32[64,128]{1,0:T(8,128)S(1)}, f32[64,128]{1,0:T(8,128)S(1)}, u32[]{:S(2)}, u32[]{:S(2)}) collective-permute-start(f32[64,128]{1,0:T(8,128)S(1)} %level2.1.refs_1_), channel_id=1, source_target_pairs={{0,6},{1,7},{2,4},{3,5},{4,2},{5,3},{6,0},{7,1},{8,14},{9,15},{10,... | collective-permute-start | bytes 98312 | tf_op jit(solution)/shard_map/ppermute | solution.py:35
  36.1 4.3 %collective-permute-start.17 = (f32[64,256]{1,0:T(8,128)S(1)}, f32[64,256]{1,0:T(8,128)S(1)}, u32[]{:S(2)}, u32[]{:S(2)}) collective-permute-start(f32[64,256]{1,0:T(8,128)S(1)} %pack.1.ref), channel_id=1, source_target_pairs={{0,2},{1,3},{2,0},{3,1},{4,6},{5,7},{6,4},{7,5},{8,10},{9,11},{10,... | collective-permute-start | bytes 196616 | tf_op jit(solution)/shard_map/ppermute | solution.py:35
  37.0 4.3 %collective-permute-start.19 = (f32[64,256]{1,0:T(8,128)S(1)}, f32[64,256]{1,0:T(8,128)S(1)}, u32[]{:S(2)}, u32[]{:S(2)}) collective-permute-start(f32[64,256]{1,0:T(8,128)S(1)} %pack.1.ref), channel_id=1, source_target_pairs={{0,4},{1,5},{2,6},{3,7},{4,0},{5,1},{6,2},{7,3},{8,12},{9,13},{10,... | collective-permute-start | bytes 196616 | tf_op jit(solution)/shard_map/ppermute | solution.py:35
  39.7 1.6 %collective-permute-start.16 = (f32[64,256]{1,0:T(8,128)S(1)}, f32[64,256]{1,0:T(8,128)S(1)}, u32[]{:S(2)}, u32[]{:S(2)}) collective-permute-start(f32[64,256]{1,0:T(8,128)S(1)} %relay.3.refs_0_), channel_id=1, source_target_pairs={{0,1},{1,0},{2,3},{3,2},{4,5},{5,4},{6,7},{7,6},{8,9},{9,8},{10,11... | collective-permute-start | bytes 196616 | tf_op jit(solution)/shard_map/ppermute | solution.py:35
  39.8 1.5 %collective-permute-start.22 = (f32[64,256]{1,0:T(8,128)S(1)}, f32[64,256]{1,0:T(8,128)S(1)}, u32[]{:S(2)}, u32[]{:S(2)}) collective-permute-start(f32[64,256]{1,0:T(8,128)S(1)} %join.1.refs_6_), channel_id=1, source_target_pairs={{0,1},{1,0},{2,3},{3,2},{4,5},{5,4},{6,7},{7,6},{8,9},{9,8},{10,11... | collective-permute-start | bytes 196616 | tf_op jit(solution)/shard_map/ppermute | solution.py:35
  40.4 1.3 %collective-permute-start.18 = (f32[64,256]{1,0:T(8,128)S(1)}, f32[64,256]{1,0:T(8,128)S(1)}, u32[]{:S(2)}, u32[]{:S(2)}) collective-permute-start(f32[64,256]{1,0:T(8,128)S(1)} %collective-permute-done.17.refs_2_), channel_id=1, source_target_pairs={{0,1},{1,0},{2,3},{3,2},{4,5},{5,4},{6,7},{7,6},{8,9},{9,8},{10,11... | collective-permute-start | bytes 196616 | tf_op jit(solution)/shard_map/ppermute | solution.py:35
  41.3 1.3 %collective-permute-start.20 = (f32[64,256]{1,0:T(8,128)S(1)}, f32[64,256]{1,0:T(8,128)S(1)}, u32[]{:S(2)}, u32[]{:S(2)}) collective-permute-start(f32[64,256]{1,0:T(8,128)S(1)} %collective-permute-done.19.refs_4_), channel_id=1, source_target_pairs={{0,1},{1,0},{2,3},{3,2},{4,5},{5,4},{6,7},{7,6},{8,9},{9,8},{10,11... | collective-permute-start | bytes 196616 | tf_op jit(solution)/shard_map/ppermute | solution.py:35

commit v21 on v16

--- a/solution.py
+++ b/solution.py
@@ -324,7 +324,7 @@
 
     gram_got = swap(gram_send, "rows", 1)
     moved = pl.pallas_call(
-        functools.partial(permute_kernel, blocks_per_step(nblocks, 9), width),
+        functools.partial(permute_kernel, nblocks, width),
         out_shape=jax.ShapeDtypeStruct((nblocks, width, width), jnp.bfloat16),
         name="permute",
         **settings(8, 1.5),
@@ -337,7 +337,7 @@
 
     gram = add(gram_keep, gram_got)
     factors = pl.pallas_call(
-        functools.partial(weigh_kernel, blocks_per_step(nblocks, 9), width),
+        functools.partial(weigh_kernel, nblocks, width),
         out_shape=jax.ShapeDtypeStruct((2 * kinds, rows), jnp.bfloat16),
         name="weigh",
         **settings(8, 2.4),

time: 47 us -> 46.8 us (level)
  Pallas kernels: 21.1 us -> 20.3 us
    pallas_call x2, Pallas kernels: 2.64 us -> 1.91 us  [the longest x1 1.09 us: per_device(): pl.pallas_call(functools.partial(weigh_kernel, nblocks, width), out_shape...]
  transfers between devices with their start and end apart: 22 -> 22, of which waited for: 7 -> 8; matrix products, arithmetic and copies ran while one was open for 0% -> 0% of each run, Pallas kernels for 28% -> 27%
where the time goes in v21:
time: 46.8 us; the launch traced here: 46.7 us
  starting transfers between devices  21 us (45%)
  Pallas kernels  20.3 us (43%)
  waiting for transfers between devices  5.08 us (11%)
    ppermute x22, starting transfers between devices, swap(): return lax.ppermute(value, axis, [(i, i ^ mask) for i in range(count)])  21 us
    ppermute x22, waiting for transfers between devices, swap(): return lax.ppermute(value, axis, [(i, i ^ mask) for i in range(count)])  5.08 us
    pallas_call x1, Pallas kernels, per_device(): pl.pallas_call(functools.partial(expand_kernel, levels, width, count), ou...  4.28 us
    pallas_call x2, Pallas kernels, project(): pl.pallas_call(functools.partial(project_kernel, other), out_shape=floats...  3.99 us
    pallas_call x1, Pallas kernels, per_device(): pl.pallas_call(functools.partial(gram_kernel, levels, per_step, width), i...  3.34 us
    pallas_call x1, Pallas kernels, per_device(): pl.pallas_call(functools.partial(solve_kernel, per_step, width), out_shap...  2.22 us
    pallas_call x1, Pallas kernels, per_device(): pl.pallas_call(functools.partial(prepare_kernel, levels), in_specs=[pl.Bl...  1.69 us
    pallas_call x1, Pallas kernels, per_device(): pl.pallas_call(functools.partial(apply_kernel, per_step * width), out_sha...  1.57 us
  transfers between devices with their start and end apart: 22, of which 8 were waited for; matrix products, arithmetic and copies ran while one was open for 0% of the time, Pallas kernels for 27%

profile of v21, /device:TPU:0, one launch (start us, length us, event | category | flops | bytes accessed | tf_op | source)
XLA Modules:
  0.0 46.7 jit_solution(14653364373625900224)
XLA Ops:
  0.0 3.3 %gram.1 = (bf16[384,4608]{1,0:T(8,128)(2,1)S(1)}, f32[64,384]{1,0:T(8,128)S(1)}, f32[64,384]{1,0:T(8,128)S(1)}) custom-call(bf16[3,4608,128]{2,1,0:T(8,128)(2,1)} %right_ref.1, bf16[3,4608,128]{2,1,0:T(8,128)(2,1)} %refs_9_.1), custom_call_target="tpu_custom_call" | custom-call | flops 3300000000 | tf_op jit(solution)/shard_map/gram/pallas_call | solution.py:310
  3.4 0.5 %collective-permute-start = (f32[64,384]{1,0:T(8,128)S(1)}, f32[64,384]{1,0:T(8,128)S(1)}, u32[]{:S(2)}, u32[]{:S(2)}) collective-permute-start(f32[64,384]{1,0:T(8,128)S(1)} %get-tuple-element.19), channel_id=1, source_target_pairs={{0,1},{1,0},{2,3},{3,2},{4,5},{5,4},{6,7},{7,6},{8,9},{9,8},{10,11... | collective-permute-start | bytes 294920 | tf_op jit(solution)/shard_map/ppermute | solution.py:35
  3.9 0.0 copy-done.2
  3.9 0.0 copy-done.1
  3.9 0.8 %permute.1.moved_ref = bf16[18,256,256]{2,1,0:T(8,128)(2,1)S(1)} custom-call(s32[18,256]{1,0:T(8,128)S(1)} %copy-done.2, bf16[18,256,256]{2,1,0:T(8,128)(2,1)S(1)} %copy-done.1), custom_call_target="tpu_custom_call" | custom-call | flops 1650000000 | tf_op jit(solution)/shard_map/permute/pallas_call | solution.py:326
  4.7 0.1 collective-permute-done.got_ref
  4.8 2.9 %collective-permute-start.1 = (f32[64,384]{1,0:T(8,128)S(1)}, f32[64,384]{1,0:T(8,128)S(1)}, u32[]{:S(2)}, u32[]{:S(2)}) collective-permute-start(f32[64,384]{1,0:T(8,128)S(1)} %add.2.after_ref.mine_ref), channel_id=1, source_target_pairs={{0,2},{1,3},{2,0},{3,1},{4,6},{5,7},{6,4},{7,5},{8,10},{9,11},{10,... | collective-permute-start | bytes 294920 | tf_op jit(solution)/shard_map/ppermute | solution.py:35
  7.7 1.1 %weigh.1.factor_ref = bf16[768,4608]{1,0:T(8,128)(2,1)S(1)} custom-call(bf16[18,256,256]{2,1,0:T(8,128)(2,1)S(1)} %permute.1.moved_ref, bf16[384,4608]{1,0:T(8,128)(2,1)S(1)} %get-tuple-element.17.flip_ref, f32[64,384]{1,0:T(8,128)S(1)} %add.2.after_ref.mine_ref), custom_call_target="tpu_custom_call" | custom-call | flops 2640000000 | tf_op jit(solution)/shard_map/weigh/pallas_call | solution.py:339
  8.9 2.0 %project_other.1 = f32[384,256]{1,0:T(8,128)S(1)} custom-call(bf16[768,4608]{1,0:T(8,128)(2,1)S(1)} %weigh.1.factor_ref, bf16[4608,512]{1,0:T(8,128)(2,1)S(1)} %bitcast.1, f32[64,384]{1,0:T(8,128)S(1)} %add.2.after_ref.mine_ref), custom_call_target="tpu_custom_call" | custom-call | flops 1100000000 | tf_op jit(solution)/shard_map/project_other/pallas_call | solution.py:347
  10.9 0.1 collective-permute-start.2
  11.0 0.0 collective-permute-done.1.got_ref
  11.0 0.0 copy-start.3
  11.0 1.7 %collective-permute-start.10 = (f32[64,384]{1,0:T(8,128)S(1)}, f32[64,384]{1,0:T(8,128)S(1)}, u32[]{:S(2)}, u32[]{:S(2)}) collective-permute-start(f32[64,384]{1,0:T(8,128)S(1)} %add.3.after_ref.mine_ref), channel_id=1, source_target_pairs={{0,4},{1,5},{2,6},{3,7},{4,0},{5,1},{6,2},{7,3},{8,12},{9,13},{10,... | collective-permute-start | bytes 294920 | tf_op jit(solution)/shard_map/ppermute | solution.py:35
  12.7 2.0 %project_own.1.keep_ref = f32[384,256]{1,0:T(8,128)S(1)} custom-call(bf16[768,4608]{1,0:T(8,128)(2,1)S(1)} %weigh.1.factor_ref, bf16[4608,512]{1,0:T(8,128)(2,1)S(1)} %bitcast.1, f32[64,384]{1,0:T(8,128)S(1)} %add.3.after_ref.mine_ref), custom_call_target="tpu_custom_call" | custom-call | flops 4400000000 | tf_op jit(solution)/shard_map/project_own/pallas_call | solution.py:347
  14.7 0.0 collective-permute-done.2.got_ref
  14.7 0.2 merge.1
  14.9 1.6 %collective-permute-start.3 = (f32[64,384]{1,0:T(8,128)S(1)}, f32[64,384]{1,0:T(8,128)S(1)}, u32[]{:S(2)}, u32[]{:S(2)}) collective-permute-start(f32[64,384]{1,0:T(8,128)S(1)} %get-tuple-element.21), channel_id=1, source_target_pairs={{0,2},{1,3},{2,0},{3,1},{4,6},{5,7},{6,4},{7,5},{8,10},{9,11},{10,... | collective-permute-start | bytes 294920 | tf_op jit(solution)/shard_map/ppermute | solution.py:35
  16.5 0.5 %collective-permute-start.4 = (f32[64,384]{1,0:T(8,128)S(1)}, f32[64,384]{1,0:T(8,128)S(1)}, u32[]{:S(2)}, u32[]{:S(2)}) collective-permute-start(f32[64,384]{1,0:T(8,128)S(1)} %get-tuple-element.22), channel_id=1, source_target_pairs={{0,4},{1,5},{2,6},{3,7},{4,0},{5,1},{6,2},{7,3},{8,12},{9,13},{10,... | collective-permute-start | bytes 294920 | tf_op jit(solution)/shard_map/ppermute | solution.py:35
  17.0 1.5 %collective-permute-start.5 = (f32[64,384]{1,0:T(8,128)S(1)}, f32[64,384]{1,0:T(8,128)S(1)}, u32[]{:S(2)}, u32[]{:S(2)}) collective-permute-start(f32[64,384]{1,0:T(8,128)S(1)} %get-tuple-element.23), channel_id=1, source_target_pairs={{0,6},{1,7},{2,4},{3,5},{4,2},{5,3},{6,0},{7,1},{8,14},{9,15},{10,... | collective-permute-start | bytes 294920 | tf_op jit(solution)/shard_map/ppermute | solution.py:35
  18.5 0.0 copy-done.3
  18.5 1.7 %prepare.1.refs_4_.joined_ref = bf16[3,768,256]{2,1,0:T(8,128)(2,1)S(1)} custom-call(f32[7,256,256]{2,1,0:T(8,128)} %joined_ref.1, s32[3,128]{1,0:T(4,128)S(1)} %copy-done.3), custom_call_target="tpu_custom_call" | custom-call | flops 2200000000 | tf_op jit(solution)/shard_map/prepare/pallas_call | solution.py:371
  20.2 0.1 collective-permute-start.11
  20.3 0.0 collective-permute-done.10.theirs_ref
  20.3 0.5 %collective-permute-start.12 = (f32[64,384]{1,0:T(8,128)S(1)}, f32[64,384]{1,0:T(8,128)S(1)}, u32[]{:S(2)}, u32[]{:S(2)}) collective-permute-start(f32[64,384]{1,0:T(8,128)S(1)} %collective-permute-done.10.theirs_ref), channel_id=1, source_target_pairs={{0,1},{1,0},{2,3},{3,2},{4,5},{5,4},{6,7},{7,6},{8,9},{9,8},{10,11... | collective-permute-start | bytes 294920 | tf_op jit(solution)/shard_map/ppermute | solution.py:35
  20.8 0.0 collective-permute-done.3.refs_1_
  20.8 2.1 %collective-permute-done.4.refs_2_ = f32[64,384]{1,0:T(8,128)S(1)} collective-permute-done((f32[64,384]{1,0:T(8,128)S(1)}, f32[64,384]{1,0:T(8,128)S(1)}, u32[]{:S(2)}, u32[]{:S(2)}) %collective-permute-start.4) | collective-permute-done | bytes 98336 | tf_op jit(solution)/shard_map/ppermute | solution.py:35
  22.9 0.0 collective-permute-done.5.refs_3_
  22.9 0.2 node.1
  23.1 0.0 collective-permute-done.11.pair_mine_ref
  23.1 0.0 collective-permute-done.12.pair_theirs_ref
  23.1 0.3 correct.1.sent_ref
  23.4 1.7 %collective-permute-start.13 = (f32[256,128]{1,0:T(8,128)S(1)}, f32[256,128]{1,0:T(8,128)S(1)}, u32[]{:S(2)}, u32[]{:S(2)}) collective-permute-start(f32[256,128]{1,0:T(8,128)S(1)} %correct.1.sent_ref), channel_id=1, source_target_pairs={{0,8},{8,0},{16,24},{24,16},{1,9},{9,1},{17,25},{25,17},{2,10},{10... | collective-permute-start | bytes 393224 | tf_op jit(solution)/shard_map/ppermute | solution.py:35
  25.1 0.8 %collective-permute-start.6 = (f32[64,128]{1,0:T(8,128)S(1)}, f32[64,128]{1,0:T(8,128)S(1)}, u32[]{:S(2)}, u32[]{:S(2)}) collective-permute-start(f32[64,128]{1,0:T(8,128)S(1)} %get-tuple-element.24.refs_0_.own_ref), channel_id=1, source_target_pairs={{0,2},{1,3},{2,0},{3,1},{4,6},{5,7},{6,4},{7,5},{8,10},{9,11},{10,... | collective-permute-start | bytes 98312 | tf_op jit(solution)/shard_map/ppermute | solution.py:35
  25.9 0.9 %collective-permute-start.7 = (f32[64,128]{1,0:T(8,128)S(1)}, f32[64,128]{1,0:T(8,128)S(1)}, u32[]{:S(2)}, u32[]{:S(2)}) collective-permute-start(f32[64,128]{1,0:T(8,128)S(1)} %get-tuple-element.25.other_ref), channel_id=1, source_target_pairs={{0,4},{1,5},{2,6},{3,7},{4,0},{5,1},{6,2},{7,3},{8,12},{9,13},{10,... | collective-permute-start | bytes 98312 | tf_op jit(solution)/shard_map/ppermute | solution.py:35
  26.8 1.8 %collective-permute-start.8 = (f32[64,128]{1,0:T(8,128)S(1)}, f32[64,128]{1,0:T(8,128)S(1)}, u32[]{:S(2)}, u32[]{:S(2)}) collective-permute-start(f32[64,128]{1,0:T(8,128)S(1)} %get-tuple-element.25.other_ref), channel_id=1, source_target_pairs={{0,6},{1,7},{2,4},{3,5},{4,2},{5,3},{6,0},{7,1},{8,14},{9,15},{10,... | collective-permute-start | bytes 98312 | tf_op jit(solution)/shard_map/ppermute | solution.py:35
  28.6 0.0 collective-permute-done.13.got_ref.after_ref
  28.6 0.4 level1.1
  29.0 2.7 %collective-permute-start.14 = (f32[64,128]{1,0:T(8,128)S(1)}, f32[64,128]{1,0:T(8,128)S(1)}, u32[]{:S(2)}, u32[]{:S(2)}) collective-permute-start(f32[64,128]{1,0:T(8,128)S(1)} %get-tuple-element.28.sent_ref), channel_id=1, source_target_pairs={{0,16},{8,24},{16,0},{24,8},{1,17},{9,25},{17,1},{25,9},{2,18},{10... | collective-permute-start | bytes 98312 | tf_op jit(solution)/shard_map/ppermute | solution.py:35
  31.7 2.2 %solve.1.after_ref.first_ref = f32[4608,512]{1,0:T(8,128)S(1)} custom-call(bf16[18,256,256]{2,1,0:T(8,128)(2,1)S(1)} %permute.1.moved_ref, bf16[4608,512]{1,0:T(8,128)(2,1)S(1)} %bitcast.1, f32[64,384]{1,0:T(8,128)S(1)} %get-tuple-element.20.refs_0_), custom_call_target="tpu_custom_call" | custom-call | flops 8800000000 | tf_op jit(solution)/shard_map/solve/pallas_call | solution.py:396
  33.9 0.0 collective-permute-done.6.refs_1_
  33.9 0.0 collective-permute-done.7.refs_2_
  33.9 0.0 collective-permute-done.8.refs_3_
  34.0 0.0 copy-start
  34.0 0.1 collective-permute-start.9
  34.1 0.0 collective-permute-done.14.got_ref
  34.1 0.2 level2.1.refs_1_
  34.3 1.2 %collective-permute-start.20 = (f32[64,256]{1,0:T(8,128)S(1)}, f32[64,256]{1,0:T(8,128)S(1)}, u32[]{:S(2)}, u32[]{:S(2)}) collective-permute-start(f32[64,256]{1,0:T(8,128)S(1)} %pack.1.ref), channel_id=1, source_target_pairs={{0,6},{1,7},{2,4},{3,5},{4,2},{5,3},{6,0},{7,1},{8,14},{9,15},{10,... | collective-permute-start | bytes 196616 | tf_op jit(solution)/shard_map/ppermute | solution.py:35
  35.5 1.4 %collective-permute-start.16 = (f32[64,256]{1,0:T(8,128)S(1)}, f32[64,256]{1,0:T(8,128)S(1)}, u32[]{:S(2)}, u32[]{:S(2)}) collective-permute-start(f32[64,256]{1,0:T(8,128)S(1)} %pack.1.ref), channel_id=1, source_target_pairs={{0,2},{1,3},{2,0},{3,1},{4,6},{5,7},{6,4},{7,5},{8,10},{9,11},{10,... | collective-permute-start | bytes 196616 | tf_op jit(solution)/shard_map/ppermute | solution.py:35
  36.9 1.0 %collective-permute-start.18 = (f32[64,256]{1,0:T(8,128)S(1)}, f32[64,256]{1,0:T(8,128)S(1)}, u32[]{:S(2)}, u32[]{:S(2)}) collective-permute-start(f32[64,256]{1,0:T(8,128)S(1)} %pack.1.ref), channel_id=1, source_target_pairs={{0,4},{1,5},{2,6},{3,7},{4,0},{5,1},{6,2},{7,3},{8,12},{9,13},{10,... | collective-permute-start | bytes 196616 | tf_op jit(solution)/shard_map/ppermute | solution.py:35
  37.8 0.0 collective-permute-done.9.pair_ref
  37.8 0.0 copy-done
  37.8 1.6 %apply.1.after_ref.refs_8_ = f32[4608,512]{1,0:T(8,128)S(1)} custom-call(f32[4,64,128]{2,1,0:T(8,128)S(1)} %stack.1.own_ref, f32[4,64,128]{2,1,0:T(8,128)S(1)} %collective-permute-done.9.pair_ref, f32[4608,512]{1,0:T(8,128)S(1)} %solve.1.after_ref.first_ref, bf16[3,4608,128]{2,1,0:T(8,128)(2,1)S(1)} %copy-done), custom_call_target="tpu_custom_call" | custom-call | flops 1980000000 | tf_op jit(solution)/shard_map/apply/pallas_call | solution.py:418
  39.4 0.1 collective-permute-start.15
  39.5 0.6 %collective-permute-done.20.ref = f32[64,256]{1,0:T(8,128)S(1)} collective-permute-done((f32[64,256]{1,0:T(8,128)S(1)}, f32[64,256]{1,0:T(8,128)S(1)}, u32[]{:S(2)}, u32[]{:S(2)}) %collective-permute-start.20) | collective-permute-done | bytes 65568 | tf_op jit(solution)/shard_map/ppermute | solution.py:35
  40.1 0.0 collective-permute-start.21
  40.1 0.6 %collective-permute-done.16.refs_2_ = f32[64,256]{1,0:T(8,128)S(1)} collective-permute-done((f32[64,256]{1,0:T(8,128)S(1)}, f32[64,256]{1,0:T(8,128)S(1)}, u32[]{:S(2)}, u32[]{:S(2)}) %collective-permute-start.16) | collective-permute-done | bytes 65568 | tf_op jit(solution)/shard_map/ppermute | solution.py:35
  40.7 0.0 collective-permute-start.17
  40.7 0.4 collective-permute-done.18.refs_4_
  41.2 0.1 collective-permute-start.19
  41.3 0.0 collective-permute-done.15.refs_1_
  41.3 0.1 collective-permute-done.21.refs_7_
  41.4 0.6 %collective-permute-done.17.refs_3_ = f32[64,256]{1,0:T(8,128)S(1)} collective-permute-done((f32[64,256]{1,0:T(8,128)S(1)}, f32[64,256]{1,0:T(8,128)S(1)}, u32[]{:S(2)}, u32[]{:S(2)}) %collective-permute-start.17) | collective-permute-done | bytes 65568 | tf_op jit(solution)/shard_map/ppermute | solution.py:35
  42.0 0.4 collective-permute-done.19.refs_5_
  42.4 4.3 %expand.1 = f32[4608,512]{1,0:T(8,128)} custom-call(f32[64,256]{1,0:T(8,128)S(1)} %relay.2.refs_0_, f32[64,256]{1,0:T(8,128)S(1)} %collective-permute-done.15.refs_1_, f32[64,256]{1,0:T(8,128)S(1)} %collective-permute-done.16.refs_2_, f32[64,256]{1,0:T(8,128)S(1)} %collective-permute-done.17.refs_3_, f32[64,256]{1,0:T(8,128)S(1)} %collective-permute-done.18.refs_4_, ...), custom_call_target="tpu_custom_call" | custom-call | flops 5500000256 | tf_op jit(solution)/shard_map/expand/pallas_call | solution.py:440
  (13 shorter events, 0.1 us)
Async XLA Ops:
  0.0 3.9 %copy-start.2 = (s32[18,256]{1,0:T(8,128)S(1)}, s32[18,256]{1,0:T(8,128)}, u32[]{:S(2)}) copy-start(s32[18,256]{1,0:T(8,128)} %order_ref.1) | copy-start | bytes 55300
  0.0 3.9 %copy-start.1 = (bf16[18,256,256]{2,1,0:T(8,128)(2,1)S(1)}, bf16[18,256,256]{2,1,0:T(8,128)(2,1)}, u32[]{:S(2)}) copy-start(bf16[18,256,256]{2,1,0:T(8,128)(2,1)} %inv_ref.1) | copy-start | bytes 7077892
  3.4 1.5 %collective-permute-start = (f32[64,384]{1,0:T(8,128)S(1)}, f32[64,384]{1,0:T(8,128)S(1)}, u32[]{:S(2)}, u32[]{:S(2)}) collective-permute-start(f32[64,384]{1,0:T(8,128)S(1)} %get-tuple-element.19), channel_id=1, source_target_pairs={{0,1},{1,0},{2,3},{3,2},{4,5},{5,4},{6,7},{7,6},{8,9},{9,8},{10,11... | collective-permute-start | bytes 294920 | tf_op jit(solution)/shard_map/ppermute | solution.py:35
  4.8 4.0 %slice-start = ((s8[4718592]{0:T(1024)(128)(4,1)}), s8[4194304]{0:T(1024)(128)(4,1)S(1)}, s32[]{:S(2)}) async-start(s8[4718592]{0:T(1024)(128)(4,1)} %bitcast), calls=%async_computation | async-start | bytes 8388608
  4.8 6.1 %collective-permute-start.1 = (f32[64,384]{1,0:T(8,128)S(1)}, f32[64,384]{1,0:T(8,128)S(1)}, u32[]{:S(2)}, u32[]{:S(2)}) collective-permute-start(f32[64,384]{1,0:T(8,128)S(1)} %add.2.after_ref.mine_ref), channel_id=1, source_target_pairs={{0,2},{1,3},{2,0},{3,1},{4,6},{5,7},{6,4},{7,5},{8,10},{9,11},{10,... | collective-permute-start | bytes 294920 | tf_op jit(solution)/shard_map/ppermute | solution.py:35
  7.7 1.1 %slice-start.1 = ((s8[4718592]{0:T(1024)(128)(4,1)}), s8[524288]{0:T(1024)(128)(4,1)S(1)}, s32[]{:S(2)}) async-start(s8[4718592]{0:T(1024)(128)(4,1)} %bitcast), calls=%async_computation.1 | async-start | bytes 1048576
  10.9 3.8 %collective-permute-start.2 = (f32[384,256]{1,0:T(8,128)S(1)}, f32[384,256]{1,0:T(8,128)S(1)}, u32[]{:S(2)}, u32[]{:S(2)}) collective-permute-start(f32[384,256]{1,0:T(8,128)S(1)} %project_other.1), channel_id=1, source_target_pairs={{0,1},{1,0},{2,3},{3,2},{4,5},{5,4},{6,7},{7,6},{8,9},{9,8},{10,11... | collective-permute-start | bytes 1179656 | tf_op jit(solution)/shard_map/ppermute | solution.py:35
  11.0 7.5 %copy-start.3 = (s32[3,128]{1,0:T(4,128)S(1)}, s32[3,128]{1,0:T(4,128)}, u32[]{:S(2)}) copy-start(s32[3,128]{1,0:T(4,128)} %perm_ref.1) | copy-start | bytes 4612
  11.0 9.2 %collective-permute-start.10 = (f32[64,384]{1,0:T(8,128)S(1)}, f32[64,384]{1,0:T(8,128)S(1)}, u32[]{:S(2)}, u32[]{:S(2)}) collective-permute-start(f32[64,384]{1,0:T(8,128)S(1)} %add.3.after_ref.mine_ref), channel_id=1, source_target_pairs={{0,4},{1,5},{2,6},{3,7},{4,0},{5,1},{6,2},{7,3},{8,12},{9,13},{10,... | collective-permute-start | bytes 294920 | tf_op jit(solution)/shard_map/ppermute | solution.py:35
  14.9 5.8 %collective-permute-start.3 = (f32[64,384]{1,0:T(8,128)S(1)}, f32[64,384]{1,0:T(8,128)S(1)}, u32[]{:S(2)}, u32[]{:S(2)}) collective-permute-start(f32[64,384]{1,0:T(8,128)S(1)} %get-tuple-element.21), channel_id=1, source_target_pairs={{0,2},{1,3},{2,0},{3,1},{4,6},{5,7},{6,4},{7,5},{8,10},{9,11},{10,... | collective-permute-start | bytes 294920 | tf_op jit(solution)/shard_map/ppermute | solution.py:35
  16.5 6.4 %collective-permute-start.4 = (f32[64,384]{1,0:T(8,128)S(1)}, f32[64,384]{1,0:T(8,128)S(1)}, u32[]{:S(2)}, u32[]{:S(2)}) collective-permute-start(f32[64,384]{1,0:T(8,128)S(1)} %get-tuple-element.22), channel_id=1, source_target_pairs={{0,4},{1,5},{2,6},{3,7},{4,0},{5,1},{6,2},{7,3},{8,12},{9,13},{10,... | collective-permute-start | bytes 294920 | tf_op jit(solution)/shard_map/ppermute | solution.py:35
  17.0 5.9 %collective-permute-start.5 = (f32[64,384]{1,0:T(8,128)S(1)}, f32[64,384]{1,0:T(8,128)S(1)}, u32[]{:S(2)}, u32[]{:S(2)}) collective-permute-start(f32[64,384]{1,0:T(8,128)S(1)} %get-tuple-element.23), channel_id=1, source_target_pairs={{0,6},{1,7},{2,4},{3,5},{4,2},{5,3},{6,0},{7,1},{8,14},{9,15},{10,... | collective-permute-start | bytes 294920 | tf_op jit(solution)/shard_map/ppermute | solution.py:35
  20.2 2.9 %collective-permute-start.11 = (f32[64,384]{1,0:T(8,128)S(1)}, f32[64,384]{1,0:T(8,128)S(1)}, u32[]{:S(2)}, u32[]{:S(2)}) collective-permute-start(f32[64,384]{1,0:T(8,128)S(1)} %add.3.after_ref.mine_ref), channel_id=1, source_target_pairs={{0,1},{1,0},{2,3},{3,2},{4,5},{5,4},{6,7},{7,6},{8,9},{9,8},{10,11... | collective-permute-start | bytes 294920 | tf_op jit(solution)/shard_map/ppermute | solution.py:35
  20.3 2.8 %collective-permute-start.12 = (f32[64,384]{1,0:T(8,128)S(1)}, f32[64,384]{1,0:T(8,128)S(1)}, u32[]{:S(2)}, u32[]{:S(2)}) collective-permute-start(f32[64,384]{1,0:T(8,128)S(1)} %collective-permute-done.10.theirs_ref), channel_id=1, source_target_pairs={{0,1},{1,0},{2,3},{3,2},{4,5},{5,4},{6,7},{7,6},{8,9},{9,8},{10,11... | collective-permute-start | bytes 294920 | tf_op jit(solution)/shard_map/ppermute | solution.py:35
  23.4 5.2 %collective-permute-start.13 = (f32[256,128]{1,0:T(8,128)S(1)}, f32[256,128]{1,0:T(8,128)S(1)}, u32[]{:S(2)}, u32[]{:S(2)}) collective-permute-start(f32[256,128]{1,0:T(8,128)S(1)} %correct.1.sent_ref), channel_id=1, source_target_pairs={{0,8},{8,0},{16,24},{24,16},{1,9},{9,1},{17,25},{25,17},{2,10},{10... | collective-permute-start | bytes 393224 | tf_op jit(solution)/shard_map/ppermute | solution.py:35
  25.1 8.8 %collective-permute-start.6 = (f32[64,128]{1,0:T(8,128)S(1)}, f32[64,128]{1,0:T(8,128)S(1)}, u32[]{:S(2)}, u32[]{:S(2)}) collective-permute-start(f32[64,128]{1,0:T(8,128)S(1)} %get-tuple-element.24.refs_0_.own_ref), channel_id=1, source_target_pairs={{0,2},{1,3},{2,0},{3,1},{4,6},{5,7},{6,4},{7,5},{8,10},{9,11},{10,... | collective-permute-start | bytes 98312 | tf_op jit(solution)/shard_map/ppermute | solution.py:35
  25.9 8.0 %collective-permute-start.7 = (f32[64,128]{1,0:T(8,128)S(1)}, f32[64,128]{1,0:T(8,128)S(1)}, u32[]{:S(2)}, u32[]{:S(2)}) collective-permute-start(f32[64,128]{1,0:T(8,128)S(1)} %get-tuple-element.25.other_ref), channel_id=1, source_target_pairs={{0,4},{1,5},{2,6},{3,7},{4,0},{5,1},{6,2},{7,3},{8,12},{9,13},{10,... | collective-permute-start | bytes 98312 | tf_op jit(solution)/shard_map/ppermute | solution.py:35
  26.8 7.1 %collective-permute-start.8 = (f32[64,128]{1,0:T(8,128)S(1)}, f32[64,128]{1,0:T(8,128)S(1)}, u32[]{:S(2)}, u32[]{:S(2)}) collective-permute-start(f32[64,128]{1,0:T(8,128)S(1)} %get-tuple-element.25.other_ref), channel_id=1, source_target_pairs={{0,6},{1,7},{2,4},{3,5},{4,2},{5,3},{6,0},{7,1},{8,14},{9,15},{10,... | collective-permute-start | bytes 98312 | tf_op jit(solution)/shard_map/ppermute | solution.py:35
  29.0 5.0 %collective-permute-start.14 = (f32[64,128]{1,0:T(8,128)S(1)}, f32[64,128]{1,0:T(8,128)S(1)}, u32[]{:S(2)}, u32[]{:S(2)}) collective-permute-start(f32[64,128]{1,0:T(8,128)S(1)} %get-tuple-element.28.sent_ref), channel_id=1, source_target_pairs={{0,16},{8,24},{16,0},{24,8},{1,17},{9,25},{17,1},{25,9},{2,18},{10... | collective-permute-start | bytes 98312 | tf_op jit(solution)/shard_map/ppermute | solution.py:35
  34.0 3.9 %copy-start = (bf16[3,4608,128]{2,1,0:T(8,128)(2,1)S(1)}, bf16[3,4608,128]{2,1,0:T(8,128)(2,1)}, u32[]{:S(2)}) copy-start(bf16[3,4608,128]{2,1,0:T(8,128)(2,1)} %refs_9_.1) | copy-start | bytes 10616836
  34.0 3.9 %collective-permute-start.9 = (f32[4,64,128]{2,1,0:T(8,128)S(1)}, f32[4,64,128]{2,1,0:T(8,128)S(1)}, u32[]{:S(2)}, u32[]{:S(2)}) collective-permute-start(f32[4,64,128]{2,1,0:T(8,128)S(1)} %stack.1.own_ref), channel_id=1, source_target_pairs={{0,1},{1,0},{2,3},{3,2},{4,5},{5,4},{6,7},{7,6},{8,9},{9,8},{10,11... | collective-permute-start | bytes 393224 | tf_op jit(solution)/shard_map/ppermute | solution.py:35
  34.3 5.9 %collective-permute-start.20 = (f32[64,256]{1,0:T(8,128)S(1)}, f32[64,256]{1,0:T(8,128)S(1)}, u32[]{:S(2)}, u32[]{:S(2)}) collective-permute-start(f32[64,256]{1,0:T(8,128)S(1)} %pack.1.ref), channel_id=1, source_target_pairs={{0,6},{1,7},{2,4},{3,5},{4,2},{5,3},{6,0},{7,1},{8,14},{9,15},{10,... | collective-permute-start | bytes 196616 | tf_op jit(solution)/shard_map/ppermute | solution.py:35
  35.5 5.2 %collective-permute-start.16 = (f32[64,256]{1,0:T(8,128)S(1)}, f32[64,256]{1,0:T(8,128)S(1)}, u32[]{:S(2)}, u32[]{:S(2)}) collective-permute-start(f32[64,256]{1,0:T(8,128)S(1)} %pack.1.ref), channel_id=1, source_target_pairs={{0,2},{1,3},{2,0},{3,1},{4,6},{5,7},{6,4},{7,5},{8,10},{9,11},{10,... | collective-permute-start | bytes 196616 | tf_op jit(solution)/shard_map/ppermute | solution.py:35
  36.9 4.3 %collective-permute-start.18 = (f32[64,256]{1,0:T(8,128)S(1)}, f32[64,256]{1,0:T(8,128)S(1)}, u32[]{:S(2)}, u32[]{:S(2)}) collective-permute-start(f32[64,256]{1,0:T(8,128)S(1)} %pack.1.ref), channel_id=1, source_target_pairs={{0,4},{1,5},{2,6},{3,7},{4,0},{5,1},{6,2},{7,3},{8,12},{9,13},{10,... | collective-permute-start | bytes 196616 | tf_op jit(solution)/shard_map/ppermute | solution.py:35
  39.4 1.8 %collective-permute-start.15 = (f32[64,256]{1,0:T(8,128)S(1)}, f32[64,256]{1,0:T(8,128)S(1)}, u32[]{:S(2)}, u32[]{:S(2)}) collective-permute-start(f32[64,256]{1,0:T(8,128)S(1)} %relay.2.refs_0_), channel_id=1, source_target_pairs={{0,1},{1,0},{2,3},{3,2},{4,5},{5,4},{6,7},{7,6},{8,9},{9,8},{10,11... | collective-permute-start | bytes 196616 | tf_op jit(solution)/shard_map/ppermute | solution.py:35
  40.1 1.3 %collective-permute-start.21 = (f32[64,256]{1,0:T(8,128)S(1)}, f32[64,256]{1,0:T(8,128)S(1)}, u32[]{:S(2)}, u32[]{:S(2)}) collective-permute-start(f32[64,256]{1,0:T(8,128)S(1)} %relay.3.refs_6_), channel_id=1, source_target_pairs={{0,1},{1,0},{2,3},{3,2},{4,5},{5,4},{6,7},{7,6},{8,9},{9,8},{10,11... | collective-permute-start | bytes 196616 | tf_op jit(solution)/shard_map/ppermute | solution.py:35
  40.7 1.3 %collective-permute-start.17 = (f32[64,256]{1,0:T(8,128)S(1)}, f32[64,256]{1,0:T(8,128)S(1)}, u32[]{:S(2)}, u32[]{:S(2)}) collective-permute-start(f32[64,256]{1,0:T(8,128)S(1)} %collective-permute-done.16.refs_2_), channel_id=1, source_target_pairs={{0,1},{1,0},{2,3},{3,2},{4,5},{5,4},{6,7},{7,6},{8,9},{9,8},{10,11... | collective-permute-start | bytes 196616 | tf_op jit(solution)/shard_map/ppermute | solution.py:35
  41.2 1.3 %collective-permute-start.19 = (f32[64,256]{1,0:T(8,128)S(1)}, f32[64,256]{1,0:T(8,128)S(1)}, u32[]{:S(2)}, u32[]{:S(2)}) collective-permute-start(f32[64,256]{1,0:T(8,128)S(1)} %collective-permute-done.18.refs_4_), channel_id=1, source_target_pairs={{0,1},{1,0},{2,3},{3,2},{4,5},{5,4},{6,7},{7,6},{8,9},{9,8},{10,11... | collective-permute-start | bytes 196616 | tf_op jit(solution)/shard_map/ppermute | solution.py:35

commit v22 on v21

--- a/solution.py
+++ b/solution.py
@@ -307,15 +307,16 @@
     gram_lanes = len(below_pairs(levels)) * rank
 
     per_step = blocks_per_step(nblocks, 3)
+    chunk = blocks_per_step(nblocks, 2)
     flipped, gram_keep, gram_send = pl.pallas_call(
-        functools.partial(gram_kernel, levels, per_step, width),
+        functools.partial(gram_kernel, levels, chunk, width),
         in_specs=[pl.BlockSpec(memory_space=pltpu.HBM)] * 2,
         out_shape=[jax.ShapeDtypeStruct((kinds, rows), jnp.bfloat16)] + [floats(rank // 2, gram_lanes)] * 2,
         scratch_shapes=[
             pltpu.VMEM((levels, rows, rank), jnp.bfloat16),
             pltpu.VMEM((levels - 1, rows, rank), jnp.bfloat16),
             pltpu.VMEM((size, size), jnp.float32),
-            pltpu.SemaphoreType.DMA((2, nblocks // per_step)),
+            pltpu.SemaphoreType.DMA((2, nblocks // chunk)),
         ],
         name="gram",
         **settings(24, 3),

time: 46.8 us -> 47.4 us (1.013)
  Pallas kernels: 20.3 us -> 20.9 us
    pallas_call x1, Pallas kernels: 3.34 us -> 3.92 us  [per_device(): pl.pallas_call(functools.partial(gram_kernel, levels, chunk, width), in_s...]
  transfers between devices with their start and end apart: 22 -> 22, of which waited for: 8 -> 8; matrix products, arithmetic and copies ran while one was open for 0% -> 0% of each run, Pallas kernels for 27% -> 26%
where the time goes in v22:
time: 47.4 us; the launch traced here: 47.3 us
  starting transfers between devices  21 us (44%)
  Pallas kernels  20.9 us (44%)
  waiting for transfers between devices  5.08 us (11%)
    ppermute x22, starting transfers between devices, swap(): return lax.ppermute(value, axis, [(i, i ^ mask) for i in range(count)])  21 us
    ppermute x22, waiting for transfers between devices, swap(): return lax.ppermute(value, axis, [(i, i ^ mask) for i in range(count)])  5.08 us
    pallas_call x1, Pallas kernels, per_device(): pl.pallas_call(functools.partial(expand_kernel, levels, width, count), ou...  4.28 us
    pallas_call x2, Pallas kernels, project(): pl.pallas_call(functools.partial(project_kernel, other), out_shape=floats...  3.99 us
    pallas_call x1, Pallas kernels, per_device(): pl.pallas_call(functools.partial(gram_kernel, levels, chunk, width), in_s...  3.92 us
    pallas_call x1, Pallas kernels, per_device(): pl.pallas_call(functools.partial(solve_kernel, per_step, width), out_shap...  2.22 us
    pallas_call x1, Pallas kernels, per_device(): pl.pallas_call(functools.partial(prepare_kernel, levels), in_specs=[pl.Bl...  1.69 us
    pallas_call x1, Pallas kernels, per_device(): pl.pallas_call(functools.partial(apply_kernel, per_step * width), out_sha...  1.57 us
  transfers between devices with their start and end apart: 22, of which 8 were waited for; matrix products, arithmetic and copies ran while one was open for 0% of the time, Pallas kernels for 26%

profile of v22, /device:TPU:0, one launch (start us, length us, event | category | flops | bytes accessed | tf_op | source)
XLA Modules:
  0.0 47.3 jit_solution(15164011979011812249)
XLA Ops:
  0.0 3.9 %gram.1 = (bf16[384,4608]{1,0:T(8,128)(2,1)S(1)}, f32[64,384]{1,0:T(8,128)S(1)}, f32[64,384]{1,0:T(8,128)S(1)}) custom-call(bf16[3,4608,128]{2,1,0:T(8,128)(2,1)} %right_ref.1, bf16[3,4608,128]{2,1,0:T(8,128)(2,1)} %refs_9_.1), custom_call_target="tpu_custom_call" | custom-call | flops 3300000000 | tf_op jit(solution)/shard_map/gram/pallas_call | solution.py:311
  3.9 0.5 %collective-permute-start = (f32[64,384]{1,0:T(8,128)S(1)}, f32[64,384]{1,0:T(8,128)S(1)}, u32[]{:S(2)}, u32[]{:S(2)}) collective-permute-start(f32[64,384]{1,0:T(8,128)S(1)} %get-tuple-element.19), channel_id=1, source_target_pairs={{0,1},{1,0},{2,3},{3,2},{4,5},{5,4},{6,7},{7,6},{8,9},{9,8},{10,11... | collective-permute-start | bytes 294920 | tf_op jit(solution)/shard_map/ppermute | solution.py:35
  4.4 0.0 copy-done.2
  4.4 0.0 copy-done.1
  4.5 0.8 %permute.1.moved_ref = bf16[18,256,256]{2,1,0:T(8,128)(2,1)S(1)} custom-call(s32[18,256]{1,0:T(8,128)S(1)} %copy-done.2, bf16[18,256,256]{2,1,0:T(8,128)(2,1)S(1)} %copy-done.1), custom_call_target="tpu_custom_call" | custom-call | flops 1650000000 | tf_op jit(solution)/shard_map/permute/pallas_call | solution.py:327
  5.3 0.1 collective-permute-done.got_ref
  5.4 2.9 %collective-permute-start.1 = (f32[64,384]{1,0:T(8,128)S(1)}, f32[64,384]{1,0:T(8,128)S(1)}, u32[]{:S(2)}, u32[]{:S(2)}) collective-permute-start(f32[64,384]{1,0:T(8,128)S(1)} %add.2.after_ref.mine_ref), channel_id=1, source_target_pairs={{0,2},{1,3},{2,0},{3,1},{4,6},{5,7},{6,4},{7,5},{8,10},{9,11},{10,... | collective-permute-start | bytes 294920 | tf_op jit(solution)/shard_map/ppermute | solution.py:35
  8.3 1.1 %weigh.1.factor_ref = bf16[768,4608]{1,0:T(8,128)(2,1)S(1)} custom-call(bf16[18,256,256]{2,1,0:T(8,128)(2,1)S(1)} %permute.1.moved_ref, bf16[384,4608]{1,0:T(8,128)(2,1)S(1)} %get-tuple-element.17.flip_ref, f32[64,384]{1,0:T(8,128)S(1)} %add.2.after_ref.mine_ref), custom_call_target="tpu_custom_call" | custom-call | flops 2640000000 | tf_op jit(solution)/shard_map/weigh/pallas_call | solution.py:340
  9.4 0.0 slice-done
  9.4 0.0 slice-done.1
  9.4 2.0 %project_other.1 = f32[384,256]{1,0:T(8,128)S(1)} custom-call(bf16[768,4608]{1,0:T(8,128)(2,1)S(1)} %weigh.1.factor_ref, bf16[4608,512]{1,0:T(8,128)(2,1)S(1)} %bitcast.1, f32[64,384]{1,0:T(8,128)S(1)} %add.2.after_ref.mine_ref), custom_call_target="tpu_custom_call" | custom-call | flops 1100000000 | tf_op jit(solution)/shard_map/project_other/pallas_call | solution.py:348
  11.5 0.1 collective-permute-start.2
  11.5 0.0 collective-permute-done.1.got_ref
  11.6 0.0 copy-start.3
  11.6 1.7 %collective-permute-start.10 = (f32[64,384]{1,0:T(8,128)S(1)}, f32[64,384]{1,0:T(8,128)S(1)}, u32[]{:S(2)}, u32[]{:S(2)}) collective-permute-start(f32[64,384]{1,0:T(8,128)S(1)} %add.3.after_ref.mine_ref), channel_id=1, source_target_pairs={{0,4},{1,5},{2,6},{3,7},{4,0},{5,1},{6,2},{7,3},{8,12},{9,13},{10,... | collective-permute-start | bytes 294920 | tf_op jit(solution)/shard_map/ppermute | solution.py:35
  13.3 2.0 %project_own.1.keep_ref = f32[384,256]{1,0:T(8,128)S(1)} custom-call(bf16[768,4608]{1,0:T(8,128)(2,1)S(1)} %weigh.1.factor_ref, bf16[4608,512]{1,0:T(8,128)(2,1)S(1)} %bitcast.1, f32[64,384]{1,0:T(8,128)S(1)} %add.3.after_ref.mine_ref), custom_call_target="tpu_custom_call" | custom-call | flops 4400000000 | tf_op jit(solution)/shard_map/project_own/pallas_call | solution.py:348
  15.3 0.0 collective-permute-done.2.got_ref
  15.3 0.2 merge.1
  15.5 1.6 %collective-permute-start.3 = (f32[64,384]{1,0:T(8,128)S(1)}, f32[64,384]{1,0:T(8,128)S(1)}, u32[]{:S(2)}, u32[]{:S(2)}) collective-permute-start(f32[64,384]{1,0:T(8,128)S(1)} %get-tuple-element.21), channel_id=1, source_target_pairs={{0,2},{1,3},{2,0},{3,1},{4,6},{5,7},{6,4},{7,5},{8,10},{9,11},{10,... | collective-permute-start | bytes 294920 | tf_op jit(solution)/shard_map/ppermute | solution.py:35
  17.1 0.5 %collective-permute-start.4 = (f32[64,384]{1,0:T(8,128)S(1)}, f32[64,384]{1,0:T(8,128)S(1)}, u32[]{:S(2)}, u32[]{:S(2)}) collective-permute-start(f32[64,384]{1,0:T(8,128)S(1)} %get-tuple-element.22), channel_id=1, source_target_pairs={{0,4},{1,5},{2,6},{3,7},{4,0},{5,1},{6,2},{7,3},{8,12},{9,13},{10,... | collective-permute-start | bytes 294920 | tf_op jit(solution)/shard_map/ppermute | solution.py:35
  17.6 1.5 %collective-permute-start.5 = (f32[64,384]{1,0:T(8,128)S(1)}, f32[64,384]{1,0:T(8,128)S(1)}, u32[]{:S(2)}, u32[]{:S(2)}) collective-permute-start(f32[64,384]{1,0:T(8,128)S(1)} %get-tuple-element.23), channel_id=1, source_target_pairs={{0,6},{1,7},{2,4},{3,5},{4,2},{5,3},{6,0},{7,1},{8,14},{9,15},{10,... | collective-permute-start | bytes 294920 | tf_op jit(solution)/shard_map/ppermute | solution.py:35
  19.1 1.7 %prepare.1.refs_4_.joined_ref = bf16[3,768,256]{2,1,0:T(8,128)(2,1)S(1)} custom-call(f32[7,256,256]{2,1,0:T(8,128)} %joined_ref.1, s32[3,128]{1,0:T(4,128)S(1)} %copy-done.3), custom_call_target="tpu_custom_call" | custom-call | flops 2200000000 | tf_op jit(solution)/shard_map/prepare/pallas_call | solution.py:372
  20.7 0.1 collective-permute-start.11
  20.8 0.0 collective-permute-done.10.theirs_ref
  20.8 0.5 %collective-permute-start.12 = (f32[64,384]{1,0:T(8,128)S(1)}, f32[64,384]{1,0:T(8,128)S(1)}, u32[]{:S(2)}, u32[]{:S(2)}) collective-permute-start(f32[64,384]{1,0:T(8,128)S(1)} %collective-permute-done.10.theirs_ref), channel_id=1, source_target_pairs={{0,1},{1,0},{2,3},{3,2},{4,5},{5,4},{6,7},{7,6},{8,9},{9,8},{10,11... | collective-permute-start | bytes 294920 | tf_op jit(solution)/shard_map/ppermute | solution.py:35
  21.3 0.0 collective-permute-done.3.refs_1_
  21.3 2.1 %collective-permute-done.4.refs_2_ = f32[64,384]{1,0:T(8,128)S(1)} collective-permute-done((f32[64,384]{1,0:T(8,128)S(1)}, f32[64,384]{1,0:T(8,128)S(1)}, u32[]{:S(2)}, u32[]{:S(2)}) %collective-permute-start.4) | collective-permute-done | bytes 98336 | tf_op jit(solution)/shard_map/ppermute | solution.py:35
  23.5 0.0 collective-permute-done.5.refs_3_
  23.5 0.2 node.1
  23.7 0.0 collective-permute-done.11.pair_mine_ref
  23.7 0.0 collective-permute-done.12.pair_theirs_ref
  23.7 0.3 correct.1.sent_ref
  24.0 1.7 %collective-permute-start.13 = (f32[256,128]{1,0:T(8,128)S(1)}, f32[256,128]{1,0:T(8,128)S(1)}, u32[]{:S(2)}, u32[]{:S(2)}) collective-permute-start(f32[256,128]{1,0:T(8,128)S(1)} %correct.1.sent_ref), channel_id=1, source_target_pairs={{0,8},{8,0},{16,24},{24,16},{1,9},{9,1},{17,25},{25,17},{2,10},{10... | collective-permute-start | bytes 393224 | tf_op jit(solution)/shard_map/ppermute | solution.py:35
  25.7 0.8 %collective-permute-start.6 = (f32[64,128]{1,0:T(8,128)S(1)}, f32[64,128]{1,0:T(8,128)S(1)}, u32[]{:S(2)}, u32[]{:S(2)}) collective-permute-start(f32[64,128]{1,0:T(8,128)S(1)} %get-tuple-element.24.refs_0_.own_ref), channel_id=1, source_target_pairs={{0,2},{1,3},{2,0},{3,1},{4,6},{5,7},{6,4},{7,5},{8,10},{9,11},{10,... | collective-permute-start | bytes 98312 | tf_op jit(solution)/shard_map/ppermute | solution.py:35
  26.5 0.9 %collective-permute-start.7 = (f32[64,128]{1,0:T(8,128)S(1)}, f32[64,128]{1,0:T(8,128)S(1)}, u32[]{:S(2)}, u32[]{:S(2)}) collective-permute-start(f32[64,128]{1,0:T(8,128)S(1)} %get-tuple-element.25.other_ref), channel_id=1, source_target_pairs={{0,4},{1,5},{2,6},{3,7},{4,0},{5,1},{6,2},{7,3},{8,12},{9,13},{10,... | collective-permute-start | bytes 98312 | tf_op jit(solution)/shard_map/ppermute | solution.py:35
  27.4 1.8 %collective-permute-start.8 = (f32[64,128]{1,0:T(8,128)S(1)}, f32[64,128]{1,0:T(8,128)S(1)}, u32[]{:S(2)}, u32[]{:S(2)}) collective-permute-start(f32[64,128]{1,0:T(8,128)S(1)} %get-tuple-element.25.other_ref), channel_id=1, source_target_pairs={{0,6},{1,7},{2,4},{3,5},{4,2},{5,3},{6,0},{7,1},{8,14},{9,15},{10,... | collective-permute-start | bytes 98312 | tf_op jit(solution)/shard_map/ppermute | solution.py:35
  29.2 0.0 collective-permute-done.13.got_ref.after_ref
  29.2 0.4 level1.1
  29.6 2.7 %collective-permute-start.14 = (f32[64,128]{1,0:T(8,128)S(1)}, f32[64,128]{1,0:T(8,128)S(1)}, u32[]{:S(2)}, u32[]{:S(2)}) collective-permute-start(f32[64,128]{1,0:T(8,128)S(1)} %get-tuple-element.28.sent_ref), channel_id=1, source_target_pairs={{0,16},{8,24},{16,0},{24,8},{1,17},{9,25},{17,1},{25,9},{2,18},{10... | collective-permute-start | bytes 98312 | tf_op jit(solution)/shard_map/ppermute | solution.py:35
  32.3 2.2 %solve.1.after_ref.first_ref = f32[4608,512]{1,0:T(8,128)S(1)} custom-call(bf16[18,256,256]{2,1,0:T(8,128)(2,1)S(1)} %permute.1.moved_ref, bf16[4608,512]{1,0:T(8,128)(2,1)S(1)} %bitcast.1, f32[64,384]{1,0:T(8,128)S(1)} %get-tuple-element.20.refs_0_), custom_call_target="tpu_custom_call" | custom-call | flops 8800000000 | tf_op jit(solution)/shard_map/solve/pallas_call | solution.py:397
  34.5 0.0 collective-permute-done.6.refs_1_
  34.5 0.0 collective-permute-done.7.refs_2_
  34.5 0.0 collective-permute-done.8.refs_3_
  34.5 0.0 copy-start
  34.6 0.1 collective-permute-start.9
  34.6 0.0 collective-permute-done.14.got_ref
  34.6 0.2 level2.1.refs_1_
  34.9 1.2 %collective-permute-start.20 = (f32[64,256]{1,0:T(8,128)S(1)}, f32[64,256]{1,0:T(8,128)S(1)}, u32[]{:S(2)}, u32[]{:S(2)}) collective-permute-start(f32[64,256]{1,0:T(8,128)S(1)} %pack.1.ref), channel_id=1, source_target_pairs={{0,6},{1,7},{2,4},{3,5},{4,2},{5,3},{6,0},{7,1},{8,14},{9,15},{10,... | collective-permute-start | bytes 196616 | tf_op jit(solution)/shard_map/ppermute | solution.py:35
  36.1 1.4 %collective-permute-start.16 = (f32[64,256]{1,0:T(8,128)S(1)}, f32[64,256]{1,0:T(8,128)S(1)}, u32[]{:S(2)}, u32[]{:S(2)}) collective-permute-start(f32[64,256]{1,0:T(8,128)S(1)} %pack.1.ref), channel_id=1, source_target_pairs={{0,2},{1,3},{2,0},{3,1},{4,6},{5,7},{6,4},{7,5},{8,10},{9,11},{10,... | collective-permute-start | bytes 196616 | tf_op jit(solution)/shard_map/ppermute | solution.py:35
  37.4 1.0 %collective-permute-start.18 = (f32[64,256]{1,0:T(8,128)S(1)}, f32[64,256]{1,0:T(8,128)S(1)}, u32[]{:S(2)}, u32[]{:S(2)}) collective-permute-start(f32[64,256]{1,0:T(8,128)S(1)} %pack.1.ref), channel_id=1, source_target_pairs={{0,4},{1,5},{2,6},{3,7},{4,0},{5,1},{6,2},{7,3},{8,12},{9,13},{10,... | collective-permute-start | bytes 196616 | tf_op jit(solution)/shard_map/ppermute | solution.py:35
  38.4 0.0 collective-permute-done.9.pair_ref
  38.4 1.6 %apply.1.after_ref.refs_8_ = f32[4608,512]{1,0:T(8,128)S(1)} custom-call(f32[4,64,128]{2,1,0:T(8,128)S(1)} %stack.1.own_ref, f32[4,64,128]{2,1,0:T(8,128)S(1)} %collective-permute-done.9.pair_ref, f32[4608,512]{1,0:T(8,128)S(1)} %solve.1.after_ref.first_ref, bf16[3,4608,128]{2,1,0:T(8,128)(2,1)S(1)} %copy-done), custom_call_target="tpu_custom_call" | custom-call | flops 1980000000 | tf_op jit(solution)/shard_map/apply/pallas_call | solution.py:419
  40.0 0.1 collective-permute-start.15
  40.1 0.6 %collective-permute-done.20.ref = f32[64,256]{1,0:T(8,128)S(1)} collective-permute-done((f32[64,256]{1,0:T(8,128)S(1)}, f32[64,256]{1,0:T(8,128)S(1)}, u32[]{:S(2)}, u32[]{:S(2)}) %collective-permute-start.20) | collective-permute-done | bytes 65568 | tf_op jit(solution)/shard_map/ppermute | solution.py:35
  40.7 0.0 collective-permute-start.21
  40.7 0.6 %collective-permute-done.16.refs_2_ = f32[64,256]{1,0:T(8,128)S(1)} collective-permute-done((f32[64,256]{1,0:T(8,128)S(1)}, f32[64,256]{1,0:T(8,128)S(1)}, u32[]{:S(2)}, u32[]{:S(2)}) %collective-permute-start.16) | collective-permute-done | bytes 65568 | tf_op jit(solution)/shard_map/ppermute | solution.py:35
  41.3 0.0 collective-permute-start.17
  41.3 0.4 collective-permute-done.18.refs_4_
  41.7 0.1 collective-permute-start.19
  41.8 0.0 collective-permute-done.15.refs_1_
  41.8 0.1 collective-permute-done.21.refs_7_
  42.0 0.6 %collective-permute-done.17.refs_3_ = f32[64,256]{1,0:T(8,128)S(1)} collective-permute-done((f32[64,256]{1,0:T(8,128)S(1)}, f32[64,256]{1,0:T(8,128)S(1)}, u32[]{:S(2)}, u32[]{:S(2)}) %collective-permute-start.17) | collective-permute-done | bytes 65568 | tf_op jit(solution)/shard_map/ppermute | solution.py:35
  42.6 0.4 collective-permute-done.19.refs_5_
  43.0 4.3 %expand.1 = f32[4608,512]{1,0:T(8,128)} custom-call(f32[64,256]{1,0:T(8,128)S(1)} %relay.2.refs_0_, f32[64,256]{1,0:T(8,128)S(1)} %collective-permute-done.15.refs_1_, f32[64,256]{1,0:T(8,128)S(1)} %collective-permute-done.16.refs_2_, f32[64,256]{1,0:T(8,128)S(1)} %collective-permute-done.17.refs_3_, f32[64,256]{1,0:T(8,128)S(1)} %collective-permute-done.18.refs_4_, ...), custom_call_target="tpu_custom_call" | custom-call | flops 5500000256 | tf_op jit(solution)/shard_map/expand/pallas_call | solution.py:441
  (13 shorter events, 0.1 us)
Async XLA Ops:
  0.0 4.4 %copy-start.2 = (s32[18,256]{1,0:T(8,128)S(1)}, s32[18,256]{1,0:T(8,128)}, u32[]{:S(2)}) copy-start(s32[18,256]{1,0:T(8,128)} %order_ref.1) | copy-start | bytes 55300
  0.0 4.4 %copy-start.1 = (bf16[18,256,256]{2,1,0:T(8,128)(2,1)S(1)}, bf16[18,256,256]{2,1,0:T(8,128)(2,1)}, u32[]{:S(2)}) copy-start(bf16[18,256,256]{2,1,0:T(8,128)(2,1)} %inv_ref.1) | copy-start | bytes 7077892
  3.9 1.5 %collective-permute-start = (f32[64,384]{1,0:T(8,128)S(1)}, f32[64,384]{1,0:T(8,128)S(1)}, u32[]{:S(2)}, u32[]{:S(2)}) collective-permute-start(f32[64,384]{1,0:T(8,128)S(1)} %get-tuple-element.19), channel_id=1, source_target_pairs={{0,1},{1,0},{2,3},{3,2},{4,5},{5,4},{6,7},{7,6},{8,9},{9,8},{10,11... | collective-permute-start | bytes 294920 | tf_op jit(solution)/shard_map/ppermute | solution.py:35
  5.4 4.0 %slice-start = ((s8[4718592]{0:T(1024)(128)(4,1)}), s8[4194304]{0:T(1024)(128)(4,1)S(1)}, s32[]{:S(2)}) async-start(s8[4718592]{0:T(1024)(128)(4,1)} %bitcast), calls=%async_computation | async-start | bytes 8388608
  5.4 6.1 %collective-permute-start.1 = (f32[64,384]{1,0:T(8,128)S(1)}, f32[64,384]{1,0:T(8,128)S(1)}, u32[]{:S(2)}, u32[]{:S(2)}) collective-permute-start(f32[64,384]{1,0:T(8,128)S(1)} %add.2.after_ref.mine_ref), channel_id=1, source_target_pairs={{0,2},{1,3},{2,0},{3,1},{4,6},{5,7},{6,4},{7,5},{8,10},{9,11},{10,... | collective-permute-start | bytes 294920 | tf_op jit(solution)/shard_map/ppermute | solution.py:35
  8.3 1.1 %slice-start.1 = ((s8[4718592]{0:T(1024)(128)(4,1)}), s8[524288]{0:T(1024)(128)(4,1)S(1)}, s32[]{:S(2)}) async-start(s8[4718592]{0:T(1024)(128)(4,1)} %bitcast), calls=%async_computation.1 | async-start | bytes 1048576
  11.5 3.8 %collective-permute-start.2 = (f32[384,256]{1,0:T(8,128)S(1)}, f32[384,256]{1,0:T(8,128)S(1)}, u32[]{:S(2)}, u32[]{:S(2)}) collective-permute-start(f32[384,256]{1,0:T(8,128)S(1)} %project_other.1), channel_id=1, source_target_pairs={{0,1},{1,0},{2,3},{3,2},{4,5},{5,4},{6,7},{7,6},{8,9},{9,8},{10,11... | collective-permute-start | bytes 1179656 | tf_op jit(solution)/shard_map/ppermute | solution.py:35
  11.6 7.5 %copy-start.3 = (s32[3,128]{1,0:T(4,128)S(1)}, s32[3,128]{1,0:T(4,128)}, u32[]{:S(2)}) copy-start(s32[3,128]{1,0:T(4,128)} %perm_ref.1) | copy-start | bytes 4612
  11.6 9.2 %collective-permute-start.10 = (f32[64,384]{1,0:T(8,128)S(1)}, f32[64,384]{1,0:T(8,128)S(1)}, u32[]{:S(2)}, u32[]{:S(2)}) collective-permute-start(f32[64,384]{1,0:T(8,128)S(1)} %add.3.after_ref.mine_ref), channel_id=1, source_target_pairs={{0,4},{1,5},{2,6},{3,7},{4,0},{5,1},{6,2},{7,3},{8,12},{9,13},{10,... | collective-permute-start | bytes 294920 | tf_op jit(solution)/shard_map/ppermute | solution.py:35
  15.5 5.8 %collective-permute-start.3 = (f32[64,384]{1,0:T(8,128)S(1)}, f32[64,384]{1,0:T(8,128)S(1)}, u32[]{:S(2)}, u32[]{:S(2)}) collective-permute-start(f32[64,384]{1,0:T(8,128)S(1)} %get-tuple-element.21), channel_id=1, source_target_pairs={{0,2},{1,3},{2,0},{3,1},{4,6},{5,7},{6,4},{7,5},{8,10},{9,11},{10,... | collective-permute-start | bytes 294920 | tf_op jit(solution)/shard_map/ppermute | solution.py:35
  17.1 6.4 %collective-permute-start.4 = (f32[64,384]{1,0:T(8,128)S(1)}, f32[64,384]{1,0:T(8,128)S(1)}, u32[]{:S(2)}, u32[]{:S(2)}) collective-permute-start(f32[64,384]{1,0:T(8,128)S(1)} %get-tuple-element.22), channel_id=1, source_target_pairs={{0,4},{1,5},{2,6},{3,7},{4,0},{5,1},{6,2},{7,3},{8,12},{9,13},{10,... | collective-permute-start | bytes 294920 | tf_op jit(solution)/shard_map/ppermute | solution.py:35
  17.6 5.9 %collective-permute-start.5 = (f32[64,384]{1,0:T(8,128)S(1)}, f32[64,384]{1,0:T(8,128)S(1)}, u32[]{:S(2)}, u32[]{:S(2)}) collective-permute-start(f32[64,384]{1,0:T(8,128)S(1)} %get-tuple-element.23), channel_id=1, source_target_pairs={{0,6},{1,7},{2,4},{3,5},{4,2},{5,3},{6,0},{7,1},{8,14},{9,15},{10,... | collective-permute-start | bytes 294920 | tf_op jit(solution)/shard_map/ppermute | solution.py:35
  20.7 2.9 %collective-permute-start.11 = (f32[64,384]{1,0:T(8,128)S(1)}, f32[64,384]{1,0:T(8,128)S(1)}, u32[]{:S(2)}, u32[]{:S(2)}) collective-permute-start(f32[64,384]{1,0:T(8,128)S(1)} %add.3.after_ref.mine_ref), channel_id=1, source_target_pairs={{0,1},{1,0},{2,3},{3,2},{4,5},{5,4},{6,7},{7,6},{8,9},{9,8},{10,11... | collective-permute-start | bytes 294920 | tf_op jit(solution)/shard_map/ppermute | solution.py:35
  20.8 2.8 %collective-permute-start.12 = (f32[64,384]{1,0:T(8,128)S(1)}, f32[64,384]{1,0:T(8,128)S(1)}, u32[]{:S(2)}, u32[]{:S(2)}) collective-permute-start(f32[64,384]{1,0:T(8,128)S(1)} %collective-permute-done.10.theirs_ref), channel_id=1, source_target_pairs={{0,1},{1,0},{2,3},{3,2},{4,5},{5,4},{6,7},{7,6},{8,9},{9,8},{10,11... | collective-permute-start | bytes 294920 | tf_op jit(solution)/shard_map/ppermute | solution.py:35
  24.0 5.2 %collective-permute-start.13 = (f32[256,128]{1,0:T(8,128)S(1)}, f32[256,128]{1,0:T(8,128)S(1)}, u32[]{:S(2)}, u32[]{:S(2)}) collective-permute-start(f32[256,128]{1,0:T(8,128)S(1)} %correct.1.sent_ref), channel_id=1, source_target_pairs={{0,8},{8,0},{16,24},{24,16},{1,9},{9,1},{17,25},{25,17},{2,10},{10... | collective-permute-start | bytes 393224 | tf_op jit(solution)/shard_map/ppermute | solution.py:35
  25.7 8.8 %collective-permute-start.6 = (f32[64,128]{1,0:T(8,128)S(1)}, f32[64,128]{1,0:T(8,128)S(1)}, u32[]{:S(2)}, u32[]{:S(2)}) collective-permute-start(f32[64,128]{1,0:T(8,128)S(1)} %get-tuple-element.24.refs_0_.own_ref), channel_id=1, source_target_pairs={{0,2},{1,3},{2,0},{3,1},{4,6},{5,7},{6,4},{7,5},{8,10},{9,11},{10,... | collective-permute-start | bytes 98312 | tf_op jit(solution)/shard_map/ppermute | solution.py:35
  26.5 8.0 %collective-permute-start.7 = (f32[64,128]{1,0:T(8,128)S(1)}, f32[64,128]{1,0:T(8,128)S(1)}, u32[]{:S(2)}, u32[]{:S(2)}) collective-permute-start(f32[64,128]{1,0:T(8,128)S(1)} %get-tuple-element.25.other_ref), channel_id=1, source_target_pairs={{0,4},{1,5},{2,6},{3,7},{4,0},{5,1},{6,2},{7,3},{8,12},{9,13},{10,... | collective-permute-start | bytes 98312 | tf_op jit(solution)/shard_map/ppermute | solution.py:35
  27.4 7.1 %collective-permute-start.8 = (f32[64,128]{1,0:T(8,128)S(1)}, f32[64,128]{1,0:T(8,128)S(1)}, u32[]{:S(2)}, u32[]{:S(2)}) collective-permute-start(f32[64,128]{1,0:T(8,128)S(1)} %get-tuple-element.25.other_ref), channel_id=1, source_target_pairs={{0,6},{1,7},{2,4},{3,5},{4,2},{5,3},{6,0},{7,1},{8,14},{9,15},{10,... | collective-permute-start | bytes 98312 | tf_op jit(solution)/shard_map/ppermute | solution.py:35
  29.6 5.0 %collective-permute-start.14 = (f32[64,128]{1,0:T(8,128)S(1)}, f32[64,128]{1,0:T(8,128)S(1)}, u32[]{:S(2)}, u32[]{:S(2)}) collective-permute-start(f32[64,128]{1,0:T(8,128)S(1)} %get-tuple-element.28.sent_ref), channel_id=1, source_target_pairs={{0,16},{8,24},{16,0},{24,8},{1,17},{9,25},{17,1},{25,9},{2,18},{10... | collective-permute-start | bytes 98312 | tf_op jit(solution)/shard_map/ppermute | solution.py:35
  34.5 3.9 %copy-start = (bf16[3,4608,128]{2,1,0:T(8,128)(2,1)S(1)}, bf16[3,4608,128]{2,1,0:T(8,128)(2,1)}, u32[]{:S(2)}) copy-start(bf16[3,4608,128]{2,1,0:T(8,128)(2,1)} %refs_9_.1) | copy-start | bytes 10616836
  34.6 3.9 %collective-permute-start.9 = (f32[4,64,128]{2,1,0:T(8,128)S(1)}, f32[4,64,128]{2,1,0:T(8,128)S(1)}, u32[]{:S(2)}, u32[]{:S(2)}) collective-permute-start(f32[4,64,128]{2,1,0:T(8,128)S(1)} %stack.1.own_ref), channel_id=1, source_target_pairs={{0,1},{1,0},{2,3},{3,2},{4,5},{5,4},{6,7},{7,6},{8,9},{9,8},{10,11... | collective-permute-start | bytes 393224 | tf_op jit(solution)/shard_map/ppermute | solution.py:35
  34.9 5.9 %collective-permute-start.20 = (f32[64,256]{1,0:T(8,128)S(1)}, f32[64,256]{1,0:T(8,128)S(1)}, u32[]{:S(2)}, u32[]{:S(2)}) collective-permute-start(f32[64,256]{1,0:T(8,128)S(1)} %pack.1.ref), channel_id=1, source_target_pairs={{0,6},{1,7},{2,4},{3,5},{4,2},{5,3},{6,0},{7,1},{8,14},{9,15},{10,... | collective-permute-start | bytes 196616 | tf_op jit(solution)/shard_map/ppermute | solution.py:35
  36.1 5.2 %collective-permute-start.16 = (f32[64,256]{1,0:T(8,128)S(1)}, f32[64,256]{1,0:T(8,128)S(1)}, u32[]{:S(2)}, u32[]{:S(2)}) collective-permute-start(f32[64,256]{1,0:T(8,128)S(1)} %pack.1.ref), channel_id=1, source_target_pairs={{0,2},{1,3},{2,0},{3,1},{4,6},{5,7},{6,4},{7,5},{8,10},{9,11},{10,... | collective-permute-start | bytes 196616 | tf_op jit(solution)/shard_map/ppermute | solution.py:35
  37.4 4.3 %collective-permute-start.18 = (f32[64,256]{1,0:T(8,128)S(1)}, f32[64,256]{1,0:T(8,128)S(1)}, u32[]{:S(2)}, u32[]{:S(2)}) collective-permute-start(f32[64,256]{1,0:T(8,128)S(1)} %pack.1.ref), channel_id=1, source_target_pairs={{0,4},{1,5},{2,6},{3,7},{4,0},{5,1},{6,2},{7,3},{8,12},{9,13},{10,... | collective-permute-start | bytes 196616 | tf_op jit(solution)/shard_map/ppermute | solution.py:35
  40.0 1.8 %collective-permute-start.15 = (f32[64,256]{1,0:T(8,128)S(1)}, f32[64,256]{1,0:T(8,128)S(1)}, u32[]{:S(2)}, u32[]{:S(2)}) collective-permute-start(f32[64,256]{1,0:T(8,128)S(1)} %relay.2.refs_0_), channel_id=1, source_target_pairs={{0,1},{1,0},{2,3},{3,2},{4,5},{5,4},{6,7},{7,6},{8,9},{9,8},{10,11... | collective-permute-start | bytes 196616 | tf_op jit(solution)/shard_map/ppermute | solution.py:35
  40.7 1.3 %collective-permute-start.21 = (f32[64,256]{1,0:T(8,128)S(1)}, f32[64,256]{1,0:T(8,128)S(1)}, u32[]{:S(2)}, u32[]{:S(2)}) collective-permute-start(f32[64,256]{1,0:T(8,128)S(1)} %relay.3.refs_6_), channel_id=1, source_target_pairs={{0,1},{1,0},{2,3},{3,2},{4,5},{5,4},{6,7},{7,6},{8,9},{9,8},{10,11... | collective-permute-start | bytes 196616 | tf_op jit(solution)/shard_map/ppermute | solution.py:35
  41.3 1.3 %collective-permute-start.17 = (f32[64,256]{1,0:T(8,128)S(1)}, f32[64,256]{1,0:T(8,128)S(1)}, u32[]{:S(2)}, u32[]{:S(2)}) collective-permute-start(f32[64,256]{1,0:T(8,128)S(1)} %collective-permute-done.16.refs_2_), channel_id=1, source_target_pairs={{0,1},{1,0},{2,3},{3,2},{4,5},{5,4},{6,7},{7,6},{8,9},{9,8},{10,11... | collective-permute-start | bytes 196616 | tf_op jit(solution)/shard_map/ppermute | solution.py:35
  41.7 1.3 %collective-permute-start.19 = (f32[64,256]{1,0:T(8,128)S(1)}, f32[64,256]{1,0:T(8,128)S(1)}, u32[]{:S(2)}, u32[]{:S(2)}) collective-permute-start(f32[64,256]{1,0:T(8,128)S(1)} %collective-permute-done.18.refs_4_), channel_id=1, source_target_pairs={{0,1},{1,0},{2,3},{3,2},{4,5},{5,4},{6,7},{7,6},{8,9},{9,8},{10,11... | collective-permute-start | bytes 196616 | tf_op jit(solution)/shard_map/ppermute | solution.py:35
